TPU v7x, 32 devices: a whole 2x2x4 slice. The times are simulated.
32 devices in a mesh: seq: 4 (over z), exp: 8 (over y, x, core).
Axes of the slice: x: 2, y: 2, z: 4, core: 2. Of those that a mesh axis runs over, the one named last changes fastest.
Arguments:
- attn_query: bfloat16 [1024, 6144], P('seq', 'exp'), may hold values from -6 to 6
- attn_key: bfloat16 [1024, 6144], P('seq', 'exp'), may hold values from -6 to 6
- attn_value: bfloat16 [1024, 6144], P('seq', 'exp'), may hold values from -40 to 40
- log_decay: float32 [48, 1024], P('exp', 'seq'), may hold values from -1.5 to 0
- residual: bfloat16 [1024, 6144], P('seq', 'exp'), may hold values from -6 to 6
- norm_gain: bfloat16 [6144], P('exp'), may hold values from 0.099609375 to 1.8984375
- expert_ids: int32 [1024, 2], P('seq'), may hold values from 0 to 7, as said below
- router_weight: bfloat16 [6144, 8], P(None, 'seq'), may hold values from -0.078125 to 0.078125
- gate_weight: bfloat16 [8, 6144, 4608], P('seq', None, 'exp'), may hold values from -0.078125 to 0.078125
- up_weight: bfloat16 [8, 6144, 4608], P('seq', None, 'exp'), may hold values from -0.078125 to 0.078125
- down_weight: bfloat16 [8, 4608, 6144], P('seq', 'exp'), may hold values from -0.125 to 0.125
Outputs:
- layer_out: bfloat16 [1024, 6144], P('seq', 'exp')
Inputs may be any that keep to these rules, and one draw needn't show every extreme that they name: `expert_ids`: each row names two different experts. In every section of 256 consecutive rows no expert is named more than 128 times, and in every section some experts are named exactly 128 times.
All inputs are finite; a program needn't handle non-finite values.
Results may differ from a plain program's by a relative error of at most 0.017.
Values may be sent and summed in bfloat16 or wider, within the bound.
No kernel may reach another device: no remote copies, remote signals or barrier semaphores. Data moves between devices by JAX's collectives and lax.ppermute only.
A program may use at most 192 MiB of HBM per device.

v0:
```python
import jax
import jax.numpy as jnp
from jax import lax
from jax.sharding import PartitionSpec as P


def shifted(array, axis, by):
    count = lax.axis_size(axis)
    pairs = [(i, i + by) for i in range(count) if 0 <= i + by < count]
    return lax.ppermute(array, axis, pairs)


def on_device(
    attn_query,
    attn_key,
    attn_value,
    log_decay,
    residual,
    norm_gain,
    expert_ids,
    router_weight,
    gate_weight,
    up_weight,
    down_weight,
):
    heads_here = log_decay.shape[0]
    length = log_decay.shape[1]
    head_size = attn_query.shape[1] // heads_here
    query_rows = attn_query.reshape(length, heads_here, head_size)
    key_rows = attn_key.reshape(length, heads_here, head_size)
    value_rows = attn_value.reshape(length, heads_here, head_size)
    cumulative = jnp.cumsum(log_decay, axis=1)
    causal = lax.broadcasted_iota(jnp.int32, (length, length), 0) >= lax.broadcasted_iota(
        jnp.int32, (length, length), 1
    )
    decay_gap = jnp.where(causal[None], cumulative[:, :, None] - cumulative[:, None, :], 0.0)
    decay_mask = jnp.where(causal[None], jnp.exp(decay_gap), 0.0)
    scores = jnp.einsum("thd,shd->hts", query_rows, key_rows, preferred_element_type=jnp.float32)
    weights = (scores * decay_mask).astype(jnp.bfloat16)
    intra_part = jnp.einsum("hts,shd->thd", weights, value_rows, preferred_element_type=jnp.float32)
    key_fade = jnp.exp(cumulative[:, -1:] - cumulative)
    scaled = (key_fade.T[:, :, None] * key_rows.astype(jnp.float32)).astype(jnp.bfloat16)
    local_state = jnp.einsum("shd,she->hde", scaled, value_rows, preferred_element_type=jnp.float32)
    section_fade = jnp.exp(cumulative[:, -1])
    incoming = jnp.zeros_like(local_state)
    for repeat_index in range(lax.axis_size("seq") - 1):
        incoming = shifted(section_fade[:, None, None] * incoming + local_state, "seq", 1)
    inter_part = jnp.einsum(
        "thd,hde->the", query_rows.astype(jnp.float32), incoming, precision=lax.Precision.HIGHEST
    )
    attn_out = intra_part + jnp.exp(cumulative).T[:, :, None] * inter_part
    mean_square = jnp.mean(attn_out * attn_out, axis=2, keepdims=True)
    normed = (attn_out / jnp.sqrt(mean_square + 1e-06)).reshape(length, heads_here * head_size)
    stream = (residual.astype(jnp.float32) + norm_gain.astype(jnp.float32) * normed).astype(
        jnp.bfloat16
    )
    experts_here = router_weight.shape[1]
    groups = lax.axis_size("seq")
    expert_count = experts_here * groups
    capacity = 4 * length // expert_count
    features = stream.shape[1]
    choices_per_token = expert_ids.shape[1]
    flat_ids = expert_ids.reshape(-1)
    expert_iota = lax.broadcasted_iota(jnp.int32, (1, expert_count), 1)
    onehot = (flat_ids[:, None] == expert_iota).astype(jnp.int32)
    running = jnp.cumsum(onehot, axis=0)
    slot_index = jnp.sum(running * onehot, axis=1) - 1
    target = flat_ids * capacity + slot_index
    place_iota = lax.broadcasted_iota(jnp.int32, (expert_count * capacity, 1), 0)
    route_matrix = (
        (place_iota == target[None, :])
        .astype(jnp.bfloat16)
        .reshape(expert_count * capacity, length, choices_per_token)
        .sum(axis=2)
    )
    outgoing = jnp.dot(route_matrix, stream, preferred_element_type=jnp.float32).astype(
        jnp.bfloat16
    )
    outgoing = outgoing.reshape(groups, experts_here, capacity, features)
    portion = lax.all_gather(
        lax.all_to_all(outgoing, "seq", split_axis=0, concat_axis=0, tiled=True),
        "exp",
        axis=3,
        tiled=True,
    )
    gate_acc = jnp.einsum(
        "sjcd,jdf->sjcf", portion, gate_weight, preferred_element_type=jnp.float32
    )
    upward = jnp.einsum("sjcd,jdf->sjcf", portion, up_weight, preferred_element_type=jnp.float32)
    logits = jnp.einsum("sjcd,dj->sjc", portion, router_weight, preferred_element_type=jnp.float32)
    hidden_act = (jax.nn.silu(gate_acc) * upward).astype(jnp.bfloat16)
    expert_out = lax.psum_scatter(
        jnp.einsum(
            "sjcf,jfd->dsjc", hidden_act, down_weight, preferred_element_type=jnp.float32
        ).astype(jnp.bfloat16),
        "exp",
        scatter_dimension=0,
        tiled=True,
    ).astype(jnp.float32)
    routed = (jax.nn.sigmoid(logits)[None] * expert_out).astype(jnp.bfloat16)
    returned = lax.all_to_all(routed, "seq", split_axis=1, concat_axis=1, tiled=True)
    returned = returned.reshape(features, expert_count * capacity)
    combined = lax.dot_general(
        route_matrix, returned, (((0,), (1,)), ((), ())), preferred_element_type=jnp.float32
    )
    return (stream.astype(jnp.float32) + combined).astype(jnp.bfloat16)


def solution(mesh):
    in_specs = (
        P("seq", "exp"),
        P("seq", "exp"),
        P("seq", "exp"),
        P("exp", "seq"),
        P("seq", "exp"),
        P("exp"),
        P("seq", None),
        P(None, "seq"),
        P("seq", None, "exp"),
        P("seq", None, "exp"),
        P("seq", "exp", None),
    )
    out_specs = P("seq", "exp")
    return jax.shard_map(
        on_device, mesh=mesh, in_specs=in_specs, out_specs=out_specs, check_vma=False
    )
```

profile of v0, /device:TPU:0, one launch (start us, length us, event | category | flops | bytes accessed | tf_op | source)
XLA Modules:
  0.0 359.8 jit_solution(287767826483079912)
XLA Ops:
  6.5 0.0 copy-start
  6.5 0.0 copy-start.3
  6.5 0.0 all-gather.2.cloned.1.call-start
  6.5 0.7 reshape.116
  7.3 1.8 reduce-window.14
  9.1 0.1 slice.21
  9.1 0.1 copy.80
  9.3 0.1 copy.81
  9.4 0.1 add_bitcast_fusion
  9.5 0.1 slice.22
  9.5 0.1 copy.103
  9.7 0.1 exponential_bitcast_fusion.1
  9.7 1.2 copy.77
  10.9 1.2 copy.82
  12.1 0.0 copy-start.1
  12.1 0.3 broadcast_add_fusion
  12.4 0.0 copy-start.4
  12.4 5.0 %collective-permute-start = (f32[6,128,128]{2,1,0:T(8,128)S(1)}, f32[6,128,128]{2,1,0:T(8,128)S(1)}, u32[]{:S(2)}, u32[]{:S(2)}) collective-permute-start(f32[6,128,128]{2,1,0:T(8,128)S(1)} %get-tuple-element.9), channel_id=1, source_target_pairs={{0,8},{8,16},{16,24},{1,9},{9,17},{17,25},{2,10},{10,18},{18,26},{... | collective-permute-start | bytes 1179656 | tf_op jit(solution)/shard_map/ppermute | solution.py:10
  17.3 0.0 copy-done.3
  17.3 0.1 copy.88
  17.5 0.1 eq.44
  17.6 0.1 eq.40
  17.8 1.1 reduce-window.16
  18.9 0.2 slice_reduce_fusion
  19.2 0.1 fusion.32
  19.3 6.4 %collective-permute-done = f32[6,128,128]{2,1,0:T(8,128)S(1)} collective-permute-done((f32[6,128,128]{2,1,0:T(8,128)S(1)}, f32[6,128,128]{2,1,0:T(8,128)S(1)}, u32[]{:S(2)}, u32[]{:S(2)}) %collective-permute-start) | collective-permute-done | bytes 393248 | tf_op jit(solution)/shard_map/ppermute | solution.py:10
  25.7 0.1 multiply_add_fusion.1
  25.8 4.4 %collective-permute-start.1 = (f32[6,128,128]{2,1,0:T(8,128)S(1)}, f32[6,128,128]{2,1,0:T(8,128)S(1)}, u32[]{:S(2)}, u32[]{:S(2)}) collective-permute-start(f32[6,128,128]{2,1,0:T(8,128)S(1)} %multiply_add_fusion.1), channel_id=1, source_target_pairs={{0,8},{8,16},{16,24},{1,9},{9,17},{17,25},{2,10},{10,18},{18,26},{... | collective-permute-start | bytes 1179656 | tf_op jit(solution)/shard_map/ppermute | solution.py:10
  30.2 0.1 sub.33
  30.4 0.1 copy.90
  30.4 7.2 %collective-permute-done.1 = f32[6,128,128]{2,1,0:T(8,128)S(1)} collective-permute-done((f32[6,128,128]{2,1,0:T(8,128)S(1)}, f32[6,128,128]{2,1,0:T(8,128)S(1)}, u32[]{:S(2)}, u32[]{:S(2)}) %collective-permute-start.1) | collective-permute-done | bytes 393248 | tf_op jit(solution)/shard_map/ppermute | solution.py:10
  37.7 0.1 multiply_add_fusion
  37.8 4.4 %collective-permute-start.2 = (f32[6,128,128]{2,1,0:T(8,128)S(1)}, f32[6,128,128]{2,1,0:T(8,128)S(1)}, u32[]{:S(2)}, u32[]{:S(2)}) collective-permute-start(f32[6,128,128]{2,1,0:T(8,128)S(1)} %multiply_add_fusion), channel_id=1, source_target_pairs={{0,8},{8,16},{16,24},{1,9},{9,17},{17,25},{2,10},{10,18},{18,26},{... | collective-permute-start | bytes 1179656 | tf_op jit(solution)/shard_map/ppermute | solution.py:10
  42.2 0.5 fusion.23
  42.6 0.0 copy-done.1
  42.7 0.2 copy.76
  42.8 0.0 copy-done.4
  42.9 0.8 fusion.20
  43.7 5.0 %collective-permute-done.2 = f32[6,128,128]{2,1,0:T(8,128)S(1)} collective-permute-done((f32[6,128,128]{2,1,0:T(8,128)S(1)}, f32[6,128,128]{2,1,0:T(8,128)S(1)}, u32[]{:S(2)}, u32[]{:S(2)}) %collective-permute-start.2) | collective-permute-done | bytes 393248 | tf_op jit(solution)/shard_map/ppermute | solution.py:10
  48.7 0.0 copy-start.2
  48.7 0.6 multiply_reduce_fusion
  49.3 0.1 broadcast_divide_fusion
  49.4 0.3 copy.87
  49.7 0.0 copy-done.2
  49.7 0.1 add_convert_fusion
  49.8 0.6 convolution_convert_fusion
  50.4 39.9 %all_to_all.10 = bf16[4,2,128,768]{3,2,1,0:T(8,128)(2,1)S(1)} all-to-all(bf16[4,2,128,768]{3,2,1,0:T(8,128)(2,1)S(1)} %bitcast.101), channel_id=1, replica_groups=mesh['seq'=4,'exp'=8] {'seq'}, dimensions={0} | all-to-all | bytes 3145728 | tf_op jit(solution)/shard_map/all_to_all | solution.py:81
  90.3 1.3 copy.91
  91.6 0.0 all-gather.2.cloned.1.call-update
  91.6 0.2 reduce-scatter.2.cloned.1.call-start
  91.8 70.8 %all-gather.2.cloned.1.call-done = bf16[4,2,128,6144]{3,2,0,1:T(8,128)(2,1)} async-done(((bf16[4,2,128,768]{3,2,0,1:T(8,128)(2,1)}), bf16[4,2,128,6144]{3,2,0,1:T(8,128)(2,1)}) %all-gather.2.cloned.1.call-update) | async-done | bytes 12582928 | tf_op jit(solution)/shard_map/all_gather | solution.py:80
  162.7 12.6 %fusion.2 = f32[2,4,128,576]{2,3,1,0:T(8,128)S(1)} fusion(bf16[4,2,128,6144]{3,2,0,1:T(8,128)(2,1)} %all-gather.2.cloned.1.call-done, bf16[2,6144,576]{1,2,0:T(8,128)(2,1)} %param.20), kind=kOutput, calls=%fused_computation.2 | convolution fusion | flops 7247757312 | bytes 29097984 | tf_op jit(solution)/shard_map/sjcd,jdf->sjcf/dot_general | solution.py:89
  175.2 40.6 %convert_bitcast_fusion = bf16[6144,4,2,128]{0,3,1,2:T(8,128)(2,1)} fusion(bf16[2,576,6144]{2,1,0:T(8,128)(2,1)} %param.21, f32[2,4,128,576]{2,3,1,0:T(8,128)S(1)} %fusion.2, bf16[4,2,128,6144]{3,2,0,1:T(8,128)(2,1)} %all-gather.2.cloned.1.call-done, bf16[2,6144,576]{1,2,0:T(8,128)(2,1)} %param.19), kind=kOutput, calls=%fused_computation.6 | convolution fusion | flops 14505345024 | bytes 55836672 | tf_op jit(solution)/shard_map/sjcf,jfd->dsjc/dot_general | solution.py:93
  215.9 0.0 reduce-scatter.2.cloned.1.call-update
  215.9 0.0 copy-done
  215.9 6.3 %fusion.30 = f32[2,1,4,128]{3,1,2,0:T(1,128)S(1)} fusion(bf16[4,2,128,6144]{3,2,0,1:T(8,128)(2,1)} %all-gather.2.cloned.1.call-done, bf16[6144,2,1,1]{0,1,2,3:T(2,128)(2,1)S(1)} %bitcast.100), kind=kOutput, calls=%fused_computation.42 | convolution fusion | flops 12582912 | bytes 12611584 | tf_op jit(solution)/shard_map/sjcd,dj->sjc/dot_general | solution.py:90
  222.3 86.2 %reduce-scatter.2.cloned.1.call-done = bf16[768,4,2,128]{0,3,1,2:T(8,128)(2,1)} async-done(((bf16[6144,4,2,128]{0,3,1,2:T(8,128)(2,1)}), bf16[768,4,2,128]{0,3,1,2:T(8,128)(2,1)}) %reduce-scatter.2.cloned.1.call-update) | async-done | bytes 1572880 | tf_op jit(solution)/shard_map/reduce_scatter | solution.py:92
  308.5 1.7 multiply_convert_fusion
  310.2 0.1 copy.92
  310.3 41.3 %all_to_all.11 = bf16[768,4,2,128]{0,3,2,1:T(8,128)(2,1)S(1)} all-to-all(bf16[768,4,2,128]{0,3,2,1:T(8,128)(2,1)S(1)} %copy.92), channel_id=1, replica_groups=mesh['seq'=4,'exp'=8] {'seq'}, dimensions={1} | all-to-all | bytes 3145728 | tf_op jit(solution)/shard_map/all_to_all | solution.py:101
  351.6 1.4 fusion.21
  (13 shorter events, 0.2 us)
Async XLA Ops:
  6.5 209.4 %copy-start = (bf16[6144,2]{0,1:T(2,128)(2,1)S(1)}, bf16[6144,2]{0,1:T(2,128)(2,1)}, u32[]{:S(2)}) copy-start(bf16[6144,2]{0,1:T(2,128)(2,1)} %param.18) | copy-start | bytes 73732
  6.5 10.8 %copy-start.3 = (s32[256,2]{0,1:T(2,128)S(1)}, s32[256,2]{0,1:T(2,128)}, u32[]{:S(2)}) copy-start(s32[256,2]{0,1:T(2,128)} %param.17) | copy-start | bytes 6148
  6.5 156.1 %all-gather.2.cloned.1.call-start = ((), (), s32[]{:S(2)}) async-start(), calls=%async_computation.3 | async-start | bytes 14155776 | tf_op jit(solution)/shard_map/all_gather | solution.py:80
  12.1 30.6 %copy-start.1 = (bf16[256,768]{1,0:T(8,128)(2,1)S(1)}, bf16[256,768]{1,0:T(8,128)(2,1)}, u32[]{:S(2)}) copy-start(bf16[256,768]{1,0:T(8,128)(2,1)} %param.11) | copy-start | bytes 1179652
  12.4 30.5 %copy-start.4 = (bf16[768]{0:T(1024)(128)(2,1)S(1)}, bf16[768]{0:T(1024)(128)(2,1)}, u32[]{:S(2)}) copy-start(bf16[768]{0:T(1024)(128)(2,1)} %param.16) | copy-start | bytes 4612
  12.4 13.3 %collective-permute-start = (f32[6,128,128]{2,1,0:T(8,128)S(1)}, f32[6,128,128]{2,1,0:T(8,128)S(1)}, u32[]{:S(2)}, u32[]{:S(2)}) collective-permute-start(f32[6,128,128]{2,1,0:T(8,128)S(1)} %get-tuple-element.9), channel_id=1, source_target_pairs={{0,8},{8,16},{16,24},{1,9},{9,17},{17,25},{2,10},{10,18},{18,26},{... | collective-permute-start | bytes 1179656 | tf_op jit(solution)/shard_map/ppermute | solution.py:10
  25.8 11.9 %collective-permute-start.1 = (f32[6,128,128]{2,1,0:T(8,128)S(1)}, f32[6,128,128]{2,1,0:T(8,128)S(1)}, u32[]{:S(2)}, u32[]{:S(2)}) collective-permute-start(f32[6,128,128]{2,1,0:T(8,128)S(1)} %multiply_add_fusion.1), channel_id=1, source_target_pairs={{0,8},{8,16},{16,24},{1,9},{9,17},{17,25},{2,10},{10,18},{18,26},{... | collective-permute-start | bytes 1179656 | tf_op jit(solution)/shard_map/ppermute | solution.py:10
  37.8 10.9 %collective-permute-start.2 = (f32[6,128,128]{2,1,0:T(8,128)S(1)}, f32[6,128,128]{2,1,0:T(8,128)S(1)}, u32[]{:S(2)}, u32[]{:S(2)}) collective-permute-start(f32[6,128,128]{2,1,0:T(8,128)S(1)} %multiply_add_fusion), channel_id=1, source_target_pairs={{0,8},{8,16},{16,24},{1,9},{9,17},{17,25},{2,10},{10,18},{18,26},{... | collective-permute-start | bytes 1179656 | tf_op jit(solution)/shard_map/ppermute | solution.py:10
  48.7 1.0 copy-start.2
  91.6 216.8 %reduce-scatter.2.cloned.1.call-start = ((), (), s32[]{:S(2)}) async-start(), calls=%async_computation.4 | async-start | bytes 14155776 | tf_op jit(solution)/shard_map/reduce_scatter | solution.py:92
Sparse Core Ops, SparseCore 0:
  91.7 70.8 all-gather.1
  216.0 92.3 reduce-scatter.1
where the time goes:
time: 360 us
  waiting for transfers between devices  176 us (49%)
  blocking collectives  81.2 us (23%)
  matrix products  63.2 us (18%)
  starting transfers between devices  14 us (4%)
  between operations  13.6 us (4%)
  local copies, waits for them, and re-layouts  6.23 us (2%)
  other arithmetic  5.92 us (2%)
    reduce_scatter x1, waiting for transfers between devices, on_device(): lax.psum_scatter(jnp.einsum('sjcf,jfd->dsjc', hidden_act, down_weight, pr...  86.2 us
    all_gather x1, waiting for transfers between devices, on_device(): lax.all_gather(lax.all_to_all(outgoing, 'seq', split_axis=0, concat_axis=...  70.8 us
    all_to_all x1, blocking collectives, on_device(): lax.all_to_all(routed, 'seq', split_axis=1, concat_axis=1, tiled=True)  41.3 us
    dot_general x1, matrix products, on_device(): jnp.einsum('sjcf,jfd->dsjc', hidden_act, down_weight, preferred_element_t...  40.6 us
    all_to_all x1, blocking collectives, on_device(): lax.all_to_all(outgoing, 'seq', split_axis=0, concat_axis=0, tiled=True)  39.9 us
    ppermute x3, waiting for transfers between devices, shifted(): return lax.ppermute(array, axis, pairs)  18.6 us
    ppermute x3, starting transfers between devices, shifted(): return lax.ppermute(array, axis, pairs)  13.8 us
    dot_general x1, matrix products, on_device(): jnp.einsum('sjcd,jdf->sjcf', portion, up_weight, preferred_element_type=j...  12.6 us
  transfers between devices with their start and end apart: 5, of which 5 were waited for; matrix products, arithmetic and copies ran while one was open for 3% of the time, Pallas kernels for 0%

commit v1 on v0

v1 whole, which is shorter than its diff:
```python
import functools

import jax
import jax.numpy as jnp
from jax import lax
from jax.experimental import pallas as pl
from jax.experimental.pallas import tpu as pltpu
from jax.sharding import PartitionSpec as P

F32 = jnp.float32
BF16 = jnp.bfloat16
HIGHEST = lax.Precision.HIGHEST
VMEM_LIMIT = 48 * 1024 * 1024


def lower_ones(length):
    rows = lax.broadcasted_iota(jnp.int32, (length, length), 0)
    columns = lax.broadcasted_iota(jnp.int32, (length, length), 1)
    return rows >= columns


def shifted(array, axis, by, wrap=False):
    count = lax.axis_size(axis)
    if wrap:
        pairs = [(i, (i + by) % count) for i in range(count)]
    else:
        pairs = [(i, i + by) for i in range(count) if 0 <= i + by < count]
    return lax.ppermute(array, axis, pairs)


def state_kernel(key_ref, value_ref, decay_ref, message_ref, cumulative_ref):
    heads, length = decay_ref.shape
    size = key_ref.shape[1] // heads
    ones = lower_ones(length).astype(F32)
    cumulative = lax.dot_general(
        ones, decay_ref[...], (((1,), (1,)), ((), ())), precision=HIGHEST, preferred_element_type=F32
    )
    cumulative_ref[...] = cumulative
    last = cumulative[length - 1 : length, :]
    key_fade = jnp.exp(last - cumulative)
    message_ref[heads * size :, :] = jnp.zeros((message_ref.shape[0] - heads * size, size), BF16)
    half = (message_ref.shape[0] - heads * size) // 2
    rows = []
    for h in range(heads):
        columns = slice(h * size, (h + 1) * size)
        scaled = (key_fade[:, h : h + 1] * key_ref[:, columns].astype(F32)).astype(BF16)
        state = lax.dot_general(
            scaled, value_ref[:, columns], (((0,), (0,)), ((), ())), preferred_element_type=F32
        )
        message_ref[columns, :] = state.astype(BF16)
        rows.append(jnp.broadcast_to(jnp.exp(last[:, h : h + 1]), (1, size)))
    rows.append(jnp.zeros((half - heads, size), F32))
    fade = jnp.concatenate(rows, axis=0)
    leading = fade.astype(BF16)
    trailing = (fade - leading.astype(F32)).astype(BF16)
    message_ref[heads * size :, :] = jnp.concatenate([leading, trailing], axis=0)


def section_state(attn_key, attn_value, log_decay):
    heads, length = log_decay.shape
    width = attn_key.shape[1]
    half = -(-heads // 8) * 8
    return pl.pallas_call(
        state_kernel,
        out_shape=(
            jax.ShapeDtypeStruct((width + 2 * half, width // heads), BF16),
            jax.ShapeDtypeStruct((length, heads), F32),
        ),
        cost_estimate=pl.CostEstimate(
            flops=2 * length * width * (width // heads), bytes_accessed=4 * length * width, transcendentals=0
        ),
        compiler_params=pltpu.CompilerParams(vmem_limit_bytes=VMEM_LIMIT),
    )(attn_key, attn_value, log_decay)


def intra_kernel(query_ref, key_ref, value_ref, decay_ref, cumulative_ref, out_ref):
    heads, length = decay_ref.shape
    size = key_ref.shape[1] // heads
    causal = lower_ones(length)
    along = lax.dot_general(
        decay_ref[...],
        causal.astype(F32),
        (((1,), (1,)), ((), ())),
        precision=HIGHEST,
        preferred_element_type=F32,
    )
    for h in range(heads):
        columns = slice(h * size, (h + 1) * size)
        gap = jnp.where(causal, cumulative_ref[:, h : h + 1] - along[h : h + 1, :], 0.0)
        mask = jnp.where(causal, jnp.exp(gap), 0.0)
        scores = lax.dot_general(
            query_ref[:, columns], key_ref[:, columns], (((1,), (1,)), ((), ())), preferred_element_type=F32
        )
        weights = (scores * mask).astype(BF16)
        out_ref[:, columns] = jnp.dot(weights, value_ref[:, columns], preferred_element_type=F32)


def intra_section(attn_query, attn_key, attn_value, log_decay, cumulative):
    length, width = attn_query.shape
    return pl.pallas_call(
        intra_kernel,
        out_shape=jax.ShapeDtypeStruct((length, width), F32),
        cost_estimate=pl.CostEstimate(
            flops=4 * length * length * width, bytes_accessed=10 * length * width, transcendentals=0
        ),
        compiler_params=pltpu.CompilerParams(vmem_limit_bytes=VMEM_LIMIT),
    )(attn_query, attn_key, attn_value, log_decay, cumulative)


def stream_kernel(query_ref, intra_ref, cumulative_ref, incoming_ref, residual_ref, gain_ref, out_ref):
    heads, size = incoming_ref.shape[0], incoming_ref.shape[1]
    faded = jnp.exp(cumulative_ref[...])
    for h in range(heads):
        columns = slice(h * size, (h + 1) * size)
        state = incoming_ref[h]
        leading = state.astype(BF16)
        trailing = (state - leading.astype(F32)).astype(BF16)
        query = query_ref[:, columns]
        inter = jnp.dot(query, leading, preferred_element_type=F32) + jnp.dot(
            query, trailing, preferred_element_type=F32
        )
        attn_out = intra_ref[:, columns] + faded[:, h : h + 1] * inter
        mean_square = jnp.mean(attn_out * attn_out, axis=1, keepdims=True)
        normed = attn_out * lax.rsqrt(mean_square + 1e-06)
        out_ref[:, columns] = (
            residual_ref[:, columns].astype(F32) + gain_ref[:, columns].astype(F32) * normed
        ).astype(BF16)


def make_stream(attn_query, intra, cumulative, incoming, residual, norm_gain):
    length, width = attn_query.shape
    return pl.pallas_call(
        stream_kernel,
        out_shape=jax.ShapeDtypeStruct((length, width), BF16),
        compiler_params=pltpu.CompilerParams(vmem_limit_bytes=VMEM_LIMIT),
    )(attn_query, intra, cumulative, incoming, residual, norm_gain.reshape(1, width))


def read_message(message, heads):
    size = message.shape[1]
    half = (message.shape[0] - heads * size) // 2
    state = message[: heads * size].astype(F32).reshape(heads, size, size)
    tail = message[heads * size :].astype(F32)
    fade = tail[:heads] + tail[half : half + heads]
    return fade[:, None, :], state


def write_message(fade, state, rows):
    heads, size = state.shape[0], state.shape[1]
    half = (rows - heads * size) // 2
    leading = fade[:, 0, :].astype(BF16)
    trailing = (fade[:, 0, :] - leading.astype(F32)).astype(BF16)
    spare = jnp.zeros((half - heads, size), BF16)
    return jnp.concatenate(
        [state.astype(BF16).reshape(heads * size, size), leading, spare, trailing, spare], axis=0
    )


def incoming_state(message, heads):
    count = lax.axis_size("seq")
    window_fade, window = read_message(message, heads)
    incoming_fade, incoming = None, None
    distance = 1
    while distance < count:
        got_fade, got = read_message(shifted(message, "seq", distance), heads)
        if incoming is None:
            incoming_fade, incoming = got_fade, got
        else:
            incoming, incoming_fade = incoming + incoming_fade * got, incoming_fade * got_fade
        window, window_fade = window + window_fade * got, window_fade * got_fade
        distance *= 2
        if distance < count:
            message = write_message(window_fade, window, message.shape[0])
    return incoming


def expert_kernel(
    capacity, steps, first_ref, ids_ref, x_ref, router_ref, gate_ref, up_ref, down_ref, out_ref,
    gate_acc, up_acc, score_acc, place, hidden,
):
    step = pl.program_id(0)
    experts = gate_ref.shape[0]
    length = x_ref.shape[1]

    @pl.when(step == 0)
    def _():
        tokens_before = lower_ones(length)
        slot = lax.broadcasted_iota(jnp.int32, (capacity, length), 0)
        for j in range(experts):
            chosen = ids_ref[0:1, :] == first_ref[0] + j
            for choice in range(1, ids_ref.shape[0]):
                chosen = chosen | (ids_ref[choice : choice + 1, :] == first_ref[0] + j)
            flag = jnp.where(chosen, 1.0, 0.0)
            rank = lax.dot_general(
                jnp.broadcast_to(flag, (8, length)).astype(BF16),
                tokens_before.astype(BF16),
                (((1,), (1,)), ((), ())),
                preferred_element_type=F32,
            )[0:1, :]
            here = (rank.astype(jnp.int32) - 1 == slot) & (flag > 0.5)
            place[j * capacity : (j + 1) * capacity, :] = jnp.where(here, 1.0, 0.0).astype(BF16)
        gate_acc[...] = jnp.zeros_like(gate_acc)
        up_acc[...] = jnp.zeros_like(up_acc)
        score_acc[...] = jnp.zeros_like(score_acc)

    @pl.when(step < steps)
    def _():
        rows = jnp.dot(place[...], x_ref[0], preferred_element_type=F32).astype(BF16)
        score_acc[...] += lax.dot_general(
            rows, router_ref[0], (((1,), (1,)), ((), ())), preferred_element_type=F32
        )
        for j in range(experts):
            mine = slice(j * capacity, (j + 1) * capacity)
            gate_acc[mine, :] += jnp.dot(rows[mine], gate_ref[j], preferred_element_type=F32)
            up_acc[mine, :] += jnp.dot(rows[mine], up_ref[j], preferred_element_type=F32)

    @pl.when(step == steps - 1)
    def _():
        gate = gate_acc[...]
        hidden[...] = (gate / (1.0 + jnp.exp(-gate)) * up_acc[...]).astype(BF16)

    @pl.when(step >= steps)
    def _():
        parts = []
        for j in range(experts):
            mine = slice(j * capacity, (j + 1) * capacity)
            share = jnp.dot(hidden[mine, :], down_ref[j], preferred_element_type=F32)
            score = score_acc[mine, j : j + 1]
            parts.append((share / (1.0 + jnp.exp(-score))).astype(BF16))
        routed = jnp.concatenate(parts, axis=0)
        out_ref[0] = lax.dot_general(
            place[...], routed, (((0,), (0,)), ((), ())), preferred_element_type=F32
        ).astype(BF16)


def expert_section(first, ids, x, router_rows, gate_weight, up_weight, down_weight, capacity):
    steps, length, width = x.shape
    experts, _, units = gate_weight.shape
    slots = experts * capacity
    early = lambda i: jnp.minimum(i, steps - 1)
    late = lambda i: jnp.maximum(i - steps, 0)
    return pl.pallas_call(
        functools.partial(expert_kernel, capacity, steps),
        grid=(2 * steps,),
        in_specs=[
            pl.BlockSpec(memory_space=pltpu.SMEM),
            pl.BlockSpec(ids.shape, lambda i: (0, 0)),
            pl.BlockSpec((1, length, width), lambda i: (early(i), 0, 0)),
            pl.BlockSpec((1, experts, width), lambda i: (early(i), 0, 0)),
            pl.BlockSpec((experts, width, units), lambda i: (0, early(i), 0)),
            pl.BlockSpec((experts, width, units), lambda i: (0, early(i), 0)),
            pl.BlockSpec((experts, units, width), lambda i: (0, 0, late(i))),
        ],
        out_specs=pl.BlockSpec((1, length, width), lambda i: (late(i), 0, 0)),
        out_shape=jax.ShapeDtypeStruct((steps, length, width), BF16),
        scratch_shapes=[
            pltpu.VMEM((slots, units), F32),
            pltpu.VMEM((slots, units), F32),
            pltpu.VMEM((slots, experts), F32),
            pltpu.VMEM((slots, length), BF16),
            pltpu.VMEM((slots, units), BF16),
        ],
        cost_estimate=pl.CostEstimate(
            flops=6 * slots * steps * width * units,
            bytes_accessed=6 * experts * steps * width * units,
            transcendentals=0,
        ),
        compiler_params=pltpu.CompilerParams(vmem_limit_bytes=VMEM_LIMIT),
    )(first, ids, x, router_rows, gate_weight, up_weight, down_weight)


def on_device(
    attn_query,
    attn_key,
    attn_value,
    log_decay,
    residual,
    norm_gain,
    expert_ids,
    router_weight,
    gate_weight,
    up_weight,
    down_weight,
):
    heads_here, length = log_decay.shape
    groups = lax.axis_size("seq")
    shares = lax.axis_size("exp")
    width = attn_query.shape[1]
    experts_here = router_weight.shape[1]
    capacity = 4 * length // (experts_here * groups)
    section = lax.axis_index("seq")
    first = (section * experts_here).astype(jnp.int32).reshape(1)
    router_rows = router_weight.reshape(shares, width, experts_here).transpose(0, 2, 1)

    all_ids = lax.all_gather(expert_ids.T, "seq", axis=0)
    message, cumulative = section_state(attn_key, attn_value, log_decay)
    intra = intra_section(attn_query, attn_key, attn_value, log_decay, cumulative)
    incoming = incoming_state(message, heads_here)
    stream = make_stream(attn_query, intra, cumulative, incoming, residual, norm_gain)

    total = stream.astype(F32)
    for offset in range(groups):
        part = stream if offset == 0 else shifted(stream, "seq", offset, wrap=True)
        ids = lax.dynamic_index_in_dim(all_ids, (section - offset) % groups, 0, keepdims=False)
        gathered = lax.all_gather(part, "exp", axis=0)
        partial = expert_section(
            first, ids, gathered, router_rows, gate_weight, up_weight, down_weight, capacity
        )
        share = lax.psum_scatter(partial, "exp", scatter_dimension=0)
        if offset:
            share = shifted(share, "seq", -offset, wrap=True)
        total = total + share.astype(F32)
    return total.astype(BF16)


def solution(mesh):
    in_specs = (
        P("seq", "exp"),
        P("seq", "exp"),
        P("seq", "exp"),
        P("exp", "seq"),
        P("seq", "exp"),
        P("exp"),
        P("seq", None),
        P(None, "seq"),
        P("seq", None, "exp"),
        P("seq", None, "exp"),
        P("seq", "exp", None),
    )
    out_specs = P("seq", "exp")
    return jax.shard_map(
        on_device, mesh=mesh, in_specs=in_specs, out_specs=out_specs, check_vma=False
    )
```

time: 360 us -> 393 us (1.092)
  Pallas kernels: 0 us -> 111 us
  blocking collectives: 81.2 us -> 12.2 us
  matrix products: 63.2 us -> 0 us
  local copies, waits for them, and re-layouts: 6.23 us -> 46.7 us
  starting transfers between devices: 14 us -> 25.5 us
  waiting for transfers between devices: 176 us -> 180 us
    pallas_call x0 -> x7, Pallas kernels: none -> 111 us  [the longest x4 107 us: expert_section(): pl.pallas_call(functools.partial(expert_kernel, capacity, steps), grid=(2...]
    all_to_all x2 -> x0, blocking collectives: 81.2 us -> none  [the longest x1 41.3 us: on_device(): lax.all_to_all(routed, 'seq', split_axis=1, concat_axis=1, tiled=True)]
    all_gather x1 -> x4, waiting for transfers between devices: 70.8 us -> 0.07 us  [on_device(): gathered = lax.all_gather(part, 'exp', axis=0)]
    dot_general x8 -> x0, matrix products: 63.2 us -> none  [the longest x1 40.6 us: on_device(): jnp.einsum('sjcf,jfd->dsjc', hidden_act, down_weight, preferred_element_t...]
    reduce_scatter x1 -> x4, waiting for transfers between devices: 86.2 us -> 134 us  [on_device(): share = lax.psum_scatter(partial, 'exp', scatter_dimension=0)]
    unnamed x16 -> x24, local copies, waits for them, and re-layouts: 2.78 us -> 45.8 us
    ppermute x3 -> x8, waiting for transfers between devices: 18.6 us -> 44.5 us  [shifted(): return lax.ppermute(array, axis, pairs)]
    all_gather x0 -> x1, blocking collectives: none -> 12.2 us  [on_device(): all_ids = lax.all_gather(expert_ids.T, 'seq', axis=0)]
  transfers between devices with their start and end apart: 5 -> 16, of which waited for: 5 -> 8; matrix products, arithmetic and copies ran while one was open for 3% -> 10% of each run, Pallas kernels for 0% -> 28%
where the time goes in v1:
time: 393 us; the launch traced here: 392 us
  waiting for transfers between devices  180 us (46%)
  Pallas kernels  111 us (28%)
  local copies, waits for them, and re-layouts  46.7 us (12%)
  starting transfers between devices  25.5 us (6%)
  between operations  13.7 us (3%)
  blocking collectives  12.2 us (3%)
    reduce_scatter x4, waiting for transfers between devices, on_device(): share = lax.psum_scatter(partial, 'exp', scatter_dimension=0)  134 us
    pallas_call x4, Pallas kernels, expert_section(): pl.pallas_call(functools.partial(expert_kernel, capacity, steps), grid=(2...  107 us
    unnamed x24, local copies, waits for them, and re-layouts  45.8 us
    ppermute x8, waiting for transfers between devices, shifted(): return lax.ppermute(array, axis, pairs)  44.5 us
    ppermute x8, starting transfers between devices, shifted(): return lax.ppermute(array, axis, pairs)  25 us
    all_gather x1, blocking collectives, on_device(): all_ids = lax.all_gather(expert_ids.T, 'seq', axis=0)  12.2 us
  transfers between devices with their start and end apart: 16, of which 8 were waited for; matrix products, arithmetic and copies ran while one was open for 10% of the time, Pallas kernels for 28%

profile of v1, /device:TPU:0, one launch (start us, length us, event | category | flops | bytes accessed | tf_op | source)
XLA Modules:
  0.0 391.5 jit_solution(12759585420475484260)
XLA Ops:
  6.5 0.0 all-gather.13.cloned.1.call-start
  6.5 1.0 copy-done
  7.5 1.0 copy-done.1
  8.5 0.7 copy-done.6
  9.2 1.0 shard_map.109
  10.3 4.9 %collective-permute-start = (bf16[784,128]{1,0:T(8,128)(2,1)S(1)}, bf16[784,128]{1,0:T(8,128)(2,1)S(1)}, u32[]{:S(2)}, u32[]{:S(2)}) collective-permute-start(bf16[784,128]{1,0:T(8,128)(2,1)S(1)} %get-tuple-element.8), channel_id=1, source_target_pairs={{0,8},{8,16},{16,24},{1,9},{9,17},{17,25},{2,10},{10,18},{18,26},{... | collective-permute-start | bytes 602120 | tf_op jit(solution)/shard_map/ppermute | solution.py:28
  15.2 0.7 reshape.30.gain_ref
  15.9 1.0 copy-done.2
  16.9 1.4 shard_map.110.intra_ref
  18.3 1.1 collective-permute-done
  19.5 0.1 fusion.6
  19.5 0.2 concatenate.3
  19.7 5.4 %collective-permute-start.1 = (bf16[784,128]{1,0:T(8,128)(2,1)S(1)}, bf16[784,128]{1,0:T(8,128)(2,1)S(1)}, u32[]{:S(2)}, u32[]{:S(2)}) collective-permute-start(bf16[784,128]{1,0:T(8,128)(2,1)S(1)} %concatenate.3), channel_id=1, source_target_pairs={{0,16},{8,24},{1,17},{9,25},{2,18},{10,26},{3,19},{11,27},{4,20},{... | collective-permute-start | bytes 602120 | tf_op jit(solution)/shard_map/ppermute | solution.py:28
  25.2 3.4 collective-permute-done.1
  28.6 0.0 copy-done.3
  28.6 0.0 copy-done.5
  28.6 1.6 shard_map.111
  30.2 5.7 %collective-permute-start.2 = (bf16[256,768]{1,0:T(8,128)(2,1)}, bf16[256,768]{1,0:T(8,128)(2,1)S(1)}, u32[]{:S(2)}, u32[]{:S(2)}) collective-permute-start(bf16[256,768]{1,0:T(8,128)(2,1)} %shard_map.111), channel_id=1, source_target_pairs={{0,8},{8,16},{16,24},{24,0},{1,9},{9,17},{17,25},{25,1},{2,10},{10... | collective-permute-start | bytes 1179656 | tf_op jit(solution)/shard_map/ppermute | solution.py:28
  35.9 12.3 %collective-permute-done.2 = bf16[256,768]{1,0:T(8,128)(2,1)S(1)} collective-permute-done((bf16[256,768]{1,0:T(8,128)(2,1)}, bf16[256,768]{1,0:T(8,128)(2,1)S(1)}, u32[]{:S(2)}, u32[]{:S(2)}) %collective-permute-start.2) | collective-permute-done | bytes 393248 | tf_op jit(solution)/shard_map/ppermute | solution.py:28
  48.3 0.8 copy-done.7
  49.0 0.0 all-gather.13.cloned.1.call-update
  49.0 0.0 all-gather.15.cloned.1.call-start
  49.1 0.1 collective-permute-start.4
  49.2 18.8 %collective-permute-done.4 = bf16[256,768]{1,0:T(8,128)(2,1)S(1)} collective-permute-done((bf16[256,768]{1,0:T(8,128)(2,1)}, bf16[256,768]{1,0:T(8,128)(2,1)S(1)}, u32[]{:S(2)}, u32[]{:S(2)}) %collective-permute-start.4) | collective-permute-done | bytes 393248 | tf_op jit(solution)/shard_map/ppermute | solution.py:28
  68.0 0.7 copy-done.8
  68.7 0.0 all-gather.15.cloned.1.call-update
  68.7 0.0 all-gather.17.cloned.1.call-start
  68.8 2.5 collective-permute-start.6
  71.2 8.9 %collective-permute-done.6 = bf16[256,768]{1,0:T(8,128)(2,1)S(1)} collective-permute-done((bf16[256,768]{1,0:T(8,128)(2,1)}, bf16[256,768]{1,0:T(8,128)(2,1)S(1)}, u32[]{:S(2)}, u32[]{:S(2)}) %collective-permute-start.6) | collective-permute-done | bytes 393248 | tf_op jit(solution)/shard_map/ppermute | solution.py:28
  80.1 0.7 copy-done.9
  80.9 0.0 all-gather.17.cloned.1.call-update
  80.9 0.0 all-gather.11.cloned.1.call-start
  80.9 0.5 all-gather.11.cloned.1.call-update
  81.5 0.0 reduce-scatter.7.cloned.1.call-start
  81.6 20.0 %copy.20.gate_ref = bf16[2,6144,576]{2,1,0:T(8,128)(2,1)} copy(bf16[2,6144,576]{1,2,0:T(8,128)(2,1)} %param.19) | data formatting | bytes 28311552 | tf_op args[8]
  101.6 19.9 %copy.21.up_ref = bf16[2,6144,576]{2,1,0:T(8,128)(2,1)} copy(bf16[2,6144,576]{1,2,0:T(8,128)(2,1)} %param.20) | data formatting | bytes 28311552 | tf_op args[9]
  121.5 0.0 copy-done.10
  121.5 12.2 %all-gather.5 = s32[4,2,256]{2,1,0:T(2,128)S(1)} all-gather(s32[1,2,256]{2,1,0:T(2,128)S(1)} %bitcast.44), channel_id=2, replica_groups=mesh['seq'=4,'exp'=8] {'seq'}, dimensions={0}, use_global_device_ids=true | all-gather | bytes 10240 | tf_op jit(solution)/shard_map/all_gather | solution.py:295
  133.7 0.0 all-gather.13.cloned.1.call-done
  133.8 26.7 %shard_map.113 = bf16[8,256,768]{2,1,0:T(8,128)(2,1)} custom-call(s32[1]{0:T(128)} %bitcast.3.first_ref, s32[2,256]{1,0:T(2,128)S(1)} %get-tuple-element.13.ids_ref, bf16[8,256,768]{2,1,0:T(8,128)(2,1)} %bitcast.39, bf16[8,2,768]{2,1,0:T(2,128)(2,1)S(1)} %bitcast.34, bf16[2,6144,576]{2,1,0:T(8,128)(2,1)} %copy.20.gate_ref, ...), custom_call_target="tpu_custom_call" | custom-call | flops 5435817984 | bytes 42467328 | tf_op jit(solution)/shard_map/pallas_call | solution.py:242
  160.4 0.0 reduce-scatter.7.cloned.1.call-update
  160.4 0.0 reduce-scatter.9.cloned.1.call-start
  160.5 0.0 all-gather.15.cloned.1.call-done
  160.5 26.8 %shard_map.114 = bf16[8,256,768]{2,1,0:T(8,128)(2,1)} custom-call(s32[1]{0:T(128)} %bitcast.3.first_ref, s32[2,256]{1,0:T(2,128)S(1)} %get-tuple-element.15.ids_ref, bf16[8,256,768]{2,1,0:T(8,128)(2,1)} %bitcast.40, bf16[8,2,768]{2,1,0:T(2,128)(2,1)S(1)} %bitcast.35, bf16[2,6144,576]{2,1,0:T(8,128)(2,1)} %copy.20.gate_ref, ...), custom_call_target="tpu_custom_call" | custom-call | flops 5435817984 | bytes 42467328 | tf_op jit(solution)/shard_map/pallas_call | solution.py:242
  187.3 0.0 reduce-scatter.9.cloned.1.call-update
  187.3 0.0 reduce-scatter.11.cloned.1.call-start
  187.4 0.0 all-gather.17.cloned.1.call-done
  187.4 27.2 %shard_map.115 = bf16[8,256,768]{2,1,0:T(8,128)(2,1)} custom-call(s32[1]{0:T(128)} %bitcast.3.first_ref, s32[2,256]{1,0:T(2,128)S(1)} %get-tuple-element.14.ids_ref, bf16[8,256,768]{2,1,0:T(8,128)(2,1)} %bitcast.41, bf16[8,2,768]{2,1,0:T(2,128)(2,1)S(1)} %bitcast.36, bf16[2,6144,576]{2,1,0:T(8,128)(2,1)} %copy.20.gate_ref, ...), custom_call_target="tpu_custom_call" | custom-call | flops 5435817984 | bytes 42467328 | tf_op jit(solution)/shard_map/pallas_call | solution.py:242
  214.6 0.0 reduce-scatter.11.cloned.1.call-update
  214.6 0.2 reduce-scatter.5.cloned.1.call-start
  214.8 0.0 all-gather.11.cloned.1.call-done
  214.9 26.8 %shard_map.112 = bf16[8,256,768]{2,1,0:T(8,128)(2,1)} custom-call(s32[1]{0:T(128)} %bitcast.3.first_ref, s32[2,256]{1,0:T(2,128)S(1)} %get-tuple-element.12.ids_ref, bf16[8,256,768]{2,1,0:T(8,128)(2,1)} %bitcast.38, bf16[8,2,768]{2,1,0:T(2,128)(2,1)S(1)} %bitcast.37, bf16[2,6144,576]{2,1,0:T(8,128)(2,1)} %copy.20.gate_ref, ...), custom_call_target="tpu_custom_call" | custom-call | flops 5435817984 | bytes 42467328 | tf_op jit(solution)/shard_map/pallas_call | solution.py:242
  241.7 0.0 reduce-scatter.5.cloned.1.call-update
  241.7 0.0 reduce-scatter.7.cloned.1.call-done
  241.7 2.5 collective-permute-start.3
  244.3 38.6 %reduce-scatter.9.cloned.1.call-done = bf16[1,256,768]{2,1,0:T(8,128)(2,1)} async-done(((bf16[8,256,768]{2,1,0:T(8,128)(2,1)}), bf16[1,256,768]{2,1,0:T(8,128)(2,1)}) %reduce-scatter.9.cloned.1.call-update) | async-done | bytes 393232 | tf_op jit(solution)/shard_map/reduce_scatter | solution.py:309
  282.9 2.4 collective-permute-start.5
  285.3 47.2 %reduce-scatter.11.cloned.1.call-done = bf16[1,256,768]{2,1,0:T(8,128)(2,1)} async-done(((bf16[8,256,768]{2,1,0:T(8,128)(2,1)}), bf16[1,256,768]{2,1,0:T(8,128)(2,1)}) %reduce-scatter.11.cloned.1.call-update) | async-done | bytes 393232 | tf_op jit(solution)/shard_map/reduce_scatter | solution.py:309
  332.5 1.5 collective-permute-start.7
  334.0 48.5 %reduce-scatter.5.cloned.1.call-done = bf16[1,256,768]{2,1,0:T(8,128)(2,1)} async-done(((bf16[8,256,768]{2,1,0:T(8,128)(2,1)}), bf16[1,256,768]{2,1,0:T(8,128)(2,1)}) %reduce-scatter.5.cloned.1.call-update) | async-done | bytes 393232 | tf_op jit(solution)/shard_map/reduce_scatter | solution.py:309
  382.5 0.0 collective-permute-done.3
  382.5 0.0 collective-permute-done.5
  382.6 0.0 collective-permute-done.7
  382.6 2.1 fusion.3
  (21 shorter events, 0.1 us)
Async XLA Ops:
  6.5 127.2 %all-gather.13.cloned.1.call-start = ((), (), s32[]{:S(2)}) async-start(), calls=%async_computation.9 | async-start | bytes 3538944 | tf_op jit(solution)/shard_map/all_gather | solution.py:305
  6.5 1.0 copy-start
  7.5 1.0 copy-start.1
  8.5 0.7 copy-start.6
  9.2 19.4 %copy-start.3 = (bf16[256,768]{1,0:T(8,128)(2,1)S(1)}, bf16[256,768]{1,0:T(8,128)(2,1)}, u32[]{:S(2)}) copy-start(bf16[256,768]{1,0:T(8,128)(2,1)} %query_ref.3) | copy-start | bytes 1179652
  9.2 19.4 %copy-start.5 = (bf16[256,768]{1,0:T(8,128)(2,1)S(1)}, bf16[256,768]{1,0:T(8,128)(2,1)}, u32[]{:S(2)}) copy-start(bf16[256,768]{1,0:T(8,128)(2,1)} %residual_ref.1) | copy-start | bytes 1179652
  10.3 9.2 %collective-permute-start = (bf16[784,128]{1,0:T(8,128)(2,1)S(1)}, bf16[784,128]{1,0:T(8,128)(2,1)S(1)}, u32[]{:S(2)}, u32[]{:S(2)}) collective-permute-start(bf16[784,128]{1,0:T(8,128)(2,1)S(1)} %get-tuple-element.8), channel_id=1, source_target_pairs={{0,8},{8,16},{16,24},{1,9},{9,17},{17,25},{2,10},{10,18},{18,26},{... | collective-permute-start | bytes 602120 | tf_op jit(solution)/shard_map/ppermute | solution.py:28
  15.9 1.0 copy-start.2
  19.7 8.8 %collective-permute-start.1 = (bf16[784,128]{1,0:T(8,128)(2,1)S(1)}, bf16[784,128]{1,0:T(8,128)(2,1)S(1)}, u32[]{:S(2)}, u32[]{:S(2)}) collective-permute-start(bf16[784,128]{1,0:T(8,128)(2,1)S(1)} %concatenate.3), channel_id=1, source_target_pairs={{0,16},{8,24},{1,17},{9,25},{2,18},{10,26},{3,19},{11,27},{4,20},{... | collective-permute-start | bytes 602120 | tf_op jit(solution)/shard_map/ppermute | solution.py:28
  30.2 18.0 %collective-permute-start.2 = (bf16[256,768]{1,0:T(8,128)(2,1)}, bf16[256,768]{1,0:T(8,128)(2,1)S(1)}, u32[]{:S(2)}, u32[]{:S(2)}) collective-permute-start(bf16[256,768]{1,0:T(8,128)(2,1)} %shard_map.111), channel_id=1, source_target_pairs={{0,8},{8,16},{16,24},{24,0},{1,9},{9,17},{17,25},{25,1},{2,10},{10... | collective-permute-start | bytes 1179656 | tf_op jit(solution)/shard_map/ppermute | solution.py:28
  48.3 0.8 copy-start.7
  49.0 111.5 %all-gather.15.cloned.1.call-start = ((), (), s32[]{:S(2)}) async-start(), calls=%async_computation.10 | async-start | bytes 3538944 | tf_op jit(solution)/shard_map/all_gather | solution.py:305
  49.1 18.9 %collective-permute-start.4 = (bf16[256,768]{1,0:T(8,128)(2,1)}, bf16[256,768]{1,0:T(8,128)(2,1)S(1)}, u32[]{:S(2)}, u32[]{:S(2)}) collective-permute-start(bf16[256,768]{1,0:T(8,128)(2,1)} %shard_map.111), channel_id=1, source_target_pairs={{0,16},{8,24},{16,0},{24,8},{1,17},{9,25},{17,1},{25,9},{2,18},{10... | collective-permute-start | bytes 1179656 | tf_op jit(solution)/shard_map/ppermute | solution.py:28
  68.0 0.7 copy-start.8
  68.7 118.6 %all-gather.17.cloned.1.call-start = ((), (), s32[]{:S(2)}) async-start(), calls=%async_computation.11 | async-start | bytes 3538944 | tf_op jit(solution)/shard_map/all_gather | solution.py:305
  68.8 11.3 %collective-permute-start.6 = (bf16[256,768]{1,0:T(8,128)(2,1)}, bf16[256,768]{1,0:T(8,128)(2,1)S(1)}, u32[]{:S(2)}, u32[]{:S(2)}) collective-permute-start(bf16[256,768]{1,0:T(8,128)(2,1)} %shard_map.111), channel_id=1, source_target_pairs={{0,24},{8,0},{16,8},{24,16},{1,25},{9,1},{17,9},{25,17},{2,26},{10... | collective-permute-start | bytes 1179656 | tf_op jit(solution)/shard_map/ppermute | solution.py:28
  80.1 0.7 copy-start.9
  80.9 134.0 %all-gather.11.cloned.1.call-start = ((), (), s32[]{:S(2)}) async-start(), calls=%async_computation.8 | async-start | bytes 3538944 | tf_op jit(solution)/shard_map/all_gather | solution.py:305
  81.5 160.3 %reduce-scatter.7.cloned.1.call-start = ((), (), s32[]{:S(2)}) async-start(), calls=%async_computation.5 | async-start | bytes 3538944 | tf_op jit(solution)/shard_map/reduce_scatter | solution.py:309
  101.6 19.9 %copy-start.10 = (s32[256,2]{0,1:T(2,128)S(1)}, s32[256,2]{0,1:T(2,128)}, u32[]{:S(2)}) copy-start(s32[256,2]{0,1:T(2,128)} %param.17) | copy-start | bytes 6148
  101.6 32.2 %copy-start.4 = (bf16[6144,2]{0,1:T(2,128)(2,1)S(1)}, bf16[6144,2]{0,1:T(2,128)(2,1)}, u32[]{:S(2)}) copy-start(bf16[6144,2]{0,1:T(2,128)(2,1)} %param.18) | copy-start | bytes 73732
  160.4 122.4 %reduce-scatter.9.cloned.1.call-start = ((), (), s32[]{:S(2)}) async-start(), calls=%async_computation.6 | async-start | bytes 3538944 | tf_op jit(solution)/shard_map/reduce_scatter | solution.py:309
  187.3 145.2 %reduce-scatter.11.cloned.1.call-start = ((), (), s32[]{:S(2)}) async-start(), calls=%async_computation.7 | async-start | bytes 3538944 | tf_op jit(solution)/shard_map/reduce_scatter | solution.py:309
  214.6 167.9 %reduce-scatter.5.cloned.1.call-start = ((), (), s32[]{:S(2)}) async-start(), calls=%async_computation.4 | async-start | bytes 3538944 | tf_op jit(solution)/shard_map/reduce_scatter | solution.py:309
  241.7 140.8 %collective-permute-start.3 = (bf16[256,768]{1,0:T(8,128)(2,1)}, bf16[256,768]{1,0:T(8,128)(2,1)S(1)}, u32[]{:S(2)}, u32[]{:S(2)}) collective-permute-start(bf16[256,768]{1,0:T(8,128)(2,1)} %bitcast.45), channel_id=1, source_target_pairs={{0,24},{8,0},{16,8},{24,16},{1,25},{9,1},{17,9},{25,17},{2,26},{10... | collective-permute-start | bytes 1179656 | tf_op jit(solution)/shard_map/ppermute | solution.py:28
  282.9 99.7 %collective-permute-start.5 = (bf16[256,768]{1,0:T(8,128)(2,1)}, bf16[256,768]{1,0:T(8,128)(2,1)S(1)}, u32[]{:S(2)}, u32[]{:S(2)}) collective-permute-start(bf16[256,768]{1,0:T(8,128)(2,1)} %bitcast.46), channel_id=1, source_target_pairs={{0,16},{8,24},{16,0},{24,8},{1,17},{9,25},{17,1},{25,9},{2,18},{10... | collective-permute-start | bytes 1179656 | tf_op jit(solution)/shard_map/ppermute | solution.py:28
  332.5 50.0 %collective-permute-start.7 = (bf16[256,768]{1,0:T(8,128)(2,1)}, bf16[256,768]{1,0:T(8,128)(2,1)S(1)}, u32[]{:S(2)}, u32[]{:S(2)}) collective-permute-start(bf16[256,768]{1,0:T(8,128)(2,1)} %bitcast.47), channel_id=1, source_target_pairs={{0,8},{8,16},{16,24},{24,0},{1,9},{9,17},{17,25},{25,1},{2,10},{10... | collective-permute-start | bytes 1179656 | tf_op jit(solution)/shard_map/ppermute | solution.py:28
Sparse Core Ops, SparseCore 0:
  49.2 31.6 all-gather.12
  82.8 32.3 all-gather.14
  117.0 32.3 all-gather.16
  151.1 32.3 all-gather.10
  186.7 46.2 reduce-scatter.6
  236.6 46.2 reduce-scatter.8
  286.3 46.2 reduce-scatter.10
  336.3 46.2 reduce-scatter.4

commit v2 on v1

--- a/solution.py
+++ b/solution.py
@@ -10,7 +10,7 @@
 F32 = jnp.float32
 BF16 = jnp.bfloat16
 HIGHEST = lax.Precision.HIGHEST
-VMEM_LIMIT = 48 * 1024 * 1024
+VMEM_LIMIT = 40 * 1024 * 1024
 
 
 def lower_ones(length):
@@ -19,12 +19,9 @@
     return rows >= columns
 
 
-def shifted(array, axis, by, wrap=False):
+def shifted(array, axis, by):
     count = lax.axis_size(axis)
-    if wrap:
-        pairs = [(i, (i + by) % count) for i in range(count)]
-    else:
-        pairs = [(i, i + by) for i in range(count) if 0 <= i + by < count]
+    pairs = [(i, i + by) for i in range(count) if 0 <= i + by < count]
     return lax.ppermute(array, axis, pairs)
 
 
@@ -174,99 +171,171 @@
     return incoming
 
 
-def expert_kernel(
-    capacity, steps, first_ref, ids_ref, x_ref, router_ref, gate_ref, up_ref, down_ref, out_ref,
-    gate_acc, up_acc, score_acc, place, hidden,
-):
+def gate_kernel(counts, last, plan_ref, ids_ref, *refs):
     step = pl.program_id(0)
+    blocks = sum(counts)
+    x_refs, refs = refs[: len(counts)], refs[len(counts) :]
+    router_ref, gate_ref, up_ref = refs[:3]
+    refs = refs[3:]
+    if last:
+        gate_in, up_in, score_in, hidden_ref, gate_acc, up_acc, score_acc = refs
+    else:
+        gate_acc, up_acc, score_acc = refs
     experts = gate_ref.shape[0]
-    length = x_ref.shape[1]
 
     @pl.when(step == 0)
     def _():
-        tokens_before = lower_ones(length)
-        slot = lax.broadcasted_iota(jnp.int32, (capacity, length), 0)
-        for j in range(experts):
-            chosen = ids_ref[0:1, :] == first_ref[0] + j
-            for choice in range(1, ids_ref.shape[0]):
-                chosen = chosen | (ids_ref[choice : choice + 1, :] == first_ref[0] + j)
-            flag = jnp.where(chosen, 1.0, 0.0)
-            rank = lax.dot_general(
-                jnp.broadcast_to(flag, (8, length)).astype(BF16),
-                tokens_before.astype(BF16),
-                (((1,), (1,)), ((), ())),
-                preferred_element_type=F32,
-            )[0:1, :]
-            here = (rank.astype(jnp.int32) - 1 == slot) & (flag > 0.5)
-            place[j * capacity : (j + 1) * capacity, :] = jnp.where(here, 1.0, 0.0).astype(BF16)
-        gate_acc[...] = jnp.zeros_like(gate_acc)
-        up_acc[...] = jnp.zeros_like(up_acc)
-        score_acc[...] = jnp.zeros_like(score_acc)
-
-    @pl.when(step < steps)
-    def _():
-        rows = jnp.dot(place[...], x_ref[0], preferred_element_type=F32).astype(BF16)
-        score_acc[...] += lax.dot_general(
-            rows, router_ref[0], (((1,), (1,)), ((), ())), preferred_element_type=F32
+        if last:
+            gate_acc[...] = gate_in[...]
+            up_acc[...] = up_in[...]
+            score_acc[...] = score_in[...]
+        else:
+            gate_acc[...] = jnp.zeros_like(gate_acc)
+            up_acc[...] = jnp.zeros_like(up_acc)
+            score_acc[...] = jnp.zeros_like(score_acc)
+
+    x = x_refs[-1][0]
+    for i in range(len(counts) - 2, -1, -1):
+        x = jnp.where(step < sum(counts[: i + 1]), x_refs[i][0], x)
+    across = (((1,), (1,)), ((), ()))
+    score_acc[...] += lax.dot_general(router_ref[0], x, across, preferred_element_type=F32)
+    for j in range(experts):
+        gate_acc[j] += lax.dot_general(gate_ref[j], x, across, preferred_element_type=F32)
+        up_acc[j] += lax.dot_general(up_ref[j], x, across, preferred_element_type=F32)
+
+    if last:
+
+        @pl.when(step == blocks - 1)
+        def _():
+            parts = []
+            for j in range(experts):
+                chosen = ids_ref[0:1, :] == plan_ref[blocks] + j
+                for choice in range(1, ids_ref.shape[0]):
+                    chosen = chosen | (ids_ref[choice : choice + 1, :] == plan_ref[blocks] + j)
+                gate = gate_acc[j]
+                routed = gate / (1.0 + jnp.exp(-gate)) * up_acc[j]
+                routed = routed / (1.0 + jnp.exp(-score_acc[j : j + 1, :]))
+                parts.append(jnp.where(chosen, routed, 0.0))
+            hidden_ref[...] = jnp.concatenate(parts, axis=0).T.astype(BF16)
+
+
+def gate_part(plan, ids, xs, router_rows, gate_rows, up_rows, sums=None):
+    counts = tuple(x.shape[0] for x in xs)
+    blocks = sum(counts)
+    _, length, width = xs[0].shape
+    experts, units, _ = gate_rows.shape
+    whole = pl.BlockSpec(memory_space=pltpu.VMEM)
+    last = sums is not None
+
+    def x_spec(i):
+        before = sum(counts[:i])
+        return pl.BlockSpec(
+            (1, length, width), lambda p, plan: (jnp.clip(p - before, 0, counts[i] - 1), 0, 0)
         )
-        for j in range(experts):
-            mine = slice(j * capacity, (j + 1) * capacity)
-            gate_acc[mine, :] += jnp.dot(rows[mine], gate_ref[j], preferred_element_type=F32)
-            up_acc[mine, :] += jnp.dot(rows[mine], up_ref[j], preferred_element_type=F32)
-
-    @pl.when(step == steps - 1)
-    def _():
-        gate = gate_acc[...]
-        hidden[...] = (gate / (1.0 + jnp.exp(-gate)) * up_acc[...]).astype(BF16)
-
-    @pl.when(step >= steps)
-    def _():
-        parts = []
-        for j in range(experts):
-            mine = slice(j * capacity, (j + 1) * capacity)
-            share = jnp.dot(hidden[mine, :], down_ref[j], preferred_element_type=F32)
-            score = score_acc[mine, j : j + 1]
-            parts.append((share / (1.0 + jnp.exp(-score))).astype(BF16))
-        routed = jnp.concatenate(parts, axis=0)
-        out_ref[0] = lax.dot_general(
-            place[...], routed, (((0,), (0,)), ((), ())), preferred_element_type=F32
-        ).astype(BF16)
-
-
-def expert_section(first, ids, x, router_rows, gate_weight, up_weight, down_weight, capacity):
-    steps, length, width = x.shape
-    experts, _, units = gate_weight.shape
-    slots = experts * capacity
-    early = lambda i: jnp.minimum(i, steps - 1)
-    late = lambda i: jnp.maximum(i - steps, 0)
+
+    weight_spec = pl.BlockSpec((experts, units, width), lambda p, plan: (0, 0, plan[p]))
+    sum_shapes = [(experts, units, length), (experts, units, length), (experts, length)]
+    if last:
+        out_shape = jax.ShapeDtypeStruct((length, experts * units), BF16)
+        out_specs = whole
+        scratch = [pltpu.VMEM(shape, F32) for shape in sum_shapes]
+    else:
+        out_shape = tuple(jax.ShapeDtypeStruct(shape, F32) for shape in sum_shapes)
+        out_specs = (whole, whole, whole)
+        scratch = []
     return pl.pallas_call(
-        functools.partial(expert_kernel, capacity, steps),
-        grid=(2 * steps,),
-        in_specs=[
-            pl.BlockSpec(memory_space=pltpu.SMEM),
-            pl.BlockSpec(ids.shape, lambda i: (0, 0)),
-            pl.BlockSpec((1, length, width), lambda i: (early(i), 0, 0)),
-            pl.BlockSpec((1, experts, width), lambda i: (early(i), 0, 0)),
-            pl.BlockSpec((experts, width, units), lambda i: (0, early(i), 0)),
-            pl.BlockSpec((experts, width, units), lambda i: (0, early(i), 0)),
-            pl.BlockSpec((experts, units, width), lambda i: (0, 0, late(i))),
-        ],
-        out_specs=pl.BlockSpec((1, length, width), lambda i: (late(i), 0, 0)),
-        out_shape=jax.ShapeDtypeStruct((steps, length, width), BF16),
-        scratch_shapes=[
-            pltpu.VMEM((slots, units), F32),
-            pltpu.VMEM((slots, units), F32),
-            pltpu.VMEM((slots, experts), F32),
-            pltpu.VMEM((slots, length), BF16),
-            pltpu.VMEM((slots, units), BF16),
-        ],
+        functools.partial(gate_kernel, counts, last),
+        grid_spec=pltpu.PrefetchScalarGridSpec(
+            num_scalar_prefetch=1,
+            grid=(blocks,),
+            in_specs=[
+                whole,
+                *[x_spec(i) for i in range(len(counts))],
+                pl.BlockSpec((1, experts, width), lambda p, plan: (plan[p], 0, 0)),
+                weight_spec,
+                weight_spec,
+                *([whole] * 3 if last else []),
+            ],
+            out_specs=out_specs,
+            scratch_shapes=scratch,
+        ),
+        out_shape=out_shape,
         cost_estimate=pl.CostEstimate(
-            flops=6 * slots * steps * width * units,
-            bytes_accessed=6 * experts * steps * width * units,
+            flops=4 * experts * length * blocks * width * units,
+            bytes_accessed=4 * experts * blocks * width * units,
             transcendentals=0,
         ),
         compiler_params=pltpu.CompilerParams(vmem_limit_bytes=VMEM_LIMIT),
-    )(first, ids, x, router_rows, gate_weight, up_weight, down_weight)
+    )(plan, ids, *xs, router_rows, gate_rows, up_rows, *(sums if last else ()))
+
+
+def down_kernel(plan_ref, hidden_ref, down_ref, out_ref):
+    experts, units, width = down_ref.shape
+    out_ref[0] = jnp.dot(
+        hidden_ref[...], down_ref[...].reshape(experts * units, width), preferred_element_type=F32
+    ).astype(BF16)
+
+
+def down_part(plan, hidden, down_weight, width):
+    blocks = plan.shape[0]
+    length = hidden.shape[0]
+    experts, units, _ = down_weight.shape
+    return pl.pallas_call(
+        down_kernel,
+        grid_spec=pltpu.PrefetchScalarGridSpec(
+            num_scalar_prefetch=1,
+            grid=(blocks,),
+            in_specs=[
+                pl.BlockSpec(memory_space=pltpu.VMEM),
+                pl.BlockSpec((experts, units, width), lambda p, plan: (0, 0, plan[p])),
+            ],
+            out_specs=pl.BlockSpec((1, length, width), lambda p, plan: (p, 0, 0)),
+        ),
+        out_shape=jax.ShapeDtypeStruct((blocks, length, width), BF16),
+        cost_estimate=pl.CostEstimate(
+            flops=2 * experts * length * blocks * width * units,
+            bytes_accessed=2 * experts * blocks * width * units,
+            transcendentals=0,
+        ),
+        compiler_params=pltpu.CompilerParams(vmem_limit_bytes=VMEM_LIMIT),
+    )(plan, hidden, down_weight)
+
+
+def added(left, right):
+    return (left.astype(F32) + right.astype(F32)).astype(BF16)
+
+
+def swapped(array, axis, even, odd):
+    count = lax.axis_size(axis)
+    pairs = [(i, i ^ (odd if i % 2 else even)) for i in range(count)]
+    return lax.ppermute(array, axis, pairs)
+
+
+class PairedPlane:
+    def __init__(self):
+        me = lax.axis_index("exp").astype(jnp.int32)
+        other = me ^ 1
+        near = jnp.where(me % 2 == 0, 2, 4)
+        far = 6 - near
+        self.early = jnp.stack([me, me ^ near, other, other ^ far])
+        self.late = jnp.stack([me ^ far, me ^ 6, other ^ near, other ^ 6])
+        self.mine = jnp.stack([me, me ^ near, me ^ far, me ^ 6])
+        self.theirs = jnp.stack([other, other ^ far, other ^ near, other ^ 6])
+
+    def first(self, part):
+        return jnp.stack([part, swapped(part, "exp", 2, 4)])
+
+    def second(self, two):
+        return swapped(two, "exp", 4, 2)
+
+    def across(self, two):
+        return swapped(two, "exp", 1, 1)
+
+    def scatter(self, mine, theirs):
+        got = swapped(theirs, "exp", 1, 1)
+        got_two = swapped(added(mine[2:], got[2:]), "exp", 4, 2)
+        got_one = swapped(added(added(mine[1], got[1]), got_two[1]), "exp", 2, 4)
+        return added(added(added(mine[0], got[0]), got_two[0]), got_one), got, got_two
 
 
 def on_device(
@@ -287,29 +356,74 @@
     shares = lax.axis_size("exp")
     width = attn_query.shape[1]
     experts_here = router_weight.shape[1]
-    capacity = 4 * length // (experts_here * groups)
-    section = lax.axis_index("seq")
-    first = (section * experts_here).astype(jnp.int32).reshape(1)
+    base = (lax.axis_index("seq") * experts_here).astype(jnp.int32).reshape(1)
     router_rows = router_weight.reshape(shares, width, experts_here).transpose(0, 2, 1)
-
-    all_ids = lax.all_gather(expert_ids.T, "seq", axis=0)
+    gate_rows = gate_weight.swapaxes(1, 2)
+    up_rows = up_weight.swapaxes(1, 2)
+
+    ids = expert_ids.T[None]
+    distance = 1
+    while distance < groups:
+        ids = jnp.concatenate([ids, swapped(ids, "seq", distance, distance)])
+        distance *= 2
+
     message, cumulative = section_state(attn_key, attn_value, log_decay)
     intra = intra_section(attn_query, attn_key, attn_value, log_decay, cumulative)
     incoming = incoming_state(message, heads_here)
+    incoming, ids = lax.optimization_barrier((incoming, ids))
     stream = make_stream(attn_query, intra, cumulative, incoming, residual, norm_gain)
 
+    half = groups // 2
+    chunks = [(i, i + half) for i in range(half)]
+    parts = {0: stream}
+    parts[half] = swapped(stream, "seq", half, half)
+    later, _ = lax.optimization_barrier((stream, parts[half]))
+    for i in range(1, half):
+        for offset in chunks[i]:
+            parts[offset] = swapped(later, "seq", offset, offset)
+
     total = stream.astype(F32)
-    for offset in range(groups):
-        part = stream if offset == 0 else shifted(stream, "seq", offset, wrap=True)
-        ids = lax.dynamic_index_in_dim(all_ids, (section - offset) % groups, 0, keepdims=False)
-        gathered = lax.all_gather(part, "exp", axis=0)
-        partial = expert_section(
-            first, ids, gathered, router_rows, gate_weight, up_weight, down_weight, capacity
-        )
-        share = lax.psum_scatter(partial, "exp", scatter_dimension=0)
-        if offset:
-            share = shifted(share, "seq", -offset, wrap=True)
-        total = total + share.astype(F32)
+    plane = PairedPlane() if shares == 8 else None
+    links_free, core_free, sum_free = None, None, None
+    for chunk in chunks:
+        part = jnp.concatenate([parts[offset] for offset in chunk])
+        chunk_ids = jnp.concatenate([ids[offset] for offset in chunk], axis=1)
+        weights = (router_rows, gate_rows, up_rows)
+        if plane:
+            if links_free is not None:
+                part, _ = lax.optimization_barrier((part, links_free))
+            two = plane.first(part)
+            far_two = plane.second(two)
+            links_free = far_two
+            near_two = plane.across(two)
+            if core_free is not None:
+                near_two, _ = lax.optimization_barrier((near_two, core_free))
+            plan = jnp.concatenate([plane.early, base])
+            sums = gate_part(plan, chunk_ids, [two, near_two], *weights)
+            far_two, sums = lax.optimization_barrier((far_two, sums))
+            plan = jnp.concatenate([plane.late, base])
+            hidden = gate_part(plan, chunk_ids, [far_two, plane.across(far_two)], *weights, sums)
+            if sum_free is not None:
+                hidden, _ = lax.optimization_barrier((hidden, sum_free))
+            theirs = down_part(plane.theirs, hidden, down_weight, width)
+            hidden, theirs = lax.optimization_barrier((hidden, theirs))
+            mine = down_part(plane.mine, hidden, down_weight, width)
+            share, core_free, sum_free = plane.scatter(mine, theirs)
+        else:
+            gathered = lax.all_gather(part, "exp", axis=0)
+            order = jnp.arange(shares, dtype=jnp.int32)
+            middle = shares // 2
+            plan = jnp.concatenate([order[:middle], base])
+            sums = gate_part(plan, chunk_ids, [gathered[:middle]], *weights)
+            plan = jnp.concatenate([order[middle:], base])
+            hidden = gate_part(plan, chunk_ids, [gathered[middle:]], *weights, sums)
+            partial = down_part(order, hidden, down_weight, width)
+            share = lax.psum_scatter(partial, "exp", scatter_dimension=0)
+        for i, offset in enumerate(chunk):
+            piece = share[i * length : (i + 1) * length]
+            if offset:
+                piece = swapped(piece, "seq", offset, offset)
+            total = total + piece.astype(F32)
     return total.astype(BF16)
 
 

time: 393 us -> 279 us (0.71)
  waiting for transfers between devices: 180 us -> 125 us
  local copies, waits for them, and re-layouts: 46.7 us -> 12.4 us
  Pallas kernels: 111 us -> 82.7 us
  starting transfers between devices: 25.5 us -> 52.6 us
  between operations: 13.7 us -> 0.37 us
  blocking collectives: 12.2 us -> 0 us
    reduce_scatter x4 -> x0, waiting for transfers between devices: 134 us -> none  [on_device(): share = lax.psum_scatter(partial, 'exp', scatter_dimension=0)]
    ppermute x0 -> x22, waiting for transfers between devices: none -> 122 us  [swapped(): return lax.ppermute(array, axis, pairs)]
    ppermute x0 -> x22, starting transfers between devices: none -> 43.7 us  [swapped(): return lax.ppermute(array, axis, pairs)]
    ppermute x8 -> x2, waiting for transfers between devices: 44.5 us -> 3.22 us  [shifted(): return lax.ppermute(array, axis, pairs)]
    unnamed x24 -> x38, local copies, waits for them, and re-layouts: 45.8 us -> 11.4 us
    pallas_call x4 -> x8, Pallas kernels: 107 us -> 79.4 us  [the longest x4 50.4 us: gate_part(): pl.pallas_call(functools.partial(gate_kernel, counts, last), grid_spec=pl...]
    ppermute x8 -> x2, starting transfers between devices: 25 us -> 8.89 us  [shifted(): return lax.ppermute(array, axis, pairs)]
    all_gather x1 -> x0, blocking collectives: 12.2 us -> none  [on_device(): all_ids = lax.all_gather(expert_ids.T, 'seq', axis=0)]
  transfers between devices with their start and end apart: 16 -> 24, of which waited for: 8 -> 17; matrix products, arithmetic and copies ran while one was open for 10% -> 1% of each run, Pallas kernels for 28% -> 19%
where the time goes in v2:
time: 279 us; the launch traced here: 278 us
  waiting for transfers between devices  125 us (45%)
  Pallas kernels  82.7 us (30%)
  starting transfers between devices  52.6 us (19%)
  local copies, waits for them, and re-layouts  12.4 us (4%)
  other arithmetic  4.65 us (2%)
    ppermute x22, waiting for transfers between devices, swapped(): return lax.ppermute(array, axis, pairs)  122 us
    pallas_call x4, Pallas kernels, gate_part(): pl.pallas_call(functools.partial(gate_kernel, counts, last), grid_spec=pl...  50.4 us
    ppermute x22, starting transfers between devices, swapped(): return lax.ppermute(array, axis, pairs)  43.7 us
    pallas_call x4, Pallas kernels, down_part(): pl.pallas_call(down_kernel, grid_spec=pltpu.PrefetchScalarGridSpec(num_sc...  29.1 us
    unnamed x38, local copies, waits for them, and re-layouts  11.4 us
    ppermute x2, starting transfers between devices, shifted(): return lax.ppermute(array, axis, pairs)  8.89 us
  transfers between devices with their start and end apart: 24, of which 17 were waited for; matrix products, arithmetic and copies ran while one was open for 1% of the time, Pallas kernels for 19%

profile of v2, /device:TPU:0, one launch (start us, length us, event | category | flops | bytes accessed | tf_op | source)
XLA Modules:
  0.0 277.9 jit_solution(17718598970382381096)
XLA Ops:
  0.0 1.0 copy-done.4
  1.0 1.0 copy-done.5
  2.0 0.7 copy-done.12
  2.7 1.0 shard_map.109
  3.7 4.9 %collective-permute-start = (bf16[784,128]{1,0:T(8,128)(2,1)S(1)}, bf16[784,128]{1,0:T(8,128)(2,1)S(1)}, u32[]{:S(2)}, u32[]{:S(2)}) collective-permute-start(bf16[784,128]{1,0:T(8,128)(2,1)S(1)} %get-tuple-element.32), channel_id=1, source_target_pairs={{0,8},{8,16},{16,24},{1,9},{9,17},{17,25},{2,10},{10,18},{18,26},{... | collective-permute-start | bytes 602120 | tf_op jit(solution)/shard_map/ppermute | solution.py:25
  8.7 1.6 collective-permute-start.2
  10.3 2.6 collective-permute-done.2
  12.9 0.7 pad_add_fusion.1
  13.6 2.6 collective-permute-start.3
  16.2 1.0 copy-done.6
  17.2 1.4 shard_map.110.intra_ref
  19.0 4.0 %collective-permute-start.1 = (bf16[784,128]{1,0:T(8,128)(2,1)S(1)}, bf16[784,128]{1,0:T(8,128)(2,1)S(1)}, u32[]{:S(2)}, u32[]{:S(2)}) collective-permute-start(bf16[784,128]{1,0:T(8,128)(2,1)S(1)} %concatenate.34), channel_id=1, source_target_pairs={{0,16},{8,24},{1,17},{9,25},{2,18},{10,26},{3,19},{11,27},{4,20},{... | collective-permute-start | bytes 602120 | tf_op jit(solution)/shard_map/ppermute | solution.py:25
  23.0 3.2 %collective-permute-done.1 = bf16[784,128]{1,0:T(8,128)(2,1)S(1)} collective-permute-done((bf16[784,128]{1,0:T(8,128)(2,1)S(1)}, bf16[784,128]{1,0:T(8,128)(2,1)S(1)}, u32[]{:S(2)}, u32[]{:S(2)}) %collective-permute-start.1) | collective-permute-done | bytes 200736 | tf_op jit(solution)/shard_map/ppermute | solution.py:25
  26.3 0.8 shard_map.111
  27.1 3.5 %collective-permute-start.4 = (bf16[256,768]{1,0:T(8,128)(2,1)S(1)}, bf16[256,768]{1,0:T(8,128)(2,1)S(1)}, u32[]{:S(2)}, u32[]{:S(2)}) collective-permute-start(bf16[256,768]{1,0:T(8,128)(2,1)S(1)} %shard_map.111), channel_id=1, source_target_pairs={{0,16},{8,24},{16,0},{24,8},{1,17},{9,25},{17,1},{25,9},{2,18},{10... | collective-permute-start | bytes 1179656 | tf_op jit(solution)/shard_map/ppermute | solution.py:311
  30.6 5.9 %collective-permute-done.4 = bf16[256,768]{1,0:T(8,128)(2,1)S(1)} collective-permute-done((bf16[256,768]{1,0:T(8,128)(2,1)S(1)}, bf16[256,768]{1,0:T(8,128)(2,1)S(1)}, u32[]{:S(2)}, u32[]{:S(2)}) %collective-permute-start.4) | collective-permute-done | bytes 393248 | tf_op jit(solution)/shard_map/ppermute | solution.py:311
  36.7 1.6 collective-permute-start.5
  38.2 10.5 %collective-permute-done.5 = bf16[512,768]{1,0:T(8,128)(2,1)S(1)} collective-permute-done((bf16[512,768]{1,0:T(8,128)(2,1)S(1)}, bf16[512,768]{1,0:T(8,128)(2,1)S(1)}, u32[]{:S(2)}, u32[]{:S(2)}) %collective-permute-start.5) | collective-permute-done | bytes 786464 | tf_op jit(solution)/shard_map/ppermute | solution.py:311
  49.0 1.6 collective-permute-start.6
  50.6 0.6 slice_bitcast_fusion.3
  51.2 1.3 collective-permute-done.7.refs_1_
  52.5 0.7 copy-done.8
  53.2 12.4 %shard_map.112 = (f32[2,576,512]{2,1,0:T(8,128)S(1)}, f32[2,576,512]{2,1,0:T(8,128)S(1)}, f32[2,512]{1,0:T(2,128)S(1)}) custom-call(s32[5]{0:T(128)S(1)} %concatenate.40.plan_ref, s32[2,512]{1,0:T(2,128)S(1)} %pad_add_fusion.2.ids_ref, bf16[2,512,768]{2,1,0:T(8,128)(2,1)S(1)} %pad_maximum_fusion.refs_0_, ...), custom_call_target="tpu_custom_call" | custom-call | flops 7247757312 | bytes 14155776 | tf_op jit(solution)/shard_map/pallas_call | solution.py:246
  65.7 1.4 copy-done
  67.1 1.4 copy-done.2
  68.5 0.9 collective-permute-done.6.refs_0_
  69.6 3.2 %collective-permute-done.8.refs_1_ = bf16[2,512,768]{2,1,0:T(8,128)(2,1)S(1)} collective-permute-done((bf16[2,512,768]{2,1,0:T(8,128)(2,1)S(1)}, bf16[2,512,768]{2,1,0:T(8,128)(2,1)S(1)}, u32[]{:S(2)}, u32[]{:S(2)}) %collective-permute-start.8) | collective-permute-done | bytes 1572896 | tf_op jit(solution)/shard_map/ppermute | solution.py:311
  72.9 1.7 copy-done.1
  74.5 1.7 copy-done.3
  76.2 0.7 copy-done.9
  76.9 13.0 %shard_map.113.hidden_ref = bf16[512,1152]{1,0:T(8,128)(2,1)S(1)} custom-call(s32[5]{0:T(128)S(1)} %concatenate.37.plan_ref, s32[2,512]{1,0:T(2,128)S(1)} %pad_add_fusion.2.ids_ref, bf16[2,512,768]{2,1,0:T(8,128)(2,1)S(1)} %collective-permute-done.6.refs_0_, bf16[2,512,768]{2,1,0:T(8,128)(2,1)S(1)} %collective-permute-done.8.refs_1_, ...), custom_call_target="tpu_custom_call" | custom-call | flops 7247757312 | bytes 14155776 | tf_op jit(solution)/shard_map/pallas_call | solution.py:246
  89.9 7.2 %shard_map.114 = bf16[4,512,768]{2,1,0:T(8,128)(2,1)S(1)} custom-call(s32[4]{0:T(128)S(1)} %pad_add_fusion.5.plan_ref, bf16[512,1152]{1,0:T(8,128)(2,1)S(1)} %shard_map.113.hidden_ref, bf16[2,576,6144]{2,1,0:T(8,128)(2,1)} %down_ref.7), custom_call_target="tpu_custom_call" | custom-call | flops 3623878656 | bytes 7077888 | tf_op jit(solution)/shard_map/pallas_call | solution.py:283
  97.3 15.4 %collective-permute-start.13 = (bf16[256,768]{1,0:T(8,128)(2,1)S(1)}, bf16[256,768]{1,0:T(8,128)(2,1)S(1)}, u32[]{:S(2)}, u32[]{:S(2)}) collective-permute-start(bf16[256,768]{1,0:T(8,128)(2,1)S(1)} %shard_map.111), channel_id=1, source_target_pairs={{0,8},{8,0},{16,24},{24,16},{1,9},{9,1},{17,25},{25,17},{2,10},{10... | collective-permute-start | bytes 1179656 | tf_op jit(solution)/shard_map/ppermute | solution.py:311
  112.7 2.1 collective-permute-start.14
  114.8 7.5 %collective-permute-done.13 = bf16[256,768]{1,0:T(8,128)(2,1)S(1)} collective-permute-done((bf16[256,768]{1,0:T(8,128)(2,1)S(1)}, bf16[256,768]{1,0:T(8,128)(2,1)S(1)}, u32[]{:S(2)}, u32[]{:S(2)}) %collective-permute-start.13) | collective-permute-done | bytes 393248 | tf_op jit(solution)/shard_map/ppermute | solution.py:311
  122.3 10.6 %collective-permute-done.14 = bf16[256,768]{1,0:T(8,128)(2,1)S(1)} collective-permute-done((bf16[256,768]{1,0:T(8,128)(2,1)S(1)}, bf16[256,768]{1,0:T(8,128)(2,1)S(1)}, u32[]{:S(2)}, u32[]{:S(2)}) %collective-permute-start.14) | collective-permute-done | bytes 393248 | tf_op jit(solution)/shard_map/ppermute | solution.py:311
  133.0 1.6 collective-permute-start.15
  134.6 10.5 %collective-permute-done.15 = bf16[512,768]{1,0:T(8,128)(2,1)S(1)} collective-permute-done((bf16[512,768]{1,0:T(8,128)(2,1)S(1)}, bf16[512,768]{1,0:T(8,128)(2,1)S(1)}, u32[]{:S(2)}, u32[]{:S(2)}) %collective-permute-start.15) | collective-permute-done | bytes 786464 | tf_op jit(solution)/shard_map/ppermute | solution.py:311
  145.3 1.6 collective-permute-start.16
  147.0 1.7 collective-permute-done.17.refs_1_
  148.7 12.0 %shard_map.116 = (f32[2,576,512]{2,1,0:T(8,128)S(1)}, f32[2,576,512]{2,1,0:T(8,128)S(1)}, f32[2,512]{1,0:T(2,128)S(1)}) custom-call(s32[5]{0:T(128)S(1)} %concatenate.40.plan_ref, s32[2,512]{1,0:T(2,128)S(1)} %pad_add_fusion.3.ids_ref, bf16[2,512,768]{2,1,0:T(8,128)(2,1)S(1)} %pad_maximum_fusion.1.refs_0_, ...), custom_call_target="tpu_custom_call" | custom-call | flops 7247757312 | bytes 14155776 | tf_op jit(solution)/shard_map/pallas_call | solution.py:246
  160.7 5.0 %collective-permute-done.16.refs_0_ = bf16[2,512,768]{2,1,0:T(8,128)(2,1)S(1)} collective-permute-done((bf16[2,512,768]{2,1,0:T(8,128)(2,1)S(1)}, bf16[2,512,768]{2,1,0:T(8,128)(2,1)S(1)}, u32[]{:S(2)}, u32[]{:S(2)}) %collective-permute-start.16) | collective-permute-done | bytes 1572896 | tf_op jit(solution)/shard_map/ppermute | solution.py:311
  165.8 7.2 %shard_map.115 = bf16[4,512,768]{2,1,0:T(8,128)(2,1)S(1)} custom-call(s32[4]{0:T(128)S(1)} %pad_add_fusion.4.plan_ref, bf16[512,1152]{1,0:T(8,128)(2,1)S(1)} %shard_map.113.hidden_ref, bf16[2,576,6144]{2,1,0:T(8,128)(2,1)} %down_ref.7), custom_call_target="tpu_custom_call" | custom-call | flops 3623878656 | bytes 7077888 | tf_op jit(solution)/shard_map/pallas_call | solution.py:283
  173.0 0.4 add_convert_fusion.1
  173.4 1.6 collective-permute-start.10
  175.0 13.0 %shard_map.117.hidden_ref = bf16[512,1152]{1,0:T(8,128)(2,1)S(1)} custom-call(s32[5]{0:T(128)S(1)} %concatenate.37.plan_ref, s32[2,512]{1,0:T(2,128)S(1)} %pad_add_fusion.3.ids_ref, bf16[2,512,768]{2,1,0:T(8,128)(2,1)S(1)} %collective-permute-done.16.refs_0_, bf16[2,512,768]{2,1,0:T(8,128)(2,1)S(1)} %collective-permute-done.18.refs_1_, ...), custom_call_target="tpu_custom_call" | custom-call | flops 7247757312 | bytes 14155776 | tf_op jit(solution)/shard_map/pallas_call | solution.py:246
  188.0 5.9 %collective-permute-done.10 = bf16[2,512,768]{2,1,0:T(8,128)(2,1)S(1)} collective-permute-done((bf16[2,512,768]{2,1,0:T(8,128)(2,1)S(1)}, bf16[2,512,768]{2,1,0:T(8,128)(2,1)S(1)}, u32[]{:S(2)}, u32[]{:S(2)}) %collective-permute-start.10) | collective-permute-done | bytes 1572896 | tf_op jit(solution)/shard_map/ppermute | solution.py:311
  193.9 7.4 %shard_map.118 = bf16[4,512,768]{2,1,0:T(8,128)(2,1)S(1)} custom-call(s32[4]{0:T(128)S(1)} %pad_add_fusion.5.plan_ref, bf16[512,1152]{1,0:T(8,128)(2,1)S(1)} %shard_map.117.hidden_ref, bf16[2,576,6144]{2,1,0:T(8,128)(2,1)} %down_ref.7), custom_call_target="tpu_custom_call" | custom-call | flops 3623878656 | bytes 7077888 | tf_op jit(solution)/shard_map/pallas_call | solution.py:283
  201.4 7.2 %shard_map.119 = bf16[4,512,768]{2,1,0:T(8,128)(2,1)S(1)} custom-call(s32[4]{0:T(128)S(1)} %pad_add_fusion.4.plan_ref, bf16[512,1152]{1,0:T(8,128)(2,1)S(1)} %shard_map.117.hidden_ref, bf16[2,576,6144]{2,1,0:T(8,128)(2,1)} %down_ref.7), custom_call_target="tpu_custom_call" | custom-call | flops 3623878656 | bytes 7077888 | tf_op jit(solution)/shard_map/pallas_call | solution.py:283
  208.6 0.4 add_convert_fusion
  209.0 1.6 collective-permute-start.20
  210.9 1.6 collective-permute-start.11
  212.5 25.5 %collective-permute-done.20 = bf16[2,512,768]{2,1,0:T(8,128)(2,1)S(1)} collective-permute-done((bf16[2,512,768]{2,1,0:T(8,128)(2,1)S(1)}, bf16[2,512,768]{2,1,0:T(8,128)(2,1)S(1)}, u32[]{:S(2)}, u32[]{:S(2)}) %collective-permute-start.20) | collective-permute-done | bytes 1572896 | tf_op jit(solution)/shard_map/ppermute | solution.py:311
  238.0 0.3 fusion.5
  238.3 1.6 collective-permute-start.21
  239.8 0.4 fusion.1
  240.3 2.0 collective-permute-start.12
  242.2 8.1 %collective-permute-done.21 = bf16[512,768]{1,0:T(8,128)(2,1)S(1)} collective-permute-done((bf16[512,768]{1,0:T(8,128)(2,1)S(1)}, bf16[512,768]{1,0:T(8,128)(2,1)S(1)}, u32[]{:S(2)}, u32[]{:S(2)}) %collective-permute-start.21) | collective-permute-done | bytes 786464 | tf_op jit(solution)/shard_map/ppermute | solution.py:311
  250.3 0.4 fusion
  250.8 0.8 collective-permute-start.22
  251.6 2.6 collective-permute-start.23
  254.2 6.8 %collective-permute-done.12 = bf16[256,768]{1,0:T(8,128)(2,1)S(1)} collective-permute-done((bf16[256,768]{1,0:T(8,128)(2,1)S(1)}, bf16[256,768]{1,0:T(8,128)(2,1)S(1)}, u32[]{:S(2)}, u32[]{:S(2)}) %collective-permute-start.12) | collective-permute-done | bytes 393248 | tf_op jit(solution)/shard_map/ppermute | solution.py:311
  261.0 15.9 %collective-permute-done.22 = bf16[256,768]{1,0:T(8,128)(2,1)S(1)} collective-permute-done((bf16[256,768]{1,0:T(8,128)(2,1)S(1)}, bf16[256,768]{1,0:T(8,128)(2,1)S(1)}, u32[]{:S(2)}, u32[]{:S(2)}) %collective-permute-start.22) | collective-permute-done | bytes 393248 | tf_op jit(solution)/shard_map/ppermute | solution.py:311
  276.9 1.0 add_convert_fusion.10
  (66 shorter events, 2.0 us)
Async XLA Ops:
  0.0 1.0 copy-start.4
  1.0 1.0 copy-start.5
  2.0 0.7 copy-start.12
  2.7 15.9 %copy-start.18 = (bf16[768]{0:T(1024)(128)(2,1)S(1)}, bf16[768]{0:T(1024)(128)(2,1)}, u32[]{:S(2)}) copy-start(bf16[768]{0:T(1024)(128)(2,1)} %param.16) | copy-start | bytes 4612
  2.7 16.0 %copy-start.15 = (s32[256,2]{0,1:T(2,128)S(1)}, s32[256,2]{0,1:T(2,128)}, u32[]{:S(2)}) copy-start(s32[256,2]{0,1:T(2,128)} %param.17) | copy-start | bytes 6148
  3.7 14.9 %collective-permute-start = (bf16[784,128]{1,0:T(8,128)(2,1)S(1)}, bf16[784,128]{1,0:T(8,128)(2,1)S(1)}, u32[]{:S(2)}, u32[]{:S(2)}) collective-permute-start(bf16[784,128]{1,0:T(8,128)(2,1)S(1)} %get-tuple-element.32), channel_id=1, source_target_pairs={{0,8},{8,16},{16,24},{1,9},{9,17},{17,25},{2,10},{10,18},{18,26},{... | collective-permute-start | bytes 602120 | tf_op jit(solution)/shard_map/ppermute | solution.py:25
  8.7 4.3 %collective-permute-start.2 = (s32[1,2,256]{2,1,0:T(2,128)}, s32[1,2,256]{2,1,0:T(2,128)S(1)}, u32[]{:S(2)}, u32[]{:S(2)}) collective-permute-start(s32[1,2,256]{2,1,0:T(2,128)} %bitcast.70), channel_id=1, source_target_pairs={{0,8},{8,0},{16,24},{24,16},{1,9},{9,1},{17,25},{25,17},{2,10},{10... | collective-permute-start | bytes 6152 | tf_op jit(solution)/shard_map/ppermute | solution.py:311
  13.6 5.0 %collective-permute-start.3 = (s32[2,2,256]{2,1,0:T(2,128)S(1)}, s32[2,2,256]{2,1,0:T(2,128)S(1)}, u32[]{:S(2)}, u32[]{:S(2)}) collective-permute-start(s32[2,2,256]{2,1,0:T(2,128)S(1)} %pad_add_fusion.1), channel_id=1, source_target_pairs={{0,16},{8,24},{16,0},{24,8},{1,17},{9,25},{17,1},{25,9},{2,18},{10... | collective-permute-start | bytes 12296 | tf_op jit(solution)/shard_map/ppermute | solution.py:311
  16.2 1.0 copy-start.6
  18.6 7.7 %copy-start.7 = (bf16[256,768]{1,0:T(8,128)(2,1)S(1)}, bf16[256,768]{1,0:T(8,128)(2,1)}, u32[]{:S(2)}) copy-start(bf16[256,768]{1,0:T(8,128)(2,1)} %query_ref.3) | copy-start | bytes 1179652
  18.6 7.7 %copy-start.11 = (bf16[256,768]{1,0:T(8,128)(2,1)S(1)}, bf16[256,768]{1,0:T(8,128)(2,1)}, u32[]{:S(2)}) copy-start(bf16[256,768]{1,0:T(8,128)(2,1)} %residual_ref.1) | copy-start | bytes 1179652
  19.0 7.2 %collective-permute-start.1 = (bf16[784,128]{1,0:T(8,128)(2,1)S(1)}, bf16[784,128]{1,0:T(8,128)(2,1)S(1)}, u32[]{:S(2)}, u32[]{:S(2)}) collective-permute-start(bf16[784,128]{1,0:T(8,128)(2,1)S(1)} %concatenate.34), channel_id=1, source_target_pairs={{0,16},{8,24},{1,17},{9,25},{2,18},{10,26},{3,19},{11,27},{4,20},{... | collective-permute-start | bytes 602120 | tf_op jit(solution)/shard_map/ppermute | solution.py:25
  27.1 9.4 %collective-permute-start.4 = (bf16[256,768]{1,0:T(8,128)(2,1)S(1)}, bf16[256,768]{1,0:T(8,128)(2,1)S(1)}, u32[]{:S(2)}, u32[]{:S(2)}) collective-permute-start(bf16[256,768]{1,0:T(8,128)(2,1)S(1)} %shard_map.111), channel_id=1, source_target_pairs={{0,16},{8,24},{16,0},{24,8},{1,17},{9,25},{17,1},{25,9},{2,18},{10... | collective-permute-start | bytes 1179656 | tf_op jit(solution)/shard_map/ppermute | solution.py:311
  36.7 12.1 %collective-permute-start.5 = (bf16[512,768]{1,0:T(8,128)(2,1)S(1)}, bf16[512,768]{1,0:T(8,128)(2,1)S(1)}, u32[]{:S(2)}, u32[]{:S(2)}) collective-permute-start(bf16[512,768]{1,0:T(8,128)(2,1)S(1)} %get-tuple-element.63), channel_id=1, source_target_pairs={{0,2},{1,5},{2,0},{3,7},{4,6},{5,1},{6,4},{7,3},{8,10},{9,13},{10,... | collective-permute-start | bytes 2359304 | tf_op jit(solution)/shard_map/ppermute | solution.py:311
  48.9 3.6 %collective-permute-start.7 = (bf16[2,512,768]{2,1,0:T(8,128)(2,1)S(1)}, bf16[2,512,768]{2,1,0:T(8,128)(2,1)}, u32[]{:S(2)}, u32[]{:S(2)}) collective-permute-start(bf16[2,512,768]{2,1,0:T(8,128)(2,1)S(1)} %pad_maximum_fusion.refs_0_), channel_id=1, source_target_pairs={{0,1},{1,0},{2,3},{3,2},{4,5},{5,4},{6,7},{7,6},{8,9},{9,8},{10,11... | collective-permute-start | bytes 4718600 | tf_op jit(solution)/shard_map/ppermute | solution.py:311
  49.0 20.5 %collective-permute-start.6 = (bf16[2,512,768]{2,1,0:T(8,128)(2,1)S(1)}, bf16[2,512,768]{2,1,0:T(8,128)(2,1)S(1)}, u32[]{:S(2)}, u32[]{:S(2)}) collective-permute-start(bf16[2,512,768]{2,1,0:T(8,128)(2,1)S(1)} %pad_maximum_fusion.refs_0_), channel_id=1, source_target_pairs={{0,4},{1,3},{2,6},{3,1},{4,0},{5,7},{6,2},{7,5},{8,12},{9,11},{10,... | collective-permute-start | bytes 4718600 | tf_op jit(solution)/shard_map/ppermute | solution.py:311
  52.5 0.7 copy-start.8
  65.7 1.4 copy-start
  67.1 1.4 copy-start.2
  69.4 3.4 %collective-permute-start.8 = (bf16[2,512,768]{2,1,0:T(8,128)(2,1)S(1)}, bf16[2,512,768]{2,1,0:T(8,128)(2,1)S(1)}, u32[]{:S(2)}, u32[]{:S(2)}) collective-permute-start(bf16[2,512,768]{2,1,0:T(8,128)(2,1)S(1)} %collective-permute-done.6.refs_0_), channel_id=1, source_target_pairs={{0,1},{1,0},{2,3},{3,2},{4,5},{5,4},{6,7},{7,6},{8,9},{9,8},{10,11... | collective-permute-start | bytes 4718600 | tf_op jit(solution)/shard_map/ppermute | solution.py:311
  72.9 1.7 copy-start.1
  74.5 1.7 copy-start.3
  76.2 0.7 copy-start.9
  97.1 51.6 %collective-permute-start.9 = (bf16[4,512,768]{2,1,0:T(8,128)(2,1)S(1)}, bf16[4,512,768]{2,1,0:T(8,128)(2,1)S(1)}, u32[]{:S(2)}, u32[]{:S(2)}) collective-permute-start(bf16[4,512,768]{2,1,0:T(8,128)(2,1)S(1)} %shard_map.114), channel_id=1, source_target_pairs={{0,1},{1,0},{2,3},{3,2},{4,5},{5,4},{6,7},{7,6},{8,9},{9,8},{10,11... | collective-permute-start | bytes 9437192 | tf_op jit(solution)/shard_map/ppermute | solution.py:311
  97.3 25.0 %collective-permute-start.13 = (bf16[256,768]{1,0:T(8,128)(2,1)S(1)}, bf16[256,768]{1,0:T(8,128)(2,1)S(1)}, u32[]{:S(2)}, u32[]{:S(2)}) collective-permute-start(bf16[256,768]{1,0:T(8,128)(2,1)S(1)} %shard_map.111), channel_id=1, source_target_pairs={{0,8},{8,0},{16,24},{24,16},{1,9},{9,1},{17,25},{25,17},{2,10},{10... | collective-permute-start | bytes 1179656 | tf_op jit(solution)/shard_map/ppermute | solution.py:311
  112.7 20.2 %collective-permute-start.14 = (bf16[256,768]{1,0:T(8,128)(2,1)S(1)}, bf16[256,768]{1,0:T(8,128)(2,1)S(1)}, u32[]{:S(2)}, u32[]{:S(2)}) collective-permute-start(bf16[256,768]{1,0:T(8,128)(2,1)S(1)} %shard_map.111), channel_id=1, source_target_pairs={{0,24},{8,16},{16,8},{24,0},{1,25},{9,17},{17,9},{25,1},{2,26},{10... | collective-permute-start | bytes 1179656 | tf_op jit(solution)/shard_map/ppermute | solution.py:311
  133.0 12.1 %collective-permute-start.15 = (bf16[512,768]{1,0:T(8,128)(2,1)S(1)}, bf16[512,768]{1,0:T(8,128)(2,1)S(1)}, u32[]{:S(2)}, u32[]{:S(2)}) collective-permute-start(bf16[512,768]{1,0:T(8,128)(2,1)S(1)} %pad_maximum_fusion.3), channel_id=1, source_target_pairs={{0,2},{1,5},{2,0},{3,7},{4,6},{5,1},{6,4},{7,3},{8,10},{9,13},{10,... | collective-permute-start | bytes 2359304 | tf_op jit(solution)/shard_map/ppermute | solution.py:311
  145.0 1.9 copy-start.16
  145.0 1.9 copy-start.17
  145.0 3.6 %copy-start.10 = (bf16[6144,2]{0,1:T(2,128)(2,1)S(1)}, bf16[6144,2]{0,1:T(2,128)(2,1)}, u32[]{:S(2)}) copy-start(bf16[6144,2]{0,1:T(2,128)(2,1)} %param.18) | copy-start | bytes 73732
  145.2 3.5 %collective-permute-start.17 = (bf16[2,512,768]{2,1,0:T(8,128)(2,1)S(1)}, bf16[2,512,768]{2,1,0:T(8,128)(2,1)S(1)}, u32[]{:S(2)}, u32[]{:S(2)}) collective-permute-start(bf16[2,512,768]{2,1,0:T(8,128)(2,1)S(1)} %pad_maximum_fusion.1.refs_0_), channel_id=1, source_target_pairs={{0,1},{1,0},{2,3},{3,2},{4,5},{5,4},{6,7},{7,6},{8,9},{9,8},{10,11... | collective-permute-start | bytes 4718600 | tf_op jit(solution)/shard_map/ppermute | solution.py:311
  145.3 20.5 %collective-permute-start.16 = (bf16[2,512,768]{2,1,0:T(8,128)(2,1)S(1)}, bf16[2,512,768]{2,1,0:T(8,128)(2,1)S(1)}, u32[]{:S(2)}, u32[]{:S(2)}) collective-permute-start(bf16[2,512,768]{2,1,0:T(8,128)(2,1)S(1)} %pad_maximum_fusion.1.refs_0_), channel_id=1, source_target_pairs={{0,4},{1,3},{2,6},{3,1},{4,0},{5,7},{6,2},{7,5},{8,12},{9,11},{10,... | collective-permute-start | bytes 4718600 | tf_op jit(solution)/shard_map/ppermute | solution.py:311
  165.8 9.2 %collective-permute-start.18 = (bf16[2,512,768]{2,1,0:T(8,128)(2,1)S(1)}, bf16[2,512,768]{2,1,0:T(8,128)(2,1)S(1)}, u32[]{:S(2)}, u32[]{:S(2)}) collective-permute-start(bf16[2,512,768]{2,1,0:T(8,128)(2,1)S(1)} %collective-permute-done.16.refs_0_), channel_id=1, source_target_pairs={{0,1},{1,0},{2,3},{3,2},{4,5},{5,4},{6,7},{7,6},{8,9},{9,8},{10,11... | collective-permute-start | bytes 4718600 | tf_op jit(solution)/shard_map/ppermute | solution.py:311
  173.4 20.5 %collective-permute-start.10 = (bf16[2,512,768]{2,1,0:T(8,128)(2,1)S(1)}, bf16[2,512,768]{2,1,0:T(8,128)(2,1)S(1)}, u32[]{:S(2)}, u32[]{:S(2)}) collective-permute-start(bf16[2,512,768]{2,1,0:T(8,128)(2,1)S(1)} %add_convert_fusion.1), channel_id=1, source_target_pairs={{0,4},{1,3},{2,6},{3,1},{4,0},{5,7},{6,2},{7,5},{8,12},{9,11},{10,... | collective-permute-start | bytes 4718600 | tf_op jit(solution)/shard_map/ppermute | solution.py:311
  193.9 7.4 %copy-start.13 = (bf16[2,512,768]{2,1,0:T(8,128)(2,1)}, bf16[2,512,768]{2,1,0:T(8,128)(2,1)S(1)}, u32[]{:S(2)}) copy-start(bf16[2,512,768]{2,1,0:T(8,128)(2,1)S(1)} %collective-permute-done.10) | copy-start | bytes 4718596
  201.3 7.3 %collective-permute-start.19 = (bf16[4,512,768]{2,1,0:T(8,128)(2,1)S(1)}, bf16[4,512,768]{2,1,0:T(8,128)(2,1)S(1)}, u32[]{:S(2)}, u32[]{:S(2)}) collective-permute-start(bf16[4,512,768]{2,1,0:T(8,128)(2,1)S(1)} %shard_map.118), channel_id=1, source_target_pairs={{0,1},{1,0},{2,3},{3,2},{4,5},{5,4},{6,7},{7,6},{8,9},{9,8},{10,11... | collective-permute-start | bytes 9437192 | tf_op jit(solution)/shard_map/ppermute | solution.py:311
  208.6 2.0 copy-start.14
  209.0 28.9 %collective-permute-start.20 = (bf16[2,512,768]{2,1,0:T(8,128)(2,1)S(1)}, bf16[2,512,768]{2,1,0:T(8,128)(2,1)S(1)}, u32[]{:S(2)}, u32[]{:S(2)}) collective-permute-start(bf16[2,512,768]{2,1,0:T(8,128)(2,1)S(1)} %add_convert_fusion), channel_id=1, source_target_pairs={{0,4},{1,3},{2,6},{3,1},{4,0},{5,7},{6,2},{7,5},{8,12},{9,11},{10,... | collective-permute-start | bytes 4718600 | tf_op jit(solution)/shard_map/ppermute | solution.py:311
  210.9 28.9 %collective-permute-start.11 = (bf16[512,768]{1,0:T(8,128)(2,1)S(1)}, bf16[512,768]{1,0:T(8,128)(2,1)S(1)}, u32[]{:S(2)}, u32[]{:S(2)}) collective-permute-start(bf16[512,768]{1,0:T(8,128)(2,1)S(1)} %fusion.3), channel_id=1, source_target_pairs={{0,2},{1,5},{2,0},{3,7},{4,6},{5,1},{6,4},{7,3},{8,10},{9,13},{10,... | collective-permute-start | bytes 2359304 | tf_op jit(solution)/shard_map/ppermute | solution.py:311
  238.3 12.1 %collective-permute-start.21 = (bf16[512,768]{1,0:T(8,128)(2,1)S(1)}, bf16[512,768]{1,0:T(8,128)(2,1)S(1)}, u32[]{:S(2)}, u32[]{:S(2)}) collective-permute-start(bf16[512,768]{1,0:T(8,128)(2,1)S(1)} %fusion.5), channel_id=1, source_target_pairs={{0,2},{1,5},{2,0},{3,7},{4,6},{5,1},{6,4},{7,3},{8,10},{9,13},{10,... | collective-permute-start | bytes 2359304 | tf_op jit(solution)/shard_map/ppermute | solution.py:311
  240.3 20.8 %collective-permute-start.12 = (bf16[256,768]{1,0:T(8,128)(2,1)S(1)}, bf16[256,768]{1,0:T(8,128)(2,1)S(1)}, u32[]{:S(2)}, u32[]{:S(2)}) collective-permute-start(bf16[256,768]{1,0:T(8,128)(2,1)S(1)} %slice.148), channel_id=1, source_target_pairs={{0,16},{8,24},{16,0},{24,8},{1,17},{9,25},{17,1},{25,9},{2,18},{10... | collective-permute-start | bytes 1179656 | tf_op jit(solution)/shard_map/ppermute | solution.py:311
  250.8 26.1 %collective-permute-start.22 = (bf16[256,768]{1,0:T(8,128)(2,1)S(1)}, bf16[256,768]{1,0:T(8,128)(2,1)S(1)}, u32[]{:S(2)}, u32[]{:S(2)}) collective-permute-start(bf16[256,768]{1,0:T(8,128)(2,1)S(1)} %get-tuple-element.60), channel_id=1, source_target_pairs={{0,8},{8,0},{16,24},{24,16},{1,9},{9,1},{17,25},{25,17},{2,10},{10... | collective-permute-start | bytes 1179656 | tf_op jit(solution)/shard_map/ppermute | solution.py:311
  251.6 25.3 %collective-permute-start.23 = (bf16[256,768]{1,0:T(8,128)(2,1)S(1)}, bf16[256,768]{1,0:T(8,128)(2,1)S(1)}, u32[]{:S(2)}, u32[]{:S(2)}) collective-permute-start(bf16[256,768]{1,0:T(8,128)(2,1)S(1)} %get-tuple-element.61), channel_id=1, source_target_pairs={{0,24},{8,16},{16,8},{24,0},{1,25},{9,17},{17,9},{25,1},{2,26},{10... | collective-permute-start | bytes 1179656 | tf_op jit(solution)/shard_map/ppermute | solution.py:311

commit v3 on v2

--- a/solution.py
+++ b/solution.py
@@ -11,6 +11,7 @@
 BF16 = jnp.bfloat16
 HIGHEST = lax.Precision.HIGHEST
 VMEM_LIMIT = 40 * 1024 * 1024
+ID_ROWS = 16
 
 
 def lower_ones(length):
@@ -104,8 +105,22 @@
     )(attn_query, attn_key, attn_value, log_decay, cumulative)
 
 
-def stream_kernel(query_ref, intra_ref, cumulative_ref, incoming_ref, residual_ref, gain_ref, out_ref):
+def stream_kernel(
+    query_ref, intra_ref, cumulative_ref, incoming_ref, residual_ref, gain_ref, ids_ref, out_ref
+):
     heads, size = incoming_ref.shape[0], incoming_ref.shape[1]
+    length, width = residual_ref.shape
+    choices = ids_ref.shape[0]
+    below = jnp.concatenate(
+        [
+            ids_ref[...].astype(F32),
+            jnp.zeros((ID_ROWS - choices, length), F32),
+        ],
+        axis=0,
+    )
+    out_ref[length:, :] = jnp.concatenate(
+        [below, jnp.zeros((ID_ROWS, width - length), F32)], axis=1
+    ).astype(BF16)
     faded = jnp.exp(cumulative_ref[...])
     for h in range(heads):
         columns = slice(h * size, (h + 1) * size)
@@ -119,18 +134,18 @@
         attn_out = intra_ref[:, columns] + faded[:, h : h + 1] * inter
         mean_square = jnp.mean(attn_out * attn_out, axis=1, keepdims=True)
         normed = attn_out * lax.rsqrt(mean_square + 1e-06)
-        out_ref[:, columns] = (
+        out_ref[:length, columns] = (
             residual_ref[:, columns].astype(F32) + gain_ref[:, columns].astype(F32) * normed
         ).astype(BF16)
 
 
-def make_stream(attn_query, intra, cumulative, incoming, residual, norm_gain):
+def make_stream(attn_query, intra, cumulative, incoming, residual, norm_gain, ids):
     length, width = attn_query.shape
     return pl.pallas_call(
         stream_kernel,
-        out_shape=jax.ShapeDtypeStruct((length, width), BF16),
-        compiler_params=pltpu.CompilerParams(vmem_limit_bytes=VMEM_LIMIT),
-    )(attn_query, intra, cumulative, incoming, residual, norm_gain.reshape(1, width))
+        out_shape=jax.ShapeDtypeStruct((length + ID_ROWS, width), BF16),
+        compiler_params=pltpu.CompilerParams(vmem_limit_bytes=VMEM_LIMIT),
+    )(attn_query, intra, cumulative, incoming, residual, norm_gain.reshape(1, width), ids)
 
 
 def read_message(message, heads):
@@ -171,7 +186,89 @@
     return incoming
 
 
-def gate_kernel(counts, last, plan_ref, ids_ref, *refs):
+def select_kernel(capacity, choices, experts, base_ref, *refs):
+    parts, (out_ref, place_ref) = refs[:-2], refs[-2:]
+    length = parts[0].shape[0] - ID_ROWS
+    before = lower_ones(length).astype(BF16)
+    slot = lax.broadcasted_iota(jnp.int32, (capacity, length), 0).astype(F32)
+    nothing = jnp.zeros((capacity, length), BF16)
+    rows = []
+    for j in range(experts):
+        expert = (base_ref[0] + j).astype(F32)
+        for i, part in enumerate(parts):
+            ids = part[length:, :length].astype(F32)
+            chosen = ids[0:1, :] == expert
+            for choice in range(1, choices):
+                chosen = chosen | (ids[choice : choice + 1, :] == expert)
+            flag = jnp.where(chosen, 1.0, 0.0)
+            rank = lax.dot_general(
+                jnp.broadcast_to(flag, (16, length)).astype(BF16),
+                before,
+                (((1,), (1,)), ((), ())),
+                preferred_element_type=F32,
+            )[0:1, :]
+            rank = jnp.where(chosen, rank - 1.0, -1.0)
+            here = jnp.where(slot == rank, 1.0, 0.0).astype(BF16)
+            rows.append(
+                jnp.concatenate([here if k == i else nothing for k in range(len(parts))], axis=1)
+            )
+    place = jnp.concatenate(rows, axis=0)
+    place_ref[...] = place
+    tokens = jnp.concatenate([part[:length, :] for part in parts], axis=0)
+    out_ref[...] = lax.dot_general(
+        tokens, place, (((0,), (1,)), ((), ())), preferred_element_type=F32
+    ).astype(BF16)
+
+
+def select_slots(base, parts, capacity, choices, experts):
+    rows, width = parts[0].shape
+    length = rows - ID_ROWS
+    slots = len(parts) * experts * capacity
+    tokens = len(parts) * length
+    whole = pl.BlockSpec(memory_space=pltpu.VMEM)
+    return pl.pallas_call(
+        functools.partial(select_kernel, capacity, choices, experts),
+        in_specs=[pl.BlockSpec(memory_space=pltpu.SMEM), *([whole] * len(parts))],
+        out_shape=(
+            jax.ShapeDtypeStruct((width, slots), BF16),
+            jax.ShapeDtypeStruct((slots, tokens), BF16),
+        ),
+        cost_estimate=pl.CostEstimate(
+            flops=2 * slots * tokens * width, bytes_accessed=4 * slots * width, transcendentals=0
+        ),
+        compiler_params=pltpu.CompilerParams(vmem_limit_bytes=VMEM_LIMIT),
+    )(base, *parts)
+
+
+def combine_kernel(length, place_ref, *refs):
+    sections = place_ref.shape[1] // length
+    shares, outs = refs[:-sections], refs[-sections:]
+    total = shares[0][...].astype(F32)
+    for share in shares[1:]:
+        total = total + share[...].astype(F32)
+    tokens = lax.dot_general(
+        place_ref[...], total.astype(BF16), (((0,), (0,)), ((), ())), preferred_element_type=F32
+    ).astype(BF16)
+    for i, out in enumerate(outs):
+        out[...] = tokens[i * length : (i + 1) * length, :]
+
+
+def combine_slots(place, shares, length):
+    slots, tokens = place.shape
+    width = shares[0].shape[1]
+    return pl.pallas_call(
+        functools.partial(combine_kernel, length),
+        out_shape=tuple(
+            jax.ShapeDtypeStruct((length, width), BF16) for _ in range(tokens // length)
+        ),
+        cost_estimate=pl.CostEstimate(
+            flops=2 * slots * tokens * width, bytes_accessed=8 * slots * width, transcendentals=0
+        ),
+        compiler_params=pltpu.CompilerParams(vmem_limit_bytes=VMEM_LIMIT),
+    )(place, *shares)
+
+
+def gate_kernel(counts, last, plan_ref, *refs):
     step = pl.program_id(0)
     blocks = sum(counts)
     x_refs, refs = refs[: len(counts)], refs[len(counts) :]
@@ -182,6 +279,7 @@
     else:
         gate_acc, up_acc, score_acc = refs
     experts = gate_ref.shape[0]
+    slots = gate_acc.shape[2]
 
     @pl.when(step == 0)
     def _():
@@ -197,46 +295,43 @@
     x = x_refs[-1][0]
     for i in range(len(counts) - 2, -1, -1):
         x = jnp.where(step < sum(counts[: i + 1]), x_refs[i][0], x)
-    across = (((1,), (1,)), ((), ()))
-    score_acc[...] += lax.dot_general(router_ref[0], x, across, preferred_element_type=F32)
+    score_acc[...] += jnp.dot(router_ref[0], x, preferred_element_type=F32)
     for j in range(experts):
-        gate_acc[j] += lax.dot_general(gate_ref[j], x, across, preferred_element_type=F32)
-        up_acc[j] += lax.dot_general(up_ref[j], x, across, preferred_element_type=F32)
+        mine = x[:, j * slots : (j + 1) * slots]
+        gate_acc[j] += jnp.dot(gate_ref[j], mine, preferred_element_type=F32)
+        up_acc[j] += jnp.dot(up_ref[j], mine, preferred_element_type=F32)
 
     if last:
 
         @pl.when(step == blocks - 1)
         def _():
-            parts = []
             for j in range(experts):
-                chosen = ids_ref[0:1, :] == plan_ref[blocks] + j
-                for choice in range(1, ids_ref.shape[0]):
-                    chosen = chosen | (ids_ref[choice : choice + 1, :] == plan_ref[blocks] + j)
+                score = score_acc[j : j + 1, j * slots : (j + 1) * slots]
                 gate = gate_acc[j]
                 routed = gate / (1.0 + jnp.exp(-gate)) * up_acc[j]
-                routed = routed / (1.0 + jnp.exp(-score_acc[j : j + 1, :]))
-                parts.append(jnp.where(chosen, routed, 0.0))
-            hidden_ref[...] = jnp.concatenate(parts, axis=0).T.astype(BF16)
-
-
-def gate_part(plan, ids, xs, router_rows, gate_rows, up_rows, sums=None):
+                routed = routed / (1.0 + jnp.exp(-score))
+                hidden_ref[j] = routed.T.astype(BF16)
+
+
+def gate_part(plan, xs, router_rows, gate_rows, up_rows, sums=None):
     counts = tuple(x.shape[0] for x in xs)
     blocks = sum(counts)
-    _, length, width = xs[0].shape
+    _, width, total = xs[0].shape
     experts, units, _ = gate_rows.shape
+    slots = total // experts
     whole = pl.BlockSpec(memory_space=pltpu.VMEM)
     last = sums is not None
 
     def x_spec(i):
         before = sum(counts[:i])
         return pl.BlockSpec(
-            (1, length, width), lambda p, plan: (jnp.clip(p - before, 0, counts[i] - 1), 0, 0)
+            (1, width, total), lambda p, plan: (jnp.clip(p - before, 0, counts[i] - 1), 0, 0)
         )
 
     weight_spec = pl.BlockSpec((experts, units, width), lambda p, plan: (0, 0, plan[p]))
-    sum_shapes = [(experts, units, length), (experts, units, length), (experts, length)]
+    sum_shapes = [(experts, units, slots), (experts, units, slots), (experts, total)]
     if last:
-        out_shape = jax.ShapeDtypeStruct((length, experts * units), BF16)
+        out_shape = jax.ShapeDtypeStruct((experts, slots, units), BF16)
         out_specs = whole
         scratch = [pltpu.VMEM(shape, F32) for shape in sum_shapes]
     else:
@@ -249,7 +344,6 @@
             num_scalar_prefetch=1,
             grid=(blocks,),
             in_specs=[
-                whole,
                 *[x_spec(i) for i in range(len(counts))],
                 pl.BlockSpec((1, experts, width), lambda p, plan: (plan[p], 0, 0)),
                 weight_spec,
@@ -261,25 +355,25 @@
         ),
         out_shape=out_shape,
         cost_estimate=pl.CostEstimate(
-            flops=4 * experts * length * blocks * width * units,
+            flops=4 * total * blocks * width * units,
             bytes_accessed=4 * experts * blocks * width * units,
             transcendentals=0,
         ),
         compiler_params=pltpu.CompilerParams(vmem_limit_bytes=VMEM_LIMIT),
-    )(plan, ids, *xs, router_rows, gate_rows, up_rows, *(sums if last else ()))
+    )(plan, *xs, router_rows, gate_rows, up_rows, *(sums if last else ()))
 
 
 def down_kernel(plan_ref, hidden_ref, down_ref, out_ref):
-    experts, units, width = down_ref.shape
-    out_ref[0] = jnp.dot(
-        hidden_ref[...], down_ref[...].reshape(experts * units, width), preferred_element_type=F32
-    ).astype(BF16)
+    experts, slots, _ = hidden_ref.shape
+    for j in range(experts):
+        out_ref[0, j * slots : (j + 1) * slots, :] = jnp.dot(
+            hidden_ref[j], down_ref[j], preferred_element_type=F32
+        ).astype(BF16)
 
 
 def down_part(plan, hidden, down_weight, width):
     blocks = plan.shape[0]
-    length = hidden.shape[0]
-    experts, units, _ = down_weight.shape
+    experts, slots, units = hidden.shape
     return pl.pallas_call(
         down_kernel,
         grid_spec=pltpu.PrefetchScalarGridSpec(
@@ -289,11 +383,11 @@
                 pl.BlockSpec(memory_space=pltpu.VMEM),
                 pl.BlockSpec((experts, units, width), lambda p, plan: (0, 0, plan[p])),
             ],
-            out_specs=pl.BlockSpec((1, length, width), lambda p, plan: (p, 0, 0)),
-        ),
-        out_shape=jax.ShapeDtypeStruct((blocks, length, width), BF16),
+            out_specs=pl.BlockSpec((1, experts * slots, width), lambda p, plan: (p, 0, 0)),
+        ),
+        out_shape=jax.ShapeDtypeStruct((blocks, experts * slots, width), BF16),
         cost_estimate=pl.CostEstimate(
-            flops=2 * experts * length * blocks * width * units,
+            flops=2 * experts * slots * blocks * width * units,
             bytes_accessed=2 * experts * blocks * width * units,
             transcendentals=0,
         ),
@@ -333,9 +427,10 @@
 
     def scatter(self, mine, theirs):
         got = swapped(theirs, "exp", 1, 1)
-        got_two = swapped(added(mine[2:], got[2:]), "exp", 4, 2)
+        sent_two = added(mine[2:], got[2:])
+        got_two = swapped(sent_two, "exp", 4, 2)
         got_one = swapped(added(added(mine[1], got[1]), got_two[1]), "exp", 2, 4)
-        return added(added(added(mine[0], got[0]), got_two[0]), got_one), got, got_two
+        return (mine[0], got[0], got_two[0], got_one), sent_two, got_two
 
 
 def on_device(
@@ -361,17 +456,12 @@
     gate_rows = gate_weight.swapaxes(1, 2)
     up_rows = up_weight.swapaxes(1, 2)
 
-    ids = expert_ids.T[None]
-    distance = 1
-    while distance < groups:
-        ids = jnp.concatenate([ids, swapped(ids, "seq", distance, distance)])
-        distance *= 2
-
     message, cumulative = section_state(attn_key, attn_value, log_decay)
     intra = intra_section(attn_query, attn_key, attn_value, log_decay, cumulative)
     incoming = incoming_state(message, heads_here)
-    incoming, ids = lax.optimization_barrier((incoming, ids))
-    stream = make_stream(attn_query, intra, cumulative, incoming, residual, norm_gain)
+    stream = make_stream(
+        attn_query, intra, cumulative, incoming, residual, norm_gain, expert_ids.T
+    )
 
     half = groups // 2
     chunks = [(i, i + half) for i in range(half)]
@@ -382,49 +472,74 @@
         for offset in chunks[i]:
             parts[offset] = swapped(later, "seq", offset, offset)
 
-    total = stream.astype(F32)
-    plane = PairedPlane() if shares == 8 else None
-    links_free, core_free, sum_free = None, None, None
-    for chunk in chunks:
-        part = jnp.concatenate([parts[offset] for offset in chunk])
-        chunk_ids = jnp.concatenate([ids[offset] for offset in chunk], axis=1)
-        weights = (router_rows, gate_rows, up_rows)
-        if plane:
-            if links_free is not None:
-                part, _ = lax.optimization_barrier((part, links_free))
-            two = plane.first(part)
-            far_two = plane.second(two)
-            links_free = far_two
-            near_two = plane.across(two)
-            if core_free is not None:
-                near_two, _ = lax.optimization_barrier((near_two, core_free))
-            plan = jnp.concatenate([plane.early, base])
-            sums = gate_part(plan, chunk_ids, [two, near_two], *weights)
-            far_two, sums = lax.optimization_barrier((far_two, sums))
-            plan = jnp.concatenate([plane.late, base])
-            hidden = gate_part(plan, chunk_ids, [far_two, plane.across(far_two)], *weights, sums)
-            if sum_free is not None:
-                hidden, _ = lax.optimization_barrier((hidden, sum_free))
-            theirs = down_part(plane.theirs, hidden, down_weight, width)
-            hidden, theirs = lax.optimization_barrier((hidden, theirs))
-            mine = down_part(plane.mine, hidden, down_weight, width)
-            share, core_free, sum_free = plane.scatter(mine, theirs)
-        else:
-            gathered = lax.all_gather(part, "exp", axis=0)
-            order = jnp.arange(shares, dtype=jnp.int32)
-            middle = shares // 2
-            plan = jnp.concatenate([order[:middle], base])
-            sums = gate_part(plan, chunk_ids, [gathered[:middle]], *weights)
-            plan = jnp.concatenate([order[middle:], base])
-            hidden = gate_part(plan, chunk_ids, [gathered[middle:]], *weights, sums)
+    capacity = 4 * length // (experts_here * groups)
+    weights = (router_rows, gate_rows, up_rows)
+    total = stream[:length].astype(F32)
+    if shares == 8:
+        pieces = paired_chunks(
+            PairedPlane(),
+            [[parts[offset] for offset in chunk] for chunk in chunks],
+            base,
+            weights,
+            down_weight,
+            capacity,
+            expert_ids.shape[1],
+        )
+    else:
+        order = jnp.arange(shares, dtype=jnp.int32)
+        middle = shares // 2
+        pieces = []
+        for chunk in chunks:
+            chosen, place = select_slots(
+                base, [parts[offset] for offset in chunk], capacity, expert_ids.shape[1], experts_here
+            )
+            gathered = lax.all_gather(chosen, "exp", axis=0)
+            sums = gate_part(order[:middle], [gathered[:middle]], *weights)
+            hidden = gate_part(order[middle:], [gathered[middle:]], *weights, sums)
             partial = down_part(order, hidden, down_weight, width)
             share = lax.psum_scatter(partial, "exp", scatter_dimension=0)
-        for i, offset in enumerate(chunk):
-            piece = share[i * length : (i + 1) * length]
+            pieces.append(combine_slots(place, [share], length))
+    for chunk, chunk_pieces in zip(chunks, pieces):
+        for offset, piece in zip(chunk, chunk_pieces):
             if offset:
                 piece = swapped(piece, "seq", offset, offset)
             total = total + piece.astype(F32)
     return total.astype(BF16)
+
+
+def paired_chunks(plane, chunk_parts, base, weights, down_weight, capacity, choices):
+    experts = down_weight.shape[0]
+    length = chunk_parts[0][0].shape[0] - ID_ROWS
+    width = chunk_parts[0][0].shape[1]
+    tie = lax.optimization_barrier
+    chosen = [
+        select_slots(base, parts, capacity, choices, experts) for parts in chunk_parts
+    ]
+    two = [plane.first(slots) for slots, _ in chosen]
+    pieces = []
+    sent_two, got_two = None, None
+    for i, (_, place) in enumerate(chosen):
+        follows = i + 1 < len(chosen)
+        far_two = plane.second(two[i])
+        near_two = plane.across(two[i])
+        if follows:
+            near_two, _ = tie((near_two, chosen[i + 1]))
+        if sent_two is not None:
+            near_two, _ = tie((near_two, sent_two))
+        sums = gate_part(plane.early, [two[i], near_two], *weights)
+        far_two, sums = tie((far_two, sums))
+        near_far = plane.across(far_two)
+        if follows:
+            near_far, _ = tie((near_far, two[i + 1]))
+        hidden = gate_part(plane.late, [far_two, near_far], *weights, sums)
+        if got_two is not None:
+            hidden, _ = tie((hidden, got_two))
+        theirs = down_part(plane.theirs, hidden, down_weight, width)
+        hidden, theirs = tie((hidden, theirs))
+        mine = down_part(plane.mine, hidden, down_weight, width)
+        share, sent_two, got_two = plane.scatter(mine, theirs)
+        pieces.append(combine_slots(place, share, length))
+    return pieces
 
 
 def solution(mesh):

time: 279 us -> 252 us (0.903)
  Pallas kernels: 82.7 us -> 67.6 us
  starting transfers between devices: 52.6 us -> 46.9 us
  local copies, waits for them, and re-layouts: 12.4 us -> 7.19 us
    pallas_call x4, Pallas kernels: 50.4 us -> 36.4 us  [gate_part(): pl.pallas_call(functools.partial(gate_kernel, counts, last), grid_spec=pl...]
    ppermute x22 -> x20, starting transfers between devices: 43.7 us -> 36.6 us  [swapped(): return lax.ppermute(array, axis, pairs)]
    unnamed x38 -> x28, local copies, waits for them, and re-layouts: 11.4 us -> 6.01 us
    pallas_call x4, Pallas kernels: 29.1 us -> 24.1 us  [down_part(): pl.pallas_call(down_kernel, grid_spec=pltpu.PrefetchScalarGridSpec(num_sc...]
    pallas_call x1 -> x5, Pallas kernels: 0.85 us -> 4.74 us  [the longest x2 2.5 us: select_slots(): pl.pallas_call(functools.partial(select_kernel, capacity, choices, expert...]
    ppermute x22 -> x20, waiting for transfers between devices: 122 us -> 121 us  [swapped(): return lax.ppermute(array, axis, pairs)]
  transfers between devices with their start and end apart: 24 -> 22, of which waited for: 17 -> 14; matrix products, arithmetic and copies ran while one was open for 1% -> 2% of each run, Pallas kernels for 19% -> 17%
where the time goes in v3:
time: 252 us
  waiting for transfers between devices  125 us (50%)
  Pallas kernels  67.6 us (27%)
  starting transfers between devices  46.9 us (19%)
  local copies, waits for them, and re-layouts  7.19 us (3%)
  other arithmetic  4.55 us (2%)
    ppermute x20, waiting for transfers between devices, swapped(): return lax.ppermute(array, axis, pairs)  121 us
    ppermute x20, starting transfers between devices, swapped(): return lax.ppermute(array, axis, pairs)  36.6 us
    pallas_call x4, Pallas kernels, gate_part(): pl.pallas_call(functools.partial(gate_kernel, counts, last), grid_spec=pl...  36.4 us
    pallas_call x4, Pallas kernels, down_part(): pl.pallas_call(down_kernel, grid_spec=pltpu.PrefetchScalarGridSpec(num_sc...  24.1 us
    ppermute x2, starting transfers between devices, shifted(): return lax.ppermute(array, axis, pairs)  10.3 us
    unnamed x28, local copies, waits for them, and re-layouts  6.01 us
  transfers between devices with their start and end apart: 22, of which 14 were waited for; matrix products, arithmetic and copies ran while one was open for 2% of the time, Pallas kernels for 17%

profile of v3, /device:TPU:0, one launch (start us, length us, event | category | flops | bytes accessed | tf_op | source)
XLA Modules:
  0.0 251.8 jit_solution(12611102155157367388)
XLA Ops:
  0.0 1.0 copy-done.2
  1.0 1.0 copy-done.3
  2.0 0.7 copy-done.12
  2.7 1.0 shard_map.109
  3.7 4.9 %collective-permute-start = (bf16[784,128]{1,0:T(8,128)(2,1)S(1)}, bf16[784,128]{1,0:T(8,128)(2,1)S(1)}, u32[]{:S(2)}, u32[]{:S(2)}) collective-permute-start(bf16[784,128]{1,0:T(8,128)(2,1)S(1)} %get-tuple-element.39), channel_id=1, source_target_pairs={{0,8},{8,16},{16,24},{1,9},{9,17},{17,25},{2,10},{10,18},{18,26},{... | collective-permute-start | bytes 602120 | tf_op jit(solution)/shard_map/ppermute | solution.py:26
  8.7 0.7 reshape.44.gain_ref
  9.4 1.0 copy-done
  10.4 1.4 shard_map.110.intra_ref
  11.8 1.1 collective-permute-done
  13.0 0.2 concatenate.3
  13.2 5.4 %collective-permute-start.1 = (bf16[784,128]{1,0:T(8,128)(2,1)S(1)}, bf16[784,128]{1,0:T(8,128)(2,1)S(1)}, u32[]{:S(2)}, u32[]{:S(2)}) collective-permute-start(bf16[784,128]{1,0:T(8,128)(2,1)S(1)} %concatenate.3), channel_id=1, source_target_pairs={{0,16},{8,24},{1,17},{9,25},{2,18},{10,26},{3,19},{11,27},{4,20},{... | collective-permute-start | bytes 602120 | tf_op jit(solution)/shard_map/ppermute | solution.py:26
  18.6 3.3 %collective-permute-done.1 = bf16[784,128]{1,0:T(8,128)(2,1)S(1)} collective-permute-done((bf16[784,128]{1,0:T(8,128)(2,1)S(1)}, bf16[784,128]{1,0:T(8,128)(2,1)S(1)}, u32[]{:S(2)}, u32[]{:S(2)}) %collective-permute-start.1) | collective-permute-done | bytes 200736 | tf_op jit(solution)/shard_map/ppermute | solution.py:26
  22.1 0.9 shard_map.111.refs_0_
  22.9 3.5 %collective-permute-start.2 = (bf16[272,768]{1,0:T(8,128)(2,1)S(1)}, bf16[272,768]{1,0:T(8,128)(2,1)S(1)}, u32[]{:S(2)}, u32[]{:S(2)}) collective-permute-start(bf16[272,768]{1,0:T(8,128)(2,1)S(1)} %shard_map.111.refs_0_), channel_id=1, source_target_pairs={{0,16},{8,24},{16,0},{24,8},{1,17},{9,25},{17,1},{25,9},{2,18},{10... | collective-permute-start | bytes 1253384 | tf_op jit(solution)/shard_map/ppermute | solution.py:405
  26.4 7.8 %collective-permute-done.2.refs_1_ = bf16[272,768]{1,0:T(8,128)(2,1)S(1)} collective-permute-done((bf16[272,768]{1,0:T(8,128)(2,1)S(1)}, bf16[272,768]{1,0:T(8,128)(2,1)S(1)}, u32[]{:S(2)}, u32[]{:S(2)}) %collective-permute-start.2) | collective-permute-done | bytes 417824 | tf_op jit(solution)/shard_map/ppermute | solution.py:405
  34.3 0.8 shard_map.112
  35.1 1.6 collective-permute-start.3
  36.7 10.5 %collective-permute-done.3 = bf16[768,512]{1,0:T(8,128)(2,1)S(1)} collective-permute-done((bf16[768,512]{1,0:T(8,128)(2,1)S(1)}, bf16[768,512]{1,0:T(8,128)(2,1)S(1)}, u32[]{:S(2)}, u32[]{:S(2)}) %collective-permute-start.3) | collective-permute-done | bytes 786464 | tf_op jit(solution)/shard_map/ppermute | solution.py:405
  47.1 0.1 pad_maximum_fusion.refs_0_
  47.4 1.6 collective-permute-start.4
  49.0 16.6 %collective-permute-start.6 = (bf16[272,768]{1,0:T(8,128)(2,1)S(1)}, bf16[272,768]{1,0:T(8,128)(2,1)S(1)}, u32[]{:S(2)}, u32[]{:S(2)}) collective-permute-start(bf16[272,768]{1,0:T(8,128)(2,1)S(1)} %shard_map.111.refs_0_), channel_id=1, source_target_pairs={{0,8},{8,0},{16,24},{24,16},{1,9},{9,1},{17,25},{25,17},{2,10},{10... | collective-permute-start | bytes 1253384 | tf_op jit(solution)/shard_map/ppermute | solution.py:405
  65.6 2.1 collective-permute-start.7
  67.7 7.9 %collective-permute-done.6.refs_0_ = bf16[272,768]{1,0:T(8,128)(2,1)S(1)} collective-permute-done((bf16[272,768]{1,0:T(8,128)(2,1)S(1)}, bf16[272,768]{1,0:T(8,128)(2,1)S(1)}, u32[]{:S(2)}, u32[]{:S(2)}) %collective-permute-start.6) | collective-permute-done | bytes 417824 | tf_op jit(solution)/shard_map/ppermute | solution.py:405
  75.6 11.1 %collective-permute-done.7.refs_1_ = bf16[272,768]{1,0:T(8,128)(2,1)S(1)} collective-permute-done((bf16[272,768]{1,0:T(8,128)(2,1)S(1)}, bf16[272,768]{1,0:T(8,128)(2,1)S(1)}, u32[]{:S(2)}, u32[]{:S(2)}) %collective-permute-start.7) | collective-permute-done | bytes 417824 | tf_op jit(solution)/shard_map/ppermute | solution.py:405
  86.6 1.7 shard_map.113
  88.3 0.8 copy-done.8
  89.1 9.4 %shard_map.114 = (f32[2,576,256]{2,1,0:T(8,128)S(1)}, f32[2,576,256]{2,1,0:T(8,128)S(1)}, f32[2,512]{1,0:T(2,128)S(1)}) custom-call(s32[4]{0:T(128)S(1)} %pad_add_fusion.2.plan_ref, bf16[2,768,512]{2,1,0:T(8,128)(2,1)S(1)} %pad_maximum_fusion.refs_0_, bf16[2,768,512]{2,1,0:T(8,128)(2,1)} %collective-permute-done.5.refs_1_, bf16[8,2,768]{2,1,0:T(2,128)(2,1)S(1)} %bitcast.45, ...), custom_call_target="tpu_custom_call" | custom-call | flops 3623878656 | bytes 14155776 | tf_op jit(solution)/shard_map/pallas_call | solution.py:341
  98.5 1.0 copy-done.4
  99.5 0.5 collective-permute-start.9
  100.1 0.1 add_add_fusion
  100.1 11.7 %collective-permute-done.9 = bf16[768,512]{1,0:T(8,128)(2,1)} collective-permute-done((bf16[768,512]{1,0:T(8,128)(2,1)}, bf16[768,512]{1,0:T(8,128)(2,1)}, u32[]{:S(2)}, u32[]{:S(2)}) %collective-permute-start.9) | collective-permute-done | bytes 786464 | tf_op jit(solution)/shard_map/ppermute | solution.py:405
  111.8 1.6 pad_maximum_fusion.1.refs_0_
  113.5 0.1 copy-done.5
  113.6 9.3 %shard_map.115.hidden_ref = bf16[2,256,576]{2,1,0:T(8,128)(2,1)S(1)} custom-call(s32[4]{0:T(128)S(1)} %get-tuple-element.74.plan_ref, bf16[2,768,512]{2,1,0:T(8,128)(2,1)} %collective-permute-done.4.refs_0_, bf16[2,768,512]{2,1,0:T(8,128)(2,1)S(1)} %collective-permute-done.8.refs_1_, bf16[8,2,768]{2,1,0:T(2,128)(2,1)S(1)} %bitcast.46, ...), custom_call_target="tpu_custom_call" | custom-call | flops 3623878656 | bytes 14155776 | tf_op jit(solution)/shard_map/pallas_call | solution.py:341
  122.9 6.0 %shard_map.116 = bf16[4,512,768]{2,1,0:T(8,128)(2,1)S(1)} custom-call(s32[4]{0:T(128)S(1)} %get-tuple-element.75.plan_ref, bf16[2,256,576]{2,1,0:T(8,128)(2,1)S(1)} %shard_map.115.hidden_ref, bf16[2,576,6144]{2,1,0:T(8,128)(2,1)} %down_ref.7), custom_call_target="tpu_custom_call" | custom-call | flops 1811939328 | bytes 7077888 | tf_op jit(solution)/shard_map/pallas_call | solution.py:377
  129.0 0.5 collective-permute-start.15
  129.5 0.9 collective-permute-start.14
  130.5 6.0 %shard_map.117 = bf16[4,512,768]{2,1,0:T(8,128)(2,1)S(1)} custom-call(s32[4]{0:T(128)S(1)} %pad_add_fusion.plan_ref, bf16[2,256,576]{2,1,0:T(8,128)(2,1)S(1)} %shard_map.115.hidden_ref, bf16[2,576,6144]{2,1,0:T(8,128)(2,1)} %down_ref.7), custom_call_target="tpu_custom_call" | custom-call | flops 1811939328 | bytes 7077888 | tf_op jit(solution)/shard_map/pallas_call | solution.py:377
  136.5 0.4 add_convert_fusion.1
  136.9 8.7 %shard_map.119 = (f32[2,576,256]{2,1,0:T(8,128)S(1)}, f32[2,576,256]{2,1,0:T(8,128)S(1)}, f32[2,512]{1,0:T(2,128)S(1)}) custom-call(s32[4]{0:T(128)S(1)} %pad_add_fusion.2.plan_ref, bf16[2,768,512]{2,1,0:T(8,128)(2,1)S(1)} %pad_maximum_fusion.1.refs_0_, bf16[2,768,512]{2,1,0:T(8,128)(2,1)S(1)} %collective-permute-done.15.refs_1_, ...), custom_call_target="tpu_custom_call" | custom-call | flops 3623878656 | bytes 14155776 | tf_op jit(solution)/shard_map/pallas_call | solution.py:341
  145.6 4.3 %collective-permute-done.14.refs_0_ = bf16[2,768,512]{2,1,0:T(8,128)(2,1)S(1)} collective-permute-done((bf16[2,768,512]{2,1,0:T(8,128)(2,1)S(1)}, bf16[2,768,512]{2,1,0:T(8,128)(2,1)S(1)}, u32[]{:S(2)}, u32[]{:S(2)}) %collective-permute-start.14) | collective-permute-done | bytes 1572896 | tf_op jit(solution)/shard_map/ppermute | solution.py:405
  149.9 0.9 collective-permute-start.11
  150.8 2.5 %collective-permute-done.16.refs_1_ = bf16[2,768,512]{2,1,0:T(8,128)(2,1)S(1)} collective-permute-done((bf16[2,768,512]{2,1,0:T(8,128)(2,1)S(1)}, bf16[2,768,512]{2,1,0:T(8,128)(2,1)S(1)}, u32[]{:S(2)}, u32[]{:S(2)}) %collective-permute-start.16) | collective-permute-done | bytes 1572896 | tf_op jit(solution)/shard_map/ppermute | solution.py:405
  153.3 9.1 %shard_map.120.hidden_ref = bf16[2,256,576]{2,1,0:T(8,128)(2,1)S(1)} custom-call(s32[4]{0:T(128)S(1)} %get-tuple-element.74.plan_ref, bf16[2,768,512]{2,1,0:T(8,128)(2,1)S(1)} %collective-permute-done.14.refs_0_, bf16[2,768,512]{2,1,0:T(8,128)(2,1)S(1)} %collective-permute-done.16.refs_1_, bf16[8,2,768]{2,1,0:T(2,128)(2,1)S(1)} %bitcast.48, ...), custom_call_target="tpu_custom_call" | custom-call | flops 3623878656 | bytes 14155776 | tf_op jit(solution)/shard_map/pallas_call | solution.py:341
  162.4 8.0 %collective-permute-done.11 = bf16[2,512,768]{2,1,0:T(8,128)(2,1)S(1)} collective-permute-done((bf16[2,512,768]{2,1,0:T(8,128)(2,1)S(1)}, bf16[2,512,768]{2,1,0:T(8,128)(2,1)S(1)}, u32[]{:S(2)}, u32[]{:S(2)}) %collective-permute-start.11) | collective-permute-done | bytes 1572896 | tf_op jit(solution)/shard_map/ppermute | solution.py:405
  170.3 6.0 %shard_map.121 = bf16[4,512,768]{2,1,0:T(8,128)(2,1)S(1)} custom-call(s32[4]{0:T(128)S(1)} %get-tuple-element.75.plan_ref, bf16[2,256,576]{2,1,0:T(8,128)(2,1)S(1)} %shard_map.120.hidden_ref, bf16[2,576,6144]{2,1,0:T(8,128)(2,1)} %down_ref.7), custom_call_target="tpu_custom_call" | custom-call | flops 1811939328 | bytes 7077888 | tf_op jit(solution)/shard_map/pallas_call | solution.py:377
  176.4 6.0 %shard_map.122 = bf16[4,512,768]{2,1,0:T(8,128)(2,1)S(1)} custom-call(s32[4]{0:T(128)S(1)} %pad_add_fusion.plan_ref, bf16[2,256,576]{2,1,0:T(8,128)(2,1)S(1)} %shard_map.120.hidden_ref, bf16[2,576,6144]{2,1,0:T(8,128)(2,1)} %down_ref.7), custom_call_target="tpu_custom_call" | custom-call | flops 1811939328 | bytes 7077888 | tf_op jit(solution)/shard_map/pallas_call | solution.py:377
  182.5 0.4 add_convert_fusion
  182.9 1.0 collective-permute-start.18
  184.0 0.3 fusion
  184.3 1.2 collective-permute-start.12
  185.5 26.3 %collective-permute-done.18 = bf16[2,512,768]{2,1,0:T(8,128)(2,1)S(1)} collective-permute-done((bf16[2,512,768]{2,1,0:T(8,128)(2,1)S(1)}, bf16[2,512,768]{2,1,0:T(8,128)(2,1)S(1)}, u32[]{:S(2)}, u32[]{:S(2)}) %collective-permute-start.18) | collective-permute-done | bytes 1572896 | tf_op jit(solution)/shard_map/ppermute | solution.py:405
  211.8 0.3 fusion.1
  212.1 0.6 collective-permute-start.19
  212.8 0.4 copy-done.7
  213.2 0.7 shard_map.118
  213.9 2.0 collective-permute-start.13
  216.0 8.2 %collective-permute-done.19.refs_3_ = bf16[512,768]{1,0:T(8,128)(2,1)S(1)} collective-permute-done((bf16[512,768]{1,0:T(8,128)(2,1)S(1)}, bf16[512,768]{1,0:T(8,128)(2,1)S(1)}, u32[]{:S(2)}, u32[]{:S(2)}) %collective-permute-start.19) | collective-permute-done | bytes 786464 | tf_op jit(solution)/shard_map/ppermute | solution.py:405
  224.2 0.7 shard_map.123
  224.9 0.8 collective-permute-start.20
  225.7 2.6 %collective-permute-start.21 = (bf16[256,768]{1,0:T(8,128)(2,1)S(1)}, bf16[256,768]{1,0:T(8,128)(2,1)S(1)}, u32[]{:S(2)}, u32[]{:S(2)}) collective-permute-start(bf16[256,768]{1,0:T(8,128)(2,1)S(1)} %get-tuple-element.70), channel_id=1, source_target_pairs={{0,24},{8,16},{16,8},{24,0},{1,25},{9,17},{17,9},{25,1},{2,26},{10... | collective-permute-start | bytes 1179656 | tf_op jit(solution)/shard_map/ppermute | solution.py:405
  228.3 6.6 %collective-permute-done.13 = bf16[256,768]{1,0:T(8,128)(2,1)S(1)} collective-permute-done((bf16[256,768]{1,0:T(8,128)(2,1)S(1)}, bf16[256,768]{1,0:T(8,128)(2,1)S(1)}, u32[]{:S(2)}, u32[]{:S(2)}) %collective-permute-start.13) | collective-permute-done | bytes 393248 | tf_op jit(solution)/shard_map/ppermute | solution.py:405
  235.0 15.8 %collective-permute-done.20 = bf16[256,768]{1,0:T(8,128)(2,1)S(1)} collective-permute-done((bf16[256,768]{1,0:T(8,128)(2,1)S(1)}, bf16[256,768]{1,0:T(8,128)(2,1)S(1)}, u32[]{:S(2)}, u32[]{:S(2)}) %collective-permute-start.20) | collective-permute-done | bytes 393248 | tf_op jit(solution)/shard_map/ppermute | solution.py:405
  250.8 1.0 add_convert_fusion.6
  (50 shorter events, 1.0 us)
Async XLA Ops:
  0.0 1.0 copy-start.2
  1.0 1.0 copy-start.3
  2.0 0.7 copy-start.12
  3.7 9.2 %collective-permute-start = (bf16[784,128]{1,0:T(8,128)(2,1)S(1)}, bf16[784,128]{1,0:T(8,128)(2,1)S(1)}, u32[]{:S(2)}, u32[]{:S(2)}) collective-permute-start(bf16[784,128]{1,0:T(8,128)(2,1)S(1)} %get-tuple-element.39), channel_id=1, source_target_pairs={{0,8},{8,16},{16,24},{1,9},{9,17},{17,25},{2,10},{10,18},{18,26},{... | collective-permute-start | bytes 602120 | tf_op jit(solution)/shard_map/ppermute | solution.py:26
  9.4 1.0 copy-start
  11.7 10.3 %copy-start.1 = (bf16[256,768]{1,0:T(8,128)(2,1)S(1)}, bf16[256,768]{1,0:T(8,128)(2,1)}, u32[]{:S(2)}) copy-start(bf16[256,768]{1,0:T(8,128)(2,1)} %query_ref.3) | copy-start | bytes 1179652
  11.8 10.3 %copy-start.11 = (bf16[256,768]{1,0:T(8,128)(2,1)S(1)}, bf16[256,768]{1,0:T(8,128)(2,1)}, u32[]{:S(2)}) copy-start(bf16[256,768]{1,0:T(8,128)(2,1)} %residual_ref.1) | copy-start | bytes 1179652
  11.8 10.3 %copy-start.13 = (s32[256,2]{0,1:T(2,128)S(1)}, s32[256,2]{0,1:T(2,128)}, u32[]{:S(2)}) copy-start(s32[256,2]{0,1:T(2,128)} %param.17) | copy-start | bytes 6148
  13.2 8.8 %collective-permute-start.1 = (bf16[784,128]{1,0:T(8,128)(2,1)S(1)}, bf16[784,128]{1,0:T(8,128)(2,1)S(1)}, u32[]{:S(2)}, u32[]{:S(2)}) collective-permute-start(bf16[784,128]{1,0:T(8,128)(2,1)S(1)} %concatenate.3), channel_id=1, source_target_pairs={{0,16},{8,24},{1,17},{9,25},{2,18},{10,26},{3,19},{11,27},{4,20},{... | collective-permute-start | bytes 602120 | tf_op jit(solution)/shard_map/ppermute | solution.py:26
  22.9 11.3 %collective-permute-start.2 = (bf16[272,768]{1,0:T(8,128)(2,1)S(1)}, bf16[272,768]{1,0:T(8,128)(2,1)S(1)}, u32[]{:S(2)}, u32[]{:S(2)}) collective-permute-start(bf16[272,768]{1,0:T(8,128)(2,1)S(1)} %shard_map.111.refs_0_), channel_id=1, source_target_pairs={{0,16},{8,24},{16,0},{24,8},{1,17},{9,25},{17,1},{25,9},{2,18},{10... | collective-permute-start | bytes 1253384 | tf_op jit(solution)/shard_map/ppermute | solution.py:405
  35.1 12.2 %copy-start.6 = (bf16[512,512]{1,0:T(8,128)(2,1)}, bf16[512,512]{1,0:T(8,128)(2,1)S(1)}, u32[]{:S(2)}) copy-start(bf16[512,512]{1,0:T(8,128)(2,1)S(1)} %get-tuple-element.40.place_ref) | copy-start | bytes 1572868
  35.1 12.1 %collective-permute-start.3 = (bf16[768,512]{1,0:T(8,128)(2,1)S(1)}, bf16[768,512]{1,0:T(8,128)(2,1)S(1)}, u32[]{:S(2)}, u32[]{:S(2)}) collective-permute-start(bf16[768,512]{1,0:T(8,128)(2,1)S(1)} %get-tuple-element.41), channel_id=1, source_target_pairs={{0,2},{1,5},{2,0},{3,7},{4,6},{5,1},{6,4},{7,3},{8,10},{9,13},{10,... | collective-permute-start | bytes 2359304 | tf_op jit(solution)/shard_map/ppermute | solution.py:405
  47.1 42.0 %copy-start.10 = (bf16[6144,2]{0,1:T(2,128)(2,1)S(1)}, bf16[6144,2]{0,1:T(2,128)(2,1)}, u32[]{:S(2)}) copy-start(bf16[6144,2]{0,1:T(2,128)(2,1)} %param.18) | copy-start | bytes 73732
  47.3 41.8 %collective-permute-start.5 = (bf16[2,768,512]{2,1,0:T(8,128)(2,1)S(1)}, bf16[2,768,512]{2,1,0:T(8,128)(2,1)}, u32[]{:S(2)}, u32[]{:S(2)}) collective-permute-start(bf16[2,768,512]{2,1,0:T(8,128)(2,1)S(1)} %pad_maximum_fusion.refs_0_), channel_id=1, source_target_pairs={{0,1},{1,0},{2,3},{3,2},{4,5},{5,4},{6,7},{7,6},{8,9},{9,8},{10,11... | collective-permute-start | bytes 4718600 | tf_op jit(solution)/shard_map/ppermute | solution.py:405
  47.4 52.2 %collective-permute-start.4 = (bf16[2,768,512]{2,1,0:T(8,128)(2,1)S(1)}, bf16[2,768,512]{2,1,0:T(8,128)(2,1)}, u32[]{:S(2)}, u32[]{:S(2)}) collective-permute-start(bf16[2,768,512]{2,1,0:T(8,128)(2,1)S(1)} %pad_maximum_fusion.refs_0_), channel_id=1, source_target_pairs={{0,4},{1,3},{2,6},{3,1},{4,0},{5,7},{6,2},{7,5},{8,12},{9,11},{10,... | collective-permute-start | bytes 4718600 | tf_op jit(solution)/shard_map/ppermute | solution.py:405
  49.0 26.6 %collective-permute-start.6 = (bf16[272,768]{1,0:T(8,128)(2,1)S(1)}, bf16[272,768]{1,0:T(8,128)(2,1)S(1)}, u32[]{:S(2)}, u32[]{:S(2)}) collective-permute-start(bf16[272,768]{1,0:T(8,128)(2,1)S(1)} %shard_map.111.refs_0_), channel_id=1, source_target_pairs={{0,8},{8,0},{16,24},{24,16},{1,9},{9,1},{17,25},{25,17},{2,10},{10... | collective-permute-start | bytes 1253384 | tf_op jit(solution)/shard_map/ppermute | solution.py:405
  65.6 21.1 %collective-permute-start.7 = (bf16[272,768]{1,0:T(8,128)(2,1)S(1)}, bf16[272,768]{1,0:T(8,128)(2,1)S(1)}, u32[]{:S(2)}, u32[]{:S(2)}) collective-permute-start(bf16[272,768]{1,0:T(8,128)(2,1)S(1)} %shard_map.111.refs_0_), channel_id=1, source_target_pairs={{0,24},{8,16},{16,8},{24,0},{1,25},{9,17},{17,9},{25,1},{2,26},{10... | collective-permute-start | bytes 1253384 | tf_op jit(solution)/shard_map/ppermute | solution.py:405
  88.3 0.8 copy-start.8
  98.5 1.0 copy-start.4
  99.5 13.9 %collective-permute-start.8 = (bf16[2,768,512]{2,1,0:T(8,128)(2,1)}, bf16[2,768,512]{2,1,0:T(8,128)(2,1)S(1)}, u32[]{:S(2)}, u32[]{:S(2)}) collective-permute-start(bf16[2,768,512]{2,1,0:T(8,128)(2,1)} %collective-permute-done.4.refs_0_), channel_id=1, source_target_pairs={{0,1},{1,0},{2,3},{3,2},{4,5},{5,4},{6,7},{7,6},{8,9},{9,8},{10,11... | collective-permute-start | bytes 4718600 | tf_op jit(solution)/shard_map/ppermute | solution.py:405
  99.5 12.3 %collective-permute-start.9 = (bf16[768,512]{1,0:T(8,128)(2,1)}, bf16[768,512]{1,0:T(8,128)(2,1)}, u32[]{:S(2)}, u32[]{:S(2)}) collective-permute-start(bf16[768,512]{1,0:T(8,128)(2,1)} %get-tuple-element.43), channel_id=1, source_target_pairs={{0,2},{1,5},{2,0},{3,7},{4,6},{5,1},{6,4},{7,3},{8,10},{9,13},{10,... | collective-permute-start | bytes 2359304 | tf_op jit(solution)/shard_map/ppermute | solution.py:405
  111.8 1.7 copy-start.5
  128.9 7.6 %collective-permute-start.10 = (bf16[4,512,768]{2,1,0:T(8,128)(2,1)S(1)}, bf16[4,512,768]{2,1,0:T(8,128)(2,1)S(1)}, u32[]{:S(2)}, u32[]{:S(2)}) collective-permute-start(bf16[4,512,768]{2,1,0:T(8,128)(2,1)S(1)} %shard_map.116), channel_id=1, source_target_pairs={{0,1},{1,0},{2,3},{3,2},{4,5},{5,4},{6,7},{7,6},{8,9},{9,8},{10,11... | collective-permute-start | bytes 9437192 | tf_op jit(solution)/shard_map/ppermute | solution.py:405
  129.0 7.9 %collective-permute-start.15 = (bf16[2,768,512]{2,1,0:T(8,128)(2,1)S(1)}, bf16[2,768,512]{2,1,0:T(8,128)(2,1)S(1)}, u32[]{:S(2)}, u32[]{:S(2)}) collective-permute-start(bf16[2,768,512]{2,1,0:T(8,128)(2,1)S(1)} %pad_maximum_fusion.1.refs_0_), channel_id=1, source_target_pairs={{0,1},{1,0},{2,3},{3,2},{4,5},{5,4},{6,7},{7,6},{8,9},{9,8},{10,11... | collective-permute-start | bytes 4718600 | tf_op jit(solution)/shard_map/ppermute | solution.py:405
  129.5 20.4 %collective-permute-start.14 = (bf16[2,768,512]{2,1,0:T(8,128)(2,1)S(1)}, bf16[2,768,512]{2,1,0:T(8,128)(2,1)S(1)}, u32[]{:S(2)}, u32[]{:S(2)}) collective-permute-start(bf16[2,768,512]{2,1,0:T(8,128)(2,1)S(1)} %pad_maximum_fusion.1.refs_0_), channel_id=1, source_target_pairs={{0,4},{1,3},{2,6},{3,1},{4,0},{5,7},{6,2},{7,5},{8,12},{9,11},{10,... | collective-permute-start | bytes 4718600 | tf_op jit(solution)/shard_map/ppermute | solution.py:405
  149.9 3.4 %collective-permute-start.16 = (bf16[2,768,512]{2,1,0:T(8,128)(2,1)S(1)}, bf16[2,768,512]{2,1,0:T(8,128)(2,1)S(1)}, u32[]{:S(2)}, u32[]{:S(2)}) collective-permute-start(bf16[2,768,512]{2,1,0:T(8,128)(2,1)S(1)} %collective-permute-done.14.refs_0_), channel_id=1, source_target_pairs={{0,1},{1,0},{2,3},{3,2},{4,5},{5,4},{6,7},{7,6},{8,9},{9,8},{10,11... | collective-permute-start | bytes 4718600 | tf_op jit(solution)/shard_map/ppermute | solution.py:405
  149.9 20.4 %collective-permute-start.11 = (bf16[2,512,768]{2,1,0:T(8,128)(2,1)S(1)}, bf16[2,512,768]{2,1,0:T(8,128)(2,1)S(1)}, u32[]{:S(2)}, u32[]{:S(2)}) collective-permute-start(bf16[2,512,768]{2,1,0:T(8,128)(2,1)S(1)} %add_convert_fusion.1), channel_id=1, source_target_pairs={{0,4},{1,3},{2,6},{3,1},{4,0},{5,7},{6,2},{7,5},{8,12},{9,11},{10,... | collective-permute-start | bytes 4718600 | tf_op jit(solution)/shard_map/ppermute | solution.py:405
  176.4 6.1 %collective-permute-start.17 = (bf16[4,512,768]{2,1,0:T(8,128)(2,1)S(1)}, bf16[4,512,768]{2,1,0:T(8,128)(2,1)S(1)}, u32[]{:S(2)}, u32[]{:S(2)}) collective-permute-start(bf16[4,512,768]{2,1,0:T(8,128)(2,1)S(1)} %shard_map.121), channel_id=1, source_target_pairs={{0,1},{1,0},{2,3},{3,2},{4,5},{5,4},{6,7},{7,6},{8,9},{9,8},{10,11... | collective-permute-start | bytes 9437192 | tf_op jit(solution)/shard_map/ppermute | solution.py:405
  182.9 28.9 %collective-permute-start.18 = (bf16[2,512,768]{2,1,0:T(8,128)(2,1)S(1)}, bf16[2,512,768]{2,1,0:T(8,128)(2,1)S(1)}, u32[]{:S(2)}, u32[]{:S(2)}) collective-permute-start(bf16[2,512,768]{2,1,0:T(8,128)(2,1)S(1)} %add_convert_fusion), channel_id=1, source_target_pairs={{0,4},{1,3},{2,6},{3,1},{4,0},{5,7},{6,2},{7,5},{8,12},{9,11},{10,... | collective-permute-start | bytes 4718600 | tf_op jit(solution)/shard_map/ppermute | solution.py:405
  184.3 28.5 %collective-permute-start.12 = (bf16[512,768]{1,0:T(8,128)(2,1)S(1)}, bf16[512,768]{1,0:T(8,128)(2,1)S(1)}, u32[]{:S(2)}, u32[]{:S(2)}) collective-permute-start(bf16[512,768]{1,0:T(8,128)(2,1)S(1)} %fusion), channel_id=1, source_target_pairs={{0,2},{1,5},{2,0},{3,7},{4,6},{5,1},{6,4},{7,3},{8,10},{9,13},{10,... | collective-permute-start | bytes 2359304 | tf_op jit(solution)/shard_map/ppermute | solution.py:405
  212.1 1.0 copy-start.7
  212.1 12.1 %collective-permute-start.19 = (bf16[512,768]{1,0:T(8,128)(2,1)S(1)}, bf16[512,768]{1,0:T(8,128)(2,1)S(1)}, u32[]{:S(2)}, u32[]{:S(2)}) collective-permute-start(bf16[512,768]{1,0:T(8,128)(2,1)S(1)} %fusion.1), channel_id=1, source_target_pairs={{0,2},{1,5},{2,0},{3,7},{4,6},{5,1},{6,4},{7,3},{8,10},{9,13},{10,... | collective-permute-start | bytes 2359304 | tf_op jit(solution)/shard_map/ppermute | solution.py:405
  213.9 10.3 %copy-start.9 = (bf16[512,512]{1,0:T(8,128)(2,1)S(1)}, bf16[512,512]{1,0:T(8,128)(2,1)}, u32[]{:S(2)}) copy-start(bf16[512,512]{1,0:T(8,128)(2,1)} %copy-done.8) | copy-start | bytes 1572868
  213.9 21.1 %collective-permute-start.13 = (bf16[256,768]{1,0:T(8,128)(2,1)S(1)}, bf16[256,768]{1,0:T(8,128)(2,1)S(1)}, u32[]{:S(2)}, u32[]{:S(2)}) collective-permute-start(bf16[256,768]{1,0:T(8,128)(2,1)S(1)} %get-tuple-element.57), channel_id=1, source_target_pairs={{0,16},{8,24},{16,0},{24,8},{1,17},{9,25},{17,1},{25,9},{2,18},{10... | collective-permute-start | bytes 1179656 | tf_op jit(solution)/shard_map/ppermute | solution.py:405
  224.9 25.9 %collective-permute-start.20 = (bf16[256,768]{1,0:T(8,128)(2,1)S(1)}, bf16[256,768]{1,0:T(8,128)(2,1)S(1)}, u32[]{:S(2)}, u32[]{:S(2)}) collective-permute-start(bf16[256,768]{1,0:T(8,128)(2,1)S(1)} %get-tuple-element.69), channel_id=1, source_target_pairs={{0,8},{8,0},{16,24},{24,16},{1,9},{9,1},{17,25},{25,17},{2,10},{10... | collective-permute-start | bytes 1179656 | tf_op jit(solution)/shard_map/ppermute | solution.py:405
  225.7 25.1 %collective-permute-start.21 = (bf16[256,768]{1,0:T(8,128)(2,1)S(1)}, bf16[256,768]{1,0:T(8,128)(2,1)S(1)}, u32[]{:S(2)}, u32[]{:S(2)}) collective-permute-start(bf16[256,768]{1,0:T(8,128)(2,1)S(1)} %get-tuple-element.70), channel_id=1, source_target_pairs={{0,24},{8,16},{16,8},{24,0},{1,25},{9,17},{17,9},{25,1},{2,26},{10... | collective-permute-start | bytes 1179656 | tf_op jit(solution)/shard_map/ppermute | solution.py:405

commit v4 on v3

--- a/solution.py
+++ b/solution.py
@@ -10,7 +10,7 @@
 F32 = jnp.float32
 BF16 = jnp.bfloat16
 HIGHEST = lax.Precision.HIGHEST
-VMEM_LIMIT = 40 * 1024 * 1024
+VMEM_LIMIT = 50 * 1024 * 1024
 ID_ROWS = 16
 
 
@@ -186,92 +186,80 @@
     return incoming
 
 
-def select_kernel(capacity, choices, experts, base_ref, *refs):
-    parts, (out_ref, place_ref) = refs[:-2], refs[-2:]
-    length = parts[0].shape[0] - ID_ROWS
+def select_kernel(capacity, choices, experts, base_ref, part_ref, out_ref, place_ref):
+    length = part_ref.shape[0] - ID_ROWS
     before = lower_ones(length).astype(BF16)
     slot = lax.broadcasted_iota(jnp.int32, (capacity, length), 0).astype(F32)
-    nothing = jnp.zeros((capacity, length), BF16)
+    ids = part_ref[length:, :length].astype(F32)
     rows = []
     for j in range(experts):
         expert = (base_ref[0] + j).astype(F32)
-        for i, part in enumerate(parts):
-            ids = part[length:, :length].astype(F32)
-            chosen = ids[0:1, :] == expert
-            for choice in range(1, choices):
-                chosen = chosen | (ids[choice : choice + 1, :] == expert)
-            flag = jnp.where(chosen, 1.0, 0.0)
-            rank = lax.dot_general(
-                jnp.broadcast_to(flag, (16, length)).astype(BF16),
-                before,
-                (((1,), (1,)), ((), ())),
-                preferred_element_type=F32,
-            )[0:1, :]
-            rank = jnp.where(chosen, rank - 1.0, -1.0)
-            here = jnp.where(slot == rank, 1.0, 0.0).astype(BF16)
-            rows.append(
-                jnp.concatenate([here if k == i else nothing for k in range(len(parts))], axis=1)
-            )
+        chosen = ids[0:1, :] == expert
+        for choice in range(1, choices):
+            chosen = chosen | (ids[choice : choice + 1, :] == expert)
+        flag = jnp.where(chosen, 1.0, 0.0)
+        rank = lax.dot_general(
+            jnp.broadcast_to(flag, (16, length)).astype(BF16),
+            before,
+            (((1,), (1,)), ((), ())),
+            preferred_element_type=F32,
+        )[0:1, :]
+        rank = jnp.where(chosen, rank - 1.0, -1.0)
+        rows.append(jnp.where(slot == rank, 1.0, 0.0).astype(BF16))
     place = jnp.concatenate(rows, axis=0)
     place_ref[...] = place
-    tokens = jnp.concatenate([part[:length, :] for part in parts], axis=0)
     out_ref[...] = lax.dot_general(
-        tokens, place, (((0,), (1,)), ((), ())), preferred_element_type=F32
+        part_ref[:length, :], place, (((0,), (1,)), ((), ())), preferred_element_type=F32
     ).astype(BF16)
 
 
-def select_slots(base, parts, capacity, choices, experts):
-    rows, width = parts[0].shape
+def select_slots(base, part, capacity, choices, experts):
+    rows, width = part.shape
     length = rows - ID_ROWS
-    slots = len(parts) * experts * capacity
-    tokens = len(parts) * length
+    slots = experts * capacity
     whole = pl.BlockSpec(memory_space=pltpu.VMEM)
     return pl.pallas_call(
         functools.partial(select_kernel, capacity, choices, experts),
-        in_specs=[pl.BlockSpec(memory_space=pltpu.SMEM), *([whole] * len(parts))],
+        in_specs=[pl.BlockSpec(memory_space=pltpu.SMEM), whole],
         out_shape=(
             jax.ShapeDtypeStruct((width, slots), BF16),
-            jax.ShapeDtypeStruct((slots, tokens), BF16),
+            jax.ShapeDtypeStruct((slots, length), BF16),
         ),
         cost_estimate=pl.CostEstimate(
-            flops=2 * slots * tokens * width, bytes_accessed=4 * slots * width, transcendentals=0
-        ),
-        compiler_params=pltpu.CompilerParams(vmem_limit_bytes=VMEM_LIMIT),
-    )(base, *parts)
-
-
-def combine_kernel(length, place_ref, *refs):
-    sections = place_ref.shape[1] // length
-    shares, outs = refs[:-sections], refs[-sections:]
+            flops=2 * slots * length * width, bytes_accessed=4 * slots * width, transcendentals=0
+        ),
+        compiler_params=pltpu.CompilerParams(vmem_limit_bytes=VMEM_LIMIT),
+    )(base, part)
+
+
+def combine_kernel(place_ref, *refs):
+    shares, out_ref = refs[:-1], refs[-1]
     total = shares[0][...].astype(F32)
     for share in shares[1:]:
         total = total + share[...].astype(F32)
-    tokens = lax.dot_general(
+    out_ref[...] = lax.dot_general(
         place_ref[...], total.astype(BF16), (((0,), (0,)), ((), ())), preferred_element_type=F32
     ).astype(BF16)
-    for i, out in enumerate(outs):
-        out[...] = tokens[i * length : (i + 1) * length, :]
-
-
-def combine_slots(place, shares, length):
-    slots, tokens = place.shape
+
+
+def combine_slots(place, shares):
+    slots, length = place.shape
     width = shares[0].shape[1]
     return pl.pallas_call(
-        functools.partial(combine_kernel, length),
-        out_shape=tuple(
-            jax.ShapeDtypeStruct((length, width), BF16) for _ in range(tokens // length)
-        ),
+        combine_kernel,
+        out_shape=jax.ShapeDtypeStruct((length, width), BF16),
         cost_estimate=pl.CostEstimate(
-            flops=2 * slots * tokens * width, bytes_accessed=8 * slots * width, transcendentals=0
+            flops=2 * slots * length * width, bytes_accessed=8 * slots * width, transcendentals=0
         ),
         compiler_params=pltpu.CompilerParams(vmem_limit_bytes=VMEM_LIMIT),
     )(place, *shares)
 
 
-def gate_kernel(counts, last, plan_ref, *refs):
+def gate_kernel(counts, sections, last, plan_ref, *refs):
     step = pl.program_id(0)
     blocks = sum(counts)
-    x_refs, refs = refs[: len(counts)], refs[len(counts) :]
+    used = len(counts) * sections
+    x_refs, refs = refs[:used], refs[used:]
     router_ref, gate_ref, up_ref = refs[:3]
     refs = refs[3:]
     if last:
@@ -279,7 +267,9 @@
     else:
         gate_acc, up_acc, score_acc = refs
     experts = gate_ref.shape[0]
+    width = x_refs[0].shape[1]
     slots = gate_acc.shape[2]
+    part = slots // sections
 
     @pl.when(step == 0)
     def _():
@@ -292,21 +282,25 @@
             up_acc[...] = jnp.zeros_like(up_acc)
             score_acc[...] = jnp.zeros_like(score_acc)
 
-    x = x_refs[-1][0]
-    for i in range(len(counts) - 2, -1, -1):
-        x = jnp.where(step < sum(counts[: i + 1]), x_refs[i][0], x)
-    score_acc[...] += jnp.dot(router_ref[0], x, preferred_element_type=F32)
+    xs = []
+    for section in range(sections):
+        mine = x_refs[section * len(counts) : (section + 1) * len(counts)]
+        x = mine[-1][0]
+        for i in range(len(counts) - 2, -1, -1):
+            x = jnp.where(step < sum(counts[: i + 1]), mine[i][0], x)
+        xs.append(x)
     for j in range(experts):
-        mine = x[:, j * slots : (j + 1) * slots]
-        gate_acc[j] += jnp.dot(gate_ref[j], mine, preferred_element_type=F32)
-        up_acc[j] += jnp.dot(up_ref[j], mine, preferred_element_type=F32)
+        x = jnp.concatenate([x[:, j * part : (j + 1) * part] for x in xs], axis=1)
+        score_acc[j] += jnp.dot(router_ref[0], x, preferred_element_type=F32)
+        gate_acc[j] += jnp.dot(gate_ref[j], x, preferred_element_type=F32)
+        up_acc[j] += jnp.dot(up_ref[j], x, preferred_element_type=F32)
 
     if last:
 
         @pl.when(step == blocks - 1)
         def _():
             for j in range(experts):
-                score = score_acc[j : j + 1, j * slots : (j + 1) * slots]
+                score = score_acc[j, j : j + 1, :]
                 gate = gate_acc[j]
                 routed = gate / (1.0 + jnp.exp(-gate)) * up_acc[j]
                 routed = routed / (1.0 + jnp.exp(-score))
@@ -314,11 +308,11 @@
 
 
 def gate_part(plan, xs, router_rows, gate_rows, up_rows, sums=None):
-    counts = tuple(x.shape[0] for x in xs)
+    counts = tuple(x.shape[0] for x in xs[0])
     blocks = sum(counts)
-    _, width, total = xs[0].shape
+    _, width, total = xs[0][0].shape
     experts, units, _ = gate_rows.shape
-    slots = total // experts
+    slots = total // experts * len(xs)
     whole = pl.BlockSpec(memory_space=pltpu.VMEM)
     last = sums is not None
 
@@ -329,7 +323,7 @@
         )
 
     weight_spec = pl.BlockSpec((experts, units, width), lambda p, plan: (0, 0, plan[p]))
-    sum_shapes = [(experts, units, slots), (experts, units, slots), (experts, total)]
+    sum_shapes = [(experts, units, slots), (experts, units, slots), (experts, experts, slots)]
     if last:
         out_shape = jax.ShapeDtypeStruct((experts, slots, units), BF16)
         out_specs = whole
@@ -339,12 +333,12 @@
         out_specs = (whole, whole, whole)
         scratch = []
     return pl.pallas_call(
-        functools.partial(gate_kernel, counts, last),
+        functools.partial(gate_kernel, counts, len(xs), last),
         grid_spec=pltpu.PrefetchScalarGridSpec(
             num_scalar_prefetch=1,
             grid=(blocks,),
             in_specs=[
-                *[x_spec(i) for i in range(len(counts))],
+                *[x_spec(i) for _ in xs for i in range(len(counts))],
                 pl.BlockSpec((1, experts, width), lambda p, plan: (plan[p], 0, 0)),
                 weight_spec,
                 weight_spec,
@@ -355,25 +349,28 @@
         ),
         out_shape=out_shape,
         cost_estimate=pl.CostEstimate(
-            flops=4 * total * blocks * width * units,
+            flops=4 * experts * slots * blocks * width * units,
             bytes_accessed=4 * experts * blocks * width * units,
             transcendentals=0,
         ),
         compiler_params=pltpu.CompilerParams(vmem_limit_bytes=VMEM_LIMIT),
-    )(plan, *xs, router_rows, gate_rows, up_rows, *(sums if last else ()))
-
-
-def down_kernel(plan_ref, hidden_ref, down_ref, out_ref):
+    )(plan, *[x for section in xs for x in section], router_rows, gate_rows, up_rows, *(sums or ()))
+
+
+def down_kernel(plan_ref, hidden_ref, down_ref, *out_refs):
     experts, slots, _ = hidden_ref.shape
+    width = out_refs[0].shape[2]
+    part = slots // len(out_refs)
     for j in range(experts):
-        out_ref[0, j * slots : (j + 1) * slots, :] = jnp.dot(
-            hidden_ref[j], down_ref[j], preferred_element_type=F32
-        ).astype(BF16)
-
-
-def down_part(plan, hidden, down_weight, width):
+        share = jnp.dot(hidden_ref[j], down_ref[j], preferred_element_type=F32).astype(BF16)
+        for section, out_ref in enumerate(out_refs):
+            out_ref[0, j * part : (j + 1) * part, :] = share[section * part : (section + 1) * part]
+
+
+def down_part(plan, hidden, down_weight, width, sections):
     blocks = plan.shape[0]
     experts, slots, units = hidden.shape
+    rows = experts * slots // sections
     return pl.pallas_call(
         down_kernel,
         grid_spec=pltpu.PrefetchScalarGridSpec(
@@ -383,9 +380,9 @@
                 pl.BlockSpec(memory_space=pltpu.VMEM),
                 pl.BlockSpec((experts, units, width), lambda p, plan: (0, 0, plan[p])),
             ],
-            out_specs=pl.BlockSpec((1, experts * slots, width), lambda p, plan: (p, 0, 0)),
-        ),
-        out_shape=jax.ShapeDtypeStruct((blocks, experts * slots, width), BF16),
+            out_specs=[pl.BlockSpec((1, rows, width), lambda p, plan: (p, 0, 0))] * sections,
+        ),
+        out_shape=[jax.ShapeDtypeStruct((blocks, rows, width), BF16)] * sections,
         cost_estimate=pl.CostEstimate(
             flops=2 * experts * slots * blocks * width * units,
             bytes_accessed=2 * experts * blocks * width * units,
@@ -416,22 +413,17 @@
         self.mine = jnp.stack([me, me ^ near, me ^ far, me ^ 6])
         self.theirs = jnp.stack([other, other ^ far, other ^ near, other ^ 6])
 
+    def once(self, part):
+        return swapped(part, "exp", 2, 4)
+
     def first(self, part):
-        return jnp.stack([part, swapped(part, "exp", 2, 4)])
+        return jnp.stack([part, self.once(part)])
 
     def second(self, two):
         return swapped(two, "exp", 4, 2)
 
     def across(self, two):
         return swapped(two, "exp", 1, 1)
-
-    def scatter(self, mine, theirs):
-        got = swapped(theirs, "exp", 1, 1)
-        sent_two = added(mine[2:], got[2:])
-        got_two = swapped(sent_two, "exp", 4, 2)
-        got_one = swapped(added(added(mine[1], got[1]), got_two[1]), "exp", 2, 4)
-        return (mine[0], got[0], got_two[0], got_one), sent_two, got_two
-
 
 def on_device(
     attn_query,
@@ -464,81 +456,90 @@
     )
 
     half = groups // 2
-    chunks = [(i, i + half) for i in range(half)]
+    chunks = [(0, half)] + [(half + i, i) for i in range(1, half)]
     parts = {0: stream}
     parts[half] = swapped(stream, "seq", half, half)
     later, _ = lax.optimization_barrier((stream, parts[half]))
-    for i in range(1, half):
-        for offset in chunks[i]:
+    for chunk in chunks[1:]:
+        for offset in reversed(chunk):
             parts[offset] = swapped(later, "seq", offset, offset)
 
     capacity = 4 * length // (experts_here * groups)
+    choices = expert_ids.shape[1]
+    chosen = {
+        offset: select_slots(base, parts[offset], capacity, choices, experts_here)
+        for chunk in chunks
+        for offset in chunk
+    }
     weights = (router_rows, gate_rows, up_rows)
-    total = stream[:length].astype(F32)
     if shares == 8:
-        pieces = paired_chunks(
-            PairedPlane(),
-            [[parts[offset] for offset in chunk] for chunk in chunks],
-            base,
-            weights,
-            down_weight,
-            capacity,
-            expert_ids.shape[1],
-        )
+        pieces = paired_chunks(PairedPlane(), chunks, chosen, weights, down_weight)
     else:
         order = jnp.arange(shares, dtype=jnp.int32)
         middle = shares // 2
-        pieces = []
+        pieces = {}
         for chunk in chunks:
-            chosen, place = select_slots(
-                base, [parts[offset] for offset in chunk], capacity, expert_ids.shape[1], experts_here
+            gathered = [lax.all_gather(chosen[offset][0], "exp", axis=0) for offset in chunk]
+            sums = gate_part(order[:middle], [[x[:middle]] for x in gathered], *weights)
+            hidden = gate_part(order[middle:], [[x[middle:]] for x in gathered], *weights, sums)
+            partial = down_part(order, hidden, down_weight, width, len(chunk))
+            for offset, share in zip(chunk, partial):
+                share = lax.psum_scatter(share, "exp", scatter_dimension=0)
+                pieces[offset] = combine_slots(chosen[offset][1], [share])
+    total = stream[:length].astype(F32)
+    for offset, piece in pieces.items():
+        if offset:
+            piece = swapped(piece, "seq", offset, offset)
+        total = total + piece.astype(F32)
+    return total.astype(BF16)
+
+
+def paired_chunks(plane, chunks, chosen, weights, down_weight):
+    width = chosen[0][0].shape[0]
+    tie = lax.optimization_barrier
+    two, far_two, near, near_far = {}, {}, {}, {}
+    for chunk in chunks:
+        for offset in sorted(chunk):
+            two[offset] = plane.first(chosen[offset][0])
+            near[offset] = plane.across(two[offset])
+            far_two[offset] = plane.second(two[offset])
+            near_far[offset] = plane.across(far_two[offset])
+    pieces = {}
+    sent, got = [], []
+    for i, chunk in enumerate(chunks):
+        after = sorted(chunks[i + 1]) if i + 1 < len(chunks) else []
+        early = [[two[offset], near[offset]] for offset in chunk]
+        late = [[far_two[offset], near_far[offset]] for offset in chunk]
+        if after:
+            early, _ = tie((early, chosen[after[0]]))
+        if sent:
+            early, _ = tie((early, sent))
+        sums = gate_part(plane.early, early, *weights)
+        late, sums = tie((late, sums))
+        if after:
+            late, _ = tie((late, [two[after[0]], chosen[after[1]]]))
+        hidden = gate_part(plane.late, late, *weights, sums)
+        if after:
+            hidden, _ = tie((hidden, two[after[1]]))
+        if got:
+            hidden, _ = tie((hidden, got))
+        theirs = down_part(plane.theirs, hidden, down_weight, width, len(chunk))
+        hidden, theirs = tie((hidden, theirs))
+        mine = down_part(plane.mine, hidden, down_weight, width, len(chunk))
+        sent, got = [], []
+        for k, offset in enumerate(chunk):
+            near_share = plane.across(theirs[k])
+            two_share = added(mine[k][2:], near_share[2:])
+            sent.append(two_share)
+            if got:
+                two_share, _ = tie((two_share, got))
+            got_two = plane.second(two_share)
+            got.append(got_two)
+            one_share = added(added(mine[k][1], near_share[1]), got_two[1])
+            got_one = plane.once(one_share)
+            pieces[offset] = combine_slots(
+                chosen[offset][1], [mine[k][0], near_share[0], got_two[0], got_one]
             )
-            gathered = lax.all_gather(chosen, "exp", axis=0)
-            sums = gate_part(order[:middle], [gathered[:middle]], *weights)
-            hidden = gate_part(order[middle:], [gathered[middle:]], *weights, sums)
-            partial = down_part(order, hidden, down_weight, width)
-            share = lax.psum_scatter(partial, "exp", scatter_dimension=0)
-            pieces.append(combine_slots(place, [share], length))
-    for chunk, chunk_pieces in zip(chunks, pieces):
-        for offset, piece in zip(chunk, chunk_pieces):
-            if offset:
-                piece = swapped(piece, "seq", offset, offset)
-            total = total + piece.astype(F32)
-    return total.astype(BF16)
-
-
-def paired_chunks(plane, chunk_parts, base, weights, down_weight, capacity, choices):
-    experts = down_weight.shape[0]
-    length = chunk_parts[0][0].shape[0] - ID_ROWS
-    width = chunk_parts[0][0].shape[1]
-    tie = lax.optimization_barrier
-    chosen = [
-        select_slots(base, parts, capacity, choices, experts) for parts in chunk_parts
-    ]
-    two = [plane.first(slots) for slots, _ in chosen]
-    pieces = []
-    sent_two, got_two = None, None
-    for i, (_, place) in enumerate(chosen):
-        follows = i + 1 < len(chosen)
-        far_two = plane.second(two[i])
-        near_two = plane.across(two[i])
-        if follows:
-            near_two, _ = tie((near_two, chosen[i + 1]))
-        if sent_two is not None:
-            near_two, _ = tie((near_two, sent_two))
-        sums = gate_part(plane.early, [two[i], near_two], *weights)
-        far_two, sums = tie((far_two, sums))
-        near_far = plane.across(far_two)
-        if follows:
-            near_far, _ = tie((near_far, two[i + 1]))
-        hidden = gate_part(plane.late, [far_two, near_far], *weights, sums)
-        if got_two is not None:
-            hidden, _ = tie((hidden, got_two))
-        theirs = down_part(plane.theirs, hidden, down_weight, width)
-        hidden, theirs = tie((hidden, theirs))
-        mine = down_part(plane.mine, hidden, down_weight, width)
-        share, sent_two, got_two = plane.scatter(mine, theirs)
-        pieces.append(combine_slots(place, share, length))
     return pieces
 
 

time: 252 us -> 240 us (0.952)
  waiting for transfers between devices: 125 us -> 60 us
  starting transfers between devices: 46.9 us -> 84.4 us
  other arithmetic: 4.55 us -> 11.4 us
  Pallas kernels: 67.6 us -> 73.9 us
    ppermute x20 -> x34, waiting for transfers between devices: 121 us -> 55.5 us  [swapped(): return lax.ppermute(array, axis, pairs)]
    ppermute x20 -> x34, starting transfers between devices: 36.6 us -> 74.1 us  [swapped(): return lax.ppermute(array, axis, pairs)]
    convert_element_type x4 -> x8, other arithmetic: 1.39 us -> 7.54 us  [added(): return (left.astype(F32) + right.astype(F32)).astype(BF16)]
    pallas_call x6 -> x8, Pallas kernels: 37.8 us -> 42.8 us  [the longest x4 41.1 us: gate_part(): pl.pallas_call(functools.partial(gate_kernel, counts, len(xs), last), gri...]
    squeeze x6 -> x12, local copies, waits for them, and re-layouts: 0.31 us -> 3.31 us  [the longest x4 3.09 us: paired_chunks(): near_share[0]]
    unnamed x28 -> x38, local copies, waits for them, and re-layouts: 6.01 us -> 5.07 us
  transfers between devices with their start and end apart: 22 -> 36, of which waited for: 14 -> 14; matrix products, arithmetic and copies ran while one was open for 2% -> 6% of each run, Pallas kernels for 17% -> 21%
where the time goes in v4:
time: 240 us; the launch traced here: 239 us
  starting transfers between devices  84.4 us (35%)
  Pallas kernels  73.9 us (31%)
  waiting for transfers between devices  60 us (25%)
  other arithmetic  11.4 us (5%)
  local copies, waits for them, and re-layouts  9.24 us (4%)
    ppermute x34, starting transfers between devices, swapped(): return lax.ppermute(array, axis, pairs)  74.1 us
    ppermute x34, waiting for transfers between devices, swapped(): return lax.ppermute(array, axis, pairs)  55.5 us
    pallas_call x4, Pallas kernels, gate_part(): pl.pallas_call(functools.partial(gate_kernel, counts, len(xs), last), gri...  41.1 us
    pallas_call x4, Pallas kernels, down_part(): pl.pallas_call(down_kernel, grid_spec=pltpu.PrefetchScalarGridSpec(num_sc...  24.4 us
    ppermute x2, starting transfers between devices, shifted(): return lax.ppermute(array, axis, pairs)  10.3 us
    convert_element_type x8, other arithmetic, added(): return (left.astype(F32) + right.astype(F32)).astype(BF16)  7.54 us
    unnamed x38, local copies, waits for them, and re-layouts  5.07 us
  transfers between devices with their start and end apart: 36, of which 14 were waited for; matrix products, arithmetic and copies ran while one was open for 6% of the time, Pallas kernels for 21%

profile of v4, /device:TPU:0, one launch (start us, length us, event | category | flops | bytes accessed | tf_op | source)
XLA Modules:
  0.0 239.4 jit_solution(14131408425539934078)
XLA Ops:
  0.0 1.0 copy-done.2
  1.0 1.0 copy-done.3
  2.0 0.7 copy-done.10
  2.7 1.0 shard_map.109
  3.7 4.9 %collective-permute-start = (bf16[784,128]{1,0:T(8,128)(2,1)S(1)}, bf16[784,128]{1,0:T(8,128)(2,1)S(1)}, u32[]{:S(2)}, u32[]{:S(2)}) collective-permute-start(bf16[784,128]{1,0:T(8,128)(2,1)S(1)} %get-tuple-element.67), channel_id=1, source_target_pairs={{0,8},{8,16},{16,24},{1,9},{9,17},{17,25},{2,10},{10,18},{18,26},{... | collective-permute-start | bytes 602120 | tf_op jit(solution)/shard_map/ppermute | solution.py:26
  8.7 0.7 reshape.60.gain_ref
  9.4 1.0 copy-done
  10.4 1.4 shard_map.110.intra_ref
  11.8 1.1 collective-permute-done
  13.2 5.4 %collective-permute-start.1 = (bf16[784,128]{1,0:T(8,128)(2,1)S(1)}, bf16[784,128]{1,0:T(8,128)(2,1)S(1)}, u32[]{:S(2)}, u32[]{:S(2)}) collective-permute-start(bf16[784,128]{1,0:T(8,128)(2,1)S(1)} %concatenate.3), channel_id=1, source_target_pairs={{0,16},{8,24},{1,17},{9,25},{2,18},{10,26},{3,19},{11,27},{4,20},{... | collective-permute-start | bytes 602120 | tf_op jit(solution)/shard_map/ppermute | solution.py:26
  18.6 3.3 %collective-permute-done.1 = bf16[784,128]{1,0:T(8,128)(2,1)S(1)} collective-permute-done((bf16[784,128]{1,0:T(8,128)(2,1)S(1)}, bf16[784,128]{1,0:T(8,128)(2,1)S(1)}, u32[]{:S(2)}, u32[]{:S(2)}) %collective-permute-start.1) | collective-permute-done | bytes 200736 | tf_op jit(solution)/shard_map/ppermute | solution.py:26
  22.1 0.9 shard_map.111.part_ref
  22.9 3.5 %collective-permute-start.5 = (bf16[272,768]{1,0:T(8,128)(2,1)S(1)}, bf16[272,768]{1,0:T(8,128)(2,1)S(1)}, u32[]{:S(2)}, u32[]{:S(2)}) collective-permute-start(bf16[272,768]{1,0:T(8,128)(2,1)S(1)} %shard_map.111.part_ref), channel_id=1, source_target_pairs={{0,16},{8,24},{16,0},{24,8},{1,17},{9,25},{17,1},{25,9},{2,18},{10... | collective-permute-start | bytes 1253384 | tf_op jit(solution)/shard_map/ppermute | solution.py:402
  26.9 1.6 collective-permute-start.2
  28.5 5.8 %collective-permute-done.5.part_ref = bf16[272,768]{1,0:T(8,128)(2,1)S(1)} collective-permute-done((bf16[272,768]{1,0:T(8,128)(2,1)S(1)}, bf16[272,768]{1,0:T(8,128)(2,1)S(1)}, u32[]{:S(2)}, u32[]{:S(2)}) %collective-permute-start.5) | collective-permute-done | bytes 417824 | tf_op jit(solution)/shard_map/ppermute | solution.py:402
  34.8 0.6 copy-done.6
  35.4 1.5 collective-permute-start.6
  37.0 1.6 collective-permute-start.3
  38.6 16.6 %collective-permute-start.11 = (bf16[272,768]{1,0:T(8,128)(2,1)S(1)}, bf16[272,768]{1,0:T(8,128)(2,1)S(1)}, u32[]{:S(2)}, u32[]{:S(2)}) collective-permute-start(bf16[272,768]{1,0:T(8,128)(2,1)S(1)} %shard_map.111.part_ref), channel_id=1, source_target_pairs={{0,8},{8,0},{16,24},{24,16},{1,9},{9,1},{17,25},{25,17},{2,10},{10... | collective-permute-start | bytes 1253384 | tf_op jit(solution)/shard_map/ppermute | solution.py:402
  55.3 0.6 collective-permute-start.7
  55.8 12.0 %collective-permute-start.13 = (bf16[272,768]{1,0:T(8,128)(2,1)S(1)}, bf16[272,768]{1,0:T(8,128)(2,1)S(1)}, u32[]{:S(2)}, u32[]{:S(2)}) collective-permute-start(bf16[272,768]{1,0:T(8,128)(2,1)S(1)} %shard_map.111.part_ref), channel_id=1, source_target_pairs={{0,24},{8,16},{16,8},{24,0},{1,25},{9,17},{17,9},{25,1},{2,26},{10... | collective-permute-start | bytes 1253384 | tf_op jit(solution)/shard_map/ppermute | solution.py:402
  67.8 1.2 shard_map.114
  69.0 1.5 collective-permute-start.12
  70.5 4.2 %collective-permute-done.13.part_ref = bf16[272,768]{1,0:T(8,128)(2,1)S(1)} collective-permute-done((bf16[272,768]{1,0:T(8,128)(2,1)S(1)}, bf16[272,768]{1,0:T(8,128)(2,1)S(1)}, u32[]{:S(2)}, u32[]{:S(2)}) %collective-permute-start.13) | collective-permute-done | bytes 417824 | tf_op jit(solution)/shard_map/ppermute | solution.py:402
  74.7 1.2 shard_map.116
  76.0 0.7 copy-done.8
  76.7 0.6 collective-permute-start.14
  78.1 1.2 pad_maximum_fusion.2.refs_2_
  79.3 5.4 %collective-permute-done.14 = bf16[768,256]{1,0:T(8,128)(2,1)S(1)} collective-permute-done((bf16[768,256]{1,0:T(8,128)(2,1)}, bf16[768,256]{1,0:T(8,128)(2,1)S(1)}, u32[]{:S(2)}, u32[]{:S(2)}) %collective-permute-start.14) | collective-permute-done | bytes 393248 | tf_op jit(solution)/shard_map/ppermute | solution.py:402
  84.6 1.1 pad_maximum_fusion.3.refs_0_
  85.7 10.7 %shard_map.115 = (f32[2,576,256]{2,1,0:T(8,128)}, f32[2,576,256]{2,1,0:T(8,128)}, f32[2,2,256]{2,1,0:T(2,128)S(1)}) custom-call(s32[4]{0:T(128)S(1)} %get-tuple-element.131.plan_ref, bf16[2,768,256]{2,1,0:T(8,128)(2,1)S(1)} %pad_maximum_fusion.refs_0_, bf16[2,768,256]{2,1,0:T(8,128)(2,1)} %collective-permute-done.9.refs_1_, ...), custom_call_target="tpu_custom_call" | custom-call | flops 3623878656 | bytes 14155776 | tf_op jit(solution)/shard_map/pallas_call | solution.py:335
  96.5 10.5 %shard_map.117.hidden_ref = bf16[2,256,576]{2,1,0:T(8,128)(2,1)S(1)} custom-call(s32[4]{0:T(128)S(1)} %add_add_fusion.plan_ref, bf16[2,768,256]{2,1,0:T(8,128)(2,1)S(1)} %collective-permute-done.3.refs_0_, bf16[2,768,256]{2,1,0:T(8,128)(2,1)S(1)} %collective-permute-done.4.refs_1_, bf16[2,768,256]{2,1,0:T(8,128)(2,1)} %collective-permute-done.7.refs_2_, ...), custom_call_target="tpu_custom_call" | custom-call | flops 3623878656 | bytes 14155776 | tf_op jit(solution)/shard_map/pallas_call | solution.py:335
  107.0 6.0 %shard_map.118 = (bf16[4,256,768]{2,1,0:T(8,128)(2,1)S(1)}, bf16[4,256,768]{2,1,0:T(8,128)(2,1)S(1)}) custom-call(s32[4]{0:T(128)S(1)} %add_add_fusion.1.plan_ref, bf16[2,256,576]{2,1,0:T(8,128)(2,1)S(1)} %shard_map.117.hidden_ref, bf16[2,576,6144]{2,1,0:T(8,128)(2,1)} %down_ref.7), custom_call_target="tpu_custom_call" | custom-call | flops 1811939328 | bytes 7077888 | tf_op jit(solution)/shard_map/pallas_call | solution.py:374
  114.1 1.5 collective-permute-start.22
  115.7 6.0 %shard_map.119 = (bf16[4,256,768]{2,1,0:T(8,128)(2,1)S(1)}, bf16[4,256,768]{2,1,0:T(8,128)(2,1)S(1)}) custom-call(s32[4]{0:T(128)S(1)} %get-tuple-element.130.plan_ref, bf16[2,256,576]{2,1,0:T(8,128)(2,1)S(1)} %shard_map.117.hidden_ref, bf16[2,576,6144]{2,1,0:T(8,128)(2,1)} %down_ref.7), custom_call_target="tpu_custom_call" | custom-call | flops 1811939328 | bytes 7077888 | tf_op jit(solution)/shard_map/pallas_call | solution.py:374
  121.9 0.6 collective-permute-start.16
  122.5 3.1 %collective-permute-done.24.refs_2_ = bf16[2,768,256]{2,1,0:T(8,128)(2,1)S(1)} collective-permute-done((bf16[2,768,256]{2,1,0:T(8,128)(2,1)S(1)}, bf16[2,768,256]{2,1,0:T(8,128)(2,1)S(1)}, u32[]{:S(2)}, u32[]{:S(2)}) %collective-permute-start.24) | collective-permute-done | bytes 786464 | tf_op jit(solution)/shard_map/ppermute | solution.py:402
  125.6 8.4 %collective-permute-done.22.refs_0_ = bf16[2,768,256]{2,1,0:T(8,128)(2,1)S(1)} collective-permute-done((bf16[2,768,256]{2,1,0:T(8,128)(2,1)S(1)}, bf16[2,768,256]{2,1,0:T(8,128)(2,1)S(1)}, u32[]{:S(2)}, u32[]{:S(2)}) %collective-permute-start.22) | collective-permute-done | bytes 786464 | tf_op jit(solution)/shard_map/ppermute | solution.py:402
  134.6 1.3 add_convert_fusion.2
  135.9 6.6 %collective-permute-done.16 = bf16[2,256,768]{2,1,0:T(8,128)(2,1)S(1)} collective-permute-done((bf16[2,256,768]{2,1,0:T(8,128)(2,1)S(1)}, bf16[2,256,768]{2,1,0:T(8,128)(2,1)S(1)}, u32[]{:S(2)}, u32[]{:S(2)}) %collective-permute-start.16) | collective-permute-done | bytes 786464 | tf_op jit(solution)/shard_map/ppermute | solution.py:402
  143.0 10.0 %shard_map.122 = (f32[2,576,256]{2,1,0:T(8,128)}, f32[2,576,256]{2,1,0:T(8,128)}, f32[2,2,256]{2,1,0:T(2,128)S(1)}) custom-call(s32[4]{0:T(128)S(1)} %get-tuple-element.131.plan_ref, bf16[2,768,256]{2,1,0:T(8,128)(2,1)S(1)} %pad_maximum_fusion.3.refs_0_, bf16[2,768,256]{2,1,0:T(8,128)(2,1)S(1)} %collective-permute-done.26.refs_1_, ...), custom_call_target="tpu_custom_call" | custom-call | flops 3623878656 | bytes 14155776 | tf_op jit(solution)/shard_map/pallas_call | solution.py:335
  153.0 9.8 %shard_map.123.hidden_ref = bf16[2,256,576]{2,1,0:T(8,128)(2,1)S(1)} custom-call(s32[4]{0:T(128)S(1)} %add_add_fusion.plan_ref, bf16[2,768,256]{2,1,0:T(8,128)(2,1)S(1)} %collective-permute-done.22.refs_0_, bf16[2,768,256]{2,1,0:T(8,128)(2,1)S(1)} %collective-permute-done.23.refs_1_, bf16[2,768,256]{2,1,0:T(8,128)(2,1)S(1)} %collective-permute-done.24.refs_2_, ...), custom_call_target="tpu_custom_call" | custom-call | flops 3623878656 | bytes 14155776 | tf_op jit(solution)/shard_map/pallas_call | solution.py:335
  162.9 6.0 %shard_map.124 = (bf16[4,256,768]{2,1,0:T(8,128)(2,1)S(1)}, bf16[4,256,768]{2,1,0:T(8,128)(2,1)S(1)}) custom-call(s32[4]{0:T(128)S(1)} %add_add_fusion.1.plan_ref, bf16[2,256,576]{2,1,0:T(8,128)(2,1)S(1)} %shard_map.123.hidden_ref, bf16[2,576,6144]{2,1,0:T(8,128)(2,1)} %down_ref.7), custom_call_target="tpu_custom_call" | custom-call | flops 1811939328 | bytes 7077888 | tf_op jit(solution)/shard_map/pallas_call | solution.py:374
  169.7 1.0 slice_bitcast_fusion.5.refs_1_
  170.7 1.9 fusion
  173.1 6.3 %shard_map.125 = (bf16[4,256,768]{2,1,0:T(8,128)(2,1)S(1)}, bf16[4,256,768]{2,1,0:T(8,128)(2,1)S(1)}) custom-call(s32[4]{0:T(128)S(1)} %get-tuple-element.130.plan_ref, bf16[2,256,576]{2,1,0:T(8,128)(2,1)S(1)} %shard_map.123.hidden_ref, bf16[2,576,6144]{2,1,0:T(8,128)(2,1)} %down_ref.7), custom_call_target="tpu_custom_call" | custom-call | flops 1811939328 | bytes 7077888 | tf_op jit(solution)/shard_map/pallas_call | solution.py:374
  179.6 1.7 collective-permute-start.29
  181.3 1.2 fusion.1
  182.5 1.5 collective-permute-start.20
  184.0 1.4 add_convert_fusion
  185.4 10.5 %collective-permute-done.29 = bf16[2,256,768]{2,1,0:T(8,128)(2,1)S(1)} collective-permute-done((bf16[2,256,768]{2,1,0:T(8,128)(2,1)S(1)}, bf16[2,256,768]{2,1,0:T(8,128)(2,1)S(1)}, u32[]{:S(2)}, u32[]{:S(2)}) %collective-permute-start.29) | collective-permute-done | bytes 786464 | tf_op jit(solution)/shard_map/ppermute | solution.py:402
  195.9 1.6 collective-permute-start.33
  198.0 7.1 %collective-permute-start.21 = (bf16[256,768]{1,0:T(8,128)(2,1)S(1)}, bf16[256,768]{1,0:T(8,128)(2,1)S(1)}, u32[]{:S(2)}, u32[]{:S(2)}) collective-permute-start(bf16[256,768]{1,0:T(8,128)(2,1)S(1)} %shard_map.121), channel_id=1, source_target_pairs={{0,16},{8,24},{16,0},{24,8},{1,17},{9,25},{17,1},{25,9},{2,18},{10... | collective-permute-start | bytes 1179656 | tf_op jit(solution)/shard_map/ppermute | solution.py:402
  205.1 1.0 slice_bitcast_fusion.1.refs_1_
  206.4 1.7 collective-permute-start.30
  208.5 1.2 fusion.3
  209.6 1.3 collective-permute-start.34
  211.0 3.2 %collective-permute-done.30.refs_3_ = bf16[256,768]{1,0:T(8,128)(2,1)S(1)} collective-permute-done((bf16[256,768]{1,0:T(8,128)(2,1)S(1)}, bf16[256,768]{1,0:T(8,128)(2,1)S(1)}, u32[]{:S(2)}, u32[]{:S(2)}) %collective-permute-start.30) | collective-permute-done | bytes 393248 | tf_op jit(solution)/shard_map/ppermute | solution.py:402
  214.6 2.7 %collective-permute-start.31 = (bf16[256,768]{1,0:T(8,128)(2,1)S(1)}, bf16[256,768]{1,0:T(8,128)(2,1)S(1)}, u32[]{:S(2)}, u32[]{:S(2)}) collective-permute-start(bf16[256,768]{1,0:T(8,128)(2,1)S(1)} %shard_map.126), channel_id=1, source_target_pairs={{0,24},{8,16},{16,8},{24,0},{1,25},{9,17},{17,9},{25,1},{2,26},{10... | collective-permute-start | bytes 1179656 | tf_op jit(solution)/shard_map/ppermute | solution.py:402
  217.4 1.1 collective-permute-done.34.refs_3_
  218.8 11.1 %collective-permute-start.35 = (bf16[256,768]{1,0:T(8,128)(2,1)S(1)}, bf16[256,768]{1,0:T(8,128)(2,1)S(1)}, u32[]{:S(2)}, u32[]{:S(2)}) collective-permute-start(bf16[256,768]{1,0:T(8,128)(2,1)S(1)} %shard_map.127), channel_id=1, source_target_pairs={{0,8},{8,0},{16,24},{24,16},{1,9},{9,1},{17,25},{25,17},{2,10},{10... | collective-permute-start | bytes 1179656 | tf_op jit(solution)/shard_map/ppermute | solution.py:402
  230.0 1.0 slice_bitcast_fusion.7.refs_1_
  232.0 6.4 %collective-permute-done.35 = bf16[256,768]{1,0:T(8,128)(2,1)S(1)} collective-permute-done((bf16[256,768]{1,0:T(8,128)(2,1)S(1)}, bf16[256,768]{1,0:T(8,128)(2,1)S(1)}, u32[]{:S(2)}, u32[]{:S(2)}) %collective-permute-start.35) | collective-permute-done | bytes 393248 | tf_op jit(solution)/shard_map/ppermute | solution.py:402
  238.4 1.0 add_convert_fusion.8
  (104 shorter events, 9.0 us)
Async XLA Ops:
  0.0 1.0 copy-start.2
  1.0 1.0 copy-start.3
  2.0 0.7 copy-start.10
  3.7 9.2 %collective-permute-start = (bf16[784,128]{1,0:T(8,128)(2,1)S(1)}, bf16[784,128]{1,0:T(8,128)(2,1)S(1)}, u32[]{:S(2)}, u32[]{:S(2)}) collective-permute-start(bf16[784,128]{1,0:T(8,128)(2,1)S(1)} %get-tuple-element.67), channel_id=1, source_target_pairs={{0,8},{8,16},{16,24},{1,9},{9,17},{17,25},{2,10},{10,18},{18,26},{... | collective-permute-start | bytes 602120 | tf_op jit(solution)/shard_map/ppermute | solution.py:26
  9.4 1.0 copy-start
  11.7 10.3 %copy-start.1 = (bf16[256,768]{1,0:T(8,128)(2,1)S(1)}, bf16[256,768]{1,0:T(8,128)(2,1)}, u32[]{:S(2)}) copy-start(bf16[256,768]{1,0:T(8,128)(2,1)} %query_ref.3) | copy-start | bytes 1179652
  11.8 10.3 %copy-start.5 = (bf16[256,768]{1,0:T(8,128)(2,1)S(1)}, bf16[256,768]{1,0:T(8,128)(2,1)}, u32[]{:S(2)}) copy-start(bf16[256,768]{1,0:T(8,128)(2,1)} %residual_ref.1) | copy-start | bytes 1179652
  11.8 10.3 %copy-start.11 = (s32[256,2]{0,1:T(2,128)S(1)}, s32[256,2]{0,1:T(2,128)}, u32[]{:S(2)}) copy-start(s32[256,2]{0,1:T(2,128)} %param.17) | copy-start | bytes 6148
  13.2 8.8 %collective-permute-start.1 = (bf16[784,128]{1,0:T(8,128)(2,1)S(1)}, bf16[784,128]{1,0:T(8,128)(2,1)S(1)}, u32[]{:S(2)}, u32[]{:S(2)}) collective-permute-start(bf16[784,128]{1,0:T(8,128)(2,1)S(1)} %concatenate.3), channel_id=1, source_target_pairs={{0,16},{8,24},{1,17},{9,25},{2,18},{10,26},{3,19},{11,27},{4,20},{... | collective-permute-start | bytes 602120 | tf_op jit(solution)/shard_map/ppermute | solution.py:26
  22.9 11.3 %collective-permute-start.5 = (bf16[272,768]{1,0:T(8,128)(2,1)S(1)}, bf16[272,768]{1,0:T(8,128)(2,1)S(1)}, u32[]{:S(2)}, u32[]{:S(2)}) collective-permute-start(bf16[272,768]{1,0:T(8,128)(2,1)S(1)} %shard_map.111.part_ref), channel_id=1, source_target_pairs={{0,16},{8,24},{16,0},{24,8},{1,17},{9,25},{17,1},{25,9},{2,18},{10... | collective-permute-start | bytes 1253384 | tf_op jit(solution)/shard_map/ppermute | solution.py:402
  26.9 10.0 %collective-permute-start.2 = (bf16[768,256]{1,0:T(8,128)(2,1)S(1)}, bf16[768,256]{1,0:T(8,128)(2,1)S(1)}, u32[]{:S(2)}, u32[]{:S(2)}) collective-permute-start(bf16[768,256]{1,0:T(8,128)(2,1)S(1)} %get-tuple-element.69), channel_id=1, source_target_pairs={{0,2},{1,5},{2,0},{3,7},{4,6},{5,1},{6,4},{7,3},{8,10},{9,13},{10,... | collective-permute-start | bytes 1179656 | tf_op jit(solution)/shard_map/ppermute | solution.py:402
  34.7 0.6 copy-start.6
  35.4 19.8 %collective-permute-start.6 = (bf16[768,256]{1,0:T(8,128)(2,1)S(1)}, bf16[768,256]{1,0:T(8,128)(2,1)S(1)}, u32[]{:S(2)}, u32[]{:S(2)}) collective-permute-start(bf16[768,256]{1,0:T(8,128)(2,1)S(1)} %get-tuple-element.70), channel_id=1, source_target_pairs={{0,2},{1,5},{2,0},{3,7},{4,6},{5,1},{6,4},{7,3},{8,10},{9,13},{10,... | collective-permute-start | bytes 1179656 | tf_op jit(solution)/shard_map/ppermute | solution.py:402
  37.0 39.7 %collective-permute-start.3 = (bf16[2,768,256]{2,1,0:T(8,128)(2,1)S(1)}, bf16[2,768,256]{2,1,0:T(8,128)(2,1)S(1)}, u32[]{:S(2)}, u32[]{:S(2)}) collective-permute-start(bf16[2,768,256]{2,1,0:T(8,128)(2,1)S(1)} %pad_maximum_fusion.refs_0_), channel_id=1, source_target_pairs={{0,4},{1,3},{2,6},{3,1},{4,0},{5,7},{6,2},{7,5},{8,12},{9,11},{10,... | collective-permute-start | bytes 2359304 | tf_op jit(solution)/shard_map/ppermute | solution.py:402
  38.6 29.2 %collective-permute-start.11 = (bf16[272,768]{1,0:T(8,128)(2,1)S(1)}, bf16[272,768]{1,0:T(8,128)(2,1)S(1)}, u32[]{:S(2)}, u32[]{:S(2)}) collective-permute-start(bf16[272,768]{1,0:T(8,128)(2,1)S(1)} %shard_map.111.part_ref), channel_id=1, source_target_pairs={{0,8},{8,0},{16,24},{24,16},{1,9},{9,1},{17,25},{25,17},{2,10},{10... | collective-permute-start | bytes 1253384 | tf_op jit(solution)/shard_map/ppermute | solution.py:402
  55.3 22.2 %collective-permute-start.7 = (bf16[2,768,256]{2,1,0:T(8,128)(2,1)S(1)}, bf16[2,768,256]{2,1,0:T(8,128)(2,1)}, u32[]{:S(2)}, u32[]{:S(2)}) collective-permute-start(bf16[2,768,256]{2,1,0:T(8,128)(2,1)S(1)} %pad_maximum_fusion.1.refs_2_), channel_id=1, source_target_pairs={{0,4},{1,3},{2,6},{3,1},{4,0},{5,7},{6,2},{7,5},{8,12},{9,11},{10,... | collective-permute-start | bytes 2359304 | tf_op jit(solution)/shard_map/ppermute | solution.py:402
  55.8 18.9 %collective-permute-start.13 = (bf16[272,768]{1,0:T(8,128)(2,1)S(1)}, bf16[272,768]{1,0:T(8,128)(2,1)S(1)}, u32[]{:S(2)}, u32[]{:S(2)}) collective-permute-start(bf16[272,768]{1,0:T(8,128)(2,1)S(1)} %shard_map.111.part_ref), channel_id=1, source_target_pairs={{0,24},{8,16},{16,8},{24,0},{1,25},{9,17},{17,9},{25,1},{2,26},{10... | collective-permute-start | bytes 1253384 | tf_op jit(solution)/shard_map/ppermute | solution.py:402
  69.0 8.3 %collective-permute-start.12 = (bf16[768,256]{1,0:T(8,128)(2,1)}, bf16[768,256]{1,0:T(8,128)(2,1)}, u32[]{:S(2)}, u32[]{:S(2)}) collective-permute-start(bf16[768,256]{1,0:T(8,128)(2,1)} %get-tuple-element.72), channel_id=1, source_target_pairs={{0,2},{1,5},{2,0},{3,7},{4,6},{5,1},{6,4},{7,3},{8,10},{9,13},{10,... | collective-permute-start | bytes 1179656 | tf_op jit(solution)/shard_map/ppermute | solution.py:402
  70.5 15.2 %collective-permute-start.9 = (bf16[2,768,256]{2,1,0:T(8,128)(2,1)S(1)}, bf16[2,768,256]{2,1,0:T(8,128)(2,1)}, u32[]{:S(2)}, u32[]{:S(2)}) collective-permute-start(bf16[2,768,256]{2,1,0:T(8,128)(2,1)S(1)} %pad_maximum_fusion.refs_0_), channel_id=1, source_target_pairs={{0,1},{1,0},{2,3},{3,2},{4,5},{5,4},{6,7},{7,6},{8,9},{9,8},{10,11... | collective-permute-start | bytes 2359304 | tf_op jit(solution)/shard_map/ppermute | solution.py:402
  74.7 11.0 %collective-permute-start.10 = (bf16[2,768,256]{2,1,0:T(8,128)(2,1)S(1)}, bf16[2,768,256]{2,1,0:T(8,128)(2,1)}, u32[]{:S(2)}, u32[]{:S(2)}) collective-permute-start(bf16[2,768,256]{2,1,0:T(8,128)(2,1)S(1)} %pad_maximum_fusion.1.refs_2_), channel_id=1, source_target_pairs={{0,1},{1,0},{2,3},{3,2},{4,5},{5,4},{6,7},{7,6},{8,9},{9,8},{10,11... | collective-permute-start | bytes 2359304 | tf_op jit(solution)/shard_map/ppermute | solution.py:402
  76.0 0.7 copy-start.8
  76.7 8.0 %collective-permute-start.14 = (bf16[768,256]{1,0:T(8,128)(2,1)}, bf16[768,256]{1,0:T(8,128)(2,1)S(1)}, u32[]{:S(2)}, u32[]{:S(2)}) collective-permute-start(bf16[768,256]{1,0:T(8,128)(2,1)} %get-tuple-element.85), channel_id=1, source_target_pairs={{0,2},{1,5},{2,0},{3,7},{4,6},{5,1},{6,4},{7,3},{8,10},{9,13},{10,... | collective-permute-start | bytes 1179656 | tf_op jit(solution)/shard_map/ppermute | solution.py:402
  77.4 19.1 %collective-permute-start.4 = (bf16[2,768,256]{2,1,0:T(8,128)(2,1)S(1)}, bf16[2,768,256]{2,1,0:T(8,128)(2,1)S(1)}, u32[]{:S(2)}, u32[]{:S(2)}) collective-permute-start(bf16[2,768,256]{2,1,0:T(8,128)(2,1)S(1)} %collective-permute-done.3.refs_0_), channel_id=1, source_target_pairs={{0,1},{1,0},{2,3},{3,2},{4,5},{5,4},{6,7},{7,6},{8,9},{9,8},{10,11... | collective-permute-start | bytes 2359304 | tf_op jit(solution)/shard_map/ppermute | solution.py:402
  77.5 19.0 %collective-permute-start.8 = (bf16[2,768,256]{2,1,0:T(8,128)(2,1)}, bf16[2,768,256]{2,1,0:T(8,128)(2,1)S(1)}, u32[]{:S(2)}, u32[]{:S(2)}) collective-permute-start(bf16[2,768,256]{2,1,0:T(8,128)(2,1)} %collective-permute-done.7.refs_2_), channel_id=1, source_target_pairs={{0,1},{1,0},{2,3},{3,2},{4,5},{5,4},{6,7},{7,6},{8,9},{9,8},{10,11... | collective-permute-start | bytes 2359304 | tf_op jit(solution)/shard_map/ppermute | solution.py:402
  78.1 7.7 %copy-start.4 = (bf16[6144,2]{0,1:T(2,128)(2,1)S(1)}, bf16[6144,2]{0,1:T(2,128)(2,1)}, u32[]{:S(2)}) copy-start(bf16[6144,2]{0,1:T(2,128)(2,1)} %param.18) | copy-start | bytes 73732
  113.0 8.7 %collective-permute-start.15 = (bf16[4,256,768]{2,1,0:T(8,128)(2,1)S(1)}, bf16[4,256,768]{2,1,0:T(8,128)(2,1)S(1)}, u32[]{:S(2)}, u32[]{:S(2)}) collective-permute-start(bf16[4,256,768]{2,1,0:T(8,128)(2,1)S(1)} %get-tuple-element.99), channel_id=1, source_target_pairs={{0,1},{1,0},{2,3},{3,2},{4,5},{5,4},{6,7},{7,6},{8,9},{9,8},{10,11... | collective-permute-start | bytes 4718600 | tf_op jit(solution)/shard_map/ppermute | solution.py:402
  113.1 20.9 %collective-permute-start.18 = (bf16[4,256,768]{2,1,0:T(8,128)(2,1)S(1)}, bf16[4,256,768]{2,1,0:T(8,128)(2,1)}, u32[]{:S(2)}, u32[]{:S(2)}) collective-permute-start(bf16[4,256,768]{2,1,0:T(8,128)(2,1)S(1)} %get-tuple-element.102), channel_id=1, source_target_pairs={{0,1},{1,0},{2,3},{3,2},{4,5},{5,4},{6,7},{7,6},{8,9},{9,8},{10,11... | collective-permute-start | bytes 4718600 | tf_op jit(solution)/shard_map/ppermute | solution.py:402
  113.6 12.0 %collective-permute-start.24 = (bf16[2,768,256]{2,1,0:T(8,128)(2,1)S(1)}, bf16[2,768,256]{2,1,0:T(8,128)(2,1)S(1)}, u32[]{:S(2)}, u32[]{:S(2)}) collective-permute-start(bf16[2,768,256]{2,1,0:T(8,128)(2,1)S(1)} %pad_maximum_fusion.2.refs_2_), channel_id=1, source_target_pairs={{0,4},{1,3},{2,6},{3,1},{4,0},{5,7},{6,2},{7,5},{8,12},{9,11},{10,... | collective-permute-start | bytes 2359304 | tf_op jit(solution)/shard_map/ppermute | solution.py:402
  114.1 19.9 %collective-permute-start.22 = (bf16[2,768,256]{2,1,0:T(8,128)(2,1)S(1)}, bf16[2,768,256]{2,1,0:T(8,128)(2,1)S(1)}, u32[]{:S(2)}, u32[]{:S(2)}) collective-permute-start(bf16[2,768,256]{2,1,0:T(8,128)(2,1)S(1)} %pad_maximum_fusion.3.refs_0_), channel_id=1, source_target_pairs={{0,4},{1,3},{2,6},{3,1},{4,0},{5,7},{6,2},{7,5},{8,12},{9,11},{10,... | collective-permute-start | bytes 2359304 | tf_op jit(solution)/shard_map/ppermute | solution.py:402
  121.7 3.9 %copy-start.12 = (bf16[4,256,768]{2,1,0:T(8,128)(2,1)}, bf16[4,256,768]{2,1,0:T(8,128)(2,1)S(1)}, u32[]{:S(2)}) copy-start(bf16[4,256,768]{2,1,0:T(8,128)(2,1)S(1)} %collective-permute-done.15) | copy-start | bytes 4718596
  121.9 20.5 %collective-permute-start.16 = (bf16[2,256,768]{2,1,0:T(8,128)(2,1)S(1)}, bf16[2,256,768]{2,1,0:T(8,128)(2,1)S(1)}, u32[]{:S(2)}, u32[]{:S(2)}) collective-permute-start(bf16[2,256,768]{2,1,0:T(8,128)(2,1)S(1)} %add_convert_fusion.3), channel_id=1, source_target_pairs={{0,4},{1,3},{2,6},{3,1},{4,0},{5,7},{6,2},{7,5},{8,12},{9,11},{10,... | collective-permute-start | bytes 2359304 | tf_op jit(solution)/shard_map/ppermute | solution.py:402
  122.5 20.5 %collective-permute-start.27 = (bf16[2,768,256]{2,1,0:T(8,128)(2,1)S(1)}, bf16[2,768,256]{2,1,0:T(8,128)(2,1)S(1)}, u32[]{:S(2)}, u32[]{:S(2)}) collective-permute-start(bf16[2,768,256]{2,1,0:T(8,128)(2,1)S(1)} %pad_maximum_fusion.2.refs_2_), channel_id=1, source_target_pairs={{0,1},{1,0},{2,3},{3,2},{4,5},{5,4},{6,7},{7,6},{8,9},{9,8},{10,11... | collective-permute-start | bytes 2359304 | tf_op jit(solution)/shard_map/ppermute | solution.py:402
  125.6 17.4 %collective-permute-start.26 = (bf16[2,768,256]{2,1,0:T(8,128)(2,1)S(1)}, bf16[2,768,256]{2,1,0:T(8,128)(2,1)S(1)}, u32[]{:S(2)}, u32[]{:S(2)}) collective-permute-start(bf16[2,768,256]{2,1,0:T(8,128)(2,1)S(1)} %pad_maximum_fusion.3.refs_0_), channel_id=1, source_target_pairs={{0,1},{1,0},{2,3},{3,2},{4,5},{5,4},{6,7},{7,6},{8,9},{9,8},{10,11... | collective-permute-start | bytes 2359304 | tf_op jit(solution)/shard_map/ppermute | solution.py:402
  134.0 19.0 %collective-permute-start.25 = (bf16[2,768,256]{2,1,0:T(8,128)(2,1)S(1)}, bf16[2,768,256]{2,1,0:T(8,128)(2,1)S(1)}, u32[]{:S(2)}, u32[]{:S(2)}) collective-permute-start(bf16[2,768,256]{2,1,0:T(8,128)(2,1)S(1)} %collective-permute-done.24.refs_2_), channel_id=1, source_target_pairs={{0,1},{1,0},{2,3},{3,2},{4,5},{5,4},{6,7},{7,6},{8,9},{9,8},{10,11... | collective-permute-start | bytes 2359304 | tf_op jit(solution)/shard_map/ppermute | solution.py:402
  134.0 19.0 %collective-permute-start.23 = (bf16[2,768,256]{2,1,0:T(8,128)(2,1)S(1)}, bf16[2,768,256]{2,1,0:T(8,128)(2,1)S(1)}, u32[]{:S(2)}, u32[]{:S(2)}) collective-permute-start(bf16[2,768,256]{2,1,0:T(8,128)(2,1)S(1)} %collective-permute-done.22.refs_0_), channel_id=1, source_target_pairs={{0,1},{1,0},{2,3},{3,2},{4,5},{5,4},{6,7},{7,6},{8,9},{9,8},{10,11... | collective-permute-start | bytes 2359304 | tf_op jit(solution)/shard_map/ppermute | solution.py:402
  142.5 20.4 %collective-permute-start.19 = (bf16[2,256,768]{2,1,0:T(8,128)(2,1)S(1)}, bf16[2,256,768]{2,1,0:T(8,128)(2,1)S(1)}, u32[]{:S(2)}, u32[]{:S(2)}) collective-permute-start(bf16[2,256,768]{2,1,0:T(8,128)(2,1)S(1)} %add_convert_fusion.2), channel_id=1, source_target_pairs={{0,4},{1,3},{2,6},{3,1},{4,0},{5,7},{6,2},{7,5},{8,12},{9,11},{10,... | collective-permute-start | bytes 2359304 | tf_op jit(solution)/shard_map/ppermute | solution.py:402
  162.9 6.1 %copy-start.15 = (bf16[2,256,768]{2,1,0:T(8,128)(2,1)}, bf16[2,256,768]{2,1,0:T(8,128)(2,1)S(1)}, u32[]{:S(2)}) copy-start(bf16[2,256,768]{2,1,0:T(8,128)(2,1)S(1)} %collective-permute-done.19) | copy-start | bytes 2359300
  169.0 10.4 %collective-permute-start.28 = (bf16[4,256,768]{2,1,0:T(8,128)(2,1)S(1)}, bf16[4,256,768]{2,1,0:T(8,128)(2,1)S(1)}, u32[]{:S(2)}, u32[]{:S(2)}) collective-permute-start(bf16[4,256,768]{2,1,0:T(8,128)(2,1)S(1)} %get-tuple-element.123), channel_id=1, source_target_pairs={{0,1},{1,0},{2,3},{3,2},{4,5},{5,4},{6,7},{7,6},{8,9},{9,8},{10,11... | collective-permute-start | bytes 4718600 | tf_op jit(solution)/shard_map/ppermute | solution.py:402
  169.1 14.9 %collective-permute-start.32 = (bf16[4,256,768]{2,1,0:T(8,128)(2,1)S(1)}, bf16[4,256,768]{2,1,0:T(8,128)(2,1)}, u32[]{:S(2)}, u32[]{:S(2)}) collective-permute-start(bf16[4,256,768]{2,1,0:T(8,128)(2,1)S(1)} %get-tuple-element.125), channel_id=1, source_target_pairs={{0,1},{1,0},{2,3},{3,2},{4,5},{5,4},{6,7},{7,6},{8,9},{9,8},{10,11... | collective-permute-start | bytes 4718600 | tf_op jit(solution)/shard_map/ppermute | solution.py:402
  172.6 58.4 %collective-permute-start.17 = (bf16[256,768]{1,0:T(8,128)(2,1)}, bf16[256,768]{1,0:T(8,128)(2,1)S(1)}, u32[]{:S(2)}, u32[]{:S(2)}) collective-permute-start(bf16[256,768]{1,0:T(8,128)(2,1)} %fusion), channel_id=1, source_target_pairs={{0,2},{1,5},{2,0},{3,7},{4,6},{5,1},{6,4},{7,3},{8,10},{9,13},{10,... | collective-permute-start | bytes 1179656 | tf_op jit(solution)/shard_map/ppermute | solution.py:402
  179.4 1.9 copy-start.16
  179.4 3.1 %copy-start.13 = (bf16[4,256,768]{2,1,0:T(8,128)(2,1)}, bf16[4,256,768]{2,1,0:T(8,128)(2,1)S(1)}, u32[]{:S(2)}) copy-start(bf16[4,256,768]{2,1,0:T(8,128)(2,1)S(1)} %collective-permute-done.28) | copy-start | bytes 4718596
  179.6 16.3 %collective-permute-start.29 = (bf16[2,256,768]{2,1,0:T(8,128)(2,1)S(1)}, bf16[2,256,768]{2,1,0:T(8,128)(2,1)S(1)}, u32[]{:S(2)}, u32[]{:S(2)}) collective-permute-start(bf16[2,256,768]{2,1,0:T(8,128)(2,1)S(1)} %add_convert_fusion.1), channel_id=1, source_target_pairs={{0,4},{1,3},{2,6},{3,1},{4,0},{5,7},{6,2},{7,5},{8,12},{9,11},{10,... | collective-permute-start | bytes 2359304 | tf_op jit(solution)/shard_map/ppermute | solution.py:402
  182.5 15.1 %collective-permute-start.20 = (bf16[256,768]{1,0:T(8,128)(2,1)S(1)}, bf16[256,768]{1,0:T(8,128)(2,1)S(1)}, u32[]{:S(2)}, u32[]{:S(2)}) collective-permute-start(bf16[256,768]{1,0:T(8,128)(2,1)S(1)} %fusion.1), channel_id=1, source_target_pairs={{0,2},{1,5},{2,0},{3,7},{4,6},{5,1},{6,4},{7,3},{8,10},{9,13},{10,... | collective-permute-start | bytes 1179656 | tf_op jit(solution)/shard_map/ppermute | solution.py:402
  184.0 13.6 %copy-start.7 = (bf16[256,256]{1,0:T(8,128)(2,1)S(1)}, bf16[256,256]{1,0:T(8,128)(2,1)}, u32[]{:S(2)}) copy-start(bf16[256,256]{1,0:T(8,128)(2,1)} %copy-done.6) | copy-start | bytes 393220
  185.4 19.7 %copy-start.14 = (bf16[4,256,768]{2,1,0:T(8,128)(2,1)S(1)}, bf16[4,256,768]{2,1,0:T(8,128)(2,1)}, u32[]{:S(2)}) copy-start(bf16[4,256,768]{2,1,0:T(8,128)(2,1)} %copy-done.13) | copy-start | bytes 4718596
  195.9 10.2 %copy-start.17 = (bf16[2,256,768]{2,1,0:T(8,128)(2,1)}, bf16[2,256,768]{2,1,0:T(8,128)(2,1)S(1)}, u32[]{:S(2)}) copy-start(bf16[2,256,768]{2,1,0:T(8,128)(2,1)S(1)} %collective-permute-done.29) | copy-start | bytes 2359300
  195.9 12.6 %collective-permute-start.33 = (bf16[2,256,768]{2,1,0:T(8,128)(2,1)S(1)}, bf16[2,256,768]{2,1,0:T(8,128)(2,1)S(1)}, u32[]{:S(2)}, u32[]{:S(2)}) collective-permute-start(bf16[2,256,768]{2,1,0:T(8,128)(2,1)S(1)} %add_convert_fusion), channel_id=1, source_target_pairs={{0,4},{1,3},{2,6},{3,1},{4,0},{5,7},{6,2},{7,5},{8,12},{9,11},{10,... | collective-permute-start | bytes 2359304 | tf_op jit(solution)/shard_map/ppermute | solution.py:402
  198.0 34.0 %collective-permute-start.21 = (bf16[256,768]{1,0:T(8,128)(2,1)S(1)}, bf16[256,768]{1,0:T(8,128)(2,1)S(1)}, u32[]{:S(2)}, u32[]{:S(2)}) collective-permute-start(bf16[256,768]{1,0:T(8,128)(2,1)S(1)} %shard_map.121), channel_id=1, source_target_pairs={{0,16},{8,24},{16,0},{24,8},{1,17},{9,25},{17,1},{25,9},{2,18},{10... | collective-permute-start | bytes 1179656 | tf_op jit(solution)/shard_map/ppermute | solution.py:402
  206.2 8.0 %copy-start.9 = (bf16[256,256]{1,0:T(8,128)(2,1)S(1)}, bf16[256,256]{1,0:T(8,128)(2,1)}, u32[]{:S(2)}) copy-start(bf16[256,256]{1,0:T(8,128)(2,1)} %copy-done.8) | copy-start | bytes 393220
  206.3 4.6 %copy-start.18 = (bf16[2,256,768]{2,1,0:T(8,128)(2,1)S(1)}, bf16[2,256,768]{2,1,0:T(8,128)(2,1)}, u32[]{:S(2)}) copy-start(bf16[2,256,768]{2,1,0:T(8,128)(2,1)} %copy-done.17) | copy-start | bytes 2359300
  206.4 7.8 %collective-permute-start.30 = (bf16[256,768]{1,0:T(8,128)(2,1)S(1)}, bf16[256,768]{1,0:T(8,128)(2,1)S(1)}, u32[]{:S(2)}, u32[]{:S(2)}) collective-permute-start(bf16[256,768]{1,0:T(8,128)(2,1)S(1)} %fusion.2), channel_id=1, source_target_pairs={{0,2},{1,5},{2,0},{3,7},{4,6},{5,1},{6,4},{7,3},{8,10},{9,13},{10,... | collective-permute-start | bytes 1179656 | tf_op jit(solution)/shard_map/ppermute | solution.py:402
  209.6 8.8 %collective-permute-start.34 = (bf16[256,768]{1,0:T(8,128)(2,1)S(1)}, bf16[256,768]{1,0:T(8,128)(2,1)S(1)}, u32[]{:S(2)}, u32[]{:S(2)}) collective-permute-start(bf16[256,768]{1,0:T(8,128)(2,1)S(1)} %fusion.3), channel_id=1, source_target_pairs={{0,2},{1,5},{2,0},{3,7},{4,6},{5,1},{6,4},{7,3},{8,10},{9,13},{10,... | collective-permute-start | bytes 1179656 | tf_op jit(solution)/shard_map/ppermute | solution.py:402
  214.6 17.4 %collective-permute-start.31 = (bf16[256,768]{1,0:T(8,128)(2,1)S(1)}, bf16[256,768]{1,0:T(8,128)(2,1)S(1)}, u32[]{:S(2)}, u32[]{:S(2)}) collective-permute-start(bf16[256,768]{1,0:T(8,128)(2,1)S(1)} %shard_map.126), channel_id=1, source_target_pairs={{0,24},{8,16},{16,8},{24,0},{1,25},{9,17},{17,9},{25,1},{2,26},{10... | collective-permute-start | bytes 1179656 | tf_op jit(solution)/shard_map/ppermute | solution.py:402
  218.8 19.6 %collective-permute-start.35 = (bf16[256,768]{1,0:T(8,128)(2,1)S(1)}, bf16[256,768]{1,0:T(8,128)(2,1)S(1)}, u32[]{:S(2)}, u32[]{:S(2)}) collective-permute-start(bf16[256,768]{1,0:T(8,128)(2,1)S(1)} %shard_map.127), channel_id=1, source_target_pairs={{0,8},{8,0},{16,24},{24,16},{1,9},{9,1},{17,25},{25,17},{2,10},{10... | collective-permute-start | bytes 1179656 | tf_op jit(solution)/shard_map/ppermute | solution.py:402

commit v5 on v4

--- a/solution.py
+++ b/solution.py
@@ -10,7 +10,7 @@
 F32 = jnp.float32
 BF16 = jnp.bfloat16
 HIGHEST = lax.Precision.HIGHEST
-VMEM_LIMIT = 50 * 1024 * 1024
+VMEM_LIMIT = 40 * 1024 * 1024
 ID_ROWS = 16
 
 
@@ -457,88 +457,98 @@
 
     half = groups // 2
     chunks = [(0, half)] + [(half + i, i) for i in range(1, half)]
-    parts = {0: stream}
-    parts[half] = swapped(stream, "seq", half, half)
-    later, _ = lax.optimization_barrier((stream, parts[half]))
-    for chunk in chunks[1:]:
-        for offset in reversed(chunk):
-            parts[offset] = swapped(later, "seq", offset, offset)
-
     capacity = 4 * length // (experts_here * groups)
     choices = expert_ids.shape[1]
-    chosen = {
-        offset: select_slots(base, parts[offset], capacity, choices, experts_here)
-        for chunk in chunks
-        for offset in chunk
-    }
+
+    def moved(part, offset):
+        return swapped(part, "seq", offset, offset)
+
+    def select(part):
+        return select_slots(base, part, capacity, choices, experts_here)
+
     weights = (router_rows, gate_rows, up_rows)
     if shares == 8:
-        pieces = paired_chunks(PairedPlane(), chunks, chosen, weights, down_weight)
+        pieces = paired_chunks(chunks, stream, moved, select, weights, down_weight)
     else:
         order = jnp.arange(shares, dtype=jnp.int32)
         middle = shares // 2
         pieces = {}
         for chunk in chunks:
-            gathered = [lax.all_gather(chosen[offset][0], "exp", axis=0) for offset in chunk]
+            chosen = [select(moved(stream, offset) if offset else stream) for offset in chunk]
+            gathered = [lax.all_gather(slots, "exp", axis=0) for slots, _ in chosen]
             sums = gate_part(order[:middle], [[x[:middle]] for x in gathered], *weights)
             hidden = gate_part(order[middle:], [[x[middle:]] for x in gathered], *weights, sums)
             partial = down_part(order, hidden, down_weight, width, len(chunk))
-            for offset, share in zip(chunk, partial):
+            for offset, share, (_, place) in zip(chunk, partial, chosen):
                 share = lax.psum_scatter(share, "exp", scatter_dimension=0)
-                pieces[offset] = combine_slots(chosen[offset][1], [share])
+                pieces[offset] = combine_slots(place, [share])
     total = stream[:length].astype(F32)
     for offset, piece in pieces.items():
         if offset:
-            piece = swapped(piece, "seq", offset, offset)
+            piece = moved(piece, offset)
         total = total + piece.astype(F32)
     return total.astype(BF16)
 
 
-def paired_chunks(plane, chunks, chosen, weights, down_weight):
-    width = chosen[0][0].shape[0]
+def paired_chunks(chunks, stream, moved, select, weights, down_weight):
+    plane = PairedPlane()
+    width = stream.shape[1]
     tie = lax.optimization_barrier
-    two, far_two, near, near_far = {}, {}, {}, {}
-    for chunk in chunks:
-        for offset in sorted(chunk):
-            two[offset] = plane.first(chosen[offset][0])
-            near[offset] = plane.across(two[offset])
-            far_two[offset] = plane.second(two[offset])
-            near_far[offset] = plane.across(far_two[offset])
+    two, far_two, near, near_far, chosen = {}, {}, {}, {}, {}
+
+    def gather(offset, part):
+        chosen[offset] = select(part)
+        two[offset] = plane.first(chosen[offset][0])
+        near[offset] = plane.across(two[offset])
+        far_two[offset] = plane.second(two[offset])
+        near_far[offset] = plane.across(far_two[offset])
+
+    gather(0, stream)
+    later, _ = tie((stream, two[0]))
+    arrived = moved(later, chunks[0][1])
+    part, _ = tie((arrived, far_two[0]))
+    gather(chunks[0][1], part)
+    later, _ = tie((stream, arrived))
+    parts = {offset: moved(later, offset) for chunk in chunks[1:] for offset in reversed(chunk)}
+
     pieces = {}
-    sent, got = [], []
+    sent, got_two, one = [], [], []
     for i, chunk in enumerate(chunks):
-        after = sorted(chunks[i + 1]) if i + 1 < len(chunks) else []
+        after = chunks[i + 1][::-1] if i + 1 < len(chunks) else ()
         early = [[two[offset], near[offset]] for offset in chunk]
         late = [[far_two[offset], near_far[offset]] for offset in chunk]
         if after:
+            gather(after[0], parts[after[0]])
             early, _ = tie((early, chosen[after[0]]))
         if sent:
             early, _ = tie((early, sent))
         sums = gate_part(plane.early, early, *weights)
         late, sums = tie((late, sums))
         if after:
+            part, _ = tie((parts[after[1]], sums))
+            gather(after[1], part)
             late, _ = tie((late, [two[after[0]], chosen[after[1]]]))
         hidden = gate_part(plane.late, late, *weights, sums)
         if after:
-            hidden, _ = tie((hidden, two[after[1]]))
-        if got:
-            hidden, _ = tie((hidden, got))
+            hidden, _ = tie((hidden, [far_two[after[0]], two[after[1]]]))
+        if one:
+            hidden, _ = tie((hidden, one))
         theirs = down_part(plane.theirs, hidden, down_weight, width, len(chunk))
         hidden, theirs = tie((hidden, theirs))
         mine = down_part(plane.mine, hidden, down_weight, width, len(chunk))
-        sent, got = [], []
+        sent, got_two, one = [], [], []
         for k, offset in enumerate(chunk):
             near_share = plane.across(theirs[k])
             two_share = added(mine[k][2:], near_share[2:])
             sent.append(two_share)
-            if got:
-                two_share, _ = tie((two_share, got))
-            got_two = plane.second(two_share)
-            got.append(got_two)
-            one_share = added(added(mine[k][1], near_share[1]), got_two[1])
+            if got_two and not after:
+                two_share, _ = tie((two_share, got_two))
+            got_two.append(plane.second(two_share))
+            one_share = added(added(mine[k][1], near_share[1]), got_two[k][1])
+            one.append(one_share)
             got_one = plane.once(one_share)
             pieces[offset] = combine_slots(
-                chosen[offset][1], [mine[k][0], near_share[0], got_two[0], got_one]
+                chosen[offset][1], [mine[k][0], near_share[0], got_two[k][0], got_one]
             )
     return pieces
 

time: 240 us -> 224 us (0.933)
  starting transfers between devices: 84.4 us -> 46.7 us
  waiting for transfers between devices: 60 us -> 96 us
  other arithmetic: 11.4 us -> 4.14 us
  Pallas kernels: 73.9 us -> 68 us
    ppermute x34, starting transfers between devices: 74.1 us -> 37.3 us  [swapped(): return lax.ppermute(array, axis, pairs)]
    ppermute x34, waiting for transfers between devices: 55.5 us -> 92 us  [swapped(): return lax.ppermute(array, axis, pairs)]
    convert_element_type x8, other arithmetic: 7.54 us -> 1.46 us  [added(): return (left.astype(F32) + right.astype(F32)).astype(BF16)]
    pallas_call x4, Pallas kernels: 41.1 us -> 36.8 us  [gate_part(): pl.pallas_call(functools.partial(gate_kernel, counts, len(xs), last), gri...]
    squeeze x4, local copies, waits for them, and re-layouts: 3.09 us -> 0.11 us  [paired_chunks(): near_share[0]]
    unnamed x38 -> x24, local copies, waits for them, and re-layouts: 5.07 us -> 6.35 us
  transfers between devices with their start and end apart: 36 -> 36, of which waited for: 14 -> 14; matrix products, arithmetic and copies ran while one was open for 6% -> 2% of each run, Pallas kernels for 21% -> 24%
where the time goes in v5:
time: 224 us; the launch traced here: 223 us
  waiting for transfers between devices  96 us (43%)
  Pallas kernels  68 us (30%)
  starting transfers between devices  46.7 us (21%)
  local copies, waits for them, and re-layouts  7.53 us (3%)
  other arithmetic  4.14 us (2%)
    ppermute x34, waiting for transfers between devices, swapped(): return lax.ppermute(array, axis, pairs)  92 us
    ppermute x34, starting transfers between devices, swapped(): return lax.ppermute(array, axis, pairs)  37.3 us
    pallas_call x4, Pallas kernels, gate_part(): pl.pallas_call(functools.partial(gate_kernel, counts, len(xs), last), gri...  36.8 us
    pallas_call x4, Pallas kernels, down_part(): pl.pallas_call(down_kernel, grid_spec=pltpu.PrefetchScalarGridSpec(num_sc...  24.3 us
    ppermute x2, starting transfers between devices, shifted(): return lax.ppermute(array, axis, pairs)  9.42 us
    unnamed x24, local copies, waits for them, and re-layouts  6.35 us
  transfers between devices with their start and end apart: 36, of which 14 were waited for; matrix products, arithmetic and copies ran while one was open for 2% of the time, Pallas kernels for 24%

profile of v5, /device:TPU:0, one launch (start us, length us, event | category | flops | bytes accessed | tf_op | source)
XLA Modules:
  0.0 223.0 jit_solution(9235869186789557337)
XLA Ops:
  0.0 1.0 copy-done.2
  1.0 1.0 copy-done.4
  2.0 0.7 copy-done.10
  2.7 1.0 shard_map.109
  3.7 4.9 %collective-permute-start = (bf16[784,128]{1,0:T(8,128)(2,1)S(1)}, bf16[784,128]{1,0:T(8,128)(2,1)S(1)}, u32[]{:S(2)}, u32[]{:S(2)}) collective-permute-start(bf16[784,128]{1,0:T(8,128)(2,1)S(1)} %get-tuple-element.69), channel_id=1, source_target_pairs={{0,8},{8,16},{16,24},{1,9},{9,17},{17,25},{2,10},{10,18},{18,26},{... | collective-permute-start | bytes 602120 | tf_op jit(solution)/shard_map/ppermute | solution.py:26
  8.7 0.7 reshape.60.gain_ref
  9.4 1.0 copy-done
  10.4 1.0 copy-done.3
  11.4 1.0 copy-done.5
  12.4 1.4 shard_map.110.intra_ref
  14.1 4.5 %collective-permute-start.1 = (bf16[784,128]{1,0:T(8,128)(2,1)S(1)}, bf16[784,128]{1,0:T(8,128)(2,1)S(1)}, u32[]{:S(2)}, u32[]{:S(2)}) collective-permute-start(bf16[784,128]{1,0:T(8,128)(2,1)S(1)} %concatenate.3), channel_id=1, source_target_pairs={{0,16},{8,24},{1,17},{9,25},{2,18},{10,26},{3,19},{11,27},{4,20},{... | collective-permute-start | bytes 602120 | tf_op jit(solution)/shard_map/ppermute | solution.py:26
  18.6 3.9 %collective-permute-done.1 = bf16[784,128]{1,0:T(8,128)(2,1)S(1)} collective-permute-done((bf16[784,128]{1,0:T(8,128)(2,1)S(1)}, bf16[784,128]{1,0:T(8,128)(2,1)S(1)}, u32[]{:S(2)}, u32[]{:S(2)}) %collective-permute-start.1) | collective-permute-done | bytes 200736 | tf_op jit(solution)/shard_map/ppermute | solution.py:26
  22.7 0.9 shard_map.111.part_ref
  23.5 0.5 shard_map.112
  24.0 1.6 collective-permute-start.2
  25.6 6.3 %collective-permute-done.2 = bf16[768,256]{1,0:T(8,128)(2,1)S(1)} collective-permute-done((bf16[768,256]{1,0:T(8,128)(2,1)S(1)}, bf16[768,256]{1,0:T(8,128)(2,1)S(1)}, u32[]{:S(2)}, u32[]{:S(2)}) %collective-permute-start.2) | collective-permute-done | bytes 393248 | tf_op jit(solution)/shard_map/ppermute | solution.py:402
  31.9 1.6 collective-permute-start.3
  33.5 3.4 %collective-permute-start.5 = (bf16[272,768]{1,0:T(8,128)(2,1)S(1)}, bf16[272,768]{1,0:T(8,128)(2,1)S(1)}, u32[]{:S(2)}, u32[]{:S(2)}) collective-permute-start(bf16[272,768]{1,0:T(8,128)(2,1)S(1)} %shard_map.111.part_ref), channel_id=1, source_target_pairs={{0,16},{8,24},{16,0},{24,8},{1,17},{9,25},{17,1},{25,9},{2,18},{10... | collective-permute-start | bytes 1253384 | tf_op jit(solution)/shard_map/ppermute | solution.py:402
  37.0 16.2 %collective-permute-done.5.part_ref = bf16[272,768]{1,0:T(8,128)(2,1)S(1)} collective-permute-done((bf16[272,768]{1,0:T(8,128)(2,1)S(1)}, bf16[272,768]{1,0:T(8,128)(2,1)S(1)}, u32[]{:S(2)}, u32[]{:S(2)}) %collective-permute-start.5) | collective-permute-done | bytes 417824 | tf_op jit(solution)/shard_map/ppermute | solution.py:402
  53.2 0.5 shard_map.113
  53.7 0.6 copy-done.8
  54.3 0.5 collective-permute-start.6
  54.9 7.7 %collective-permute-done.6 = bf16[768,256]{1,0:T(8,128)(2,1)S(1)} collective-permute-done((bf16[768,256]{1,0:T(8,128)(2,1)S(1)}, bf16[768,256]{1,0:T(8,128)(2,1)S(1)}, u32[]{:S(2)}, u32[]{:S(2)}) %collective-permute-start.6) | collective-permute-done | bytes 393248 | tf_op jit(solution)/shard_map/ppermute | solution.py:402
  62.6 1.4 collective-permute-start.7
  64.0 0.5 collective-permute-start.11
  64.5 0.5 collective-permute-start.10
  65.0 7.2 %collective-permute-done.11.part_ref = bf16[272,768]{1,0:T(8,128)(2,1)S(1)} collective-permute-done((bf16[272,768]{1,0:T(8,128)(2,1)S(1)}, bf16[272,768]{1,0:T(8,128)(2,1)S(1)}, u32[]{:S(2)}, u32[]{:S(2)}) %collective-permute-start.11) | collective-permute-done | bytes 417824 | tf_op jit(solution)/shard_map/ppermute | solution.py:402
  72.2 0.5 shard_map.114
  72.7 1.6 collective-permute-start.12
  74.3 2.7 %collective-permute-done.7.refs_2_ = bf16[2,768,256]{2,1,0:T(8,128)(2,1)} collective-permute-done((bf16[2,768,256]{2,1,0:T(8,128)(2,1)S(1)}, bf16[2,768,256]{2,1,0:T(8,128)(2,1)}, u32[]{:S(2)}, u32[]{:S(2)}) %collective-permute-start.7) | collective-permute-done | bytes 786464 | tf_op jit(solution)/shard_map/ppermute | solution.py:402
  77.2 3.5 %collective-permute-done.12 = bf16[768,256]{1,0:T(8,128)(2,1)} collective-permute-done((bf16[768,256]{1,0:T(8,128)(2,1)S(1)}, bf16[768,256]{1,0:T(8,128)(2,1)}, u32[]{:S(2)}, u32[]{:S(2)}) %collective-permute-start.12) | collective-permute-done | bytes 393248 | tf_op jit(solution)/shard_map/ppermute | solution.py:402
  80.7 4.6 %collective-permute-start.13 = (bf16[272,768]{1,0:T(8,128)(2,1)S(1)}, bf16[272,768]{1,0:T(8,128)(2,1)S(1)}, u32[]{:S(2)}, u32[]{:S(2)}) collective-permute-start(bf16[272,768]{1,0:T(8,128)(2,1)S(1)} %shard_map.111.part_ref), channel_id=1, source_target_pairs={{0,24},{8,16},{16,8},{24,0},{1,25},{9,17},{17,9},{25,1},{2,26},{10... | collective-permute-start | bytes 1253384 | tf_op jit(solution)/shard_map/ppermute | solution.py:402
  85.2 1.1 pad_maximum_fusion.2.refs_2_
  86.3 1.6 collective-permute-start.14
  87.9 9.3 %shard_map.115 = (f32[2,576,256]{2,1,0:T(8,128)S(1)}, f32[2,576,256]{2,1,0:T(8,128)S(1)}, f32[2,2,256]{2,1,0:T(2,128)S(1)}) custom-call(s32[4]{0:T(128)S(1)} %get-tuple-element.135.plan_ref, bf16[2,768,256]{2,1,0:T(8,128)(2,1)S(1)} %pad_maximum_fusion.refs_0_, bf16[2,768,256]{2,1,0:T(8,128)(2,1)} %collective-permute-done.9.refs_1_, ...), custom_call_target="tpu_custom_call" | custom-call | flops 3623878656 | bytes 14155776 | tf_op jit(solution)/shard_map/pallas_call | solution.py:335
  97.3 0.5 shard_map.116
  97.8 1.6 collective-permute-start.15
  99.4 9.8 %shard_map.117.hidden_ref = bf16[2,256,576]{2,1,0:T(8,128)(2,1)S(1)} custom-call(s32[4]{0:T(128)S(1)} %add_add_fusion.plan_ref, bf16[2,768,256]{2,1,0:T(8,128)(2,1)S(1)} %collective-permute-done.3.refs_0_, bf16[2,768,256]{2,1,0:T(8,128)(2,1)} %collective-permute-done.4.refs_1_, bf16[2,768,256]{2,1,0:T(8,128)(2,1)} %collective-permute-done.7.refs_2_, ...), custom_call_target="tpu_custom_call" | custom-call | flops 3623878656 | bytes 14155776 | tf_op jit(solution)/shard_map/pallas_call | solution.py:335
  109.3 6.0 %shard_map.118 = (bf16[4,256,768]{2,1,0:T(8,128)(2,1)S(1)}, bf16[4,256,768]{2,1,0:T(8,128)(2,1)S(1)}) custom-call(s32[4]{0:T(128)S(1)} %add_add_fusion.1.plan_ref, bf16[2,256,576]{2,1,0:T(8,128)(2,1)S(1)} %shard_map.117.hidden_ref, bf16[2,576,6144]{2,1,0:T(8,128)(2,1)} %down_ref.7), custom_call_target="tpu_custom_call" | custom-call | flops 1811939328 | bytes 7077888 | tf_op jit(solution)/shard_map/pallas_call | solution.py:374
  115.4 0.5 collective-permute-start.19
  115.9 0.5 collective-permute-start.23
  116.4 0.5 collective-permute-start.26
  116.9 6.0 %shard_map.119 = (bf16[4,256,768]{2,1,0:T(8,128)(2,1)S(1)}, bf16[4,256,768]{2,1,0:T(8,128)(2,1)S(1)}) custom-call(s32[4]{0:T(128)S(1)} %get-tuple-element.134.plan_ref, bf16[2,256,576]{2,1,0:T(8,128)(2,1)S(1)} %shard_map.117.hidden_ref, bf16[2,576,6144]{2,1,0:T(8,128)(2,1)} %down_ref.7), custom_call_target="tpu_custom_call" | custom-call | flops 1811939328 | bytes 7077888 | tf_op jit(solution)/shard_map/pallas_call | solution.py:374
  122.9 5.0 %collective-permute-done.23.refs_0_ = bf16[2,768,256]{2,1,0:T(8,128)(2,1)S(1)} collective-permute-done((bf16[2,768,256]{2,1,0:T(8,128)(2,1)S(1)}, bf16[2,768,256]{2,1,0:T(8,128)(2,1)S(1)}, u32[]{:S(2)}, u32[]{:S(2)}) %collective-permute-start.23) | collective-permute-done | bytes 786464 | tf_op jit(solution)/shard_map/ppermute | solution.py:402
  127.9 0.5 collective-permute-start.24
  128.6 0.6 collective-permute-start.17
  129.4 1.6 collective-permute-start.20
  131.0 8.6 %shard_map.122 = (f32[2,576,256]{2,1,0:T(8,128)S(1)}, f32[2,576,256]{2,1,0:T(8,128)S(1)}, f32[2,2,256]{2,1,0:T(2,128)S(1)}) custom-call(s32[4]{0:T(128)S(1)} %get-tuple-element.135.plan_ref, bf16[2,768,256]{2,1,0:T(8,128)(2,1)S(1)} %pad_maximum_fusion.3.refs_0_, bf16[2,768,256]{2,1,0:T(8,128)(2,1)S(1)} %collective-permute-done.26.refs_1_, ...), custom_call_target="tpu_custom_call" | custom-call | flops 3623878656 | bytes 14155776 | tf_op jit(solution)/shard_map/pallas_call | solution.py:335
  139.6 9.1 %shard_map.123.hidden_ref = bf16[2,256,576]{2,1,0:T(8,128)(2,1)S(1)} custom-call(s32[4]{0:T(128)S(1)} %add_add_fusion.plan_ref, bf16[2,768,256]{2,1,0:T(8,128)(2,1)S(1)} %collective-permute-done.23.refs_0_, bf16[2,768,256]{2,1,0:T(8,128)(2,1)S(1)} %collective-permute-done.24.refs_1_, bf16[2,768,256]{2,1,0:T(8,128)(2,1)S(1)} %collective-permute-done.14.refs_2_, ...), custom_call_target="tpu_custom_call" | custom-call | flops 3623878656 | bytes 14155776 | tf_op jit(solution)/shard_map/pallas_call | solution.py:335
  149.2 6.0 %shard_map.124 = (bf16[4,256,768]{2,1,0:T(8,128)(2,1)S(1)}, bf16[4,256,768]{2,1,0:T(8,128)(2,1)S(1)}) custom-call(s32[4]{0:T(128)S(1)} %add_add_fusion.1.plan_ref, bf16[2,256,576]{2,1,0:T(8,128)(2,1)S(1)} %shard_map.123.hidden_ref, bf16[2,576,6144]{2,1,0:T(8,128)(2,1)} %down_ref.7), custom_call_target="tpu_custom_call" | custom-call | flops 1811939328 | bytes 7077888 | tf_op jit(solution)/shard_map/pallas_call | solution.py:374
  155.4 0.5 collective-permute-start.32
  155.9 6.2 %shard_map.125 = (bf16[4,256,768]{2,1,0:T(8,128)(2,1)S(1)}, bf16[4,256,768]{2,1,0:T(8,128)(2,1)S(1)}) custom-call(s32[4]{0:T(128)S(1)} %get-tuple-element.134.plan_ref, bf16[2,256,576]{2,1,0:T(8,128)(2,1)S(1)} %shard_map.123.hidden_ref, bf16[2,576,6144]{2,1,0:T(8,128)(2,1)} %down_ref.7), custom_call_target="tpu_custom_call" | custom-call | flops 1811939328 | bytes 7077888 | tf_op jit(solution)/shard_map/pallas_call | solution.py:374
  162.4 0.6 collective-permute-start.29
  163.0 0.6 collective-permute-start.18
  163.6 1.5 collective-permute-start.21
  165.4 17.0 %collective-permute-done.29 = bf16[2,256,768]{2,1,0:T(8,128)(2,1)S(1)} collective-permute-done((bf16[2,256,768]{2,1,0:T(8,128)(2,1)S(1)}, bf16[2,256,768]{2,1,0:T(8,128)(2,1)S(1)}, u32[]{:S(2)}, u32[]{:S(2)}) %collective-permute-start.29) | collective-permute-done | bytes 786464 | tf_op jit(solution)/shard_map/ppermute | solution.py:402
  182.3 0.5 collective-permute-start.33
  183.3 6.6 %collective-permute-start.22 = (bf16[256,768]{1,0:T(8,128)(2,1)S(1)}, bf16[256,768]{1,0:T(8,128)(2,1)S(1)}, u32[]{:S(2)}, u32[]{:S(2)}) collective-permute-start(bf16[256,768]{1,0:T(8,128)(2,1)S(1)} %shard_map.121), channel_id=1, source_target_pairs={{0,16},{8,24},{16,0},{24,8},{1,17},{9,25},{17,1},{25,9},{2,18},{10... | collective-permute-start | bytes 1179656 | tf_op jit(solution)/shard_map/ppermute | solution.py:402
  190.2 8.3 %collective-permute-done.33 = bf16[2,256,768]{2,1,0:T(8,128)(2,1)S(1)} collective-permute-done((bf16[2,256,768]{2,1,0:T(8,128)(2,1)S(1)}, bf16[2,256,768]{2,1,0:T(8,128)(2,1)S(1)}, u32[]{:S(2)}, u32[]{:S(2)}) %collective-permute-start.33) | collective-permute-done | bytes 786464 | tf_op jit(solution)/shard_map/ppermute | solution.py:402
  199.7 6.8 %collective-permute-done.34.refs_3_ = bf16[256,768]{1,0:T(8,128)(2,1)S(1)} collective-permute-done((bf16[256,768]{1,0:T(8,128)(2,1)S(1)}, bf16[256,768]{1,0:T(8,128)(2,1)S(1)}, u32[]{:S(2)}, u32[]{:S(2)}) %collective-permute-start.34) | collective-permute-done | bytes 393248 | tf_op jit(solution)/shard_map/ppermute | solution.py:402
  206.9 3.4 %collective-permute-start.35 = (bf16[256,768]{1,0:T(8,128)(2,1)S(1)}, bf16[256,768]{1,0:T(8,128)(2,1)S(1)}, u32[]{:S(2)}, u32[]{:S(2)}) collective-permute-start(bf16[256,768]{1,0:T(8,128)(2,1)S(1)} %shard_map.127), channel_id=1, source_target_pairs={{0,8},{8,0},{16,24},{24,16},{1,9},{9,1},{17,25},{25,17},{2,10},{10... | collective-permute-start | bytes 1179656 | tf_op jit(solution)/shard_map/ppermute | solution.py:402
  210.9 3.8 %collective-permute-done.22 = bf16[256,768]{1,0:T(8,128)(2,1)S(1)} collective-permute-done((bf16[256,768]{1,0:T(8,128)(2,1)S(1)}, bf16[256,768]{1,0:T(8,128)(2,1)S(1)}, u32[]{:S(2)}, u32[]{:S(2)}) %collective-permute-start.22) | collective-permute-done | bytes 393248 | tf_op jit(solution)/shard_map/ppermute | solution.py:402
  214.7 7.3 %collective-permute-done.35 = bf16[256,768]{1,0:T(8,128)(2,1)S(1)} collective-permute-done((bf16[256,768]{1,0:T(8,128)(2,1)S(1)}, bf16[256,768]{1,0:T(8,128)(2,1)S(1)}, u32[]{:S(2)}, u32[]{:S(2)}) %collective-permute-start.35) | collective-permute-done | bytes 393248 | tf_op jit(solution)/shard_map/ppermute | solution.py:402
  222.0 1.0 add_convert_fusion.8
  (90 shorter events, 5.2 us)
Async XLA Ops:
  0.0 1.0 copy-start.2
  1.0 1.0 copy-start.4
  2.0 0.7 copy-start.10
  3.7 10.1 %collective-permute-start = (bf16[784,128]{1,0:T(8,128)(2,1)S(1)}, bf16[784,128]{1,0:T(8,128)(2,1)S(1)}, u32[]{:S(2)}, u32[]{:S(2)}) collective-permute-start(bf16[784,128]{1,0:T(8,128)(2,1)S(1)} %get-tuple-element.69), channel_id=1, source_target_pairs={{0,8},{8,16},{16,24},{1,9},{9,17},{17,25},{2,10},{10,18},{18,26},{... | collective-permute-start | bytes 602120 | tf_op jit(solution)/shard_map/ppermute | solution.py:26
  9.4 1.0 copy-start
  10.4 1.0 copy-start.3
  11.4 1.0 copy-start.5
  13.7 8.9 %copy-start.1 = (bf16[256,768]{1,0:T(8,128)(2,1)S(1)}, bf16[256,768]{1,0:T(8,128)(2,1)}, u32[]{:S(2)}) copy-start(bf16[256,768]{1,0:T(8,128)(2,1)} %query_ref.3) | copy-start | bytes 1179652
  13.8 8.9 %copy-start.7 = (bf16[256,768]{1,0:T(8,128)(2,1)S(1)}, bf16[256,768]{1,0:T(8,128)(2,1)}, u32[]{:S(2)}) copy-start(bf16[256,768]{1,0:T(8,128)(2,1)} %residual_ref.1) | copy-start | bytes 1179652
  13.8 8.9 %copy-start.11 = (s32[256,2]{0,1:T(2,128)S(1)}, s32[256,2]{0,1:T(2,128)}, u32[]{:S(2)}) copy-start(s32[256,2]{0,1:T(2,128)} %param.17) | copy-start | bytes 6148
  14.1 8.5 %collective-permute-start.1 = (bf16[784,128]{1,0:T(8,128)(2,1)S(1)}, bf16[784,128]{1,0:T(8,128)(2,1)S(1)}, u32[]{:S(2)}, u32[]{:S(2)}) collective-permute-start(bf16[784,128]{1,0:T(8,128)(2,1)S(1)} %concatenate.3), channel_id=1, source_target_pairs={{0,16},{8,24},{1,17},{9,25},{2,18},{10,26},{3,19},{11,27},{4,20},{... | collective-permute-start | bytes 602120 | tf_op jit(solution)/shard_map/ppermute | solution.py:26
  24.0 7.8 %collective-permute-start.2 = (bf16[768,256]{1,0:T(8,128)(2,1)S(1)}, bf16[768,256]{1,0:T(8,128)(2,1)S(1)}, u32[]{:S(2)}, u32[]{:S(2)}) collective-permute-start(bf16[768,256]{1,0:T(8,128)(2,1)S(1)} %get-tuple-element.71), channel_id=1, source_target_pairs={{0,2},{1,5},{2,0},{3,7},{4,6},{5,1},{6,4},{7,3},{8,10},{9,13},{10,... | collective-permute-start | bytes 1179656 | tf_op jit(solution)/shard_map/ppermute | solution.py:402
  31.9 21.2 %collective-permute-start.3 = (bf16[2,768,256]{2,1,0:T(8,128)(2,1)S(1)}, bf16[2,768,256]{2,1,0:T(8,128)(2,1)S(1)}, u32[]{:S(2)}, u32[]{:S(2)}) collective-permute-start(bf16[2,768,256]{2,1,0:T(8,128)(2,1)S(1)} %pad_maximum_fusion.refs_0_), channel_id=1, source_target_pairs={{0,4},{1,3},{2,6},{3,1},{4,0},{5,7},{6,2},{7,5},{8,12},{9,11},{10,... | collective-permute-start | bytes 2359304 | tf_op jit(solution)/shard_map/ppermute | solution.py:402
  33.5 19.6 %collective-permute-start.5 = (bf16[272,768]{1,0:T(8,128)(2,1)S(1)}, bf16[272,768]{1,0:T(8,128)(2,1)S(1)}, u32[]{:S(2)}, u32[]{:S(2)}) collective-permute-start(bf16[272,768]{1,0:T(8,128)(2,1)S(1)} %shard_map.111.part_ref), channel_id=1, source_target_pairs={{0,16},{8,24},{16,0},{24,8},{1,17},{9,25},{17,1},{25,9},{2,18},{10... | collective-permute-start | bytes 1253384 | tf_op jit(solution)/shard_map/ppermute | solution.py:402
  53.7 0.7 copy-start.8
  54.3 8.2 %collective-permute-start.6 = (bf16[768,256]{1,0:T(8,128)(2,1)S(1)}, bf16[768,256]{1,0:T(8,128)(2,1)S(1)}, u32[]{:S(2)}, u32[]{:S(2)}) collective-permute-start(bf16[768,256]{1,0:T(8,128)(2,1)S(1)} %get-tuple-element.74), channel_id=1, source_target_pairs={{0,2},{1,5},{2,0},{3,7},{4,6},{5,1},{6,4},{7,3},{8,10},{9,13},{10,... | collective-permute-start | bytes 1179656 | tf_op jit(solution)/shard_map/ppermute | solution.py:402
  62.6 25.3 %copy-start.6 = (bf16[6144,2]{0,1:T(2,128)(2,1)S(1)}, bf16[6144,2]{0,1:T(2,128)(2,1)}, u32[]{:S(2)}) copy-start(bf16[6144,2]{0,1:T(2,128)(2,1)} %param.18) | copy-start | bytes 73732
  62.6 14.4 %collective-permute-start.7 = (bf16[2,768,256]{2,1,0:T(8,128)(2,1)S(1)}, bf16[2,768,256]{2,1,0:T(8,128)(2,1)}, u32[]{:S(2)}, u32[]{:S(2)}) collective-permute-start(bf16[2,768,256]{2,1,0:T(8,128)(2,1)S(1)} %pad_maximum_fusion.1.refs_2_), channel_id=1, source_target_pairs={{0,4},{1,3},{2,6},{3,1},{4,0},{5,7},{6,2},{7,5},{8,12},{9,11},{10,... | collective-permute-start | bytes 2359304 | tf_op jit(solution)/shard_map/ppermute | solution.py:402
  64.0 8.2 %collective-permute-start.11 = (bf16[272,768]{1,0:T(8,128)(2,1)S(1)}, bf16[272,768]{1,0:T(8,128)(2,1)S(1)}, u32[]{:S(2)}, u32[]{:S(2)}) collective-permute-start(bf16[272,768]{1,0:T(8,128)(2,1)S(1)} %shard_map.111.part_ref), channel_id=1, source_target_pairs={{0,8},{8,0},{16,24},{24,16},{1,9},{9,1},{17,25},{25,17},{2,10},{10... | collective-permute-start | bytes 1253384 | tf_op jit(solution)/shard_map/ppermute | solution.py:402
  64.5 21.8 %collective-permute-start.9 = (bf16[2,768,256]{2,1,0:T(8,128)(2,1)S(1)}, bf16[2,768,256]{2,1,0:T(8,128)(2,1)}, u32[]{:S(2)}, u32[]{:S(2)}) collective-permute-start(bf16[2,768,256]{2,1,0:T(8,128)(2,1)S(1)} %pad_maximum_fusion.refs_0_), channel_id=1, source_target_pairs={{0,1},{1,0},{2,3},{3,2},{4,5},{5,4},{6,7},{7,6},{8,9},{9,8},{10,11... | collective-permute-start | bytes 2359304 | tf_op jit(solution)/shard_map/ppermute | solution.py:402
  64.5 23.4 %collective-permute-start.10 = (bf16[2,768,256]{2,1,0:T(8,128)(2,1)S(1)}, bf16[2,768,256]{2,1,0:T(8,128)(2,1)}, u32[]{:S(2)}, u32[]{:S(2)}) collective-permute-start(bf16[2,768,256]{2,1,0:T(8,128)(2,1)S(1)} %pad_maximum_fusion.1.refs_2_), channel_id=1, source_target_pairs={{0,1},{1,0},{2,3},{3,2},{4,5},{5,4},{6,7},{7,6},{8,9},{9,8},{10,11... | collective-permute-start | bytes 2359304 | tf_op jit(solution)/shard_map/ppermute | solution.py:402
  72.7 7.9 %collective-permute-start.12 = (bf16[768,256]{1,0:T(8,128)(2,1)S(1)}, bf16[768,256]{1,0:T(8,128)(2,1)}, u32[]{:S(2)}, u32[]{:S(2)}) collective-permute-start(bf16[768,256]{1,0:T(8,128)(2,1)S(1)} %get-tuple-element.76), channel_id=1, source_target_pairs={{0,2},{1,5},{2,0},{3,7},{4,6},{5,1},{6,4},{7,3},{8,10},{9,13},{10,... | collective-permute-start | bytes 1179656 | tf_op jit(solution)/shard_map/ppermute | solution.py:402
  74.3 23.0 %collective-permute-start.4 = (bf16[2,768,256]{2,1,0:T(8,128)(2,1)S(1)}, bf16[2,768,256]{2,1,0:T(8,128)(2,1)}, u32[]{:S(2)}, u32[]{:S(2)}) collective-permute-start(bf16[2,768,256]{2,1,0:T(8,128)(2,1)S(1)} %collective-permute-done.3.refs_0_), channel_id=1, source_target_pairs={{0,1},{1,0},{2,3},{3,2},{4,5},{5,4},{6,7},{7,6},{8,9},{9,8},{10,11... | collective-permute-start | bytes 2359304 | tf_op jit(solution)/shard_map/ppermute | solution.py:402
  77.0 20.3 %collective-permute-start.8 = (bf16[2,768,256]{2,1,0:T(8,128)(2,1)}, bf16[2,768,256]{2,1,0:T(8,128)(2,1)}, u32[]{:S(2)}, u32[]{:S(2)}) collective-permute-start(bf16[2,768,256]{2,1,0:T(8,128)(2,1)} %collective-permute-done.7.refs_2_), channel_id=1, source_target_pairs={{0,1},{1,0},{2,3},{3,2},{4,5},{5,4},{6,7},{7,6},{8,9},{9,8},{10,11... | collective-permute-start | bytes 2359304 | tf_op jit(solution)/shard_map/ppermute | solution.py:402
  80.7 16.6 %collective-permute-start.13 = (bf16[272,768]{1,0:T(8,128)(2,1)S(1)}, bf16[272,768]{1,0:T(8,128)(2,1)S(1)}, u32[]{:S(2)}, u32[]{:S(2)}) collective-permute-start(bf16[272,768]{1,0:T(8,128)(2,1)S(1)} %shard_map.111.part_ref), channel_id=1, source_target_pairs={{0,24},{8,16},{16,8},{24,0},{1,25},{9,17},{17,9},{25,1},{2,26},{10... | collective-permute-start | bytes 1253384 | tf_op jit(solution)/shard_map/ppermute | solution.py:402
  86.3 23.0 %collective-permute-start.14 = (bf16[2,768,256]{2,1,0:T(8,128)(2,1)S(1)}, bf16[2,768,256]{2,1,0:T(8,128)(2,1)S(1)}, u32[]{:S(2)}, u32[]{:S(2)}) collective-permute-start(bf16[2,768,256]{2,1,0:T(8,128)(2,1)S(1)} %pad_maximum_fusion.2.refs_2_), channel_id=1, source_target_pairs={{0,4},{1,3},{2,6},{3,1},{4,0},{5,7},{6,2},{7,5},{8,12},{9,11},{10,... | collective-permute-start | bytes 2359304 | tf_op jit(solution)/shard_map/ppermute | solution.py:402
  97.8 11.4 %collective-permute-start.15 = (bf16[768,256]{1,0:T(8,128)(2,1)S(1)}, bf16[768,256]{1,0:T(8,128)(2,1)S(1)}, u32[]{:S(2)}, u32[]{:S(2)}) collective-permute-start(bf16[768,256]{1,0:T(8,128)(2,1)S(1)} %get-tuple-element.93), channel_id=1, source_target_pairs={{0,2},{1,5},{2,0},{3,7},{4,6},{5,1},{6,4},{7,3},{8,10},{9,13},{10,... | collective-permute-start | bytes 1179656 | tf_op jit(solution)/shard_map/ppermute | solution.py:402
  115.3 12.6 %collective-permute-start.16 = (bf16[4,256,768]{2,1,0:T(8,128)(2,1)S(1)}, bf16[4,256,768]{2,1,0:T(8,128)(2,1)S(1)}, u32[]{:S(2)}, u32[]{:S(2)}) collective-permute-start(bf16[4,256,768]{2,1,0:T(8,128)(2,1)S(1)} %get-tuple-element.104), channel_id=1, source_target_pairs={{0,1},{1,0},{2,3},{3,2},{4,5},{5,4},{6,7},{7,6},{8,9},{9,8},{10,11... | collective-permute-start | bytes 4718600 | tf_op jit(solution)/shard_map/ppermute | solution.py:402
  115.4 13.2 %collective-permute-start.19 = (bf16[4,256,768]{2,1,0:T(8,128)(2,1)S(1)}, bf16[4,256,768]{2,1,0:T(8,128)(2,1)S(1)}, u32[]{:S(2)}, u32[]{:S(2)}) collective-permute-start(bf16[4,256,768]{2,1,0:T(8,128)(2,1)S(1)} %get-tuple-element.107), channel_id=1, source_target_pairs={{0,1},{1,0},{2,3},{3,2},{4,5},{5,4},{6,7},{7,6},{8,9},{9,8},{10,11... | collective-permute-start | bytes 4718600 | tf_op jit(solution)/shard_map/ppermute | solution.py:402
  115.9 12.0 %collective-permute-start.23 = (bf16[2,768,256]{2,1,0:T(8,128)(2,1)S(1)}, bf16[2,768,256]{2,1,0:T(8,128)(2,1)S(1)}, u32[]{:S(2)}, u32[]{:S(2)}) collective-permute-start(bf16[2,768,256]{2,1,0:T(8,128)(2,1)S(1)} %pad_maximum_fusion.3.refs_0_), channel_id=1, source_target_pairs={{0,4},{1,3},{2,6},{3,1},{4,0},{5,7},{6,2},{7,5},{8,12},{9,11},{10,... | collective-permute-start | bytes 2359304 | tf_op jit(solution)/shard_map/ppermute | solution.py:402
  116.4 13.0 %collective-permute-start.27 = (bf16[2,768,256]{2,1,0:T(8,128)(2,1)S(1)}, bf16[2,768,256]{2,1,0:T(8,128)(2,1)S(1)}, u32[]{:S(2)}, u32[]{:S(2)}) collective-permute-start(bf16[2,768,256]{2,1,0:T(8,128)(2,1)S(1)} %pad_maximum_fusion.2.refs_2_), channel_id=1, source_target_pairs={{0,1},{1,0},{2,3},{3,2},{4,5},{5,4},{6,7},{7,6},{8,9},{9,8},{10,11... | collective-permute-start | bytes 2359304 | tf_op jit(solution)/shard_map/ppermute | solution.py:402
  116.4 14.6 %collective-permute-start.26 = (bf16[2,768,256]{2,1,0:T(8,128)(2,1)S(1)}, bf16[2,768,256]{2,1,0:T(8,128)(2,1)S(1)}, u32[]{:S(2)}, u32[]{:S(2)}) collective-permute-start(bf16[2,768,256]{2,1,0:T(8,128)(2,1)S(1)} %pad_maximum_fusion.3.refs_0_), channel_id=1, source_target_pairs={{0,1},{1,0},{2,3},{3,2},{4,5},{5,4},{6,7},{7,6},{8,9},{9,8},{10,11... | collective-permute-start | bytes 2359304 | tf_op jit(solution)/shard_map/ppermute | solution.py:402
  127.9 11.7 %collective-permute-start.25 = (bf16[2,768,256]{2,1,0:T(8,128)(2,1)S(1)}, bf16[2,768,256]{2,1,0:T(8,128)(2,1)S(1)}, u32[]{:S(2)}, u32[]{:S(2)}) collective-permute-start(bf16[2,768,256]{2,1,0:T(8,128)(2,1)S(1)} %collective-permute-done.14.refs_2_), channel_id=1, source_target_pairs={{0,1},{1,0},{2,3},{3,2},{4,5},{5,4},{6,7},{7,6},{8,9},{9,8},{10,11... | collective-permute-start | bytes 2359304 | tf_op jit(solution)/shard_map/ppermute | solution.py:402
  127.9 11.7 %collective-permute-start.24 = (bf16[2,768,256]{2,1,0:T(8,128)(2,1)S(1)}, bf16[2,768,256]{2,1,0:T(8,128)(2,1)S(1)}, u32[]{:S(2)}, u32[]{:S(2)}) collective-permute-start(bf16[2,768,256]{2,1,0:T(8,128)(2,1)S(1)} %collective-permute-done.23.refs_0_), channel_id=1, source_target_pairs={{0,1},{1,0},{2,3},{3,2},{4,5},{5,4},{6,7},{7,6},{8,9},{9,8},{10,11... | collective-permute-start | bytes 2359304 | tf_op jit(solution)/shard_map/ppermute | solution.py:402
  128.6 20.2 %collective-permute-start.17 = (bf16[2,256,768]{2,1,0:T(8,128)(2,1)S(1)}, bf16[2,256,768]{2,1,0:T(8,128)(2,1)S(1)}, u32[]{:S(2)}, u32[]{:S(2)}) collective-permute-start(bf16[2,256,768]{2,1,0:T(8,128)(2,1)S(1)} %add_convert_fusion.3), channel_id=1, source_target_pairs={{0,4},{1,3},{2,6},{3,1},{4,0},{5,7},{6,2},{7,5},{8,12},{9,11},{10,... | collective-permute-start | bytes 2359304 | tf_op jit(solution)/shard_map/ppermute | solution.py:402
  129.4 19.7 %collective-permute-start.20 = (bf16[2,256,768]{2,1,0:T(8,128)(2,1)S(1)}, bf16[2,256,768]{2,1,0:T(8,128)(2,1)S(1)}, u32[]{:S(2)}, u32[]{:S(2)}) collective-permute-start(bf16[2,256,768]{2,1,0:T(8,128)(2,1)S(1)} %add_convert_fusion.2), channel_id=1, source_target_pairs={{0,4},{1,3},{2,6},{3,1},{4,0},{5,7},{6,2},{7,5},{8,12},{9,11},{10,... | collective-permute-start | bytes 2359304 | tf_op jit(solution)/shard_map/ppermute | solution.py:402
  155.3 6.9 %collective-permute-start.28 = (bf16[4,256,768]{2,1,0:T(8,128)(2,1)S(1)}, bf16[4,256,768]{2,1,0:T(8,128)(2,1)S(1)}, u32[]{:S(2)}, u32[]{:S(2)}) collective-permute-start(bf16[4,256,768]{2,1,0:T(8,128)(2,1)S(1)} %get-tuple-element.127), channel_id=1, source_target_pairs={{0,1},{1,0},{2,3},{3,2},{4,5},{5,4},{6,7},{7,6},{8,9},{9,8},{10,11... | collective-permute-start | bytes 4718600 | tf_op jit(solution)/shard_map/ppermute | solution.py:402
  155.4 9.8 %collective-permute-start.32 = (bf16[4,256,768]{2,1,0:T(8,128)(2,1)S(1)}, bf16[4,256,768]{2,1,0:T(8,128)(2,1)S(1)}, u32[]{:S(2)}, u32[]{:S(2)}) collective-permute-start(bf16[4,256,768]{2,1,0:T(8,128)(2,1)S(1)} %get-tuple-element.129), channel_id=1, source_target_pairs={{0,1},{1,0},{2,3},{3,2},{4,5},{5,4},{6,7},{7,6},{8,9},{9,8},{10,11... | collective-permute-start | bytes 4718600 | tf_op jit(solution)/shard_map/ppermute | solution.py:402
  162.4 19.9 %collective-permute-start.29 = (bf16[2,256,768]{2,1,0:T(8,128)(2,1)S(1)}, bf16[2,256,768]{2,1,0:T(8,128)(2,1)S(1)}, u32[]{:S(2)}, u32[]{:S(2)}) collective-permute-start(bf16[2,256,768]{2,1,0:T(8,128)(2,1)S(1)} %add_convert_fusion.1), channel_id=1, source_target_pairs={{0,4},{1,3},{2,6},{3,1},{4,0},{5,7},{6,2},{7,5},{8,12},{9,11},{10,... | collective-permute-start | bytes 2359304 | tf_op jit(solution)/shard_map/ppermute | solution.py:402
  163.0 47.4 %collective-permute-start.18 = (bf16[256,768]{1,0:T(8,128)(2,1)S(1)}, bf16[256,768]{1,0:T(8,128)(2,1)S(1)}, u32[]{:S(2)}, u32[]{:S(2)}) collective-permute-start(bf16[256,768]{1,0:T(8,128)(2,1)S(1)} %fusion), channel_id=1, source_target_pairs={{0,2},{1,5},{2,0},{3,7},{4,6},{5,1},{6,4},{7,3},{8,10},{9,13},{10,... | collective-permute-start | bytes 1179656 | tf_op jit(solution)/shard_map/ppermute | solution.py:402
  163.6 19.3 %collective-permute-start.21 = (bf16[256,768]{1,0:T(8,128)(2,1)S(1)}, bf16[256,768]{1,0:T(8,128)(2,1)S(1)}, u32[]{:S(2)}, u32[]{:S(2)}) collective-permute-start(bf16[256,768]{1,0:T(8,128)(2,1)S(1)} %fusion.1), channel_id=1, source_target_pairs={{0,2},{1,5},{2,0},{3,7},{4,6},{5,1},{6,4},{7,3},{8,10},{9,13},{10,... | collective-permute-start | bytes 1179656 | tf_op jit(solution)/shard_map/ppermute | solution.py:402
  165.1 17.7 %copy-start.9 = (bf16[256,256]{1,0:T(8,128)(2,1)S(1)}, bf16[256,256]{1,0:T(8,128)(2,1)}, u32[]{:S(2)}) copy-start(bf16[256,256]{1,0:T(8,128)(2,1)} %copy-done.8) | copy-start | bytes 393220
  182.3 16.2 %collective-permute-start.33 = (bf16[2,256,768]{2,1,0:T(8,128)(2,1)S(1)}, bf16[2,256,768]{2,1,0:T(8,128)(2,1)S(1)}, u32[]{:S(2)}, u32[]{:S(2)}) collective-permute-start(bf16[2,256,768]{2,1,0:T(8,128)(2,1)S(1)} %add_convert_fusion), channel_id=1, source_target_pairs={{0,4},{1,3},{2,6},{3,1},{4,0},{5,7},{6,2},{7,5},{8,12},{9,11},{10,... | collective-permute-start | bytes 2359304 | tf_op jit(solution)/shard_map/ppermute | solution.py:402
  183.3 31.4 %collective-permute-start.22 = (bf16[256,768]{1,0:T(8,128)(2,1)S(1)}, bf16[256,768]{1,0:T(8,128)(2,1)S(1)}, u32[]{:S(2)}, u32[]{:S(2)}) collective-permute-start(bf16[256,768]{1,0:T(8,128)(2,1)S(1)} %shard_map.121), channel_id=1, source_target_pairs={{0,16},{8,24},{16,0},{24,8},{1,17},{9,25},{17,1},{25,9},{2,18},{10... | collective-permute-start | bytes 1179656 | tf_op jit(solution)/shard_map/ppermute | solution.py:402
  190.1 8.9 %collective-permute-start.30 = (bf16[256,768]{1,0:T(8,128)(2,1)S(1)}, bf16[256,768]{1,0:T(8,128)(2,1)S(1)}, u32[]{:S(2)}, u32[]{:S(2)}) collective-permute-start(bf16[256,768]{1,0:T(8,128)(2,1)S(1)} %fusion.2), channel_id=1, source_target_pairs={{0,2},{1,5},{2,0},{3,7},{4,6},{5,1},{6,4},{7,3},{8,10},{9,13},{10,... | collective-permute-start | bytes 1179656 | tf_op jit(solution)/shard_map/ppermute | solution.py:402
  198.7 7.8 %collective-permute-start.34 = (bf16[256,768]{1,0:T(8,128)(2,1)S(1)}, bf16[256,768]{1,0:T(8,128)(2,1)S(1)}, u32[]{:S(2)}, u32[]{:S(2)}) collective-permute-start(bf16[256,768]{1,0:T(8,128)(2,1)S(1)} %fusion.3), channel_id=1, source_target_pairs={{0,2},{1,5},{2,0},{3,7},{4,6},{5,1},{6,4},{7,3},{8,10},{9,13},{10,... | collective-permute-start | bytes 1179656 | tf_op jit(solution)/shard_map/ppermute | solution.py:402
  199.5 15.2 %collective-permute-start.31 = (bf16[256,768]{1,0:T(8,128)(2,1)S(1)}, bf16[256,768]{1,0:T(8,128)(2,1)S(1)}, u32[]{:S(2)}, u32[]{:S(2)}) collective-permute-start(bf16[256,768]{1,0:T(8,128)(2,1)S(1)} %shard_map.126), channel_id=1, source_target_pairs={{0,24},{8,16},{16,8},{24,0},{1,25},{9,17},{17,9},{25,1},{2,26},{10... | collective-permute-start | bytes 1179656 | tf_op jit(solution)/shard_map/ppermute | solution.py:402
  206.9 15.1 %collective-permute-start.35 = (bf16[256,768]{1,0:T(8,128)(2,1)S(1)}, bf16[256,768]{1,0:T(8,128)(2,1)S(1)}, u32[]{:S(2)}, u32[]{:S(2)}) collective-permute-start(bf16[256,768]{1,0:T(8,128)(2,1)S(1)} %shard_map.127), channel_id=1, source_target_pairs={{0,8},{8,0},{16,24},{24,16},{1,9},{9,1},{17,25},{25,17},{2,10},{10... | collective-permute-start | bytes 1179656 | tf_op jit(solution)/shard_map/ppermute | solution.py:402

commit v6 on v5

--- a/solution.py
+++ b/solution.py
@@ -455,8 +455,8 @@
         attn_query, intra, cumulative, incoming, residual, norm_gain, expert_ids.T
     )
 
-    half = groups // 2
-    chunks = [(0, half)] + [(half + i, i) for i in range(1, half)]
+    offsets = [*range(1, groups), 0]
+    chunks = [tuple(offsets[i : i + 2]) for i in range(0, groups, 2)]
     capacity = 4 * length // (experts_here * groups)
     choices = expert_ids.shape[1]
 
@@ -496,43 +496,42 @@
     tie = lax.optimization_barrier
     two, far_two, near, near_far, chosen = {}, {}, {}, {}, {}
 
-    def gather(offset, part):
-        chosen[offset] = select(part)
-        two[offset] = plane.first(chosen[offset][0])
+    def gather(offset, behind=()):
+        two[offset], _ = tie((plane.first(chosen[offset][0]), behind))
         near[offset] = plane.across(two[offset])
         far_two[offset] = plane.second(two[offset])
         near_far[offset] = plane.across(far_two[offset])
 
-    gather(0, stream)
+    parts = {1: moved(stream, 1)}
+    chosen[0] = select(stream)
+    gather(0, parts[1])
     later, _ = tie((stream, two[0]))
-    arrived = moved(later, chunks[0][1])
-    part, _ = tie((arrived, far_two[0]))
-    gather(chunks[0][1], part)
-    later, _ = tie((stream, arrived))
-    parts = {offset: moved(later, offset) for chunk in chunks[1:] for offset in reversed(chunk)}
+    for offset in range(2, 2 * len(chunks)):
+        parts[offset] = moved(later, offset)
+        later, _ = tie((stream, parts[offset]))
+    chosen[1] = select(parts[1])
+    gather(1, [far_two[0], [parts[offset] for offset in chunks[0][1:]]])
+    for offset in chunks[0][1:]:
+        part, _ = tie((parts[offset], two[1]))
+        chosen[offset] = select(part)
+        gather(offset, [parts[following] for following in chunks[1] if following])
 
     pieces = {}
     sent, got_two, one = [], [], []
     for i, chunk in enumerate(chunks):
-        after = chunks[i + 1][::-1] if i + 1 < len(chunks) else ()
+        after = [offset for following in chunks[i + 1 : i + 2] for offset in following if offset]
         early = [[two[offset], near[offset]] for offset in chunk]
         late = [[far_two[offset], near_far[offset]] for offset in chunk]
-        if after:
-            gather(after[0], parts[after[0]])
-            early, _ = tie((early, chosen[after[0]]))
-        if sent:
-            early, _ = tie((early, sent))
+        for offset in after:
+            chosen[offset] = select(parts[offset])
+        early, _ = tie((early, [sent, [chosen[offset] for offset in after]]))
         sums = gate_part(plane.early, early, *weights)
+        for offset in after:
+            gather(offset, sums)
         late, sums = tie((late, sums))
-        if after:
-            part, _ = tie((parts[after[1]], sums))
-            gather(after[1], part)
-            late, _ = tie((late, [two[after[0]], chosen[after[1]]]))
+        late, _ = tie((late, [two[offset] for offset in after]))
         hidden = gate_part(plane.late, late, *weights, sums)
-        if after:
-            hidden, _ = tie((hidden, [far_two[after[0]], two[after[1]]]))
-        if one:
-            hidden, _ = tie((hidden, one))
+        hidden, _ = tie((hidden, [one, [far_two[offset] for offset in after]]))
         theirs = down_part(plane.theirs, hidden, down_weight, width, len(chunk))
         hidden, theirs = tie((hidden, theirs))
         mine = down_part(plane.mine, hidden, down_weight, width, len(chunk))

time: 224 us -> 228 us (1.018)
  the two profiles are of different devices: /device:TPU:0 before, /device:TPU:8 now
where the time goes in v6:
time: 228 us; the launch traced here: 227 us
  waiting for transfers between devices  110 us (48%)
  Pallas kernels  68.5 us (30%)
  starting transfers between devices  30.4 us (13%)
  local copies, waits for them, and re-layouts  12.9 us (6%)
  other arithmetic  4.94 us (2%)
    ppermute x34, waiting for transfers between devices, swapped(): return lax.ppermute(array, axis, pairs)  102 us
    pallas_call x4, Pallas kernels, gate_part(): pl.pallas_call(functools.partial(gate_kernel, counts, len(xs), last), gri...  37.2 us
    pallas_call x4, Pallas kernels, down_part(): pl.pallas_call(down_kernel, grid_spec=pltpu.PrefetchScalarGridSpec(num_sc...  24.4 us
    ppermute x34, starting transfers between devices, swapped(): return lax.ppermute(array, axis, pairs)  22.5 us
    unnamed x42, local copies, waits for them, and re-layouts  11.7 us
    ppermute x2, starting transfers between devices, shifted(): return lax.ppermute(array, axis, pairs)  7.96 us
    ppermute x2, waiting for transfers between devices, shifted(): return lax.ppermute(array, axis, pairs)  7.62 us
  transfers between devices with their start and end apart: 36, of which 15 were waited for; matrix products, arithmetic and copies ran while one was open for 2% of the time, Pallas kernels for 24%

profile of v6, /device:TPU:8, one launch (start us, length us, event | category | flops | bytes accessed | tf_op | source)
XLA Modules:
  0.0 227.3 jit_solution(5155819441368976309)
XLA Ops:
  0.0 1.0 copy-done.2
  1.0 1.0 copy-done.4
  2.0 0.7 copy-done.18
  2.7 1.0 shard_map.109
  3.7 3.5 %collective-permute-start = (bf16[784,128]{1,0:T(8,128)(2,1)S(1)}, bf16[784,128]{1,0:T(8,128)(2,1)S(1)}, u32[]{:S(2)}, u32[]{:S(2)}) collective-permute-start(bf16[784,128]{1,0:T(8,128)(2,1)S(1)} %get-tuple-element.76), channel_id=1, source_target_pairs={{0,8},{8,16},{16,24},{1,9},{9,17},{17,25},{2,10},{10,18},{18,26},{... | collective-permute-start | bytes 602120 | tf_op jit(solution)/shard_map/ppermute | solution.py:26
  7.2 0.7 reshape.60.gain_ref
  7.9 1.0 copy-done
  8.9 1.0 copy-done.3
  9.9 1.0 copy-done.5
  10.9 1.4 shard_map.110.intra_ref
  12.6 4.5 %collective-permute-start.1 = (bf16[784,128]{1,0:T(8,128)(2,1)S(1)}, bf16[784,128]{1,0:T(8,128)(2,1)S(1)}, u32[]{:S(2)}, u32[]{:S(2)}) collective-permute-start(bf16[784,128]{1,0:T(8,128)(2,1)S(1)} %concatenate.3), channel_id=1, source_target_pairs={{0,16},{8,24},{1,17},{9,25},{2,18},{10,26},{3,19},{11,27},{4,20},{... | collective-permute-start | bytes 602120 | tf_op jit(solution)/shard_map/ppermute | solution.py:26
  17.2 7.6 %collective-permute-done.1 = bf16[784,128]{1,0:T(8,128)(2,1)S(1)} collective-permute-done((bf16[784,128]{1,0:T(8,128)(2,1)S(1)}, bf16[784,128]{1,0:T(8,128)(2,1)S(1)}, u32[]{:S(2)}, u32[]{:S(2)}) %collective-permute-start.1) | collective-permute-done | bytes 200736 | tf_op jit(solution)/shard_map/ppermute | solution.py:26
  24.9 0.9 shard_map.111.part_ref
  25.7 0.5 shard_map.113
  26.2 1.6 collective-permute-start.4
  27.8 6.3 %collective-permute-done.4 = bf16[768,256]{1,0:T(8,128)(2,1)S(1)} collective-permute-done((bf16[768,256]{1,0:T(8,128)(2,1)S(1)}, bf16[768,256]{1,0:T(8,128)(2,1)S(1)}, u32[]{:S(2)}, u32[]{:S(2)}) %collective-permute-start.4) | collective-permute-done | bytes 393248 | tf_op jit(solution)/shard_map/ppermute | solution.py:402
  34.2 4.4 %collective-permute-done.2.part_ref = bf16[272,768]{1,0:T(8,128)(2,1)S(1)} collective-permute-done((bf16[272,768]{1,0:T(8,128)(2,1)S(1)}, bf16[272,768]{1,0:T(8,128)(2,1)S(1)}, u32[]{:S(2)}, u32[]{:S(2)}) %collective-permute-start.2) | collective-permute-done | bytes 417824 | tf_op jit(solution)/shard_map/ppermute | solution.py:402
  38.5 0.5 collective-permute-start.5
  39.5 1.6 collective-permute-start.3
  41.1 3.4 %collective-permute-start.6 = (bf16[272,768]{1,0:T(8,128)(2,1)S(1)}, bf16[272,768]{1,0:T(8,128)(2,1)S(1)}, u32[]{:S(2)}, u32[]{:S(2)}) collective-permute-start(bf16[272,768]{1,0:T(8,128)(2,1)S(1)} %shard_map.111.part_ref), channel_id=1, source_target_pairs={{0,16},{8,24},{16,0},{24,8},{1,17},{9,25},{17,1},{25,9},{2,18},{10... | collective-permute-start | bytes 1253384 | tf_op jit(solution)/shard_map/ppermute | solution.py:402
  44.5 7.2 %collective-permute-done.3 = bf16[768,256]{1,0:T(8,128)(2,1)S(1)} collective-permute-done((bf16[768,256]{1,0:T(8,128)(2,1)S(1)}, bf16[768,256]{1,0:T(8,128)(2,1)S(1)}, u32[]{:S(2)}, u32[]{:S(2)}) %collective-permute-start.3) | collective-permute-done | bytes 393248 | tf_op jit(solution)/shard_map/ppermute | solution.py:402
  51.7 9.4 %collective-permute-done.6.part_ref = bf16[272,768]{1,0:T(8,128)(2,1)S(1)} collective-permute-done((bf16[272,768]{1,0:T(8,128)(2,1)S(1)}, bf16[272,768]{1,0:T(8,128)(2,1)S(1)}, u32[]{:S(2)}, u32[]{:S(2)}) %collective-permute-start.6) | collective-permute-done | bytes 417824 | tf_op jit(solution)/shard_map/ppermute | solution.py:402
  62.0 1.1 collective-permute-start.13
  63.1 0.6 collective-permute-start.7
  63.7 9.7 %collective-permute-done.9 = bf16[768,256]{1,0:T(8,128)(2,1)S(1)} collective-permute-done((bf16[768,256]{1,0:T(8,128)(2,1)S(1)}, bf16[768,256]{1,0:T(8,128)(2,1)S(1)}, u32[]{:S(2)}, u32[]{:S(2)}) %collective-permute-start.9) | collective-permute-done | bytes 393248 | tf_op jit(solution)/shard_map/ppermute | solution.py:402
  73.4 0.9 pad_maximum_fusion.2.refs_2_
  74.3 9.0 %collective-permute-done.10.part_ref = bf16[272,768]{1,0:T(8,128)(2,1)S(1)} collective-permute-done((bf16[272,768]{1,0:T(8,128)(2,1)S(1)}, bf16[272,768]{1,0:T(8,128)(2,1)S(1)}, u32[]{:S(2)}, u32[]{:S(2)}) %collective-permute-start.10) | collective-permute-done | bytes 417824 | tf_op jit(solution)/shard_map/ppermute | solution.py:402
  84.5 0.7 copy-done.16
  85.5 11.7 %collective-permute-done.15 = bf16[768,256]{1,0:T(8,128)(2,1)S(1)} collective-permute-done((bf16[768,256]{1,0:T(8,128)(2,1)S(1)}, bf16[768,256]{1,0:T(8,128)(2,1)S(1)}, u32[]{:S(2)}, u32[]{:S(2)}) %collective-permute-start.15) | collective-permute-done | bytes 393248 | tf_op jit(solution)/shard_map/ppermute | solution.py:402
  97.2 0.7 copy-done.20
  97.9 1.1 pad_maximum_fusion.3.refs_0_
  99.1 0.9 collective-permute-done.11.refs_2_
  100.0 9.5 %shard_map.116 = (f32[2,576,256]{2,1,0:T(8,128)S(1)}, f32[2,576,256]{2,1,0:T(8,128)S(1)}, f32[2,2,256]{2,1,0:T(2,128)S(1)}) custom-call(s32[4]{0:T(128)S(1)} %get-tuple-element.149.plan_ref, bf16[2,768,256]{2,1,0:T(8,128)(2,1)S(1)} %pad_maximum_fusion.refs_0_, bf16[2,768,256]{2,1,0:T(8,128)(2,1)} %collective-permute-done.13.refs_1_, ...), custom_call_target="tpu_custom_call" | custom-call | flops 3623878656 | bytes 14155776 | tf_op jit(solution)/shard_map/pallas_call | solution.py:335
  109.5 1.0 copy-done.6
  110.6 1.0 copy-done.8
  111.6 1.2 collective-permute-start.16
  113.0 1.3 copy-done.7
  114.2 1.3 copy-done.9
  115.5 9.8 %shard_map.117.hidden_ref = bf16[2,256,576]{2,1,0:T(8,128)(2,1)S(1)} custom-call(s32[4]{0:T(128)S(1)} %add_add_fusion.plan_ref, bf16[2,768,256]{2,1,0:T(8,128)(2,1)} %collective-permute-done.7.refs_0_, bf16[2,768,256]{2,1,0:T(8,128)(2,1)} %collective-permute-done.8.refs_1_, bf16[2,768,256]{2,1,0:T(8,128)(2,1)} %collective-permute-done.11.refs_2_, ...), custom_call_target="tpu_custom_call" | custom-call | flops 3623878656 | bytes 14155776 | tf_op jit(solution)/shard_map/pallas_call | solution.py:335
  125.3 6.0 %shard_map.118 = (bf16[4,256,768]{2,1,0:T(8,128)(2,1)S(1)}, bf16[4,256,768]{2,1,0:T(8,128)(2,1)S(1)}) custom-call(s32[4]{0:T(128)S(1)} %add_add_fusion.1.plan_ref, bf16[2,256,576]{2,1,0:T(8,128)(2,1)S(1)} %shard_map.117.hidden_ref, bf16[2,576,6144]{2,1,0:T(8,128)(2,1)} %down_ref.7), custom_call_target="tpu_custom_call" | custom-call | flops 1811939328 | bytes 7077888 | tf_op jit(solution)/shard_map/pallas_call | solution.py:374
  131.4 0.5 collective-permute-start.21
  132.5 6.0 %shard_map.119 = (bf16[4,256,768]{2,1,0:T(8,128)(2,1)S(1)}, bf16[4,256,768]{2,1,0:T(8,128)(2,1)S(1)}) custom-call(s32[4]{0:T(128)S(1)} %get-tuple-element.148.plan_ref, bf16[2,256,576]{2,1,0:T(8,128)(2,1)S(1)} %shard_map.117.hidden_ref, bf16[2,576,6144]{2,1,0:T(8,128)(2,1)} %down_ref.7), custom_call_target="tpu_custom_call" | custom-call | flops 1811939328 | bytes 7077888 | tf_op jit(solution)/shard_map/pallas_call | solution.py:374
  138.6 0.5 collective-permute-start.25
  139.3 0.9 collective-permute-start.18
  140.4 1.3 collective-permute-start.22
  141.6 8.7 %shard_map.122 = (f32[2,576,256]{2,1,0:T(8,128)S(1)}, f32[2,576,256]{2,1,0:T(8,128)S(1)}, f32[2,2,256]{2,1,0:T(2,128)S(1)}) custom-call(s32[4]{0:T(128)S(1)} %get-tuple-element.149.plan_ref, bf16[2,768,256]{2,1,0:T(8,128)(2,1)S(1)} %pad_maximum_fusion.3.refs_0_, bf16[2,768,256]{2,1,0:T(8,128)(2,1)S(1)} %collective-permute-done.27.refs_1_, ...), custom_call_target="tpu_custom_call" | custom-call | flops 3623878656 | bytes 14155776 | tf_op jit(solution)/shard_map/pallas_call | solution.py:335
  150.3 9.3 %shard_map.123.hidden_ref = bf16[2,256,576]{2,1,0:T(8,128)(2,1)S(1)} custom-call(s32[4]{0:T(128)S(1)} %add_add_fusion.plan_ref, bf16[2,768,256]{2,1,0:T(8,128)(2,1)} %collective-permute-done.16.refs_0_, bf16[2,768,256]{2,1,0:T(8,128)(2,1)S(1)} %collective-permute-done.25.refs_1_, bf16[2,768,256]{2,1,0:T(8,128)(2,1)S(1)} %copy-done.11, ...), custom_call_target="tpu_custom_call" | custom-call | flops 3623878656 | bytes 14155776 | tf_op jit(solution)/shard_map/pallas_call | solution.py:335
  159.9 6.1 %shard_map.124 = (bf16[4,256,768]{2,1,0:T(8,128)(2,1)S(1)}, bf16[4,256,768]{2,1,0:T(8,128)(2,1)S(1)}) custom-call(s32[4]{0:T(128)S(1)} %add_add_fusion.1.plan_ref, bf16[2,256,576]{2,1,0:T(8,128)(2,1)S(1)} %shard_map.123.hidden_ref, bf16[2,576,6144]{2,1,0:T(8,128)(2,1)} %down_ref.7), custom_call_target="tpu_custom_call" | custom-call | flops 1811939328 | bytes 7077888 | tf_op jit(solution)/shard_map/pallas_call | solution.py:374
  166.2 0.6 collective-permute-start.33
  166.8 0.7 collective-permute-start.19
  167.5 1.4 collective-permute-start.23
  168.9 6.3 %shard_map.125 = (bf16[4,256,768]{2,1,0:T(8,128)(2,1)S(1)}, bf16[4,256,768]{2,1,0:T(8,128)(2,1)S(1)}) custom-call(s32[4]{0:T(128)S(1)} %get-tuple-element.148.plan_ref, bf16[2,256,576]{2,1,0:T(8,128)(2,1)S(1)} %shard_map.123.hidden_ref, bf16[2,576,6144]{2,1,0:T(8,128)(2,1)} %down_ref.7), custom_call_target="tpu_custom_call" | custom-call | flops 1811939328 | bytes 7077888 | tf_op jit(solution)/shard_map/pallas_call | solution.py:374
  175.4 0.9 collective-permute-start.30
  176.6 10.9 %collective-permute-done.30 = bf16[2,256,768]{2,1,0:T(8,128)(2,1)S(1)} collective-permute-done((bf16[2,256,768]{2,1,0:T(8,128)(2,1)S(1)}, bf16[2,256,768]{2,1,0:T(8,128)(2,1)S(1)}, u32[]{:S(2)}, u32[]{:S(2)}) %collective-permute-start.30) | collective-permute-done | bytes 786464 | tf_op jit(solution)/shard_map/ppermute | solution.py:402
  187.4 0.8 collective-permute-start.34
  189.2 1.4 collective-permute-start.24
  190.8 0.8 collective-permute-start.31
  191.7 10.9 %collective-permute-done.31.refs_3_ = bf16[256,768]{1,0:T(8,128)(2,1)S(1)} collective-permute-done((bf16[256,768]{1,0:T(8,128)(2,1)S(1)}, bf16[256,768]{1,0:T(8,128)(2,1)S(1)}, u32[]{:S(2)}, u32[]{:S(2)}) %collective-permute-start.31) | collective-permute-done | bytes 393248 | tf_op jit(solution)/shard_map/ppermute | solution.py:402
  203.1 0.5 collective-permute-done.34
  203.8 0.7 collective-permute-start.35
  204.5 7.1 %collective-permute-done.35.refs_3_ = bf16[256,768]{1,0:T(8,128)(2,1)S(1)} collective-permute-done((bf16[256,768]{1,0:T(8,128)(2,1)S(1)}, bf16[256,768]{1,0:T(8,128)(2,1)S(1)}, u32[]{:S(2)}, u32[]{:S(2)}) %collective-permute-start.35) | collective-permute-done | bytes 393248 | tf_op jit(solution)/shard_map/ppermute | solution.py:402
  212.0 3.4 %collective-permute-done.24 = bf16[256,768]{1,0:T(8,128)(2,1)S(1)} collective-permute-done((bf16[256,768]{1,0:T(8,128)(2,1)S(1)}, bf16[256,768]{1,0:T(8,128)(2,1)S(1)}, u32[]{:S(2)}, u32[]{:S(2)}) %collective-permute-start.24) | collective-permute-done | bytes 393248 | tf_op jit(solution)/shard_map/ppermute | solution.py:402
  215.5 10.8 %collective-permute-done.32 = bf16[256,768]{1,0:T(8,128)(2,1)S(1)} collective-permute-done((bf16[256,768]{1,0:T(8,128)(2,1)S(1)}, bf16[256,768]{1,0:T(8,128)(2,1)S(1)}, u32[]{:S(2)}, u32[]{:S(2)}) %collective-permute-start.32) | collective-permute-done | bytes 393248 | tf_op jit(solution)/shard_map/ppermute | solution.py:402
  226.3 1.0 add_convert_fusion.8
  (108 shorter events, 7.8 us)
Async XLA Ops:
  0.0 1.0 copy-start.2
  1.0 1.0 copy-start.4
  2.0 0.7 copy-start.18
  3.7 8.6 %collective-permute-start = (bf16[784,128]{1,0:T(8,128)(2,1)S(1)}, bf16[784,128]{1,0:T(8,128)(2,1)S(1)}, u32[]{:S(2)}, u32[]{:S(2)}) collective-permute-start(bf16[784,128]{1,0:T(8,128)(2,1)S(1)} %get-tuple-element.76), channel_id=1, source_target_pairs={{0,8},{8,16},{16,24},{1,9},{9,17},{17,25},{2,10},{10,18},{18,26},{... | collective-permute-start | bytes 602120 | tf_op jit(solution)/shard_map/ppermute | solution.py:26
  7.9 1.0 copy-start
  8.9 1.0 copy-start.3
  9.9 1.0 copy-start.5
  12.3 12.6 %copy-start.1 = (bf16[256,768]{1,0:T(8,128)(2,1)S(1)}, bf16[256,768]{1,0:T(8,128)(2,1)}, u32[]{:S(2)}) copy-start(bf16[256,768]{1,0:T(8,128)(2,1)} %query_ref.3) | copy-start | bytes 1179652
  12.3 12.6 %copy-start.13 = (bf16[256,768]{1,0:T(8,128)(2,1)S(1)}, bf16[256,768]{1,0:T(8,128)(2,1)}, u32[]{:S(2)}) copy-start(bf16[256,768]{1,0:T(8,128)(2,1)} %residual_ref.1) | copy-start | bytes 1179652
  12.3 12.6 %copy-start.19 = (s32[256,2]{0,1:T(2,128)S(1)}, s32[256,2]{0,1:T(2,128)}, u32[]{:S(2)}) copy-start(s32[256,2]{0,1:T(2,128)} %param.17) | copy-start | bytes 6148
  12.6 12.1 %collective-permute-start.1 = (bf16[784,128]{1,0:T(8,128)(2,1)S(1)}, bf16[784,128]{1,0:T(8,128)(2,1)S(1)}, u32[]{:S(2)}, u32[]{:S(2)}) collective-permute-start(bf16[784,128]{1,0:T(8,128)(2,1)S(1)} %concatenate.3), channel_id=1, source_target_pairs={{0,16},{8,24},{1,17},{9,25},{2,18},{10,26},{3,19},{11,27},{4,20},{... | collective-permute-start | bytes 602120 | tf_op jit(solution)/shard_map/ppermute | solution.py:26
  26.2 7.8 %collective-permute-start.4 = (bf16[768,256]{1,0:T(8,128)(2,1)S(1)}, bf16[768,256]{1,0:T(8,128)(2,1)S(1)}, u32[]{:S(2)}, u32[]{:S(2)}) collective-permute-start(bf16[768,256]{1,0:T(8,128)(2,1)S(1)} %get-tuple-element.79), channel_id=1, source_target_pairs={{0,2},{1,5},{2,0},{3,7},{4,6},{5,1},{6,4},{7,3},{8,10},{9,13},{10,... | collective-permute-start | bytes 1179656 | tf_op jit(solution)/shard_map/ppermute | solution.py:402
  27.8 10.7 %collective-permute-start.2 = (bf16[272,768]{1,0:T(8,128)(2,1)S(1)}, bf16[272,768]{1,0:T(8,128)(2,1)S(1)}, u32[]{:S(2)}, u32[]{:S(2)}) collective-permute-start(bf16[272,768]{1,0:T(8,128)(2,1)S(1)} %shard_map.111.part_ref), channel_id=1, source_target_pairs={{0,8},{8,0},{16,24},{24,16},{1,9},{9,1},{17,25},{25,17},{2,10},{10... | collective-permute-start | bytes 1253384 | tf_op jit(solution)/shard_map/ppermute | solution.py:402
  38.5 22.6 %collective-permute-start.5 = (bf16[2,768,256]{2,1,0:T(8,128)(2,1)S(1)}, bf16[2,768,256]{2,1,0:T(8,128)(2,1)S(1)}, u32[]{:S(2)}, u32[]{:S(2)}) collective-permute-start(bf16[2,768,256]{2,1,0:T(8,128)(2,1)S(1)} %pad_maximum_fusion.1.refs_2_), channel_id=1, source_target_pairs={{0,4},{1,3},{2,6},{3,1},{4,0},{5,7},{6,2},{7,5},{8,12},{9,11},{10,... | collective-permute-start | bytes 2359304 | tf_op jit(solution)/shard_map/ppermute | solution.py:402
  39.5 12.1 %collective-permute-start.3 = (bf16[768,256]{1,0:T(8,128)(2,1)S(1)}, bf16[768,256]{1,0:T(8,128)(2,1)S(1)}, u32[]{:S(2)}, u32[]{:S(2)}) collective-permute-start(bf16[768,256]{1,0:T(8,128)(2,1)S(1)} %get-tuple-element.78), channel_id=1, source_target_pairs={{0,2},{1,5},{2,0},{3,7},{4,6},{5,1},{6,4},{7,3},{8,10},{9,13},{10,... | collective-permute-start | bytes 1179656 | tf_op jit(solution)/shard_map/ppermute | solution.py:402
  41.1 20.0 %collective-permute-start.6 = (bf16[272,768]{1,0:T(8,128)(2,1)S(1)}, bf16[272,768]{1,0:T(8,128)(2,1)S(1)}, u32[]{:S(2)}, u32[]{:S(2)}) collective-permute-start(bf16[272,768]{1,0:T(8,128)(2,1)S(1)} %shard_map.111.part_ref), channel_id=1, source_target_pairs={{0,16},{8,24},{16,0},{24,8},{1,17},{9,25},{17,1},{25,9},{2,18},{10... | collective-permute-start | bytes 1253384 | tf_op jit(solution)/shard_map/ppermute | solution.py:402
  61.1 22.2 %copy-start.10 = (bf16[2,768,256]{2,1,0:T(8,128)(2,1)}, bf16[2,768,256]{2,1,0:T(8,128)(2,1)S(1)}, u32[]{:S(2)}) copy-start(bf16[2,768,256]{2,1,0:T(8,128)(2,1)S(1)} %collective-permute-done.5.refs_2_) | copy-start | bytes 2359300
  61.6 35.5 %copy-start.14 = (bf16[256,256]{1,0:T(8,128)(2,1)}, bf16[256,256]{1,0:T(8,128)(2,1)S(1)}, u32[]{:S(2)}) copy-start(bf16[256,256]{1,0:T(8,128)(2,1)S(1)} %get-tuple-element.114.place_ref) | copy-start | bytes 393220
  61.7 11.7 %collective-permute-start.9 = (bf16[768,256]{1,0:T(8,128)(2,1)S(1)}, bf16[768,256]{1,0:T(8,128)(2,1)S(1)}, u32[]{:S(2)}, u32[]{:S(2)}) collective-permute-start(bf16[768,256]{1,0:T(8,128)(2,1)S(1)} %get-tuple-element.84), channel_id=1, source_target_pairs={{0,2},{1,5},{2,0},{3,7},{4,6},{5,1},{6,4},{7,3},{8,10},{9,13},{10,... | collective-permute-start | bytes 1179656 | tf_op jit(solution)/shard_map/ppermute | solution.py:402
  62.0 21.4 %collective-permute-start.10 = (bf16[272,768]{1,0:T(8,128)(2,1)S(1)}, bf16[272,768]{1,0:T(8,128)(2,1)S(1)}, u32[]{:S(2)}, u32[]{:S(2)}) collective-permute-start(bf16[272,768]{1,0:T(8,128)(2,1)S(1)} %shard_map.111.part_ref), channel_id=1, source_target_pairs={{0,24},{8,16},{16,8},{24,0},{1,25},{9,17},{17,9},{25,1},{2,26},{10... | collective-permute-start | bytes 1253384 | tf_op jit(solution)/shard_map/ppermute | solution.py:402
  62.0 37.1 %collective-permute-start.13 = (bf16[2,768,256]{2,1,0:T(8,128)(2,1)S(1)}, bf16[2,768,256]{2,1,0:T(8,128)(2,1)}, u32[]{:S(2)}, u32[]{:S(2)}) collective-permute-start(bf16[2,768,256]{2,1,0:T(8,128)(2,1)S(1)} %pad_maximum_fusion.refs_0_), channel_id=1, source_target_pairs={{0,1},{1,0},{2,3},{3,2},{4,5},{5,4},{6,7},{7,6},{8,9},{9,8},{10,11... | collective-permute-start | bytes 2359304 | tf_op jit(solution)/shard_map/ppermute | solution.py:402
  63.1 35.9 %collective-permute-start.7 = (bf16[2,768,256]{2,1,0:T(8,128)(2,1)S(1)}, bf16[2,768,256]{2,1,0:T(8,128)(2,1)}, u32[]{:S(2)}, u32[]{:S(2)}) collective-permute-start(bf16[2,768,256]{2,1,0:T(8,128)(2,1)S(1)} %pad_maximum_fusion.refs_0_), channel_id=1, source_target_pairs={{0,4},{1,3},{2,6},{3,1},{4,0},{5,7},{6,2},{7,5},{8,12},{9,11},{10,... | collective-permute-start | bytes 2359304 | tf_op jit(solution)/shard_map/ppermute | solution.py:402
  73.4 26.6 %copy-start.12 = (bf16[6144,2]{0,1:T(2,128)(2,1)S(1)}, bf16[6144,2]{0,1:T(2,128)(2,1)}, u32[]{:S(2)}) copy-start(bf16[6144,2]{0,1:T(2,128)(2,1)} %param.18) | copy-start | bytes 73732
  83.4 15.7 %collective-permute-start.14 = (bf16[2,768,256]{2,1,0:T(8,128)(2,1)}, bf16[2,768,256]{2,1,0:T(8,128)(2,1)}, u32[]{:S(2)}, u32[]{:S(2)}) collective-permute-start(bf16[2,768,256]{2,1,0:T(8,128)(2,1)} %pad_maximum_fusion.2.refs_2_), channel_id=1, source_target_pairs={{0,1},{1,0},{2,3},{3,2},{4,5},{5,4},{6,7},{7,6},{8,9},{9,8},{10,11... | collective-permute-start | bytes 2359304 | tf_op jit(solution)/shard_map/ppermute | solution.py:402
  83.5 16.5 %collective-permute-start.11 = (bf16[2,768,256]{2,1,0:T(8,128)(2,1)}, bf16[2,768,256]{2,1,0:T(8,128)(2,1)}, u32[]{:S(2)}, u32[]{:S(2)}) collective-permute-start(bf16[2,768,256]{2,1,0:T(8,128)(2,1)} %pad_maximum_fusion.2.refs_2_), channel_id=1, source_target_pairs={{0,4},{1,3},{2,6},{3,1},{4,0},{5,7},{6,2},{7,5},{8,12},{9,11},{10,... | collective-permute-start | bytes 2359304 | tf_op jit(solution)/shard_map/ppermute | solution.py:402
  84.4 0.7 copy-start.16
  85.1 12.1 %collective-permute-start.15 = (bf16[768,256]{1,0:T(8,128)(2,1)S(1)}, bf16[768,256]{1,0:T(8,128)(2,1)S(1)}, u32[]{:S(2)}, u32[]{:S(2)}) collective-permute-start(bf16[768,256]{1,0:T(8,128)(2,1)S(1)} %get-tuple-element.87), channel_id=1, source_target_pairs={{0,2},{1,5},{2,0},{3,7},{4,6},{5,1},{6,4},{7,3},{8,10},{9,13},{10,... | collective-permute-start | bytes 1179656 | tf_op jit(solution)/shard_map/ppermute | solution.py:402
  97.2 0.7 copy-start.20
  99.0 14.0 %collective-permute-start.8 = (bf16[2,768,256]{2,1,0:T(8,128)(2,1)}, bf16[2,768,256]{2,1,0:T(8,128)(2,1)}, u32[]{:S(2)}, u32[]{:S(2)}) collective-permute-start(bf16[2,768,256]{2,1,0:T(8,128)(2,1)} %collective-permute-done.7.refs_0_), channel_id=1, source_target_pairs={{0,1},{1,0},{2,3},{3,2},{4,5},{5,4},{6,7},{7,6},{8,9},{9,8},{10,11... | collective-permute-start | bytes 2359304 | tf_op jit(solution)/shard_map/ppermute | solution.py:402
  100.0 13.0 %collective-permute-start.12 = (bf16[2,768,256]{2,1,0:T(8,128)(2,1)}, bf16[2,768,256]{2,1,0:T(8,128)(2,1)}, u32[]{:S(2)}, u32[]{:S(2)}) collective-permute-start(bf16[2,768,256]{2,1,0:T(8,128)(2,1)} %collective-permute-done.11.refs_2_), channel_id=1, source_target_pairs={{0,1},{1,0},{2,3},{3,2},{4,5},{5,4},{6,7},{7,6},{8,9},{9,8},{10,11... | collective-permute-start | bytes 2359304 | tf_op jit(solution)/shard_map/ppermute | solution.py:402
  109.5 1.1 copy-start.6
  110.6 1.0 copy-start.8
  111.6 13.7 %collective-permute-start.16 = (bf16[2,768,256]{2,1,0:T(8,128)(2,1)S(1)}, bf16[2,768,256]{2,1,0:T(8,128)(2,1)}, u32[]{:S(2)}, u32[]{:S(2)}) collective-permute-start(bf16[2,768,256]{2,1,0:T(8,128)(2,1)S(1)} %pad_maximum_fusion.3.refs_0_), channel_id=1, source_target_pairs={{0,4},{1,3},{2,6},{3,1},{4,0},{5,7},{6,2},{7,5},{8,12},{9,11},{10,... | collective-permute-start | bytes 2359304 | tf_op jit(solution)/shard_map/ppermute | solution.py:402
  113.0 1.3 copy-start.7
  114.2 1.3 copy-start.9
  125.3 7.1 %copy-start.11 = (bf16[2,768,256]{2,1,0:T(8,128)(2,1)S(1)}, bf16[2,768,256]{2,1,0:T(8,128)(2,1)}, u32[]{:S(2)}) copy-start(bf16[2,768,256]{2,1,0:T(8,128)(2,1)} %copy-done.10) | copy-start | bytes 2359300
  131.4 7.2 %collective-permute-start.17 = (bf16[4,256,768]{2,1,0:T(8,128)(2,1)S(1)}, bf16[4,256,768]{2,1,0:T(8,128)(2,1)S(1)}, u32[]{:S(2)}, u32[]{:S(2)}) collective-permute-start(bf16[4,256,768]{2,1,0:T(8,128)(2,1)S(1)} %get-tuple-element.113), channel_id=1, source_target_pairs={{0,1},{1,0},{2,3},{3,2},{4,5},{5,4},{6,7},{7,6},{8,9},{9,8},{10,11... | collective-permute-start | bytes 4718600 | tf_op jit(solution)/shard_map/ppermute | solution.py:402
  131.4 7.8 %collective-permute-start.21 = (bf16[4,256,768]{2,1,0:T(8,128)(2,1)S(1)}, bf16[4,256,768]{2,1,0:T(8,128)(2,1)S(1)}, u32[]{:S(2)}, u32[]{:S(2)}) collective-permute-start(bf16[4,256,768]{2,1,0:T(8,128)(2,1)S(1)} %get-tuple-element.116), channel_id=1, source_target_pairs={{0,1},{1,0},{2,3},{3,2},{4,5},{5,4},{6,7},{7,6},{8,9},{9,8},{10,11... | collective-permute-start | bytes 4718600 | tf_op jit(solution)/shard_map/ppermute | solution.py:402
  131.9 8.4 %collective-permute-start.28 = (bf16[2,768,256]{2,1,0:T(8,128)(2,1)S(1)}, bf16[2,768,256]{2,1,0:T(8,128)(2,1)S(1)}, u32[]{:S(2)}, u32[]{:S(2)}) collective-permute-start(bf16[2,768,256]{2,1,0:T(8,128)(2,1)S(1)} %pad_maximum_fusion.1.refs_2_), channel_id=1, source_target_pairs={{0,1},{1,0},{2,3},{3,2},{4,5},{5,4},{6,7},{7,6},{8,9},{9,8},{10,11... | collective-permute-start | bytes 2359304 | tf_op jit(solution)/shard_map/ppermute | solution.py:402
  132.0 9.6 %collective-permute-start.27 = (bf16[2,768,256]{2,1,0:T(8,128)(2,1)S(1)}, bf16[2,768,256]{2,1,0:T(8,128)(2,1)S(1)}, u32[]{:S(2)}, u32[]{:S(2)}) collective-permute-start(bf16[2,768,256]{2,1,0:T(8,128)(2,1)S(1)} %pad_maximum_fusion.3.refs_0_), channel_id=1, source_target_pairs={{0,1},{1,0},{2,3},{3,2},{4,5},{5,4},{6,7},{7,6},{8,9},{9,8},{10,11... | collective-permute-start | bytes 2359304 | tf_op jit(solution)/shard_map/ppermute | solution.py:402
  132.5 17.9 %collective-permute-start.26 = (bf16[2,768,256]{2,1,0:T(8,128)(2,1)S(1)}, bf16[2,768,256]{2,1,0:T(8,128)(2,1)S(1)}, u32[]{:S(2)}, u32[]{:S(2)}) collective-permute-start(bf16[2,768,256]{2,1,0:T(8,128)(2,1)S(1)} %copy-done.11), channel_id=1, source_target_pairs={{0,1},{1,0},{2,3},{3,2},{4,5},{5,4},{6,7},{7,6},{8,9},{9,8},{10,11... | collective-permute-start | bytes 2359304 | tf_op jit(solution)/shard_map/ppermute | solution.py:402
  138.6 11.8 %collective-permute-start.25 = (bf16[2,768,256]{2,1,0:T(8,128)(2,1)}, bf16[2,768,256]{2,1,0:T(8,128)(2,1)S(1)}, u32[]{:S(2)}, u32[]{:S(2)}) collective-permute-start(bf16[2,768,256]{2,1,0:T(8,128)(2,1)} %collective-permute-done.16.refs_0_), channel_id=1, source_target_pairs={{0,1},{1,0},{2,3},{3,2},{4,5},{5,4},{6,7},{7,6},{8,9},{9,8},{10,11... | collective-permute-start | bytes 2359304 | tf_op jit(solution)/shard_map/ppermute | solution.py:402
  139.3 20.3 %collective-permute-start.18 = (bf16[2,256,768]{2,1,0:T(8,128)(2,1)S(1)}, bf16[2,256,768]{2,1,0:T(8,128)(2,1)S(1)}, u32[]{:S(2)}, u32[]{:S(2)}) collective-permute-start(bf16[2,256,768]{2,1,0:T(8,128)(2,1)S(1)} %add_convert_fusion.3), channel_id=1, source_target_pairs={{0,4},{1,3},{2,6},{3,1},{4,0},{5,7},{6,2},{7,5},{8,12},{9,11},{10,... | collective-permute-start | bytes 2359304 | tf_op jit(solution)/shard_map/ppermute | solution.py:402
  140.4 19.4 %collective-permute-start.22 = (bf16[2,256,768]{2,1,0:T(8,128)(2,1)S(1)}, bf16[2,256,768]{2,1,0:T(8,128)(2,1)S(1)}, u32[]{:S(2)}, u32[]{:S(2)}) collective-permute-start(bf16[2,256,768]{2,1,0:T(8,128)(2,1)S(1)} %add_convert_fusion.2), channel_id=1, source_target_pairs={{0,4},{1,3},{2,6},{3,1},{4,0},{5,7},{6,2},{7,5},{8,12},{9,11},{10,... | collective-permute-start | bytes 2359304 | tf_op jit(solution)/shard_map/ppermute | solution.py:402
  166.0 9.1 %collective-permute-start.29 = (bf16[4,256,768]{2,1,0:T(8,128)(2,1)S(1)}, bf16[4,256,768]{2,1,0:T(8,128)(2,1)S(1)}, u32[]{:S(2)}, u32[]{:S(2)}) collective-permute-start(bf16[4,256,768]{2,1,0:T(8,128)(2,1)S(1)} %get-tuple-element.140), channel_id=1, source_target_pairs={{0,1},{1,0},{2,3},{3,2},{4,5},{5,4},{6,7},{7,6},{8,9},{9,8},{10,11... | collective-permute-start | bytes 4718600 | tf_op jit(solution)/shard_map/ppermute | solution.py:402
  166.2 10.2 %collective-permute-start.33 = (bf16[4,256,768]{2,1,0:T(8,128)(2,1)S(1)}, bf16[4,256,768]{2,1,0:T(8,128)(2,1)S(1)}, u32[]{:S(2)}, u32[]{:S(2)}) collective-permute-start(bf16[4,256,768]{2,1,0:T(8,128)(2,1)S(1)} %get-tuple-element.143), channel_id=1, source_target_pairs={{0,1},{1,0},{2,3},{3,2},{4,5},{5,4},{6,7},{7,6},{8,9},{9,8},{10,11... | collective-permute-start | bytes 4718600 | tf_op jit(solution)/shard_map/ppermute | solution.py:402
  166.8 21.5 %collective-permute-start.19 = (bf16[256,768]{1,0:T(8,128)(2,1)S(1)}, bf16[256,768]{1,0:T(8,128)(2,1)S(1)}, u32[]{:S(2)}, u32[]{:S(2)}) collective-permute-start(bf16[256,768]{1,0:T(8,128)(2,1)S(1)} %fusion), channel_id=1, source_target_pairs={{0,2},{1,5},{2,0},{3,7},{4,6},{5,1},{6,4},{7,3},{8,10},{9,13},{10,... | collective-permute-start | bytes 1179656 | tf_op jit(solution)/shard_map/ppermute | solution.py:402
  167.5 21.3 %collective-permute-start.23 = (bf16[256,768]{1,0:T(8,128)(2,1)S(1)}, bf16[256,768]{1,0:T(8,128)(2,1)S(1)}, u32[]{:S(2)}, u32[]{:S(2)}) collective-permute-start(bf16[256,768]{1,0:T(8,128)(2,1)S(1)} %fusion.1), channel_id=1, source_target_pairs={{0,2},{1,5},{2,0},{3,7},{4,6},{5,1},{6,4},{7,3},{8,10},{9,13},{10,... | collective-permute-start | bytes 1179656 | tf_op jit(solution)/shard_map/ppermute | solution.py:402
  175.4 12.1 %collective-permute-start.30 = (bf16[2,256,768]{2,1,0:T(8,128)(2,1)S(1)}, bf16[2,256,768]{2,1,0:T(8,128)(2,1)S(1)}, u32[]{:S(2)}, u32[]{:S(2)}) collective-permute-start(bf16[2,256,768]{2,1,0:T(8,128)(2,1)S(1)} %add_convert_fusion.1), channel_id=1, source_target_pairs={{0,4},{1,3},{2,6},{3,1},{4,0},{5,7},{6,2},{7,5},{8,12},{9,11},{10,... | collective-permute-start | bytes 2359304 | tf_op jit(solution)/shard_map/ppermute | solution.py:402
  176.5 12.2 %copy-start.15 = (bf16[256,256]{1,0:T(8,128)(2,1)S(1)}, bf16[256,256]{1,0:T(8,128)(2,1)}, u32[]{:S(2)}) copy-start(bf16[256,256]{1,0:T(8,128)(2,1)} %copy-done.14) | copy-start | bytes 393220
  187.4 16.2 %collective-permute-start.34 = (bf16[2,256,768]{2,1,0:T(8,128)(2,1)S(1)}, bf16[2,256,768]{2,1,0:T(8,128)(2,1)S(1)}, u32[]{:S(2)}, u32[]{:S(2)}) collective-permute-start(bf16[2,256,768]{2,1,0:T(8,128)(2,1)S(1)} %add_convert_fusion), channel_id=1, source_target_pairs={{0,4},{1,3},{2,6},{3,1},{4,0},{5,7},{6,2},{7,5},{8,12},{9,11},{10,... | collective-permute-start | bytes 2359304 | tf_op jit(solution)/shard_map/ppermute | solution.py:402
  188.7 23.3 %collective-permute-start.20 = (bf16[256,768]{1,0:T(8,128)(2,1)S(1)}, bf16[256,768]{1,0:T(8,128)(2,1)S(1)}, u32[]{:S(2)}, u32[]{:S(2)}) collective-permute-start(bf16[256,768]{1,0:T(8,128)(2,1)S(1)} %shard_map.120), channel_id=1, source_target_pairs={{0,8},{8,0},{16,24},{24,16},{1,9},{9,1},{17,25},{25,17},{2,10},{10... | collective-permute-start | bytes 1179656 | tf_op jit(solution)/shard_map/ppermute | solution.py:402
  189.2 13.4 %copy-start.17 = (bf16[256,256]{1,0:T(8,128)(2,1)S(1)}, bf16[256,256]{1,0:T(8,128)(2,1)}, u32[]{:S(2)}) copy-start(bf16[256,256]{1,0:T(8,128)(2,1)} %copy-done.16) | copy-start | bytes 393220
  189.2 26.2 %collective-permute-start.24 = (bf16[256,768]{1,0:T(8,128)(2,1)S(1)}, bf16[256,768]{1,0:T(8,128)(2,1)S(1)}, u32[]{:S(2)}, u32[]{:S(2)}) collective-permute-start(bf16[256,768]{1,0:T(8,128)(2,1)S(1)} %shard_map.121), channel_id=1, source_target_pairs={{0,16},{8,24},{16,0},{24,8},{1,17},{9,25},{17,1},{25,9},{2,18},{10... | collective-permute-start | bytes 1179656 | tf_op jit(solution)/shard_map/ppermute | solution.py:402
  190.8 11.8 %collective-permute-start.31 = (bf16[256,768]{1,0:T(8,128)(2,1)S(1)}, bf16[256,768]{1,0:T(8,128)(2,1)S(1)}, u32[]{:S(2)}, u32[]{:S(2)}) collective-permute-start(bf16[256,768]{1,0:T(8,128)(2,1)S(1)} %fusion.2), channel_id=1, source_target_pairs={{0,2},{1,5},{2,0},{3,7},{4,6},{5,1},{6,4},{7,3},{8,10},{9,13},{10,... | collective-permute-start | bytes 1179656 | tf_op jit(solution)/shard_map/ppermute | solution.py:402
  203.0 23.2 %collective-permute-start.32 = (bf16[256,768]{1,0:T(8,128)(2,1)S(1)}, bf16[256,768]{1,0:T(8,128)(2,1)S(1)}, u32[]{:S(2)}, u32[]{:S(2)}) collective-permute-start(bf16[256,768]{1,0:T(8,128)(2,1)S(1)} %shard_map.126), channel_id=1, source_target_pairs={{0,24},{8,16},{16,8},{24,0},{1,25},{9,17},{17,9},{25,1},{2,26},{10... | collective-permute-start | bytes 1179656 | tf_op jit(solution)/shard_map/ppermute | solution.py:402
  203.8 7.8 %collective-permute-start.35 = (bf16[256,768]{1,0:T(8,128)(2,1)S(1)}, bf16[256,768]{1,0:T(8,128)(2,1)S(1)}, u32[]{:S(2)}, u32[]{:S(2)}) collective-permute-start(bf16[256,768]{1,0:T(8,128)(2,1)S(1)} %fusion.3), channel_id=1, source_target_pairs={{0,2},{1,5},{2,0},{3,7},{4,6},{5,1},{6,4},{7,3},{8,10},{9,13},{10,... | collective-permute-start | bytes 1179656 | tf_op jit(solution)/shard_map/ppermute | solution.py:402

commit v7 on v5

--- a/solution.py
+++ b/solution.py
@@ -186,11 +186,15 @@
     return incoming
 
 
-def select_kernel(capacity, choices, experts, base_ref, part_ref, out_ref, place_ref):
-    length = part_ref.shape[0] - ID_ROWS
+def select_kernel(capacity, choices, experts, base_ref, *refs):
+    parts, (out_ref, place_ref) = refs[:-2], refs[-2:]
+    length = parts[0].shape[0] - ID_ROWS
+    part = parts[-1][...]
+    for other in parts[:-1]:
+        part = jnp.where(base_ref[1] > 0, other[...], part)
     before = lower_ones(length).astype(BF16)
     slot = lax.broadcasted_iota(jnp.int32, (capacity, length), 0).astype(F32)
-    ids = part_ref[length:, :length].astype(F32)
+    ids = part[length:, :length].astype(F32)
     rows = []
     for j in range(experts):
         expert = (base_ref[0] + j).astype(F32)
@@ -209,18 +213,18 @@
     place = jnp.concatenate(rows, axis=0)
     place_ref[...] = place
     out_ref[...] = lax.dot_general(
-        part_ref[:length, :], place, (((0,), (1,)), ((), ())), preferred_element_type=F32
+        part[:length, :], place, (((0,), (1,)), ((), ())), preferred_element_type=F32
     ).astype(BF16)
 
 
-def select_slots(base, part, capacity, choices, experts):
-    rows, width = part.shape
+def select_slots(base, parts, capacity, choices, experts):
+    rows, width = parts[0].shape
     length = rows - ID_ROWS
     slots = experts * capacity
     whole = pl.BlockSpec(memory_space=pltpu.VMEM)
     return pl.pallas_call(
         functools.partial(select_kernel, capacity, choices, experts),
-        in_specs=[pl.BlockSpec(memory_space=pltpu.SMEM), whole],
+        in_specs=[pl.BlockSpec(memory_space=pltpu.SMEM), *([whole] * len(parts))],
         out_shape=(
             jax.ShapeDtypeStruct((width, slots), BF16),
             jax.ShapeDtypeStruct((slots, length), BF16),
@@ -229,7 +233,7 @@
             flops=2 * slots * length * width, bytes_accessed=4 * slots * width, transcendentals=0
         ),
         compiler_params=pltpu.CompilerParams(vmem_limit_bytes=VMEM_LIMIT),
-    )(base, part)
+    )(base, *parts)
 
 
 def combine_kernel(place_ref, *refs):
@@ -357,39 +361,53 @@
     )(plan, *[x for section in xs for x in section], router_rows, gate_rows, up_rows, *(sums or ()))
 
 
-def down_kernel(plan_ref, hidden_ref, down_ref, *out_refs):
+def down_kernel(blocks, sections, plan_ref, hidden_ref, down_ref, *out_refs):
     experts, slots, _ = hidden_ref.shape
-    width = out_refs[0].shape[2]
-    part = slots // len(out_refs)
+    part = slots // sections
+    turn = pl.program_id(0) // blocks
     for j in range(experts):
         share = jnp.dot(hidden_ref[j], down_ref[j], preferred_element_type=F32).astype(BF16)
-        for section, out_ref in enumerate(out_refs):
-            out_ref[0, j * part : (j + 1) * part, :] = share[section * part : (section + 1) * part]
-
-
-def down_part(plan, hidden, down_weight, width, sections):
-    blocks = plan.shape[0]
+        for i in range(len(out_refs) // sections):
+
+            @pl.when(turn == i)
+            def _():
+                for section in range(sections):
+                    out_ref = out_refs[i * sections + section]
+                    out_ref[0, j * part : (j + 1) * part, :] = share[
+                        section * part : (section + 1) * part
+                    ]
+
+
+def down_part(plans, hidden, down_weight, width, sections):
+    blocks = plans[0].shape[0]
     experts, slots, units = hidden.shape
     rows = experts * slots // sections
-    return pl.pallas_call(
-        down_kernel,
+
+    def out_spec(i):
+        return pl.BlockSpec(
+            (1, rows, width), lambda p, plan: (jnp.clip(p - i * blocks, 0, blocks - 1), 0, 0)
+        )
+
+    out = pl.pallas_call(
+        functools.partial(down_kernel, blocks, sections),
         grid_spec=pltpu.PrefetchScalarGridSpec(
             num_scalar_prefetch=1,
-            grid=(blocks,),
+            grid=(len(plans) * blocks,),
             in_specs=[
                 pl.BlockSpec(memory_space=pltpu.VMEM),
                 pl.BlockSpec((experts, units, width), lambda p, plan: (0, 0, plan[p])),
             ],
-            out_specs=[pl.BlockSpec((1, rows, width), lambda p, plan: (p, 0, 0))] * sections,
-        ),
-        out_shape=[jax.ShapeDtypeStruct((blocks, rows, width), BF16)] * sections,
+            out_specs=[out_spec(i) for i in range(len(plans)) for _ in range(sections)],
+        ),
+        out_shape=[jax.ShapeDtypeStruct((blocks, rows, width), BF16)] * (len(plans) * sections),
         cost_estimate=pl.CostEstimate(
-            flops=2 * experts * slots * blocks * width * units,
-            bytes_accessed=2 * experts * blocks * width * units,
+            flops=2 * experts * slots * len(plans) * blocks * width * units,
+            bytes_accessed=2 * experts * len(plans) * blocks * width * units,
             transcendentals=0,
         ),
         compiler_params=pltpu.CompilerParams(vmem_limit_bytes=VMEM_LIMIT),
-    )(plan, hidden, down_weight)
+    )(jnp.concatenate(plans), hidden, down_weight)
+    return [out[i * sections : (i + 1) * sections] for i in range(len(plans))]
 
 
 def added(left, right):
@@ -443,7 +461,9 @@
     shares = lax.axis_size("exp")
     width = attn_query.shape[1]
     experts_here = router_weight.shape[1]
-    base = (lax.axis_index("seq") * experts_here).astype(jnp.int32).reshape(1)
+    section = lax.axis_index("seq")
+    inner = (section > 0) & (section < groups - 1)
+    base = jnp.stack([section * experts_here, inner]).astype(jnp.int32)
     router_rows = router_weight.reshape(shares, width, experts_here).transpose(0, 2, 1)
     gate_rows = gate_weight.swapaxes(1, 2)
     up_rows = up_weight.swapaxes(1, 2)
@@ -455,89 +475,95 @@
         attn_query, intra, cumulative, incoming, residual, norm_gain, expert_ids.T
     )
 
-    half = groups // 2
-    chunks = [(0, half)] + [(half + i, i) for i in range(1, half)]
     capacity = 4 * length // (experts_here * groups)
     choices = expert_ids.shape[1]
 
-    def moved(part, offset):
-        return swapped(part, "seq", offset, offset)
-
-    def select(part):
-        return select_slots(base, part, capacity, choices, experts_here)
+    def select(*parts):
+        return select_slots(base, parts, capacity, choices, experts_here)
 
     weights = (router_rows, gate_rows, up_rows)
-    if shares == 8:
-        pieces = paired_chunks(chunks, stream, moved, select, weights, down_weight)
+    if shares == 8 and groups == 4:
+        pieces = paired_chunks(stream, select, weights, down_weight)
     else:
         order = jnp.arange(shares, dtype=jnp.int32)
         middle = shares // 2
-        pieces = {}
-        for chunk in chunks:
-            chosen = [select(moved(stream, offset) if offset else stream) for offset in chunk]
+        pieces = []
+        for first in range(0, groups, 2):
+            chunk = (first, first + 1)
+            chosen = [
+                select(swapped(stream, "seq", offset, offset) if offset else stream)
+                for offset in chunk
+            ]
             gathered = [lax.all_gather(slots, "exp", axis=0) for slots, _ in chosen]
             sums = gate_part(order[:middle], [[x[:middle]] for x in gathered], *weights)
             hidden = gate_part(order[middle:], [[x[middle:]] for x in gathered], *weights, sums)
-            partial = down_part(order, hidden, down_weight, width, len(chunk))
+            (partial,) = down_part([order], hidden, down_weight, width, len(chunk))
             for offset, share, (_, place) in zip(chunk, partial, chosen):
                 share = lax.psum_scatter(share, "exp", scatter_dimension=0)
-                pieces[offset] = combine_slots(place, [share])
+                piece = combine_slots(place, [share])
+                pieces.append(swapped(piece, "seq", offset, offset) if offset else piece)
     total = stream[:length].astype(F32)
-    for offset, piece in pieces.items():
-        if offset:
-            piece = moved(piece, offset)
+    for piece in pieces:
         total = total + piece.astype(F32)
     return total.astype(BF16)
 
 
-def paired_chunks(chunks, stream, moved, select, weights, down_weight):
+def paired_chunks(stream, select, weights, down_weight):
     plane = PairedPlane()
     width = stream.shape[1]
     tie = lax.optimization_barrier
     two, far_two, near, near_far, chosen = {}, {}, {}, {}, {}
 
-    def gather(offset, part):
-        chosen[offset] = select(part)
-        two[offset] = plane.first(chosen[offset][0])
-        near[offset] = plane.across(two[offset])
-        far_two[offset] = plane.second(two[offset])
-        near_far[offset] = plane.across(far_two[offset])
-
-    gather(0, stream)
-    later, _ = tie((stream, two[0]))
-    arrived = moved(later, chunks[0][1])
-    part, _ = tie((arrived, far_two[0]))
-    gather(chunks[0][1], part)
-    later, _ = tie((stream, arrived))
-    parts = {offset: moved(later, offset) for chunk in chunks[1:] for offset in reversed(chunk)}
+    def across_middle(part):
+        return lax.ppermute(part, "seq", [(1, 2), (2, 1)])
+
+    def outward(part):
+        return lax.ppermute(part, "seq", [(1, 0), (2, 3)])
+
+    def gather(name, behind):
+        two[name], _ = tie((plane.first(chosen[name][0]), behind))
+        near[name] = plane.across(two[name])
+        far_two[name] = plane.second(two[name])
+
+    neighbour = swapped(stream, "seq", 1, 1)
+    third = across_middle(stream)
+    chosen["own"] = select(stream)
+    gather("own", [neighbour, third])
+    passed_third = outward(third)
+    fourth = across_middle(neighbour)
+    chosen["neighbour"] = select(neighbour)
+    gather("neighbour", [passed_third, fourth, far_two["own"]])
+    passed_fourth = outward(fourth)
+    chosen["third"] = select(third, passed_third)
+    gather("third", passed_fourth)
+    chosen["fourth"] = select(fourth, passed_fourth)
 
     pieces = {}
-    sent, got_two, one = [], [], []
-    for i, chunk in enumerate(chunks):
-        after = chunks[i + 1][::-1] if i + 1 < len(chunks) else ()
-        early = [[two[offset], near[offset]] for offset in chunk]
-        late = [[far_two[offset], near_far[offset]] for offset in chunk]
+    sent, one = [], []
+    for chunk, after in ((("neighbour", "third"), "fourth"), (("fourth", "own"), None)):
+        early = [[two[name], near[name]] for name in chunk]
         if after:
-            gather(after[0], parts[after[0]])
-            early, _ = tie((early, chosen[after[0]]))
-        if sent:
-            early, _ = tie((early, sent))
+            early, _ = tie((early, chosen[after]))
+        early, _ = tie((early, sent))
         sums = gate_part(plane.early, early, *weights)
-        late, sums = tie((late, sums))
         if after:
-            part, _ = tie((parts[after[1]], sums))
-            gather(after[1], part)
-            late, _ = tie((late, [two[after[0]], chosen[after[1]]]))
+            gather(after, sums)
+            far_two[chunk[1]], sums = tie((far_two[chunk[1]], sums))
+        late = [[far_two[name], plane.across(far_two[name])] for name in chunk]
+        if after:
+            late, _ = tie((late, two[after]))
         hidden = gate_part(plane.late, late, *weights, sums)
         if after:
-            hidden, _ = tie((hidden, [far_two[after[0]], two[after[1]]]))
-        if one:
+            hidden, _ = tie((hidden, far_two[after]))
+            (theirs,) = down_part([plane.theirs], hidden, down_weight, width, len(chunk))
+            hidden, theirs = tie((hidden, theirs))
+            (mine,) = down_part([plane.mine], hidden, down_weight, width, len(chunk))
+        else:
             hidden, _ = tie((hidden, one))
-        theirs = down_part(plane.theirs, hidden, down_weight, width, len(chunk))
-        hidden, theirs = tie((hidden, theirs))
-        mine = down_part(plane.mine, hidden, down_weight, width, len(chunk))
+            theirs, mine = down_part([plane.theirs, plane.mine], hidden, down_weight, width, len(chunk))
+            theirs, _ = tie((theirs, list(pieces.values())))
         sent, got_two, one = [], [], []
-        for k, offset in enumerate(chunk):
+        for k, name in enumerate(chunk):
             near_share = plane.across(theirs[k])
             two_share = added(mine[k][2:], near_share[2:])
             sent.append(two_share)
@@ -547,10 +573,17 @@
             one_share = added(added(mine[k][1], near_share[1]), got_two[k][1])
             one.append(one_share)
             got_one = plane.once(one_share)
-            pieces[offset] = combine_slots(
-                chosen[offset][1], [mine[k][0], near_share[0], got_two[k][0], got_one]
+            pieces[name] = combine_slots(
+                chosen[name][1], [mine[k][0], near_share[0], got_two[k][0], got_one]
             )
-    return pieces
+    return [
+        pieces["own"],
+        swapped(pieces["neighbour"], "seq", 1, 1),
+        lax.ppermute(pieces["third"], "seq", [(1, 2), (2, 1)]),
+        lax.ppermute(pieces["third"], "seq", [(0, 2), (3, 1)]),
+        lax.ppermute(pieces["fourth"], "seq", [(1, 3), (2, 0)]),
+        lax.ppermute(pieces["fourth"], "seq", [(0, 3), (3, 0)]),
+    ]
 
 
 def solution(mesh):

time: 224 us -> 226 us (level)
  waiting for transfers between devices: 96 us -> 73.6 us
  local copies, waits for them, and re-layouts: 7.53 us -> 19.1 us
  Pallas kernels: 68 us -> 74.5 us
  other arithmetic: 4.14 us -> 7.58 us
  starting transfers between devices: 46.7 us -> 49.1 us
    ppermute x34 -> x30, waiting for transfers between devices: 92 us -> 52.4 us  [swapped(): return lax.ppermute(array, axis, pairs)]
    ppermute x0 -> x8, starting transfers between devices: none -> 18.4 us  [the longest x1 6.44 us: paired_chunks(): lax.ppermute(pieces['third'], 'seq', [(0, 2), (3, 1)])]
    ppermute x0 -> x8, waiting for transfers between devices: none -> 17.2 us  [the longest x1 10.5 us: paired_chunks(): lax.ppermute(pieces['fourth'], 'seq', [(1, 3), (2, 0)])]
    ppermute x34 -> x30, starting transfers between devices: 37.3 us -> 21.3 us  [swapped(): return lax.ppermute(array, axis, pairs)]
    unnamed x24 -> x58, local copies, waits for them, and re-layouts: 6.35 us -> 15.9 us
    convert_element_type x8, other arithmetic: 1.46 us -> 5.68 us  [added(): return (left.astype(F32) + right.astype(F32)).astype(BF16)]
    pallas_call x4 -> x3, Pallas kernels: 24.3 us -> 28.5 us  [down_part(): pl.pallas_call(functools.partial(down_kernel, blocks, sections), grid_spe...]
  transfers between devices with their start and end apart: 36 -> 40, of which waited for: 14 -> 15; matrix products, arithmetic and copies ran while one was open for 2% -> 4% of each run, Pallas kernels for 24% -> 28%
where the time goes in v7:
time: 226 us; the launch traced here: 225 us
  Pallas kernels  74.5 us (33%)
  waiting for transfers between devices  73.6 us (33%)
  starting transfers between devices  49.1 us (22%)
  local copies, waits for them, and re-layouts  19.1 us (8%)
  other arithmetic  7.58 us (3%)
    ppermute x30, waiting for transfers between devices, swapped(): return lax.ppermute(array, axis, pairs)  52.4 us
    pallas_call x4, Pallas kernels, gate_part(): pl.pallas_call(functools.partial(gate_kernel, counts, len(xs), last), gri...  37 us
    pallas_call x3, Pallas kernels, down_part(): pl.pallas_call(functools.partial(down_kernel, blocks, sections), grid_spe...  28.5 us
    ppermute x30, starting transfers between devices, swapped(): return lax.ppermute(array, axis, pairs)  21.3 us
    unnamed x58, local copies, waits for them, and re-layouts  15.9 us
    ppermute x1, waiting for transfers between devices, paired_chunks(): lax.ppermute(pieces['fourth'], 'seq', [(1, 3), (2, 0)])  10.5 us
    ppermute x2, starting transfers between devices, shifted(): return lax.ppermute(array, axis, pairs)  9.42 us
    ppermute x2, waiting for transfers between devices, outward(): return lax.ppermute(part, 'seq', [(1, 0), (2, 3)])  6.67 us
  transfers between devices with their start and end apart: 40, of which 15 were waited for; matrix products, arithmetic and copies ran while one was open for 4% of the time, Pallas kernels for 28%

profile of v7, /device:TPU:0, one launch (start us, length us, event | category | flops | bytes accessed | tf_op | source)
XLA Modules:
  0.0 224.8 jit_solution(7756575107038833475)
XLA Ops:
  0.0 1.0 copy-done.2
  1.0 1.0 copy-done.4
  2.0 0.7 copy-done.26
  2.7 1.0 shard_map.109
  3.7 4.9 %collective-permute-start = (bf16[784,128]{1,0:T(8,128)(2,1)S(1)}, bf16[784,128]{1,0:T(8,128)(2,1)S(1)}, u32[]{:S(2)}, u32[]{:S(2)}) collective-permute-start(bf16[784,128]{1,0:T(8,128)(2,1)S(1)} %get-tuple-element.62), channel_id=1, source_target_pairs={{0,8},{8,16},{16,24},{1,9},{9,17},{17,25},{2,10},{10,18},{18,26},{... | collective-permute-start | bytes 602120 | tf_op jit(solution)/shard_map/ppermute | solution.py:26
  9.4 1.0 copy-done
  10.4 1.0 copy-done.3
  11.4 1.0 copy-done.5
  13.1 1.4 shard_map.110.intra_ref
  14.8 4.5 %collective-permute-start.1 = (bf16[784,128]{1,0:T(8,128)(2,1)S(1)}, bf16[784,128]{1,0:T(8,128)(2,1)S(1)}, u32[]{:S(2)}, u32[]{:S(2)}) collective-permute-start(bf16[784,128]{1,0:T(8,128)(2,1)S(1)} %concatenate.7), channel_id=1, source_target_pairs={{0,16},{8,24},{1,17},{9,25},{2,18},{10,26},{3,19},{11,27},{4,20},{... | collective-permute-start | bytes 602120 | tf_op jit(solution)/shard_map/ppermute | solution.py:26
  19.3 3.9 %collective-permute-done.1 = bf16[784,128]{1,0:T(8,128)(2,1)S(1)} collective-permute-done((bf16[784,128]{1,0:T(8,128)(2,1)S(1)}, bf16[784,128]{1,0:T(8,128)(2,1)S(1)}, u32[]{:S(2)}, u32[]{:S(2)}) %collective-permute-start.1) | collective-permute-done | bytes 200736 | tf_op jit(solution)/shard_map/ppermute | solution.py:26
  23.4 0.9 shard_map.111.refs_0_
  25.0 1.0 shard_map.112
  26.7 1.5 collective-permute-start.9
  28.2 5.8 %collective-permute-start.2 = (bf16[272,768]{1,0:T(8,128)(2,1)S(1)}, bf16[272,768]{1,0:T(8,128)(2,1)S(1)}, u32[]{:S(2)}, u32[]{:S(2)}) collective-permute-start(bf16[272,768]{1,0:T(8,128)(2,1)S(1)} %shard_map.111.refs_0_), channel_id=1, source_target_pairs={{0,8},{8,0},{16,24},{24,16},{1,9},{9,1},{17,25},{25,17},{2,10},{10... | collective-permute-start | bytes 1253384 | tf_op jit(solution)/shard_map/ppermute | solution.py:420
  34.0 1.3 collective-permute-start.8
  35.3 8.2 %collective-permute-done.2.refs_0_ = bf16[272,768]{1,0:T(8,128)(2,1)S(1)} collective-permute-done((bf16[272,768]{1,0:T(8,128)(2,1)S(1)}, bf16[272,768]{1,0:T(8,128)(2,1)S(1)}, u32[]{:S(2)}, u32[]{:S(2)}) %collective-permute-start.2) | collective-permute-done | bytes 417824 | tf_op jit(solution)/shard_map/ppermute | solution.py:420
  44.2 1.0 shard_map.114
  45.3 1.5 collective-permute-start.6
  46.8 4.4 %collective-permute-done.8.refs_1_ = bf16[272,768]{1,0:T(8,128)(2,1)S(1)} collective-permute-done((bf16[272,768]{1,0:T(8,128)(2,1)S(1)}, bf16[272,768]{1,0:T(8,128)(2,1)S(1)}, u32[]{:S(2)}, u32[]{:S(2)}) %collective-permute-start.8) | collective-permute-done | bytes 417824 | tf_op jit(solution)/shard_map/ppermute | solution.py:521
  51.2 1.0 shard_map.115
  52.3 1.6 collective-permute-start.12
  53.8 1.3 collective-permute-start.4
  55.1 1.0 collective-permute-done.6
  56.2 7.4 %collective-permute-done.10.refs_2_ = bf16[2,768,256]{2,1,0:T(8,128)(2,1)S(1)} collective-permute-done((bf16[2,768,256]{2,1,0:T(8,128)(2,1)S(1)}, bf16[2,768,256]{2,1,0:T(8,128)(2,1)S(1)}, u32[]{:S(2)}, u32[]{:S(2)}) %collective-permute-start.10) | collective-permute-done | bytes 786464 | tf_op jit(solution)/shard_map/ppermute | solution.py:420
  64.0 2.3 %collective-permute-done.4.refs_1_ = bf16[272,768]{1,0:T(8,128)(2,1)S(1)} collective-permute-done((bf16[272,768]{1,0:T(8,128)(2,1)S(1)}, bf16[272,768]{1,0:T(8,128)(2,1)S(1)}, u32[]{:S(2)}, u32[]{:S(2)}) %collective-permute-start.4) | collective-permute-done | bytes 417824 | tf_op jit(solution)/shard_map/ppermute | solution.py:521
  66.2 0.8 copy-done.14
  67.1 1.0 copy-done.15
  68.1 1.0 shard_map.113
  69.2 1.4 collective-permute-start.5
  70.5 8.3 %collective-permute-done.19.refs_0_ = bf16[2,768,256]{2,1,0:T(8,128)(2,1)} collective-permute-done((bf16[2,768,256]{2,1,0:T(8,128)(2,1)S(1)}, bf16[2,768,256]{2,1,0:T(8,128)(2,1)}, u32[]{:S(2)}, u32[]{:S(2)}) %collective-permute-start.19) | collective-permute-done | bytes 786464 | tf_op jit(solution)/shard_map/ppermute | solution.py:420
  78.9 9.4 %shard_map.116 = (f32[2,576,256]{2,1,0:T(8,128)S(1)}, f32[2,576,256]{2,1,0:T(8,128)S(1)}, f32[2,2,256]{2,1,0:T(2,128)S(1)}) custom-call(s32[4]{0:T(128)S(1)} %get-tuple-element.120.plan_ref, bf16[2,768,256]{2,1,0:T(8,128)(2,1)S(1)} %pad_maximum_fusion.1.refs_0_, bf16[2,768,256]{2,1,0:T(8,128)(2,1)} %collective-permute-done.11.refs_1_, ...), custom_call_target="tpu_custom_call" | custom-call | flops 3623878656 | bytes 14155776 | tf_op jit(solution)/shard_map/pallas_call | solution.py:339
  88.3 1.0 copy-done.6
  89.4 1.0 copy-done.8
  91.1 2.0 collective-permute-done.22.refs_3_
  93.2 1.3 copy-done.7
  94.4 1.3 copy-done.9
  95.7 9.8 %shard_map.117.hidden_ref = bf16[2,256,576]{2,1,0:T(8,128)(2,1)S(1)} custom-call(s32[4]{0:T(128)S(1)} %add_add_fusion.plan_ref, bf16[2,768,256]{2,1,0:T(8,128)(2,1)} %collective-permute-done.19.refs_0_, bf16[2,768,256]{2,1,0:T(8,128)(2,1)} %collective-permute-done.20.refs_1_, bf16[2,768,256]{2,1,0:T(8,128)(2,1)} %collective-permute-done.21.refs_2_, ...), custom_call_target="tpu_custom_call" | custom-call | flops 3623878656 | bytes 14155776 | tf_op jit(solution)/shard_map/pallas_call | solution.py:339
  105.5 0.9 copy-done.12
  106.4 8.5 %shard_map.118 = (bf16[4,256,768]{2,1,0:T(8,128)(2,1)}, bf16[4,256,768]{2,1,0:T(8,128)(2,1)}) custom-call(s32[4]{0:T(128)S(1)} %get-tuple-element.121.plan_ref, bf16[2,256,576]{2,1,0:T(8,128)(2,1)S(1)} %shard_map.117.hidden_ref, bf16[2,576,6144]{2,1,0:T(8,128)(2,1)} %down_ref.5), custom_call_target="tpu_custom_call" | custom-call | flops 1811939328 | bytes 7077888 | tf_op jit(solution)/shard_map/pallas_call | solution.py:391
  116.5 7.2 %shard_map.119 = (bf16[4,256,768]{2,1,0:T(8,128)(2,1)S(1)}, bf16[4,256,768]{2,1,0:T(8,128)(2,1)S(1)}) custom-call(s32[4]{0:T(128)S(1)} %pad_add_fusion.3.plan_ref, bf16[2,256,576]{2,1,0:T(8,128)(2,1)S(1)} %shard_map.117.hidden_ref, bf16[2,576,6144]{2,1,0:T(8,128)(2,1)} %down_ref.5), custom_call_target="tpu_custom_call" | custom-call | flops 1811939328 | bytes 7077888 | tf_op jit(solution)/shard_map/pallas_call | solution.py:391
  123.8 1.0 copy-done.13
  125.0 1.3 add_convert_fusion.2
  126.4 1.3 add_convert_fusion.3
  127.8 2.1 collective-permute-start.25
  129.8 8.7 %shard_map.120 = (f32[2,576,256]{2,1,0:T(8,128)S(1)}, f32[2,576,256]{2,1,0:T(8,128)S(1)}, f32[2,2,256]{2,1,0:T(2,128)S(1)}) custom-call(s32[4]{0:T(128)S(1)} %get-tuple-element.120.plan_ref, bf16[2,768,256]{2,1,0:T(8,128)(2,1)S(1)} %pad_maximum_fusion.refs_0_, bf16[2,768,256]{2,1,0:T(8,128)(2,1)S(1)} %collective-permute-done.17.refs_1_, ...), custom_call_target="tpu_custom_call" | custom-call | flops 3623878656 | bytes 14155776 | tf_op jit(solution)/shard_map/pallas_call | solution.py:339
  138.6 1.0 slice_bitcast_fusion.5.refs_1_
  139.6 1.0 slice_bitcast_fusion.7.refs_1_
  140.6 9.1 %shard_map.121.hidden_ref = bf16[2,256,576]{2,1,0:T(8,128)(2,1)S(1)} custom-call(s32[4]{0:T(128)S(1)} %add_add_fusion.plan_ref, bf16[2,768,256]{2,1,0:T(8,128)(2,1)S(1)} %copy-done.13, bf16[2,768,256]{2,1,0:T(8,128)(2,1)S(1)} %collective-permute-done.15.refs_1_, bf16[2,768,256]{2,1,0:T(8,128)(2,1)S(1)} %copy-done.11, ...), custom_call_target="tpu_custom_call" | custom-call | flops 3623878656 | bytes 14155776 | tf_op jit(solution)/shard_map/pallas_call | solution.py:339
  149.8 1.2 fusion.1
  151.0 1.1 fusion
  152.2 2.1 collective-permute-start.27
  154.3 12.8 %shard_map.122 = (bf16[4,256,768]{2,1,0:T(8,128)(2,1)S(1)}, bf16[4,256,768]{2,1,0:T(8,128)(2,1)S(1)}, bf16[4,256,768]{2,1,0:T(8,128)(2,1)S(1)}, bf16[4,256,768]{2,1,0:T(8,128)(2,1)S(1)}) custom-call(s32[8]{0:T(128)S(1)} %concatenate.8.plan_ref, bf16[2,256,576]{2,1,0:T(8,128)(2,1)S(1)} %shard_map.121.hidden_ref, bf16[2,576,6144]{2,1,0:T(8,128)(2,1)} %down_ref.5), custom_call_target="tpu_custom_call" | custom-call | flops 3623878656 | bytes 14155776 | tf_op jit(solution)/shard_map/pallas_call | solution.py:391
  169.0 2.9 %collective-permute-done.30 = bf16[4,256,768]{2,1,0:T(8,128)(2,1)S(1)} collective-permute-done((bf16[4,256,768]{2,1,0:T(8,128)(2,1)S(1)}, bf16[4,256,768]{2,1,0:T(8,128)(2,1)S(1)}, u32[]{:S(2)}, u32[]{:S(2)}) %collective-permute-start.30) | collective-permute-done | bytes 1572896 | tf_op jit(solution)/shard_map/ppermute | solution.py:420
  172.2 2.0 collective-permute-done.29
  174.4 9.8 %collective-permute-done.31 = bf16[2,256,768]{2,1,0:T(8,128)(2,1)S(1)} collective-permute-done((bf16[2,256,768]{2,1,0:T(8,128)(2,1)S(1)}, bf16[2,256,768]{2,1,0:T(8,128)(2,1)S(1)}, u32[]{:S(2)}, u32[]{:S(2)}) %collective-permute-start.31) | collective-permute-done | bytes 786464 | tf_op jit(solution)/shard_map/ppermute | solution.py:420
  185.0 6.4 %collective-permute-start.36 = (bf16[256,768]{1,0:T(8,128)(2,1)S(1)}, bf16[256,768]{1,0:T(8,128)(2,1)S(1)}, u32[]{:S(2)}, u32[]{:S(2)}) collective-permute-start(bf16[256,768]{1,0:T(8,128)(2,1)S(1)} %shard_map.124), channel_id=1, source_target_pairs={{0,16},{24,8},{1,17},{25,9},{2,18},{26,10},{3,19},{27,11},{4,20},{... | collective-permute-start | bytes 1179656 | tf_op jit(solution)/shard_map/ppermute | solution.py:583
  191.6 2.1 collective-permute-start.37
  193.7 4.8 %collective-permute-done.32 = bf16[2,256,768]{2,1,0:T(8,128)(2,1)S(1)} collective-permute-done((bf16[2,256,768]{2,1,0:T(8,128)(2,1)S(1)}, bf16[2,256,768]{2,1,0:T(8,128)(2,1)S(1)}, u32[]{:S(2)}, u32[]{:S(2)}) %collective-permute-start.32) | collective-permute-done | bytes 786464 | tf_op jit(solution)/shard_map/ppermute | solution.py:420
  199.9 1.3 collective-permute-start.38
  201.2 5.4 %collective-permute-done.33.refs_3_ = bf16[256,768]{1,0:T(8,128)(2,1)S(1)} collective-permute-done((bf16[256,768]{1,0:T(8,128)(2,1)S(1)}, bf16[256,768]{1,0:T(8,128)(2,1)S(1)}, u32[]{:S(2)}, u32[]{:S(2)}) %collective-permute-start.33) | collective-permute-done | bytes 393248 | tf_op jit(solution)/shard_map/ppermute | solution.py:420
  206.6 6.0 %collective-permute-start.39 = (bf16[256,768]{1,0:T(8,128)(2,1)S(1)}, bf16[256,768]{1,0:T(8,128)(2,1)S(1)}, u32[]{:S(2)}, u32[]{:S(2)}) collective-permute-start(bf16[256,768]{1,0:T(8,128)(2,1)S(1)} %shard_map.126), channel_id=1, source_target_pairs={{0,24},{24,0},{1,25},{25,1},{2,26},{26,2},{3,27},{27,3},{4,28},{28... | collective-permute-start | bytes 1179656 | tf_op jit(solution)/shard_map/ppermute | solution.py:585
  213.2 10.5 %collective-permute-done.38 = bf16[256,768]{1,0:T(8,128)(2,1)S(1)} collective-permute-done((bf16[256,768]{1,0:T(8,128)(2,1)S(1)}, bf16[256,768]{1,0:T(8,128)(2,1)S(1)}, u32[]{:S(2)}, u32[]{:S(2)}) %collective-permute-start.38) | collective-permute-done | bytes 393248 | tf_op jit(solution)/shard_map/ppermute | solution.py:584
  223.7 1.1 add_convert_fusion.8
  (133 shorter events, 12.3 us)
Async XLA Ops:
  0.0 1.0 copy-start.2
  1.0 1.0 copy-start.4
  3.7 10.8 %collective-permute-start = (bf16[784,128]{1,0:T(8,128)(2,1)S(1)}, bf16[784,128]{1,0:T(8,128)(2,1)S(1)}, u32[]{:S(2)}, u32[]{:S(2)}) collective-permute-start(bf16[784,128]{1,0:T(8,128)(2,1)S(1)} %get-tuple-element.62), channel_id=1, source_target_pairs={{0,8},{8,16},{16,24},{1,9},{9,17},{17,25},{2,10},{10,18},{18,26},{... | collective-permute-start | bytes 602120 | tf_op jit(solution)/shard_map/ppermute | solution.py:26
  9.4 1.0 copy-start
  10.4 1.0 copy-start.3
  11.4 1.0 copy-start.5
  14.4 8.9 %copy-start.1 = (bf16[256,768]{1,0:T(8,128)(2,1)S(1)}, bf16[256,768]{1,0:T(8,128)(2,1)}, u32[]{:S(2)}) copy-start(bf16[256,768]{1,0:T(8,128)(2,1)} %query_ref.3) | copy-start | bytes 1179652
  14.5 8.9 %copy-start.17 = (bf16[256,768]{1,0:T(8,128)(2,1)S(1)}, bf16[256,768]{1,0:T(8,128)(2,1)}, u32[]{:S(2)}) copy-start(bf16[256,768]{1,0:T(8,128)(2,1)} %residual_ref.1) | copy-start | bytes 1179652
  14.5 8.9 %copy-start.28 = (s32[256,2]{0,1:T(2,128)S(1)}, s32[256,2]{0,1:T(2,128)}, u32[]{:S(2)}) copy-start(s32[256,2]{0,1:T(2,128)} %param.17) | copy-start | bytes 6148
  14.8 8.5 %collective-permute-start.1 = (bf16[784,128]{1,0:T(8,128)(2,1)S(1)}, bf16[784,128]{1,0:T(8,128)(2,1)S(1)}, u32[]{:S(2)}, u32[]{:S(2)}) collective-permute-start(bf16[784,128]{1,0:T(8,128)(2,1)S(1)} %concatenate.7), channel_id=1, source_target_pairs={{0,16},{8,24},{1,17},{9,25},{2,18},{10,26},{3,19},{11,27},{4,20},{... | collective-permute-start | bytes 602120 | tf_op jit(solution)/shard_map/ppermute | solution.py:26
  24.2 9.7 %collective-permute-start.7 = (bf16[272,768]{1,0:T(8,128)(2,1)S(1)}, bf16[272,768]{1,0:T(8,128)(2,1)S(1)}, u32[]{:S(2)}, u32[]{:S(2)}) collective-permute-start(bf16[272,768]{1,0:T(8,128)(2,1)S(1)} %shard_map.111.refs_0_), channel_id=1, source_target_pairs={{8,16},{16,8},{9,17},{17,9},{10,18},{18,10},{11,19},{19,11},{12,20... | collective-permute-start | bytes 1253384 | tf_op jit(solution)/shard_map/ppermute | solution.py:518
  26.7 8.6 %collective-permute-start.9 = (bf16[768,256]{1,0:T(8,128)(2,1)S(1)}, bf16[768,256]{1,0:T(8,128)(2,1)S(1)}, u32[]{:S(2)}, u32[]{:S(2)}) collective-permute-start(bf16[768,256]{1,0:T(8,128)(2,1)S(1)} %get-tuple-element.66), channel_id=1, source_target_pairs={{0,2},{1,5},{2,0},{3,7},{4,6},{5,1},{6,4},{7,3},{8,10},{9,13},{10,... | collective-permute-start | bytes 1179656 | tf_op jit(solution)/shard_map/ppermute | solution.py:420
  28.2 15.3 %collective-permute-start.2 = (bf16[272,768]{1,0:T(8,128)(2,1)S(1)}, bf16[272,768]{1,0:T(8,128)(2,1)S(1)}, u32[]{:S(2)}, u32[]{:S(2)}) collective-permute-start(bf16[272,768]{1,0:T(8,128)(2,1)S(1)} %shard_map.111.refs_0_), channel_id=1, source_target_pairs={{0,8},{8,0},{16,24},{24,16},{1,9},{9,1},{17,25},{25,17},{2,10},{10... | collective-permute-start | bytes 1253384 | tf_op jit(solution)/shard_map/ppermute | solution.py:420
  34.0 17.3 %collective-permute-start.8 = (bf16[272,768]{1,0:T(8,128)(2,1)S(1)}, bf16[272,768]{1,0:T(8,128)(2,1)S(1)}, u32[]{:S(2)}, u32[]{:S(2)}) collective-permute-start(bf16[272,768]{1,0:T(8,128)(2,1)S(1)} %collective-permute-done.7.refs_0_), channel_id=1, source_target_pairs={{8,0},{16,24},{9,1},{17,25},{10,2},{18,26},{11,3},{19,27},{12,4},{... | collective-permute-start | bytes 1253384 | tf_op jit(solution)/shard_map/ppermute | solution.py:521
  43.5 20.1 %collective-permute-start.10 = (bf16[2,768,256]{2,1,0:T(8,128)(2,1)S(1)}, bf16[2,768,256]{2,1,0:T(8,128)(2,1)S(1)}, u32[]{:S(2)}, u32[]{:S(2)}) collective-permute-start(bf16[2,768,256]{2,1,0:T(8,128)(2,1)S(1)} %pad_maximum_fusion.2.refs_2_), channel_id=1, source_target_pairs={{0,4},{1,3},{2,6},{3,1},{4,0},{5,7},{6,2},{7,5},{8,12},{9,11},{10,... | collective-permute-start | bytes 2359304 | tf_op jit(solution)/shard_map/ppermute | solution.py:420
  43.5 10.3 %collective-permute-start.3 = (bf16[272,768]{1,0:T(8,128)(2,1)S(1)}, bf16[272,768]{1,0:T(8,128)(2,1)S(1)}, u32[]{:S(2)}, u32[]{:S(2)}) collective-permute-start(bf16[272,768]{1,0:T(8,128)(2,1)S(1)} %collective-permute-done.2.refs_0_), channel_id=1, source_target_pairs={{8,16},{16,8},{9,17},{17,9},{10,18},{18,10},{11,19},{19,11},{12,20... | collective-permute-start | bytes 1253384 | tf_op jit(solution)/shard_map/ppermute | solution.py:518
  45.3 18.7 %copy-start.20 = (bf16[256,256]{1,0:T(8,128)(2,1)}, bf16[256,256]{1,0:T(8,128)(2,1)S(1)}, u32[]{:S(2)}) copy-start(bf16[256,256]{1,0:T(8,128)(2,1)S(1)} %get-tuple-element.111.place_ref) | copy-start | bytes 393220
  45.3 10.9 %collective-permute-start.6 = (bf16[768,256]{1,0:T(8,128)(2,1)S(1)}, bf16[768,256]{1,0:T(8,128)(2,1)S(1)}, u32[]{:S(2)}, u32[]{:S(2)}) collective-permute-start(bf16[768,256]{1,0:T(8,128)(2,1)S(1)} %get-tuple-element.65), channel_id=1, source_target_pairs={{0,2},{1,5},{2,0},{3,7},{4,6},{5,1},{6,4},{7,3},{8,10},{9,13},{10,... | collective-permute-start | bytes 1179656 | tf_op jit(solution)/shard_map/ppermute | solution.py:420
  52.3 11.7 %copy-start.22 = (bf16[256,256]{1,0:T(8,128)(2,1)}, bf16[256,256]{1,0:T(8,128)(2,1)S(1)}, u32[]{:S(2)}) copy-start(bf16[256,256]{1,0:T(8,128)(2,1)S(1)} %get-tuple-element.112.place_ref) | copy-start | bytes 393220
  52.3 11.6 %collective-permute-start.12 = (bf16[768,256]{1,0:T(8,128)(2,1)S(1)}, bf16[768,256]{1,0:T(8,128)(2,1)S(1)}, u32[]{:S(2)}, u32[]{:S(2)}) collective-permute-start(bf16[768,256]{1,0:T(8,128)(2,1)S(1)} %get-tuple-element.69), channel_id=1, source_target_pairs={{0,2},{1,5},{2,0},{3,7},{4,6},{5,1},{6,4},{7,3},{8,10},{9,13},{10,... | collective-permute-start | bytes 1179656 | tf_op jit(solution)/shard_map/ppermute | solution.py:420
  53.8 12.4 %collective-permute-start.4 = (bf16[272,768]{1,0:T(8,128)(2,1)S(1)}, bf16[272,768]{1,0:T(8,128)(2,1)S(1)}, u32[]{:S(2)}, u32[]{:S(2)}) collective-permute-start(bf16[272,768]{1,0:T(8,128)(2,1)S(1)} %collective-permute-done.3.refs_0_), channel_id=1, source_target_pairs={{8,0},{16,24},{9,1},{17,25},{10,2},{18,26},{11,3},{19,27},{12,4},{... | collective-permute-start | bytes 1253384 | tf_op jit(solution)/shard_map/ppermute | solution.py:521
  56.2 22.7 %copy-start.16 = (bf16[6144,2]{0,1:T(2,128)(2,1)S(1)}, bf16[6144,2]{0,1:T(2,128)(2,1)}, u32[]{:S(2)}) copy-start(bf16[6144,2]{0,1:T(2,128)(2,1)} %param.18) | copy-start | bytes 73732
  63.6 2.7 %copy-start.10 = (bf16[2,768,256]{2,1,0:T(8,128)(2,1)}, bf16[2,768,256]{2,1,0:T(8,128)(2,1)S(1)}, u32[]{:S(2)}) copy-start(bf16[2,768,256]{2,1,0:T(8,128)(2,1)S(1)} %collective-permute-done.10.refs_2_) | copy-start | bytes 2359300
  63.6 15.3 %collective-permute-start.11 = (bf16[2,768,256]{2,1,0:T(8,128)(2,1)S(1)}, bf16[2,768,256]{2,1,0:T(8,128)(2,1)}, u32[]{:S(2)}, u32[]{:S(2)}) collective-permute-start(bf16[2,768,256]{2,1,0:T(8,128)(2,1)S(1)} %pad_maximum_fusion.1.refs_0_), channel_id=1, source_target_pairs={{0,1},{1,0},{2,3},{3,2},{4,5},{5,4},{6,7},{7,6},{8,9},{9,8},{10,11... | collective-permute-start | bytes 2359304 | tf_op jit(solution)/shard_map/ppermute | solution.py:420
  63.6 15.3 %collective-permute-start.19 = (bf16[2,768,256]{2,1,0:T(8,128)(2,1)S(1)}, bf16[2,768,256]{2,1,0:T(8,128)(2,1)}, u32[]{:S(2)}, u32[]{:S(2)}) collective-permute-start(bf16[2,768,256]{2,1,0:T(8,128)(2,1)S(1)} %pad_maximum_fusion.1.refs_0_), channel_id=1, source_target_pairs={{0,4},{1,3},{2,6},{3,1},{4,0},{5,7},{6,2},{7,5},{8,12},{9,11},{10,... | collective-permute-start | bytes 2359304 | tf_op jit(solution)/shard_map/ppermute | solution.py:420
  67.0 11.9 %collective-permute-start.13 = (bf16[2,768,256]{2,1,0:T(8,128)(2,1)S(1)}, bf16[2,768,256]{2,1,0:T(8,128)(2,1)}, u32[]{:S(2)}, u32[]{:S(2)}) collective-permute-start(bf16[2,768,256]{2,1,0:T(8,128)(2,1)S(1)} %pad_maximum_fusion.3.refs_2_), channel_id=1, source_target_pairs={{0,1},{1,0},{2,3},{3,2},{4,5},{5,4},{6,7},{7,6},{8,9},{9,8},{10,11... | collective-permute-start | bytes 2359304 | tf_op jit(solution)/shard_map/ppermute | solution.py:420
  67.0 23.4 %collective-permute-start.21 = (bf16[2,768,256]{2,1,0:T(8,128)(2,1)S(1)}, bf16[2,768,256]{2,1,0:T(8,128)(2,1)}, u32[]{:S(2)}, u32[]{:S(2)}) collective-permute-start(bf16[2,768,256]{2,1,0:T(8,128)(2,1)S(1)} %pad_maximum_fusion.3.refs_2_), channel_id=1, source_target_pairs={{0,4},{1,3},{2,6},{3,1},{4,0},{5,7},{6,2},{7,5},{8,12},{9,11},{10,... | collective-permute-start | bytes 2359304 | tf_op jit(solution)/shard_map/ppermute | solution.py:420
  67.1 1.0 copy-start.15
  69.1 19.2 %copy-start.24 = (bf16[256,256]{1,0:T(8,128)(2,1)}, bf16[256,256]{1,0:T(8,128)(2,1)S(1)}, u32[]{:S(2)}) copy-start(bf16[256,256]{1,0:T(8,128)(2,1)S(1)} %get-tuple-element.71.place_ref) | copy-start | bytes 393220
  69.2 21.7 %collective-permute-start.5 = (bf16[768,256]{1,0:T(8,128)(2,1)S(1)}, bf16[768,256]{1,0:T(8,128)(2,1)S(1)}, u32[]{:S(2)}, u32[]{:S(2)}) collective-permute-start(bf16[768,256]{1,0:T(8,128)(2,1)S(1)} %get-tuple-element.64), channel_id=1, source_target_pairs={{0,2},{1,5},{2,0},{3,7},{4,6},{5,1},{6,4},{7,3},{8,10},{9,13},{10,... | collective-permute-start | bytes 1179656 | tf_op jit(solution)/shard_map/ppermute | solution.py:420
  78.9 12.3 %collective-permute-start.20 = (bf16[2,768,256]{2,1,0:T(8,128)(2,1)}, bf16[2,768,256]{2,1,0:T(8,128)(2,1)}, u32[]{:S(2)}, u32[]{:S(2)}) collective-permute-start(bf16[2,768,256]{2,1,0:T(8,128)(2,1)} %collective-permute-done.19.refs_0_), channel_id=1, source_target_pairs={{0,1},{1,0},{2,3},{3,2},{4,5},{5,4},{6,7},{7,6},{8,9},{9,8},{10,11... | collective-permute-start | bytes 2359304 | tf_op jit(solution)/shard_map/ppermute | solution.py:420
  88.3 1.0 copy-start.6
  89.4 1.0 copy-start.8
  90.4 2.8 %collective-permute-start.22 = (bf16[2,768,256]{2,1,0:T(8,128)(2,1)}, bf16[2,768,256]{2,1,0:T(8,128)(2,1)}, u32[]{:S(2)}, u32[]{:S(2)}) collective-permute-start(bf16[2,768,256]{2,1,0:T(8,128)(2,1)} %collective-permute-done.21.refs_2_), channel_id=1, source_target_pairs={{0,1},{1,0},{2,3},{3,2},{4,5},{5,4},{6,7},{7,6},{8,9},{9,8},{10,11... | collective-permute-start | bytes 2359304 | tf_op jit(solution)/shard_map/ppermute | solution.py:420
  91.0 14.5 %collective-permute-start.14 = (bf16[2,768,256]{2,1,0:T(8,128)(2,1)S(1)}, bf16[2,768,256]{2,1,0:T(8,128)(2,1)S(1)}, u32[]{:S(2)}, u32[]{:S(2)}) collective-permute-start(bf16[2,768,256]{2,1,0:T(8,128)(2,1)S(1)} %pad_maximum_fusion.refs_0_), channel_id=1, source_target_pairs={{0,4},{1,3},{2,6},{3,1},{4,0},{5,7},{6,2},{7,5},{8,12},{9,11},{10,... | collective-permute-start | bytes 2359304 | tf_op jit(solution)/shard_map/ppermute | solution.py:420
  93.2 1.3 copy-start.7
  94.4 1.3 copy-start.9
  105.5 0.9 copy-start.12
  106.4 9.5 %copy-start.11 = (bf16[2,768,256]{2,1,0:T(8,128)(2,1)S(1)}, bf16[2,768,256]{2,1,0:T(8,128)(2,1)}, u32[]{:S(2)}) copy-start(bf16[2,768,256]{2,1,0:T(8,128)(2,1)} %copy-done.10) | copy-start | bytes 2359300
  114.9 8.9 %collective-permute-start.24 = (bf16[4,256,768]{2,1,0:T(8,128)(2,1)}, bf16[4,256,768]{2,1,0:T(8,128)(2,1)}, u32[]{:S(2)}, u32[]{:S(2)}) collective-permute-start(bf16[4,256,768]{2,1,0:T(8,128)(2,1)} %get-tuple-element.99), channel_id=1, source_target_pairs={{0,1},{1,0},{2,3},{3,2},{4,5},{5,4},{6,7},{7,6},{8,9},{9,8},{10,11... | collective-permute-start | bytes 4718600 | tf_op jit(solution)/shard_map/ppermute | solution.py:420
  115.3 11.0 %collective-permute-start.23 = (bf16[4,256,768]{2,1,0:T(8,128)(2,1)}, bf16[4,256,768]{2,1,0:T(8,128)(2,1)}, u32[]{:S(2)}, u32[]{:S(2)}) collective-permute-start(bf16[4,256,768]{2,1,0:T(8,128)(2,1)} %get-tuple-element.97), channel_id=1, source_target_pairs={{0,1},{1,0},{2,3},{3,2},{4,5},{5,4},{6,7},{7,6},{8,9},{9,8},{10,11... | collective-permute-start | bytes 4718600 | tf_op jit(solution)/shard_map/ppermute | solution.py:420
  115.6 12.2 %collective-permute-start.18 = (bf16[2,768,256]{2,1,0:T(8,128)(2,1)S(1)}, bf16[2,768,256]{2,1,0:T(8,128)(2,1)S(1)}, u32[]{:S(2)}, u32[]{:S(2)}) collective-permute-start(bf16[2,768,256]{2,1,0:T(8,128)(2,1)S(1)} %pad_maximum_fusion.2.refs_2_), channel_id=1, source_target_pairs={{0,1},{1,0},{2,3},{3,2},{4,5},{5,4},{6,7},{7,6},{8,9},{9,8},{10,11... | collective-permute-start | bytes 2359304 | tf_op jit(solution)/shard_map/ppermute | solution.py:420
  116.0 24.6 %collective-permute-start.16 = (bf16[2,768,256]{2,1,0:T(8,128)(2,1)S(1)}, bf16[2,768,256]{2,1,0:T(8,128)(2,1)S(1)}, u32[]{:S(2)}, u32[]{:S(2)}) collective-permute-start(bf16[2,768,256]{2,1,0:T(8,128)(2,1)S(1)} %copy-done.11), channel_id=1, source_target_pairs={{0,1},{1,0},{2,3},{3,2},{4,5},{5,4},{6,7},{7,6},{8,9},{9,8},{10,11... | collective-permute-start | bytes 2359304 | tf_op jit(solution)/shard_map/ppermute | solution.py:420
  116.1 13.7 %collective-permute-start.17 = (bf16[2,768,256]{2,1,0:T(8,128)(2,1)S(1)}, bf16[2,768,256]{2,1,0:T(8,128)(2,1)S(1)}, u32[]{:S(2)}, u32[]{:S(2)}) collective-permute-start(bf16[2,768,256]{2,1,0:T(8,128)(2,1)S(1)} %pad_maximum_fusion.refs_0_), channel_id=1, source_target_pairs={{0,1},{1,0},{2,3},{3,2},{4,5},{5,4},{6,7},{7,6},{8,9},{9,8},{10,11... | collective-permute-start | bytes 2359304 | tf_op jit(solution)/shard_map/ppermute | solution.py:420
  123.7 1.1 copy-start.13
  124.8 15.8 %collective-permute-start.15 = (bf16[2,768,256]{2,1,0:T(8,128)(2,1)S(1)}, bf16[2,768,256]{2,1,0:T(8,128)(2,1)S(1)}, u32[]{:S(2)}, u32[]{:S(2)}) collective-permute-start(bf16[2,768,256]{2,1,0:T(8,128)(2,1)S(1)} %copy-done.13), channel_id=1, source_target_pairs={{0,1},{1,0},{2,3},{3,2},{4,5},{5,4},{6,7},{7,6},{8,9},{9,8},{10,11... | collective-permute-start | bytes 2359304 | tf_op jit(solution)/shard_map/ppermute | solution.py:420
  126.3 23.4 %collective-permute-start.26 = (bf16[2,256,768]{2,1,0:T(8,128)(2,1)S(1)}, bf16[2,256,768]{2,1,0:T(8,128)(2,1)S(1)}, u32[]{:S(2)}, u32[]{:S(2)}) collective-permute-start(bf16[2,256,768]{2,1,0:T(8,128)(2,1)S(1)} %add_convert_fusion.2), channel_id=1, source_target_pairs={{0,4},{1,3},{2,6},{3,1},{4,0},{5,7},{6,2},{7,5},{8,12},{9,11},{10,... | collective-permute-start | bytes 2359304 | tf_op jit(solution)/shard_map/ppermute | solution.py:420
  127.8 23.2 %collective-permute-start.25 = (bf16[2,256,768]{2,1,0:T(8,128)(2,1)S(1)}, bf16[2,256,768]{2,1,0:T(8,128)(2,1)S(1)}, u32[]{:S(2)}, u32[]{:S(2)}) collective-permute-start(bf16[2,256,768]{2,1,0:T(8,128)(2,1)S(1)} %add_convert_fusion.3), channel_id=1, source_target_pairs={{0,4},{1,3},{2,6},{3,1},{4,0},{5,7},{6,2},{7,5},{8,12},{9,11},{10,... | collective-permute-start | bytes 2359304 | tf_op jit(solution)/shard_map/ppermute | solution.py:420
  150.9 16.2 %collective-permute-start.28 = (bf16[256,768]{1,0:T(8,128)(2,1)S(1)}, bf16[256,768]{1,0:T(8,128)(2,1)S(1)}, u32[]{:S(2)}, u32[]{:S(2)}) collective-permute-start(bf16[256,768]{1,0:T(8,128)(2,1)S(1)} %fusion.1), channel_id=1, source_target_pairs={{0,2},{1,5},{2,0},{3,7},{4,6},{5,1},{6,4},{7,3},{8,10},{9,13},{10,... | collective-permute-start | bytes 1179656 | tf_op jit(solution)/shard_map/ppermute | solution.py:420
  152.2 15.4 %collective-permute-start.27 = (bf16[256,768]{1,0:T(8,128)(2,1)S(1)}, bf16[256,768]{1,0:T(8,128)(2,1)S(1)}, u32[]{:S(2)}, u32[]{:S(2)}) collective-permute-start(bf16[256,768]{1,0:T(8,128)(2,1)S(1)} %fusion), channel_id=1, source_target_pairs={{0,2},{1,5},{2,0},{3,7},{4,6},{5,1},{6,4},{7,3},{8,10},{9,13},{10,... | collective-permute-start | bytes 1179656 | tf_op jit(solution)/shard_map/ppermute | solution.py:420
  154.3 12.8 %copy-start.23 = (bf16[256,256]{1,0:T(8,128)(2,1)S(1)}, bf16[256,256]{1,0:T(8,128)(2,1)}, u32[]{:S(2)}) copy-start(bf16[256,256]{1,0:T(8,128)(2,1)} %copy-done.22) | copy-start | bytes 393220
  168.5 3.5 %collective-permute-start.30 = (bf16[4,256,768]{2,1,0:T(8,128)(2,1)S(1)}, bf16[4,256,768]{2,1,0:T(8,128)(2,1)S(1)}, u32[]{:S(2)}, u32[]{:S(2)}) collective-permute-start(bf16[4,256,768]{2,1,0:T(8,128)(2,1)S(1)} %get-tuple-element.115), channel_id=1, source_target_pairs={{0,1},{1,0},{2,3},{3,2},{4,5},{5,4},{6,7},{7,6},{8,9},{9,8},{10,11... | collective-permute-start | bytes 4718600 | tf_op jit(solution)/shard_map/ppermute | solution.py:420
  168.5 5.6 %collective-permute-start.29 = (bf16[4,256,768]{2,1,0:T(8,128)(2,1)S(1)}, bf16[4,256,768]{2,1,0:T(8,128)(2,1)S(1)}, u32[]{:S(2)}, u32[]{:S(2)}) collective-permute-start(bf16[4,256,768]{2,1,0:T(8,128)(2,1)S(1)} %get-tuple-element.113), channel_id=1, source_target_pairs={{0,1},{1,0},{2,3},{3,2},{4,5},{5,4},{6,7},{7,6},{8,9},{9,8},{10,11... | collective-permute-start | bytes 4718600 | tf_op jit(solution)/shard_map/ppermute | solution.py:420
  172.1 12.1 %collective-permute-start.31 = (bf16[2,256,768]{2,1,0:T(8,128)(2,1)S(1)}, bf16[2,256,768]{2,1,0:T(8,128)(2,1)S(1)}, u32[]{:S(2)}, u32[]{:S(2)}) collective-permute-start(bf16[2,256,768]{2,1,0:T(8,128)(2,1)S(1)} %add_convert_fusion), channel_id=1, source_target_pairs={{0,4},{1,3},{2,6},{3,1},{4,0},{5,7},{6,2},{7,5},{8,12},{9,11},{10,... | collective-permute-start | bytes 2359304 | tf_op jit(solution)/shard_map/ppermute | solution.py:420
  184.2 14.4 %collective-permute-start.32 = (bf16[2,256,768]{2,1,0:T(8,128)(2,1)S(1)}, bf16[2,256,768]{2,1,0:T(8,128)(2,1)S(1)}, u32[]{:S(2)}, u32[]{:S(2)}) collective-permute-start(bf16[2,256,768]{2,1,0:T(8,128)(2,1)S(1)} %add_convert_fusion.1), channel_id=1, source_target_pairs={{0,4},{1,3},{2,6},{3,1},{4,0},{5,7},{6,2},{7,5},{8,12},{9,11},{10,... | collective-permute-start | bytes 2359304 | tf_op jit(solution)/shard_map/ppermute | solution.py:420
  184.3 28.9 %collective-permute-start.35 = (bf16[256,768]{1,0:T(8,128)(2,1)S(1)}, bf16[256,768]{1,0:T(8,128)(2,1)S(1)}, u32[]{:S(2)}, u32[]{:S(2)}) collective-permute-start(bf16[256,768]{1,0:T(8,128)(2,1)S(1)} %shard_map.124), channel_id=1, source_target_pairs={{8,16},{16,8},{9,17},{17,9},{10,18},{18,10},{11,19},{19,11},{12,20... | collective-permute-start | bytes 1179656 | tf_op jit(solution)/shard_map/ppermute | solution.py:582
  185.0 28.2 %collective-permute-start.36 = (bf16[256,768]{1,0:T(8,128)(2,1)S(1)}, bf16[256,768]{1,0:T(8,128)(2,1)S(1)}, u32[]{:S(2)}, u32[]{:S(2)}) collective-permute-start(bf16[256,768]{1,0:T(8,128)(2,1)S(1)} %shard_map.124), channel_id=1, source_target_pairs={{0,16},{24,8},{1,17},{25,9},{2,18},{26,10},{3,19},{27,11},{4,20},{... | collective-permute-start | bytes 1179656 | tf_op jit(solution)/shard_map/ppermute | solution.py:583
  191.4 21.8 %collective-permute-start.34 = (bf16[256,768]{1,0:T(8,128)(2,1)S(1)}, bf16[256,768]{1,0:T(8,128)(2,1)S(1)}, u32[]{:S(2)}, u32[]{:S(2)}) collective-permute-start(bf16[256,768]{1,0:T(8,128)(2,1)S(1)} %shard_map.123), channel_id=1, source_target_pairs={{0,8},{8,0},{16,24},{24,16},{1,9},{9,1},{17,25},{25,17},{2,10},{10... | collective-permute-start | bytes 1179656 | tf_op jit(solution)/shard_map/ppermute | solution.py:420
  191.6 7.9 %copy-start.25 = (bf16[256,256]{1,0:T(8,128)(2,1)S(1)}, bf16[256,256]{1,0:T(8,128)(2,1)}, u32[]{:S(2)}) copy-start(bf16[256,256]{1,0:T(8,128)(2,1)} %copy-done.24) | copy-start | bytes 393220
  191.6 7.8 %collective-permute-start.37 = (bf16[256,768]{1,0:T(8,128)(2,1)S(1)}, bf16[256,768]{1,0:T(8,128)(2,1)S(1)}, u32[]{:S(2)}, u32[]{:S(2)}) collective-permute-start(bf16[256,768]{1,0:T(8,128)(2,1)S(1)} %fusion.3), channel_id=1, source_target_pairs={{0,2},{1,5},{2,0},{3,7},{4,6},{5,1},{6,4},{7,3},{8,10},{9,13},{10,... | collective-permute-start | bytes 1179656 | tf_op jit(solution)/shard_map/ppermute | solution.py:420
  198.7 7.8 %collective-permute-start.33 = (bf16[256,768]{1,0:T(8,128)(2,1)S(1)}, bf16[256,768]{1,0:T(8,128)(2,1)S(1)}, u32[]{:S(2)}, u32[]{:S(2)}) collective-permute-start(bf16[256,768]{1,0:T(8,128)(2,1)S(1)} %fusion.2), channel_id=1, source_target_pairs={{0,2},{1,5},{2,0},{3,7},{4,6},{5,1},{6,4},{7,3},{8,10},{9,13},{10,... | collective-permute-start | bytes 1179656 | tf_op jit(solution)/shard_map/ppermute | solution.py:420
  198.9 13.8 %copy-start.19 = (bf16[256,256]{1,0:T(8,128)(2,1)S(1)}, bf16[256,256]{1,0:T(8,128)(2,1)}, u32[]{:S(2)}) copy-start(bf16[256,256]{1,0:T(8,128)(2,1)} %copy-done.18) | copy-start | bytes 393220
  199.9 23.8 %collective-permute-start.38 = (bf16[256,768]{1,0:T(8,128)(2,1)S(1)}, bf16[256,768]{1,0:T(8,128)(2,1)S(1)}, u32[]{:S(2)}, u32[]{:S(2)}) collective-permute-start(bf16[256,768]{1,0:T(8,128)(2,1)S(1)} %shard_map.126), channel_id=1, source_target_pairs={{8,24},{16,0},{9,25},{17,1},{10,26},{18,2},{11,27},{19,3},{12,28},... | collective-permute-start | bytes 1179656 | tf_op jit(solution)/shard_map/ppermute | solution.py:584
  206.6 17.1 %collective-permute-start.39 = (bf16[256,768]{1,0:T(8,128)(2,1)S(1)}, bf16[256,768]{1,0:T(8,128)(2,1)S(1)}, u32[]{:S(2)}, u32[]{:S(2)}) collective-permute-start(bf16[256,768]{1,0:T(8,128)(2,1)S(1)} %shard_map.126), channel_id=1, source_target_pairs={{0,24},{24,0},{1,25},{25,1},{2,26},{26,2},{3,27},{27,3},{4,28},{28... | collective-permute-start | bytes 1179656 | tf_op jit(solution)/shard_map/ppermute | solution.py:585
  (5 other events, 3.7 us)

commit v8 on v7

--- a/solution.py
+++ b/solution.py
@@ -10,8 +10,12 @@
 F32 = jnp.float32
 BF16 = jnp.bfloat16
 HIGHEST = lax.Precision.HIGHEST
-VMEM_LIMIT = 40 * 1024 * 1024
+VMEM_LIMIT = 22 * 1024 * 1024
 ID_ROWS = 16
+
+
+def in_hbm(array):
+    return pltpu.with_memory_space_constraint(array, pltpu.HBM)
 
 
 def lower_ones(length):
@@ -68,7 +72,7 @@
             flops=2 * length * width * (width // heads), bytes_accessed=4 * length * width, transcendentals=0
         ),
         compiler_params=pltpu.CompilerParams(vmem_limit_bytes=VMEM_LIMIT),
-    )(attn_key, attn_value, log_decay)
+    )(in_hbm(attn_key), in_hbm(attn_value), in_hbm(log_decay))
 
 
 def intra_kernel(query_ref, key_ref, value_ref, decay_ref, cumulative_ref, out_ref):
@@ -358,7 +362,14 @@
             transcendentals=0,
         ),
         compiler_params=pltpu.CompilerParams(vmem_limit_bytes=VMEM_LIMIT),
-    )(plan, *[x for section in xs for x in section], router_rows, gate_rows, up_rows, *(sums or ()))
+    )(
+        plan,
+        *[x for section in xs for x in section],
+        router_rows,
+        in_hbm(gate_rows),
+        in_hbm(up_rows),
+        *(sums or ()),
+    )
 
 
 def down_kernel(blocks, sections, plan_ref, hidden_ref, down_ref, *out_refs):
@@ -406,7 +417,7 @@
             transcendentals=0,
         ),
         compiler_params=pltpu.CompilerParams(vmem_limit_bytes=VMEM_LIMIT),
-    )(jnp.concatenate(plans), hidden, down_weight)
+    )(jnp.concatenate(plans), hidden, in_hbm(down_weight))
     return [out[i * sections : (i + 1) * sections] for i in range(len(plans))]
 
 
@@ -548,7 +559,8 @@
         sums = gate_part(plane.early, early, *weights)
         if after:
             gather(after, sums)
-            far_two[chunk[1]], sums = tie((far_two[chunk[1]], sums))
+            for name in chunk:
+                far_two[name], _ = tie((far_two[name], sums))
         late = [[far_two[name], plane.across(far_two[name])] for name in chunk]
         if after:
             late, _ = tie((late, two[after]))
@@ -570,6 +582,13 @@
             if got_two and not after:
                 two_share, _ = tie((two_share, got_two))
             got_two.append(plane.second(two_share))
+            if not after and k == 0:
+                home = [
+                    swapped(pieces["neighbour"], "seq", 1, 1),
+                    lax.ppermute(pieces["third"], "seq", [(1, 2), (2, 1)]),
+                    lax.ppermute(pieces["third"], "seq", [(0, 2), (3, 1)]),
+                ]
+                got_two[0], _ = tie((got_two[0], home))
             one_share = added(added(mine[k][1], near_share[1]), got_two[k][1])
             one.append(one_share)
             got_one = plane.once(one_share)
@@ -578,9 +597,7 @@
             )
     return [
         pieces["own"],
-        swapped(pieces["neighbour"], "seq", 1, 1),
-        lax.ppermute(pieces["third"], "seq", [(1, 2), (2, 1)]),
-        lax.ppermute(pieces["third"], "seq", [(0, 2), (3, 1)]),
+        *home,
         lax.ppermute(pieces["fourth"], "seq", [(1, 3), (2, 0)]),
         lax.ppermute(pieces["fourth"], "seq", [(0, 3), (3, 0)]),
     ]

time: 226 us -> 230 us (1.018)
  waiting for transfers between devices: 73.6 us -> 83.1 us
  starting transfers between devices: 49.1 us -> 45.8 us
  local copies, waits for them, and re-layouts: 19.1 us -> 16.4 us
    ppermute x1, waiting for transfers between devices: 0.01 us -> 9.14 us  [paired_chunks(): lax.ppermute(pieces['third'], 'seq', [(0, 2), (3, 1)])]
    ppermute x30, waiting for transfers between devices: 52.4 us -> 57.3 us  [swapped(): return lax.ppermute(array, axis, pairs)]
    ppermute x1, waiting for transfers between devices: 10.5 us -> 5.68 us  [paired_chunks(): lax.ppermute(pieces['fourth'], 'seq', [(1, 3), (2, 0)])]
    unnamed x58 -> x52, local copies, waits for them, and re-layouts: 15.9 us -> 13.2 us
where the time goes in v8:
time: 230 us; the launch traced here: 229 us
  waiting for transfers between devices  83.1 us (36%)
  Pallas kernels  75.5 us (33%)
  starting transfers between devices  45.8 us (20%)
  local copies, waits for them, and re-layouts  16.4 us (7%)
  other arithmetic  7.61 us (3%)
    ppermute x30, waiting for transfers between devices, swapped(): return lax.ppermute(array, axis, pairs)  57.3 us
    pallas_call x4, Pallas kernels, gate_part(): pl.pallas_call(functools.partial(gate_kernel, counts, len(xs), last), gri...  36.8 us
    pallas_call x3, Pallas kernels, down_part(): pl.pallas_call(functools.partial(down_kernel, blocks, sections), grid_spe...  28.5 us
    ppermute x30, starting transfers between devices, swapped(): return lax.ppermute(array, axis, pairs)  21.5 us
    unnamed x52, local copies, waits for them, and re-layouts  13.2 us
    ppermute x2, starting transfers between devices, shifted(): return lax.ppermute(array, axis, pairs)  9.43 us
    ppermute x1, waiting for transfers between devices, paired_chunks(): lax.ppermute(pieces['third'], 'seq', [(0, 2), (3, 1)])  9.14 us
    ppermute x2, waiting for transfers between devices, outward(): return lax.ppermute(part, 'seq', [(1, 0), (2, 3)])  6.99 us
  transfers between devices with their start and end apart: 40, of which 15 were waited for; matrix products, arithmetic and copies ran while one was open for 4% of the time, Pallas kernels for 28%

profile of v8, /device:TPU:0, one launch (start us, length us, event | category | flops | bytes accessed | tf_op | source)
XLA Modules:
  0.0 229.2 jit_solution(11904045757050131973)
XLA Ops:
  0.0 2.1 shard_map.109
  2.2 4.9 %collective-permute-start = (bf16[784,128]{1,0:T(8,128)(2,1)S(1)}, bf16[784,128]{1,0:T(8,128)(2,1)S(1)}, u32[]{:S(2)}, u32[]{:S(2)}) collective-permute-start(bf16[784,128]{1,0:T(8,128)(2,1)S(1)} %get-tuple-element.61), channel_id=1, source_target_pairs={{0,8},{8,16},{16,24},{1,9},{9,17},{17,25},{2,10},{10,18},{18,26},{... | collective-permute-start | bytes 602120 | tf_op jit(solution)/shard_map/ppermute | solution.py:30
  7.1 0.7 reshape.57.gain_ref
  7.8 1.0 copy-done
  8.8 1.0 copy-done.2
  9.8 1.0 copy-done.3
  10.8 0.7 copy-done.24
  11.5 1.4 shard_map.110.intra_ref
  13.2 4.5 %collective-permute-start.1 = (bf16[784,128]{1,0:T(8,128)(2,1)S(1)}, bf16[784,128]{1,0:T(8,128)(2,1)S(1)}, u32[]{:S(2)}, u32[]{:S(2)}) collective-permute-start(bf16[784,128]{1,0:T(8,128)(2,1)S(1)} %concatenate.7), channel_id=1, source_target_pairs={{0,16},{8,24},{1,17},{9,25},{2,18},{10,26},{3,19},{11,27},{4,20},{... | collective-permute-start | bytes 602120 | tf_op jit(solution)/shard_map/ppermute | solution.py:30
  17.7 3.9 %collective-permute-done.1 = bf16[784,128]{1,0:T(8,128)(2,1)S(1)} collective-permute-done((bf16[784,128]{1,0:T(8,128)(2,1)S(1)}, bf16[784,128]{1,0:T(8,128)(2,1)S(1)}, u32[]{:S(2)}, u32[]{:S(2)}) %collective-permute-start.1) | collective-permute-done | bytes 200736 | tf_op jit(solution)/shard_map/ppermute | solution.py:30
  21.8 0.9 shard_map.111.refs_0_
  23.4 1.0 shard_map.112
  25.1 1.5 collective-permute-start.9
  26.6 5.8 %collective-permute-start.2 = (bf16[272,768]{1,0:T(8,128)(2,1)S(1)}, bf16[272,768]{1,0:T(8,128)(2,1)S(1)}, u32[]{:S(2)}, u32[]{:S(2)}) collective-permute-start(bf16[272,768]{1,0:T(8,128)(2,1)S(1)} %shard_map.111.refs_0_), channel_id=1, source_target_pairs={{0,8},{8,0},{16,24},{24,16},{1,9},{9,1},{17,25},{25,17},{2,10},{10... | collective-permute-start | bytes 1253384 | tf_op jit(solution)/shard_map/ppermute | solution.py:431
  32.4 1.3 collective-permute-start.8
  33.8 8.2 %collective-permute-done.2.refs_0_ = bf16[272,768]{1,0:T(8,128)(2,1)S(1)} collective-permute-done((bf16[272,768]{1,0:T(8,128)(2,1)S(1)}, bf16[272,768]{1,0:T(8,128)(2,1)S(1)}, u32[]{:S(2)}, u32[]{:S(2)}) %collective-permute-start.2) | collective-permute-done | bytes 417824 | tf_op jit(solution)/shard_map/ppermute | solution.py:431
  42.7 1.0 shard_map.114
  43.7 1.5 collective-permute-start.6
  45.2 4.4 %collective-permute-done.8.refs_1_ = bf16[272,768]{1,0:T(8,128)(2,1)S(1)} collective-permute-done((bf16[272,768]{1,0:T(8,128)(2,1)S(1)}, bf16[272,768]{1,0:T(8,128)(2,1)S(1)}, u32[]{:S(2)}, u32[]{:S(2)}) %collective-permute-start.8) | collective-permute-done | bytes 417824 | tf_op jit(solution)/shard_map/ppermute | solution.py:532
  49.7 1.0 shard_map.115
  50.7 1.6 collective-permute-start.12
  52.3 1.5 collective-permute-start.4
  53.7 0.8 collective-permute-done.6
  54.6 7.4 %collective-permute-done.10.refs_2_ = bf16[2,768,256]{2,1,0:T(8,128)(2,1)S(1)} collective-permute-done((bf16[2,768,256]{2,1,0:T(8,128)(2,1)S(1)}, bf16[2,768,256]{2,1,0:T(8,128)(2,1)S(1)}, u32[]{:S(2)}, u32[]{:S(2)}) %collective-permute-start.10) | collective-permute-done | bytes 786464 | tf_op jit(solution)/shard_map/ppermute | solution.py:431
  62.1 2.6 %collective-permute-done.4.refs_1_ = bf16[272,768]{1,0:T(8,128)(2,1)S(1)} collective-permute-done((bf16[272,768]{1,0:T(8,128)(2,1)S(1)}, bf16[272,768]{1,0:T(8,128)(2,1)S(1)}, u32[]{:S(2)}, u32[]{:S(2)}) %collective-permute-start.4) | collective-permute-done | bytes 417824 | tf_op jit(solution)/shard_map/ppermute | solution.py:532
  64.7 0.8 copy-done.12
  65.5 2.0 collective-permute-start.19
  67.6 1.0 copy-done.13
  68.6 1.0 shard_map.113
  69.7 9.2 %shard_map.116 = (f32[2,576,256]{2,1,0:T(8,128)S(1)}, f32[2,576,256]{2,1,0:T(8,128)S(1)}, f32[2,2,256]{2,1,0:T(2,128)S(1)}) custom-call(s32[4]{0:T(128)S(1)} %get-tuple-element.118.plan_ref, bf16[2,768,256]{2,1,0:T(8,128)(2,1)S(1)} %pad_maximum_fusion.1.refs_0_, bf16[2,768,256]{2,1,0:T(8,128)(2,1)} %collective-permute-done.11.refs_1_, ...), custom_call_target="tpu_custom_call" | custom-call | flops 3623878656 | bytes 14155776 | tf_op jit(solution)/shard_map/pallas_call | solution.py:343
  79.0 1.0 copy-done.4
  80.0 1.0 copy-done.6
  81.0 0.7 collective-permute-done.21.refs_2_
  81.8 8.4 %collective-permute-done.19.refs_0_ = bf16[2,768,256]{2,1,0:T(8,128)(2,1)} collective-permute-done((bf16[2,768,256]{2,1,0:T(8,128)(2,1)S(1)}, bf16[2,768,256]{2,1,0:T(8,128)(2,1)}, u32[]{:S(2)}, u32[]{:S(2)}) %collective-permute-start.19) | collective-permute-done | bytes 786464 | tf_op jit(solution)/shard_map/ppermute | solution.py:431
  90.5 2.4 %collective-permute-done.20.refs_1_ = bf16[2,768,256]{2,1,0:T(8,128)(2,1)} collective-permute-done((bf16[2,768,256]{2,1,0:T(8,128)(2,1)}, bf16[2,768,256]{2,1,0:T(8,128)(2,1)}, u32[]{:S(2)}, u32[]{:S(2)}) %collective-permute-start.20) | collective-permute-done | bytes 786464 | tf_op jit(solution)/shard_map/ppermute | solution.py:431
  92.8 1.3 copy-done.5
  94.1 1.3 copy-done.7
  95.4 9.8 %shard_map.117.hidden_ref = bf16[2,256,576]{2,1,0:T(8,128)(2,1)S(1)} custom-call(s32[4]{0:T(128)S(1)} %add_add_fusion.plan_ref, bf16[2,768,256]{2,1,0:T(8,128)(2,1)} %collective-permute-done.19.refs_0_, bf16[2,768,256]{2,1,0:T(8,128)(2,1)} %collective-permute-done.20.refs_1_, bf16[2,768,256]{2,1,0:T(8,128)(2,1)} %collective-permute-done.21.refs_2_, ...), custom_call_target="tpu_custom_call" | custom-call | flops 3623878656 | bytes 14155776 | tf_op jit(solution)/shard_map/pallas_call | solution.py:343
  105.2 0.9 copy-done.10
  106.1 8.5 %shard_map.118 = (bf16[4,256,768]{2,1,0:T(8,128)(2,1)}, bf16[4,256,768]{2,1,0:T(8,128)(2,1)}) custom-call(s32[4]{0:T(128)S(1)} %get-tuple-element.119.plan_ref, bf16[2,256,576]{2,1,0:T(8,128)(2,1)S(1)} %shard_map.117.hidden_ref, bf16[2,576,6144]{2,1,0:T(8,128)(2,1)} %down_ref.5), custom_call_target="tpu_custom_call" | custom-call | flops 1811939328 | bytes 7077888 | tf_op jit(solution)/shard_map/pallas_call | solution.py:402
  115.9 7.2 %shard_map.119 = (bf16[4,256,768]{2,1,0:T(8,128)(2,1)S(1)}, bf16[4,256,768]{2,1,0:T(8,128)(2,1)S(1)}) custom-call(s32[4]{0:T(128)S(1)} %pad_add_fusion.3.plan_ref, bf16[2,256,576]{2,1,0:T(8,128)(2,1)S(1)} %shard_map.117.hidden_ref, bf16[2,576,6144]{2,1,0:T(8,128)(2,1)} %down_ref.5), custom_call_target="tpu_custom_call" | custom-call | flops 1811939328 | bytes 7077888 | tf_op jit(solution)/shard_map/pallas_call | solution.py:402
  123.2 1.0 copy-done.11
  124.7 1.3 add_convert_fusion.2
  126.1 1.3 add_convert_fusion.3
  127.4 2.1 collective-permute-start.25
  129.5 8.7 %shard_map.120 = (f32[2,576,256]{2,1,0:T(8,128)S(1)}, f32[2,576,256]{2,1,0:T(8,128)S(1)}, f32[2,2,256]{2,1,0:T(2,128)S(1)}) custom-call(s32[4]{0:T(128)S(1)} %get-tuple-element.118.plan_ref, bf16[2,768,256]{2,1,0:T(8,128)(2,1)S(1)} %pad_maximum_fusion.refs_0_, bf16[2,768,256]{2,1,0:T(8,128)(2,1)S(1)} %collective-permute-done.17.refs_1_, ...), custom_call_target="tpu_custom_call" | custom-call | flops 3623878656 | bytes 14155776 | tf_op jit(solution)/shard_map/pallas_call | solution.py:343
  138.2 1.0 slice_bitcast_fusion.4.refs_1_
  139.3 1.0 slice_bitcast_fusion.6.refs_1_
  140.3 9.1 %shard_map.121.hidden_ref = bf16[2,256,576]{2,1,0:T(8,128)(2,1)S(1)} custom-call(s32[4]{0:T(128)S(1)} %add_add_fusion.plan_ref, bf16[2,768,256]{2,1,0:T(8,128)(2,1)S(1)} %copy-done.11, bf16[2,768,256]{2,1,0:T(8,128)(2,1)S(1)} %collective-permute-done.15.refs_1_, bf16[2,768,256]{2,1,0:T(8,128)(2,1)S(1)} %copy-done.9, ...), custom_call_target="tpu_custom_call" | custom-call | flops 3623878656 | bytes 14155776 | tf_op jit(solution)/shard_map/pallas_call | solution.py:343
  149.4 1.2 fusion.1
  150.7 1.1 fusion
  151.9 2.1 collective-permute-start.27
  154.0 12.8 %shard_map.122 = (bf16[4,256,768]{2,1,0:T(8,128)(2,1)S(1)}, bf16[4,256,768]{2,1,0:T(8,128)(2,1)S(1)}, bf16[4,256,768]{2,1,0:T(8,128)(2,1)S(1)}, bf16[4,256,768]{2,1,0:T(8,128)(2,1)S(1)}) custom-call(s32[8]{0:T(128)S(1)} %concatenate.8.plan_ref, bf16[2,256,576]{2,1,0:T(8,128)(2,1)S(1)} %shard_map.121.hidden_ref, bf16[2,576,6144]{2,1,0:T(8,128)(2,1)} %down_ref.5), custom_call_target="tpu_custom_call" | custom-call | flops 3623878656 | bytes 14155776 | tf_op jit(solution)/shard_map/pallas_call | solution.py:402
  168.7 2.9 %collective-permute-done.30 = bf16[4,256,768]{2,1,0:T(8,128)(2,1)S(1)} collective-permute-done((bf16[4,256,768]{2,1,0:T(8,128)(2,1)S(1)}, bf16[4,256,768]{2,1,0:T(8,128)(2,1)S(1)}, u32[]{:S(2)}, u32[]{:S(2)}) %collective-permute-start.30) | collective-permute-done | bytes 1572896 | tf_op jit(solution)/shard_map/ppermute | solution.py:431
  172.6 4.2 %collective-permute-start.34 = (bf16[256,768]{1,0:T(8,128)(2,1)S(1)}, bf16[256,768]{1,0:T(8,128)(2,1)S(1)}, u32[]{:S(2)}, u32[]{:S(2)}) collective-permute-start(bf16[256,768]{1,0:T(8,128)(2,1)S(1)} %shard_map.124), channel_id=1, source_target_pairs={{0,16},{24,8},{1,17},{25,9},{2,18},{26,10},{3,19},{27,11},{4,20},{... | collective-permute-start | bytes 1179656 | tf_op jit(solution)/shard_map/ppermute | solution.py:589
  177.1 9.1 %collective-permute-done.34 = bf16[256,768]{1,0:T(8,128)(2,1)S(1)} collective-permute-done((bf16[256,768]{1,0:T(8,128)(2,1)S(1)}, bf16[256,768]{1,0:T(8,128)(2,1)S(1)}, u32[]{:S(2)}, u32[]{:S(2)}) %collective-permute-start.34) | collective-permute-done | bytes 393248 | tf_op jit(solution)/shard_map/ppermute | solution.py:589
  186.2 7.4 %collective-permute-done.32 = bf16[256,768]{1,0:T(8,128)(2,1)S(1)} collective-permute-done((bf16[256,768]{1,0:T(8,128)(2,1)S(1)}, bf16[256,768]{1,0:T(8,128)(2,1)S(1)}, u32[]{:S(2)}, u32[]{:S(2)}) %collective-permute-start.32) | collective-permute-done | bytes 393248 | tf_op jit(solution)/shard_map/ppermute | solution.py:431
  193.6 1.7 collective-permute-start.35
  195.9 11.7 %collective-permute-done.37.refs_3_ = bf16[256,768]{1,0:T(8,128)(2,1)S(1)} collective-permute-done((bf16[256,768]{1,0:T(8,128)(2,1)S(1)}, bf16[256,768]{1,0:T(8,128)(2,1)S(1)}, u32[]{:S(2)}, u32[]{:S(2)}) %collective-permute-start.37) | collective-permute-done | bytes 393248 | tf_op jit(solution)/shard_map/ppermute | solution.py:431
  208.0 1.4 collective-permute-start.38
  209.5 4.5 %collective-permute-start.39 = (bf16[256,768]{1,0:T(8,128)(2,1)S(1)}, bf16[256,768]{1,0:T(8,128)(2,1)S(1)}, u32[]{:S(2)}, u32[]{:S(2)}) collective-permute-start(bf16[256,768]{1,0:T(8,128)(2,1)S(1)} %shard_map.126), channel_id=1, source_target_pairs={{0,24},{24,0},{1,25},{25,1},{2,26},{26,2},{3,27},{27,3},{4,28},{28... | collective-permute-start | bytes 1179656 | tf_op jit(solution)/shard_map/ppermute | solution.py:602
  214.6 7.4 %collective-permute-done.36.refs_3_ = bf16[256,768]{1,0:T(8,128)(2,1)S(1)} collective-permute-done((bf16[256,768]{1,0:T(8,128)(2,1)S(1)}, bf16[256,768]{1,0:T(8,128)(2,1)S(1)}, u32[]{:S(2)}, u32[]{:S(2)}) %collective-permute-start.36) | collective-permute-done | bytes 393248 | tf_op jit(solution)/shard_map/ppermute | solution.py:431
  222.4 5.7 %collective-permute-done.38 = bf16[256,768]{1,0:T(8,128)(2,1)S(1)} collective-permute-done((bf16[256,768]{1,0:T(8,128)(2,1)S(1)}, bf16[256,768]{1,0:T(8,128)(2,1)S(1)}, u32[]{:S(2)}, u32[]{:S(2)}) %collective-permute-start.38) | collective-permute-done | bytes 393248 | tf_op jit(solution)/shard_map/ppermute | solution.py:601
  228.1 1.1 add_convert_fusion.8
  (127 shorter events, 10.3 us)
Async XLA Ops:
  2.2 10.8 %collective-permute-start = (bf16[784,128]{1,0:T(8,128)(2,1)S(1)}, bf16[784,128]{1,0:T(8,128)(2,1)S(1)}, u32[]{:S(2)}, u32[]{:S(2)}) collective-permute-start(bf16[784,128]{1,0:T(8,128)(2,1)S(1)} %get-tuple-element.61), channel_id=1, source_target_pairs={{0,8},{8,16},{16,24},{1,9},{9,17},{17,25},{2,10},{10,18},{18,26},{... | collective-permute-start | bytes 602120 | tf_op jit(solution)/shard_map/ppermute | solution.py:30
  7.8 1.0 copy-start
  8.8 1.0 copy-start.2
  9.8 1.0 copy-start.3
  12.9 8.9 %copy-start.1 = (bf16[256,768]{1,0:T(8,128)(2,1)S(1)}, bf16[256,768]{1,0:T(8,128)(2,1)}, u32[]{:S(2)}) copy-start(bf16[256,768]{1,0:T(8,128)(2,1)} %query_ref.3) | copy-start | bytes 1179652
  12.9 8.9 %copy-start.15 = (bf16[256,768]{1,0:T(8,128)(2,1)S(1)}, bf16[256,768]{1,0:T(8,128)(2,1)}, u32[]{:S(2)}) copy-start(bf16[256,768]{1,0:T(8,128)(2,1)} %residual_ref.1) | copy-start | bytes 1179652
  12.9 8.9 %copy-start.25 = (s32[256,2]{0,1:T(2,128)S(1)}, s32[256,2]{0,1:T(2,128)}, u32[]{:S(2)}) copy-start(s32[256,2]{0,1:T(2,128)} %param.17) | copy-start | bytes 6148
  13.2 8.5 %collective-permute-start.1 = (bf16[784,128]{1,0:T(8,128)(2,1)S(1)}, bf16[784,128]{1,0:T(8,128)(2,1)S(1)}, u32[]{:S(2)}, u32[]{:S(2)}) collective-permute-start(bf16[784,128]{1,0:T(8,128)(2,1)S(1)} %concatenate.7), channel_id=1, source_target_pairs={{0,16},{8,24},{1,17},{9,25},{2,18},{10,26},{3,19},{11,27},{4,20},{... | collective-permute-start | bytes 602120 | tf_op jit(solution)/shard_map/ppermute | solution.py:30
  22.7 9.7 %collective-permute-start.7 = (bf16[272,768]{1,0:T(8,128)(2,1)S(1)}, bf16[272,768]{1,0:T(8,128)(2,1)S(1)}, u32[]{:S(2)}, u32[]{:S(2)}) collective-permute-start(bf16[272,768]{1,0:T(8,128)(2,1)S(1)} %shard_map.111.refs_0_), channel_id=1, source_target_pairs={{8,16},{16,8},{9,17},{17,9},{10,18},{18,10},{11,19},{19,11},{12,20... | collective-permute-start | bytes 1253384 | tf_op jit(solution)/shard_map/ppermute | solution.py:529
  25.1 8.5 %collective-permute-start.9 = (bf16[768,256]{1,0:T(8,128)(2,1)S(1)}, bf16[768,256]{1,0:T(8,128)(2,1)S(1)}, u32[]{:S(2)}, u32[]{:S(2)}) collective-permute-start(bf16[768,256]{1,0:T(8,128)(2,1)S(1)} %get-tuple-element.65), channel_id=1, source_target_pairs={{0,2},{1,5},{2,0},{3,7},{4,6},{5,1},{6,4},{7,3},{8,10},{9,13},{10,... | collective-permute-start | bytes 1179656 | tf_op jit(solution)/shard_map/ppermute | solution.py:431
  26.6 15.4 %collective-permute-start.2 = (bf16[272,768]{1,0:T(8,128)(2,1)S(1)}, bf16[272,768]{1,0:T(8,128)(2,1)S(1)}, u32[]{:S(2)}, u32[]{:S(2)}) collective-permute-start(bf16[272,768]{1,0:T(8,128)(2,1)S(1)} %shard_map.111.refs_0_), channel_id=1, source_target_pairs={{0,8},{8,0},{16,24},{24,16},{1,9},{9,1},{17,25},{25,17},{2,10},{10... | collective-permute-start | bytes 1253384 | tf_op jit(solution)/shard_map/ppermute | solution.py:431
  32.4 17.3 %collective-permute-start.8 = (bf16[272,768]{1,0:T(8,128)(2,1)S(1)}, bf16[272,768]{1,0:T(8,128)(2,1)S(1)}, u32[]{:S(2)}, u32[]{:S(2)}) collective-permute-start(bf16[272,768]{1,0:T(8,128)(2,1)S(1)} %collective-permute-done.7.refs_0_), channel_id=1, source_target_pairs={{8,0},{16,24},{9,1},{17,25},{10,2},{18,26},{11,3},{19,27},{12,4},{... | collective-permute-start | bytes 1253384 | tf_op jit(solution)/shard_map/ppermute | solution.py:532
  42.0 20.0 %collective-permute-start.10 = (bf16[2,768,256]{2,1,0:T(8,128)(2,1)S(1)}, bf16[2,768,256]{2,1,0:T(8,128)(2,1)S(1)}, u32[]{:S(2)}, u32[]{:S(2)}) collective-permute-start(bf16[2,768,256]{2,1,0:T(8,128)(2,1)S(1)} %pad_maximum_fusion.2.refs_2_), channel_id=1, source_target_pairs={{0,4},{1,3},{2,6},{3,1},{4,0},{5,7},{6,2},{7,5},{8,12},{9,11},{10,... | collective-permute-start | bytes 2359304 | tf_op jit(solution)/shard_map/ppermute | solution.py:431
  42.0 10.3 %collective-permute-start.3 = (bf16[272,768]{1,0:T(8,128)(2,1)S(1)}, bf16[272,768]{1,0:T(8,128)(2,1)S(1)}, u32[]{:S(2)}, u32[]{:S(2)}) collective-permute-start(bf16[272,768]{1,0:T(8,128)(2,1)S(1)} %collective-permute-done.2.refs_0_), channel_id=1, source_target_pairs={{8,16},{16,8},{9,17},{17,9},{10,18},{18,10},{11,19},{19,11},{12,20... | collective-permute-start | bytes 1253384 | tf_op jit(solution)/shard_map/ppermute | solution.py:529
  43.7 18.4 %copy-start.18 = (bf16[256,256]{1,0:T(8,128)(2,1)}, bf16[256,256]{1,0:T(8,128)(2,1)S(1)}, u32[]{:S(2)}) copy-start(bf16[256,256]{1,0:T(8,128)(2,1)S(1)} %get-tuple-element.108.place_ref) | copy-start | bytes 393220
  43.7 10.8 %collective-permute-start.6 = (bf16[768,256]{1,0:T(8,128)(2,1)S(1)}, bf16[768,256]{1,0:T(8,128)(2,1)S(1)}, u32[]{:S(2)}, u32[]{:S(2)}) collective-permute-start(bf16[768,256]{1,0:T(8,128)(2,1)S(1)} %get-tuple-element.64), channel_id=1, source_target_pairs={{0,2},{1,5},{2,0},{3,7},{4,6},{5,1},{6,4},{7,3},{8,10},{9,13},{10,... | collective-permute-start | bytes 1179656 | tf_op jit(solution)/shard_map/ppermute | solution.py:431
  50.7 11.4 %copy-start.20 = (bf16[256,256]{1,0:T(8,128)(2,1)}, bf16[256,256]{1,0:T(8,128)(2,1)S(1)}, u32[]{:S(2)}) copy-start(bf16[256,256]{1,0:T(8,128)(2,1)S(1)} %get-tuple-element.109.place_ref) | copy-start | bytes 393220
  50.7 11.3 %collective-permute-start.12 = (bf16[768,256]{1,0:T(8,128)(2,1)S(1)}, bf16[768,256]{1,0:T(8,128)(2,1)S(1)}, u32[]{:S(2)}, u32[]{:S(2)}) collective-permute-start(bf16[768,256]{1,0:T(8,128)(2,1)S(1)} %get-tuple-element.68), channel_id=1, source_target_pairs={{0,2},{1,5},{2,0},{3,7},{4,6},{5,1},{6,4},{7,3},{8,10},{9,13},{10,... | collective-permute-start | bytes 1179656 | tf_op jit(solution)/shard_map/ppermute | solution.py:431
  52.3 12.4 %collective-permute-start.4 = (bf16[272,768]{1,0:T(8,128)(2,1)S(1)}, bf16[272,768]{1,0:T(8,128)(2,1)S(1)}, u32[]{:S(2)}, u32[]{:S(2)}) collective-permute-start(bf16[272,768]{1,0:T(8,128)(2,1)S(1)} %collective-permute-done.3.refs_0_), channel_id=1, source_target_pairs={{8,0},{16,24},{9,1},{17,25},{10,2},{18,26},{11,3},{19,27},{12,4},{... | collective-permute-start | bytes 1253384 | tf_op jit(solution)/shard_map/ppermute | solution.py:532
  54.6 15.1 %copy-start.14 = (bf16[6144,2]{0,1:T(2,128)(2,1)S(1)}, bf16[6144,2]{0,1:T(2,128)(2,1)}, u32[]{:S(2)}) copy-start(bf16[6144,2]{0,1:T(2,128)(2,1)} %param.18) | copy-start | bytes 73732
  62.0 3.5 %copy-start.8 = (bf16[2,768,256]{2,1,0:T(8,128)(2,1)}, bf16[2,768,256]{2,1,0:T(8,128)(2,1)S(1)}, u32[]{:S(2)}) copy-start(bf16[2,768,256]{2,1,0:T(8,128)(2,1)S(1)} %collective-permute-done.10.refs_2_) | copy-start | bytes 2359300
  62.0 7.7 %collective-permute-start.11 = (bf16[2,768,256]{2,1,0:T(8,128)(2,1)S(1)}, bf16[2,768,256]{2,1,0:T(8,128)(2,1)}, u32[]{:S(2)}, u32[]{:S(2)}) collective-permute-start(bf16[2,768,256]{2,1,0:T(8,128)(2,1)S(1)} %pad_maximum_fusion.1.refs_0_), channel_id=1, source_target_pairs={{0,1},{1,0},{2,3},{3,2},{4,5},{5,4},{6,7},{7,6},{8,9},{9,8},{10,11... | collective-permute-start | bytes 2359304 | tf_op jit(solution)/shard_map/ppermute | solution.py:431
  64.7 0.8 copy-start.12
  65.5 4.3 %collective-permute-start.13 = (bf16[2,768,256]{2,1,0:T(8,128)(2,1)S(1)}, bf16[2,768,256]{2,1,0:T(8,128)(2,1)}, u32[]{:S(2)}, u32[]{:S(2)}) collective-permute-start(bf16[2,768,256]{2,1,0:T(8,128)(2,1)S(1)} %pad_maximum_fusion.3.refs_2_), channel_id=1, source_target_pairs={{0,1},{1,0},{2,3},{3,2},{4,5},{5,4},{6,7},{7,6},{8,9},{9,8},{10,11... | collective-permute-start | bytes 2359304 | tf_op jit(solution)/shard_map/ppermute | solution.py:431
  65.5 16.3 %collective-permute-start.21 = (bf16[2,768,256]{2,1,0:T(8,128)(2,1)S(1)}, bf16[2,768,256]{2,1,0:T(8,128)(2,1)}, u32[]{:S(2)}, u32[]{:S(2)}) collective-permute-start(bf16[2,768,256]{2,1,0:T(8,128)(2,1)S(1)} %pad_maximum_fusion.3.refs_2_), channel_id=1, source_target_pairs={{0,4},{1,3},{2,6},{3,1},{4,0},{5,7},{6,2},{7,5},{8,12},{9,11},{10,... | collective-permute-start | bytes 2359304 | tf_op jit(solution)/shard_map/ppermute | solution.py:431
  65.5 24.7 %collective-permute-start.19 = (bf16[2,768,256]{2,1,0:T(8,128)(2,1)S(1)}, bf16[2,768,256]{2,1,0:T(8,128)(2,1)}, u32[]{:S(2)}, u32[]{:S(2)}) collective-permute-start(bf16[2,768,256]{2,1,0:T(8,128)(2,1)S(1)} %pad_maximum_fusion.1.refs_0_), channel_id=1, source_target_pairs={{0,4},{1,3},{2,6},{3,1},{4,0},{5,7},{6,2},{7,5},{8,12},{9,11},{10,... | collective-permute-start | bytes 2359304 | tf_op jit(solution)/shard_map/ppermute | solution.py:431
  67.6 1.0 copy-start.13
  69.6 9.3 %copy-start.22 = (bf16[256,256]{1,0:T(8,128)(2,1)}, bf16[256,256]{1,0:T(8,128)(2,1)S(1)}, u32[]{:S(2)}) copy-start(bf16[256,256]{1,0:T(8,128)(2,1)S(1)} %get-tuple-element.70.place_ref) | copy-start | bytes 393220
  69.6 20.6 %collective-permute-start.5 = (bf16[768,256]{1,0:T(8,128)(2,1)S(1)}, bf16[768,256]{1,0:T(8,128)(2,1)S(1)}, u32[]{:S(2)}, u32[]{:S(2)}) collective-permute-start(bf16[768,256]{1,0:T(8,128)(2,1)S(1)} %get-tuple-element.63), channel_id=1, source_target_pairs={{0,2},{1,5},{2,0},{3,7},{4,6},{5,1},{6,4},{7,3},{8,10},{9,13},{10,... | collective-permute-start | bytes 1179656 | tf_op jit(solution)/shard_map/ppermute | solution.py:431
  79.0 1.0 copy-start.4
  80.0 1.0 copy-start.6
  81.8 8.7 %collective-permute-start.22 = (bf16[2,768,256]{2,1,0:T(8,128)(2,1)}, bf16[2,768,256]{2,1,0:T(8,128)(2,1)}, u32[]{:S(2)}, u32[]{:S(2)}) collective-permute-start(bf16[2,768,256]{2,1,0:T(8,128)(2,1)} %collective-permute-done.21.refs_2_), channel_id=1, source_target_pairs={{0,1},{1,0},{2,3},{3,2},{4,5},{5,4},{6,7},{7,6},{8,9},{9,8},{10,11... | collective-permute-start | bytes 2359304 | tf_op jit(solution)/shard_map/ppermute | solution.py:431
  90.2 2.6 %collective-permute-start.20 = (bf16[2,768,256]{2,1,0:T(8,128)(2,1)}, bf16[2,768,256]{2,1,0:T(8,128)(2,1)}, u32[]{:S(2)}, u32[]{:S(2)}) collective-permute-start(bf16[2,768,256]{2,1,0:T(8,128)(2,1)} %collective-permute-done.19.refs_0_), channel_id=1, source_target_pairs={{0,1},{1,0},{2,3},{3,2},{4,5},{5,4},{6,7},{7,6},{8,9},{9,8},{10,11... | collective-permute-start | bytes 2359304 | tf_op jit(solution)/shard_map/ppermute | solution.py:431
  90.3 14.9 %collective-permute-start.14 = (bf16[2,768,256]{2,1,0:T(8,128)(2,1)S(1)}, bf16[2,768,256]{2,1,0:T(8,128)(2,1)S(1)}, u32[]{:S(2)}, u32[]{:S(2)}) collective-permute-start(bf16[2,768,256]{2,1,0:T(8,128)(2,1)S(1)} %pad_maximum_fusion.refs_0_), channel_id=1, source_target_pairs={{0,4},{1,3},{2,6},{3,1},{4,0},{5,7},{6,2},{7,5},{8,12},{9,11},{10,... | collective-permute-start | bytes 2359304 | tf_op jit(solution)/shard_map/ppermute | solution.py:431
  92.8 1.3 copy-start.5
  94.1 1.3 copy-start.7
  105.2 0.9 copy-start.10
  106.1 9.3 %copy-start.9 = (bf16[2,768,256]{2,1,0:T(8,128)(2,1)S(1)}, bf16[2,768,256]{2,1,0:T(8,128)(2,1)}, u32[]{:S(2)}) copy-start(bf16[2,768,256]{2,1,0:T(8,128)(2,1)} %copy-done.8) | copy-start | bytes 2359300
  114.6 8.6 %collective-permute-start.24 = (bf16[4,256,768]{2,1,0:T(8,128)(2,1)}, bf16[4,256,768]{2,1,0:T(8,128)(2,1)}, u32[]{:S(2)}, u32[]{:S(2)}) collective-permute-start(bf16[4,256,768]{2,1,0:T(8,128)(2,1)} %get-tuple-element.96), channel_id=1, source_target_pairs={{0,1},{1,0},{2,3},{3,2},{4,5},{5,4},{6,7},{7,6},{8,9},{9,8},{10,11... | collective-permute-start | bytes 4718600 | tf_op jit(solution)/shard_map/ppermute | solution.py:431
  114.7 11.3 %collective-permute-start.23 = (bf16[4,256,768]{2,1,0:T(8,128)(2,1)}, bf16[4,256,768]{2,1,0:T(8,128)(2,1)}, u32[]{:S(2)}, u32[]{:S(2)}) collective-permute-start(bf16[4,256,768]{2,1,0:T(8,128)(2,1)} %get-tuple-element.94), channel_id=1, source_target_pairs={{0,1},{1,0},{2,3},{3,2},{4,5},{5,4},{6,7},{7,6},{8,9},{9,8},{10,11... | collective-permute-start | bytes 4718600 | tf_op jit(solution)/shard_map/ppermute | solution.py:431
  115.3 12.2 %collective-permute-start.18 = (bf16[2,768,256]{2,1,0:T(8,128)(2,1)S(1)}, bf16[2,768,256]{2,1,0:T(8,128)(2,1)S(1)}, u32[]{:S(2)}, u32[]{:S(2)}) collective-permute-start(bf16[2,768,256]{2,1,0:T(8,128)(2,1)S(1)} %pad_maximum_fusion.2.refs_2_), channel_id=1, source_target_pairs={{0,1},{1,0},{2,3},{3,2},{4,5},{5,4},{6,7},{7,6},{8,9},{9,8},{10,11... | collective-permute-start | bytes 2359304 | tf_op jit(solution)/shard_map/ppermute | solution.py:431
  115.4 24.9 %collective-permute-start.16 = (bf16[2,768,256]{2,1,0:T(8,128)(2,1)S(1)}, bf16[2,768,256]{2,1,0:T(8,128)(2,1)S(1)}, u32[]{:S(2)}, u32[]{:S(2)}) collective-permute-start(bf16[2,768,256]{2,1,0:T(8,128)(2,1)S(1)} %copy-done.9), channel_id=1, source_target_pairs={{0,1},{1,0},{2,3},{3,2},{4,5},{5,4},{6,7},{7,6},{8,9},{9,8},{10,11... | collective-permute-start | bytes 2359304 | tf_op jit(solution)/shard_map/ppermute | solution.py:431
  115.8 13.7 %collective-permute-start.17 = (bf16[2,768,256]{2,1,0:T(8,128)(2,1)S(1)}, bf16[2,768,256]{2,1,0:T(8,128)(2,1)S(1)}, u32[]{:S(2)}, u32[]{:S(2)}) collective-permute-start(bf16[2,768,256]{2,1,0:T(8,128)(2,1)S(1)} %pad_maximum_fusion.refs_0_), channel_id=1, source_target_pairs={{0,1},{1,0},{2,3},{3,2},{4,5},{5,4},{6,7},{7,6},{8,9},{9,8},{10,11... | collective-permute-start | bytes 2359304 | tf_op jit(solution)/shard_map/ppermute | solution.py:431
  123.1 1.1 copy-start.11
  124.3 16.0 %collective-permute-start.15 = (bf16[2,768,256]{2,1,0:T(8,128)(2,1)S(1)}, bf16[2,768,256]{2,1,0:T(8,128)(2,1)S(1)}, u32[]{:S(2)}, u32[]{:S(2)}) collective-permute-start(bf16[2,768,256]{2,1,0:T(8,128)(2,1)S(1)} %copy-done.11), channel_id=1, source_target_pairs={{0,1},{1,0},{2,3},{3,2},{4,5},{5,4},{6,7},{7,6},{8,9},{9,8},{10,11... | collective-permute-start | bytes 2359304 | tf_op jit(solution)/shard_map/ppermute | solution.py:431
  126.0 23.4 %collective-permute-start.26 = (bf16[2,256,768]{2,1,0:T(8,128)(2,1)S(1)}, bf16[2,256,768]{2,1,0:T(8,128)(2,1)S(1)}, u32[]{:S(2)}, u32[]{:S(2)}) collective-permute-start(bf16[2,256,768]{2,1,0:T(8,128)(2,1)S(1)} %add_convert_fusion.2), channel_id=1, source_target_pairs={{0,4},{1,3},{2,6},{3,1},{4,0},{5,7},{6,2},{7,5},{8,12},{9,11},{10,... | collective-permute-start | bytes 2359304 | tf_op jit(solution)/shard_map/ppermute | solution.py:431
  127.4 23.2 %collective-permute-start.25 = (bf16[2,256,768]{2,1,0:T(8,128)(2,1)S(1)}, bf16[2,256,768]{2,1,0:T(8,128)(2,1)S(1)}, u32[]{:S(2)}, u32[]{:S(2)}) collective-permute-start(bf16[2,256,768]{2,1,0:T(8,128)(2,1)S(1)} %add_convert_fusion.3), channel_id=1, source_target_pairs={{0,4},{1,3},{2,6},{3,1},{4,0},{5,7},{6,2},{7,5},{8,12},{9,11},{10,... | collective-permute-start | bytes 2359304 | tf_op jit(solution)/shard_map/ppermute | solution.py:431
  150.6 16.2 %collective-permute-start.28 = (bf16[256,768]{1,0:T(8,128)(2,1)S(1)}, bf16[256,768]{1,0:T(8,128)(2,1)S(1)}, u32[]{:S(2)}, u32[]{:S(2)}) collective-permute-start(bf16[256,768]{1,0:T(8,128)(2,1)S(1)} %fusion.1), channel_id=1, source_target_pairs={{0,2},{1,5},{2,0},{3,7},{4,6},{5,1},{6,4},{7,3},{8,10},{9,13},{10,... | collective-permute-start | bytes 1179656 | tf_op jit(solution)/shard_map/ppermute | solution.py:431
  151.9 15.4 %collective-permute-start.27 = (bf16[256,768]{1,0:T(8,128)(2,1)S(1)}, bf16[256,768]{1,0:T(8,128)(2,1)S(1)}, u32[]{:S(2)}, u32[]{:S(2)}) collective-permute-start(bf16[256,768]{1,0:T(8,128)(2,1)S(1)} %fusion), channel_id=1, source_target_pairs={{0,2},{1,5},{2,0},{3,7},{4,6},{5,1},{6,4},{7,3},{8,10},{9,13},{10,... | collective-permute-start | bytes 1179656 | tf_op jit(solution)/shard_map/ppermute | solution.py:431
  154.0 12.8 %copy-start.21 = (bf16[256,256]{1,0:T(8,128)(2,1)S(1)}, bf16[256,256]{1,0:T(8,128)(2,1)}, u32[]{:S(2)}) copy-start(bf16[256,256]{1,0:T(8,128)(2,1)} %copy-done.20) | copy-start | bytes 393220
  166.8 0.9 copy-start.19
  168.1 3.5 %collective-permute-start.30 = (bf16[4,256,768]{2,1,0:T(8,128)(2,1)S(1)}, bf16[4,256,768]{2,1,0:T(8,128)(2,1)S(1)}, u32[]{:S(2)}, u32[]{:S(2)}) collective-permute-start(bf16[4,256,768]{2,1,0:T(8,128)(2,1)S(1)} %get-tuple-element.112), channel_id=1, source_target_pairs={{0,1},{1,0},{2,3},{3,2},{4,5},{5,4},{6,7},{7,6},{8,9},{9,8},{10,11... | collective-permute-start | bytes 4718600 | tf_op jit(solution)/shard_map/ppermute | solution.py:431
  168.2 8.7 %collective-permute-start.29 = (bf16[4,256,768]{2,1,0:T(8,128)(2,1)S(1)}, bf16[4,256,768]{2,1,0:T(8,128)(2,1)S(1)}, u32[]{:S(2)}, u32[]{:S(2)}) collective-permute-start(bf16[4,256,768]{2,1,0:T(8,128)(2,1)S(1)} %get-tuple-element.110), channel_id=1, source_target_pairs={{0,1},{1,0},{2,3},{3,2},{4,5},{5,4},{6,7},{7,6},{8,9},{9,8},{10,11... | collective-permute-start | bytes 4718600 | tf_op jit(solution)/shard_map/ppermute | solution.py:431
  171.8 21.8 %collective-permute-start.31 = (bf16[2,256,768]{2,1,0:T(8,128)(2,1)S(1)}, bf16[2,256,768]{2,1,0:T(8,128)(2,1)S(1)}, u32[]{:S(2)}, u32[]{:S(2)}) collective-permute-start(bf16[2,256,768]{2,1,0:T(8,128)(2,1)S(1)} %add_convert_fusion), channel_id=1, source_target_pairs={{0,4},{1,3},{2,6},{3,1},{4,0},{5,7},{6,2},{7,5},{8,12},{9,11},{10,... | collective-permute-start | bytes 2359304 | tf_op jit(solution)/shard_map/ppermute | solution.py:431
  171.9 5.2 %collective-permute-start.33 = (bf16[256,768]{1,0:T(8,128)(2,1)S(1)}, bf16[256,768]{1,0:T(8,128)(2,1)S(1)}, u32[]{:S(2)}, u32[]{:S(2)}) collective-permute-start(bf16[256,768]{1,0:T(8,128)(2,1)S(1)} %shard_map.124), channel_id=1, source_target_pairs={{8,16},{16,8},{9,17},{17,9},{10,18},{18,10},{11,19},{19,11},{12,20... | collective-permute-start | bytes 1179656 | tf_op jit(solution)/shard_map/ppermute | solution.py:588
  172.6 13.6 %collective-permute-start.34 = (bf16[256,768]{1,0:T(8,128)(2,1)S(1)}, bf16[256,768]{1,0:T(8,128)(2,1)S(1)}, u32[]{:S(2)}, u32[]{:S(2)}) collective-permute-start(bf16[256,768]{1,0:T(8,128)(2,1)S(1)} %shard_map.124), channel_id=1, source_target_pairs={{0,16},{24,8},{1,17},{25,9},{2,18},{26,10},{3,19},{27,11},{4,20},{... | collective-permute-start | bytes 1179656 | tf_op jit(solution)/shard_map/ppermute | solution.py:589
  176.8 16.8 %collective-permute-start.32 = (bf16[256,768]{1,0:T(8,128)(2,1)S(1)}, bf16[256,768]{1,0:T(8,128)(2,1)S(1)}, u32[]{:S(2)}, u32[]{:S(2)}) collective-permute-start(bf16[256,768]{1,0:T(8,128)(2,1)S(1)} %shard_map.123), channel_id=1, source_target_pairs={{0,8},{8,0},{16,24},{24,16},{1,9},{9,1},{17,25},{25,17},{2,10},{10... | collective-permute-start | bytes 1179656 | tf_op jit(solution)/shard_map/ppermute | solution.py:431
  193.6 20.4 %collective-permute-start.35 = (bf16[2,256,768]{2,1,0:T(8,128)(2,1)S(1)}, bf16[2,256,768]{2,1,0:T(8,128)(2,1)S(1)}, u32[]{:S(2)}, u32[]{:S(2)}) collective-permute-start(bf16[2,256,768]{2,1,0:T(8,128)(2,1)S(1)} %add_convert_fusion.1), channel_id=1, source_target_pairs={{0,4},{1,3},{2,6},{3,1},{4,0},{5,7},{6,2},{7,5},{8,12},{9,11},{10,... | collective-permute-start | bytes 2359304 | tf_op jit(solution)/shard_map/ppermute | solution.py:431
  195.3 12.3 %copy-start.23 = (bf16[256,256]{1,0:T(8,128)(2,1)S(1)}, bf16[256,256]{1,0:T(8,128)(2,1)}, u32[]{:S(2)}) copy-start(bf16[256,256]{1,0:T(8,128)(2,1)} %copy-done.22) | copy-start | bytes 393220
  195.5 12.1 %collective-permute-start.37 = (bf16[256,768]{1,0:T(8,128)(2,1)S(1)}, bf16[256,768]{1,0:T(8,128)(2,1)S(1)}, u32[]{:S(2)}, u32[]{:S(2)}) collective-permute-start(bf16[256,768]{1,0:T(8,128)(2,1)S(1)} %fusion.3), channel_id=1, source_target_pairs={{0,2},{1,5},{2,0},{3,7},{4,6},{5,1},{6,4},{7,3},{8,10},{9,13},{10,... | collective-permute-start | bytes 1179656 | tf_op jit(solution)/shard_map/ppermute | solution.py:431
  208.0 14.0 %copy-start.17 = (bf16[256,256]{1,0:T(8,128)(2,1)S(1)}, bf16[256,256]{1,0:T(8,128)(2,1)}, u32[]{:S(2)}) copy-start(bf16[256,256]{1,0:T(8,128)(2,1)} %copy-done.16) | copy-start | bytes 393220
  208.0 20.1 %collective-permute-start.38 = (bf16[256,768]{1,0:T(8,128)(2,1)S(1)}, bf16[256,768]{1,0:T(8,128)(2,1)S(1)}, u32[]{:S(2)}, u32[]{:S(2)}) collective-permute-start(bf16[256,768]{1,0:T(8,128)(2,1)S(1)} %shard_map.126), channel_id=1, source_target_pairs={{8,24},{16,0},{9,25},{17,1},{10,26},{18,2},{11,27},{19,3},{12,28},... | collective-permute-start | bytes 1179656 | tf_op jit(solution)/shard_map/ppermute | solution.py:601
  209.5 18.7 %collective-permute-start.39 = (bf16[256,768]{1,0:T(8,128)(2,1)S(1)}, bf16[256,768]{1,0:T(8,128)(2,1)S(1)}, u32[]{:S(2)}, u32[]{:S(2)}) collective-permute-start(bf16[256,768]{1,0:T(8,128)(2,1)S(1)} %shard_map.126), channel_id=1, source_target_pairs={{0,24},{24,0},{1,25},{25,1},{2,26},{26,2},{3,27},{27,3},{4,28},{28... | collective-permute-start | bytes 1179656 | tf_op jit(solution)/shard_map/ppermute | solution.py:602
  214.2 7.8 %collective-permute-start.36 = (bf16[256,768]{1,0:T(8,128)(2,1)S(1)}, bf16[256,768]{1,0:T(8,128)(2,1)S(1)}, u32[]{:S(2)}, u32[]{:S(2)}) collective-permute-start(bf16[256,768]{1,0:T(8,128)(2,1)S(1)} %fusion.2), channel_id=1, source_target_pairs={{0,2},{1,5},{2,0},{3,7},{4,6},{5,1},{6,4},{7,3},{8,10},{9,13},{10,... | collective-permute-start | bytes 1179656 | tf_op jit(solution)/shard_map/ppermute | solution.py:431
  (2 other events, 1.4 us)

commit v9 on v8

--- a/solution.py
+++ b/solution.py
@@ -242,9 +242,9 @@
 
 def combine_kernel(place_ref, *refs):
     shares, out_ref = refs[:-1], refs[-1]
-    total = shares[0][...].astype(F32)
+    total = shares[0][0].astype(F32)
     for share in shares[1:]:
-        total = total + share[...].astype(F32)
+        total = total + share[0].astype(F32)
     out_ref[...] = lax.dot_general(
         place_ref[...], total.astype(BF16), (((0,), (0,)), ((), ())), preferred_element_type=F32
     ).astype(BF16)
@@ -252,9 +252,12 @@
 
 def combine_slots(place, shares):
     slots, length = place.shape
-    width = shares[0].shape[1]
+    width = shares[0].shape[2]
+    first = pl.BlockSpec((1, slots, width), lambda _: (0, 0, 0))
     return pl.pallas_call(
         combine_kernel,
+        grid=(1,),
+        in_specs=[pl.BlockSpec(memory_space=pltpu.VMEM), *([first] * len(shares))],
         out_shape=jax.ShapeDtypeStruct((length, width), BF16),
         cost_estimate=pl.CostEstimate(
             flops=2 * slots * length * width, bytes_accessed=8 * slots * width, transcendentals=0
@@ -511,7 +514,7 @@
             (partial,) = down_part([order], hidden, down_weight, width, len(chunk))
             for offset, share, (_, place) in zip(chunk, partial, chosen):
                 share = lax.psum_scatter(share, "exp", scatter_dimension=0)
-                piece = combine_slots(place, [share])
+                piece = combine_slots(place, [share[None]])
                 pieces.append(swapped(piece, "seq", offset, offset) if offset else piece)
     total = stream[:length].astype(F32)
     for piece in pieces:
@@ -543,14 +546,14 @@
     passed_third = outward(third)
     fourth = across_middle(neighbour)
     chosen["neighbour"] = select(neighbour)
-    gather("neighbour", [passed_third, fourth, far_two["own"]])
+    gather("neighbour", [passed_third, fourth, two["own"]])
     passed_fourth = outward(fourth)
     chosen["third"] = select(third, passed_third)
     gather("third", passed_fourth)
     chosen["fourth"] = select(fourth, passed_fourth)
 
     pieces = {}
-    sent, one = [], []
+    sent, finish = [], None
     for chunk, after in ((("neighbour", "third"), "fourth"), (("fourth", "own"), None)):
         early = [[two[name], near[name]] for name in chunk]
         if after:
@@ -571,33 +574,35 @@
             hidden, theirs = tie((hidden, theirs))
             (mine,) = down_part([plane.mine], hidden, down_weight, width, len(chunk))
         else:
+            one = finish(hidden)
             hidden, _ = tie((hidden, one))
             theirs, mine = down_part([plane.theirs, plane.mine], hidden, down_weight, width, len(chunk))
             theirs, _ = tie((theirs, list(pieces.values())))
-        sent, got_two, one = [], [], []
-        for k, name in enumerate(chunk):
-            near_share = plane.across(theirs[k])
-            two_share = added(mine[k][2:], near_share[2:])
-            sent.append(two_share)
-            if got_two and not after:
-                two_share, _ = tie((two_share, got_two))
-            got_two.append(plane.second(two_share))
-            if not after and k == 0:
-                home = [
-                    swapped(pieces["neighbour"], "seq", 1, 1),
-                    lax.ppermute(pieces["third"], "seq", [(1, 2), (2, 1)]),
-                    lax.ppermute(pieces["third"], "seq", [(0, 2), (3, 1)]),
-                ]
-                got_two[0], _ = tie((got_two[0], home))
-            one_share = added(added(mine[k][1], near_share[1]), got_two[k][1])
-            one.append(one_share)
-            got_one = plane.once(one_share)
-            pieces[name] = combine_slots(
-                chosen[name][1], [mine[k][0], near_share[0], got_two[k][0], got_one]
-            )
+        near_share = [plane.across(part) for part in theirs]
+        sent = [added(kept[2:], got[2:]) for kept, got in zip(mine, near_share)]
+        got_two = [plane.second(sent[0])]
+        part = sent[1] if after else tie((sent[1], got_two))[0]
+        got_two.append(plane.second(part))
+
+        def finish(behind, chunk=chunk, mine=mine, near_share=near_share, got_two=got_two):
+            got_two = [tie((far, behind))[0] for far in got_two]
+            one = [
+                added(added(kept[1], got[1]), far[1])
+                for kept, got, far in zip(mine, near_share, got_two)
+            ]
+            for k, name in enumerate(chunk):
+                got_one = plane.once(one[k])[None]
+                pieces[name] = combine_slots(
+                    chosen[name][1], [mine[k], near_share[k], got_two[k], got_one]
+                )
+            return one
+
+    finish([])
     return [
         pieces["own"],
-        *home,
+        swapped(pieces["neighbour"], "seq", 1, 1),
+        lax.ppermute(pieces["third"], "seq", [(1, 2), (2, 1)]),
+        lax.ppermute(pieces["third"], "seq", [(0, 2), (3, 1)]),
         lax.ppermute(pieces["fourth"], "seq", [(1, 3), (2, 0)]),
         lax.ppermute(pieces["fourth"], "seq", [(0, 3), (3, 0)]),
     ]

time: 230 us -> 241 us (1.048)
  waiting for transfers between devices: 83.1 us -> 92.2 us
  starting transfers between devices: 45.8 us -> 49.5 us
    ppermute x1, waiting for transfers between devices: 5.68 us -> 13.7 us  [paired_chunks(): lax.ppermute(pieces['fourth'], 'seq', [(1, 3), (2, 0)])]
    ppermute x1, waiting for transfers between devices: 9.14 us -> 2.84 us  [paired_chunks(): lax.ppermute(pieces['third'], 'seq', [(0, 2), (3, 1)])]
    ppermute x30, waiting for transfers between devices: 57.3 us -> 63.3 us  [swapped(): return lax.ppermute(array, axis, pairs)]
    ppermute x30, starting transfers between devices: 21.5 us -> 25.6 us  [swapped(): return lax.ppermute(array, axis, pairs)]
    convert_element_type x8, other arithmetic: 5.7 us -> 3.19 us  [added(): return (left.astype(F32) + right.astype(F32)).astype(BF16)]
    unnamed x52 -> x86, local copies, waits for them, and re-layouts: 13.2 us -> 15.5 us
  transfers between devices with their start and end apart: 40 -> 40, of which waited for: 15 -> 16; matrix products, arithmetic and copies ran while one was open for 4% -> 2% of each run, Pallas kernels for 28% -> 27%
where the time goes in v9:
time: 241 us; the launch traced here: 240 us
  waiting for transfers between devices  92.2 us (38%)
  Pallas kernels  75.3 us (31%)
  starting transfers between devices  49.5 us (21%)
  local copies, waits for them, and re-layouts  16.5 us (7%)
  other arithmetic  5.98 us (2%)
    ppermute x30, waiting for transfers between devices, swapped(): return lax.ppermute(array, axis, pairs)  63.3 us
    pallas_call x4, Pallas kernels, gate_part(): pl.pallas_call(functools.partial(gate_kernel, counts, len(xs), last), gri...  36.5 us
    pallas_call x3, Pallas kernels, down_part(): pl.pallas_call(functools.partial(down_kernel, blocks, sections), grid_spe...  27.5 us
    ppermute x30, starting transfers between devices, swapped(): return lax.ppermute(array, axis, pairs)  25.6 us
    unnamed x86, local copies, waits for them, and re-layouts  15.5 us
    ppermute x1, waiting for transfers between devices, paired_chunks(): lax.ppermute(pieces['fourth'], 'seq', [(1, 3), (2, 0)])  13.7 us
    ppermute x2, starting transfers between devices, shifted(): return lax.ppermute(array, axis, pairs)  9.43 us
    ppermute x2, waiting for transfers between devices, outward(): return lax.ppermute(part, 'seq', [(1, 0), (2, 3)])  8.38 us
  transfers between devices with their start and end apart: 40, of which 16 were waited for; matrix products, arithmetic and copies ran while one was open for 2% of the time, Pallas kernels for 27%

profile of v9, /device:TPU:0, one launch (start us, length us, event | category | flops | bytes accessed | tf_op | source)
XLA Modules:
  0.0 240.3 jit_solution(11660077432802655551)
XLA Ops:
  0.0 2.1 shard_map.109
  2.2 4.9 %collective-permute-start = (bf16[784,128]{1,0:T(8,128)(2,1)S(1)}, bf16[784,128]{1,0:T(8,128)(2,1)S(1)}, u32[]{:S(2)}, u32[]{:S(2)}) collective-permute-start(bf16[784,128]{1,0:T(8,128)(2,1)S(1)} %get-tuple-element.62), channel_id=1, source_target_pairs={{0,8},{8,16},{16,24},{1,9},{9,17},{17,25},{2,10},{10,18},{18,26},{... | collective-permute-start | bytes 602120 | tf_op jit(solution)/shard_map/ppermute | solution.py:30
  7.8 1.0 copy-done.15
  8.8 1.0 copy-done.17
  9.8 1.0 copy-done.18
  11.5 1.4 shard_map.110.intra_ref
  13.2 4.5 %collective-permute-start.1 = (bf16[784,128]{1,0:T(8,128)(2,1)S(1)}, bf16[784,128]{1,0:T(8,128)(2,1)S(1)}, u32[]{:S(2)}, u32[]{:S(2)}) collective-permute-start(bf16[784,128]{1,0:T(8,128)(2,1)S(1)} %concatenate.7), channel_id=1, source_target_pairs={{0,16},{8,24},{1,17},{9,25},{2,18},{10,26},{3,19},{11,27},{4,20},{... | collective-permute-start | bytes 602120 | tf_op jit(solution)/shard_map/ppermute | solution.py:30
  17.7 3.9 %collective-permute-done.1 = bf16[784,128]{1,0:T(8,128)(2,1)S(1)} collective-permute-done((bf16[784,128]{1,0:T(8,128)(2,1)S(1)}, bf16[784,128]{1,0:T(8,128)(2,1)S(1)}, u32[]{:S(2)}, u32[]{:S(2)}) %collective-permute-start.1) | collective-permute-done | bytes 200736 | tf_op jit(solution)/shard_map/ppermute | solution.py:30
  23.4 5.8 %collective-permute-start.2 = (bf16[272,768]{1,0:T(8,128)(2,1)S(1)}, bf16[272,768]{1,0:T(8,128)(2,1)S(1)}, u32[]{:S(2)}, u32[]{:S(2)}) collective-permute-start(bf16[272,768]{1,0:T(8,128)(2,1)S(1)} %shard_map.111.refs_0_), channel_id=1, source_target_pairs={{0,8},{8,0},{16,24},{24,16},{1,9},{9,1},{17,25},{25,17},{2,10},{10... | collective-permute-start | bytes 1253384 | tf_op jit(solution)/shard_map/ppermute | solution.py:434
  29.2 1.3 collective-permute-start.8
  30.5 7.3 %collective-permute-done.2.refs_0_ = bf16[272,768]{1,0:T(8,128)(2,1)S(1)} collective-permute-done((bf16[272,768]{1,0:T(8,128)(2,1)S(1)}, bf16[272,768]{1,0:T(8,128)(2,1)S(1)}, u32[]{:S(2)}, u32[]{:S(2)}) %collective-permute-start.2) | collective-permute-done | bytes 417824 | tf_op jit(solution)/shard_map/ppermute | solution.py:434
  38.5 1.0 shard_map.112
  40.2 1.5 collective-permute-start.9
  41.7 1.0 shard_map.114
  44.0 4.4 %collective-permute-done.8.refs_1_ = bf16[272,768]{1,0:T(8,128)(2,1)S(1)} collective-permute-done((bf16[272,768]{1,0:T(8,128)(2,1)S(1)}, bf16[272,768]{1,0:T(8,128)(2,1)S(1)}, u32[]{:S(2)}, u32[]{:S(2)}) %collective-permute-start.8) | collective-permute-done | bytes 417824 | tf_op jit(solution)/shard_map/ppermute | solution.py:535
  48.3 1.0 shard_map.115
  49.4 1.5 collective-permute-start.11
  50.9 1.3 collective-permute-start.4
  52.2 1.0 pad_maximum_fusion.2.refs_2_
  53.4 3.8 %collective-permute-done.11 = bf16[768,256]{1,0:T(8,128)(2,1)S(1)} collective-permute-done((bf16[768,256]{1,0:T(8,128)(2,1)S(1)}, bf16[768,256]{1,0:T(8,128)(2,1)S(1)}, u32[]{:S(2)}, u32[]{:S(2)}) %collective-permute-start.11) | collective-permute-done | bytes 393248 | tf_op jit(solution)/shard_map/ppermute | solution.py:434
  57.3 4.0 %collective-permute-done.4.refs_1_ = bf16[272,768]{1,0:T(8,128)(2,1)S(1)} collective-permute-done((bf16[272,768]{1,0:T(8,128)(2,1)S(1)}, bf16[272,768]{1,0:T(8,128)(2,1)S(1)}, u32[]{:S(2)}, u32[]{:S(2)}) %collective-permute-start.4) | collective-permute-done | bytes 417824 | tf_op jit(solution)/shard_map/ppermute | solution.py:535
  62.1 1.1 collective-permute-start.21
  63.2 0.9 collective-permute-start.19
  64.2 1.0 copy-done.26
  65.2 1.0 copy-done.28
  66.2 1.0 shard_map.113
  67.9 1.5 collective-permute-start.5
  69.4 0.9 copy-done.23
  70.3 1.1 copy-done.24
  72.2 9.1 %shard_map.116 = (f32[2,576,256]{2,1,0:T(8,128)S(1)}, f32[2,576,256]{2,1,0:T(8,128)S(1)}, f32[2,2,256]{2,1,0:T(2,128)S(1)}) custom-call(s32[4]{0:T(128)S(1)} %get-tuple-element.120.plan_ref, bf16[2,768,256]{2,1,0:T(8,128)(2,1)S(1)} %pad_maximum_fusion.1.refs_0_, bf16[2,768,256]{2,1,0:T(8,128)(2,1)S(1)} %copy-done.24, ...), custom_call_target="tpu_custom_call" | custom-call | flops 3623878656 | bytes 14155776 | tf_op jit(solution)/shard_map/pallas_call | solution.py:346
  81.3 1.0 copy-done.19
  82.3 4.5 %collective-permute-done.19.refs_0_ = bf16[2,768,256]{2,1,0:T(8,128)(2,1)} collective-permute-done((bf16[2,768,256]{2,1,0:T(8,128)(2,1)S(1)}, bf16[2,768,256]{2,1,0:T(8,128)(2,1)}, u32[]{:S(2)}, u32[]{:S(2)}) %collective-permute-start.19) | collective-permute-done | bytes 786464 | tf_op jit(solution)/shard_map/ppermute | solution.py:434
  86.9 1.1 collective-permute-start.13
  88.1 1.3 collective-permute-done.20.refs_1_
  89.4 1.3 copy-done.20
  91.5 9.7 %shard_map.117.hidden_ref = bf16[2,256,576]{2,1,0:T(8,128)(2,1)S(1)} custom-call(s32[4]{0:T(128)S(1)} %add_add_fusion.plan_ref, bf16[2,768,256]{2,1,0:T(8,128)(2,1)} %collective-permute-done.19.refs_0_, bf16[2,768,256]{2,1,0:T(8,128)(2,1)} %collective-permute-done.20.refs_1_, bf16[2,768,256]{2,1,0:T(8,128)(2,1)S(1)} %collective-permute-done.21.refs_2_, ...), custom_call_target="tpu_custom_call" | custom-call | flops 3623878656 | bytes 14155776 | tf_op jit(solution)/shard_map/pallas_call | solution.py:346
  101.2 7.4 %shard_map.118 = (bf16[4,256,768]{2,1,0:T(8,128)(2,1)S(1)}, bf16[4,256,768]{2,1,0:T(8,128)(2,1)S(1)}) custom-call(s32[4]{0:T(128)S(1)} %get-tuple-element.121.plan_ref, bf16[2,256,576]{2,1,0:T(8,128)(2,1)S(1)} %shard_map.117.hidden_ref, bf16[2,576,6144]{2,1,0:T(8,128)(2,1)} %down_ref.5), custom_call_target="tpu_custom_call" | custom-call | flops 1811939328 | bytes 7077888 | tf_op jit(solution)/shard_map/pallas_call | solution.py:405
  109.2 1.1 collective-permute-start.15
  110.8 10.3 %collective-permute-done.15.refs_2_ = bf16[2,768,256]{2,1,0:T(8,128)(2,1)S(1)} collective-permute-done((bf16[2,768,256]{2,1,0:T(8,128)(2,1)S(1)}, bf16[2,768,256]{2,1,0:T(8,128)(2,1)S(1)}, u32[]{:S(2)}, u32[]{:S(2)}) %collective-permute-start.15) | collective-permute-done | bytes 786464 | tf_op jit(solution)/shard_map/ppermute | solution.py:434
  121.2 7.2 %shard_map.119 = (bf16[4,256,768]{2,1,0:T(8,128)(2,1)S(1)}, bf16[4,256,768]{2,1,0:T(8,128)(2,1)S(1)}) custom-call(s32[4]{0:T(128)S(1)} %pad_add_fusion.3.plan_ref, bf16[2,256,576]{2,1,0:T(8,128)(2,1)S(1)} %shard_map.117.hidden_ref, bf16[2,576,6144]{2,1,0:T(8,128)(2,1)} %down_ref.5), custom_call_target="tpu_custom_call" | custom-call | flops 1811939328 | bytes 7077888 | tf_op jit(solution)/shard_map/pallas_call | solution.py:405
  129.2 1.1 collective-permute-start.26
  130.5 1.0 collective-permute-start.25
  131.6 8.6 %shard_map.120 = (f32[2,576,256]{2,1,0:T(8,128)S(1)}, f32[2,576,256]{2,1,0:T(8,128)S(1)}, f32[2,2,256]{2,1,0:T(2,128)S(1)}) custom-call(s32[4]{0:T(128)S(1)} %get-tuple-element.120.plan_ref, bf16[2,768,256]{2,1,0:T(8,128)(2,1)S(1)} %copy-done.8, bf16[2,768,256]{2,1,0:T(8,128)(2,1)S(1)} %collective-permute-done.17.refs_1_, ...), custom_call_target="tpu_custom_call" | custom-call | flops 3623878656 | bytes 14155776 | tf_op jit(solution)/shard_map/pallas_call | solution.py:346
  140.2 9.1 %shard_map.121.hidden_ref = bf16[2,256,576]{2,1,0:T(8,128)(2,1)S(1)} custom-call(s32[4]{0:T(128)S(1)} %add_add_fusion.plan_ref, bf16[2,768,256]{2,1,0:T(8,128)(2,1)S(1)} %copy-done.22, bf16[2,768,256]{2,1,0:T(8,128)(2,1)S(1)} %collective-permute-done.14.refs_1_, bf16[2,768,256]{2,1,0:T(8,128)(2,1)S(1)} %collective-permute-done.15.refs_2_, ...), custom_call_target="tpu_custom_call" | custom-call | flops 3623878656 | bytes 14155776 | tf_op jit(solution)/shard_map/pallas_call | solution.py:346
  149.4 1.1 fusion.1
  150.5 1.5 collective-permute-start.28
  152.0 1.0 fusion
  153.7 1.1 copy-done.10
  154.8 12.9 %shard_map.122 = (bf16[4,256,768]{2,1,0:T(8,128)(2,1)S(1)}, bf16[4,256,768]{2,1,0:T(8,128)(2,1)S(1)}, bf16[4,256,768]{2,1,0:T(8,128)(2,1)S(1)}, bf16[4,256,768]{2,1,0:T(8,128)(2,1)S(1)}) custom-call(s32[8]{0:T(128)S(1)} %concatenate.8.plan_ref, bf16[2,256,576]{2,1,0:T(8,128)(2,1)S(1)} %copy-done.10, bf16[2,576,6144]{2,1,0:T(8,128)(2,1)} %down_ref.5), custom_call_target="tpu_custom_call" | custom-call | flops 3623878656 | bytes 14155776 | tf_op jit(solution)/shard_map/pallas_call | solution.py:405
  167.8 1.6 shard_map.124
  170.5 2.9 %collective-permute-done.30.refs_1_ = bf16[4,256,768]{2,1,0:T(8,128)(2,1)S(1)} collective-permute-done((bf16[4,256,768]{2,1,0:T(8,128)(2,1)S(1)}, bf16[4,256,768]{2,1,0:T(8,128)(2,1)S(1)}, u32[]{:S(2)}, u32[]{:S(2)}) %collective-permute-start.30) | collective-permute-done | bytes 1572896 | tf_op jit(solution)/shard_map/ppermute | solution.py:434
  173.6 1.1 collective-permute-start.31
  174.7 0.9 collective-permute-done.29.refs_1_
  175.8 9.8 %collective-permute-done.31.refs_2_ = bf16[2,256,768]{2,1,0:T(8,128)(2,1)S(1)} collective-permute-done((bf16[2,256,768]{2,1,0:T(8,128)(2,1)S(1)}, bf16[2,256,768]{2,1,0:T(8,128)(2,1)S(1)}, u32[]{:S(2)}, u32[]{:S(2)}) %collective-permute-start.31) | collective-permute-done | bytes 786464 | tf_op jit(solution)/shard_map/ppermute | solution.py:434
  185.6 1.1 collective-permute-start.32
  186.8 1.0 collective-permute-start.37
  187.8 13.8 %collective-permute-done.32.refs_2_ = bf16[2,256,768]{2,1,0:T(8,128)(2,1)S(1)} collective-permute-done((bf16[2,256,768]{2,1,0:T(8,128)(2,1)S(1)}, bf16[2,256,768]{2,1,0:T(8,128)(2,1)S(1)}, u32[]{:S(2)}, u32[]{:S(2)}) %collective-permute-start.32) | collective-permute-done | bytes 786464 | tf_op jit(solution)/shard_map/ppermute | solution.py:434
  203.0 4.5 %collective-permute-start.36 = (bf16[256,768]{1,0:T(8,128)(2,1)S(1)}, bf16[256,768]{1,0:T(8,128)(2,1)S(1)}, u32[]{:S(2)}, u32[]{:S(2)}) collective-permute-start(bf16[256,768]{1,0:T(8,128)(2,1)S(1)} %shard_map.124), channel_id=1, source_target_pairs={{0,16},{24,8},{1,17},{25,9},{2,18},{26,10},{3,19},{27,11},{4,20},{... | collective-permute-start | bytes 1179656 | tf_op jit(solution)/shard_map/ppermute | solution.py:605
  208.1 1.3 collective-permute-start.38
  209.6 4.1 %collective-permute-start.39 = (bf16[256,768]{1,0:T(8,128)(2,1)S(1)}, bf16[256,768]{1,0:T(8,128)(2,1)S(1)}, u32[]{:S(2)}, u32[]{:S(2)}) collective-permute-start(bf16[256,768]{1,0:T(8,128)(2,1)S(1)} %shard_map.126), channel_id=1, source_target_pairs={{0,24},{24,0},{1,25},{25,1},{2,26},{26,2},{3,27},{27,3},{4,28},{28... | collective-permute-start | bytes 1179656 | tf_op jit(solution)/shard_map/ppermute | solution.py:607
  214.2 2.8 %collective-permute-done.36 = bf16[256,768]{1,0:T(8,128)(2,1)S(1)} collective-permute-done((bf16[256,768]{1,0:T(8,128)(2,1)S(1)}, bf16[256,768]{1,0:T(8,128)(2,1)S(1)}, u32[]{:S(2)}, u32[]{:S(2)}) %collective-permute-start.36) | collective-permute-done | bytes 393248 | tf_op jit(solution)/shard_map/ppermute | solution.py:605
  217.1 8.4 %collective-permute-done.34 = bf16[256,768]{1,0:T(8,128)(2,1)S(1)} collective-permute-done((bf16[256,768]{1,0:T(8,128)(2,1)S(1)}, bf16[256,768]{1,0:T(8,128)(2,1)S(1)}, u32[]{:S(2)}, u32[]{:S(2)}) %collective-permute-start.34) | collective-permute-done | bytes 393248 | tf_op jit(solution)/shard_map/ppermute | solution.py:434
  225.5 13.7 %collective-permute-done.38 = bf16[256,768]{1,0:T(8,128)(2,1)S(1)} collective-permute-done((bf16[256,768]{1,0:T(8,128)(2,1)S(1)}, bf16[256,768]{1,0:T(8,128)(2,1)S(1)}, u32[]{:S(2)}, u32[]{:S(2)}) %collective-permute-start.38) | collective-permute-done | bytes 393248 | tf_op jit(solution)/shard_map/ppermute | solution.py:606
  239.2 1.1 add_convert_fusion.8
  (149 shorter events, 16.4 us)
Async XLA Ops:
  2.2 10.8 %collective-permute-start = (bf16[784,128]{1,0:T(8,128)(2,1)S(1)}, bf16[784,128]{1,0:T(8,128)(2,1)S(1)}, u32[]{:S(2)}, u32[]{:S(2)}) collective-permute-start(bf16[784,128]{1,0:T(8,128)(2,1)S(1)} %get-tuple-element.62), channel_id=1, source_target_pairs={{0,8},{8,16},{16,24},{1,9},{9,17},{17,25},{2,10},{10,18},{18,26},{... | collective-permute-start | bytes 602120 | tf_op jit(solution)/shard_map/ppermute | solution.py:30
  12.9 8.9 %copy-start.16 = (bf16[256,768]{1,0:T(8,128)(2,1)S(1)}, bf16[256,768]{1,0:T(8,128)(2,1)}, u32[]{:S(2)}) copy-start(bf16[256,768]{1,0:T(8,128)(2,1)} %query_ref.3) | copy-start | bytes 1179652
  12.9 8.9 %copy-start.32 = (bf16[256,768]{1,0:T(8,128)(2,1)S(1)}, bf16[256,768]{1,0:T(8,128)(2,1)}, u32[]{:S(2)}) copy-start(bf16[256,768]{1,0:T(8,128)(2,1)} %residual_ref.1) | copy-start | bytes 1179652
  12.9 8.9 %copy-start.42 = (s32[256,2]{0,1:T(2,128)S(1)}, s32[256,2]{0,1:T(2,128)}, u32[]{:S(2)}) copy-start(s32[256,2]{0,1:T(2,128)} %param.17) | copy-start | bytes 6148
  13.2 8.5 %collective-permute-start.1 = (bf16[784,128]{1,0:T(8,128)(2,1)S(1)}, bf16[784,128]{1,0:T(8,128)(2,1)S(1)}, u32[]{:S(2)}, u32[]{:S(2)}) collective-permute-start(bf16[784,128]{1,0:T(8,128)(2,1)S(1)} %concatenate.7), channel_id=1, source_target_pairs={{0,16},{8,24},{1,17},{9,25},{2,18},{10,26},{3,19},{11,27},{4,20},{... | collective-permute-start | bytes 602120 | tf_op jit(solution)/shard_map/ppermute | solution.py:30
  22.7 30.5 %copy-start.4 = (bf16[272,768]{1,0:T(8,128)(2,1)}, bf16[272,768]{1,0:T(8,128)(2,1)S(1)}, u32[]{:S(2)}) copy-start(bf16[272,768]{1,0:T(8,128)(2,1)S(1)} %shard_map.111.refs_0_) | copy-start | bytes 1253380
  22.7 6.5 %collective-permute-start.7 = (bf16[272,768]{1,0:T(8,128)(2,1)S(1)}, bf16[272,768]{1,0:T(8,128)(2,1)S(1)}, u32[]{:S(2)}, u32[]{:S(2)}) collective-permute-start(bf16[272,768]{1,0:T(8,128)(2,1)S(1)} %shard_map.111.refs_0_), channel_id=1, source_target_pairs={{8,16},{16,8},{9,17},{17,9},{10,18},{18,10},{11,19},{19,11},{12,20... | collective-permute-start | bytes 1253384 | tf_op jit(solution)/shard_map/ppermute | solution.py:532
  23.4 14.4 %collective-permute-start.2 = (bf16[272,768]{1,0:T(8,128)(2,1)S(1)}, bf16[272,768]{1,0:T(8,128)(2,1)S(1)}, u32[]{:S(2)}, u32[]{:S(2)}) collective-permute-start(bf16[272,768]{1,0:T(8,128)(2,1)S(1)} %shard_map.111.refs_0_), channel_id=1, source_target_pairs={{0,8},{8,0},{16,24},{24,16},{1,9},{9,1},{17,25},{25,17},{2,10},{10... | collective-permute-start | bytes 1253384 | tf_op jit(solution)/shard_map/ppermute | solution.py:434
  29.2 19.1 %collective-permute-start.8 = (bf16[272,768]{1,0:T(8,128)(2,1)S(1)}, bf16[272,768]{1,0:T(8,128)(2,1)S(1)}, u32[]{:S(2)}, u32[]{:S(2)}) collective-permute-start(bf16[272,768]{1,0:T(8,128)(2,1)S(1)} %collective-permute-done.7.refs_0_), channel_id=1, source_target_pairs={{8,0},{16,24},{9,1},{17,25},{10,2},{18,26},{11,3},{19,27},{12,4},{... | collective-permute-start | bytes 1253384 | tf_op jit(solution)/shard_map/ppermute | solution.py:535
  37.8 13.1 %collective-permute-start.3 = (bf16[272,768]{1,0:T(8,128)(2,1)S(1)}, bf16[272,768]{1,0:T(8,128)(2,1)S(1)}, u32[]{:S(2)}, u32[]{:S(2)}) collective-permute-start(bf16[272,768]{1,0:T(8,128)(2,1)S(1)} %collective-permute-done.2.refs_0_), channel_id=1, source_target_pairs={{8,16},{16,8},{9,17},{17,9},{10,18},{18,10},{11,19},{19,11},{12,20... | collective-permute-start | bytes 1253384 | tf_op jit(solution)/shard_map/ppermute | solution.py:532
  40.2 12.0 %collective-permute-start.9 = (bf16[768,256]{1,0:T(8,128)(2,1)S(1)}, bf16[768,256]{1,0:T(8,128)(2,1)S(1)}, u32[]{:S(2)}, u32[]{:S(2)}) collective-permute-start(bf16[768,256]{1,0:T(8,128)(2,1)S(1)} %get-tuple-element.66), channel_id=1, source_target_pairs={{0,2},{1,5},{2,0},{3,7},{4,6},{5,1},{6,4},{7,3},{8,10},{9,13},{10,... | collective-permute-start | bytes 1179656 | tf_op jit(solution)/shard_map/ppermute | solution.py:434
  43.4 9.8 %collective-permute-start.6 = (bf16[768,256]{1,0:T(8,128)(2,1)S(1)}, bf16[768,256]{1,0:T(8,128)(2,1)S(1)}, u32[]{:S(2)}, u32[]{:S(2)}) collective-permute-start(bf16[768,256]{1,0:T(8,128)(2,1)S(1)} %get-tuple-element.65), channel_id=1, source_target_pairs={{0,2},{1,5},{2,0},{3,7},{4,6},{5,1},{6,4},{7,3},{8,10},{9,13},{10,... | collective-permute-start | bytes 1179656 | tf_op jit(solution)/shard_map/ppermute | solution.py:434
  49.4 3.9 %copy-start.37 = (bf16[256,256]{1,0:T(8,128)(2,1)}, bf16[256,256]{1,0:T(8,128)(2,1)S(1)}, u32[]{:S(2)}) copy-start(bf16[256,256]{1,0:T(8,128)(2,1)S(1)} %get-tuple-element.112.place_ref) | copy-start | bytes 393220
  49.4 7.8 %collective-permute-start.11 = (bf16[768,256]{1,0:T(8,128)(2,1)S(1)}, bf16[768,256]{1,0:T(8,128)(2,1)S(1)}, u32[]{:S(2)}, u32[]{:S(2)}) collective-permute-start(bf16[768,256]{1,0:T(8,128)(2,1)S(1)} %get-tuple-element.69), channel_id=1, source_target_pairs={{0,2},{1,5},{2,0},{3,7},{4,6},{5,1},{6,4},{7,3},{8,10},{9,13},{10,... | collective-permute-start | bytes 1179656 | tf_op jit(solution)/shard_map/ppermute | solution.py:434
  50.9 2.4 copy-start.25
  50.9 10.4 %collective-permute-start.4 = (bf16[272,768]{1,0:T(8,128)(2,1)S(1)}, bf16[272,768]{1,0:T(8,128)(2,1)S(1)}, u32[]{:S(2)}, u32[]{:S(2)}) collective-permute-start(bf16[272,768]{1,0:T(8,128)(2,1)S(1)} %collective-permute-done.3.refs_0_), channel_id=1, source_target_pairs={{8,0},{16,24},{9,1},{17,25},{10,2},{18,26},{11,3},{19,27},{12,4},{... | collective-permute-start | bytes 1253384 | tf_op jit(solution)/shard_map/ppermute | solution.py:535
  53.3 16.1 %collective-permute-start.10 = (bf16[2,768,256]{2,1,0:T(8,128)(2,1)S(1)}, bf16[2,768,256]{2,1,0:T(8,128)(2,1)S(1)}, u32[]{:S(2)}, u32[]{:S(2)}) collective-permute-start(bf16[2,768,256]{2,1,0:T(8,128)(2,1)S(1)} %pad_maximum_fusion.1.refs_0_), channel_id=1, source_target_pairs={{0,1},{1,0},{2,3},{3,2},{4,5},{5,4},{6,7},{7,6},{8,9},{9,8},{10,11... | collective-permute-start | bytes 2359304 | tf_op jit(solution)/shard_map/ppermute | solution.py:434
  62.1 8.2 %collective-permute-start.12 = (bf16[2,768,256]{2,1,0:T(8,128)(2,1)S(1)}, bf16[2,768,256]{2,1,0:T(8,128)(2,1)}, u32[]{:S(2)}, u32[]{:S(2)}) collective-permute-start(bf16[2,768,256]{2,1,0:T(8,128)(2,1)S(1)} %pad_maximum_fusion.3.refs_2_), channel_id=1, source_target_pairs={{0,1},{1,0},{2,3},{3,2},{4,5},{5,4},{6,7},{7,6},{8,9},{9,8},{10,11... | collective-permute-start | bytes 2359304 | tf_op jit(solution)/shard_map/ppermute | solution.py:434
  62.1 20.2 %collective-permute-start.21 = (bf16[2,768,256]{2,1,0:T(8,128)(2,1)S(1)}, bf16[2,768,256]{2,1,0:T(8,128)(2,1)S(1)}, u32[]{:S(2)}, u32[]{:S(2)}) collective-permute-start(bf16[2,768,256]{2,1,0:T(8,128)(2,1)S(1)} %pad_maximum_fusion.3.refs_2_), channel_id=1, source_target_pairs={{0,4},{1,3},{2,6},{3,1},{4,0},{5,7},{6,2},{7,5},{8,12},{9,11},{10,... | collective-permute-start | bytes 2359304 | tf_op jit(solution)/shard_map/ppermute | solution.py:434
  63.2 23.7 %collective-permute-start.19 = (bf16[2,768,256]{2,1,0:T(8,128)(2,1)S(1)}, bf16[2,768,256]{2,1,0:T(8,128)(2,1)}, u32[]{:S(2)}, u32[]{:S(2)}) collective-permute-start(bf16[2,768,256]{2,1,0:T(8,128)(2,1)S(1)} %pad_maximum_fusion.1.refs_0_), channel_id=1, source_target_pairs={{0,4},{1,3},{2,6},{3,1},{4,0},{5,7},{6,2},{7,5},{8,12},{9,11},{10,... | collective-permute-start | bytes 2359304 | tf_op jit(solution)/shard_map/ppermute | solution.py:434
  67.9 18.9 %collective-permute-start.5 = (bf16[768,256]{1,0:T(8,128)(2,1)S(1)}, bf16[768,256]{1,0:T(8,128)(2,1)S(1)}, u32[]{:S(2)}, u32[]{:S(2)}) collective-permute-start(bf16[768,256]{1,0:T(8,128)(2,1)S(1)} %get-tuple-element.64), channel_id=1, source_target_pairs={{0,2},{1,5},{2,0},{3,7},{4,6},{5,1},{6,4},{7,3},{8,10},{9,13},{10,... | collective-permute-start | bytes 1179656 | tf_op jit(solution)/shard_map/ppermute | solution.py:434
  82.3 5.9 %collective-permute-start.22 = (bf16[2,768,256]{2,1,0:T(8,128)(2,1)S(1)}, bf16[2,768,256]{2,1,0:T(8,128)(2,1)}, u32[]{:S(2)}, u32[]{:S(2)}) collective-permute-start(bf16[2,768,256]{2,1,0:T(8,128)(2,1)S(1)} %collective-permute-done.21.refs_2_), channel_id=1, source_target_pairs={{0,1},{1,0},{2,3},{3,2},{4,5},{5,4},{6,7},{7,6},{8,9},{9,8},{10,11... | collective-permute-start | bytes 2359304 | tf_op jit(solution)/shard_map/ppermute | solution.py:434
  86.8 2.6 %collective-permute-start.20 = (bf16[2,768,256]{2,1,0:T(8,128)(2,1)}, bf16[2,768,256]{2,1,0:T(8,128)(2,1)}, u32[]{:S(2)}, u32[]{:S(2)}) collective-permute-start(bf16[2,768,256]{2,1,0:T(8,128)(2,1)} %collective-permute-done.19.refs_0_), channel_id=1, source_target_pairs={{0,1},{1,0},{2,3},{3,2},{4,5},{5,4},{6,7},{7,6},{8,9},{9,8},{10,11... | collective-permute-start | bytes 2359304 | tf_op jit(solution)/shard_map/ppermute | solution.py:434
  86.9 14.2 %copy-start.7 = (bf16[2,768,256]{2,1,0:T(8,128)(2,1)}, bf16[2,768,256]{2,1,0:T(8,128)(2,1)S(1)}, u32[]{:S(2)}) copy-start(bf16[2,768,256]{2,1,0:T(8,128)(2,1)S(1)} %pad_maximum_fusion.refs_0_) | copy-start | bytes 2359300
  86.9 14.2 %collective-permute-start.13 = (bf16[2,768,256]{2,1,0:T(8,128)(2,1)S(1)}, bf16[2,768,256]{2,1,0:T(8,128)(2,1)S(1)}, u32[]{:S(2)}, u32[]{:S(2)}) collective-permute-start(bf16[2,768,256]{2,1,0:T(8,128)(2,1)S(1)} %pad_maximum_fusion.refs_0_), channel_id=1, source_target_pairs={{0,4},{1,3},{2,6},{3,1},{4,0},{5,7},{6,2},{7,5},{8,12},{9,11},{10,... | collective-permute-start | bytes 2359304 | tf_op jit(solution)/shard_map/ppermute | solution.py:434
  101.2 7.4 %copy-start.21 = (bf16[2,768,256]{2,1,0:T(8,128)(2,1)}, bf16[2,768,256]{2,1,0:T(8,128)(2,1)S(1)}, u32[]{:S(2)}) copy-start(bf16[2,768,256]{2,1,0:T(8,128)(2,1)S(1)} %collective-permute-done.13.refs_0_) | copy-start | bytes 2359300
  101.2 8.0 %copy-start.6 = (bf16[2,768,256]{2,1,0:T(8,128)(2,1)S(1)}, bf16[2,768,256]{2,1,0:T(8,128)(2,1)}, u32[]{:S(2)}) copy-start(bf16[2,768,256]{2,1,0:T(8,128)(2,1)} %pad_maximum_fusion.2.refs_2_) | copy-start | bytes 2359300
  101.2 9.4 %copy-start.8 = (bf16[2,768,256]{2,1,0:T(8,128)(2,1)S(1)}, bf16[2,768,256]{2,1,0:T(8,128)(2,1)}, u32[]{:S(2)}) copy-start(bf16[2,768,256]{2,1,0:T(8,128)(2,1)} %copy-done.7) | copy-start | bytes 2359300
  108.6 19.8 %collective-permute-start.24 = (bf16[4,256,768]{2,1,0:T(8,128)(2,1)S(1)}, bf16[4,256,768]{2,1,0:T(8,128)(2,1)S(1)}, u32[]{:S(2)}, u32[]{:S(2)}) collective-permute-start(bf16[4,256,768]{2,1,0:T(8,128)(2,1)S(1)} %get-tuple-element.97), channel_id=1, source_target_pairs={{0,1},{1,0},{2,3},{3,2},{4,5},{5,4},{6,7},{7,6},{8,9},{9,8},{10,11... | collective-permute-start | bytes 4718600 | tf_op jit(solution)/shard_map/ppermute | solution.py:434
  108.8 20.4 %collective-permute-start.23 = (bf16[4,256,768]{2,1,0:T(8,128)(2,1)S(1)}, bf16[4,256,768]{2,1,0:T(8,128)(2,1)S(1)}, u32[]{:S(2)}, u32[]{:S(2)}) collective-permute-start(bf16[4,256,768]{2,1,0:T(8,128)(2,1)S(1)} %get-tuple-element.95), channel_id=1, source_target_pairs={{0,1},{1,0},{2,3},{3,2},{4,5},{5,4},{6,7},{7,6},{8,9},{9,8},{10,11... | collective-permute-start | bytes 4718600 | tf_op jit(solution)/shard_map/ppermute | solution.py:434
  109.2 12.0 %collective-permute-start.15 = (bf16[2,768,256]{2,1,0:T(8,128)(2,1)S(1)}, bf16[2,768,256]{2,1,0:T(8,128)(2,1)S(1)}, u32[]{:S(2)}, u32[]{:S(2)}) collective-permute-start(bf16[2,768,256]{2,1,0:T(8,128)(2,1)S(1)} %copy-done.6), channel_id=1, source_target_pairs={{0,4},{1,3},{2,6},{3,1},{4,0},{5,7},{6,2},{7,5},{8,12},{9,11},{10,... | collective-permute-start | bytes 2359304 | tf_op jit(solution)/shard_map/ppermute | solution.py:434
  110.2 20.3 %collective-permute-start.18 = (bf16[2,768,256]{2,1,0:T(8,128)(2,1)S(1)}, bf16[2,768,256]{2,1,0:T(8,128)(2,1)S(1)}, u32[]{:S(2)}, u32[]{:S(2)}) collective-permute-start(bf16[2,768,256]{2,1,0:T(8,128)(2,1)S(1)} %copy-done.6), channel_id=1, source_target_pairs={{0,1},{1,0},{2,3},{3,2},{4,5},{5,4},{6,7},{7,6},{8,9},{9,8},{10,11... | collective-permute-start | bytes 2359304 | tf_op jit(solution)/shard_map/ppermute | solution.py:434
  110.5 21.0 %collective-permute-start.17 = (bf16[2,768,256]{2,1,0:T(8,128)(2,1)S(1)}, bf16[2,768,256]{2,1,0:T(8,128)(2,1)S(1)}, u32[]{:S(2)}, u32[]{:S(2)}) collective-permute-start(bf16[2,768,256]{2,1,0:T(8,128)(2,1)S(1)} %copy-done.8), channel_id=1, source_target_pairs={{0,1},{1,0},{2,3},{3,2},{4,5},{5,4},{6,7},{7,6},{8,9},{9,8},{10,11... | collective-permute-start | bytes 2359304 | tf_op jit(solution)/shard_map/ppermute | solution.py:434
  110.8 17.6 %copy-start.22 = (bf16[2,768,256]{2,1,0:T(8,128)(2,1)S(1)}, bf16[2,768,256]{2,1,0:T(8,128)(2,1)}, u32[]{:S(2)}) copy-start(bf16[2,768,256]{2,1,0:T(8,128)(2,1)} %copy-done.21) | copy-start | bytes 2359300
  121.2 19.0 %collective-permute-start.16 = (bf16[2,768,256]{2,1,0:T(8,128)(2,1)S(1)}, bf16[2,768,256]{2,1,0:T(8,128)(2,1)S(1)}, u32[]{:S(2)}, u32[]{:S(2)}) collective-permute-start(bf16[2,768,256]{2,1,0:T(8,128)(2,1)S(1)} %collective-permute-done.15.refs_2_), channel_id=1, source_target_pairs={{0,1},{1,0},{2,3},{3,2},{4,5},{5,4},{6,7},{7,6},{8,9},{9,8},{10,11... | collective-permute-start | bytes 2359304 | tf_op jit(solution)/shard_map/ppermute | solution.py:434
  128.4 21.0 %copy-start.2 = (bf16[4,256,768]{2,1,0:T(8,128)(2,1)}, bf16[4,256,768]{2,1,0:T(8,128)(2,1)S(1)}, u32[]{:S(2)}) copy-start(bf16[4,256,768]{2,1,0:T(8,128)(2,1)S(1)} %get-tuple-element.96.refs_0_) | copy-start | bytes 4718596
  128.4 23.6 %copy-start = (bf16[4,256,768]{2,1,0:T(8,128)(2,1)}, bf16[4,256,768]{2,1,0:T(8,128)(2,1)S(1)}, u32[]{:S(2)}) copy-start(bf16[4,256,768]{2,1,0:T(8,128)(2,1)S(1)} %get-tuple-element.94.refs_0_) | copy-start | bytes 4718596
  128.4 11.8 %collective-permute-start.14 = (bf16[2,768,256]{2,1,0:T(8,128)(2,1)S(1)}, bf16[2,768,256]{2,1,0:T(8,128)(2,1)S(1)}, u32[]{:S(2)}, u32[]{:S(2)}) collective-permute-start(bf16[2,768,256]{2,1,0:T(8,128)(2,1)S(1)} %copy-done.22), channel_id=1, source_target_pairs={{0,1},{1,0},{2,3},{3,2},{4,5},{5,4},{6,7},{7,6},{8,9},{9,8},{10,11... | collective-permute-start | bytes 2359304 | tf_op jit(solution)/shard_map/ppermute | solution.py:434
  129.2 2.4 copy-start.31
  129.2 20.2 %collective-permute-start.26 = (bf16[2,256,768]{2,1,0:T(8,128)(2,1)S(1)}, bf16[2,256,768]{2,1,0:T(8,128)(2,1)S(1)}, u32[]{:S(2)}, u32[]{:S(2)}) collective-permute-start(bf16[2,256,768]{2,1,0:T(8,128)(2,1)S(1)} %add_convert_fusion.2), channel_id=1, source_target_pairs={{0,4},{1,3},{2,6},{3,1},{4,0},{5,7},{6,2},{7,5},{8,12},{9,11},{10,... | collective-permute-start | bytes 2359304 | tf_op jit(solution)/shard_map/ppermute | solution.py:434
  130.5 21.4 %collective-permute-start.25 = (bf16[2,256,768]{2,1,0:T(8,128)(2,1)S(1)}, bf16[2,256,768]{2,1,0:T(8,128)(2,1)S(1)}, u32[]{:S(2)}, u32[]{:S(2)}) collective-permute-start(bf16[2,256,768]{2,1,0:T(8,128)(2,1)S(1)} %add_convert_fusion.3), channel_id=1, source_target_pairs={{0,4},{1,3},{2,6},{3,1},{4,0},{5,7},{6,2},{7,5},{8,12},{9,11},{10,... | collective-permute-start | bytes 2359304 | tf_op jit(solution)/shard_map/ppermute | solution.py:434
  149.3 3.7 %copy-start.9 = (bf16[2,256,576]{2,1,0:T(8,128)(2,1)}, bf16[2,256,576]{2,1,0:T(8,128)(2,1)S(1)}, u32[]{:S(2)}) copy-start(bf16[2,256,576]{2,1,0:T(8,128)(2,1)S(1)} %shard_map.121.hidden_ref) | copy-start | bytes 1769476
  149.4 3.6 %copy-start.13 = (bf16[2,256,768]{2,1,0:T(8,128)(2,1)}, bf16[2,256,768]{2,1,0:T(8,128)(2,1)S(1)}, u32[]{:S(2)}) copy-start(bf16[2,256,768]{2,1,0:T(8,128)(2,1)S(1)} %collective-permute-done.26.refs_2_) | copy-start | bytes 2359300
  150.5 17.2 %collective-permute-start.28 = (bf16[256,768]{1,0:T(8,128)(2,1)}, bf16[256,768]{1,0:T(8,128)(2,1)}, u32[]{:S(2)}, u32[]{:S(2)}) collective-permute-start(bf16[256,768]{1,0:T(8,128)(2,1)} %fusion.1), channel_id=1, source_target_pairs={{0,2},{1,5},{2,0},{3,7},{4,6},{5,1},{6,4},{7,3},{8,10},{9,13},{10,... | collective-permute-start | bytes 1179656 | tf_op jit(solution)/shard_map/ppermute | solution.py:434
  153.0 16.3 %collective-permute-start.27 = (bf16[256,768]{1,0:T(8,128)(2,1)}, bf16[256,768]{1,0:T(8,128)(2,1)S(1)}, u32[]{:S(2)}, u32[]{:S(2)}) collective-permute-start(bf16[256,768]{1,0:T(8,128)(2,1)} %fusion), channel_id=1, source_target_pairs={{0,2},{1,5},{2,0},{3,7},{4,6},{5,1},{6,4},{7,3},{8,10},{9,13},{10,... | collective-permute-start | bytes 1179656 | tf_op jit(solution)/shard_map/ppermute | solution.py:434
  154.8 12.9 %copy-start.3 = (bf16[4,256,768]{2,1,0:T(8,128)(2,1)S(1)}, bf16[4,256,768]{2,1,0:T(8,128)(2,1)}, u32[]{:S(2)}) copy-start(bf16[4,256,768]{2,1,0:T(8,128)(2,1)} %copy-done.2) | copy-start | bytes 4718596
  154.8 12.9 %copy-start.14 = (bf16[2,256,768]{2,1,0:T(8,128)(2,1)S(1)}, bf16[2,256,768]{2,1,0:T(8,128)(2,1)}, u32[]{:S(2)}) copy-start(bf16[2,256,768]{2,1,0:T(8,128)(2,1)} %copy-done.13) | copy-start | bytes 2359300
  154.8 13.0 %copy-start.38 = (bf16[256,256]{1,0:T(8,128)(2,1)S(1)}, bf16[256,256]{1,0:T(8,128)(2,1)}, u32[]{:S(2)}) copy-start(bf16[256,256]{1,0:T(8,128)(2,1)} %copy-done.37) | copy-start | bytes 393220
  167.7 1.7 copy-start.12
  167.8 1.7 copy-start.36
  169.9 3.5 %collective-permute-start.30 = (bf16[4,256,768]{2,1,0:T(8,128)(2,1)S(1)}, bf16[4,256,768]{2,1,0:T(8,128)(2,1)S(1)}, u32[]{:S(2)}, u32[]{:S(2)}) collective-permute-start(bf16[4,256,768]{2,1,0:T(8,128)(2,1)S(1)} %get-tuple-element.115), channel_id=1, source_target_pairs={{0,1},{1,0},{2,3},{3,2},{4,5},{5,4},{6,7},{7,6},{8,9},{9,8},{10,11... | collective-permute-start | bytes 4718600 | tf_op jit(solution)/shard_map/ppermute | solution.py:434
  170.0 5.6 %collective-permute-start.29 = (bf16[4,256,768]{2,1,0:T(8,128)(2,1)S(1)}, bf16[4,256,768]{2,1,0:T(8,128)(2,1)S(1)}, u32[]{:S(2)}, u32[]{:S(2)}) collective-permute-start(bf16[4,256,768]{2,1,0:T(8,128)(2,1)S(1)} %get-tuple-element.113), channel_id=1, source_target_pairs={{0,1},{1,0},{2,3},{3,2},{4,5},{5,4},{6,7},{7,6},{8,9},{9,8},{10,11... | collective-permute-start | bytes 4718600 | tf_op jit(solution)/shard_map/ppermute | solution.py:434
  173.6 12.1 %collective-permute-start.31 = (bf16[2,256,768]{2,1,0:T(8,128)(2,1)S(1)}, bf16[2,256,768]{2,1,0:T(8,128)(2,1)S(1)}, u32[]{:S(2)}, u32[]{:S(2)}) collective-permute-start(bf16[2,256,768]{2,1,0:T(8,128)(2,1)S(1)} %add_convert_fusion), channel_id=1, source_target_pairs={{0,4},{1,3},{2,6},{3,1},{4,0},{5,7},{6,2},{7,5},{8,12},{9,11},{10,... | collective-permute-start | bytes 2359304 | tf_op jit(solution)/shard_map/ppermute | solution.py:434
  175.8 31.8 %copy-start.40 = (bf16[256,256]{1,0:T(8,128)(2,1)S(1)}, bf16[256,256]{1,0:T(8,128)(2,1)}, u32[]{:S(2)}) copy-start(bf16[256,256]{1,0:T(8,128)(2,1)} %copy-done.39) | copy-start | bytes 393220
  185.6 16.0 %collective-permute-start.32 = (bf16[2,256,768]{2,1,0:T(8,128)(2,1)S(1)}, bf16[2,256,768]{2,1,0:T(8,128)(2,1)S(1)}, u32[]{:S(2)}, u32[]{:S(2)}) collective-permute-start(bf16[2,256,768]{2,1,0:T(8,128)(2,1)S(1)} %add_convert_fusion.1), channel_id=1, source_target_pairs={{0,4},{1,3},{2,6},{3,1},{4,0},{5,7},{6,2},{7,5},{8,12},{9,11},{10,... | collective-permute-start | bytes 2359304 | tf_op jit(solution)/shard_map/ppermute | solution.py:434
  186.8 20.8 %collective-permute-start.37 = (bf16[256,768]{1,0:T(8,128)(2,1)S(1)}, bf16[256,768]{1,0:T(8,128)(2,1)S(1)}, u32[]{:S(2)}, u32[]{:S(2)}) collective-permute-start(bf16[256,768]{1,0:T(8,128)(2,1)S(1)} %fusion.3), channel_id=1, source_target_pairs={{0,2},{1,5},{2,0},{3,7},{4,6},{5,1},{6,4},{7,3},{8,10},{9,13},{10,... | collective-permute-start | bytes 1179656 | tf_op jit(solution)/shard_map/ppermute | solution.py:434
  201.8 7.8 %collective-permute-start.33 = (bf16[256,768]{1,0:T(8,128)(2,1)S(1)}, bf16[256,768]{1,0:T(8,128)(2,1)S(1)}, u32[]{:S(2)}, u32[]{:S(2)}) collective-permute-start(bf16[256,768]{1,0:T(8,128)(2,1)S(1)} %fusion.2), channel_id=1, source_target_pairs={{0,2},{1,5},{2,0},{3,7},{4,6},{5,1},{6,4},{7,3},{8,10},{9,13},{10,... | collective-permute-start | bytes 1179656 | tf_op jit(solution)/shard_map/ppermute | solution.py:434
  202.3 11.9 %collective-permute-start.35 = (bf16[256,768]{1,0:T(8,128)(2,1)S(1)}, bf16[256,768]{1,0:T(8,128)(2,1)S(1)}, u32[]{:S(2)}, u32[]{:S(2)}) collective-permute-start(bf16[256,768]{1,0:T(8,128)(2,1)S(1)} %shard_map.124), channel_id=1, source_target_pairs={{8,16},{16,8},{9,17},{17,9},{10,18},{18,10},{11,19},{19,11},{12,20... | collective-permute-start | bytes 1179656 | tf_op jit(solution)/shard_map/ppermute | solution.py:604
  203.0 14.0 %collective-permute-start.36 = (bf16[256,768]{1,0:T(8,128)(2,1)S(1)}, bf16[256,768]{1,0:T(8,128)(2,1)S(1)}, u32[]{:S(2)}, u32[]{:S(2)}) collective-permute-start(bf16[256,768]{1,0:T(8,128)(2,1)S(1)} %shard_map.124), channel_id=1, source_target_pairs={{0,16},{24,8},{1,17},{25,9},{2,18},{26,10},{3,19},{27,11},{4,20},{... | collective-permute-start | bytes 1179656 | tf_op jit(solution)/shard_map/ppermute | solution.py:605
  207.5 18.0 %collective-permute-start.34 = (bf16[256,768]{1,0:T(8,128)(2,1)S(1)}, bf16[256,768]{1,0:T(8,128)(2,1)S(1)}, u32[]{:S(2)}, u32[]{:S(2)}) collective-permute-start(bf16[256,768]{1,0:T(8,128)(2,1)S(1)} %shard_map.123), channel_id=1, source_target_pairs={{0,8},{8,0},{16,24},{24,16},{1,9},{9,1},{17,25},{25,17},{2,10},{10... | collective-permute-start | bytes 1179656 | tf_op jit(solution)/shard_map/ppermute | solution.py:434
  207.6 6.1 %copy-start.34 = (bf16[256,256]{1,0:T(8,128)(2,1)S(1)}, bf16[256,256]{1,0:T(8,128)(2,1)}, u32[]{:S(2)}) copy-start(bf16[256,256]{1,0:T(8,128)(2,1)} %copy-done.33) | copy-start | bytes 393220
  208.1 31.1 %collective-permute-start.38 = (bf16[256,768]{1,0:T(8,128)(2,1)S(1)}, bf16[256,768]{1,0:T(8,128)(2,1)S(1)}, u32[]{:S(2)}, u32[]{:S(2)}) collective-permute-start(bf16[256,768]{1,0:T(8,128)(2,1)S(1)} %shard_map.126), channel_id=1, source_target_pairs={{8,24},{16,0},{9,25},{17,1},{10,26},{18,2},{11,27},{19,3},{12,28},... | collective-permute-start | bytes 1179656 | tf_op jit(solution)/shard_map/ppermute | solution.py:606
  209.6 29.6 %collective-permute-start.39 = (bf16[256,768]{1,0:T(8,128)(2,1)S(1)}, bf16[256,768]{1,0:T(8,128)(2,1)S(1)}, u32[]{:S(2)}, u32[]{:S(2)}) collective-permute-start(bf16[256,768]{1,0:T(8,128)(2,1)S(1)} %shard_map.126), channel_id=1, source_target_pairs={{0,24},{24,0},{1,25},{25,1},{2,26},{26,2},{3,27},{27,3},{4,28},{28... | collective-permute-start | bytes 1179656 | tf_op jit(solution)/shard_map/ppermute | solution.py:607
  213.8 25.5 %copy-start.5 = (bf16[272,768]{1,0:T(8,128)(2,1)S(1)}, bf16[272,768]{1,0:T(8,128)(2,1)}, u32[]{:S(2)}) copy-start(bf16[272,768]{1,0:T(8,128)(2,1)} %copy-done.4) | copy-start | bytes 1253380
  (19 other events, 18.0 us)

commit v10 on v9

--- a/solution.py
+++ b/solution.py
@@ -375,35 +375,31 @@
     )
 
 
-def down_kernel(blocks, sections, plan_ref, hidden_ref, down_ref, *out_refs):
-    experts, slots, _ = hidden_ref.shape
-    part = slots // sections
+def down_kernel(blocks, low, part, plan_ref, hidden_ref, down_ref, *out_refs):
     turn = pl.program_id(0) // blocks
-    for j in range(experts):
-        share = jnp.dot(hidden_ref[j], down_ref[j], preferred_element_type=F32).astype(BF16)
-        for i in range(len(out_refs) // sections):
+    for j in range(hidden_ref.shape[0]):
+        mine = hidden_ref[j, low : low + part, :]
+        share = jnp.dot(mine, down_ref[j], preferred_element_type=F32).astype(BF16)
+        for i, out_ref in enumerate(out_refs):
 
             @pl.when(turn == i)
             def _():
-                for section in range(sections):
-                    out_ref = out_refs[i * sections + section]
-                    out_ref[0, j * part : (j + 1) * part, :] = share[
-                        section * part : (section + 1) * part
-                    ]
-
-
-def down_part(plans, hidden, down_weight, width, sections):
+                out_ref[0, j * part : (j + 1) * part, :] = share
+
+
+def down_part(plans, hidden, down_weight, width, sections, section):
     blocks = plans[0].shape[0]
     experts, slots, units = hidden.shape
-    rows = experts * slots // sections
+    part = slots // sections
 
     def out_spec(i):
         return pl.BlockSpec(
-            (1, rows, width), lambda p, plan: (jnp.clip(p - i * blocks, 0, blocks - 1), 0, 0)
+            (1, experts * part, width),
+            lambda p, plan: (jnp.clip(p - i * blocks, 0, blocks - 1), 0, 0),
         )
 
-    out = pl.pallas_call(
-        functools.partial(down_kernel, blocks, sections),
+    return pl.pallas_call(
+        functools.partial(down_kernel, blocks, section * part, part),
         grid_spec=pltpu.PrefetchScalarGridSpec(
             num_scalar_prefetch=1,
             grid=(len(plans) * blocks,),
@@ -411,17 +407,16 @@
                 pl.BlockSpec(memory_space=pltpu.VMEM),
                 pl.BlockSpec((experts, units, width), lambda p, plan: (0, 0, plan[p])),
             ],
-            out_specs=[out_spec(i) for i in range(len(plans)) for _ in range(sections)],
-        ),
-        out_shape=[jax.ShapeDtypeStruct((blocks, rows, width), BF16)] * (len(plans) * sections),
+            out_specs=[out_spec(i) for i in range(len(plans))],
+        ),
+        out_shape=[jax.ShapeDtypeStruct((blocks, experts * part, width), BF16)] * len(plans),
         cost_estimate=pl.CostEstimate(
-            flops=2 * experts * slots * len(plans) * blocks * width * units,
+            flops=2 * experts * part * len(plans) * blocks * width * units,
             bytes_accessed=2 * experts * len(plans) * blocks * width * units,
             transcendentals=0,
         ),
         compiler_params=pltpu.CompilerParams(vmem_limit_bytes=VMEM_LIMIT),
     )(jnp.concatenate(plans), hidden, in_hbm(down_weight))
-    return [out[i * sections : (i + 1) * sections] for i in range(len(plans))]
 
 
 def added(left, right):
@@ -511,8 +506,9 @@
             gathered = [lax.all_gather(slots, "exp", axis=0) for slots, _ in chosen]
             sums = gate_part(order[:middle], [[x[:middle]] for x in gathered], *weights)
             hidden = gate_part(order[middle:], [[x[middle:]] for x in gathered], *weights, sums)
-            (partial,) = down_part([order], hidden, down_weight, width, len(chunk))
-            for offset, share, (_, place) in zip(chunk, partial, chosen):
+            for i, offset in enumerate(chunk):
+                place = chosen[i][1]
+                (share,) = down_part([order], hidden, down_weight, width, len(chunk), i)
                 share = lax.psum_scatter(share, "exp", scatter_dimension=0)
                 piece = combine_slots(place, [share[None]])
                 pieces.append(swapped(piece, "seq", offset, offset) if offset else piece)
@@ -539,72 +535,91 @@
         near[name] = plane.across(two[name])
         far_two[name] = plane.second(two[name])
 
-    neighbour = swapped(stream, "seq", 1, 1)
-    third = across_middle(stream)
+    swap = swapped(stream, "seq", 1, 1)
+    crossed = across_middle(stream)
     chosen["own"] = select(stream)
-    gather("own", [neighbour, third])
-    passed_third = outward(third)
-    fourth = across_middle(neighbour)
-    chosen["neighbour"] = select(neighbour)
-    gather("neighbour", [passed_third, fourth, two["own"]])
-    passed_fourth = outward(fourth)
-    chosen["third"] = select(third, passed_third)
-    gather("third", passed_fourth)
-    chosen["fourth"] = select(fourth, passed_fourth)
-
-    pieces = {}
-    sent, finish = [], None
-    for chunk, after in ((("neighbour", "third"), "fourth"), (("fourth", "own"), None)):
+    gather("own", [swap, crossed])
+    passed = outward(crossed)
+    crossed_swap = across_middle(swap)
+    chosen["neighbour"] = select(swap)
+    gather("neighbour", [passed, crossed_swap, two["own"]])
+    passed_fourth = outward(crossed_swap)
+    chosen["third"] = select(crossed, passed)
+    gather("third", [passed_fourth, far_two["neighbour"]])
+    chosen["fourth"] = select(crossed_swap, passed_fourth)
+
+    def gate(chunk, behind):
         early = [[two[name], near[name]] for name in chunk]
-        if after:
-            early, _ = tie((early, chosen[after]))
-        early, _ = tie((early, sent))
-        sums = gate_part(plane.early, early, *weights)
-        if after:
-            gather(after, sums)
-            for name in chunk:
-                far_two[name], _ = tie((far_two[name], sums))
-        late = [[far_two[name], plane.across(far_two[name])] for name in chunk]
-        if after:
-            late, _ = tie((late, two[after]))
-        hidden = gate_part(plane.late, late, *weights, sums)
-        if after:
-            hidden, _ = tie((hidden, far_two[after]))
-            (theirs,) = down_part([plane.theirs], hidden, down_weight, width, len(chunk))
-            hidden, theirs = tie((hidden, theirs))
-            (mine,) = down_part([plane.mine], hidden, down_weight, width, len(chunk))
-        else:
-            one = finish(hidden)
-            hidden, _ = tie((hidden, one))
-            theirs, mine = down_part([plane.theirs, plane.mine], hidden, down_weight, width, len(chunk))
-            theirs, _ = tie((theirs, list(pieces.values())))
-        near_share = [plane.across(part) for part in theirs]
-        sent = [added(kept[2:], got[2:]) for kept, got in zip(mine, near_share)]
-        got_two = [plane.second(sent[0])]
-        part = sent[1] if after else tie((sent[1], got_two))[0]
-        got_two.append(plane.second(part))
-
-        def finish(behind, chunk=chunk, mine=mine, near_share=near_share, got_two=got_two):
-            got_two = [tie((far, behind))[0] for far in got_two]
-            one = [
-                added(added(kept[1], got[1]), far[1])
-                for kept, got, far in zip(mine, near_share, got_two)
-            ]
-            for k, name in enumerate(chunk):
-                got_one = plane.once(one[k])[None]
-                pieces[name] = combine_slots(
-                    chosen[name][1], [mine[k], near_share[k], got_two[k], got_one]
-                )
-            return one
-
-    finish([])
+        return gate_part(plane.early, tie((early, behind))[0], *weights)
+
+    def gate_last(chunk, sums, behind):
+        late = [[far_two[name], near_far[name]] for name in chunk]
+        (late, sums), _ = tie(((late, sums), behind))
+        return gate_part(plane.late, late, *weights, sums)
+
+    def down(hidden, section, behind):
+        hidden, _ = tie((hidden, behind))
+        plans = [plane.theirs, plane.mine]
+        return down_part(plans, hidden, down_weight, width, 2, section)
+
+    class Scatter:
+        def __init__(self, name, shares):
+            self.name = name
+            self.theirs, self.mine = shares
+
+        def two_blocks(self, behind):
+            self.near = plane.across(self.theirs)
+            self.sent = added(self.mine[2:], self.near[2:])
+            self.got_two = plane.second(tie((self.sent, behind))[0])
+
+        def one_block(self, behind):
+            got_two, _ = tie((self.got_two, behind))
+            self.one = added(added(self.mine[1], self.near[1]), got_two[1])
+            self.got_one = plane.once(self.one)
+
+        def own_block(self, behind):
+            got_one, _ = tie((self.got_one, behind))
+            shares = [self.mine, self.near, self.got_two, got_one[None]]
+            return combine_slots(chosen[self.name][1], shares)
+
+    chunk = ("third", "neighbour")
+    sums = gate(chunk, chosen["fourth"])
+    gather("fourth", sums)
+    for name in chunk:
+        near_far[name] = plane.across(tie((far_two[name], sums))[0])
+    hidden = gate_last(chunk, sums, two["fourth"])
+    third = Scatter("third", down(hidden, 0, far_two["fourth"]))
+    neighbour = Scatter("neighbour", down(hidden, 1, [third.theirs, far_two["own"]]))
+    third.two_blocks([])
+
+    chunk = ("fourth", "own")
+    sums = gate(chunk, third.sent)
+    for name in chunk:
+        near_far[name] = plane.across(tie((far_two[name], third.sent))[0])
+    third.one_block(sums)
+    neighbour.two_blocks(third.one)
+    hidden = gate_last(chunk, sums, [third.one, neighbour.sent])
+    third_piece = third.own_block(hidden)
+    neighbour.one_block(hidden)
+    fourth = Scatter("fourth", down(hidden, 0, third_piece))
+    third_home = lax.ppermute(third_piece, "seq", [(1, 2), (2, 1)])
+    own = Scatter("own", down(hidden, 1, [fourth.theirs, neighbour.one, third_home]))
+    third_piece, _ = tie((third_piece, third_home))
+    third_far_home = lax.ppermute(third_piece, "seq", [(0, 2), (3, 1)])
+    neighbour_piece = neighbour.own_block([])
+    own.theirs, _ = tie((own.theirs, [third_far_home, neighbour_piece]))
+    fourth.two_blocks([])
+    fourth.one_block([])
+    own.two_blocks(fourth.got_two)
+    own.one_block([])
+    fourth_piece = fourth.own_block([])
     return [
-        pieces["own"],
-        swapped(pieces["neighbour"], "seq", 1, 1),
-        lax.ppermute(pieces["third"], "seq", [(1, 2), (2, 1)]),
-        lax.ppermute(pieces["third"], "seq", [(0, 2), (3, 1)]),
-        lax.ppermute(pieces["fourth"], "seq", [(1, 3), (2, 0)]),
-        lax.ppermute(pieces["fourth"], "seq", [(0, 3), (3, 0)]),
+        own.own_block([]),
+        swapped(neighbour_piece, "seq", 1, 1),
+        third_home,
+        third_far_home,
+        lax.ppermute(fourth_piece, "seq", [(1, 3), (2, 0)]),
+        lax.ppermute(fourth_piece, "seq", [(0, 3), (3, 0)]),
     ]
 
 

time: 241 us -> 238 us (0.988)
  Pallas kernels: 75.3 us -> 90.7 us
  waiting for transfers between devices: 92.2 us -> 84.6 us
  local copies, waits for them, and re-layouts: 16.5 us -> 11.1 us
  other arithmetic: 5.98 us -> 3.14 us
  starting transfers between devices: 49.5 us -> 46.9 us
    ppermute x4, waiting for transfers between devices: 16.6 us -> 0.01 us  [the longest x1 0.01 us: paired_chunks(): third_home = lax.ppermute(third_piece, 'seq', [(1, 2), (2, 1)])]
    pallas_call x3 -> x4, Pallas kernels: 27.5 us -> 43.2 us  [down_part(): pl.pallas_call(functools.partial(down_kernel, blocks, section * part, par...]
    ppermute x30, waiting for transfers between devices: 63.3 us -> 71.2 us  [swapped(): return lax.ppermute(array, axis, pairs)]
    unnamed x86 -> x36, local copies, waits for them, and re-layouts: 15.5 us -> 10.1 us
  transfers between devices with their start and end apart: 40 -> 40, of which waited for: 16 -> 18; matrix products, arithmetic and copies ran while one was open for 2% -> 1% of each run, Pallas kernels for 27% -> 37%
where the time goes in v10:
time: 238 us; the launch traced here: 237 us
  Pallas kernels  90.7 us (38%)
  waiting for transfers between devices  84.6 us (36%)
  starting transfers between devices  46.9 us (20%)
  local copies, waits for them, and re-layouts  11.1 us (5%)
  other arithmetic  3.14 us (1%)
    ppermute x30, waiting for transfers between devices, swapped(): return lax.ppermute(array, axis, pairs)  71.2 us
    pallas_call x4, Pallas kernels, down_part(): pl.pallas_call(functools.partial(down_kernel, blocks, section * part, par...  43.2 us
    pallas_call x4, Pallas kernels, gate_part(): pl.pallas_call(functools.partial(gate_kernel, counts, len(xs), last), gri...  36.9 us
    ppermute x30, starting transfers between devices, swapped(): return lax.ppermute(array, axis, pairs)  23.3 us
    unnamed x36, local copies, waits for them, and re-layouts  10.1 us
    ppermute x2, starting transfers between devices, shifted(): return lax.ppermute(array, axis, pairs)  9.43 us
    ppermute x2, waiting for transfers between devices, outward(): return lax.ppermute(part, 'seq', [(1, 0), (2, 3)])  9.41 us
  transfers between devices with their start and end apart: 40, of which 18 were waited for; matrix products, arithmetic and copies ran while one was open for 1% of the time, Pallas kernels for 37%

profile of v10, /device:TPU:0, one launch (start us, length us, event | category | flops | bytes accessed | tf_op | source)
XLA Modules:
  0.0 237.0 jit_solution(5982721661730823372)
XLA Ops:
  0.0 2.1 shard_map.109
  2.2 4.9 %collective-permute-start = (bf16[784,128]{1,0:T(8,128)(2,1)S(1)}, bf16[784,128]{1,0:T(8,128)(2,1)S(1)}, u32[]{:S(2)}, u32[]{:S(2)}) collective-permute-start(bf16[784,128]{1,0:T(8,128)(2,1)S(1)} %get-tuple-element.71), channel_id=1, source_target_pairs={{0,8},{8,16},{16,24},{1,9},{9,17},{17,25},{2,10},{10,18},{18,26},{... | collective-permute-start | bytes 602120 | tf_op jit(solution)/shard_map/ppermute | solution.py:30
  7.1 0.7 reshape.57.gain_ref
  7.8 1.0 copy-done
  8.8 1.0 copy-done.2
  9.8 1.0 copy-done.3
  10.8 0.7 copy-done.16
  11.5 1.4 shard_map.110.intra_ref
  13.2 4.5 %collective-permute-start.1 = (bf16[784,128]{1,0:T(8,128)(2,1)S(1)}, bf16[784,128]{1,0:T(8,128)(2,1)S(1)}, u32[]{:S(2)}, u32[]{:S(2)}) collective-permute-start(bf16[784,128]{1,0:T(8,128)(2,1)S(1)} %concatenate.13), channel_id=1, source_target_pairs={{0,16},{8,24},{1,17},{9,25},{2,18},{10,26},{3,19},{11,27},{4,20},{... | collective-permute-start | bytes 602120 | tf_op jit(solution)/shard_map/ppermute | solution.py:30
  17.7 3.9 %collective-permute-done.1 = bf16[784,128]{1,0:T(8,128)(2,1)S(1)} collective-permute-done((bf16[784,128]{1,0:T(8,128)(2,1)S(1)}, bf16[784,128]{1,0:T(8,128)(2,1)S(1)}, u32[]{:S(2)}, u32[]{:S(2)}) %collective-permute-start.1) | collective-permute-done | bytes 200736 | tf_op jit(solution)/shard_map/ppermute | solution.py:30
  21.8 0.9 shard_map.111.refs_0_
  22.7 4.6 %collective-permute-start.2 = (bf16[272,768]{1,0:T(8,128)(2,1)S(1)}, bf16[272,768]{1,0:T(8,128)(2,1)}, u32[]{:S(2)}, u32[]{:S(2)}) collective-permute-start(bf16[272,768]{1,0:T(8,128)(2,1)S(1)} %shard_map.111.refs_0_), channel_id=1, source_target_pairs={{0,8},{8,0},{16,24},{24,16},{1,9},{9,1},{17,25},{25,17},{2,10},{10... | collective-permute-start | bytes 1253384 | tf_op jit(solution)/shard_map/ppermute | solution.py:429
  27.3 0.7 collective-permute-start.6
  28.0 1.0 shard_map.112
  29.1 1.5 collective-permute-start.10
  30.6 5.3 %collective-permute-done.2.refs_0_ = bf16[272,768]{1,0:T(8,128)(2,1)} collective-permute-done((bf16[272,768]{1,0:T(8,128)(2,1)S(1)}, bf16[272,768]{1,0:T(8,128)(2,1)}, u32[]{:S(2)}, u32[]{:S(2)}) %collective-permute-start.2) | collective-permute-done | bytes 417824 | tf_op jit(solution)/shard_map/ppermute | solution.py:429
  35.9 1.5 shard_map.115
  37.4 1.5 collective-permute-start.9
  39.0 0.7 collective-permute-start.3
  39.7 1.3 collective-permute-start.7
  41.1 4.2 %collective-permute-done.9 = bf16[768,256]{1,0:T(8,128)(2,1)S(1)} collective-permute-done((bf16[768,256]{1,0:T(8,128)(2,1)S(1)}, bf16[768,256]{1,0:T(8,128)(2,1)S(1)}, u32[]{:S(2)}, u32[]{:S(2)}) %collective-permute-start.9) | collective-permute-done | bytes 393248 | tf_op jit(solution)/shard_map/ppermute | solution.py:429
  45.4 8.1 %collective-permute-done.7.refs_1_ = bf16[272,768]{1,0:T(8,128)(2,1)S(1)} collective-permute-done((bf16[272,768]{1,0:T(8,128)(2,1)S(1)}, bf16[272,768]{1,0:T(8,128)(2,1)S(1)}, u32[]{:S(2)}, u32[]{:S(2)}) %collective-permute-start.7) | collective-permute-done | bytes 417824 | tf_op jit(solution)/shard_map/ppermute | solution.py:531
  54.0 1.0 shard_map.114
  55.7 1.5 collective-permute-start.8
  57.2 1.5 collective-permute-start.4
  58.7 7.7 %collective-permute-done.8 = bf16[768,256]{1,0:T(8,128)(2,1)S(1)} collective-permute-done((bf16[768,256]{1,0:T(8,128)(2,1)S(1)}, bf16[768,256]{1,0:T(8,128)(2,1)S(1)}, u32[]{:S(2)}, u32[]{:S(2)}) %collective-permute-start.8) | collective-permute-done | bytes 393248 | tf_op jit(solution)/shard_map/ppermute | solution.py:429
  66.5 1.3 collective-permute-done.4.refs_1_
  67.8 0.8 copy-done.8
  68.5 1.1 collective-permute-done.11.refs_2_
  70.4 1.0 copy-done.9
  71.4 1.0 shard_map.113
  73.4 9.2 %shard_map.116 = (f32[2,576,256]{2,1,0:T(8,128)S(1)}, f32[2,576,256]{2,1,0:T(8,128)S(1)}, f32[2,2,256]{2,1,0:T(2,128)S(1)}) custom-call(s32[4]{0:T(128)S(1)} %pad_add_fusion.2.plan_ref, bf16[2,768,256]{2,1,0:T(8,128)(2,1)S(1)} %pad_maximum_fusion.1.refs_0_, bf16[2,768,256]{2,1,0:T(8,128)(2,1)} %collective-permute-done.12.refs_1_, ...), custom_call_target="tpu_custom_call" | custom-call | flops 3623878656 | bytes 14155776 | tf_op jit(solution)/shard_map/pallas_call | solution.py:346
  82.6 1.0 copy-done.4
  83.6 1.0 copy-done.6
  84.6 1.3 collective-permute-done.15.refs_0_
  87.4 1.4 collective-permute-start.20
  88.8 0.9 collective-permute-done.17.refs_3_
  89.7 1.3 copy-done.7
  91.0 9.8 %shard_map.117.hidden_ref = bf16[2,256,576]{2,1,0:T(8,128)(2,1)S(1)} custom-call(s32[4]{0:T(128)S(1)} %pad_add_fusion.1.plan_ref, bf16[2,768,256]{2,1,0:T(8,128)(2,1)} %collective-permute-done.15.refs_0_, bf16[2,768,256]{2,1,0:T(8,128)(2,1)} %collective-permute-done.16.refs_1_, bf16[2,768,256]{2,1,0:T(8,128)(2,1)} %collective-permute-done.11.refs_2_, ...), custom_call_target="tpu_custom_call" | custom-call | flops 3623878656 | bytes 14155776 | tf_op jit(solution)/shard_map/pallas_call | solution.py:346
  100.8 10.8 %shard_map.118 = (bf16[4,256,768]{2,1,0:T(8,128)(2,1)S(1)}, bf16[4,256,768]{2,1,0:T(8,128)(2,1)S(1)}) custom-call(s32[8]{0:T(128)S(1)} %concatenate.14.plan_ref, bf16[2,256,576]{2,1,0:T(8,128)(2,1)S(1)} %shard_map.117.hidden_ref, bf16[2,576,6144]{2,1,0:T(8,128)(2,1)} %down_ref.7), custom_call_target="tpu_custom_call" | custom-call | flops 1811939328 | bytes 14155776 | tf_op jit(solution)/shard_map/pallas_call | solution.py:401
  111.8 10.8 %shard_map.120 = (bf16[4,256,768]{2,1,0:T(8,128)(2,1)S(1)}, bf16[4,256,768]{2,1,0:T(8,128)(2,1)S(1)}) custom-call(s32[8]{0:T(128)S(1)} %concatenate.14.plan_ref, bf16[2,256,576]{2,1,0:T(8,128)(2,1)S(1)} %shard_map.117.hidden_ref, bf16[2,576,6144]{2,1,0:T(8,128)(2,1)} %down_ref.7), custom_call_target="tpu_custom_call" | custom-call | flops 1811939328 | bytes 14155776 | tf_op jit(solution)/shard_map/pallas_call | solution.py:401
  123.8 0.7 collective-permute-start.24
  124.5 1.7 collective-permute-done.25.refs_1_
  126.7 1.7 collective-permute-done.23.refs_3_
  128.4 1.1 collective-permute-done.22.refs_1_
  129.5 8.7 %shard_map.119 = (f32[2,576,256]{2,1,0:T(8,128)S(1)}, f32[2,576,256]{2,1,0:T(8,128)S(1)}, f32[2,2,256]{2,1,0:T(2,128)S(1)}) custom-call(s32[4]{0:T(128)S(1)} %pad_add_fusion.2.plan_ref, bf16[2,768,256]{2,1,0:T(8,128)(2,1)S(1)} %pad_maximum_fusion.refs_0_, bf16[2,768,256]{2,1,0:T(8,128)(2,1)S(1)} %collective-permute-done.22.refs_1_, ...), custom_call_target="tpu_custom_call" | custom-call | flops 3623878656 | bytes 14155776 | tf_op jit(solution)/shard_map/pallas_call | solution.py:346
  139.0 1.2 collective-permute-start.26
  140.2 9.2 %shard_map.121.hidden_ref = bf16[2,256,576]{2,1,0:T(8,128)(2,1)S(1)} custom-call(s32[4]{0:T(128)S(1)} %pad_add_fusion.1.plan_ref, bf16[2,768,256]{2,1,0:T(8,128)(2,1)} %collective-permute-done.14.refs_0_, bf16[2,768,256]{2,1,0:T(8,128)(2,1)S(1)} %collective-permute-done.19.refs_1_, bf16[2,768,256]{2,1,0:T(8,128)(2,1)S(1)} %collective-permute-done.20.refs_2_, ...), custom_call_target="tpu_custom_call" | custom-call | flops 3623878656 | bytes 14155776 | tf_op jit(solution)/shard_map/pallas_call | solution.py:346
  149.5 1.6 collective-permute-done.26
  151.4 0.7 collective-permute-start.28
  152.1 10.8 %shard_map.123 = (bf16[4,256,768]{2,1,0:T(8,128)(2,1)S(1)}, bf16[4,256,768]{2,1,0:T(8,128)(2,1)S(1)}) custom-call(s32[8]{0:T(128)S(1)} %concatenate.14.plan_ref, bf16[2,256,576]{2,1,0:T(8,128)(2,1)S(1)} %shard_map.121.hidden_ref, bf16[2,576,6144]{2,1,0:T(8,128)(2,1)} %down_ref.7), custom_call_target="tpu_custom_call" | custom-call | flops 1811939328 | bytes 14155776 | tf_op jit(solution)/shard_map/pallas_call | solution.py:401
  163.2 1.3 collective-permute-start.30
  164.5 4.4 %collective-permute-start.29 = (bf16[256,768]{1,0:T(8,128)(2,1)S(1)}, bf16[256,768]{1,0:T(8,128)(2,1)S(1)}, u32[]{:S(2)}, u32[]{:S(2)}) collective-permute-start(bf16[256,768]{1,0:T(8,128)(2,1)S(1)} %shard_map.122), channel_id=1, source_target_pairs={{0,16},{24,8},{1,17},{25,9},{2,18},{26,10},{3,19},{27,11},{4,20},{... | collective-permute-start | bytes 1179656 | tf_op jit(solution)/shard_map/ppermute | solution.py:608
  168.9 10.8 %shard_map.124 = (bf16[4,256,768]{2,1,0:T(8,128)(2,1)S(1)}, bf16[4,256,768]{2,1,0:T(8,128)(2,1)S(1)}) custom-call(s32[8]{0:T(128)S(1)} %concatenate.14.plan_ref, bf16[2,256,576]{2,1,0:T(8,128)(2,1)S(1)} %shard_map.121.hidden_ref, bf16[2,576,6144]{2,1,0:T(8,128)(2,1)} %down_ref.7), custom_call_target="tpu_custom_call" | custom-call | flops 1811939328 | bytes 14155776 | tf_op jit(solution)/shard_map/pallas_call | solution.py:401
  181.2 2.4 %collective-permute-done.31.refs_1_ = bf16[4,256,768]{2,1,0:T(8,128)(2,1)S(1)} collective-permute-done((bf16[4,256,768]{2,1,0:T(8,128)(2,1)S(1)}, bf16[4,256,768]{2,1,0:T(8,128)(2,1)S(1)}, u32[]{:S(2)}, u32[]{:S(2)}) %collective-permute-start.31) | collective-permute-done | bytes 1572896 | tf_op jit(solution)/shard_map/ppermute | solution.py:429
  183.8 8.8 %collective-permute-done.33.refs_2_ = bf16[2,256,768]{2,1,0:T(8,128)(2,1)S(1)} collective-permute-done((bf16[2,256,768]{2,1,0:T(8,128)(2,1)S(1)}, bf16[2,256,768]{2,1,0:T(8,128)(2,1)S(1)}, u32[]{:S(2)}, u32[]{:S(2)}) %collective-permute-start.33) | collective-permute-done | bytes 786464 | tf_op jit(solution)/shard_map/ppermute | solution.py:429
  193.3 1.6 collective-permute-start.37
  194.9 13.1 %collective-permute-done.34.refs_2_ = bf16[2,256,768]{2,1,0:T(8,128)(2,1)S(1)} collective-permute-done((bf16[2,256,768]{2,1,0:T(8,128)(2,1)S(1)}, bf16[2,256,768]{2,1,0:T(8,128)(2,1)S(1)}, u32[]{:S(2)}, u32[]{:S(2)}) %collective-permute-start.34) | collective-permute-done | bytes 786464 | tf_op jit(solution)/shard_map/ppermute | solution.py:429
  208.2 1.3 collective-permute-start.35
  210.2 3.7 %collective-permute-start.39 = (bf16[256,768]{1,0:T(8,128)(2,1)S(1)}, bf16[256,768]{1,0:T(8,128)(2,1)S(1)}, u32[]{:S(2)}, u32[]{:S(2)}) collective-permute-start(bf16[256,768]{1,0:T(8,128)(2,1)S(1)} %shard_map.127), channel_id=1, source_target_pairs={{0,24},{24,0},{1,25},{25,1},{2,26},{26,2},{3,27},{27,3},{4,28},{28... | collective-permute-start | bytes 1179656 | tf_op jit(solution)/shard_map/ppermute | solution.py:622
  213.9 1.3 collective-permute-start.38
  215.2 0.8 collective-permute-done.35
  216.5 19.4 %collective-permute-done.36 = bf16[256,768]{1,0:T(8,128)(2,1)S(1)} collective-permute-done((bf16[256,768]{1,0:T(8,128)(2,1)S(1)}, bf16[256,768]{1,0:T(8,128)(2,1)S(1)}, u32[]{:S(2)}, u32[]{:S(2)}) %collective-permute-start.36) | collective-permute-done | bytes 393248 | tf_op jit(solution)/shard_map/ppermute | solution.py:429
  235.9 1.1 add_convert_fusion.8
  (99 shorter events, 11.9 us)
Async XLA Ops:
  2.2 10.8 %collective-permute-start = (bf16[784,128]{1,0:T(8,128)(2,1)S(1)}, bf16[784,128]{1,0:T(8,128)(2,1)S(1)}, u32[]{:S(2)}, u32[]{:S(2)}) collective-permute-start(bf16[784,128]{1,0:T(8,128)(2,1)S(1)} %get-tuple-element.71), channel_id=1, source_target_pairs={{0,8},{8,16},{16,24},{1,9},{9,17},{17,25},{2,10},{10,18},{18,26},{... | collective-permute-start | bytes 602120 | tf_op jit(solution)/shard_map/ppermute | solution.py:30
  7.8 1.0 copy-start
  8.8 1.0 copy-start.2
  9.8 1.0 copy-start.3
  10.8 0.7 copy-start.16
  12.9 8.9 %copy-start.1 = (bf16[256,768]{1,0:T(8,128)(2,1)S(1)}, bf16[256,768]{1,0:T(8,128)(2,1)}, u32[]{:S(2)}) copy-start(bf16[256,768]{1,0:T(8,128)(2,1)} %query_ref.3) | copy-start | bytes 1179652
  12.9 8.9 %copy-start.11 = (bf16[256,768]{1,0:T(8,128)(2,1)S(1)}, bf16[256,768]{1,0:T(8,128)(2,1)}, u32[]{:S(2)}) copy-start(bf16[256,768]{1,0:T(8,128)(2,1)} %residual_ref.1) | copy-start | bytes 1179652
  12.9 8.9 %copy-start.17 = (s32[256,2]{0,1:T(2,128)S(1)}, s32[256,2]{0,1:T(2,128)}, u32[]{:S(2)}) copy-start(s32[256,2]{0,1:T(2,128)} %param.17) | copy-start | bytes 6148
  13.2 8.5 %collective-permute-start.1 = (bf16[784,128]{1,0:T(8,128)(2,1)S(1)}, bf16[784,128]{1,0:T(8,128)(2,1)S(1)}, u32[]{:S(2)}, u32[]{:S(2)}) collective-permute-start(bf16[784,128]{1,0:T(8,128)(2,1)S(1)} %concatenate.13), channel_id=1, source_target_pairs={{0,16},{8,24},{1,17},{9,25},{2,18},{10,26},{3,19},{11,27},{4,20},{... | collective-permute-start | bytes 602120 | tf_op jit(solution)/shard_map/ppermute | solution.py:30
  22.7 13.3 %collective-permute-start.2 = (bf16[272,768]{1,0:T(8,128)(2,1)S(1)}, bf16[272,768]{1,0:T(8,128)(2,1)}, u32[]{:S(2)}, u32[]{:S(2)}) collective-permute-start(bf16[272,768]{1,0:T(8,128)(2,1)S(1)} %shard_map.111.refs_0_), channel_id=1, source_target_pairs={{0,8},{8,0},{16,24},{24,16},{1,9},{9,1},{17,25},{25,17},{2,10},{10... | collective-permute-start | bytes 1253384 | tf_op jit(solution)/shard_map/ppermute | solution.py:429
  27.3 12.4 %collective-permute-start.6 = (bf16[272,768]{1,0:T(8,128)(2,1)S(1)}, bf16[272,768]{1,0:T(8,128)(2,1)S(1)}, u32[]{:S(2)}, u32[]{:S(2)}) collective-permute-start(bf16[272,768]{1,0:T(8,128)(2,1)S(1)} %shard_map.111.refs_0_), channel_id=1, source_target_pairs={{8,16},{16,8},{9,17},{17,9},{10,18},{18,10},{11,19},{19,11},{12,20... | collective-permute-start | bytes 1253384 | tf_op jit(solution)/shard_map/ppermute | solution.py:528
  29.1 11.9 %collective-permute-start.10 = (bf16[768,256]{1,0:T(8,128)(2,1)S(1)}, bf16[768,256]{1,0:T(8,128)(2,1)S(1)}, u32[]{:S(2)}, u32[]{:S(2)}) collective-permute-start(bf16[768,256]{1,0:T(8,128)(2,1)S(1)} %get-tuple-element.76), channel_id=1, source_target_pairs={{0,2},{1,5},{2,0},{3,7},{4,6},{5,1},{6,4},{7,3},{8,10},{9,13},{10,... | collective-permute-start | bytes 1179656 | tf_op jit(solution)/shard_map/ppermute | solution.py:429
  37.4 7.8 %collective-permute-start.9 = (bf16[768,256]{1,0:T(8,128)(2,1)S(1)}, bf16[768,256]{1,0:T(8,128)(2,1)S(1)}, u32[]{:S(2)}, u32[]{:S(2)}) collective-permute-start(bf16[768,256]{1,0:T(8,128)(2,1)S(1)} %get-tuple-element.75), channel_id=1, source_target_pairs={{0,2},{1,5},{2,0},{3,7},{4,6},{5,1},{6,4},{7,3},{8,10},{9,13},{10,... | collective-permute-start | bytes 1179656 | tf_op jit(solution)/shard_map/ppermute | solution.py:429
  39.0 6.4 %collective-permute-start.3 = (bf16[272,768]{1,0:T(8,128)(2,1)}, bf16[272,768]{1,0:T(8,128)(2,1)S(1)}, u32[]{:S(2)}, u32[]{:S(2)}) collective-permute-start(bf16[272,768]{1,0:T(8,128)(2,1)} %collective-permute-done.2.refs_0_), channel_id=1, source_target_pairs={{8,16},{16,8},{9,17},{17,9},{10,18},{18,10},{11,19},{19,11},{12,20... | collective-permute-start | bytes 1253384 | tf_op jit(solution)/shard_map/ppermute | solution.py:528
  39.7 13.9 %collective-permute-start.7 = (bf16[272,768]{1,0:T(8,128)(2,1)S(1)}, bf16[272,768]{1,0:T(8,128)(2,1)S(1)}, u32[]{:S(2)}, u32[]{:S(2)}) collective-permute-start(bf16[272,768]{1,0:T(8,128)(2,1)S(1)} %collective-permute-done.6.refs_0_), channel_id=1, source_target_pairs={{8,0},{16,24},{9,1},{17,25},{10,2},{18,26},{11,3},{19,27},{12,4},{... | collective-permute-start | bytes 1253384 | tf_op jit(solution)/shard_map/ppermute | solution.py:531
  45.4 28.0 %copy-start.10 = (bf16[6144,2]{0,1:T(2,128)(2,1)S(1)}, bf16[6144,2]{0,1:T(2,128)(2,1)}, u32[]{:S(2)}) copy-start(bf16[6144,2]{0,1:T(2,128)(2,1)} %param.18) | copy-start | bytes 73732
  53.5 16.1 %collective-permute-start.11 = (bf16[2,768,256]{2,1,0:T(8,128)(2,1)S(1)}, bf16[2,768,256]{2,1,0:T(8,128)(2,1)}, u32[]{:S(2)}, u32[]{:S(2)}) collective-permute-start(bf16[2,768,256]{2,1,0:T(8,128)(2,1)S(1)} %pad_maximum_fusion.2.refs_2_), channel_id=1, source_target_pairs={{0,4},{1,3},{2,6},{3,1},{4,0},{5,7},{6,2},{7,5},{8,12},{9,11},{10,... | collective-permute-start | bytes 2359304 | tf_op jit(solution)/shard_map/ppermute | solution.py:429
  55.1 0.6 copy-start.14
  55.7 10.7 %collective-permute-start.8 = (bf16[768,256]{1,0:T(8,128)(2,1)S(1)}, bf16[768,256]{1,0:T(8,128)(2,1)S(1)}, u32[]{:S(2)}, u32[]{:S(2)}) collective-permute-start(bf16[768,256]{1,0:T(8,128)(2,1)S(1)} %get-tuple-element.74), channel_id=1, source_target_pairs={{0,2},{1,5},{2,0},{3,7},{4,6},{5,1},{6,4},{7,3},{8,10},{9,13},{10,... | collective-permute-start | bytes 1179656 | tf_op jit(solution)/shard_map/ppermute | solution.py:429
  57.2 10.6 %collective-permute-start.4 = (bf16[272,768]{1,0:T(8,128)(2,1)S(1)}, bf16[272,768]{1,0:T(8,128)(2,1)S(1)}, u32[]{:S(2)}, u32[]{:S(2)}) collective-permute-start(bf16[272,768]{1,0:T(8,128)(2,1)S(1)} %collective-permute-done.3.refs_0_), channel_id=1, source_target_pairs={{8,0},{16,24},{9,1},{17,25},{10,2},{18,26},{11,3},{19,27},{12,4},{... | collective-permute-start | bytes 1253384 | tf_op jit(solution)/shard_map/ppermute | solution.py:531
  58.7 14.7 %collective-permute-start.13 = (bf16[2,768,256]{2,1,0:T(8,128)(2,1)S(1)}, bf16[2,768,256]{2,1,0:T(8,128)(2,1)}, u32[]{:S(2)}, u32[]{:S(2)}) collective-permute-start(bf16[2,768,256]{2,1,0:T(8,128)(2,1)S(1)} %pad_maximum_fusion.2.refs_2_), channel_id=1, source_target_pairs={{0,1},{1,0},{2,3},{3,2},{4,5},{5,4},{6,7},{7,6},{8,9},{9,8},{10,11... | collective-permute-start | bytes 2359304 | tf_op jit(solution)/shard_map/ppermute | solution.py:429
  67.8 0.8 copy-start.8
  69.7 3.7 %collective-permute-start.12 = (bf16[2,768,256]{2,1,0:T(8,128)(2,1)S(1)}, bf16[2,768,256]{2,1,0:T(8,128)(2,1)}, u32[]{:S(2)}, u32[]{:S(2)}) collective-permute-start(bf16[2,768,256]{2,1,0:T(8,128)(2,1)S(1)} %pad_maximum_fusion.1.refs_0_), channel_id=1, source_target_pairs={{0,1},{1,0},{2,3},{3,2},{4,5},{5,4},{6,7},{7,6},{8,9},{9,8},{10,11... | collective-permute-start | bytes 2359304 | tf_op jit(solution)/shard_map/ppermute | solution.py:429
  69.7 16.3 %collective-permute-start.15 = (bf16[2,768,256]{2,1,0:T(8,128)(2,1)S(1)}, bf16[2,768,256]{2,1,0:T(8,128)(2,1)}, u32[]{:S(2)}, u32[]{:S(2)}) collective-permute-start(bf16[2,768,256]{2,1,0:T(8,128)(2,1)S(1)} %pad_maximum_fusion.1.refs_0_), channel_id=1, source_target_pairs={{0,4},{1,3},{2,6},{3,1},{4,0},{5,7},{6,2},{7,5},{8,12},{9,11},{10,... | collective-permute-start | bytes 2359304 | tf_op jit(solution)/shard_map/ppermute | solution.py:429
  70.4 1.0 copy-start.9
  72.4 0.7 copy-start.12
  73.1 13.4 %collective-permute-start.5 = (bf16[768,256]{1,0:T(8,128)(2,1)S(1)}, bf16[768,256]{1,0:T(8,128)(2,1)S(1)}, u32[]{:S(2)}, u32[]{:S(2)}) collective-permute-start(bf16[768,256]{1,0:T(8,128)(2,1)S(1)} %get-tuple-element.73), channel_id=1, source_target_pairs={{0,2},{1,5},{2,0},{3,7},{4,6},{5,1},{6,4},{7,3},{8,10},{9,13},{10,... | collective-permute-start | bytes 1179656 | tf_op jit(solution)/shard_map/ppermute | solution.py:429
  82.6 1.1 copy-start.4
  83.6 1.0 copy-start.6
  86.0 3.8 %copy-start.5 = (f32[2,576,256]{2,1,0:T(8,128)S(1)}, f32[2,576,256]{2,1,0:T(8,128)}, u32[]{:S(2)}) copy-start(f32[2,576,256]{2,1,0:T(8,128)} %copy-done.4) | copy-start | bytes 3538948
  86.0 2.9 %collective-permute-start.16 = (bf16[2,768,256]{2,1,0:T(8,128)(2,1)}, bf16[2,768,256]{2,1,0:T(8,128)(2,1)}, u32[]{:S(2)}, u32[]{:S(2)}) collective-permute-start(bf16[2,768,256]{2,1,0:T(8,128)(2,1)} %collective-permute-done.15.refs_0_), channel_id=1, source_target_pairs={{0,1},{1,0},{2,3},{3,2},{4,5},{5,4},{6,7},{7,6},{8,9},{9,8},{10,11... | collective-permute-start | bytes 2359304 | tf_op jit(solution)/shard_map/ppermute | solution.py:429
  86.0 3.7 %collective-permute-start.17 = (bf16[2,768,256]{2,1,0:T(8,128)(2,1)}, bf16[2,768,256]{2,1,0:T(8,128)(2,1)}, u32[]{:S(2)}, u32[]{:S(2)}) collective-permute-start(bf16[2,768,256]{2,1,0:T(8,128)(2,1)} %collective-permute-done.11.refs_2_), channel_id=1, source_target_pairs={{0,1},{1,0},{2,3},{3,2},{4,5},{5,4},{6,7},{7,6},{8,9},{9,8},{10,11... | collective-permute-start | bytes 2359304 | tf_op jit(solution)/shard_map/ppermute | solution.py:429
  86.6 14.2 %collective-permute-start.14 = (bf16[2,768,256]{2,1,0:T(8,128)(2,1)S(1)}, bf16[2,768,256]{2,1,0:T(8,128)(2,1)}, u32[]{:S(2)}, u32[]{:S(2)}) collective-permute-start(bf16[2,768,256]{2,1,0:T(8,128)(2,1)S(1)} %pad_maximum_fusion.refs_0_), channel_id=1, source_target_pairs={{0,4},{1,3},{2,6},{3,1},{4,0},{5,7},{6,2},{7,5},{8,12},{9,11},{10,... | collective-permute-start | bytes 2359304 | tf_op jit(solution)/shard_map/ppermute | solution.py:429
  87.4 24.4 %collective-permute-start.20 = (bf16[2,768,256]{2,1,0:T(8,128)(2,1)S(1)}, bf16[2,768,256]{2,1,0:T(8,128)(2,1)S(1)}, u32[]{:S(2)}, u32[]{:S(2)}) collective-permute-start(bf16[2,768,256]{2,1,0:T(8,128)(2,1)S(1)} %pad_maximum_fusion.3.refs_2_), channel_id=1, source_target_pairs={{0,4},{1,3},{2,6},{3,1},{4,0},{5,7},{6,2},{7,5},{8,12},{9,11},{10,... | collective-permute-start | bytes 2359304 | tf_op jit(solution)/shard_map/ppermute | solution.py:429
  89.7 1.3 copy-start.7
  111.6 12.0 %collective-permute-start.18 = (bf16[4,256,768]{2,1,0:T(8,128)(2,1)S(1)}, bf16[4,256,768]{2,1,0:T(8,128)(2,1)S(1)}, u32[]{:S(2)}, u32[]{:S(2)}) collective-permute-start(bf16[4,256,768]{2,1,0:T(8,128)(2,1)S(1)} %get-tuple-element.100), channel_id=1, source_target_pairs={{0,1},{1,0},{2,3},{3,2},{4,5},{5,4},{6,7},{7,6},{8,9},{9,8},{10,11... | collective-permute-start | bytes 4718600 | tf_op jit(solution)/shard_map/ppermute | solution.py:429
  122.7 3.5 %collective-permute-start.25 = (bf16[4,256,768]{2,1,0:T(8,128)(2,1)S(1)}, bf16[4,256,768]{2,1,0:T(8,128)(2,1)S(1)}, u32[]{:S(2)}, u32[]{:S(2)}) collective-permute-start(bf16[4,256,768]{2,1,0:T(8,128)(2,1)S(1)} %get-tuple-element.113), channel_id=1, source_target_pairs={{0,1},{1,0},{2,3},{3,2},{4,5},{5,4},{6,7},{7,6},{8,9},{9,8},{10,11... | collective-permute-start | bytes 4718600 | tf_op jit(solution)/shard_map/ppermute | solution.py:429
  123.1 5.3 %collective-permute-start.23 = (bf16[2,768,256]{2,1,0:T(8,128)(2,1)S(1)}, bf16[2,768,256]{2,1,0:T(8,128)(2,1)S(1)}, u32[]{:S(2)}, u32[]{:S(2)}) collective-permute-start(bf16[2,768,256]{2,1,0:T(8,128)(2,1)S(1)} %pad_maximum_fusion.3.refs_2_), channel_id=1, source_target_pairs={{0,1},{1,0},{2,3},{3,2},{4,5},{5,4},{6,7},{7,6},{8,9},{9,8},{10,11... | collective-permute-start | bytes 2359304 | tf_op jit(solution)/shard_map/ppermute | solution.py:429
  123.2 6.3 %collective-permute-start.22 = (bf16[2,768,256]{2,1,0:T(8,128)(2,1)S(1)}, bf16[2,768,256]{2,1,0:T(8,128)(2,1)S(1)}, u32[]{:S(2)}, u32[]{:S(2)}) collective-permute-start(bf16[2,768,256]{2,1,0:T(8,128)(2,1)S(1)} %pad_maximum_fusion.refs_0_), channel_id=1, source_target_pairs={{0,1},{1,0},{2,3},{3,2},{4,5},{5,4},{6,7},{7,6},{8,9},{9,8},{10,11... | collective-permute-start | bytes 2359304 | tf_op jit(solution)/shard_map/ppermute | solution.py:429
  123.8 14.4 %collective-permute-start.24 = (bf16[2,256,768]{2,1,0:T(8,128)(2,1)S(1)}, bf16[2,256,768]{2,1,0:T(8,128)(2,1)S(1)}, u32[]{:S(2)}, u32[]{:S(2)}) collective-permute-start(bf16[2,256,768]{2,1,0:T(8,128)(2,1)S(1)} %add_convert_fusion.3), channel_id=1, source_target_pairs={{0,4},{1,3},{2,6},{3,1},{4,0},{5,7},{6,2},{7,5},{8,12},{9,11},{10,... | collective-permute-start | bytes 2359304 | tf_op jit(solution)/shard_map/ppermute | solution.py:429
  124.5 15.8 %collective-permute-start.19 = (bf16[2,768,256]{2,1,0:T(8,128)(2,1)}, bf16[2,768,256]{2,1,0:T(8,128)(2,1)S(1)}, u32[]{:S(2)}, u32[]{:S(2)}) collective-permute-start(bf16[2,768,256]{2,1,0:T(8,128)(2,1)} %collective-permute-done.14.refs_0_), channel_id=1, source_target_pairs={{0,1},{1,0},{2,3},{3,2},{4,5},{5,4},{6,7},{7,6},{8,9},{9,8},{10,11... | collective-permute-start | bytes 2359304 | tf_op jit(solution)/shard_map/ppermute | solution.py:429
  126.1 14.1 %collective-permute-start.21 = (bf16[2,768,256]{2,1,0:T(8,128)(2,1)S(1)}, bf16[2,768,256]{2,1,0:T(8,128)(2,1)S(1)}, u32[]{:S(2)}, u32[]{:S(2)}) collective-permute-start(bf16[2,768,256]{2,1,0:T(8,128)(2,1)S(1)} %collective-permute-done.20.refs_2_), channel_id=1, source_target_pairs={{0,1},{1,0},{2,3},{3,2},{4,5},{5,4},{6,7},{7,6},{8,9},{9,8},{10,11... | collective-permute-start | bytes 2359304 | tf_op jit(solution)/shard_map/ppermute | solution.py:429
  138.3 12.7 %copy-start.15 = (bf16[256,256]{1,0:T(8,128)(2,1)S(1)}, bf16[256,256]{1,0:T(8,128)(2,1)}, u32[]{:S(2)}) copy-start(bf16[256,256]{1,0:T(8,128)(2,1)} %copy-done.14) | copy-start | bytes 393220
  138.3 24.7 %collective-permute-start.27 = (bf16[2,256,768]{2,1,0:T(8,128)(2,1)S(1)}, bf16[2,256,768]{2,1,0:T(8,128)(2,1)S(1)}, u32[]{:S(2)}, u32[]{:S(2)}) collective-permute-start(bf16[2,256,768]{2,1,0:T(8,128)(2,1)S(1)} %add_convert_fusion.2), channel_id=1, source_target_pairs={{0,4},{1,3},{2,6},{3,1},{4,0},{5,7},{6,2},{7,5},{8,12},{9,11},{10,... | collective-permute-start | bytes 2359304 | tf_op jit(solution)/shard_map/ppermute | solution.py:429
  139.0 12.0 %collective-permute-start.26 = (bf16[256,768]{1,0:T(8,128)(2,1)S(1)}, bf16[256,768]{1,0:T(8,128)(2,1)S(1)}, u32[]{:S(2)}, u32[]{:S(2)}) collective-permute-start(bf16[256,768]{1,0:T(8,128)(2,1)S(1)} %fusion), channel_id=1, source_target_pairs={{0,2},{1,5},{2,0},{3,7},{4,6},{5,1},{6,4},{7,3},{8,10},{9,13},{10,... | collective-permute-start | bytes 1179656 | tf_op jit(solution)/shard_map/ppermute | solution.py:429
  151.4 13.1 %collective-permute-start.28 = (bf16[256,768]{1,0:T(8,128)(2,1)S(1)}, bf16[256,768]{1,0:T(8,128)(2,1)S(1)}, u32[]{:S(2)}, u32[]{:S(2)}) collective-permute-start(bf16[256,768]{1,0:T(8,128)(2,1)S(1)} %shard_map.122), channel_id=1, source_target_pairs={{8,16},{16,8},{9,17},{17,9},{10,18},{18,10},{11,19},{19,11},{12,20... | collective-permute-start | bytes 1179656 | tf_op jit(solution)/shard_map/ppermute | solution.py:605
  162.9 17.4 %collective-permute-start.32 = (bf16[4,256,768]{2,1,0:T(8,128)(2,1)S(1)}, bf16[4,256,768]{2,1,0:T(8,128)(2,1)S(1)}, u32[]{:S(2)}, u32[]{:S(2)}) collective-permute-start(bf16[4,256,768]{2,1,0:T(8,128)(2,1)S(1)} %get-tuple-element.124), channel_id=1, source_target_pairs={{0,1},{1,0},{2,3},{3,2},{4,5},{5,4},{6,7},{7,6},{8,9},{9,8},{10,11... | collective-permute-start | bytes 4718600 | tf_op jit(solution)/shard_map/ppermute | solution.py:429
  163.2 16.5 %collective-permute-start.30 = (bf16[256,768]{1,0:T(8,128)(2,1)S(1)}, bf16[256,768]{1,0:T(8,128)(2,1)S(1)}, u32[]{:S(2)}, u32[]{:S(2)}) collective-permute-start(bf16[256,768]{1,0:T(8,128)(2,1)S(1)} %fusion.1), channel_id=1, source_target_pairs={{0,2},{1,5},{2,0},{3,7},{4,6},{5,1},{6,4},{7,3},{8,10},{9,13},{10,... | collective-permute-start | bytes 1179656 | tf_op jit(solution)/shard_map/ppermute | solution.py:429
  164.5 15.6 %collective-permute-start.29 = (bf16[256,768]{1,0:T(8,128)(2,1)S(1)}, bf16[256,768]{1,0:T(8,128)(2,1)S(1)}, u32[]{:S(2)}, u32[]{:S(2)}) collective-permute-start(bf16[256,768]{1,0:T(8,128)(2,1)S(1)} %shard_map.122), channel_id=1, source_target_pairs={{0,16},{24,8},{1,17},{25,9},{2,18},{26,10},{3,19},{27,11},{4,20},{... | collective-permute-start | bytes 1179656 | tf_op jit(solution)/shard_map/ppermute | solution.py:608
  180.2 3.5 %collective-permute-start.31 = (bf16[4,256,768]{2,1,0:T(8,128)(2,1)S(1)}, bf16[4,256,768]{2,1,0:T(8,128)(2,1)S(1)}, u32[]{:S(2)}, u32[]{:S(2)}) collective-permute-start(bf16[4,256,768]{2,1,0:T(8,128)(2,1)S(1)} %get-tuple-element.132), channel_id=1, source_target_pairs={{0,1},{1,0},{2,3},{3,2},{4,5},{5,4},{6,7},{7,6},{8,9},{9,8},{10,11... | collective-permute-start | bytes 4718600 | tf_op jit(solution)/shard_map/ppermute | solution.py:429
  180.6 12.1 %collective-permute-start.33 = (bf16[2,256,768]{2,1,0:T(8,128)(2,1)S(1)}, bf16[2,256,768]{2,1,0:T(8,128)(2,1)S(1)}, u32[]{:S(2)}, u32[]{:S(2)}) collective-permute-start(bf16[2,256,768]{2,1,0:T(8,128)(2,1)S(1)} %add_convert_fusion), channel_id=1, source_target_pairs={{0,4},{1,3},{2,6},{3,1},{4,0},{5,7},{6,2},{7,5},{8,12},{9,11},{10,... | collective-permute-start | bytes 2359304 | tf_op jit(solution)/shard_map/ppermute | solution.py:429
  183.8 26.0 %copy-start.13 = (bf16[256,256]{1,0:T(8,128)(2,1)S(1)}, bf16[256,256]{1,0:T(8,128)(2,1)}, u32[]{:S(2)}) copy-start(bf16[256,256]{1,0:T(8,128)(2,1)} %copy-done.12) | copy-start | bytes 393220
  192.6 15.4 %collective-permute-start.34 = (bf16[2,256,768]{2,1,0:T(8,128)(2,1)S(1)}, bf16[2,256,768]{2,1,0:T(8,128)(2,1)S(1)}, u32[]{:S(2)}, u32[]{:S(2)}) collective-permute-start(bf16[2,256,768]{2,1,0:T(8,128)(2,1)S(1)} %add_convert_fusion.1), channel_id=1, source_target_pairs={{0,4},{1,3},{2,6},{3,1},{4,0},{5,7},{6,2},{7,5},{8,12},{9,11},{10,... | collective-permute-start | bytes 2359304 | tf_op jit(solution)/shard_map/ppermute | solution.py:429
  193.3 16.4 %collective-permute-start.37 = (bf16[256,768]{1,0:T(8,128)(2,1)S(1)}, bf16[256,768]{1,0:T(8,128)(2,1)S(1)}, u32[]{:S(2)}, u32[]{:S(2)}) collective-permute-start(bf16[256,768]{1,0:T(8,128)(2,1)S(1)} %fusion.3), channel_id=1, source_target_pairs={{0,2},{1,5},{2,0},{3,7},{4,6},{5,1},{6,4},{7,3},{8,10},{9,13},{10,... | collective-permute-start | bytes 1179656 | tf_op jit(solution)/shard_map/ppermute | solution.py:429
  208.2 7.8 %collective-permute-start.35 = (bf16[256,768]{1,0:T(8,128)(2,1)S(1)}, bf16[256,768]{1,0:T(8,128)(2,1)S(1)}, u32[]{:S(2)}, u32[]{:S(2)}) collective-permute-start(bf16[256,768]{1,0:T(8,128)(2,1)S(1)} %fusion.2), channel_id=1, source_target_pairs={{0,2},{1,5},{2,0},{3,7},{4,6},{5,1},{6,4},{7,3},{8,10},{9,13},{10,... | collective-permute-start | bytes 1179656 | tf_op jit(solution)/shard_map/ppermute | solution.py:429
  209.5 26.3 %collective-permute-start.36 = (bf16[256,768]{1,0:T(8,128)(2,1)S(1)}, bf16[256,768]{1,0:T(8,128)(2,1)S(1)}, u32[]{:S(2)}, u32[]{:S(2)}) collective-permute-start(bf16[256,768]{1,0:T(8,128)(2,1)S(1)} %shard_map.125), channel_id=1, source_target_pairs={{0,8},{8,0},{16,24},{24,16},{1,9},{9,1},{17,25},{25,17},{2,10},{10... | collective-permute-start | bytes 1179656 | tf_op jit(solution)/shard_map/ppermute | solution.py:429
  210.2 25.6 %collective-permute-start.39 = (bf16[256,768]{1,0:T(8,128)(2,1)S(1)}, bf16[256,768]{1,0:T(8,128)(2,1)S(1)}, u32[]{:S(2)}, u32[]{:S(2)}) collective-permute-start(bf16[256,768]{1,0:T(8,128)(2,1)S(1)} %shard_map.127), channel_id=1, source_target_pairs={{0,24},{24,0},{1,25},{25,1},{2,26},{26,2},{3,27},{27,3},{4,28},{28... | collective-permute-start | bytes 1179656 | tf_op jit(solution)/shard_map/ppermute | solution.py:622
  213.9 21.9 %collective-permute-start.38 = (bf16[256,768]{1,0:T(8,128)(2,1)S(1)}, bf16[256,768]{1,0:T(8,128)(2,1)S(1)}, u32[]{:S(2)}, u32[]{:S(2)}) collective-permute-start(bf16[256,768]{1,0:T(8,128)(2,1)S(1)} %shard_map.127), channel_id=1, source_target_pairs={{8,24},{16,0},{9,25},{17,1},{10,26},{18,2},{11,27},{19,3},{12,28},... | collective-permute-start | bytes 1179656 | tf_op jit(solution)/shard_map/ppermute | solution.py:621

commit v11 on v10

--- a/solution.py
+++ b/solution.py
@@ -10,7 +10,7 @@
 F32 = jnp.float32
 BF16 = jnp.bfloat16
 HIGHEST = lax.Precision.HIGHEST
-VMEM_LIMIT = 22 * 1024 * 1024
+VMEM_LIMIT = 32 * 1024 * 1024
 ID_ROWS = 16
 
 
@@ -335,13 +335,14 @@
 
     weight_spec = pl.BlockSpec((experts, units, width), lambda p, plan: (0, 0, plan[p]))
     sum_shapes = [(experts, units, slots), (experts, units, slots), (experts, experts, slots)]
+    sum_specs = [pl.BlockSpec(shape, lambda p, plan: (0, 0, 0)) for shape in sum_shapes]
     if last:
         out_shape = jax.ShapeDtypeStruct((experts, slots, units), BF16)
         out_specs = whole
         scratch = [pltpu.VMEM(shape, F32) for shape in sum_shapes]
     else:
         out_shape = tuple(jax.ShapeDtypeStruct(shape, F32) for shape in sum_shapes)
-        out_specs = (whole, whole, whole)
+        out_specs = tuple(sum_specs)
         scratch = []
     return pl.pallas_call(
         functools.partial(gate_kernel, counts, len(xs), last),
@@ -353,7 +354,7 @@
                 pl.BlockSpec((1, experts, width), lambda p, plan: (plan[p], 0, 0)),
                 weight_spec,
                 weight_spec,
-                *([whole] * 3 if last else []),
+                *(sum_specs if last else []),
             ],
             out_specs=out_specs,
             scratch_shapes=scratch,
@@ -375,31 +376,35 @@
     )
 
 
-def down_kernel(blocks, low, part, plan_ref, hidden_ref, down_ref, *out_refs):
+def down_kernel(blocks, sections, plan_ref, hidden_ref, down_ref, *out_refs):
+    experts, slots, _ = hidden_ref.shape
+    part = slots // sections
     turn = pl.program_id(0) // blocks
-    for j in range(hidden_ref.shape[0]):
-        mine = hidden_ref[j, low : low + part, :]
-        share = jnp.dot(mine, down_ref[j], preferred_element_type=F32).astype(BF16)
-        for i, out_ref in enumerate(out_refs):
+    for j in range(experts):
+        share = jnp.dot(hidden_ref[j], down_ref[j], preferred_element_type=F32).astype(BF16)
+        for i in range(len(out_refs) // sections):
 
             @pl.when(turn == i)
             def _():
-                out_ref[0, j * part : (j + 1) * part, :] = share
-
-
-def down_part(plans, hidden, down_weight, width, sections, section):
+                for section in range(sections):
+                    out_ref = out_refs[i * sections + section]
+                    out_ref[0, j * part : (j + 1) * part, :] = share[
+                        section * part : (section + 1) * part
+                    ]
+
+
+def down_part(plans, hidden, down_weight, width, sections):
     blocks = plans[0].shape[0]
     experts, slots, units = hidden.shape
-    part = slots // sections
+    rows = experts * slots // sections
 
     def out_spec(i):
         return pl.BlockSpec(
-            (1, experts * part, width),
-            lambda p, plan: (jnp.clip(p - i * blocks, 0, blocks - 1), 0, 0),
+            (1, rows, width), lambda p, plan: (jnp.clip(p - i * blocks, 0, blocks - 1), 0, 0)
         )
 
-    return pl.pallas_call(
-        functools.partial(down_kernel, blocks, section * part, part),
+    out = pl.pallas_call(
+        functools.partial(down_kernel, blocks, sections),
         grid_spec=pltpu.PrefetchScalarGridSpec(
             num_scalar_prefetch=1,
             grid=(len(plans) * blocks,),
@@ -407,16 +412,17 @@
                 pl.BlockSpec(memory_space=pltpu.VMEM),
                 pl.BlockSpec((experts, units, width), lambda p, plan: (0, 0, plan[p])),
             ],
-            out_specs=[out_spec(i) for i in range(len(plans))],
-        ),
-        out_shape=[jax.ShapeDtypeStruct((blocks, experts * part, width), BF16)] * len(plans),
+            out_specs=[out_spec(i) for i in range(len(plans)) for _ in range(sections)],
+        ),
+        out_shape=[jax.ShapeDtypeStruct((blocks, rows, width), BF16)] * (len(plans) * sections),
         cost_estimate=pl.CostEstimate(
-            flops=2 * experts * part * len(plans) * blocks * width * units,
+            flops=2 * experts * slots * len(plans) * blocks * width * units,
             bytes_accessed=2 * experts * len(plans) * blocks * width * units,
             transcendentals=0,
         ),
         compiler_params=pltpu.CompilerParams(vmem_limit_bytes=VMEM_LIMIT),
     )(jnp.concatenate(plans), hidden, in_hbm(down_weight))
+    return [out[i * sections : (i + 1) * sections] for i in range(len(plans))]
 
 
 def added(left, right):
@@ -506,9 +512,8 @@
             gathered = [lax.all_gather(slots, "exp", axis=0) for slots, _ in chosen]
             sums = gate_part(order[:middle], [[x[:middle]] for x in gathered], *weights)
             hidden = gate_part(order[middle:], [[x[middle:]] for x in gathered], *weights, sums)
-            for i, offset in enumerate(chunk):
-                place = chosen[i][1]
-                (share,) = down_part([order], hidden, down_weight, width, len(chunk), i)
+            (partial,) = down_part([order], hidden, down_weight, width, len(chunk))
+            for offset, share, (_, place) in zip(chunk, partial, chosen):
                 share = lax.psum_scatter(share, "exp", scatter_dimension=0)
                 piece = combine_slots(place, [share[None]])
                 pieces.append(swapped(piece, "seq", offset, offset) if offset else piece)
@@ -538,11 +543,11 @@
     swap = swapped(stream, "seq", 1, 1)
     crossed = across_middle(stream)
     chosen["own"] = select(stream)
-    gather("own", [swap, crossed])
+    gather("own", [])
     passed = outward(crossed)
     crossed_swap = across_middle(swap)
     chosen["neighbour"] = select(swap)
-    gather("neighbour", [passed, crossed_swap, two["own"]])
+    gather("neighbour", [passed, crossed_swap, far_two["own"]])
     passed_fourth = outward(crossed_swap)
     chosen["third"] = select(crossed, passed)
     gather("third", [passed_fourth, far_two["neighbour"]])
@@ -557,15 +562,13 @@
         (late, sums), _ = tie(((late, sums), behind))
         return gate_part(plane.late, late, *weights, sums)
 
-    def down(hidden, section, behind):
+    def down(plans, hidden, behind):
         hidden, _ = tie((hidden, behind))
-        plans = [plane.theirs, plane.mine]
-        return down_part(plans, hidden, down_weight, width, 2, section)
+        return down_part(plans, hidden, down_weight, width, 2)
 
     class Scatter:
-        def __init__(self, name, shares):
-            self.name = name
-            self.theirs, self.mine = shares
+        def __init__(self, name, theirs, mine):
+            self.name, self.theirs, self.mine = name, theirs, mine
 
         def two_blocks(self, behind):
             self.near = plane.across(self.theirs)
@@ -588,8 +591,9 @@
     for name in chunk:
         near_far[name] = plane.across(tie((far_two[name], sums))[0])
     hidden = gate_last(chunk, sums, two["fourth"])
-    third = Scatter("third", down(hidden, 0, far_two["fourth"]))
-    neighbour = Scatter("neighbour", down(hidden, 1, [third.theirs, far_two["own"]]))
+    (theirs,) = down([plane.theirs], hidden, far_two["fourth"])
+    (mine,) = down([plane.mine], hidden, theirs)
+    third, neighbour = (Scatter(*shares) for shares in zip(chunk, theirs, mine))
     third.two_blocks([])
 
     chunk = ("fourth", "own")
@@ -601,21 +605,21 @@
     hidden = gate_last(chunk, sums, [third.one, neighbour.sent])
     third_piece = third.own_block(hidden)
     neighbour.one_block(hidden)
-    fourth = Scatter("fourth", down(hidden, 0, third_piece))
     third_home = lax.ppermute(third_piece, "seq", [(1, 2), (2, 1)])
-    own = Scatter("own", down(hidden, 1, [fourth.theirs, neighbour.one, third_home]))
-    third_piece, _ = tie((third_piece, third_home))
-    third_far_home = lax.ppermute(third_piece, "seq", [(0, 2), (3, 1)])
+    theirs, mine = down([plane.theirs, plane.mine], hidden, neighbour.one)
     neighbour_piece = neighbour.own_block([])
-    own.theirs, _ = tie((own.theirs, [third_far_home, neighbour_piece]))
+    theirs, _ = tie((theirs, [third_home, neighbour_piece]))
+    fourth, own = (Scatter(*shares) for shares in zip(chunk, theirs, mine))
+    third_far_home = lax.ppermute(tie((third_piece, third_home))[0], "seq", [(0, 2), (3, 1)])
+    neighbour_home = swapped(neighbour_piece, "seq", 1, 1)
     fourth.two_blocks([])
-    fourth.one_block([])
-    own.two_blocks(fourth.got_two)
-    own.one_block([])
+    fourth.one_block([third_far_home, neighbour_home])
+    own.two_blocks(fourth.got_one)
     fourth_piece = fourth.own_block([])
+    own.one_block(fourth_piece)
     return [
         own.own_block([]),
-        swapped(neighbour_piece, "seq", 1, 1),
+        neighbour_home,
         third_home,
         third_far_home,
         lax.ppermute(fourth_piece, "seq", [(1, 3), (2, 0)]),

time: 238 us -> 238 us (level)
  Pallas kernels: 90.7 us -> 75.1 us
  starting transfers between devices: 46.9 us -> 53.1 us
  other arithmetic: 3.14 us -> 6.91 us
  waiting for transfers between devices: 84.6 us -> 87.3 us
  local copies, waits for them, and re-layouts: 11.1 us -> 13.8 us
    ppermute x30, waiting for transfers between devices: 71.2 us -> 52.1 us  [swapped(): return lax.ppermute(array, axis, pairs)]
    pallas_call x4 -> x3, Pallas kernels: 43.2 us -> 27.1 us  [down_part(): pl.pallas_call(functools.partial(down_kernel, blocks, sections), grid_spe...]
    ppermute x1, waiting for transfers between devices: 0.01 us -> 9.3 us  [paired_chunks(): lax.ppermute(tie((third_piece, third_home))[0], 'seq', [(0, 2), (3, 1)])]
    ppermute x1, waiting for transfers between devices: 0.01 us -> 8.33 us  [paired_chunks(): lax.ppermute(fourth_piece, 'seq', [(1, 3), (2, 0)])]
    ppermute x1, waiting for transfers between devices: 0.01 us -> 4.7 us  [paired_chunks(): lax.ppermute(fourth_piece, 'seq', [(0, 3), (3, 0)])]
    ppermute x30, starting transfers between devices: 23.3 us -> 26.7 us  [swapped(): return lax.ppermute(array, axis, pairs)]
    unnamed x36 -> x64, local copies, waits for them, and re-layouts: 10.1 us -> 12.8 us
  transfers between devices with their start and end apart: 40 -> 40, of which waited for: 18 -> 19; matrix products, arithmetic and copies ran while one was open for 1% -> 2% of each run, Pallas kernels for 37% -> 27%
where the time goes in v11:
time: 238 us; the launch traced here: 237 us
  waiting for transfers between devices  87.3 us (37%)
  Pallas kernels  75.1 us (32%)
  starting transfers between devices  53.1 us (22%)
  local copies, waits for them, and re-layouts  13.8 us (6%)
  other arithmetic  6.91 us (3%)
    ppermute x30, waiting for transfers between devices, swapped(): return lax.ppermute(array, axis, pairs)  52.1 us
    pallas_call x4, Pallas kernels, gate_part(): pl.pallas_call(functools.partial(gate_kernel, counts, len(xs), last), gri...  36.8 us
    pallas_call x3, Pallas kernels, down_part(): pl.pallas_call(functools.partial(down_kernel, blocks, sections), grid_spe...  27.1 us
    ppermute x30, starting transfers between devices, swapped(): return lax.ppermute(array, axis, pairs)  26.7 us
    unnamed x64, local copies, waits for them, and re-layouts  12.8 us
    ppermute x2, starting transfers between devices, shifted(): return lax.ppermute(array, axis, pairs)  9.43 us
    ppermute x1, waiting for transfers between devices, paired_chunks(): lax.ppermute(tie((third_piece, third_home))[0], 'seq', [(0, 2), (3, 1)])  9.3 us
    ppermute x2, waiting for transfers between devices, outward(): return lax.ppermute(part, 'seq', [(1, 0), (2, 3)])  8.98 us
  transfers between devices with their start and end apart: 40, of which 19 were waited for; matrix products, arithmetic and copies ran while one was open for 2% of the time, Pallas kernels for 27%

profile of v11, /device:TPU:0, one launch (start us, length us, event | category | flops | bytes accessed | tf_op | source)
XLA Modules:
  0.0 236.8 jit_solution(17735675581592062475)
XLA Ops:
  0.0 2.1 shard_map.109
  2.2 4.9 %collective-permute-start = (bf16[784,128]{1,0:T(8,128)(2,1)S(1)}, bf16[784,128]{1,0:T(8,128)(2,1)S(1)}, u32[]{:S(2)}, u32[]{:S(2)}) collective-permute-start(bf16[784,128]{1,0:T(8,128)(2,1)S(1)} %get-tuple-element.72), channel_id=1, source_target_pairs={{0,8},{8,16},{16,24},{1,9},{9,17},{17,25},{2,10},{10,18},{18,26},{... | collective-permute-start | bytes 602120 | tf_op jit(solution)/shard_map/ppermute | solution.py:30
  7.9 1.0 copy-done.6
  8.9 1.0 copy-done.8
  9.9 1.0 copy-done.9
  11.6 1.4 shard_map.110.intra_ref
  13.3 4.5 %collective-permute-start.1 = (bf16[784,128]{1,0:T(8,128)(2,1)S(1)}, bf16[784,128]{1,0:T(8,128)(2,1)S(1)}, u32[]{:S(2)}, u32[]{:S(2)}) collective-permute-start(bf16[784,128]{1,0:T(8,128)(2,1)S(1)} %concatenate.7), channel_id=1, source_target_pairs={{0,16},{8,24},{1,17},{9,25},{2,18},{10,26},{3,19},{11,27},{4,20},{... | collective-permute-start | bytes 602120 | tf_op jit(solution)/shard_map/ppermute | solution.py:30
  17.8 3.9 %collective-permute-done.1 = bf16[784,128]{1,0:T(8,128)(2,1)S(1)} collective-permute-done((bf16[784,128]{1,0:T(8,128)(2,1)S(1)}, bf16[784,128]{1,0:T(8,128)(2,1)S(1)}, u32[]{:S(2)}, u32[]{:S(2)}) %collective-permute-start.1) | collective-permute-done | bytes 200736 | tf_op jit(solution)/shard_map/ppermute | solution.py:30
  22.7 1.0 shard_map.112
  23.8 1.6 collective-permute-start.10
  25.3 4.4 %collective-permute-start.2 = (bf16[272,768]{1,0:T(8,128)(2,1)S(1)}, bf16[272,768]{1,0:T(8,128)(2,1)S(1)}, u32[]{:S(2)}, u32[]{:S(2)}) collective-permute-start(bf16[272,768]{1,0:T(8,128)(2,1)S(1)} %shard_map.111.refs_0_), channel_id=1, source_target_pairs={{0,8},{8,0},{16,24},{24,16},{1,9},{9,1},{17,25},{25,17},{2,10},{10... | collective-permute-start | bytes 1253384 | tf_op jit(solution)/shard_map/ppermute | solution.py:435
  30.5 1.2 collective-permute-done.10
  31.6 1.0 pad_maximum_fusion.3.refs_2_
  32.6 1.5 collective-permute-start.11
  34.1 3.9 %collective-permute-done.2.refs_0_ = bf16[272,768]{1,0:T(8,128)(2,1)S(1)} collective-permute-done((bf16[272,768]{1,0:T(8,128)(2,1)S(1)}, bf16[272,768]{1,0:T(8,128)(2,1)S(1)}, u32[]{:S(2)}, u32[]{:S(2)}) %collective-permute-start.2) | collective-permute-done | bytes 417824 | tf_op jit(solution)/shard_map/ppermute | solution.py:435
  38.0 1.0 shard_map.115
  39.1 1.6 collective-permute-start.9
  40.6 1.3 collective-permute-start.7
  42.6 4.3 %collective-permute-done.9 = bf16[768,256]{1,0:T(8,128)(2,1)S(1)} collective-permute-done((bf16[768,256]{1,0:T(8,128)(2,1)S(1)}, bf16[768,256]{1,0:T(8,128)(2,1)S(1)}, u32[]{:S(2)}, u32[]{:S(2)}) %collective-permute-start.9) | collective-permute-done | bytes 393248 | tf_op jit(solution)/shard_map/ppermute | solution.py:435
  47.0 5.3 %collective-permute-done.7.refs_1_ = bf16[272,768]{1,0:T(8,128)(2,1)S(1)} collective-permute-done((bf16[272,768]{1,0:T(8,128)(2,1)S(1)}, bf16[272,768]{1,0:T(8,128)(2,1)S(1)}, u32[]{:S(2)}, u32[]{:S(2)}) %collective-permute-start.7) | collective-permute-done | bytes 417824 | tf_op jit(solution)/shard_map/ppermute | solution.py:536
  52.4 1.0 shard_map.114
  53.4 2.5 %collective-permute-start.8 = (bf16[768,256]{1,0:T(8,128)(2,1)S(1)}, bf16[768,256]{1,0:T(8,128)(2,1)S(1)}, u32[]{:S(2)}, u32[]{:S(2)}) collective-permute-start(bf16[768,256]{1,0:T(8,128)(2,1)S(1)} %get-tuple-element.75), channel_id=1, source_target_pairs={{0,2},{1,5},{2,0},{3,7},{4,6},{5,1},{6,4},{7,3},{8,10},{9,13},{10,... | collective-permute-start | bytes 1179656 | tf_op jit(solution)/shard_map/ppermute | solution.py:435
  55.9 1.5 collective-permute-start.4
  57.5 8.5 %collective-permute-done.8 = bf16[768,256]{1,0:T(8,128)(2,1)S(1)} collective-permute-done((bf16[768,256]{1,0:T(8,128)(2,1)S(1)}, bf16[768,256]{1,0:T(8,128)(2,1)S(1)}, u32[]{:S(2)}, u32[]{:S(2)}) %collective-permute-start.8) | collective-permute-done | bytes 393248 | tf_op jit(solution)/shard_map/ppermute | solution.py:435
  66.0 3.7 %collective-permute-done.4.refs_1_ = bf16[272,768]{1,0:T(8,128)(2,1)S(1)} collective-permute-done((bf16[272,768]{1,0:T(8,128)(2,1)S(1)}, bf16[272,768]{1,0:T(8,128)(2,1)S(1)}, u32[]{:S(2)}, u32[]{:S(2)}) %collective-permute-start.4) | collective-permute-done | bytes 417824 | tf_op jit(solution)/shard_map/ppermute | solution.py:536
  71.0 1.0 copy-done.15
  72.0 1.0 copy-done.17
  73.0 1.0 shard_map.113
  75.0 0.9 copy-done.12
  75.9 1.1 copy-done.13
  77.8 8.9 %shard_map.116 = (f32[2,576,256]{2,1,0:T(8,128)S(1)}, f32[2,576,256]{2,1,0:T(8,128)S(1)}, f32[2,2,256]{2,1,0:T(2,128)S(1)}) custom-call(s32[4]{0:T(128)S(1)} %get-tuple-element.140.plan_ref, bf16[2,768,256]{2,1,0:T(8,128)(2,1)S(1)} %pad_maximum_fusion.1.refs_0_, bf16[2,768,256]{2,1,0:T(8,128)(2,1)} %collective-permute-done.13.refs_1_, ...), custom_call_target="tpu_custom_call" | custom-call | flops 3623878656 | bytes 14155776 | tf_op jit(solution)/shard_map/pallas_call | solution.py:347
  86.7 1.0 copy-done.10
  88.2 1.0 pad_maximum_fusion.refs_0_
  89.2 1.7 collective-permute-start.15
  92.0 9.7 %shard_map.117.hidden_ref = bf16[2,256,576]{2,1,0:T(8,128)(2,1)S(1)} custom-call(s32[4]{0:T(128)S(1)} %add_add_fusion.plan_ref, bf16[2,768,256]{2,1,0:T(8,128)(2,1)} %collective-permute-done.16.refs_0_, bf16[2,768,256]{2,1,0:T(8,128)(2,1)} %collective-permute-done.17.refs_1_, bf16[2,768,256]{2,1,0:T(8,128)(2,1)S(1)} %collective-permute-done.12.refs_2_, ...), custom_call_target="tpu_custom_call" | custom-call | flops 3623878656 | bytes 14155776 | tf_op jit(solution)/shard_map/pallas_call | solution.py:347
  101.7 7.2 %shard_map.118 = (bf16[4,256,768]{2,1,0:T(8,128)(2,1)S(1)}, bf16[4,256,768]{2,1,0:T(8,128)(2,1)S(1)}) custom-call(s32[4]{0:T(128)S(1)} %get-tuple-element.141.plan_ref, bf16[2,256,576]{2,1,0:T(8,128)(2,1)S(1)} %shard_map.117.hidden_ref, bf16[2,576,6144]{2,1,0:T(8,128)(2,1)} %down_ref.5), custom_call_target="tpu_custom_call" | custom-call | flops 1811939328 | bytes 7077888 | tf_op jit(solution)/shard_map/pallas_call | solution.py:406
  110.0 7.2 %shard_map.119 = (bf16[4,256,768]{2,1,0:T(8,128)(2,1)S(1)}, bf16[4,256,768]{2,1,0:T(8,128)(2,1)S(1)}) custom-call(s32[4]{0:T(128)S(1)} %pad_add_fusion.3.plan_ref, bf16[2,256,576]{2,1,0:T(8,128)(2,1)S(1)} %shard_map.117.hidden_ref, bf16[2,576,6144]{2,1,0:T(8,128)(2,1)} %down_ref.5), custom_call_target="tpu_custom_call" | custom-call | flops 1811939328 | bytes 7077888 | tf_op jit(solution)/shard_map/pallas_call | solution.py:406
  117.5 1.8 collective-permute-start.24
  119.8 8.9 %shard_map.120 = (f32[2,576,256]{2,1,0:T(8,128)S(1)}, f32[2,576,256]{2,1,0:T(8,128)S(1)}, f32[2,2,256]{2,1,0:T(2,128)S(1)}) custom-call(s32[4]{0:T(128)S(1)} %get-tuple-element.140.plan_ref, bf16[2,768,256]{2,1,0:T(8,128)(2,1)} %pad_maximum_fusion.refs_0_, bf16[2,768,256]{2,1,0:T(8,128)(2,1)S(1)} %collective-permute-done.22.refs_1_, ...), custom_call_target="tpu_custom_call" | custom-call | flops 3623878656 | bytes 14155776 | tf_op jit(solution)/shard_map/pallas_call | solution.py:347
  129.7 1.8 collective-permute-start.26
  131.5 1.7 collective-permute-start.27
  133.2 9.3 %shard_map.121.hidden_ref = bf16[2,256,576]{2,1,0:T(8,128)(2,1)S(1)} custom-call(s32[4]{0:T(128)S(1)} %add_add_fusion.plan_ref, bf16[2,768,256]{2,1,0:T(8,128)(2,1)} %collective-permute-done.15.refs_0_, bf16[2,768,256]{2,1,0:T(8,128)(2,1)S(1)} %collective-permute-done.20.refs_1_, bf16[2,768,256]{2,1,0:T(8,128)(2,1)} %collective-permute-done.11.refs_2_, ...), custom_call_target="tpu_custom_call" | custom-call | flops 3623878656 | bytes 14155776 | tf_op jit(solution)/shard_map/pallas_call | solution.py:347
  142.5 1.0 collective-permute-done.27
  143.5 2.4 collective-permute-done.26.refs_2_
  145.9 1.0 fusion.1
  147.7 1.4 collective-permute-start.28
  149.2 1.1 copy-done.3
  150.3 12.7 %shard_map.122 = (bf16[4,256,768]{2,1,0:T(8,128)(2,1)S(1)}, bf16[4,256,768]{2,1,0:T(8,128)(2,1)S(1)}, bf16[4,256,768]{2,1,0:T(8,128)(2,1)S(1)}, bf16[4,256,768]{2,1,0:T(8,128)(2,1)S(1)}) custom-call(s32[8]{0:T(128)S(1)} %concatenate.8.plan_ref, bf16[2,256,576]{2,1,0:T(8,128)(2,1)S(1)} %copy-done.3, bf16[2,576,6144]{2,1,0:T(8,128)(2,1)} %down_ref.5), custom_call_target="tpu_custom_call" | custom-call | flops 3623878656 | bytes 14155776 | tf_op jit(solution)/shard_map/pallas_call | solution.py:406
  163.1 1.4 shard_map.124
  165.1 2.9 %collective-permute-done.31.refs_1_ = bf16[4,256,768]{2,1,0:T(8,128)(2,1)S(1)} collective-permute-done((bf16[4,256,768]{2,1,0:T(8,128)(2,1)S(1)}, bf16[4,256,768]{2,1,0:T(8,128)(2,1)S(1)}, u32[]{:S(2)}, u32[]{:S(2)}) %collective-permute-start.31) | collective-permute-done | bytes 1572896 | tf_op jit(solution)/shard_map/ppermute | solution.py:435
  168.2 1.6 collective-permute-start.32
  169.8 5.9 %collective-permute-start.33 = (bf16[256,768]{1,0:T(8,128)(2,1)S(1)}, bf16[256,768]{1,0:T(8,128)(2,1)S(1)}, u32[]{:S(2)}, u32[]{:S(2)}) collective-permute-start(bf16[256,768]{1,0:T(8,128)(2,1)S(1)} %shard_map.123), channel_id=1, source_target_pairs={{0,16},{24,8},{1,17},{25,9},{2,18},{26,10},{3,19},{27,11},{4,20},{... | collective-permute-start | bytes 1179656 | tf_op jit(solution)/shard_map/ppermute | solution.py:613
  175.8 9.3 %collective-permute-done.33 = bf16[256,768]{1,0:T(8,128)(2,1)S(1)} collective-permute-done((bf16[256,768]{1,0:T(8,128)(2,1)S(1)}, bf16[256,768]{1,0:T(8,128)(2,1)S(1)}, u32[]{:S(2)}, u32[]{:S(2)}) %collective-permute-start.33) | collective-permute-done | bytes 393248 | tf_op jit(solution)/shard_map/ppermute | solution.py:613
  185.1 8.1 %collective-permute-done.34 = bf16[256,768]{1,0:T(8,128)(2,1)S(1)} collective-permute-done((bf16[256,768]{1,0:T(8,128)(2,1)S(1)}, bf16[256,768]{1,0:T(8,128)(2,1)S(1)}, u32[]{:S(2)}, u32[]{:S(2)}) %collective-permute-start.34) | collective-permute-done | bytes 393248 | tf_op jit(solution)/shard_map/ppermute | solution.py:435
  193.4 0.9 collective-permute-start.35
  194.5 6.7 %collective-permute-done.35 = bf16[256,768]{1,0:T(8,128)(2,1)S(1)} collective-permute-done((bf16[256,768]{1,0:T(8,128)(2,1)S(1)}, bf16[256,768]{1,0:T(8,128)(2,1)S(1)}, u32[]{:S(2)}, u32[]{:S(2)}) %collective-permute-start.35) | collective-permute-done | bytes 393248 | tf_op jit(solution)/shard_map/ppermute | solution.py:435
  202.4 10.8 %collective-permute-done.36.refs_2_ = bf16[2,256,768]{2,1,0:T(8,128)(2,1)S(1)} collective-permute-done((bf16[2,256,768]{2,1,0:T(8,128)(2,1)S(1)}, bf16[2,256,768]{2,1,0:T(8,128)(2,1)S(1)}, u32[]{:S(2)}, u32[]{:S(2)}) %collective-permute-start.36) | collective-permute-done | bytes 786464 | tf_op jit(solution)/shard_map/ppermute | solution.py:435
  213.4 0.9 collective-permute-start.37
  214.3 4.2 %collective-permute-start.39 = (bf16[256,768]{1,0:T(8,128)(2,1)S(1)}, bf16[256,768]{1,0:T(8,128)(2,1)S(1)}, u32[]{:S(2)}, u32[]{:S(2)}) collective-permute-start(bf16[256,768]{1,0:T(8,128)(2,1)S(1)} %shard_map.125), channel_id=1, source_target_pairs={{0,24},{24,0},{1,25},{25,1},{2,26},{26,2},{3,27},{27,3},{4,28},{28... | collective-permute-start | bytes 1179656 | tf_op jit(solution)/shard_map/ppermute | solution.py:626
  218.6 1.3 collective-permute-start.38
  219.9 1.4 collective-permute-done.37
  221.7 4.7 %collective-permute-done.39 = bf16[256,768]{1,0:T(8,128)(2,1)S(1)} collective-permute-done((bf16[256,768]{1,0:T(8,128)(2,1)S(1)}, bf16[256,768]{1,0:T(8,128)(2,1)S(1)}, u32[]{:S(2)}, u32[]{:S(2)}) %collective-permute-start.39) | collective-permute-done | bytes 393248 | tf_op jit(solution)/shard_map/ppermute | solution.py:626
  226.4 8.3 %collective-permute-done.38 = bf16[256,768]{1,0:T(8,128)(2,1)S(1)} collective-permute-done((bf16[256,768]{1,0:T(8,128)(2,1)S(1)}, bf16[256,768]{1,0:T(8,128)(2,1)S(1)}, u32[]{:S(2)}, u32[]{:S(2)}) %collective-permute-start.38) | collective-permute-done | bytes 393248 | tf_op jit(solution)/shard_map/ppermute | solution.py:625
  234.7 2.1 add_convert_fusion.8
  (127 shorter events, 15.6 us)
Async XLA Ops:
  2.2 10.8 %collective-permute-start = (bf16[784,128]{1,0:T(8,128)(2,1)S(1)}, bf16[784,128]{1,0:T(8,128)(2,1)S(1)}, u32[]{:S(2)}, u32[]{:S(2)}) collective-permute-start(bf16[784,128]{1,0:T(8,128)(2,1)S(1)} %get-tuple-element.72), channel_id=1, source_target_pairs={{0,8},{8,16},{16,24},{1,9},{9,17},{17,25},{2,10},{10,18},{18,26},{... | collective-permute-start | bytes 602120 | tf_op jit(solution)/shard_map/ppermute | solution.py:30
  9.9 1.0 copy-start.9
  13.0 8.9 %copy-start.7 = (bf16[256,768]{1,0:T(8,128)(2,1)S(1)}, bf16[256,768]{1,0:T(8,128)(2,1)}, u32[]{:S(2)}) copy-start(bf16[256,768]{1,0:T(8,128)(2,1)} %query_ref.3) | copy-start | bytes 1179652
  13.0 8.9 %copy-start.21 = (bf16[256,768]{1,0:T(8,128)(2,1)S(1)}, bf16[256,768]{1,0:T(8,128)(2,1)}, u32[]{:S(2)}) copy-start(bf16[256,768]{1,0:T(8,128)(2,1)} %residual_ref.1) | copy-start | bytes 1179652
  13.0 8.9 %copy-start.31 = (s32[256,2]{0,1:T(2,128)S(1)}, s32[256,2]{0,1:T(2,128)}, u32[]{:S(2)}) copy-start(s32[256,2]{0,1:T(2,128)} %param.17) | copy-start | bytes 6148
  13.3 8.5 %collective-permute-start.1 = (bf16[784,128]{1,0:T(8,128)(2,1)S(1)}, bf16[784,128]{1,0:T(8,128)(2,1)S(1)}, u32[]{:S(2)}, u32[]{:S(2)}) collective-permute-start(bf16[784,128]{1,0:T(8,128)(2,1)S(1)} %concatenate.7), channel_id=1, source_target_pairs={{0,16},{8,24},{1,17},{9,25},{2,18},{10,26},{3,19},{11,27},{4,20},{... | collective-permute-start | bytes 602120 | tf_op jit(solution)/shard_map/ppermute | solution.py:30
  22.7 24.3 %copy-start = (bf16[272,768]{1,0:T(8,128)(2,1)}, bf16[272,768]{1,0:T(8,128)(2,1)S(1)}, u32[]{:S(2)}) copy-start(bf16[272,768]{1,0:T(8,128)(2,1)S(1)} %shard_map.111.refs_0_) | copy-start | bytes 1253380
  23.8 10.3 %copy-start.22 = (bf16[256,256]{1,0:T(8,128)(2,1)}, bf16[256,256]{1,0:T(8,128)(2,1)S(1)}, u32[]{:S(2)}) copy-start(bf16[256,256]{1,0:T(8,128)(2,1)S(1)} %get-tuple-element.73.place_ref) | copy-start | bytes 393220
  23.8 7.8 %collective-permute-start.10 = (bf16[768,256]{1,0:T(8,128)(2,1)S(1)}, bf16[768,256]{1,0:T(8,128)(2,1)S(1)}, u32[]{:S(2)}, u32[]{:S(2)}) collective-permute-start(bf16[768,256]{1,0:T(8,128)(2,1)S(1)} %get-tuple-element.77), channel_id=1, source_target_pairs={{0,2},{1,5},{2,0},{3,7},{4,6},{5,1},{6,4},{7,3},{8,10},{9,13},{10,... | collective-permute-start | bytes 1179656 | tf_op jit(solution)/shard_map/ppermute | solution.py:435
  25.3 12.7 %collective-permute-start.2 = (bf16[272,768]{1,0:T(8,128)(2,1)S(1)}, bf16[272,768]{1,0:T(8,128)(2,1)S(1)}, u32[]{:S(2)}, u32[]{:S(2)}) collective-permute-start(bf16[272,768]{1,0:T(8,128)(2,1)S(1)} %shard_map.111.refs_0_), channel_id=1, source_target_pairs={{0,8},{8,0},{16,24},{24,16},{1,9},{9,1},{17,25},{25,17},{2,10},{10... | collective-permute-start | bytes 1253384 | tf_op jit(solution)/shard_map/ppermute | solution.py:435
  29.8 10.8 %collective-permute-start.6 = (bf16[272,768]{1,0:T(8,128)(2,1)S(1)}, bf16[272,768]{1,0:T(8,128)(2,1)S(1)}, u32[]{:S(2)}, u32[]{:S(2)}) collective-permute-start(bf16[272,768]{1,0:T(8,128)(2,1)S(1)} %shard_map.111.refs_0_), channel_id=1, source_target_pairs={{8,16},{16,8},{9,17},{17,9},{10,18},{18,10},{11,19},{19,11},{12,20... | collective-permute-start | bytes 1253384 | tf_op jit(solution)/shard_map/ppermute | solution.py:533
  32.6 19.7 %collective-permute-start.11 = (bf16[2,768,256]{2,1,0:T(8,128)(2,1)}, bf16[2,768,256]{2,1,0:T(8,128)(2,1)}, u32[]{:S(2)}, u32[]{:S(2)}) collective-permute-start(bf16[2,768,256]{2,1,0:T(8,128)(2,1)} %pad_maximum_fusion.3.refs_2_), channel_id=1, source_target_pairs={{0,4},{1,3},{2,6},{3,1},{4,0},{5,7},{6,2},{7,5},{8,12},{9,11},{10,... | collective-permute-start | bytes 2359304 | tf_op jit(solution)/shard_map/ppermute | solution.py:435
  39.1 27.0 %copy-start.24 = (bf16[256,256]{1,0:T(8,128)(2,1)}, bf16[256,256]{1,0:T(8,128)(2,1)S(1)}, u32[]{:S(2)}) copy-start(bf16[256,256]{1,0:T(8,128)(2,1)S(1)} %get-tuple-element.129.place_ref) | copy-start | bytes 393220
  39.1 7.8 %collective-permute-start.9 = (bf16[768,256]{1,0:T(8,128)(2,1)S(1)}, bf16[768,256]{1,0:T(8,128)(2,1)S(1)}, u32[]{:S(2)}, u32[]{:S(2)}) collective-permute-start(bf16[768,256]{1,0:T(8,128)(2,1)S(1)} %get-tuple-element.76), channel_id=1, source_target_pairs={{0,2},{1,5},{2,0},{3,7},{4,6},{5,1},{6,4},{7,3},{8,10},{9,13},{10,... | collective-permute-start | bytes 1179656 | tf_op jit(solution)/shard_map/ppermute | solution.py:435
  40.6 11.6 %collective-permute-start.7 = (bf16[272,768]{1,0:T(8,128)(2,1)S(1)}, bf16[272,768]{1,0:T(8,128)(2,1)S(1)}, u32[]{:S(2)}, u32[]{:S(2)}) collective-permute-start(bf16[272,768]{1,0:T(8,128)(2,1)S(1)} %collective-permute-done.6.refs_0_), channel_id=1, source_target_pairs={{8,0},{16,24},{9,1},{17,25},{10,2},{18,26},{11,3},{19,27},{12,4},{... | collective-permute-start | bytes 1253384 | tf_op jit(solution)/shard_map/ppermute | solution.py:536
  41.9 10.4 %collective-permute-start.3 = (bf16[272,768]{1,0:T(8,128)(2,1)S(1)}, bf16[272,768]{1,0:T(8,128)(2,1)S(1)}, u32[]{:S(2)}, u32[]{:S(2)}) collective-permute-start(bf16[272,768]{1,0:T(8,128)(2,1)S(1)} %collective-permute-done.2.refs_0_), channel_id=1, source_target_pairs={{8,16},{16,8},{9,17},{17,9},{10,18},{18,10},{11,19},{19,11},{12,20... | collective-permute-start | bytes 1253384 | tf_op jit(solution)/shard_map/ppermute | solution.py:533
  52.3 18.3 %copy-start.14 = (bf16[272,768]{1,0:T(8,128)(2,1)}, bf16[272,768]{1,0:T(8,128)(2,1)S(1)}, u32[]{:S(2)}) copy-start(bf16[272,768]{1,0:T(8,128)(2,1)S(1)} %collective-permute-done.3.refs_0_) | copy-start | bytes 1253380
  52.3 18.2 %collective-permute-start.12 = (bf16[2,768,256]{2,1,0:T(8,128)(2,1)S(1)}, bf16[2,768,256]{2,1,0:T(8,128)(2,1)S(1)}, u32[]{:S(2)}, u32[]{:S(2)}) collective-permute-start(bf16[2,768,256]{2,1,0:T(8,128)(2,1)S(1)} %pad_maximum_fusion.2.refs_2_), channel_id=1, source_target_pairs={{0,4},{1,3},{2,6},{3,1},{4,0},{5,7},{6,2},{7,5},{8,12},{9,11},{10,... | collective-permute-start | bytes 2359304 | tf_op jit(solution)/shard_map/ppermute | solution.py:435
  53.4 17.1 %copy-start.28 = (bf16[256,256]{1,0:T(8,128)(2,1)}, bf16[256,256]{1,0:T(8,128)(2,1)S(1)}, u32[]{:S(2)}) copy-start(bf16[256,256]{1,0:T(8,128)(2,1)S(1)} %get-tuple-element.127.place_ref) | copy-start | bytes 393220
  53.4 12.5 %collective-permute-start.8 = (bf16[768,256]{1,0:T(8,128)(2,1)S(1)}, bf16[768,256]{1,0:T(8,128)(2,1)S(1)}, u32[]{:S(2)}, u32[]{:S(2)}) collective-permute-start(bf16[768,256]{1,0:T(8,128)(2,1)S(1)} %get-tuple-element.75), channel_id=1, source_target_pairs={{0,2},{1,5},{2,0},{3,7},{4,6},{5,1},{6,4},{7,3},{8,10},{9,13},{10,... | collective-permute-start | bytes 1179656 | tf_op jit(solution)/shard_map/ppermute | solution.py:435
  55.9 13.8 %collective-permute-start.4 = (bf16[272,768]{1,0:T(8,128)(2,1)S(1)}, bf16[272,768]{1,0:T(8,128)(2,1)S(1)}, u32[]{:S(2)}, u32[]{:S(2)}) collective-permute-start(bf16[272,768]{1,0:T(8,128)(2,1)S(1)} %collective-permute-done.3.refs_0_), channel_id=1, source_target_pairs={{8,0},{16,24},{9,1},{17,25},{10,2},{18,26},{11,3},{19,27},{12,4},{... | collective-permute-start | bytes 1253384 | tf_op jit(solution)/shard_map/ppermute | solution.py:536
  57.4 17.6 %collective-permute-start.14 = (bf16[2,768,256]{2,1,0:T(8,128)(2,1)S(1)}, bf16[2,768,256]{2,1,0:T(8,128)(2,1)S(1)}, u32[]{:S(2)}, u32[]{:S(2)}) collective-permute-start(bf16[2,768,256]{2,1,0:T(8,128)(2,1)S(1)} %pad_maximum_fusion.2.refs_2_), channel_id=1, source_target_pairs={{0,1},{1,0},{2,3},{3,2},{4,5},{5,4},{6,7},{7,6},{8,9},{9,8},{10,11... | collective-permute-start | bytes 2359304 | tf_op jit(solution)/shard_map/ppermute | solution.py:435
  70.5 5.4 %collective-permute-start.13 = (bf16[2,768,256]{2,1,0:T(8,128)(2,1)S(1)}, bf16[2,768,256]{2,1,0:T(8,128)(2,1)}, u32[]{:S(2)}, u32[]{:S(2)}) collective-permute-start(bf16[2,768,256]{2,1,0:T(8,128)(2,1)S(1)} %pad_maximum_fusion.1.refs_0_), channel_id=1, source_target_pairs={{0,1},{1,0},{2,3},{3,2},{4,5},{5,4},{6,7},{7,6},{8,9},{9,8},{10,11... | collective-permute-start | bytes 2359304 | tf_op jit(solution)/shard_map/ppermute | solution.py:435
  70.5 17.1 %collective-permute-start.16 = (bf16[2,768,256]{2,1,0:T(8,128)(2,1)S(1)}, bf16[2,768,256]{2,1,0:T(8,128)(2,1)}, u32[]{:S(2)}, u32[]{:S(2)}) collective-permute-start(bf16[2,768,256]{2,1,0:T(8,128)(2,1)S(1)} %pad_maximum_fusion.1.refs_0_), channel_id=1, source_target_pairs={{0,4},{1,3},{2,6},{3,1},{4,0},{5,7},{6,2},{7,5},{8,12},{9,11},{10,... | collective-permute-start | bytes 2359304 | tf_op jit(solution)/shard_map/ppermute | solution.py:435
  71.0 1.0 copy-start.15
  72.0 1.0 copy-start.17
  74.7 13.5 %collective-permute-start.5 = (bf16[768,256]{1,0:T(8,128)(2,1)S(1)}, bf16[768,256]{1,0:T(8,128)(2,1)S(1)}, u32[]{:S(2)}, u32[]{:S(2)}) collective-permute-start(bf16[768,256]{1,0:T(8,128)(2,1)S(1)} %get-tuple-element.74), channel_id=1, source_target_pairs={{0,2},{1,5},{2,0},{3,7},{4,6},{5,1},{6,4},{7,3},{8,10},{9,13},{10,... | collective-permute-start | bytes 1179656 | tf_op jit(solution)/shard_map/ppermute | solution.py:435
  75.9 1.1 copy-start.13
  86.7 1.0 copy-start.10
  87.7 3.5 %copy-start.11 = (f32[2,576,256]{2,1,0:T(8,128)S(1)}, f32[2,576,256]{2,1,0:T(8,128)}, u32[]{:S(2)}) copy-start(f32[2,576,256]{2,1,0:T(8,128)} %copy-done.10) | copy-start | bytes 3538948
  87.7 3.3 %collective-permute-start.17 = (bf16[2,768,256]{2,1,0:T(8,128)(2,1)}, bf16[2,768,256]{2,1,0:T(8,128)(2,1)}, u32[]{:S(2)}, u32[]{:S(2)}) collective-permute-start(bf16[2,768,256]{2,1,0:T(8,128)(2,1)} %collective-permute-done.16.refs_0_), channel_id=1, source_target_pairs={{0,1},{1,0},{2,3},{3,2},{4,5},{5,4},{6,7},{7,6},{8,9},{9,8},{10,11... | collective-permute-start | bytes 2359304 | tf_op jit(solution)/shard_map/ppermute | solution.py:435
  87.7 3.5 %collective-permute-start.18 = (bf16[2,768,256]{2,1,0:T(8,128)(2,1)S(1)}, bf16[2,768,256]{2,1,0:T(8,128)(2,1)}, u32[]{:S(2)}, u32[]{:S(2)}) collective-permute-start(bf16[2,768,256]{2,1,0:T(8,128)(2,1)S(1)} %collective-permute-done.12.refs_2_), channel_id=1, source_target_pairs={{0,1},{1,0},{2,3},{3,2},{4,5},{5,4},{6,7},{7,6},{8,9},{9,8},{10,11... | collective-permute-start | bytes 2359304 | tf_op jit(solution)/shard_map/ppermute | solution.py:435
  89.2 12.5 %collective-permute-start.15 = (bf16[2,768,256]{2,1,0:T(8,128)(2,1)}, bf16[2,768,256]{2,1,0:T(8,128)(2,1)}, u32[]{:S(2)}, u32[]{:S(2)}) collective-permute-start(bf16[2,768,256]{2,1,0:T(8,128)(2,1)} %pad_maximum_fusion.refs_0_), channel_id=1, source_target_pairs={{0,4},{1,3},{2,6},{3,1},{4,0},{5,7},{6,2},{7,5},{8,12},{9,11},{10,... | collective-permute-start | bytes 2359304 | tf_op jit(solution)/shard_map/ppermute | solution.py:435
  108.9 8.4 %collective-permute-start.19 = (bf16[4,256,768]{2,1,0:T(8,128)(2,1)S(1)}, bf16[4,256,768]{2,1,0:T(8,128)(2,1)S(1)}, u32[]{:S(2)}, u32[]{:S(2)}) collective-permute-start(bf16[4,256,768]{2,1,0:T(8,128)(2,1)S(1)} %get-tuple-element.99), channel_id=1, source_target_pairs={{0,1},{1,0},{2,3},{3,2},{4,5},{5,4},{6,7},{7,6},{8,9},{9,8},{10,11... | collective-permute-start | bytes 4718600 | tf_op jit(solution)/shard_map/ppermute | solution.py:435
  109.1 19.6 %collective-permute-start.25 = (bf16[4,256,768]{2,1,0:T(8,128)(2,1)S(1)}, bf16[4,256,768]{2,1,0:T(8,128)(2,1)S(1)}, u32[]{:S(2)}, u32[]{:S(2)}) collective-permute-start(bf16[4,256,768]{2,1,0:T(8,128)(2,1)S(1)} %get-tuple-element.100), channel_id=1, source_target_pairs={{0,1},{1,0},{2,3},{3,2},{4,5},{5,4},{6,7},{7,6},{8,9},{9,8},{10,11... | collective-permute-start | bytes 4718600 | tf_op jit(solution)/shard_map/ppermute | solution.py:435
  109.5 9.8 %collective-permute-start.23 = (bf16[2,768,256]{2,1,0:T(8,128)(2,1)}, bf16[2,768,256]{2,1,0:T(8,128)(2,1)S(1)}, u32[]{:S(2)}, u32[]{:S(2)}) collective-permute-start(bf16[2,768,256]{2,1,0:T(8,128)(2,1)} %pad_maximum_fusion.3.refs_2_), channel_id=1, source_target_pairs={{0,1},{1,0},{2,3},{3,2},{4,5},{5,4},{6,7},{7,6},{8,9},{9,8},{10,11... | collective-permute-start | bytes 2359304 | tf_op jit(solution)/shard_map/ppermute | solution.py:435
  109.6 9.7 %collective-permute-start.22 = (bf16[2,768,256]{2,1,0:T(8,128)(2,1)}, bf16[2,768,256]{2,1,0:T(8,128)(2,1)S(1)}, u32[]{:S(2)}, u32[]{:S(2)}) collective-permute-start(bf16[2,768,256]{2,1,0:T(8,128)(2,1)} %pad_maximum_fusion.refs_0_), channel_id=1, source_target_pairs={{0,1},{1,0},{2,3},{3,2},{4,5},{5,4},{6,7},{7,6},{8,9},{9,8},{10,11... | collective-permute-start | bytes 2359304 | tf_op jit(solution)/shard_map/ppermute | solution.py:435
  117.3 2.5 %copy-start.20 = (bf16[6144,2]{0,1:T(2,128)(2,1)S(1)}, bf16[6144,2]{0,1:T(2,128)(2,1)}, u32[]{:S(2)}) copy-start(bf16[6144,2]{0,1:T(2,128)(2,1)} %param.18) | copy-start | bytes 73732
  117.5 12.1 %collective-permute-start.24 = (bf16[2,256,768]{2,1,0:T(8,128)(2,1)S(1)}, bf16[2,256,768]{2,1,0:T(8,128)(2,1)S(1)}, u32[]{:S(2)}, u32[]{:S(2)}) collective-permute-start(bf16[2,256,768]{2,1,0:T(8,128)(2,1)S(1)} %add_convert_fusion.3), channel_id=1, source_target_pairs={{0,4},{1,3},{2,6},{3,1},{4,0},{5,7},{6,2},{7,5},{8,12},{9,11},{10,... | collective-permute-start | bytes 2359304 | tf_op jit(solution)/shard_map/ppermute | solution.py:435
  119.3 13.9 %collective-permute-start.20 = (bf16[2,768,256]{2,1,0:T(8,128)(2,1)}, bf16[2,768,256]{2,1,0:T(8,128)(2,1)S(1)}, u32[]{:S(2)}, u32[]{:S(2)}) collective-permute-start(bf16[2,768,256]{2,1,0:T(8,128)(2,1)} %collective-permute-done.15.refs_0_), channel_id=1, source_target_pairs={{0,1},{1,0},{2,3},{3,2},{4,5},{5,4},{6,7},{7,6},{8,9},{9,8},{10,11... | collective-permute-start | bytes 2359304 | tf_op jit(solution)/shard_map/ppermute | solution.py:435
  119.3 13.9 %collective-permute-start.21 = (bf16[2,768,256]{2,1,0:T(8,128)(2,1)}, bf16[2,768,256]{2,1,0:T(8,128)(2,1)S(1)}, u32[]{:S(2)}, u32[]{:S(2)}) collective-permute-start(bf16[2,768,256]{2,1,0:T(8,128)(2,1)} %collective-permute-done.11.refs_2_), channel_id=1, source_target_pairs={{0,1},{1,0},{2,3},{3,2},{4,5},{5,4},{6,7},{7,6},{8,9},{9,8},{10,11... | collective-permute-start | bytes 2359304 | tf_op jit(solution)/shard_map/ppermute | solution.py:435
  129.7 16.2 %collective-permute-start.26 = (bf16[2,256,768]{2,1,0:T(8,128)(2,1)S(1)}, bf16[2,256,768]{2,1,0:T(8,128)(2,1)S(1)}, u32[]{:S(2)}, u32[]{:S(2)}) collective-permute-start(bf16[2,256,768]{2,1,0:T(8,128)(2,1)S(1)} %add_convert_fusion.2), channel_id=1, source_target_pairs={{0,4},{1,3},{2,6},{3,1},{4,0},{5,7},{6,2},{7,5},{8,12},{9,11},{10,... | collective-permute-start | bytes 2359304 | tf_op jit(solution)/shard_map/ppermute | solution.py:435
  131.5 12.1 %collective-permute-start.27 = (bf16[256,768]{1,0:T(8,128)(2,1)S(1)}, bf16[256,768]{1,0:T(8,128)(2,1)S(1)}, u32[]{:S(2)}, u32[]{:S(2)}) collective-permute-start(bf16[256,768]{1,0:T(8,128)(2,1)S(1)} %fusion), channel_id=1, source_target_pairs={{0,2},{1,5},{2,0},{3,7},{4,6},{5,1},{6,4},{7,3},{8,10},{9,13},{10,... | collective-permute-start | bytes 1179656 | tf_op jit(solution)/shard_map/ppermute | solution.py:435
  142.5 5.1 %copy-start.2 = (bf16[2,256,576]{2,1,0:T(8,128)(2,1)}, bf16[2,256,576]{2,1,0:T(8,128)(2,1)S(1)}, u32[]{:S(2)}) copy-start(bf16[2,256,576]{2,1,0:T(8,128)(2,1)S(1)} %shard_map.121.hidden_ref) | copy-start | bytes 1769476
  142.5 4.7 %copy-start.29 = (bf16[256,256]{1,0:T(8,128)(2,1)S(1)}, bf16[256,256]{1,0:T(8,128)(2,1)}, u32[]{:S(2)}) copy-start(bf16[256,256]{1,0:T(8,128)(2,1)} %copy-done.28) | copy-start | bytes 393220
  145.9 1.8 copy-start.4
  146.9 16.2 %collective-permute-start.29 = (bf16[256,768]{1,0:T(8,128)(2,1)}, bf16[256,768]{1,0:T(8,128)(2,1)}, u32[]{:S(2)}, u32[]{:S(2)}) collective-permute-start(bf16[256,768]{1,0:T(8,128)(2,1)} %fusion.1), channel_id=1, source_target_pairs={{0,2},{1,5},{2,0},{3,7},{4,6},{5,1},{6,4},{7,3},{8,10},{9,13},{10,... | collective-permute-start | bytes 1179656 | tf_op jit(solution)/shard_map/ppermute | solution.py:435
  147.7 16.8 %collective-permute-start.28 = (bf16[256,768]{1,0:T(8,128)(2,1)S(1)}, bf16[256,768]{1,0:T(8,128)(2,1)}, u32[]{:S(2)}, u32[]{:S(2)}) collective-permute-start(bf16[256,768]{1,0:T(8,128)(2,1)S(1)} %shard_map.123), channel_id=1, source_target_pairs={{8,16},{16,8},{9,17},{17,9},{10,18},{18,10},{11,19},{19,11},{12,20... | collective-permute-start | bytes 1179656 | tf_op jit(solution)/shard_map/ppermute | solution.py:608
  149.2 1.1 copy-start.3
  150.3 12.7 %copy-start.5 = (bf16[2,256,768]{2,1,0:T(8,128)(2,1)S(1)}, bf16[2,256,768]{2,1,0:T(8,128)(2,1)}, u32[]{:S(2)}) copy-start(bf16[2,256,768]{2,1,0:T(8,128)(2,1)} %copy-done.4) | copy-start | bytes 2359300
  150.3 12.8 %copy-start.25 = (bf16[256,256]{1,0:T(8,128)(2,1)S(1)}, bf16[256,256]{1,0:T(8,128)(2,1)}, u32[]{:S(2)}) copy-start(bf16[256,256]{1,0:T(8,128)(2,1)} %copy-done.24) | copy-start | bytes 393220
  164.5 3.5 %collective-permute-start.31 = (bf16[4,256,768]{2,1,0:T(8,128)(2,1)S(1)}, bf16[4,256,768]{2,1,0:T(8,128)(2,1)S(1)}, u32[]{:S(2)}, u32[]{:S(2)}) collective-permute-start(bf16[4,256,768]{2,1,0:T(8,128)(2,1)S(1)} %get-tuple-element.132), channel_id=1, source_target_pairs={{0,1},{1,0},{2,3},{3,2},{4,5},{5,4},{6,7},{7,6},{8,9},{9,8},{10,11... | collective-permute-start | bytes 4718600 | tf_op jit(solution)/shard_map/ppermute | solution.py:435
  164.6 29.7 %collective-permute-start.30 = (bf16[4,256,768]{2,1,0:T(8,128)(2,1)S(1)}, bf16[4,256,768]{2,1,0:T(8,128)(2,1)S(1)}, u32[]{:S(2)}, u32[]{:S(2)}) collective-permute-start(bf16[4,256,768]{2,1,0:T(8,128)(2,1)S(1)} %get-tuple-element.130), channel_id=1, source_target_pairs={{0,1},{1,0},{2,3},{3,2},{4,5},{5,4},{6,7},{7,6},{8,9},{9,8},{10,11... | collective-permute-start | bytes 4718600 | tf_op jit(solution)/shard_map/ppermute | solution.py:435
  168.2 25.0 %collective-permute-start.32 = (bf16[2,256,768]{2,1,0:T(8,128)(2,1)S(1)}, bf16[2,256,768]{2,1,0:T(8,128)(2,1)S(1)}, u32[]{:S(2)}, u32[]{:S(2)}) collective-permute-start(bf16[2,256,768]{2,1,0:T(8,128)(2,1)S(1)} %add_convert_fusion), channel_id=1, source_target_pairs={{0,4},{1,3},{2,6},{3,1},{4,0},{5,7},{6,2},{7,5},{8,12},{9,11},{10,... | collective-permute-start | bytes 2359304 | tf_op jit(solution)/shard_map/ppermute | solution.py:435
  169.8 15.3 %collective-permute-start.33 = (bf16[256,768]{1,0:T(8,128)(2,1)S(1)}, bf16[256,768]{1,0:T(8,128)(2,1)S(1)}, u32[]{:S(2)}, u32[]{:S(2)}) collective-permute-start(bf16[256,768]{1,0:T(8,128)(2,1)S(1)} %shard_map.123), channel_id=1, source_target_pairs={{0,16},{24,8},{1,17},{25,9},{2,18},{26,10},{3,19},{27,11},{4,20},{... | collective-permute-start | bytes 1179656 | tf_op jit(solution)/shard_map/ppermute | solution.py:613
  175.7 17.5 %collective-permute-start.34 = (bf16[256,768]{1,0:T(8,128)(2,1)S(1)}, bf16[256,768]{1,0:T(8,128)(2,1)S(1)}, u32[]{:S(2)}, u32[]{:S(2)}) collective-permute-start(bf16[256,768]{1,0:T(8,128)(2,1)S(1)} %shard_map.124), channel_id=1, source_target_pairs={{0,8},{8,0},{16,24},{24,16},{1,9},{9,1},{17,25},{25,17},{2,10},{10... | collective-permute-start | bytes 1179656 | tf_op jit(solution)/shard_map/ppermute | solution.py:435
  193.4 8.6 %copy-start.27 = (bf16[256,256]{1,0:T(8,128)(2,1)S(1)}, bf16[256,256]{1,0:T(8,128)(2,1)}, u32[]{:S(2)}) copy-start(bf16[256,256]{1,0:T(8,128)(2,1)} %copy-done.26) | copy-start | bytes 393220
  193.4 7.8 %collective-permute-start.35 = (bf16[256,768]{1,0:T(8,128)(2,1)S(1)}, bf16[256,768]{1,0:T(8,128)(2,1)S(1)}, u32[]{:S(2)}, u32[]{:S(2)}) collective-permute-start(bf16[256,768]{1,0:T(8,128)(2,1)S(1)} %fusion.2), channel_id=1, source_target_pairs={{0,2},{1,5},{2,0},{3,7},{4,6},{5,1},{6,4},{7,3},{8,10},{9,13},{10,... | collective-permute-start | bytes 1179656 | tf_op jit(solution)/shard_map/ppermute | solution.py:435
  201.2 12.0 %collective-permute-start.36 = (bf16[2,256,768]{2,1,0:T(8,128)(2,1)S(1)}, bf16[2,256,768]{2,1,0:T(8,128)(2,1)S(1)}, u32[]{:S(2)}, u32[]{:S(2)}) collective-permute-start(bf16[2,256,768]{2,1,0:T(8,128)(2,1)S(1)} %add_convert_fusion.1), channel_id=1, source_target_pairs={{0,4},{1,3},{2,6},{3,1},{4,0},{5,7},{6,2},{7,5},{8,12},{9,11},{10,... | collective-permute-start | bytes 2359304 | tf_op jit(solution)/shard_map/ppermute | solution.py:435
  202.4 18.8 %copy-start.23 = (bf16[256,256]{1,0:T(8,128)(2,1)S(1)}, bf16[256,256]{1,0:T(8,128)(2,1)}, u32[]{:S(2)}) copy-start(bf16[256,256]{1,0:T(8,128)(2,1)} %copy-done.22) | copy-start | bytes 393220
  213.4 7.8 %collective-permute-start.37 = (bf16[256,768]{1,0:T(8,128)(2,1)S(1)}, bf16[256,768]{1,0:T(8,128)(2,1)S(1)}, u32[]{:S(2)}, u32[]{:S(2)}) collective-permute-start(bf16[256,768]{1,0:T(8,128)(2,1)S(1)} %fusion.3), channel_id=1, source_target_pairs={{0,2},{1,5},{2,0},{3,7},{4,6},{5,1},{6,4},{7,3},{8,10},{9,13},{10,... | collective-permute-start | bytes 1179656 | tf_op jit(solution)/shard_map/ppermute | solution.py:435
  214.3 12.1 %collective-permute-start.39 = (bf16[256,768]{1,0:T(8,128)(2,1)S(1)}, bf16[256,768]{1,0:T(8,128)(2,1)S(1)}, u32[]{:S(2)}, u32[]{:S(2)}) collective-permute-start(bf16[256,768]{1,0:T(8,128)(2,1)S(1)} %shard_map.125), channel_id=1, source_target_pairs={{0,24},{24,0},{1,25},{25,1},{2,26},{26,2},{3,27},{27,3},{4,28},{28... | collective-permute-start | bytes 1179656 | tf_op jit(solution)/shard_map/ppermute | solution.py:626
  218.6 16.2 %collective-permute-start.38 = (bf16[256,768]{1,0:T(8,128)(2,1)S(1)}, bf16[256,768]{1,0:T(8,128)(2,1)S(1)}, u32[]{:S(2)}, u32[]{:S(2)}) collective-permute-start(bf16[256,768]{1,0:T(8,128)(2,1)S(1)} %shard_map.125), channel_id=1, source_target_pairs={{8,24},{16,0},{9,25},{17,1},{10,26},{18,2},{11,27},{19,3},{12,28},... | collective-permute-start | bytes 1179656 | tf_op jit(solution)/shard_map/ppermute | solution.py:625
  221.2 13.5 %copy-start.1 = (bf16[272,768]{1,0:T(8,128)(2,1)S(1)}, bf16[272,768]{1,0:T(8,128)(2,1)}, u32[]{:S(2)}) copy-start(bf16[272,768]{1,0:T(8,128)(2,1)} %copy-done) | copy-start | bytes 1253380
  (8 other events, 6.5 us)

commit v12 on v11

--- a/solution.py
+++ b/solution.py
@@ -547,11 +547,9 @@
     passed = outward(crossed)
     crossed_swap = across_middle(swap)
     chosen["neighbour"] = select(swap)
-    gather("neighbour", [passed, crossed_swap, far_two["own"]])
-    passed_fourth = outward(crossed_swap)
+    gather("neighbour", [passed, crossed_swap])
+    passed_swap = outward(crossed_swap)
     chosen["third"] = select(crossed, passed)
-    gather("third", [passed_fourth, far_two["neighbour"]])
-    chosen["fourth"] = select(crossed_swap, passed_fourth)
 
     def gate(chunk, behind):
         early = [[two[name], near[name]] for name in chunk]
@@ -585,43 +583,44 @@
             shares = [self.mine, self.near, self.got_two, got_one[None]]
             return combine_slots(chosen[self.name][1], shares)
 
-    chunk = ("third", "neighbour")
-    sums = gate(chunk, chosen["fourth"])
-    gather("fourth", sums)
+    chunk = ("neighbour", "own")
+    gather("third", [])
+    sums = gate(chunk, two["third"])
     for name in chunk:
         near_far[name] = plane.across(tie((far_two[name], sums))[0])
-    hidden = gate_last(chunk, sums, two["fourth"])
-    (theirs,) = down([plane.theirs], hidden, far_two["fourth"])
-    (mine,) = down([plane.mine], hidden, theirs)
-    third, neighbour = (Scatter(*shares) for shares in zip(chunk, theirs, mine))
+    chosen["fourth"] = select(crossed_swap, passed_swap)
+    hidden = gate_last(chunk, sums, [far_two["third"], chosen["fourth"]])
+    gather("fourth", hidden)
+    theirs, mine = down([plane.theirs, plane.mine], hidden, two["fourth"])
+    theirs, _ = tie((theirs, far_two["fourth"]))
+    neighbour, own = (Scatter(*shares) for shares in zip(chunk, theirs, mine))
+    neighbour.two_blocks([])
+
+    chunk = ("third", "fourth")
+    sums = gate(chunk, neighbour.sent)
+    for name in chunk:
+        near_far[name] = plane.across(tie((far_two[name], neighbour.sent))[0])
+    neighbour.one_block(sums)
+    own.two_blocks(neighbour.one)
+    hidden = gate_last(chunk, sums, [neighbour.one, own.sent])
+    neighbour_piece = neighbour.own_block(hidden)
+    own.one_block(hidden)
+    neighbour_home = swapped(neighbour_piece, "seq", 1, 1)
+    theirs, mine = down([plane.theirs, plane.mine], hidden, [neighbour_piece, own.one])
+    own_piece = own.own_block([])
+    theirs, _ = tie((theirs, [neighbour_home, own_piece]))
+    third, fourth = (Scatter(*shares) for shares in zip(chunk, theirs, mine))
     third.two_blocks([])
-
-    chunk = ("fourth", "own")
-    sums = gate(chunk, third.sent)
-    for name in chunk:
-        near_far[name] = plane.across(tie((far_two[name], third.sent))[0])
-    third.one_block(sums)
-    neighbour.two_blocks(third.one)
-    hidden = gate_last(chunk, sums, [third.one, neighbour.sent])
-    third_piece = third.own_block(hidden)
-    neighbour.one_block(hidden)
-    third_home = lax.ppermute(third_piece, "seq", [(1, 2), (2, 1)])
-    theirs, mine = down([plane.theirs, plane.mine], hidden, neighbour.one)
-    neighbour_piece = neighbour.own_block([])
-    theirs, _ = tie((theirs, [third_home, neighbour_piece]))
-    fourth, own = (Scatter(*shares) for shares in zip(chunk, theirs, mine))
-    third_far_home = lax.ppermute(tie((third_piece, third_home))[0], "seq", [(0, 2), (3, 1)])
-    neighbour_home = swapped(neighbour_piece, "seq", 1, 1)
-    fourth.two_blocks([])
-    fourth.one_block([third_far_home, neighbour_home])
-    own.two_blocks(fourth.got_one)
+    third.one_block([])
+    fourth.two_blocks(third.got_two)
+    fourth.one_block([])
+    third_piece = third.own_block([])
     fourth_piece = fourth.own_block([])
-    own.one_block(fourth_piece)
     return [
-        own.own_block([]),
+        own_piece,
         neighbour_home,
-        third_home,
-        third_far_home,
+        lax.ppermute(third_piece, "seq", [(1, 2), (2, 1)]),
+        lax.ppermute(third_piece, "seq", [(0, 2), (3, 1)]),
         lax.ppermute(fourth_piece, "seq", [(1, 3), (2, 0)]),
         lax.ppermute(fourth_piece, "seq", [(0, 3), (3, 0)]),
     ]

time: 238 us -> 241 us (1.013)
  waiting for transfers between devices: 87.3 us -> 96.7 us
  local copies, waits for them, and re-layouts: 13.8 us -> 8.01 us
  starting transfers between devices: 53.1 us -> 56.2 us
    ppermute x30, waiting for transfers between devices: 52.1 us -> 62.3 us  [swapped(): return lax.ppermute(array, axis, pairs)]
    ppermute x2, waiting for transfers between devices: 9.3 us -> 0.01 us  [the longest x1 0.01 us: paired_chunks(): lax.ppermute(third_piece, 'seq', [(1, 2), (2, 1)])]
    ppermute x1, waiting for transfers between devices: 8.33 us -> 16.7 us  [paired_chunks(): lax.ppermute(fourth_piece, 'seq', [(1, 3), (2, 0)])]
    unnamed x64 -> x40, local copies, waits for them, and re-layouts: 12.8 us -> 7.07 us
    ppermute x30, starting transfers between devices: 26.7 us -> 32.3 us  [swapped(): return lax.ppermute(array, axis, pairs)]
    ppermute x2, starting transfers between devices: 7.33 us -> 3.79 us  [the longest x1 3.11 us: paired_chunks(): lax.ppermute(third_piece, 'seq', [(0, 2), (3, 1)])]
    ppermute x2, waiting for transfers between devices: 8.98 us -> 5.5 us  [outward(): return lax.ppermute(part, 'seq', [(1, 0), (2, 3)])]
    ppermute x1, waiting for transfers between devices: 4.7 us -> 8.13 us  [paired_chunks(): lax.ppermute(fourth_piece, 'seq', [(0, 3), (3, 0)])]
  transfers between devices with their start and end apart: 40 -> 40, of which waited for: 19 -> 18; matrix products, arithmetic and copies ran while one was open for 2% -> 2% of each run, Pallas kernels for 27% -> 25%
where the time goes in v12:
time: 241 us; the launch traced here: 240 us
  waiting for transfers between devices  96.7 us (40%)
  Pallas kernels  73.1 us (30%)
  starting transfers between devices  56.2 us (23%)
  local copies, waits for them, and re-layouts  8.01 us (3%)
  other arithmetic  5.21 us (2%)
    ppermute x30, waiting for transfers between devices, swapped(): return lax.ppermute(array, axis, pairs)  62.3 us
    pallas_call x4, Pallas kernels, gate_part(): pl.pallas_call(functools.partial(gate_kernel, counts, len(xs), last), gri...  36.8 us
    ppermute x30, starting transfers between devices, swapped(): return lax.ppermute(array, axis, pairs)  32.3 us
    pallas_call x2, Pallas kernels, down_part(): pl.pallas_call(functools.partial(down_kernel, blocks, sections), grid_spe...  25.6 us
    ppermute x1, waiting for transfers between devices, paired_chunks(): lax.ppermute(fourth_piece, 'seq', [(1, 3), (2, 0)])  16.7 us
    ppermute x2, starting transfers between devices, shifted(): return lax.ppermute(array, axis, pairs)  9.43 us
    ppermute x1, waiting for transfers between devices, paired_chunks(): lax.ppermute(fourth_piece, 'seq', [(0, 3), (3, 0)])  8.13 us
    unnamed x40, local copies, waits for them, and re-layouts  7.07 us
  transfers between devices with their start and end apart: 40, of which 18 were waited for; matrix products, arithmetic and copies ran while one was open for 2% of the time, Pallas kernels for 25%

profile of v12, /device:TPU:0, one launch (start us, length us, event | category | flops | bytes accessed | tf_op | source)
XLA Modules:
  0.0 239.8 jit_solution(14168359073176505162)
XLA Ops:
  0.0 2.1 shard_map.109
  2.2 4.9 %collective-permute-start = (bf16[784,128]{1,0:T(8,128)(2,1)S(1)}, bf16[784,128]{1,0:T(8,128)(2,1)S(1)}, u32[]{:S(2)}, u32[]{:S(2)}) collective-permute-start(bf16[784,128]{1,0:T(8,128)(2,1)S(1)} %get-tuple-element.69), channel_id=1, source_target_pairs={{0,8},{8,16},{16,24},{1,9},{9,17},{17,25},{2,10},{10,18},{18,26},{... | collective-permute-start | bytes 602120 | tf_op jit(solution)/shard_map/ppermute | solution.py:30
  7.8 1.0 copy-done
  8.8 1.0 copy-done.2
  9.8 1.0 copy-done.3
  11.5 1.4 shard_map.110.intra_ref
  13.2 4.5 %collective-permute-start.1 = (bf16[784,128]{1,0:T(8,128)(2,1)S(1)}, bf16[784,128]{1,0:T(8,128)(2,1)S(1)}, u32[]{:S(2)}, u32[]{:S(2)}) collective-permute-start(bf16[784,128]{1,0:T(8,128)(2,1)S(1)} %concatenate.9), channel_id=1, source_target_pairs={{0,16},{8,24},{1,17},{9,25},{2,18},{10,26},{3,19},{11,27},{4,20},{... | collective-permute-start | bytes 602120 | tf_op jit(solution)/shard_map/ppermute | solution.py:30
  17.7 3.9 %collective-permute-done.1 = bf16[784,128]{1,0:T(8,128)(2,1)S(1)} collective-permute-done((bf16[784,128]{1,0:T(8,128)(2,1)S(1)}, bf16[784,128]{1,0:T(8,128)(2,1)S(1)}, u32[]{:S(2)}, u32[]{:S(2)}) %collective-permute-start.1) | collective-permute-done | bytes 200736 | tf_op jit(solution)/shard_map/ppermute | solution.py:30
  22.7 4.6 %collective-permute-start.2 = (bf16[272,768]{1,0:T(8,128)(2,1)S(1)}, bf16[272,768]{1,0:T(8,128)(2,1)S(1)}, u32[]{:S(2)}, u32[]{:S(2)}) collective-permute-start(bf16[272,768]{1,0:T(8,128)(2,1)S(1)} %shard_map.111.refs_0_), channel_id=1, source_target_pairs={{0,8},{8,0},{16,24},{24,16},{1,9},{9,1},{17,25},{25,17},{2,10},{10... | collective-permute-start | bytes 1253384 | tf_op jit(solution)/shard_map/ppermute | solution.py:435
  28.0 1.0 shard_map.112
  29.1 1.5 collective-permute-start.9
  30.6 5.2 %collective-permute-done.2.refs_0_ = bf16[272,768]{1,0:T(8,128)(2,1)S(1)} collective-permute-done((bf16[272,768]{1,0:T(8,128)(2,1)S(1)}, bf16[272,768]{1,0:T(8,128)(2,1)S(1)}, u32[]{:S(2)}, u32[]{:S(2)}) %collective-permute-start.2) | collective-permute-done | bytes 417824 | tf_op jit(solution)/shard_map/ppermute | solution.py:435
  35.8 1.0 shard_map.113
  36.9 1.5 collective-permute-start.3
  38.4 1.3 collective-permute-start.5
  39.7 1.4 collective-permute-start.6
  41.3 3.4 %collective-permute-done.3 = bf16[768,256]{1,0:T(8,128)(2,1)S(1)} collective-permute-done((bf16[768,256]{1,0:T(8,128)(2,1)S(1)}, bf16[768,256]{1,0:T(8,128)(2,1)S(1)}, u32[]{:S(2)}, u32[]{:S(2)}) %collective-permute-start.3) | collective-permute-done | bytes 393248 | tf_op jit(solution)/shard_map/ppermute | solution.py:435
  44.8 5.5 %collective-permute-done.5.refs_1_ = bf16[272,768]{1,0:T(8,128)(2,1)S(1)} collective-permute-done((bf16[272,768]{1,0:T(8,128)(2,1)S(1)}, bf16[272,768]{1,0:T(8,128)(2,1)S(1)}, u32[]{:S(2)}, u32[]{:S(2)}) %collective-permute-start.5) | collective-permute-done | bytes 417824 | tf_op jit(solution)/shard_map/ppermute | solution.py:536
  50.3 1.0 shard_map.114
  51.4 1.5 collective-permute-start.11
  52.9 1.5 collective-permute-start.13
  55.0 7.8 %collective-permute-done.11 = bf16[768,256]{1,0:T(8,128)(2,1)} collective-permute-done((bf16[768,256]{1,0:T(8,128)(2,1)S(1)}, bf16[768,256]{1,0:T(8,128)(2,1)}, u32[]{:S(2)}, u32[]{:S(2)}) %collective-permute-start.11) | collective-permute-done | bytes 393248 | tf_op jit(solution)/shard_map/ppermute | solution.py:435
  62.8 1.5 collective-permute-start.16
  64.2 1.1 pad_maximum_fusion.2.refs_0_
  65.3 2.3 collective-permute-start.15
  67.7 9.2 %shard_map.115 = (f32[2,576,256]{2,1,0:T(8,128)S(1)}, f32[2,576,256]{2,1,0:T(8,128)S(1)}, f32[2,2,256]{2,1,0:T(2,128)S(1)}) custom-call(s32[4]{0:T(128)S(1)} %pad_add_fusion.2.plan_ref, bf16[2,768,256]{2,1,0:T(8,128)(2,1)S(1)} %pad_maximum_fusion.refs_0_, bf16[2,768,256]{2,1,0:T(8,128)(2,1)} %collective-permute-done.8.refs_1_, ...), custom_call_target="tpu_custom_call" | custom-call | flops 3623878656 | bytes 14155776 | tf_op jit(solution)/shard_map/pallas_call | solution.py:347
  76.9 1.0 copy-done.4
  77.9 1.0 copy-done.6
  79.5 1.5 shard_map.116
  81.0 1.6 collective-permute-start.17
  82.6 6.3 %collective-permute-done.17 = bf16[768,256]{1,0:T(8,128)(2,1)} collective-permute-done((bf16[768,256]{1,0:T(8,128)(2,1)S(1)}, bf16[768,256]{1,0:T(8,128)(2,1)}, u32[]{:S(2)}, u32[]{:S(2)}) %collective-permute-start.17) | collective-permute-done | bytes 393248 | tf_op jit(solution)/shard_map/ppermute | solution.py:435
  88.9 1.1 pad_maximum_fusion.3.refs_2_
  90.1 1.3 copy-done.7
  91.3 9.6 %shard_map.117.hidden_ref = bf16[2,256,576]{2,1,0:T(8,128)(2,1)S(1)} custom-call(s32[4]{0:T(128)S(1)} %pad_add_fusion.1.plan_ref, bf16[2,768,256]{2,1,0:T(8,128)(2,1)} %collective-permute-done.7.refs_0_, bf16[2,768,256]{2,1,0:T(8,128)(2,1)S(1)} %collective-permute-done.12.refs_1_, bf16[2,768,256]{2,1,0:T(8,128)(2,1)} %collective-permute-done.13.refs_2_, ...), custom_call_target="tpu_custom_call" | custom-call | flops 3623878656 | bytes 14155776 | tf_op jit(solution)/shard_map/pallas_call | solution.py:347
  101.0 1.2 collective-permute-start.18
  102.3 12.8 %shard_map.118 = (bf16[4,256,768]{2,1,0:T(8,128)(2,1)S(1)}, bf16[4,256,768]{2,1,0:T(8,128)(2,1)S(1)}, bf16[4,256,768]{2,1,0:T(8,128)(2,1)S(1)}, bf16[4,256,768]{2,1,0:T(8,128)(2,1)S(1)}) custom-call(s32[8]{0:T(128)S(1)} %concatenate.10.plan_ref, bf16[2,256,576]{2,1,0:T(8,128)(2,1)S(1)} %shard_map.117.hidden_ref, bf16[2,576,6144]{2,1,0:T(8,128)(2,1)} %down_ref.3), custom_call_target="tpu_custom_call" | custom-call | flops 3623878656 | bytes 14155776 | tf_op jit(solution)/shard_map/pallas_call | solution.py:406
  116.2 2.4 collective-permute-done.20.refs_1_
  118.8 1.0 collective-permute-start.21
  119.7 2.2 collective-permute-done.22.refs_1_
  122.0 1.1 collective-permute-done.23.refs_3_
  123.6 8.7 %shard_map.119 = (f32[2,576,256]{2,1,0:T(8,128)S(1)}, f32[2,576,256]{2,1,0:T(8,128)S(1)}, f32[2,2,256]{2,1,0:T(2,128)S(1)}) custom-call(s32[4]{0:T(128)S(1)} %pad_add_fusion.2.plan_ref, bf16[2,768,256]{2,1,0:T(8,128)(2,1)S(1)} %pad_maximum_fusion.2.refs_0_, bf16[2,768,256]{2,1,0:T(8,128)(2,1)S(1)} %collective-permute-done.22.refs_1_, ...), custom_call_target="tpu_custom_call" | custom-call | flops 3623878656 | bytes 14155776 | tf_op jit(solution)/shard_map/pallas_call | solution.py:347
  132.7 1.0 collective-permute-start.24
  133.7 1.5 collective-permute-start.28
  135.2 9.2 %shard_map.120.hidden_ref = bf16[2,256,576]{2,1,0:T(8,128)(2,1)S(1)} custom-call(s32[4]{0:T(128)S(1)} %pad_add_fusion.1.plan_ref, bf16[2,768,256]{2,1,0:T(8,128)(2,1)} %collective-permute-done.15.refs_0_, bf16[2,768,256]{2,1,0:T(8,128)(2,1)S(1)} %collective-permute-done.25.refs_1_, bf16[2,768,256]{2,1,0:T(8,128)(2,1)S(1)} %collective-permute-done.18.refs_2_, ...), custom_call_target="tpu_custom_call" | custom-call | flops 3623878656 | bytes 14155776 | tf_op jit(solution)/shard_map/pallas_call | solution.py:347
  144.4 1.3 collective-permute-done.28
  145.7 3.3 %collective-permute-done.24.refs_2_ = bf16[2,256,768]{2,1,0:T(8,128)(2,1)S(1)} collective-permute-done((bf16[2,256,768]{2,1,0:T(8,128)(2,1)S(1)}, bf16[2,256,768]{2,1,0:T(8,128)(2,1)S(1)}, u32[]{:S(2)}, u32[]{:S(2)}) %collective-permute-start.24) | collective-permute-done | bytes 786464 | tf_op jit(solution)/shard_map/ppermute | solution.py:435
  149.1 1.0 collective-permute-start.27
  150.6 4.4 %collective-permute-start.29 = (bf16[256,768]{1,0:T(8,128)(2,1)S(1)}, bf16[256,768]{1,0:T(8,128)(2,1)S(1)}, u32[]{:S(2)}, u32[]{:S(2)}) collective-permute-start(bf16[256,768]{1,0:T(8,128)(2,1)S(1)} %shard_map.122), channel_id=1, source_target_pairs={{0,8},{8,0},{16,24},{24,16},{1,9},{9,1},{17,25},{25,17},{2,10},{10... | collective-permute-start | bytes 1179656 | tf_op jit(solution)/shard_map/ppermute | solution.py:435
  154.9 12.8 %shard_map.123 = (bf16[4,256,768]{2,1,0:T(8,128)(2,1)S(1)}, bf16[4,256,768]{2,1,0:T(8,128)(2,1)S(1)}, bf16[4,256,768]{2,1,0:T(8,128)(2,1)S(1)}, bf16[4,256,768]{2,1,0:T(8,128)(2,1)S(1)}) custom-call(s32[8]{0:T(128)S(1)} %concatenate.10.plan_ref, bf16[2,256,576]{2,1,0:T(8,128)(2,1)S(1)} %shard_map.120.hidden_ref, bf16[2,576,6144]{2,1,0:T(8,128)(2,1)} %down_ref.3), custom_call_target="tpu_custom_call" | custom-call | flops 3623878656 | bytes 14155776 | tf_op jit(solution)/shard_map/pallas_call | solution.py:406
  168.8 2.9 %collective-permute-done.30.refs_1_ = bf16[4,256,768]{2,1,0:T(8,128)(2,1)S(1)} collective-permute-done((bf16[4,256,768]{2,1,0:T(8,128)(2,1)S(1)}, bf16[4,256,768]{2,1,0:T(8,128)(2,1)S(1)}, u32[]{:S(2)}, u32[]{:S(2)}) %collective-permute-start.30) | collective-permute-done | bytes 1572896 | tf_op jit(solution)/shard_map/ppermute | solution.py:435
  171.9 1.1 collective-permute-start.31
  173.0 0.9 collective-permute-done.35.refs_1_
  174.1 9.8 %collective-permute-done.31.refs_2_ = bf16[2,256,768]{2,1,0:T(8,128)(2,1)S(1)} collective-permute-done((bf16[2,256,768]{2,1,0:T(8,128)(2,1)S(1)}, bf16[2,256,768]{2,1,0:T(8,128)(2,1)S(1)}, u32[]{:S(2)}, u32[]{:S(2)}) %collective-permute-start.31) | collective-permute-done | bytes 786464 | tf_op jit(solution)/shard_map/ppermute | solution.py:435
  183.9 1.1 collective-permute-start.36
  185.1 1.2 collective-permute-start.32
  186.3 13.1 %collective-permute-done.36.refs_2_ = bf16[2,256,768]{2,1,0:T(8,128)(2,1)S(1)} collective-permute-done((bf16[2,256,768]{2,1,0:T(8,128)(2,1)S(1)}, bf16[2,256,768]{2,1,0:T(8,128)(2,1)S(1)}, u32[]{:S(2)}, u32[]{:S(2)}) %collective-permute-start.36) | collective-permute-done | bytes 786464 | tf_op jit(solution)/shard_map/ppermute | solution.py:435
  199.6 1.0 collective-permute-start.37
  201.1 3.1 %collective-permute-start.34 = (bf16[256,768]{1,0:T(8,128)(2,1)S(1)}, bf16[256,768]{1,0:T(8,128)(2,1)S(1)}, u32[]{:S(2)}, u32[]{:S(2)}) collective-permute-start(bf16[256,768]{1,0:T(8,128)(2,1)S(1)} %shard_map.124), channel_id=1, source_target_pairs={{0,16},{24,8},{1,17},{25,9},{2,18},{26,10},{3,19},{27,11},{4,20},{... | collective-permute-start | bytes 1179656 | tf_op jit(solution)/shard_map/ppermute | solution.py:623
  204.9 2.6 %collective-permute-done.37 = bf16[256,768]{1,0:T(8,128)(2,1)S(1)} collective-permute-done((bf16[256,768]{1,0:T(8,128)(2,1)S(1)}, bf16[256,768]{1,0:T(8,128)(2,1)S(1)}, u32[]{:S(2)}, u32[]{:S(2)}) %collective-permute-start.37) | collective-permute-done | bytes 393248 | tf_op jit(solution)/shard_map/ppermute | solution.py:435
  207.9 4.6 %collective-permute-start.39 = (bf16[256,768]{1,0:T(8,128)(2,1)S(1)}, bf16[256,768]{1,0:T(8,128)(2,1)S(1)}, u32[]{:S(2)}, u32[]{:S(2)}) collective-permute-start(bf16[256,768]{1,0:T(8,128)(2,1)S(1)} %shard_map.125), channel_id=1, source_target_pairs={{0,24},{24,0},{1,25},{25,1},{2,26},{26,2},{3,27},{27,3},{4,28},{28... | collective-permute-start | bytes 1179656 | tf_op jit(solution)/shard_map/ppermute | solution.py:625
  212.5 1.3 collective-permute-start.38
  213.8 8.1 %collective-permute-done.39 = bf16[256,768]{1,0:T(8,128)(2,1)S(1)} collective-permute-done((bf16[256,768]{1,0:T(8,128)(2,1)S(1)}, bf16[256,768]{1,0:T(8,128)(2,1)S(1)}, u32[]{:S(2)}, u32[]{:S(2)}) %collective-permute-start.39) | collective-permute-done | bytes 393248 | tf_op jit(solution)/shard_map/ppermute | solution.py:625
  221.9 16.7 %collective-permute-done.38 = bf16[256,768]{1,0:T(8,128)(2,1)S(1)} collective-permute-done((bf16[256,768]{1,0:T(8,128)(2,1)S(1)}, bf16[256,768]{1,0:T(8,128)(2,1)S(1)}, u32[]{:S(2)}, u32[]{:S(2)}) %collective-permute-start.38) | collective-permute-done | bytes 393248 | tf_op jit(solution)/shard_map/ppermute | solution.py:624
  238.7 1.1 add_convert_fusion.8
  (101 shorter events, 10.9 us)
Async XLA Ops:
  2.2 10.8 %collective-permute-start = (bf16[784,128]{1,0:T(8,128)(2,1)S(1)}, bf16[784,128]{1,0:T(8,128)(2,1)S(1)}, u32[]{:S(2)}, u32[]{:S(2)}) collective-permute-start(bf16[784,128]{1,0:T(8,128)(2,1)S(1)} %get-tuple-element.69), channel_id=1, source_target_pairs={{0,8},{8,16},{16,24},{1,9},{9,17},{17,25},{2,10},{10,18},{18,26},{... | collective-permute-start | bytes 602120 | tf_op jit(solution)/shard_map/ppermute | solution.py:30
  7.8 1.0 copy-start
  8.8 1.0 copy-start.2
  9.8 1.0 copy-start.3
  10.8 0.7 copy-start.18
  12.9 8.9 %copy-start.1 = (bf16[256,768]{1,0:T(8,128)(2,1)S(1)}, bf16[256,768]{1,0:T(8,128)(2,1)}, u32[]{:S(2)}) copy-start(bf16[256,768]{1,0:T(8,128)(2,1)} %query_ref.3) | copy-start | bytes 1179652
  12.9 8.9 %copy-start.9 = (bf16[256,768]{1,0:T(8,128)(2,1)S(1)}, bf16[256,768]{1,0:T(8,128)(2,1)}, u32[]{:S(2)}) copy-start(bf16[256,768]{1,0:T(8,128)(2,1)} %residual_ref.1) | copy-start | bytes 1179652
  12.9 8.9 %copy-start.19 = (s32[256,2]{0,1:T(2,128)S(1)}, s32[256,2]{0,1:T(2,128)}, u32[]{:S(2)}) copy-start(s32[256,2]{0,1:T(2,128)} %param.17) | copy-start | bytes 6148
  13.2 8.5 %collective-permute-start.1 = (bf16[784,128]{1,0:T(8,128)(2,1)S(1)}, bf16[784,128]{1,0:T(8,128)(2,1)S(1)}, u32[]{:S(2)}, u32[]{:S(2)}) collective-permute-start(bf16[784,128]{1,0:T(8,128)(2,1)S(1)} %concatenate.9), channel_id=1, source_target_pairs={{0,16},{8,24},{1,17},{9,25},{2,18},{10,26},{3,19},{11,27},{4,20},{... | collective-permute-start | bytes 602120 | tf_op jit(solution)/shard_map/ppermute | solution.py:30
  22.7 13.2 %collective-permute-start.2 = (bf16[272,768]{1,0:T(8,128)(2,1)S(1)}, bf16[272,768]{1,0:T(8,128)(2,1)S(1)}, u32[]{:S(2)}, u32[]{:S(2)}) collective-permute-start(bf16[272,768]{1,0:T(8,128)(2,1)S(1)} %shard_map.111.refs_0_), channel_id=1, source_target_pairs={{0,8},{8,0},{16,24},{24,16},{1,9},{9,1},{17,25},{25,17},{2,10},{10... | collective-permute-start | bytes 1253384 | tf_op jit(solution)/shard_map/ppermute | solution.py:435
  27.3 11.2 %collective-permute-start.4 = (bf16[272,768]{1,0:T(8,128)(2,1)S(1)}, bf16[272,768]{1,0:T(8,128)(2,1)S(1)}, u32[]{:S(2)}, u32[]{:S(2)}) collective-permute-start(bf16[272,768]{1,0:T(8,128)(2,1)S(1)} %shard_map.111.refs_0_), channel_id=1, source_target_pairs={{8,16},{16,8},{9,17},{17,9},{10,18},{18,10},{11,19},{19,11},{12,20... | collective-permute-start | bytes 1253384 | tf_op jit(solution)/shard_map/ppermute | solution.py:533
  29.1 15.7 %copy-start.12 = (bf16[256,256]{1,0:T(8,128)(2,1)}, bf16[256,256]{1,0:T(8,128)(2,1)S(1)}, u32[]{:S(2)}) copy-start(bf16[256,256]{1,0:T(8,128)(2,1)S(1)} %get-tuple-element.70.place_ref) | copy-start | bytes 393220
  29.1 12.1 %collective-permute-start.9 = (bf16[768,256]{1,0:T(8,128)(2,1)S(1)}, bf16[768,256]{1,0:T(8,128)(2,1)S(1)}, u32[]{:S(2)}, u32[]{:S(2)}) collective-permute-start(bf16[768,256]{1,0:T(8,128)(2,1)S(1)} %get-tuple-element.73), channel_id=1, source_target_pairs={{0,2},{1,5},{2,0},{3,7},{4,6},{5,1},{6,4},{7,3},{8,10},{9,13},{10,... | collective-permute-start | bytes 1179656 | tf_op jit(solution)/shard_map/ppermute | solution.py:435
  36.9 7.9 %copy-start.14 = (bf16[256,256]{1,0:T(8,128)(2,1)}, bf16[256,256]{1,0:T(8,128)(2,1)S(1)}, u32[]{:S(2)}) copy-start(bf16[256,256]{1,0:T(8,128)(2,1)S(1)} %get-tuple-element.120.place_ref) | copy-start | bytes 393220
  36.9 7.8 %collective-permute-start.3 = (bf16[768,256]{1,0:T(8,128)(2,1)S(1)}, bf16[768,256]{1,0:T(8,128)(2,1)S(1)}, u32[]{:S(2)}, u32[]{:S(2)}) collective-permute-start(bf16[768,256]{1,0:T(8,128)(2,1)S(1)} %get-tuple-element.71), channel_id=1, source_target_pairs={{0,2},{1,5},{2,0},{3,7},{4,6},{5,1},{6,4},{7,3},{8,10},{9,13},{10,... | collective-permute-start | bytes 1179656 | tf_op jit(solution)/shard_map/ppermute | solution.py:435
  38.4 11.9 %collective-permute-start.5 = (bf16[272,768]{1,0:T(8,128)(2,1)S(1)}, bf16[272,768]{1,0:T(8,128)(2,1)S(1)}, u32[]{:S(2)}, u32[]{:S(2)}) collective-permute-start(bf16[272,768]{1,0:T(8,128)(2,1)S(1)} %collective-permute-done.4.refs_0_), channel_id=1, source_target_pairs={{8,0},{16,24},{9,1},{17,25},{10,2},{18,26},{11,3},{19,27},{12,4},{... | collective-permute-start | bytes 1253384 | tf_op jit(solution)/shard_map/ppermute | solution.py:536
  39.7 10.6 %collective-permute-start.6 = (bf16[272,768]{1,0:T(8,128)(2,1)S(1)}, bf16[272,768]{1,0:T(8,128)(2,1)}, u32[]{:S(2)}, u32[]{:S(2)}) collective-permute-start(bf16[272,768]{1,0:T(8,128)(2,1)S(1)} %collective-permute-done.2.refs_0_), channel_id=1, source_target_pairs={{8,16},{16,8},{9,17},{17,9},{10,18},{18,10},{11,19},{19,11},{12,20... | collective-permute-start | bytes 1253384 | tf_op jit(solution)/shard_map/ppermute | solution.py:533
  41.2 24.1 %collective-permute-start.10 = (bf16[2,768,256]{2,1,0:T(8,128)(2,1)S(1)}, bf16[2,768,256]{2,1,0:T(8,128)(2,1)}, u32[]{:S(2)}, u32[]{:S(2)}) collective-permute-start(bf16[2,768,256]{2,1,0:T(8,128)(2,1)S(1)} %pad_maximum_fusion.1.refs_2_), channel_id=1, source_target_pairs={{0,1},{1,0},{2,3},{3,2},{4,5},{5,4},{6,7},{7,6},{8,9},{9,8},{10,11... | collective-permute-start | bytes 2359304 | tf_op jit(solution)/shard_map/ppermute | solution.py:435
  44.8 22.9 %copy-start.8 = (bf16[6144,2]{0,1:T(2,128)(2,1)S(1)}, bf16[6144,2]{0,1:T(2,128)(2,1)}, u32[]{:S(2)}) copy-start(bf16[6144,2]{0,1:T(2,128)(2,1)} %param.18) | copy-start | bytes 73732
  50.3 17.3 %collective-permute-start.8 = (bf16[2,768,256]{2,1,0:T(8,128)(2,1)S(1)}, bf16[2,768,256]{2,1,0:T(8,128)(2,1)}, u32[]{:S(2)}, u32[]{:S(2)}) collective-permute-start(bf16[2,768,256]{2,1,0:T(8,128)(2,1)S(1)} %pad_maximum_fusion.refs_0_), channel_id=1, source_target_pairs={{0,1},{1,0},{2,3},{3,2},{4,5},{5,4},{6,7},{7,6},{8,9},{9,8},{10,11... | collective-permute-start | bytes 2359304 | tf_op jit(solution)/shard_map/ppermute | solution.py:435
  51.3 25.5 %copy-start.10 = (bf16[256,256]{1,0:T(8,128)(2,1)}, bf16[256,256]{1,0:T(8,128)(2,1)S(1)}, u32[]{:S(2)}) copy-start(bf16[256,256]{1,0:T(8,128)(2,1)S(1)} %get-tuple-element.122.place_ref) | copy-start | bytes 393220
  51.4 11.4 %collective-permute-start.11 = (bf16[768,256]{1,0:T(8,128)(2,1)S(1)}, bf16[768,256]{1,0:T(8,128)(2,1)}, u32[]{:S(2)}, u32[]{:S(2)}) collective-permute-start(bf16[768,256]{1,0:T(8,128)(2,1)S(1)} %get-tuple-element.74), channel_id=1, source_target_pairs={{0,2},{1,5},{2,0},{3,7},{4,6},{5,1},{6,4},{7,3},{8,10},{9,13},{10,... | collective-permute-start | bytes 1179656 | tf_op jit(solution)/shard_map/ppermute | solution.py:435
  52.9 26.1 %collective-permute-start.13 = (bf16[2,768,256]{2,1,0:T(8,128)(2,1)S(1)}, bf16[2,768,256]{2,1,0:T(8,128)(2,1)}, u32[]{:S(2)}, u32[]{:S(2)}) collective-permute-start(bf16[2,768,256]{2,1,0:T(8,128)(2,1)S(1)} %pad_maximum_fusion.1.refs_2_), channel_id=1, source_target_pairs={{0,4},{1,3},{2,6},{3,1},{4,0},{5,7},{6,2},{7,5},{8,12},{9,11},{10,... | collective-permute-start | bytes 2359304 | tf_op jit(solution)/shard_map/ppermute | solution.py:435
  54.4 24.5 %collective-permute-start.7 = (bf16[2,768,256]{2,1,0:T(8,128)(2,1)S(1)}, bf16[2,768,256]{2,1,0:T(8,128)(2,1)}, u32[]{:S(2)}, u32[]{:S(2)}) collective-permute-start(bf16[2,768,256]{2,1,0:T(8,128)(2,1)S(1)} %pad_maximum_fusion.refs_0_), channel_id=1, source_target_pairs={{0,4},{1,3},{2,6},{3,1},{4,0},{5,7},{6,2},{7,5},{8,12},{9,11},{10,... | collective-permute-start | bytes 2359304 | tf_op jit(solution)/shard_map/ppermute | solution.py:435
  62.8 16.7 %collective-permute-start.16 = (bf16[272,768]{1,0:T(8,128)(2,1)}, bf16[272,768]{1,0:T(8,128)(2,1)S(1)}, u32[]{:S(2)}, u32[]{:S(2)}) collective-permute-start(bf16[272,768]{1,0:T(8,128)(2,1)} %collective-permute-done.6.refs_0_), channel_id=1, source_target_pairs={{8,0},{16,24},{9,1},{17,25},{10,2},{18,26},{11,3},{19,27},{12,4},{... | collective-permute-start | bytes 1253384 | tf_op jit(solution)/shard_map/ppermute | solution.py:536
  65.3 24.7 %collective-permute-start.15 = (bf16[2,768,256]{2,1,0:T(8,128)(2,1)S(1)}, bf16[2,768,256]{2,1,0:T(8,128)(2,1)}, u32[]{:S(2)}, u32[]{:S(2)}) collective-permute-start(bf16[2,768,256]{2,1,0:T(8,128)(2,1)S(1)} %pad_maximum_fusion.2.refs_0_), channel_id=1, source_target_pairs={{0,4},{1,3},{2,6},{3,1},{4,0},{5,7},{6,2},{7,5},{8,12},{9,11},{10,... | collective-permute-start | bytes 2359304 | tf_op jit(solution)/shard_map/ppermute | solution.py:435
  76.9 1.1 copy-start.4
  77.9 1.0 copy-start.6
  79.0 11.1 %collective-permute-start.14 = (bf16[2,768,256]{2,1,0:T(8,128)(2,1)}, bf16[2,768,256]{2,1,0:T(8,128)(2,1)}, u32[]{:S(2)}, u32[]{:S(2)}) collective-permute-start(bf16[2,768,256]{2,1,0:T(8,128)(2,1)} %collective-permute-done.13.refs_2_), channel_id=1, source_target_pairs={{0,1},{1,0},{2,3},{3,2},{4,5},{5,4},{6,7},{7,6},{8,9},{9,8},{10,11... | collective-permute-start | bytes 2359304 | tf_op jit(solution)/shard_map/ppermute | solution.py:435
  79.0 11.1 %collective-permute-start.12 = (bf16[2,768,256]{2,1,0:T(8,128)(2,1)}, bf16[2,768,256]{2,1,0:T(8,128)(2,1)S(1)}, u32[]{:S(2)}, u32[]{:S(2)}) collective-permute-start(bf16[2,768,256]{2,1,0:T(8,128)(2,1)} %collective-permute-done.7.refs_0_), channel_id=1, source_target_pairs={{0,1},{1,0},{2,3},{3,2},{4,5},{5,4},{6,7},{7,6},{8,9},{9,8},{10,11... | collective-permute-start | bytes 2359304 | tf_op jit(solution)/shard_map/ppermute | solution.py:435
  81.0 9.1 %copy-start.16 = (bf16[256,256]{1,0:T(8,128)(2,1)}, bf16[256,256]{1,0:T(8,128)(2,1)S(1)}, u32[]{:S(2)}) copy-start(bf16[256,256]{1,0:T(8,128)(2,1)S(1)} %get-tuple-element.85.place_ref) | copy-start | bytes 393220
  81.0 7.9 %collective-permute-start.17 = (bf16[768,256]{1,0:T(8,128)(2,1)S(1)}, bf16[768,256]{1,0:T(8,128)(2,1)}, u32[]{:S(2)}, u32[]{:S(2)}) collective-permute-start(bf16[768,256]{1,0:T(8,128)(2,1)S(1)} %get-tuple-element.84), channel_id=1, source_target_pairs={{0,2},{1,5},{2,0},{3,7},{4,6},{5,1},{6,4},{7,3},{8,10},{9,13},{10,... | collective-permute-start | bytes 1179656 | tf_op jit(solution)/shard_map/ppermute | solution.py:435
  82.6 7.5 %copy-start.5 = (f32[2,576,256]{2,1,0:T(8,128)S(1)}, f32[2,576,256]{2,1,0:T(8,128)}, u32[]{:S(2)}) copy-start(f32[2,576,256]{2,1,0:T(8,128)} %copy-done.4) | copy-start | bytes 3538948
  90.1 1.3 copy-start.7
  101.0 14.1 %collective-permute-start.18 = (bf16[2,768,256]{2,1,0:T(8,128)(2,1)S(1)}, bf16[2,768,256]{2,1,0:T(8,128)(2,1)S(1)}, u32[]{:S(2)}, u32[]{:S(2)}) collective-permute-start(bf16[2,768,256]{2,1,0:T(8,128)(2,1)S(1)} %pad_maximum_fusion.3.refs_2_), channel_id=1, source_target_pairs={{0,4},{1,3},{2,6},{3,1},{4,0},{5,7},{6,2},{7,5},{8,12},{9,11},{10,... | collective-permute-start | bytes 2359304 | tf_op jit(solution)/shard_map/ppermute | solution.py:435
  115.1 3.5 %collective-permute-start.20 = (bf16[4,256,768]{2,1,0:T(8,128)(2,1)S(1)}, bf16[4,256,768]{2,1,0:T(8,128)(2,1)S(1)}, u32[]{:S(2)}, u32[]{:S(2)}) collective-permute-start(bf16[4,256,768]{2,1,0:T(8,128)(2,1)S(1)} %get-tuple-element.100), channel_id=1, source_target_pairs={{0,1},{1,0},{2,3},{3,2},{4,5},{5,4},{6,7},{7,6},{8,9},{9,8},{10,11... | collective-permute-start | bytes 4718600 | tf_op jit(solution)/shard_map/ppermute | solution.py:435
  115.2 17.1 %collective-permute-start.19 = (bf16[4,256,768]{2,1,0:T(8,128)(2,1)S(1)}, bf16[4,256,768]{2,1,0:T(8,128)(2,1)S(1)}, u32[]{:S(2)}, u32[]{:S(2)}) collective-permute-start(bf16[4,256,768]{2,1,0:T(8,128)(2,1)S(1)} %get-tuple-element.98), channel_id=1, source_target_pairs={{0,1},{1,0},{2,3},{3,2},{4,5},{5,4},{6,7},{7,6},{8,9},{9,8},{10,11... | collective-permute-start | bytes 4718600 | tf_op jit(solution)/shard_map/ppermute | solution.py:435
  115.7 6.3 %collective-permute-start.22 = (bf16[2,768,256]{2,1,0:T(8,128)(2,1)S(1)}, bf16[2,768,256]{2,1,0:T(8,128)(2,1)S(1)}, u32[]{:S(2)}, u32[]{:S(2)}) collective-permute-start(bf16[2,768,256]{2,1,0:T(8,128)(2,1)S(1)} %pad_maximum_fusion.2.refs_0_), channel_id=1, source_target_pairs={{0,1},{1,0},{2,3},{3,2},{4,5},{5,4},{6,7},{7,6},{8,9},{9,8},{10,11... | collective-permute-start | bytes 2359304 | tf_op jit(solution)/shard_map/ppermute | solution.py:435
  115.8 7.3 %collective-permute-start.23 = (bf16[2,768,256]{2,1,0:T(8,128)(2,1)S(1)}, bf16[2,768,256]{2,1,0:T(8,128)(2,1)S(1)}, u32[]{:S(2)}, u32[]{:S(2)}) collective-permute-start(bf16[2,768,256]{2,1,0:T(8,128)(2,1)S(1)} %pad_maximum_fusion.3.refs_2_), channel_id=1, source_target_pairs={{0,1},{1,0},{2,3},{3,2},{4,5},{5,4},{6,7},{7,6},{8,9},{9,8},{10,11... | collective-permute-start | bytes 2359304 | tf_op jit(solution)/shard_map/ppermute | solution.py:435
  118.8 13.8 %collective-permute-start.21 = (bf16[2,256,768]{2,1,0:T(8,128)(2,1)S(1)}, bf16[2,256,768]{2,1,0:T(8,128)(2,1)S(1)}, u32[]{:S(2)}, u32[]{:S(2)}) collective-permute-start(bf16[2,256,768]{2,1,0:T(8,128)(2,1)S(1)} %add_convert_fusion.2), channel_id=1, source_target_pairs={{0,4},{1,3},{2,6},{3,1},{4,0},{5,7},{6,2},{7,5},{8,12},{9,11},{10,... | collective-permute-start | bytes 2359304 | tf_op jit(solution)/shard_map/ppermute | solution.py:435
  123.1 12.1 %collective-permute-start.25 = (bf16[2,768,256]{2,1,0:T(8,128)(2,1)}, bf16[2,768,256]{2,1,0:T(8,128)(2,1)S(1)}, u32[]{:S(2)}, u32[]{:S(2)}) collective-permute-start(bf16[2,768,256]{2,1,0:T(8,128)(2,1)} %collective-permute-done.15.refs_0_), channel_id=1, source_target_pairs={{0,1},{1,0},{2,3},{3,2},{4,5},{5,4},{6,7},{7,6},{8,9},{9,8},{10,11... | collective-permute-start | bytes 2359304 | tf_op jit(solution)/shard_map/ppermute | solution.py:435
  123.2 11.9 %collective-permute-start.26 = (bf16[2,768,256]{2,1,0:T(8,128)(2,1)S(1)}, bf16[2,768,256]{2,1,0:T(8,128)(2,1)S(1)}, u32[]{:S(2)}, u32[]{:S(2)}) collective-permute-start(bf16[2,768,256]{2,1,0:T(8,128)(2,1)S(1)} %collective-permute-done.18.refs_2_), channel_id=1, source_target_pairs={{0,1},{1,0},{2,3},{3,2},{4,5},{5,4},{6,7},{7,6},{8,9},{9,8},{10,11... | collective-permute-start | bytes 2359304 | tf_op jit(solution)/shard_map/ppermute | solution.py:435
  132.7 16.3 %collective-permute-start.24 = (bf16[2,256,768]{2,1,0:T(8,128)(2,1)S(1)}, bf16[2,256,768]{2,1,0:T(8,128)(2,1)S(1)}, u32[]{:S(2)}, u32[]{:S(2)}) collective-permute-start(bf16[2,256,768]{2,1,0:T(8,128)(2,1)S(1)} %add_convert_fusion.3), channel_id=1, source_target_pairs={{0,4},{1,3},{2,6},{3,1},{4,0},{5,7},{6,2},{7,5},{8,12},{9,11},{10,... | collective-permute-start | bytes 2359304 | tf_op jit(solution)/shard_map/ppermute | solution.py:435
  133.7 12.1 %collective-permute-start.28 = (bf16[256,768]{1,0:T(8,128)(2,1)S(1)}, bf16[256,768]{1,0:T(8,128)(2,1)S(1)}, u32[]{:S(2)}, u32[]{:S(2)}) collective-permute-start(bf16[256,768]{1,0:T(8,128)(2,1)S(1)} %fusion), channel_id=1, source_target_pairs={{0,2},{1,5},{2,0},{3,7},{4,6},{5,1},{6,4},{7,3},{8,10},{9,13},{10,... | collective-permute-start | bytes 1179656 | tf_op jit(solution)/shard_map/ppermute | solution.py:435
  144.4 5.7 %copy-start.15 = (bf16[256,256]{1,0:T(8,128)(2,1)S(1)}, bf16[256,256]{1,0:T(8,128)(2,1)}, u32[]{:S(2)}) copy-start(bf16[256,256]{1,0:T(8,128)(2,1)} %copy-done.14) | copy-start | bytes 393220
  149.1 18.6 %collective-permute-start.27 = (bf16[256,768]{1,0:T(8,128)(2,1)S(1)}, bf16[256,768]{1,0:T(8,128)(2,1)S(1)}, u32[]{:S(2)}, u32[]{:S(2)}) collective-permute-start(bf16[256,768]{1,0:T(8,128)(2,1)S(1)} %fusion.1), channel_id=1, source_target_pairs={{0,2},{1,5},{2,0},{3,7},{4,6},{5,1},{6,4},{7,3},{8,10},{9,13},{10,... | collective-permute-start | bytes 1179656 | tf_op jit(solution)/shard_map/ppermute | solution.py:435
  150.6 17.2 %copy-start.13 = (bf16[256,256]{1,0:T(8,128)(2,1)S(1)}, bf16[256,256]{1,0:T(8,128)(2,1)}, u32[]{:S(2)}) copy-start(bf16[256,256]{1,0:T(8,128)(2,1)} %copy-done.12) | copy-start | bytes 393220
  150.6 17.6 %collective-permute-start.29 = (bf16[256,768]{1,0:T(8,128)(2,1)S(1)}, bf16[256,768]{1,0:T(8,128)(2,1)S(1)}, u32[]{:S(2)}, u32[]{:S(2)}) collective-permute-start(bf16[256,768]{1,0:T(8,128)(2,1)S(1)} %shard_map.122), channel_id=1, source_target_pairs={{0,8},{8,0},{16,24},{24,16},{1,9},{9,1},{17,25},{25,17},{2,10},{10... | collective-permute-start | bytes 1179656 | tf_op jit(solution)/shard_map/ppermute | solution.py:435
  168.2 3.5 %collective-permute-start.30 = (bf16[4,256,768]{2,1,0:T(8,128)(2,1)S(1)}, bf16[4,256,768]{2,1,0:T(8,128)(2,1)S(1)}, u32[]{:S(2)}, u32[]{:S(2)}) collective-permute-start(bf16[4,256,768]{2,1,0:T(8,128)(2,1)S(1)} %get-tuple-element.127), channel_id=1, source_target_pairs={{0,1},{1,0},{2,3},{3,2},{4,5},{5,4},{6,7},{7,6},{8,9},{9,8},{10,11... | collective-permute-start | bytes 4718600 | tf_op jit(solution)/shard_map/ppermute | solution.py:435
  168.3 5.6 %collective-permute-start.35 = (bf16[4,256,768]{2,1,0:T(8,128)(2,1)S(1)}, bf16[4,256,768]{2,1,0:T(8,128)(2,1)S(1)}, u32[]{:S(2)}, u32[]{:S(2)}) collective-permute-start(bf16[4,256,768]{2,1,0:T(8,128)(2,1)S(1)} %get-tuple-element.129), channel_id=1, source_target_pairs={{0,1},{1,0},{2,3},{3,2},{4,5},{5,4},{6,7},{7,6},{8,9},{9,8},{10,11... | collective-permute-start | bytes 4718600 | tf_op jit(solution)/shard_map/ppermute | solution.py:435
  171.9 12.1 %collective-permute-start.31 = (bf16[2,256,768]{2,1,0:T(8,128)(2,1)S(1)}, bf16[2,256,768]{2,1,0:T(8,128)(2,1)S(1)}, u32[]{:S(2)}, u32[]{:S(2)}) collective-permute-start(bf16[2,256,768]{2,1,0:T(8,128)(2,1)S(1)} %add_convert_fusion.1), channel_id=1, source_target_pairs={{0,4},{1,3},{2,6},{3,1},{4,0},{5,7},{6,2},{7,5},{8,12},{9,11},{10,... | collective-permute-start | bytes 2359304 | tf_op jit(solution)/shard_map/ppermute | solution.py:435
  174.1 26.5 %copy-start.11 = (bf16[256,256]{1,0:T(8,128)(2,1)S(1)}, bf16[256,256]{1,0:T(8,128)(2,1)}, u32[]{:S(2)}) copy-start(bf16[256,256]{1,0:T(8,128)(2,1)} %copy-done.10) | copy-start | bytes 393220
  183.9 15.5 %collective-permute-start.36 = (bf16[2,256,768]{2,1,0:T(8,128)(2,1)S(1)}, bf16[2,256,768]{2,1,0:T(8,128)(2,1)S(1)}, u32[]{:S(2)}, u32[]{:S(2)}) collective-permute-start(bf16[2,256,768]{2,1,0:T(8,128)(2,1)S(1)} %add_convert_fusion), channel_id=1, source_target_pairs={{0,4},{1,3},{2,6},{3,1},{4,0},{5,7},{6,2},{7,5},{8,12},{9,11},{10,... | collective-permute-start | bytes 2359304 | tf_op jit(solution)/shard_map/ppermute | solution.py:435
  185.1 15.5 %collective-permute-start.32 = (bf16[256,768]{1,0:T(8,128)(2,1)S(1)}, bf16[256,768]{1,0:T(8,128)(2,1)S(1)}, u32[]{:S(2)}, u32[]{:S(2)}) collective-permute-start(bf16[256,768]{1,0:T(8,128)(2,1)S(1)} %fusion.2), channel_id=1, source_target_pairs={{0,2},{1,5},{2,0},{3,7},{4,6},{5,1},{6,4},{7,3},{8,10},{9,13},{10,... | collective-permute-start | bytes 1179656 | tf_op jit(solution)/shard_map/ppermute | solution.py:435
  199.6 7.8 %collective-permute-start.37 = (bf16[256,768]{1,0:T(8,128)(2,1)S(1)}, bf16[256,768]{1,0:T(8,128)(2,1)S(1)}, u32[]{:S(2)}, u32[]{:S(2)}) collective-permute-start(bf16[256,768]{1,0:T(8,128)(2,1)S(1)} %fusion.3), channel_id=1, source_target_pairs={{0,2},{1,5},{2,0},{3,7},{4,6},{5,1},{6,4},{7,3},{8,10},{9,13},{10,... | collective-permute-start | bytes 1179656 | tf_op jit(solution)/shard_map/ppermute | solution.py:435
  200.6 6.8 %copy-start.17 = (bf16[256,256]{1,0:T(8,128)(2,1)S(1)}, bf16[256,256]{1,0:T(8,128)(2,1)}, u32[]{:S(2)}) copy-start(bf16[256,256]{1,0:T(8,128)(2,1)} %copy-done.16) | copy-start | bytes 393220
  201.1 12.7 %collective-permute-start.34 = (bf16[256,768]{1,0:T(8,128)(2,1)S(1)}, bf16[256,768]{1,0:T(8,128)(2,1)S(1)}, u32[]{:S(2)}, u32[]{:S(2)}) collective-permute-start(bf16[256,768]{1,0:T(8,128)(2,1)S(1)} %shard_map.124), channel_id=1, source_target_pairs={{0,16},{24,8},{1,17},{25,9},{2,18},{26,10},{3,19},{27,11},{4,20},{... | collective-permute-start | bytes 1179656 | tf_op jit(solution)/shard_map/ppermute | solution.py:623
  204.2 9.6 %collective-permute-start.33 = (bf16[256,768]{1,0:T(8,128)(2,1)S(1)}, bf16[256,768]{1,0:T(8,128)(2,1)S(1)}, u32[]{:S(2)}, u32[]{:S(2)}) collective-permute-start(bf16[256,768]{1,0:T(8,128)(2,1)S(1)} %shard_map.124), channel_id=1, source_target_pairs={{8,16},{16,8},{9,17},{17,9},{10,18},{18,10},{11,19},{19,11},{12,20... | collective-permute-start | bytes 1179656 | tf_op jit(solution)/shard_map/ppermute | solution.py:622
  207.9 14.0 %collective-permute-start.39 = (bf16[256,768]{1,0:T(8,128)(2,1)S(1)}, bf16[256,768]{1,0:T(8,128)(2,1)S(1)}, u32[]{:S(2)}, u32[]{:S(2)}) collective-permute-start(bf16[256,768]{1,0:T(8,128)(2,1)S(1)} %shard_map.125), channel_id=1, source_target_pairs={{0,24},{24,0},{1,25},{25,1},{2,26},{26,2},{3,27},{27,3},{4,28},{28... | collective-permute-start | bytes 1179656 | tf_op jit(solution)/shard_map/ppermute | solution.py:625
  212.5 26.2 %collective-permute-start.38 = (bf16[256,768]{1,0:T(8,128)(2,1)S(1)}, bf16[256,768]{1,0:T(8,128)(2,1)S(1)}, u32[]{:S(2)}, u32[]{:S(2)}) collective-permute-start(bf16[256,768]{1,0:T(8,128)(2,1)S(1)} %shard_map.125), channel_id=1, source_target_pairs={{8,24},{16,0},{9,25},{17,1},{10,26},{18,2},{11,27},{19,3},{12,28},... | collective-permute-start | bytes 1179656 | tf_op jit(solution)/shard_map/ppermute | solution.py:624

commit v13 on v11

--- a/solution.py
+++ b/solution.py
@@ -604,19 +604,20 @@
     neighbour.two_blocks(third.one)
     hidden = gate_last(chunk, sums, [third.one, neighbour.sent])
     third_piece = third.own_block(hidden)
-    neighbour.one_block(hidden)
     third_home = lax.ppermute(third_piece, "seq", [(1, 2), (2, 1)])
-    theirs, mine = down([plane.theirs, plane.mine], hidden, neighbour.one)
+    theirs, mine = down([plane.theirs, plane.mine], hidden, [third_piece, neighbour.got_two])
+    neighbour.one_block(theirs)
+    theirs, _ = tie((theirs, third_home))
+    fourth, own = (Scatter(*shares) for shares in zip(chunk, theirs, mine))
+    fourth.two_blocks([])
+    third_far_home = lax.ppermute(tie((third_piece, third_home))[0], "seq", [(0, 2), (3, 1)])
     neighbour_piece = neighbour.own_block([])
-    theirs, _ = tie((theirs, [third_home, neighbour_piece]))
-    fourth, own = (Scatter(*shares) for shares in zip(chunk, theirs, mine))
-    third_far_home = lax.ppermute(tie((third_piece, third_home))[0], "seq", [(0, 2), (3, 1)])
     neighbour_home = swapped(neighbour_piece, "seq", 1, 1)
-    fourth.two_blocks([])
-    fourth.one_block([third_far_home, neighbour_home])
-    own.two_blocks(fourth.got_one)
+    fourth.one_block([])
+    own.two_blocks(fourth.got_two)
     fourth_piece = fourth.own_block([])
     own.one_block(fourth_piece)
+    fourth_piece, _ = tie((fourth_piece, [third_far_home, neighbour_home]))
     return [
         own.own_block([]),
         neighbour_home,

time: 238 us -> 227 us (0.954)
  waiting for transfers between devices: 87.3 us -> 73 us
    ppermute x1, waiting for transfers between devices: 9.3 us -> 0.01 us  [paired_chunks(): lax.ppermute(tie((third_piece, third_home))[0], 'seq', [(0, 2), (3, 1)])]
    ppermute x30, waiting for transfers between devices: 52.1 us -> 44.3 us  [swapped(): return lax.ppermute(array, axis, pairs)]
    ppermute x30, starting transfers between devices: 26.7 us -> 30.3 us  [swapped(): return lax.ppermute(array, axis, pairs)]
    ppermute x1, waiting for transfers between devices: 4.7 us -> 7.4 us  [paired_chunks(): lax.ppermute(fourth_piece, 'seq', [(0, 3), (3, 0)])]
    unnamed x64 -> x60, local copies, waits for them, and re-layouts: 12.8 us -> 12.8 us
  transfers between devices with their start and end apart: 40 -> 40, of which waited for: 19 -> 18; matrix products, arithmetic and copies ran while one was open for 2% -> 3% of each run, Pallas kernels for 27% -> 28%
where the time goes in v13:
time: 227 us; the launch traced here: 226 us
  Pallas kernels  75.1 us (33%)
  waiting for transfers between devices  73 us (32%)
  starting transfers between devices  55.2 us (24%)
  local copies, waits for them, and re-layouts  13.8 us (6%)
  other arithmetic  7.92 us (3%)
    ppermute x30, waiting for transfers between devices, swapped(): return lax.ppermute(array, axis, pairs)  44.3 us
    pallas_call x4, Pallas kernels, gate_part(): pl.pallas_call(functools.partial(gate_kernel, counts, len(xs), last), gri...  36.8 us
    ppermute x30, starting transfers between devices, swapped(): return lax.ppermute(array, axis, pairs)  30.3 us
    pallas_call x3, Pallas kernels, down_part(): pl.pallas_call(functools.partial(down_kernel, blocks, sections), grid_spe...  27.1 us
    unnamed x60, local copies, waits for them, and re-layouts  12.8 us
    ppermute x2, starting transfers between devices, shifted(): return lax.ppermute(array, axis, pairs)  9.43 us
    ppermute x2, waiting for transfers between devices, outward(): return lax.ppermute(part, 'seq', [(1, 0), (2, 3)])  8.98 us
    ppermute x1, waiting for transfers between devices, paired_chunks(): lax.ppermute(fourth_piece, 'seq', [(1, 3), (2, 0)])  8.33 us
  transfers between devices with their start and end apart: 40, of which 18 were waited for; matrix products, arithmetic and copies ran while one was open for 3% of the time, Pallas kernels for 28%

profile of v13, /device:TPU:0, one launch (start us, length us, event | category | flops | bytes accessed | tf_op | source)
XLA Modules:
  0.0 225.7 jit_solution(17337919608893811263)
XLA Ops:
  0.0 2.1 shard_map.109
  2.2 4.9 %collective-permute-start = (bf16[784,128]{1,0:T(8,128)(2,1)S(1)}, bf16[784,128]{1,0:T(8,128)(2,1)S(1)}, u32[]{:S(2)}, u32[]{:S(2)}) collective-permute-start(bf16[784,128]{1,0:T(8,128)(2,1)S(1)} %get-tuple-element.72), channel_id=1, source_target_pairs={{0,8},{8,16},{16,24},{1,9},{9,17},{17,25},{2,10},{10,18},{18,26},{... | collective-permute-start | bytes 602120 | tf_op jit(solution)/shard_map/ppermute | solution.py:30
  7.9 1.0 copy-done.4
  8.9 1.0 copy-done.6
  9.9 1.0 copy-done.7
  11.6 1.4 shard_map.110.intra_ref
  13.3 4.5 %collective-permute-start.1 = (bf16[784,128]{1,0:T(8,128)(2,1)S(1)}, bf16[784,128]{1,0:T(8,128)(2,1)S(1)}, u32[]{:S(2)}, u32[]{:S(2)}) collective-permute-start(bf16[784,128]{1,0:T(8,128)(2,1)S(1)} %concatenate.7), channel_id=1, source_target_pairs={{0,16},{8,24},{1,17},{9,25},{2,18},{10,26},{3,19},{11,27},{4,20},{... | collective-permute-start | bytes 602120 | tf_op jit(solution)/shard_map/ppermute | solution.py:30
  17.8 3.9 %collective-permute-done.1 = bf16[784,128]{1,0:T(8,128)(2,1)S(1)} collective-permute-done((bf16[784,128]{1,0:T(8,128)(2,1)S(1)}, bf16[784,128]{1,0:T(8,128)(2,1)S(1)}, u32[]{:S(2)}, u32[]{:S(2)}) %collective-permute-start.1) | collective-permute-done | bytes 200736 | tf_op jit(solution)/shard_map/ppermute | solution.py:30
  22.7 1.0 shard_map.112
  23.8 1.6 collective-permute-start.10
  25.3 4.4 %collective-permute-start.2 = (bf16[272,768]{1,0:T(8,128)(2,1)S(1)}, bf16[272,768]{1,0:T(8,128)(2,1)S(1)}, u32[]{:S(2)}, u32[]{:S(2)}) collective-permute-start(bf16[272,768]{1,0:T(8,128)(2,1)S(1)} %shard_map.111.refs_0_), channel_id=1, source_target_pairs={{0,8},{8,0},{16,24},{24,16},{1,9},{9,1},{17,25},{25,17},{2,10},{10... | collective-permute-start | bytes 1253384 | tf_op jit(solution)/shard_map/ppermute | solution.py:435
  30.5 1.2 collective-permute-done.10
  31.6 1.0 pad_maximum_fusion.3.refs_2_
  32.6 1.5 collective-permute-start.11
  34.1 3.9 %collective-permute-done.2.refs_0_ = bf16[272,768]{1,0:T(8,128)(2,1)S(1)} collective-permute-done((bf16[272,768]{1,0:T(8,128)(2,1)S(1)}, bf16[272,768]{1,0:T(8,128)(2,1)S(1)}, u32[]{:S(2)}, u32[]{:S(2)}) %collective-permute-start.2) | collective-permute-done | bytes 417824 | tf_op jit(solution)/shard_map/ppermute | solution.py:435
  38.0 1.0 shard_map.115
  39.1 1.6 collective-permute-start.9
  40.6 1.3 collective-permute-start.7
  42.6 4.3 %collective-permute-done.9 = bf16[768,256]{1,0:T(8,128)(2,1)S(1)} collective-permute-done((bf16[768,256]{1,0:T(8,128)(2,1)S(1)}, bf16[768,256]{1,0:T(8,128)(2,1)S(1)}, u32[]{:S(2)}, u32[]{:S(2)}) %collective-permute-start.9) | collective-permute-done | bytes 393248 | tf_op jit(solution)/shard_map/ppermute | solution.py:435
  47.0 5.3 %collective-permute-done.7.refs_1_ = bf16[272,768]{1,0:T(8,128)(2,1)S(1)} collective-permute-done((bf16[272,768]{1,0:T(8,128)(2,1)S(1)}, bf16[272,768]{1,0:T(8,128)(2,1)S(1)}, u32[]{:S(2)}, u32[]{:S(2)}) %collective-permute-start.7) | collective-permute-done | bytes 417824 | tf_op jit(solution)/shard_map/ppermute | solution.py:536
  52.4 1.0 shard_map.114
  53.4 2.5 %collective-permute-start.8 = (bf16[768,256]{1,0:T(8,128)(2,1)S(1)}, bf16[768,256]{1,0:T(8,128)(2,1)S(1)}, u32[]{:S(2)}, u32[]{:S(2)}) collective-permute-start(bf16[768,256]{1,0:T(8,128)(2,1)S(1)} %get-tuple-element.75), channel_id=1, source_target_pairs={{0,2},{1,5},{2,0},{3,7},{4,6},{5,1},{6,4},{7,3},{8,10},{9,13},{10,... | collective-permute-start | bytes 1179656 | tf_op jit(solution)/shard_map/ppermute | solution.py:435
  55.9 1.5 collective-permute-start.4
  57.5 8.5 %collective-permute-done.8 = bf16[768,256]{1,0:T(8,128)(2,1)S(1)} collective-permute-done((bf16[768,256]{1,0:T(8,128)(2,1)S(1)}, bf16[768,256]{1,0:T(8,128)(2,1)S(1)}, u32[]{:S(2)}, u32[]{:S(2)}) %collective-permute-start.8) | collective-permute-done | bytes 393248 | tf_op jit(solution)/shard_map/ppermute | solution.py:435
  66.0 3.7 %collective-permute-done.4.refs_1_ = bf16[272,768]{1,0:T(8,128)(2,1)S(1)} collective-permute-done((bf16[272,768]{1,0:T(8,128)(2,1)S(1)}, bf16[272,768]{1,0:T(8,128)(2,1)S(1)}, u32[]{:S(2)}, u32[]{:S(2)}) %collective-permute-start.4) | collective-permute-done | bytes 417824 | tf_op jit(solution)/shard_map/ppermute | solution.py:536
  71.0 1.0 copy-done.13
  72.0 1.0 copy-done.15
  73.0 1.0 shard_map.113
  75.9 1.1 copy-done.11
  77.8 8.9 %shard_map.116 = (f32[2,576,256]{2,1,0:T(8,128)S(1)}, f32[2,576,256]{2,1,0:T(8,128)S(1)}, f32[2,2,256]{2,1,0:T(2,128)S(1)}) custom-call(s32[4]{0:T(128)S(1)} %get-tuple-element.140.plan_ref, bf16[2,768,256]{2,1,0:T(8,128)(2,1)S(1)} %pad_maximum_fusion.1.refs_0_, bf16[2,768,256]{2,1,0:T(8,128)(2,1)} %collective-permute-done.13.refs_1_, ...), custom_call_target="tpu_custom_call" | custom-call | flops 3623878656 | bytes 14155776 | tf_op jit(solution)/shard_map/pallas_call | solution.py:347
  86.7 1.0 copy-done.8
  88.2 1.0 pad_maximum_fusion.refs_0_
  89.2 1.7 collective-permute-start.15
  92.0 9.7 %shard_map.117.hidden_ref = bf16[2,256,576]{2,1,0:T(8,128)(2,1)S(1)} custom-call(s32[4]{0:T(128)S(1)} %add_add_fusion.plan_ref, bf16[2,768,256]{2,1,0:T(8,128)(2,1)} %collective-permute-done.16.refs_0_, bf16[2,768,256]{2,1,0:T(8,128)(2,1)} %collective-permute-done.17.refs_1_, bf16[2,768,256]{2,1,0:T(8,128)(2,1)S(1)} %collective-permute-done.12.refs_2_, ...), custom_call_target="tpu_custom_call" | custom-call | flops 3623878656 | bytes 14155776 | tf_op jit(solution)/shard_map/pallas_call | solution.py:347
  101.7 7.2 %shard_map.118 = (bf16[4,256,768]{2,1,0:T(8,128)(2,1)S(1)}, bf16[4,256,768]{2,1,0:T(8,128)(2,1)S(1)}) custom-call(s32[4]{0:T(128)S(1)} %get-tuple-element.141.plan_ref, bf16[2,256,576]{2,1,0:T(8,128)(2,1)S(1)} %shard_map.117.hidden_ref, bf16[2,576,6144]{2,1,0:T(8,128)(2,1)} %down_ref.5), custom_call_target="tpu_custom_call" | custom-call | flops 1811939328 | bytes 7077888 | tf_op jit(solution)/shard_map/pallas_call | solution.py:406
  110.1 7.2 %shard_map.119 = (bf16[4,256,768]{2,1,0:T(8,128)(2,1)S(1)}, bf16[4,256,768]{2,1,0:T(8,128)(2,1)S(1)}) custom-call(s32[4]{0:T(128)S(1)} %pad_add_fusion.3.plan_ref, bf16[2,256,576]{2,1,0:T(8,128)(2,1)S(1)} %shard_map.117.hidden_ref, bf16[2,576,6144]{2,1,0:T(8,128)(2,1)} %down_ref.5), custom_call_target="tpu_custom_call" | custom-call | flops 1811939328 | bytes 7077888 | tf_op jit(solution)/shard_map/pallas_call | solution.py:406
  117.5 1.8 collective-permute-start.24
  119.8 8.9 %shard_map.120 = (f32[2,576,256]{2,1,0:T(8,128)S(1)}, f32[2,576,256]{2,1,0:T(8,128)S(1)}, f32[2,2,256]{2,1,0:T(2,128)S(1)}) custom-call(s32[4]{0:T(128)S(1)} %get-tuple-element.140.plan_ref, bf16[2,768,256]{2,1,0:T(8,128)(2,1)} %pad_maximum_fusion.refs_0_, bf16[2,768,256]{2,1,0:T(8,128)(2,1)S(1)} %collective-permute-done.22.refs_1_, ...), custom_call_target="tpu_custom_call" | custom-call | flops 3623878656 | bytes 14155776 | tf_op jit(solution)/shard_map/pallas_call | solution.py:347
  128.7 1.1 add_convert_fusion.2
  130.0 1.5 collective-permute-start.27
  131.5 1.7 collective-permute-start.26
  133.2 9.3 %shard_map.121.hidden_ref = bf16[2,256,576]{2,1,0:T(8,128)(2,1)S(1)} custom-call(s32[4]{0:T(128)S(1)} %add_add_fusion.plan_ref, bf16[2,768,256]{2,1,0:T(8,128)(2,1)} %collective-permute-done.15.refs_0_, bf16[2,768,256]{2,1,0:T(8,128)(2,1)S(1)} %collective-permute-done.20.refs_1_, bf16[2,768,256]{2,1,0:T(8,128)(2,1)} %collective-permute-done.11.refs_2_, ...), custom_call_target="tpu_custom_call" | custom-call | flops 3623878656 | bytes 14155776 | tf_op jit(solution)/shard_map/pallas_call | solution.py:347
  142.6 1.0 collective-permute-done.26
  144.0 1.4 collective-permute-start.28
  145.5 1.0 collective-permute-done.27.refs_2_
  146.6 1.1 copy-done.3
  147.7 12.7 %shard_map.123 = (bf16[4,256,768]{2,1,0:T(8,128)(2,1)S(1)}, bf16[4,256,768]{2,1,0:T(8,128)(2,1)S(1)}, bf16[4,256,768]{2,1,0:T(8,128)(2,1)S(1)}, bf16[4,256,768]{2,1,0:T(8,128)(2,1)S(1)}) custom-call(s32[8]{0:T(128)S(1)} %concatenate.8.plan_ref, bf16[2,256,576]{2,1,0:T(8,128)(2,1)S(1)} %copy-done.3, bf16[2,576,6144]{2,1,0:T(8,128)(2,1)} %down_ref.5), custom_call_target="tpu_custom_call" | custom-call | flops 3623878656 | bytes 14155776 | tf_op jit(solution)/shard_map/pallas_call | solution.py:406
  161.0 2.9 %collective-permute-done.30.refs_1_ = bf16[4,256,768]{2,1,0:T(8,128)(2,1)S(1)} collective-permute-done((bf16[4,256,768]{2,1,0:T(8,128)(2,1)S(1)}, bf16[4,256,768]{2,1,0:T(8,128)(2,1)S(1)}, u32[]{:S(2)}, u32[]{:S(2)}) %collective-permute-start.30) | collective-permute-done | bytes 1572896 | tf_op jit(solution)/shard_map/ppermute | solution.py:435
  164.1 1.1 collective-permute-start.31
  165.1 1.0 collective-permute-done.29.refs_1_
  166.3 9.8 %collective-permute-done.31.refs_2_ = bf16[2,256,768]{2,1,0:T(8,128)(2,1)S(1)} collective-permute-done((bf16[2,256,768]{2,1,0:T(8,128)(2,1)S(1)}, bf16[2,256,768]{2,1,0:T(8,128)(2,1)S(1)}, u32[]{:S(2)}, u32[]{:S(2)}) %collective-permute-start.31) | collective-permute-done | bytes 786464 | tf_op jit(solution)/shard_map/ppermute | solution.py:435
  176.1 1.0 collective-permute-start.32
  177.1 1.1 fusion.3
  178.3 1.2 collective-permute-start.35
  180.6 5.5 %collective-permute-start.37 = (bf16[256,768]{1,0:T(8,128)(2,1)S(1)}, bf16[256,768]{1,0:T(8,128)(2,1)S(1)}, u32[]{:S(2)}, u32[]{:S(2)}) collective-permute-start(bf16[256,768]{1,0:T(8,128)(2,1)S(1)} %shard_map.122), channel_id=1, source_target_pairs={{0,16},{24,8},{1,17},{25,9},{2,18},{26,10},{3,19},{27,11},{4,20},{... | collective-permute-start | bytes 1179656 | tf_op jit(solution)/shard_map/ppermute | solution.py:613
  186.1 4.3 %collective-permute-done.35 = bf16[256,768]{1,0:T(8,128)(2,1)S(1)} collective-permute-done((bf16[256,768]{1,0:T(8,128)(2,1)S(1)}, bf16[256,768]{1,0:T(8,128)(2,1)S(1)}, u32[]{:S(2)}, u32[]{:S(2)}) %collective-permute-start.35) | collective-permute-done | bytes 393248 | tf_op jit(solution)/shard_map/ppermute | solution.py:435
  190.4 1.5 shard_map.126
  191.9 3.4 %collective-permute-start.36 = (bf16[256,768]{1,0:T(8,128)(2,1)S(1)}, bf16[256,768]{1,0:T(8,128)(2,1)S(1)}, u32[]{:S(2)}, u32[]{:S(2)}) collective-permute-start(bf16[256,768]{1,0:T(8,128)(2,1)S(1)} %shard_map.126), channel_id=1, source_target_pairs={{0,8},{8,0},{16,24},{24,16},{1,9},{9,1},{17,25},{25,17},{2,10},{10... | collective-permute-start | bytes 1179656 | tf_op jit(solution)/shard_map/ppermute | solution.py:435
  197.5 5.4 %collective-permute-done.36 = bf16[256,768]{1,0:T(8,128)(2,1)S(1)} collective-permute-done((bf16[256,768]{1,0:T(8,128)(2,1)S(1)}, bf16[256,768]{1,0:T(8,128)(2,1)S(1)}, u32[]{:S(2)}, u32[]{:S(2)}) %collective-permute-start.36) | collective-permute-done | bytes 393248 | tf_op jit(solution)/shard_map/ppermute | solution.py:435
  202.8 3.2 %collective-permute-start.39 = (bf16[256,768]{1,0:T(8,128)(2,1)S(1)}, bf16[256,768]{1,0:T(8,128)(2,1)S(1)}, u32[]{:S(2)}, u32[]{:S(2)}) collective-permute-start(bf16[256,768]{1,0:T(8,128)(2,1)S(1)} %shard_map.124), channel_id=1, source_target_pairs={{0,24},{24,0},{1,25},{25,1},{2,26},{26,2},{3,27},{27,3},{4,28},{28... | collective-permute-start | bytes 1179656 | tf_op jit(solution)/shard_map/ppermute | solution.py:627
  206.1 1.3 collective-permute-start.38
  207.8 7.4 %collective-permute-done.39 = bf16[256,768]{1,0:T(8,128)(2,1)S(1)} collective-permute-done((bf16[256,768]{1,0:T(8,128)(2,1)S(1)}, bf16[256,768]{1,0:T(8,128)(2,1)S(1)}, u32[]{:S(2)}, u32[]{:S(2)}) %collective-permute-start.39) | collective-permute-done | bytes 393248 | tf_op jit(solution)/shard_map/ppermute | solution.py:627
  215.2 8.3 %collective-permute-done.38 = bf16[256,768]{1,0:T(8,128)(2,1)S(1)} collective-permute-done((bf16[256,768]{1,0:T(8,128)(2,1)S(1)}, bf16[256,768]{1,0:T(8,128)(2,1)S(1)}, u32[]{:S(2)}, u32[]{:S(2)}) %collective-permute-start.38) | collective-permute-done | bytes 393248 | tf_op jit(solution)/shard_map/ppermute | solution.py:626
  223.6 2.1 add_convert_fusion.8
  (123 shorter events, 17.0 us)
Async XLA Ops:
  2.2 10.8 %collective-permute-start = (bf16[784,128]{1,0:T(8,128)(2,1)S(1)}, bf16[784,128]{1,0:T(8,128)(2,1)S(1)}, u32[]{:S(2)}, u32[]{:S(2)}) collective-permute-start(bf16[784,128]{1,0:T(8,128)(2,1)S(1)} %get-tuple-element.72), channel_id=1, source_target_pairs={{0,8},{8,16},{16,24},{1,9},{9,17},{17,25},{2,10},{10,18},{18,26},{... | collective-permute-start | bytes 602120 | tf_op jit(solution)/shard_map/ppermute | solution.py:30
  7.9 1.0 copy-start.4
  8.9 1.0 copy-start.6
  9.9 1.0 copy-start.7
  13.0 8.9 %copy-start.5 = (bf16[256,768]{1,0:T(8,128)(2,1)S(1)}, bf16[256,768]{1,0:T(8,128)(2,1)}, u32[]{:S(2)}) copy-start(bf16[256,768]{1,0:T(8,128)(2,1)} %query_ref.3) | copy-start | bytes 1179652
  13.0 8.9 %copy-start.19 = (bf16[256,768]{1,0:T(8,128)(2,1)S(1)}, bf16[256,768]{1,0:T(8,128)(2,1)}, u32[]{:S(2)}) copy-start(bf16[256,768]{1,0:T(8,128)(2,1)} %residual_ref.1) | copy-start | bytes 1179652
  13.0 8.9 %copy-start.29 = (s32[256,2]{0,1:T(2,128)S(1)}, s32[256,2]{0,1:T(2,128)}, u32[]{:S(2)}) copy-start(s32[256,2]{0,1:T(2,128)} %param.17) | copy-start | bytes 6148
  13.3 8.5 %collective-permute-start.1 = (bf16[784,128]{1,0:T(8,128)(2,1)S(1)}, bf16[784,128]{1,0:T(8,128)(2,1)S(1)}, u32[]{:S(2)}, u32[]{:S(2)}) collective-permute-start(bf16[784,128]{1,0:T(8,128)(2,1)S(1)} %concatenate.7), channel_id=1, source_target_pairs={{0,16},{8,24},{1,17},{9,25},{2,18},{10,26},{3,19},{11,27},{4,20},{... | collective-permute-start | bytes 602120 | tf_op jit(solution)/shard_map/ppermute | solution.py:30
  22.7 24.3 %copy-start = (bf16[272,768]{1,0:T(8,128)(2,1)}, bf16[272,768]{1,0:T(8,128)(2,1)S(1)}, u32[]{:S(2)}) copy-start(bf16[272,768]{1,0:T(8,128)(2,1)S(1)} %shard_map.111.refs_0_) | copy-start | bytes 1253380
  23.8 10.3 %copy-start.20 = (bf16[256,256]{1,0:T(8,128)(2,1)}, bf16[256,256]{1,0:T(8,128)(2,1)S(1)}, u32[]{:S(2)}) copy-start(bf16[256,256]{1,0:T(8,128)(2,1)S(1)} %get-tuple-element.73.place_ref) | copy-start | bytes 393220
  23.8 7.8 %collective-permute-start.10 = (bf16[768,256]{1,0:T(8,128)(2,1)S(1)}, bf16[768,256]{1,0:T(8,128)(2,1)S(1)}, u32[]{:S(2)}, u32[]{:S(2)}) collective-permute-start(bf16[768,256]{1,0:T(8,128)(2,1)S(1)} %get-tuple-element.77), channel_id=1, source_target_pairs={{0,2},{1,5},{2,0},{3,7},{4,6},{5,1},{6,4},{7,3},{8,10},{9,13},{10,... | collective-permute-start | bytes 1179656 | tf_op jit(solution)/shard_map/ppermute | solution.py:435
  25.3 12.7 %collective-permute-start.2 = (bf16[272,768]{1,0:T(8,128)(2,1)S(1)}, bf16[272,768]{1,0:T(8,128)(2,1)S(1)}, u32[]{:S(2)}, u32[]{:S(2)}) collective-permute-start(bf16[272,768]{1,0:T(8,128)(2,1)S(1)} %shard_map.111.refs_0_), channel_id=1, source_target_pairs={{0,8},{8,0},{16,24},{24,16},{1,9},{9,1},{17,25},{25,17},{2,10},{10... | collective-permute-start | bytes 1253384 | tf_op jit(solution)/shard_map/ppermute | solution.py:435
  29.8 10.8 %collective-permute-start.6 = (bf16[272,768]{1,0:T(8,128)(2,1)S(1)}, bf16[272,768]{1,0:T(8,128)(2,1)S(1)}, u32[]{:S(2)}, u32[]{:S(2)}) collective-permute-start(bf16[272,768]{1,0:T(8,128)(2,1)S(1)} %shard_map.111.refs_0_), channel_id=1, source_target_pairs={{8,16},{16,8},{9,17},{17,9},{10,18},{18,10},{11,19},{19,11},{12,20... | collective-permute-start | bytes 1253384 | tf_op jit(solution)/shard_map/ppermute | solution.py:533
  32.6 19.7 %collective-permute-start.11 = (bf16[2,768,256]{2,1,0:T(8,128)(2,1)}, bf16[2,768,256]{2,1,0:T(8,128)(2,1)}, u32[]{:S(2)}, u32[]{:S(2)}) collective-permute-start(bf16[2,768,256]{2,1,0:T(8,128)(2,1)} %pad_maximum_fusion.3.refs_2_), channel_id=1, source_target_pairs={{0,4},{1,3},{2,6},{3,1},{4,0},{5,7},{6,2},{7,5},{8,12},{9,11},{10,... | collective-permute-start | bytes 2359304 | tf_op jit(solution)/shard_map/ppermute | solution.py:435
  39.1 27.0 %copy-start.22 = (bf16[256,256]{1,0:T(8,128)(2,1)}, bf16[256,256]{1,0:T(8,128)(2,1)S(1)}, u32[]{:S(2)}) copy-start(bf16[256,256]{1,0:T(8,128)(2,1)S(1)} %get-tuple-element.133.place_ref) | copy-start | bytes 393220
  39.1 7.8 %collective-permute-start.9 = (bf16[768,256]{1,0:T(8,128)(2,1)S(1)}, bf16[768,256]{1,0:T(8,128)(2,1)S(1)}, u32[]{:S(2)}, u32[]{:S(2)}) collective-permute-start(bf16[768,256]{1,0:T(8,128)(2,1)S(1)} %get-tuple-element.76), channel_id=1, source_target_pairs={{0,2},{1,5},{2,0},{3,7},{4,6},{5,1},{6,4},{7,3},{8,10},{9,13},{10,... | collective-permute-start | bytes 1179656 | tf_op jit(solution)/shard_map/ppermute | solution.py:435
  40.6 11.6 %collective-permute-start.7 = (bf16[272,768]{1,0:T(8,128)(2,1)S(1)}, bf16[272,768]{1,0:T(8,128)(2,1)S(1)}, u32[]{:S(2)}, u32[]{:S(2)}) collective-permute-start(bf16[272,768]{1,0:T(8,128)(2,1)S(1)} %collective-permute-done.6.refs_0_), channel_id=1, source_target_pairs={{8,0},{16,24},{9,1},{17,25},{10,2},{18,26},{11,3},{19,27},{12,4},{... | collective-permute-start | bytes 1253384 | tf_op jit(solution)/shard_map/ppermute | solution.py:536
  41.9 10.4 %collective-permute-start.3 = (bf16[272,768]{1,0:T(8,128)(2,1)S(1)}, bf16[272,768]{1,0:T(8,128)(2,1)S(1)}, u32[]{:S(2)}, u32[]{:S(2)}) collective-permute-start(bf16[272,768]{1,0:T(8,128)(2,1)S(1)} %collective-permute-done.2.refs_0_), channel_id=1, source_target_pairs={{8,16},{16,8},{9,17},{17,9},{10,18},{18,10},{11,19},{19,11},{12,20... | collective-permute-start | bytes 1253384 | tf_op jit(solution)/shard_map/ppermute | solution.py:533
  52.3 18.2 %copy-start.12 = (bf16[272,768]{1,0:T(8,128)(2,1)}, bf16[272,768]{1,0:T(8,128)(2,1)S(1)}, u32[]{:S(2)}) copy-start(bf16[272,768]{1,0:T(8,128)(2,1)S(1)} %collective-permute-done.3.refs_0_) | copy-start | bytes 1253380
  52.3 18.2 %collective-permute-start.12 = (bf16[2,768,256]{2,1,0:T(8,128)(2,1)S(1)}, bf16[2,768,256]{2,1,0:T(8,128)(2,1)S(1)}, u32[]{:S(2)}, u32[]{:S(2)}) collective-permute-start(bf16[2,768,256]{2,1,0:T(8,128)(2,1)S(1)} %pad_maximum_fusion.2.refs_2_), channel_id=1, source_target_pairs={{0,4},{1,3},{2,6},{3,1},{4,0},{5,7},{6,2},{7,5},{8,12},{9,11},{10,... | collective-permute-start | bytes 2359304 | tf_op jit(solution)/shard_map/ppermute | solution.py:435
  53.4 17.1 %copy-start.26 = (bf16[256,256]{1,0:T(8,128)(2,1)}, bf16[256,256]{1,0:T(8,128)(2,1)S(1)}, u32[]{:S(2)}) copy-start(bf16[256,256]{1,0:T(8,128)(2,1)S(1)} %get-tuple-element.121.place_ref) | copy-start | bytes 393220
  53.4 12.5 %collective-permute-start.8 = (bf16[768,256]{1,0:T(8,128)(2,1)S(1)}, bf16[768,256]{1,0:T(8,128)(2,1)S(1)}, u32[]{:S(2)}, u32[]{:S(2)}) collective-permute-start(bf16[768,256]{1,0:T(8,128)(2,1)S(1)} %get-tuple-element.75), channel_id=1, source_target_pairs={{0,2},{1,5},{2,0},{3,7},{4,6},{5,1},{6,4},{7,3},{8,10},{9,13},{10,... | collective-permute-start | bytes 1179656 | tf_op jit(solution)/shard_map/ppermute | solution.py:435
  55.9 13.8 %collective-permute-start.4 = (bf16[272,768]{1,0:T(8,128)(2,1)S(1)}, bf16[272,768]{1,0:T(8,128)(2,1)S(1)}, u32[]{:S(2)}, u32[]{:S(2)}) collective-permute-start(bf16[272,768]{1,0:T(8,128)(2,1)S(1)} %collective-permute-done.3.refs_0_), channel_id=1, source_target_pairs={{8,0},{16,24},{9,1},{17,25},{10,2},{18,26},{11,3},{19,27},{12,4},{... | collective-permute-start | bytes 1253384 | tf_op jit(solution)/shard_map/ppermute | solution.py:536
  57.4 17.6 %collective-permute-start.14 = (bf16[2,768,256]{2,1,0:T(8,128)(2,1)S(1)}, bf16[2,768,256]{2,1,0:T(8,128)(2,1)S(1)}, u32[]{:S(2)}, u32[]{:S(2)}) collective-permute-start(bf16[2,768,256]{2,1,0:T(8,128)(2,1)S(1)} %pad_maximum_fusion.2.refs_2_), channel_id=1, source_target_pairs={{0,1},{1,0},{2,3},{3,2},{4,5},{5,4},{6,7},{7,6},{8,9},{9,8},{10,11... | collective-permute-start | bytes 2359304 | tf_op jit(solution)/shard_map/ppermute | solution.py:435
  70.5 5.4 %collective-permute-start.13 = (bf16[2,768,256]{2,1,0:T(8,128)(2,1)S(1)}, bf16[2,768,256]{2,1,0:T(8,128)(2,1)}, u32[]{:S(2)}, u32[]{:S(2)}) collective-permute-start(bf16[2,768,256]{2,1,0:T(8,128)(2,1)S(1)} %pad_maximum_fusion.1.refs_0_), channel_id=1, source_target_pairs={{0,1},{1,0},{2,3},{3,2},{4,5},{5,4},{6,7},{7,6},{8,9},{9,8},{10,11... | collective-permute-start | bytes 2359304 | tf_op jit(solution)/shard_map/ppermute | solution.py:435
  70.5 17.2 %collective-permute-start.16 = (bf16[2,768,256]{2,1,0:T(8,128)(2,1)S(1)}, bf16[2,768,256]{2,1,0:T(8,128)(2,1)}, u32[]{:S(2)}, u32[]{:S(2)}) collective-permute-start(bf16[2,768,256]{2,1,0:T(8,128)(2,1)S(1)} %pad_maximum_fusion.1.refs_0_), channel_id=1, source_target_pairs={{0,4},{1,3},{2,6},{3,1},{4,0},{5,7},{6,2},{7,5},{8,12},{9,11},{10,... | collective-permute-start | bytes 2359304 | tf_op jit(solution)/shard_map/ppermute | solution.py:435
  71.0 1.0 copy-start.13
  72.0 1.0 copy-start.15
  74.7 13.5 %collective-permute-start.5 = (bf16[768,256]{1,0:T(8,128)(2,1)S(1)}, bf16[768,256]{1,0:T(8,128)(2,1)S(1)}, u32[]{:S(2)}, u32[]{:S(2)}) collective-permute-start(bf16[768,256]{1,0:T(8,128)(2,1)S(1)} %get-tuple-element.74), channel_id=1, source_target_pairs={{0,2},{1,5},{2,0},{3,7},{4,6},{5,1},{6,4},{7,3},{8,10},{9,13},{10,... | collective-permute-start | bytes 1179656 | tf_op jit(solution)/shard_map/ppermute | solution.py:435
  75.9 1.1 copy-start.11
  86.7 1.0 copy-start.8
  87.7 3.5 %copy-start.9 = (f32[2,576,256]{2,1,0:T(8,128)S(1)}, f32[2,576,256]{2,1,0:T(8,128)}, u32[]{:S(2)}) copy-start(f32[2,576,256]{2,1,0:T(8,128)} %copy-done.8) | copy-start | bytes 3538948
  87.7 3.3 %collective-permute-start.17 = (bf16[2,768,256]{2,1,0:T(8,128)(2,1)}, bf16[2,768,256]{2,1,0:T(8,128)(2,1)}, u32[]{:S(2)}, u32[]{:S(2)}) collective-permute-start(bf16[2,768,256]{2,1,0:T(8,128)(2,1)} %collective-permute-done.16.refs_0_), channel_id=1, source_target_pairs={{0,1},{1,0},{2,3},{3,2},{4,5},{5,4},{6,7},{7,6},{8,9},{9,8},{10,11... | collective-permute-start | bytes 2359304 | tf_op jit(solution)/shard_map/ppermute | solution.py:435
  87.7 3.5 %collective-permute-start.18 = (bf16[2,768,256]{2,1,0:T(8,128)(2,1)S(1)}, bf16[2,768,256]{2,1,0:T(8,128)(2,1)}, u32[]{:S(2)}, u32[]{:S(2)}) collective-permute-start(bf16[2,768,256]{2,1,0:T(8,128)(2,1)S(1)} %collective-permute-done.12.refs_2_), channel_id=1, source_target_pairs={{0,1},{1,0},{2,3},{3,2},{4,5},{5,4},{6,7},{7,6},{8,9},{9,8},{10,11... | collective-permute-start | bytes 2359304 | tf_op jit(solution)/shard_map/ppermute | solution.py:435
  89.2 12.5 %collective-permute-start.15 = (bf16[2,768,256]{2,1,0:T(8,128)(2,1)}, bf16[2,768,256]{2,1,0:T(8,128)(2,1)}, u32[]{:S(2)}, u32[]{:S(2)}) collective-permute-start(bf16[2,768,256]{2,1,0:T(8,128)(2,1)} %pad_maximum_fusion.refs_0_), channel_id=1, source_target_pairs={{0,4},{1,3},{2,6},{3,1},{4,0},{5,7},{6,2},{7,5},{8,12},{9,11},{10,... | collective-permute-start | bytes 2359304 | tf_op jit(solution)/shard_map/ppermute | solution.py:435
  108.9 8.4 %collective-permute-start.19 = (bf16[4,256,768]{2,1,0:T(8,128)(2,1)S(1)}, bf16[4,256,768]{2,1,0:T(8,128)(2,1)S(1)}, u32[]{:S(2)}, u32[]{:S(2)}) collective-permute-start(bf16[4,256,768]{2,1,0:T(8,128)(2,1)S(1)} %get-tuple-element.99), channel_id=1, source_target_pairs={{0,1},{1,0},{2,3},{3,2},{4,5},{5,4},{6,7},{7,6},{8,9},{9,8},{10,11... | collective-permute-start | bytes 4718600 | tf_op jit(solution)/shard_map/ppermute | solution.py:435
  109.1 19.6 %collective-permute-start.25 = (bf16[4,256,768]{2,1,0:T(8,128)(2,1)S(1)}, bf16[4,256,768]{2,1,0:T(8,128)(2,1)S(1)}, u32[]{:S(2)}, u32[]{:S(2)}) collective-permute-start(bf16[4,256,768]{2,1,0:T(8,128)(2,1)S(1)} %get-tuple-element.100), channel_id=1, source_target_pairs={{0,1},{1,0},{2,3},{3,2},{4,5},{5,4},{6,7},{7,6},{8,9},{9,8},{10,11... | collective-permute-start | bytes 4718600 | tf_op jit(solution)/shard_map/ppermute | solution.py:435
  109.5 9.8 %collective-permute-start.23 = (bf16[2,768,256]{2,1,0:T(8,128)(2,1)}, bf16[2,768,256]{2,1,0:T(8,128)(2,1)S(1)}, u32[]{:S(2)}, u32[]{:S(2)}) collective-permute-start(bf16[2,768,256]{2,1,0:T(8,128)(2,1)} %pad_maximum_fusion.3.refs_2_), channel_id=1, source_target_pairs={{0,1},{1,0},{2,3},{3,2},{4,5},{5,4},{6,7},{7,6},{8,9},{9,8},{10,11... | collective-permute-start | bytes 2359304 | tf_op jit(solution)/shard_map/ppermute | solution.py:435
  109.6 9.7 %collective-permute-start.22 = (bf16[2,768,256]{2,1,0:T(8,128)(2,1)}, bf16[2,768,256]{2,1,0:T(8,128)(2,1)S(1)}, u32[]{:S(2)}, u32[]{:S(2)}) collective-permute-start(bf16[2,768,256]{2,1,0:T(8,128)(2,1)} %pad_maximum_fusion.refs_0_), channel_id=1, source_target_pairs={{0,1},{1,0},{2,3},{3,2},{4,5},{5,4},{6,7},{7,6},{8,9},{9,8},{10,11... | collective-permute-start | bytes 2359304 | tf_op jit(solution)/shard_map/ppermute | solution.py:435
  117.3 2.5 %copy-start.18 = (bf16[6144,2]{0,1:T(2,128)(2,1)S(1)}, bf16[6144,2]{0,1:T(2,128)(2,1)}, u32[]{:S(2)}) copy-start(bf16[6144,2]{0,1:T(2,128)(2,1)} %param.18) | copy-start | bytes 73732
  117.5 12.3 %collective-permute-start.24 = (bf16[2,256,768]{2,1,0:T(8,128)(2,1)S(1)}, bf16[2,256,768]{2,1,0:T(8,128)(2,1)S(1)}, u32[]{:S(2)}, u32[]{:S(2)}) collective-permute-start(bf16[2,256,768]{2,1,0:T(8,128)(2,1)S(1)} %add_convert_fusion.3), channel_id=1, source_target_pairs={{0,4},{1,3},{2,6},{3,1},{4,0},{5,7},{6,2},{7,5},{8,12},{9,11},{10,... | collective-permute-start | bytes 2359304 | tf_op jit(solution)/shard_map/ppermute | solution.py:435
  119.3 14.0 %collective-permute-start.20 = (bf16[2,768,256]{2,1,0:T(8,128)(2,1)}, bf16[2,768,256]{2,1,0:T(8,128)(2,1)S(1)}, u32[]{:S(2)}, u32[]{:S(2)}) collective-permute-start(bf16[2,768,256]{2,1,0:T(8,128)(2,1)} %collective-permute-done.15.refs_0_), channel_id=1, source_target_pairs={{0,1},{1,0},{2,3},{3,2},{4,5},{5,4},{6,7},{7,6},{8,9},{9,8},{10,11... | collective-permute-start | bytes 2359304 | tf_op jit(solution)/shard_map/ppermute | solution.py:435
  119.3 13.9 %collective-permute-start.21 = (bf16[2,768,256]{2,1,0:T(8,128)(2,1)}, bf16[2,768,256]{2,1,0:T(8,128)(2,1)S(1)}, u32[]{:S(2)}, u32[]{:S(2)}) collective-permute-start(bf16[2,768,256]{2,1,0:T(8,128)(2,1)} %collective-permute-done.11.refs_2_), channel_id=1, source_target_pairs={{0,1},{1,0},{2,3},{3,2},{4,5},{5,4},{6,7},{7,6},{8,9},{9,8},{10,11... | collective-permute-start | bytes 2359304 | tf_op jit(solution)/shard_map/ppermute | solution.py:435
  130.0 13.6 %copy-start.27 = (bf16[256,256]{1,0:T(8,128)(2,1)S(1)}, bf16[256,256]{1,0:T(8,128)(2,1)}, u32[]{:S(2)}) copy-start(bf16[256,256]{1,0:T(8,128)(2,1)} %copy-done.26) | copy-start | bytes 393220
  130.0 16.6 %collective-permute-start.27 = (bf16[2,256,768]{2,1,0:T(8,128)(2,1)}, bf16[2,256,768]{2,1,0:T(8,128)(2,1)}, u32[]{:S(2)}, u32[]{:S(2)}) collective-permute-start(bf16[2,256,768]{2,1,0:T(8,128)(2,1)} %add_convert_fusion.2), channel_id=1, source_target_pairs={{0,4},{1,3},{2,6},{3,1},{4,0},{5,7},{6,2},{7,5},{8,12},{9,11},{10,... | collective-permute-start | bytes 2359304 | tf_op jit(solution)/shard_map/ppermute | solution.py:435
  131.5 12.1 %collective-permute-start.26 = (bf16[256,768]{1,0:T(8,128)(2,1)S(1)}, bf16[256,768]{1,0:T(8,128)(2,1)S(1)}, u32[]{:S(2)}, u32[]{:S(2)}) collective-permute-start(bf16[256,768]{1,0:T(8,128)(2,1)S(1)} %fusion), channel_id=1, source_target_pairs={{0,2},{1,5},{2,0},{3,7},{4,6},{5,1},{6,4},{7,3},{8,10},{9,13},{10,... | collective-permute-start | bytes 1179656 | tf_op jit(solution)/shard_map/ppermute | solution.py:435
  142.6 1.4 copy-start.2
  144.0 16.4 %collective-permute-start.28 = (bf16[256,768]{1,0:T(8,128)(2,1)S(1)}, bf16[256,768]{1,0:T(8,128)(2,1)}, u32[]{:S(2)}, u32[]{:S(2)}) collective-permute-start(bf16[256,768]{1,0:T(8,128)(2,1)S(1)} %shard_map.122), channel_id=1, source_target_pairs={{8,16},{16,8},{9,17},{17,9},{10,18},{18,10},{11,19},{19,11},{12,20... | collective-permute-start | bytes 1179656 | tf_op jit(solution)/shard_map/ppermute | solution.py:607
  146.6 1.1 copy-start.3
  160.4 3.5 %collective-permute-start.30 = (bf16[4,256,768]{2,1,0:T(8,128)(2,1)S(1)}, bf16[4,256,768]{2,1,0:T(8,128)(2,1)S(1)}, u32[]{:S(2)}, u32[]{:S(2)}) collective-permute-start(bf16[4,256,768]{2,1,0:T(8,128)(2,1)S(1)} %get-tuple-element.130), channel_id=1, source_target_pairs={{0,1},{1,0},{2,3},{3,2},{4,5},{5,4},{6,7},{7,6},{8,9},{9,8},{10,11... | collective-permute-start | bytes 4718600 | tf_op jit(solution)/shard_map/ppermute | solution.py:435
  160.5 5.6 %collective-permute-start.29 = (bf16[4,256,768]{2,1,0:T(8,128)(2,1)S(1)}, bf16[4,256,768]{2,1,0:T(8,128)(2,1)S(1)}, u32[]{:S(2)}, u32[]{:S(2)}) collective-permute-start(bf16[4,256,768]{2,1,0:T(8,128)(2,1)S(1)} %get-tuple-element.128), channel_id=1, source_target_pairs={{0,1},{1,0},{2,3},{3,2},{4,5},{5,4},{6,7},{7,6},{8,9},{9,8},{10,11... | collective-permute-start | bytes 4718600 | tf_op jit(solution)/shard_map/ppermute | solution.py:435
  164.1 12.1 %collective-permute-start.31 = (bf16[2,256,768]{2,1,0:T(8,128)(2,1)S(1)}, bf16[2,256,768]{2,1,0:T(8,128)(2,1)S(1)}, u32[]{:S(2)}, u32[]{:S(2)}) collective-permute-start(bf16[2,256,768]{2,1,0:T(8,128)(2,1)S(1)} %add_convert_fusion), channel_id=1, source_target_pairs={{0,4},{1,3},{2,6},{3,1},{4,0},{5,7},{6,2},{7,5},{8,12},{9,11},{10,... | collective-permute-start | bytes 2359304 | tf_op jit(solution)/shard_map/ppermute | solution.py:435
  166.3 24.1 %copy-start.23 = (bf16[256,256]{1,0:T(8,128)(2,1)S(1)}, bf16[256,256]{1,0:T(8,128)(2,1)}, u32[]{:S(2)}) copy-start(bf16[256,256]{1,0:T(8,128)(2,1)} %copy-done.22) | copy-start | bytes 393220
  176.1 20.4 %collective-permute-start.32 = (bf16[2,256,768]{2,1,0:T(8,128)(2,1)S(1)}, bf16[2,256,768]{2,1,0:T(8,128)(2,1)S(1)}, u32[]{:S(2)}, u32[]{:S(2)}) collective-permute-start(bf16[2,256,768]{2,1,0:T(8,128)(2,1)S(1)} %add_convert_fusion.1), channel_id=1, source_target_pairs={{0,4},{1,3},{2,6},{3,1},{4,0},{5,7},{6,2},{7,5},{8,12},{9,11},{10,... | collective-permute-start | bytes 2359304 | tf_op jit(solution)/shard_map/ppermute | solution.py:435
  178.3 12.1 %collective-permute-start.35 = (bf16[256,768]{1,0:T(8,128)(2,1)S(1)}, bf16[256,768]{1,0:T(8,128)(2,1)S(1)}, u32[]{:S(2)}, u32[]{:S(2)}) collective-permute-start(bf16[256,768]{1,0:T(8,128)(2,1)S(1)} %fusion.3), channel_id=1, source_target_pairs={{0,2},{1,5},{2,0},{3,7},{4,6},{5,1},{6,4},{7,3},{8,10},{9,13},{10,... | collective-permute-start | bytes 1179656 | tf_op jit(solution)/shard_map/ppermute | solution.py:435
  179.7 15.6 %collective-permute-start.33 = (bf16[256,768]{1,0:T(8,128)(2,1)S(1)}, bf16[256,768]{1,0:T(8,128)(2,1)S(1)}, u32[]{:S(2)}, u32[]{:S(2)}) collective-permute-start(bf16[256,768]{1,0:T(8,128)(2,1)S(1)} %fusion.1), channel_id=1, source_target_pairs={{0,2},{1,5},{2,0},{3,7},{4,6},{5,1},{6,4},{7,3},{8,10},{9,13},{10,... | collective-permute-start | bytes 1179656 | tf_op jit(solution)/shard_map/ppermute | solution.py:435
  180.6 16.9 %collective-permute-start.37 = (bf16[256,768]{1,0:T(8,128)(2,1)S(1)}, bf16[256,768]{1,0:T(8,128)(2,1)S(1)}, u32[]{:S(2)}, u32[]{:S(2)}) collective-permute-start(bf16[256,768]{1,0:T(8,128)(2,1)S(1)} %shard_map.122), channel_id=1, source_target_pairs={{0,16},{24,8},{1,17},{25,9},{2,18},{26,10},{3,19},{27,11},{4,20},{... | collective-permute-start | bytes 1179656 | tf_op jit(solution)/shard_map/ppermute | solution.py:613
  190.4 4.9 %copy-start.25 = (bf16[256,256]{1,0:T(8,128)(2,1)S(1)}, bf16[256,256]{1,0:T(8,128)(2,1)}, u32[]{:S(2)}) copy-start(bf16[256,256]{1,0:T(8,128)(2,1)} %copy-done.24) | copy-start | bytes 393220
  191.9 11.0 %collective-permute-start.36 = (bf16[256,768]{1,0:T(8,128)(2,1)S(1)}, bf16[256,768]{1,0:T(8,128)(2,1)S(1)}, u32[]{:S(2)}, u32[]{:S(2)}) collective-permute-start(bf16[256,768]{1,0:T(8,128)(2,1)S(1)} %shard_map.126), channel_id=1, source_target_pairs={{0,8},{8,0},{16,24},{24,16},{1,9},{9,1},{17,25},{25,17},{2,10},{10... | collective-permute-start | bytes 1179656 | tf_op jit(solution)/shard_map/ppermute | solution.py:435
  195.7 11.7 %copy-start.21 = (bf16[256,256]{1,0:T(8,128)(2,1)S(1)}, bf16[256,256]{1,0:T(8,128)(2,1)}, u32[]{:S(2)}) copy-start(bf16[256,256]{1,0:T(8,128)(2,1)} %copy-done.20) | copy-start | bytes 393220
  196.7 10.7 %collective-permute-start.34 = (bf16[256,768]{1,0:T(8,128)(2,1)S(1)}, bf16[256,768]{1,0:T(8,128)(2,1)S(1)}, u32[]{:S(2)}, u32[]{:S(2)}) collective-permute-start(bf16[256,768]{1,0:T(8,128)(2,1)S(1)} %fusion.2), channel_id=1, source_target_pairs={{0,2},{1,5},{2,0},{3,7},{4,6},{5,1},{6,4},{7,3},{8,10},{9,13},{10,... | collective-permute-start | bytes 1179656 | tf_op jit(solution)/shard_map/ppermute | solution.py:435
  202.8 12.4 %collective-permute-start.39 = (bf16[256,768]{1,0:T(8,128)(2,1)S(1)}, bf16[256,768]{1,0:T(8,128)(2,1)S(1)}, u32[]{:S(2)}, u32[]{:S(2)}) collective-permute-start(bf16[256,768]{1,0:T(8,128)(2,1)S(1)} %shard_map.124), channel_id=1, source_target_pairs={{0,24},{24,0},{1,25},{25,1},{2,26},{26,2},{3,27},{27,3},{4,28},{28... | collective-permute-start | bytes 1179656 | tf_op jit(solution)/shard_map/ppermute | solution.py:627
  206.1 17.5 %collective-permute-start.38 = (bf16[256,768]{1,0:T(8,128)(2,1)S(1)}, bf16[256,768]{1,0:T(8,128)(2,1)S(1)}, u32[]{:S(2)}, u32[]{:S(2)}) collective-permute-start(bf16[256,768]{1,0:T(8,128)(2,1)S(1)} %shard_map.124), channel_id=1, source_target_pairs={{8,24},{16,0},{9,25},{17,1},{10,26},{18,2},{11,27},{19,3},{12,28},... | collective-permute-start | bytes 1179656 | tf_op jit(solution)/shard_map/ppermute | solution.py:626
  207.4 16.2 %copy-start.1 = (bf16[272,768]{1,0:T(8,128)(2,1)S(1)}, bf16[272,768]{1,0:T(8,128)(2,1)}, u32[]{:S(2)}) copy-start(bf16[272,768]{1,0:T(8,128)(2,1)} %copy-done) | copy-start | bytes 1253380
  (6 other events, 4.5 us)

commit v14 on v13

--- a/solution.py
+++ b/solution.py
@@ -613,7 +613,7 @@
     third_far_home = lax.ppermute(tie((third_piece, third_home))[0], "seq", [(0, 2), (3, 1)])
     neighbour_piece = neighbour.own_block([])
     neighbour_home = swapped(neighbour_piece, "seq", 1, 1)
-    fourth.one_block([])
+    fourth.one_block([third_far_home, neighbour.got_one])
     own.two_blocks(fourth.got_two)
     fourth_piece = fourth.own_block([])
     own.one_block(fourth_piece)

time: 227 us -> 221 us (0.974)
  waiting for transfers between devices: 73 us -> 66.2 us
    ppermute x30, waiting for transfers between devices: 44.3 us -> 38.5 us  [swapped(): return lax.ppermute(array, axis, pairs)]
  transfers between devices with their start and end apart: 40 -> 40, of which waited for: 18 -> 20; matrix products, arithmetic and copies ran while one was open for 3% -> 3% of each run, Pallas kernels for 28% -> 29%
where the time goes in v14:
time: 221 us; the launch traced here: 219 us
  Pallas kernels  75.1 us (34%)
  waiting for transfers between devices  66.2 us (30%)
  starting transfers between devices  55.8 us (25%)
  local copies, waits for them, and re-layouts  13.8 us (6%)
  other arithmetic  7.92 us (4%)
    ppermute x30, waiting for transfers between devices, swapped(): return lax.ppermute(array, axis, pairs)  38.5 us
    pallas_call x4, Pallas kernels, gate_part(): pl.pallas_call(functools.partial(gate_kernel, counts, len(xs), last), gri...  36.8 us
    ppermute x30, starting transfers between devices, swapped(): return lax.ppermute(array, axis, pairs)  30.5 us
    pallas_call x3, Pallas kernels, down_part(): pl.pallas_call(functools.partial(down_kernel, blocks, sections), grid_spe...  27.1 us
    unnamed x60, local copies, waits for them, and re-layouts  12.8 us
    ppermute x2, starting transfers between devices, shifted(): return lax.ppermute(array, axis, pairs)  9.43 us
    ppermute x2, waiting for transfers between devices, outward(): return lax.ppermute(part, 'seq', [(1, 0), (2, 3)])  8.98 us
    ppermute x1, waiting for transfers between devices, paired_chunks(): lax.ppermute(fourth_piece, 'seq', [(1, 3), (2, 0)])  8.33 us
  transfers between devices with their start and end apart: 40, of which 20 were waited for; matrix products, arithmetic and copies ran while one was open for 3% of the time, Pallas kernels for 29%

profile of v14, /device:TPU:0, one launch (start us, length us, event | category | flops | bytes accessed | tf_op | source)
XLA Modules:
  0.0 219.5 jit_solution(649950630932734328)
XLA Ops:
  0.0 2.1 shard_map.109
  2.2 4.9 %collective-permute-start = (bf16[784,128]{1,0:T(8,128)(2,1)S(1)}, bf16[784,128]{1,0:T(8,128)(2,1)S(1)}, u32[]{:S(2)}, u32[]{:S(2)}) collective-permute-start(bf16[784,128]{1,0:T(8,128)(2,1)S(1)} %get-tuple-element.73), channel_id=1, source_target_pairs={{0,8},{8,16},{16,24},{1,9},{9,17},{17,25},{2,10},{10,18},{18,26},{... | collective-permute-start | bytes 602120 | tf_op jit(solution)/shard_map/ppermute | solution.py:30
  7.9 1.0 copy-done.4
  8.9 1.0 copy-done.6
  9.9 1.0 copy-done.7
  11.6 1.4 shard_map.110.intra_ref
  13.3 4.5 %collective-permute-start.1 = (bf16[784,128]{1,0:T(8,128)(2,1)S(1)}, bf16[784,128]{1,0:T(8,128)(2,1)S(1)}, u32[]{:S(2)}, u32[]{:S(2)}) collective-permute-start(bf16[784,128]{1,0:T(8,128)(2,1)S(1)} %concatenate.7), channel_id=1, source_target_pairs={{0,16},{8,24},{1,17},{9,25},{2,18},{10,26},{3,19},{11,27},{4,20},{... | collective-permute-start | bytes 602120 | tf_op jit(solution)/shard_map/ppermute | solution.py:30
  17.8 3.9 %collective-permute-done.1 = bf16[784,128]{1,0:T(8,128)(2,1)S(1)} collective-permute-done((bf16[784,128]{1,0:T(8,128)(2,1)S(1)}, bf16[784,128]{1,0:T(8,128)(2,1)S(1)}, u32[]{:S(2)}, u32[]{:S(2)}) %collective-permute-start.1) | collective-permute-done | bytes 200736 | tf_op jit(solution)/shard_map/ppermute | solution.py:30
  22.7 1.0 shard_map.112
  23.8 1.6 collective-permute-start.10
  25.3 4.4 %collective-permute-start.2 = (bf16[272,768]{1,0:T(8,128)(2,1)S(1)}, bf16[272,768]{1,0:T(8,128)(2,1)S(1)}, u32[]{:S(2)}, u32[]{:S(2)}) collective-permute-start(bf16[272,768]{1,0:T(8,128)(2,1)S(1)} %shard_map.111.refs_0_), channel_id=1, source_target_pairs={{0,8},{8,0},{16,24},{24,16},{1,9},{9,1},{17,25},{25,17},{2,10},{10... | collective-permute-start | bytes 1253384 | tf_op jit(solution)/shard_map/ppermute | solution.py:435
  30.5 1.2 collective-permute-done.10
  32.6 1.5 collective-permute-start.11
  34.1 3.9 %collective-permute-done.2.refs_0_ = bf16[272,768]{1,0:T(8,128)(2,1)S(1)} collective-permute-done((bf16[272,768]{1,0:T(8,128)(2,1)S(1)}, bf16[272,768]{1,0:T(8,128)(2,1)S(1)}, u32[]{:S(2)}, u32[]{:S(2)}) %collective-permute-start.2) | collective-permute-done | bytes 417824 | tf_op jit(solution)/shard_map/ppermute | solution.py:435
  38.0 1.0 shard_map.115
  39.1 1.6 collective-permute-start.9
  40.6 1.3 collective-permute-start.7
  42.6 4.3 %collective-permute-done.9 = bf16[768,256]{1,0:T(8,128)(2,1)S(1)} collective-permute-done((bf16[768,256]{1,0:T(8,128)(2,1)S(1)}, bf16[768,256]{1,0:T(8,128)(2,1)S(1)}, u32[]{:S(2)}, u32[]{:S(2)}) %collective-permute-start.9) | collective-permute-done | bytes 393248 | tf_op jit(solution)/shard_map/ppermute | solution.py:435
  47.0 5.3 %collective-permute-done.7.refs_1_ = bf16[272,768]{1,0:T(8,128)(2,1)S(1)} collective-permute-done((bf16[272,768]{1,0:T(8,128)(2,1)S(1)}, bf16[272,768]{1,0:T(8,128)(2,1)S(1)}, u32[]{:S(2)}, u32[]{:S(2)}) %collective-permute-start.7) | collective-permute-done | bytes 417824 | tf_op jit(solution)/shard_map/ppermute | solution.py:536
  52.4 1.0 shard_map.114
  53.4 2.5 %collective-permute-start.8 = (bf16[768,256]{1,0:T(8,128)(2,1)S(1)}, bf16[768,256]{1,0:T(8,128)(2,1)S(1)}, u32[]{:S(2)}, u32[]{:S(2)}) collective-permute-start(bf16[768,256]{1,0:T(8,128)(2,1)S(1)} %get-tuple-element.76), channel_id=1, source_target_pairs={{0,2},{1,5},{2,0},{3,7},{4,6},{5,1},{6,4},{7,3},{8,10},{9,13},{10,... | collective-permute-start | bytes 1179656 | tf_op jit(solution)/shard_map/ppermute | solution.py:435
  55.9 1.5 collective-permute-start.4
  57.5 8.5 %collective-permute-done.8 = bf16[768,256]{1,0:T(8,128)(2,1)S(1)} collective-permute-done((bf16[768,256]{1,0:T(8,128)(2,1)S(1)}, bf16[768,256]{1,0:T(8,128)(2,1)S(1)}, u32[]{:S(2)}, u32[]{:S(2)}) %collective-permute-start.8) | collective-permute-done | bytes 393248 | tf_op jit(solution)/shard_map/ppermute | solution.py:435
  66.0 3.7 %collective-permute-done.4.refs_1_ = bf16[272,768]{1,0:T(8,128)(2,1)S(1)} collective-permute-done((bf16[272,768]{1,0:T(8,128)(2,1)S(1)}, bf16[272,768]{1,0:T(8,128)(2,1)S(1)}, u32[]{:S(2)}, u32[]{:S(2)}) %collective-permute-start.4) | collective-permute-done | bytes 417824 | tf_op jit(solution)/shard_map/ppermute | solution.py:536
  71.0 1.0 copy-done.13
  72.0 1.0 copy-done.15
  73.0 1.0 shard_map.113
  75.9 1.1 copy-done.11
  77.8 8.9 %shard_map.116 = (f32[2,576,256]{2,1,0:T(8,128)S(1)}, f32[2,576,256]{2,1,0:T(8,128)S(1)}, f32[2,2,256]{2,1,0:T(2,128)S(1)}) custom-call(s32[4]{0:T(128)S(1)} %get-tuple-element.142.plan_ref, bf16[2,768,256]{2,1,0:T(8,128)(2,1)S(1)} %pad_maximum_fusion.1.refs_0_, bf16[2,768,256]{2,1,0:T(8,128)(2,1)} %collective-permute-done.13.refs_1_, ...), custom_call_target="tpu_custom_call" | custom-call | flops 3623878656 | bytes 14155776 | tf_op jit(solution)/shard_map/pallas_call | solution.py:347
  86.7 1.0 copy-done.8
  89.2 1.7 collective-permute-start.15
  92.0 9.7 %shard_map.117.hidden_ref = bf16[2,256,576]{2,1,0:T(8,128)(2,1)S(1)} custom-call(s32[4]{0:T(128)S(1)} %add_add_fusion.plan_ref, bf16[2,768,256]{2,1,0:T(8,128)(2,1)} %collective-permute-done.16.refs_0_, bf16[2,768,256]{2,1,0:T(8,128)(2,1)} %collective-permute-done.17.refs_1_, bf16[2,768,256]{2,1,0:T(8,128)(2,1)S(1)} %collective-permute-done.12.refs_2_, ...), custom_call_target="tpu_custom_call" | custom-call | flops 3623878656 | bytes 14155776 | tf_op jit(solution)/shard_map/pallas_call | solution.py:347
  101.7 7.2 %shard_map.118 = (bf16[4,256,768]{2,1,0:T(8,128)(2,1)S(1)}, bf16[4,256,768]{2,1,0:T(8,128)(2,1)S(1)}) custom-call(s32[4]{0:T(128)S(1)} %get-tuple-element.143.plan_ref, bf16[2,256,576]{2,1,0:T(8,128)(2,1)S(1)} %shard_map.117.hidden_ref, bf16[2,576,6144]{2,1,0:T(8,128)(2,1)} %down_ref.5), custom_call_target="tpu_custom_call" | custom-call | flops 1811939328 | bytes 7077888 | tf_op jit(solution)/shard_map/pallas_call | solution.py:406
  110.1 7.2 %shard_map.119 = (bf16[4,256,768]{2,1,0:T(8,128)(2,1)S(1)}, bf16[4,256,768]{2,1,0:T(8,128)(2,1)S(1)}) custom-call(s32[4]{0:T(128)S(1)} %pad_add_fusion.3.plan_ref, bf16[2,256,576]{2,1,0:T(8,128)(2,1)S(1)} %shard_map.117.hidden_ref, bf16[2,576,6144]{2,1,0:T(8,128)(2,1)} %down_ref.5), custom_call_target="tpu_custom_call" | custom-call | flops 1811939328 | bytes 7077888 | tf_op jit(solution)/shard_map/pallas_call | solution.py:406
  117.5 1.8 collective-permute-start.24
  119.8 8.9 %shard_map.120 = (f32[2,576,256]{2,1,0:T(8,128)S(1)}, f32[2,576,256]{2,1,0:T(8,128)S(1)}, f32[2,2,256]{2,1,0:T(2,128)S(1)}) custom-call(s32[4]{0:T(128)S(1)} %get-tuple-element.142.plan_ref, bf16[2,768,256]{2,1,0:T(8,128)(2,1)} %pad_maximum_fusion.refs_0_, bf16[2,768,256]{2,1,0:T(8,128)(2,1)S(1)} %collective-permute-done.22.refs_1_, ...), custom_call_target="tpu_custom_call" | custom-call | flops 3623878656 | bytes 14155776 | tf_op jit(solution)/shard_map/pallas_call | solution.py:347
  128.7 1.1 add_convert_fusion.2
  130.0 1.5 collective-permute-start.27
  131.5 1.7 collective-permute-start.26
  133.2 9.3 %shard_map.121.hidden_ref = bf16[2,256,576]{2,1,0:T(8,128)(2,1)S(1)} custom-call(s32[4]{0:T(128)S(1)} %add_add_fusion.plan_ref, bf16[2,768,256]{2,1,0:T(8,128)(2,1)} %collective-permute-done.15.refs_0_, bf16[2,768,256]{2,1,0:T(8,128)(2,1)S(1)} %collective-permute-done.20.refs_1_, bf16[2,768,256]{2,1,0:T(8,128)(2,1)} %collective-permute-done.11.refs_2_, ...), custom_call_target="tpu_custom_call" | custom-call | flops 3623878656 | bytes 14155776 | tf_op jit(solution)/shard_map/pallas_call | solution.py:347
  142.6 1.0 collective-permute-done.26
  144.0 1.4 collective-permute-start.28
  145.5 1.0 collective-permute-done.27.refs_2_
  146.6 1.1 copy-done.3
  147.7 12.7 %shard_map.123 = (bf16[4,256,768]{2,1,0:T(8,128)(2,1)S(1)}, bf16[4,256,768]{2,1,0:T(8,128)(2,1)S(1)}, bf16[4,256,768]{2,1,0:T(8,128)(2,1)S(1)}, bf16[4,256,768]{2,1,0:T(8,128)(2,1)S(1)}) custom-call(s32[8]{0:T(128)S(1)} %concatenate.8.plan_ref, bf16[2,256,576]{2,1,0:T(8,128)(2,1)S(1)} %copy-done.3, bf16[2,576,6144]{2,1,0:T(8,128)(2,1)} %down_ref.5), custom_call_target="tpu_custom_call" | custom-call | flops 3623878656 | bytes 14155776 | tf_op jit(solution)/shard_map/pallas_call | solution.py:406
  161.0 2.9 %collective-permute-done.30.refs_1_ = bf16[4,256,768]{2,1,0:T(8,128)(2,1)S(1)} collective-permute-done((bf16[4,256,768]{2,1,0:T(8,128)(2,1)S(1)}, bf16[4,256,768]{2,1,0:T(8,128)(2,1)S(1)}, u32[]{:S(2)}, u32[]{:S(2)}) %collective-permute-start.30) | collective-permute-done | bytes 1572896 | tf_op jit(solution)/shard_map/ppermute | solution.py:435
  164.1 1.1 collective-permute-start.31
  165.1 5.7 %collective-permute-start.33 = (bf16[256,768]{1,0:T(8,128)(2,1)S(1)}, bf16[256,768]{1,0:T(8,128)(2,1)S(1)}, u32[]{:S(2)}, u32[]{:S(2)}) collective-permute-start(bf16[256,768]{1,0:T(8,128)(2,1)S(1)} %shard_map.122), channel_id=1, source_target_pairs={{0,16},{24,8},{1,17},{25,9},{2,18},{26,10},{3,19},{27,11},{4,20},{... | collective-permute-start | bytes 1179656 | tf_op jit(solution)/shard_map/ppermute | solution.py:613
  170.9 1.1 fusion.1
  172.0 1.3 collective-permute-start.34
  173.5 4.6 %collective-permute-done.31.refs_2_ = bf16[2,256,768]{2,1,0:T(8,128)(2,1)S(1)} collective-permute-done((bf16[2,256,768]{2,1,0:T(8,128)(2,1)S(1)}, bf16[2,256,768]{2,1,0:T(8,128)(2,1)S(1)}, u32[]{:S(2)}, u32[]{:S(2)}) %collective-permute-start.31) | collective-permute-done | bytes 786464 | tf_op jit(solution)/shard_map/ppermute | solution.py:435
  178.9 2.7 %collective-permute-done.34 = bf16[256,768]{1,0:T(8,128)(2,1)S(1)} collective-permute-done((bf16[256,768]{1,0:T(8,128)(2,1)S(1)}, bf16[256,768]{1,0:T(8,128)(2,1)S(1)}, u32[]{:S(2)}, u32[]{:S(2)}) %collective-permute-start.34) | collective-permute-done | bytes 393248 | tf_op jit(solution)/shard_map/ppermute | solution.py:435
  181.8 1.7 collective-permute-start.35
  183.5 1.4 shard_map.126
  185.0 3.2 %collective-permute-start.37 = (bf16[256,768]{1,0:T(8,128)(2,1)S(1)}, bf16[256,768]{1,0:T(8,128)(2,1)S(1)}, u32[]{:S(2)}, u32[]{:S(2)}) collective-permute-start(bf16[256,768]{1,0:T(8,128)(2,1)S(1)} %shard_map.126), channel_id=1, source_target_pairs={{0,8},{8,0},{16,24},{24,16},{1,9},{9,1},{17,25},{25,17},{2,10},{10... | collective-permute-start | bytes 1179656 | tf_op jit(solution)/shard_map/ppermute | solution.py:435
  188.1 4.3 %collective-permute-done.35 = bf16[256,768]{1,0:T(8,128)(2,1)S(1)} collective-permute-done((bf16[256,768]{1,0:T(8,128)(2,1)S(1)}, bf16[256,768]{1,0:T(8,128)(2,1)S(1)}, u32[]{:S(2)}, u32[]{:S(2)}) %collective-permute-start.35) | collective-permute-done | bytes 393248 | tf_op jit(solution)/shard_map/ppermute | solution.py:435
  192.9 1.3 collective-permute-done.32.refs_2_
  195.1 1.0 collective-permute-done.37
  196.1 3.3 %collective-permute-start.39 = (bf16[256,768]{1,0:T(8,128)(2,1)S(1)}, bf16[256,768]{1,0:T(8,128)(2,1)S(1)}, u32[]{:S(2)}, u32[]{:S(2)}) collective-permute-start(bf16[256,768]{1,0:T(8,128)(2,1)S(1)} %shard_map.124), channel_id=1, source_target_pairs={{0,24},{24,0},{1,25},{25,1},{2,26},{26,2},{3,27},{27,3},{4,28},{28... | collective-permute-start | bytes 1179656 | tf_op jit(solution)/shard_map/ppermute | solution.py:627
  199.5 1.3 collective-permute-start.38
  200.8 1.5 collective-permute-done.36
  202.7 6.3 %collective-permute-done.39 = bf16[256,768]{1,0:T(8,128)(2,1)S(1)} collective-permute-done((bf16[256,768]{1,0:T(8,128)(2,1)S(1)}, bf16[256,768]{1,0:T(8,128)(2,1)S(1)}, u32[]{:S(2)}, u32[]{:S(2)}) %collective-permute-start.39) | collective-permute-done | bytes 393248 | tf_op jit(solution)/shard_map/ppermute | solution.py:627
  209.0 8.3 %collective-permute-done.38 = bf16[256,768]{1,0:T(8,128)(2,1)S(1)} collective-permute-done((bf16[256,768]{1,0:T(8,128)(2,1)S(1)}, bf16[256,768]{1,0:T(8,128)(2,1)S(1)}, u32[]{:S(2)}, u32[]{:S(2)}) %collective-permute-start.38) | collective-permute-done | bytes 393248 | tf_op jit(solution)/shard_map/ppermute | solution.py:626
  217.4 2.1 add_convert_fusion.8
  (123 shorter events, 18.0 us)
Async XLA Ops:
  2.2 10.8 %collective-permute-start = (bf16[784,128]{1,0:T(8,128)(2,1)S(1)}, bf16[784,128]{1,0:T(8,128)(2,1)S(1)}, u32[]{:S(2)}, u32[]{:S(2)}) collective-permute-start(bf16[784,128]{1,0:T(8,128)(2,1)S(1)} %get-tuple-element.73), channel_id=1, source_target_pairs={{0,8},{8,16},{16,24},{1,9},{9,17},{17,25},{2,10},{10,18},{18,26},{... | collective-permute-start | bytes 602120 | tf_op jit(solution)/shard_map/ppermute | solution.py:30
  7.9 1.0 copy-start.4
  8.9 1.0 copy-start.6
  9.9 1.0 copy-start.7
  13.0 8.9 %copy-start.5 = (bf16[256,768]{1,0:T(8,128)(2,1)S(1)}, bf16[256,768]{1,0:T(8,128)(2,1)}, u32[]{:S(2)}) copy-start(bf16[256,768]{1,0:T(8,128)(2,1)} %query_ref.3) | copy-start | bytes 1179652
  13.0 8.9 %copy-start.19 = (bf16[256,768]{1,0:T(8,128)(2,1)S(1)}, bf16[256,768]{1,0:T(8,128)(2,1)}, u32[]{:S(2)}) copy-start(bf16[256,768]{1,0:T(8,128)(2,1)} %residual_ref.1) | copy-start | bytes 1179652
  13.0 8.9 %copy-start.29 = (s32[256,2]{0,1:T(2,128)S(1)}, s32[256,2]{0,1:T(2,128)}, u32[]{:S(2)}) copy-start(s32[256,2]{0,1:T(2,128)} %param.17) | copy-start | bytes 6148
  13.3 8.5 %collective-permute-start.1 = (bf16[784,128]{1,0:T(8,128)(2,1)S(1)}, bf16[784,128]{1,0:T(8,128)(2,1)S(1)}, u32[]{:S(2)}, u32[]{:S(2)}) collective-permute-start(bf16[784,128]{1,0:T(8,128)(2,1)S(1)} %concatenate.7), channel_id=1, source_target_pairs={{0,16},{8,24},{1,17},{9,25},{2,18},{10,26},{3,19},{11,27},{4,20},{... | collective-permute-start | bytes 602120 | tf_op jit(solution)/shard_map/ppermute | solution.py:30
  22.7 24.3 %copy-start = (bf16[272,768]{1,0:T(8,128)(2,1)}, bf16[272,768]{1,0:T(8,128)(2,1)S(1)}, u32[]{:S(2)}) copy-start(bf16[272,768]{1,0:T(8,128)(2,1)S(1)} %shard_map.111.refs_0_) | copy-start | bytes 1253380
  23.8 10.3 %copy-start.20 = (bf16[256,256]{1,0:T(8,128)(2,1)}, bf16[256,256]{1,0:T(8,128)(2,1)S(1)}, u32[]{:S(2)}) copy-start(bf16[256,256]{1,0:T(8,128)(2,1)S(1)} %get-tuple-element.74.place_ref) | copy-start | bytes 393220
  23.8 7.8 %collective-permute-start.10 = (bf16[768,256]{1,0:T(8,128)(2,1)S(1)}, bf16[768,256]{1,0:T(8,128)(2,1)S(1)}, u32[]{:S(2)}, u32[]{:S(2)}) collective-permute-start(bf16[768,256]{1,0:T(8,128)(2,1)S(1)} %get-tuple-element.78), channel_id=1, source_target_pairs={{0,2},{1,5},{2,0},{3,7},{4,6},{5,1},{6,4},{7,3},{8,10},{9,13},{10,... | collective-permute-start | bytes 1179656 | tf_op jit(solution)/shard_map/ppermute | solution.py:435
  25.3 12.7 %collective-permute-start.2 = (bf16[272,768]{1,0:T(8,128)(2,1)S(1)}, bf16[272,768]{1,0:T(8,128)(2,1)S(1)}, u32[]{:S(2)}, u32[]{:S(2)}) collective-permute-start(bf16[272,768]{1,0:T(8,128)(2,1)S(1)} %shard_map.111.refs_0_), channel_id=1, source_target_pairs={{0,8},{8,0},{16,24},{24,16},{1,9},{9,1},{17,25},{25,17},{2,10},{10... | collective-permute-start | bytes 1253384 | tf_op jit(solution)/shard_map/ppermute | solution.py:435
  29.8 10.8 %collective-permute-start.6 = (bf16[272,768]{1,0:T(8,128)(2,1)S(1)}, bf16[272,768]{1,0:T(8,128)(2,1)S(1)}, u32[]{:S(2)}, u32[]{:S(2)}) collective-permute-start(bf16[272,768]{1,0:T(8,128)(2,1)S(1)} %shard_map.111.refs_0_), channel_id=1, source_target_pairs={{8,16},{16,8},{9,17},{17,9},{10,18},{18,10},{11,19},{19,11},{12,20... | collective-permute-start | bytes 1253384 | tf_op jit(solution)/shard_map/ppermute | solution.py:533
  32.6 19.7 %collective-permute-start.11 = (bf16[2,768,256]{2,1,0:T(8,128)(2,1)}, bf16[2,768,256]{2,1,0:T(8,128)(2,1)}, u32[]{:S(2)}, u32[]{:S(2)}) collective-permute-start(bf16[2,768,256]{2,1,0:T(8,128)(2,1)} %pad_maximum_fusion.3.refs_2_), channel_id=1, source_target_pairs={{0,4},{1,3},{2,6},{3,1},{4,0},{5,7},{6,2},{7,5},{8,12},{9,11},{10,... | collective-permute-start | bytes 2359304 | tf_op jit(solution)/shard_map/ppermute | solution.py:435
  39.1 27.0 %copy-start.22 = (bf16[256,256]{1,0:T(8,128)(2,1)}, bf16[256,256]{1,0:T(8,128)(2,1)S(1)}, u32[]{:S(2)}) copy-start(bf16[256,256]{1,0:T(8,128)(2,1)S(1)} %get-tuple-element.137.place_ref) | copy-start | bytes 393220
  39.1 7.8 %collective-permute-start.9 = (bf16[768,256]{1,0:T(8,128)(2,1)S(1)}, bf16[768,256]{1,0:T(8,128)(2,1)S(1)}, u32[]{:S(2)}, u32[]{:S(2)}) collective-permute-start(bf16[768,256]{1,0:T(8,128)(2,1)S(1)} %get-tuple-element.77), channel_id=1, source_target_pairs={{0,2},{1,5},{2,0},{3,7},{4,6},{5,1},{6,4},{7,3},{8,10},{9,13},{10,... | collective-permute-start | bytes 1179656 | tf_op jit(solution)/shard_map/ppermute | solution.py:435
  40.6 11.6 %collective-permute-start.7 = (bf16[272,768]{1,0:T(8,128)(2,1)S(1)}, bf16[272,768]{1,0:T(8,128)(2,1)S(1)}, u32[]{:S(2)}, u32[]{:S(2)}) collective-permute-start(bf16[272,768]{1,0:T(8,128)(2,1)S(1)} %collective-permute-done.6.refs_0_), channel_id=1, source_target_pairs={{8,0},{16,24},{9,1},{17,25},{10,2},{18,26},{11,3},{19,27},{12,4},{... | collective-permute-start | bytes 1253384 | tf_op jit(solution)/shard_map/ppermute | solution.py:536
  41.9 10.4 %collective-permute-start.3 = (bf16[272,768]{1,0:T(8,128)(2,1)S(1)}, bf16[272,768]{1,0:T(8,128)(2,1)S(1)}, u32[]{:S(2)}, u32[]{:S(2)}) collective-permute-start(bf16[272,768]{1,0:T(8,128)(2,1)S(1)} %collective-permute-done.2.refs_0_), channel_id=1, source_target_pairs={{8,16},{16,8},{9,17},{17,9},{10,18},{18,10},{11,19},{19,11},{12,20... | collective-permute-start | bytes 1253384 | tf_op jit(solution)/shard_map/ppermute | solution.py:533
  52.3 18.2 %copy-start.12 = (bf16[272,768]{1,0:T(8,128)(2,1)}, bf16[272,768]{1,0:T(8,128)(2,1)S(1)}, u32[]{:S(2)}) copy-start(bf16[272,768]{1,0:T(8,128)(2,1)S(1)} %collective-permute-done.3.refs_0_) | copy-start | bytes 1253380
  52.3 18.2 %collective-permute-start.12 = (bf16[2,768,256]{2,1,0:T(8,128)(2,1)S(1)}, bf16[2,768,256]{2,1,0:T(8,128)(2,1)S(1)}, u32[]{:S(2)}, u32[]{:S(2)}) collective-permute-start(bf16[2,768,256]{2,1,0:T(8,128)(2,1)S(1)} %pad_maximum_fusion.2.refs_2_), channel_id=1, source_target_pairs={{0,4},{1,3},{2,6},{3,1},{4,0},{5,7},{6,2},{7,5},{8,12},{9,11},{10,... | collective-permute-start | bytes 2359304 | tf_op jit(solution)/shard_map/ppermute | solution.py:435
  53.4 17.1 %copy-start.26 = (bf16[256,256]{1,0:T(8,128)(2,1)}, bf16[256,256]{1,0:T(8,128)(2,1)S(1)}, u32[]{:S(2)}) copy-start(bf16[256,256]{1,0:T(8,128)(2,1)S(1)} %get-tuple-element.122.place_ref) | copy-start | bytes 393220
  53.4 12.5 %collective-permute-start.8 = (bf16[768,256]{1,0:T(8,128)(2,1)S(1)}, bf16[768,256]{1,0:T(8,128)(2,1)S(1)}, u32[]{:S(2)}, u32[]{:S(2)}) collective-permute-start(bf16[768,256]{1,0:T(8,128)(2,1)S(1)} %get-tuple-element.76), channel_id=1, source_target_pairs={{0,2},{1,5},{2,0},{3,7},{4,6},{5,1},{6,4},{7,3},{8,10},{9,13},{10,... | collective-permute-start | bytes 1179656 | tf_op jit(solution)/shard_map/ppermute | solution.py:435
  55.9 13.8 %collective-permute-start.4 = (bf16[272,768]{1,0:T(8,128)(2,1)S(1)}, bf16[272,768]{1,0:T(8,128)(2,1)S(1)}, u32[]{:S(2)}, u32[]{:S(2)}) collective-permute-start(bf16[272,768]{1,0:T(8,128)(2,1)S(1)} %collective-permute-done.3.refs_0_), channel_id=1, source_target_pairs={{8,0},{16,24},{9,1},{17,25},{10,2},{18,26},{11,3},{19,27},{12,4},{... | collective-permute-start | bytes 1253384 | tf_op jit(solution)/shard_map/ppermute | solution.py:536
  57.4 17.6 %collective-permute-start.14 = (bf16[2,768,256]{2,1,0:T(8,128)(2,1)S(1)}, bf16[2,768,256]{2,1,0:T(8,128)(2,1)S(1)}, u32[]{:S(2)}, u32[]{:S(2)}) collective-permute-start(bf16[2,768,256]{2,1,0:T(8,128)(2,1)S(1)} %pad_maximum_fusion.2.refs_2_), channel_id=1, source_target_pairs={{0,1},{1,0},{2,3},{3,2},{4,5},{5,4},{6,7},{7,6},{8,9},{9,8},{10,11... | collective-permute-start | bytes 2359304 | tf_op jit(solution)/shard_map/ppermute | solution.py:435
  70.5 5.4 %collective-permute-start.13 = (bf16[2,768,256]{2,1,0:T(8,128)(2,1)S(1)}, bf16[2,768,256]{2,1,0:T(8,128)(2,1)}, u32[]{:S(2)}, u32[]{:S(2)}) collective-permute-start(bf16[2,768,256]{2,1,0:T(8,128)(2,1)S(1)} %pad_maximum_fusion.1.refs_0_), channel_id=1, source_target_pairs={{0,1},{1,0},{2,3},{3,2},{4,5},{5,4},{6,7},{7,6},{8,9},{9,8},{10,11... | collective-permute-start | bytes 2359304 | tf_op jit(solution)/shard_map/ppermute | solution.py:435
  70.5 17.2 %collective-permute-start.16 = (bf16[2,768,256]{2,1,0:T(8,128)(2,1)S(1)}, bf16[2,768,256]{2,1,0:T(8,128)(2,1)}, u32[]{:S(2)}, u32[]{:S(2)}) collective-permute-start(bf16[2,768,256]{2,1,0:T(8,128)(2,1)S(1)} %pad_maximum_fusion.1.refs_0_), channel_id=1, source_target_pairs={{0,4},{1,3},{2,6},{3,1},{4,0},{5,7},{6,2},{7,5},{8,12},{9,11},{10,... | collective-permute-start | bytes 2359304 | tf_op jit(solution)/shard_map/ppermute | solution.py:435
  71.0 1.0 copy-start.13
  72.0 1.0 copy-start.15
  74.7 13.5 %collective-permute-start.5 = (bf16[768,256]{1,0:T(8,128)(2,1)S(1)}, bf16[768,256]{1,0:T(8,128)(2,1)S(1)}, u32[]{:S(2)}, u32[]{:S(2)}) collective-permute-start(bf16[768,256]{1,0:T(8,128)(2,1)S(1)} %get-tuple-element.75), channel_id=1, source_target_pairs={{0,2},{1,5},{2,0},{3,7},{4,6},{5,1},{6,4},{7,3},{8,10},{9,13},{10,... | collective-permute-start | bytes 1179656 | tf_op jit(solution)/shard_map/ppermute | solution.py:435
  75.9 1.1 copy-start.11
  86.7 1.0 copy-start.8
  87.7 3.5 %copy-start.9 = (f32[2,576,256]{2,1,0:T(8,128)S(1)}, f32[2,576,256]{2,1,0:T(8,128)}, u32[]{:S(2)}) copy-start(f32[2,576,256]{2,1,0:T(8,128)} %copy-done.8) | copy-start | bytes 3538948
  87.7 3.3 %collective-permute-start.17 = (bf16[2,768,256]{2,1,0:T(8,128)(2,1)}, bf16[2,768,256]{2,1,0:T(8,128)(2,1)}, u32[]{:S(2)}, u32[]{:S(2)}) collective-permute-start(bf16[2,768,256]{2,1,0:T(8,128)(2,1)} %collective-permute-done.16.refs_0_), channel_id=1, source_target_pairs={{0,1},{1,0},{2,3},{3,2},{4,5},{5,4},{6,7},{7,6},{8,9},{9,8},{10,11... | collective-permute-start | bytes 2359304 | tf_op jit(solution)/shard_map/ppermute | solution.py:435
  87.7 3.5 %collective-permute-start.18 = (bf16[2,768,256]{2,1,0:T(8,128)(2,1)S(1)}, bf16[2,768,256]{2,1,0:T(8,128)(2,1)}, u32[]{:S(2)}, u32[]{:S(2)}) collective-permute-start(bf16[2,768,256]{2,1,0:T(8,128)(2,1)S(1)} %collective-permute-done.12.refs_2_), channel_id=1, source_target_pairs={{0,1},{1,0},{2,3},{3,2},{4,5},{5,4},{6,7},{7,6},{8,9},{9,8},{10,11... | collective-permute-start | bytes 2359304 | tf_op jit(solution)/shard_map/ppermute | solution.py:435
  89.2 12.5 %collective-permute-start.15 = (bf16[2,768,256]{2,1,0:T(8,128)(2,1)}, bf16[2,768,256]{2,1,0:T(8,128)(2,1)}, u32[]{:S(2)}, u32[]{:S(2)}) collective-permute-start(bf16[2,768,256]{2,1,0:T(8,128)(2,1)} %pad_maximum_fusion.refs_0_), channel_id=1, source_target_pairs={{0,4},{1,3},{2,6},{3,1},{4,0},{5,7},{6,2},{7,5},{8,12},{9,11},{10,... | collective-permute-start | bytes 2359304 | tf_op jit(solution)/shard_map/ppermute | solution.py:435
  108.9 8.4 %collective-permute-start.19 = (bf16[4,256,768]{2,1,0:T(8,128)(2,1)S(1)}, bf16[4,256,768]{2,1,0:T(8,128)(2,1)S(1)}, u32[]{:S(2)}, u32[]{:S(2)}) collective-permute-start(bf16[4,256,768]{2,1,0:T(8,128)(2,1)S(1)} %get-tuple-element.100), channel_id=1, source_target_pairs={{0,1},{1,0},{2,3},{3,2},{4,5},{5,4},{6,7},{7,6},{8,9},{9,8},{10,11... | collective-permute-start | bytes 4718600 | tf_op jit(solution)/shard_map/ppermute | solution.py:435
  109.1 19.6 %collective-permute-start.25 = (bf16[4,256,768]{2,1,0:T(8,128)(2,1)S(1)}, bf16[4,256,768]{2,1,0:T(8,128)(2,1)S(1)}, u32[]{:S(2)}, u32[]{:S(2)}) collective-permute-start(bf16[4,256,768]{2,1,0:T(8,128)(2,1)S(1)} %get-tuple-element.101), channel_id=1, source_target_pairs={{0,1},{1,0},{2,3},{3,2},{4,5},{5,4},{6,7},{7,6},{8,9},{9,8},{10,11... | collective-permute-start | bytes 4718600 | tf_op jit(solution)/shard_map/ppermute | solution.py:435
  109.5 9.8 %collective-permute-start.23 = (bf16[2,768,256]{2,1,0:T(8,128)(2,1)}, bf16[2,768,256]{2,1,0:T(8,128)(2,1)S(1)}, u32[]{:S(2)}, u32[]{:S(2)}) collective-permute-start(bf16[2,768,256]{2,1,0:T(8,128)(2,1)} %pad_maximum_fusion.3.refs_2_), channel_id=1, source_target_pairs={{0,1},{1,0},{2,3},{3,2},{4,5},{5,4},{6,7},{7,6},{8,9},{9,8},{10,11... | collective-permute-start | bytes 2359304 | tf_op jit(solution)/shard_map/ppermute | solution.py:435
  109.6 9.7 %collective-permute-start.22 = (bf16[2,768,256]{2,1,0:T(8,128)(2,1)}, bf16[2,768,256]{2,1,0:T(8,128)(2,1)S(1)}, u32[]{:S(2)}, u32[]{:S(2)}) collective-permute-start(bf16[2,768,256]{2,1,0:T(8,128)(2,1)} %pad_maximum_fusion.refs_0_), channel_id=1, source_target_pairs={{0,1},{1,0},{2,3},{3,2},{4,5},{5,4},{6,7},{7,6},{8,9},{9,8},{10,11... | collective-permute-start | bytes 2359304 | tf_op jit(solution)/shard_map/ppermute | solution.py:435
  117.3 2.5 %copy-start.18 = (bf16[6144,2]{0,1:T(2,128)(2,1)S(1)}, bf16[6144,2]{0,1:T(2,128)(2,1)}, u32[]{:S(2)}) copy-start(bf16[6144,2]{0,1:T(2,128)(2,1)} %param.18) | copy-start | bytes 73732
  117.5 12.3 %collective-permute-start.24 = (bf16[2,256,768]{2,1,0:T(8,128)(2,1)S(1)}, bf16[2,256,768]{2,1,0:T(8,128)(2,1)S(1)}, u32[]{:S(2)}, u32[]{:S(2)}) collective-permute-start(bf16[2,256,768]{2,1,0:T(8,128)(2,1)S(1)} %add_convert_fusion.3), channel_id=1, source_target_pairs={{0,4},{1,3},{2,6},{3,1},{4,0},{5,7},{6,2},{7,5},{8,12},{9,11},{10,... | collective-permute-start | bytes 2359304 | tf_op jit(solution)/shard_map/ppermute | solution.py:435
  119.3 14.0 %collective-permute-start.20 = (bf16[2,768,256]{2,1,0:T(8,128)(2,1)}, bf16[2,768,256]{2,1,0:T(8,128)(2,1)S(1)}, u32[]{:S(2)}, u32[]{:S(2)}) collective-permute-start(bf16[2,768,256]{2,1,0:T(8,128)(2,1)} %collective-permute-done.15.refs_0_), channel_id=1, source_target_pairs={{0,1},{1,0},{2,3},{3,2},{4,5},{5,4},{6,7},{7,6},{8,9},{9,8},{10,11... | collective-permute-start | bytes 2359304 | tf_op jit(solution)/shard_map/ppermute | solution.py:435
  119.3 13.9 %collective-permute-start.21 = (bf16[2,768,256]{2,1,0:T(8,128)(2,1)}, bf16[2,768,256]{2,1,0:T(8,128)(2,1)S(1)}, u32[]{:S(2)}, u32[]{:S(2)}) collective-permute-start(bf16[2,768,256]{2,1,0:T(8,128)(2,1)} %collective-permute-done.11.refs_2_), channel_id=1, source_target_pairs={{0,1},{1,0},{2,3},{3,2},{4,5},{5,4},{6,7},{7,6},{8,9},{9,8},{10,11... | collective-permute-start | bytes 2359304 | tf_op jit(solution)/shard_map/ppermute | solution.py:435
  130.0 13.6 %copy-start.27 = (bf16[256,256]{1,0:T(8,128)(2,1)S(1)}, bf16[256,256]{1,0:T(8,128)(2,1)}, u32[]{:S(2)}) copy-start(bf16[256,256]{1,0:T(8,128)(2,1)} %copy-done.26) | copy-start | bytes 393220
  130.0 16.6 %collective-permute-start.27 = (bf16[2,256,768]{2,1,0:T(8,128)(2,1)}, bf16[2,256,768]{2,1,0:T(8,128)(2,1)}, u32[]{:S(2)}, u32[]{:S(2)}) collective-permute-start(bf16[2,256,768]{2,1,0:T(8,128)(2,1)} %add_convert_fusion.2), channel_id=1, source_target_pairs={{0,4},{1,3},{2,6},{3,1},{4,0},{5,7},{6,2},{7,5},{8,12},{9,11},{10,... | collective-permute-start | bytes 2359304 | tf_op jit(solution)/shard_map/ppermute | solution.py:435
  131.5 12.1 %collective-permute-start.26 = (bf16[256,768]{1,0:T(8,128)(2,1)S(1)}, bf16[256,768]{1,0:T(8,128)(2,1)S(1)}, u32[]{:S(2)}, u32[]{:S(2)}) collective-permute-start(bf16[256,768]{1,0:T(8,128)(2,1)S(1)} %fusion), channel_id=1, source_target_pairs={{0,2},{1,5},{2,0},{3,7},{4,6},{5,1},{6,4},{7,3},{8,10},{9,13},{10,... | collective-permute-start | bytes 1179656 | tf_op jit(solution)/shard_map/ppermute | solution.py:435
  142.6 1.4 copy-start.2
  144.0 16.4 %collective-permute-start.28 = (bf16[256,768]{1,0:T(8,128)(2,1)S(1)}, bf16[256,768]{1,0:T(8,128)(2,1)}, u32[]{:S(2)}, u32[]{:S(2)}) collective-permute-start(bf16[256,768]{1,0:T(8,128)(2,1)S(1)} %shard_map.122), channel_id=1, source_target_pairs={{8,16},{16,8},{9,17},{17,9},{10,18},{18,10},{11,19},{19,11},{12,20... | collective-permute-start | bytes 1179656 | tf_op jit(solution)/shard_map/ppermute | solution.py:607
  146.6 1.1 copy-start.3
  160.4 3.5 %collective-permute-start.30 = (bf16[4,256,768]{2,1,0:T(8,128)(2,1)S(1)}, bf16[4,256,768]{2,1,0:T(8,128)(2,1)S(1)}, u32[]{:S(2)}, u32[]{:S(2)}) collective-permute-start(bf16[4,256,768]{2,1,0:T(8,128)(2,1)S(1)} %get-tuple-element.131), channel_id=1, source_target_pairs={{0,1},{1,0},{2,3},{3,2},{4,5},{5,4},{6,7},{7,6},{8,9},{9,8},{10,11... | collective-permute-start | bytes 4718600 | tf_op jit(solution)/shard_map/ppermute | solution.py:435
  160.5 12.8 %collective-permute-start.29 = (bf16[4,256,768]{2,1,0:T(8,128)(2,1)S(1)}, bf16[4,256,768]{2,1,0:T(8,128)(2,1)S(1)}, u32[]{:S(2)}, u32[]{:S(2)}) collective-permute-start(bf16[4,256,768]{2,1,0:T(8,128)(2,1)S(1)} %get-tuple-element.129), channel_id=1, source_target_pairs={{0,1},{1,0},{2,3},{3,2},{4,5},{5,4},{6,7},{7,6},{8,9},{9,8},{10,11... | collective-permute-start | bytes 4718600 | tf_op jit(solution)/shard_map/ppermute | solution.py:435
  164.1 14.0 %collective-permute-start.31 = (bf16[2,256,768]{2,1,0:T(8,128)(2,1)S(1)}, bf16[2,256,768]{2,1,0:T(8,128)(2,1)S(1)}, u32[]{:S(2)}, u32[]{:S(2)}) collective-permute-start(bf16[2,256,768]{2,1,0:T(8,128)(2,1)S(1)} %add_convert_fusion), channel_id=1, source_target_pairs={{0,4},{1,3},{2,6},{3,1},{4,0},{5,7},{6,2},{7,5},{8,12},{9,11},{10,... | collective-permute-start | bytes 2359304 | tf_op jit(solution)/shard_map/ppermute | solution.py:435
  165.1 13.8 %collective-permute-start.33 = (bf16[256,768]{1,0:T(8,128)(2,1)S(1)}, bf16[256,768]{1,0:T(8,128)(2,1)S(1)}, u32[]{:S(2)}, u32[]{:S(2)}) collective-permute-start(bf16[256,768]{1,0:T(8,128)(2,1)S(1)} %shard_map.122), channel_id=1, source_target_pairs={{0,16},{24,8},{1,17},{25,9},{2,18},{26,10},{3,19},{27,11},{4,20},{... | collective-permute-start | bytes 1179656 | tf_op jit(solution)/shard_map/ppermute | solution.py:613
  172.0 9.6 %collective-permute-start.34 = (bf16[256,768]{1,0:T(8,128)(2,1)S(1)}, bf16[256,768]{1,0:T(8,128)(2,1)S(1)}, u32[]{:S(2)}, u32[]{:S(2)}) collective-permute-start(bf16[256,768]{1,0:T(8,128)(2,1)S(1)} %fusion.1), channel_id=1, source_target_pairs={{0,2},{1,5},{2,0},{3,7},{4,6},{5,1},{6,4},{7,3},{8,10},{9,13},{10,... | collective-permute-start | bytes 1179656 | tf_op jit(solution)/shard_map/ppermute | solution.py:435
  173.3 10.2 %copy-start.23 = (bf16[256,256]{1,0:T(8,128)(2,1)S(1)}, bf16[256,256]{1,0:T(8,128)(2,1)}, u32[]{:S(2)}) copy-start(bf16[256,256]{1,0:T(8,128)(2,1)} %copy-done.22) | copy-start | bytes 393220
  178.0 16.2 %collective-permute-start.32 = (bf16[2,256,768]{2,1,0:T(8,128)(2,1)S(1)}, bf16[2,256,768]{2,1,0:T(8,128)(2,1)S(1)}, u32[]{:S(2)}, u32[]{:S(2)}) collective-permute-start(bf16[2,256,768]{2,1,0:T(8,128)(2,1)S(1)} %add_convert_fusion.1), channel_id=1, source_target_pairs={{0,4},{1,3},{2,6},{3,1},{4,0},{5,7},{6,2},{7,5},{8,12},{9,11},{10,... | collective-permute-start | bytes 2359304 | tf_op jit(solution)/shard_map/ppermute | solution.py:435
  181.8 10.7 %collective-permute-start.35 = (bf16[256,768]{1,0:T(8,128)(2,1)S(1)}, bf16[256,768]{1,0:T(8,128)(2,1)S(1)}, u32[]{:S(2)}, u32[]{:S(2)}) collective-permute-start(bf16[256,768]{1,0:T(8,128)(2,1)S(1)} %fusion.2), channel_id=1, source_target_pairs={{0,2},{1,5},{2,0},{3,7},{4,6},{5,1},{6,4},{7,3},{8,10},{9,13},{10,... | collective-permute-start | bytes 1179656 | tf_op jit(solution)/shard_map/ppermute | solution.py:435
  183.5 9.0 %copy-start.25 = (bf16[256,256]{1,0:T(8,128)(2,1)S(1)}, bf16[256,256]{1,0:T(8,128)(2,1)}, u32[]{:S(2)}) copy-start(bf16[256,256]{1,0:T(8,128)(2,1)} %copy-done.24) | copy-start | bytes 393220
  185.0 11.2 %collective-permute-start.37 = (bf16[256,768]{1,0:T(8,128)(2,1)S(1)}, bf16[256,768]{1,0:T(8,128)(2,1)S(1)}, u32[]{:S(2)}, u32[]{:S(2)}) collective-permute-start(bf16[256,768]{1,0:T(8,128)(2,1)S(1)} %shard_map.126), channel_id=1, source_target_pairs={{0,8},{8,0},{16,24},{24,16},{1,9},{9,1},{17,25},{25,17},{2,10},{10... | collective-permute-start | bytes 1179656 | tf_op jit(solution)/shard_map/ppermute | solution.py:435
  192.9 9.3 %copy-start.21 = (bf16[256,256]{1,0:T(8,128)(2,1)S(1)}, bf16[256,256]{1,0:T(8,128)(2,1)}, u32[]{:S(2)}) copy-start(bf16[256,256]{1,0:T(8,128)(2,1)} %copy-done.20) | copy-start | bytes 393220
  194.4 7.8 %collective-permute-start.36 = (bf16[256,768]{1,0:T(8,128)(2,1)S(1)}, bf16[256,768]{1,0:T(8,128)(2,1)S(1)}, u32[]{:S(2)}, u32[]{:S(2)}) collective-permute-start(bf16[256,768]{1,0:T(8,128)(2,1)S(1)} %fusion.3), channel_id=1, source_target_pairs={{0,2},{1,5},{2,0},{3,7},{4,6},{5,1},{6,4},{7,3},{8,10},{9,13},{10,... | collective-permute-start | bytes 1179656 | tf_op jit(solution)/shard_map/ppermute | solution.py:435
  196.1 12.9 %collective-permute-start.39 = (bf16[256,768]{1,0:T(8,128)(2,1)S(1)}, bf16[256,768]{1,0:T(8,128)(2,1)S(1)}, u32[]{:S(2)}, u32[]{:S(2)}) collective-permute-start(bf16[256,768]{1,0:T(8,128)(2,1)S(1)} %shard_map.124), channel_id=1, source_target_pairs={{0,24},{24,0},{1,25},{25,1},{2,26},{26,2},{3,27},{27,3},{4,28},{28... | collective-permute-start | bytes 1179656 | tf_op jit(solution)/shard_map/ppermute | solution.py:627
  199.5 17.9 %collective-permute-start.38 = (bf16[256,768]{1,0:T(8,128)(2,1)S(1)}, bf16[256,768]{1,0:T(8,128)(2,1)S(1)}, u32[]{:S(2)}, u32[]{:S(2)}) collective-permute-start(bf16[256,768]{1,0:T(8,128)(2,1)S(1)} %shard_map.124), channel_id=1, source_target_pairs={{8,24},{16,0},{9,25},{17,1},{10,26},{18,2},{11,27},{19,3},{12,28},... | collective-permute-start | bytes 1179656 | tf_op jit(solution)/shard_map/ppermute | solution.py:626
  202.3 15.1 %copy-start.1 = (bf16[272,768]{1,0:T(8,128)(2,1)S(1)}, bf16[272,768]{1,0:T(8,128)(2,1)}, u32[]{:S(2)}) copy-start(bf16[272,768]{1,0:T(8,128)(2,1)} %copy-done) | copy-start | bytes 1253380
  (6 other events, 4.5 us)

commit v15 on v14

--- a/solution.py
+++ b/solution.py
@@ -536,8 +536,9 @@
         return lax.ppermute(part, "seq", [(1, 0), (2, 3)])
 
     def gather(name, behind):
-        two[name], _ = tie((plane.first(chosen[name][0]), behind))
-        near[name] = plane.across(two[name])
+        pair = plane.first(chosen[name][0])
+        near[name] = plane.across(pair)
+        two[name], _ = tie((pair, behind))
         far_two[name] = plane.second(two[name])
 
     swap = swapped(stream, "seq", 1, 1)
@@ -610,7 +611,8 @@
     theirs, _ = tie((theirs, third_home))
     fourth, own = (Scatter(*shares) for shares in zip(chunk, theirs, mine))
     fourth.two_blocks([])
-    third_far_home = lax.ppermute(tie((third_piece, third_home))[0], "seq", [(0, 2), (3, 1)])
+    third_piece, _ = tie((third_piece, [third_home, neighbour.one]))
+    third_far_home = lax.ppermute(third_piece, "seq", [(0, 2), (3, 1)])
     neighbour_piece = neighbour.own_block([])
     neighbour_home = swapped(neighbour_piece, "seq", 1, 1)
     fourth.one_block([third_far_home, neighbour.got_one])

time: 221 us -> 225 us (1.018)
  starting transfers between devices: 55.8 us -> 63 us
  waiting for transfers between devices: 66.2 us -> 63.7 us
    ppermute x30, waiting for transfers between devices: 38.5 us -> 33 us  [swapped(): return lax.ppermute(array, axis, pairs)]
    ppermute x1, starting transfers between devices: 3.35 us -> 7.72 us  [paired_chunks(): lax.ppermute(fourth_piece, 'seq', [(0, 3), (3, 0)])]
    ppermute x2, waiting for transfers between devices: 8.98 us -> 11.5 us  [outward(): return lax.ppermute(part, 'seq', [(1, 0), (2, 3)])]
    ppermute x30, starting transfers between devices: 30.5 us -> 32.9 us  [swapped(): return lax.ppermute(array, axis, pairs)]
    unnamed x60 -> x64, local copies, waits for them, and re-layouts: 12.8 us -> 12.8 us
  transfers between devices with their start and end apart: 40 -> 40, of which waited for: 20 -> 14; matrix products, arithmetic and copies ran while one was open for 3% -> 3% of each run, Pallas kernels for 29% -> 28%
where the time goes in v15:
time: 225 us; the launch traced here: 224 us
  Pallas kernels  75 us (33%)
  waiting for transfers between devices  63.7 us (28%)
  starting transfers between devices  63 us (28%)
  local copies, waits for them, and re-layouts  13.8 us (6%)
  other arithmetic  7.94 us (4%)
    pallas_call x4, Pallas kernels, gate_part(): pl.pallas_call(functools.partial(gate_kernel, counts, len(xs), last), gri...  36.6 us
    ppermute x30, waiting for transfers between devices, swapped(): return lax.ppermute(array, axis, pairs)  33 us
    ppermute x30, starting transfers between devices, swapped(): return lax.ppermute(array, axis, pairs)  32.9 us
    pallas_call x3, Pallas kernels, down_part(): pl.pallas_call(functools.partial(down_kernel, blocks, sections), grid_spe...  27.1 us
    unnamed x64, local copies, waits for them, and re-layouts  12.8 us
    ppermute x2, waiting for transfers between devices, outward(): return lax.ppermute(part, 'seq', [(1, 0), (2, 3)])  11.5 us
    ppermute x2, starting transfers between devices, shifted(): return lax.ppermute(array, axis, pairs)  9.43 us
    ppermute x1, waiting for transfers between devices, paired_chunks(): lax.ppermute(fourth_piece, 'seq', [(1, 3), (2, 0)])  8.33 us
  transfers between devices with their start and end apart: 40, of which 14 were waited for; matrix products, arithmetic and copies ran while one was open for 3% of the time, Pallas kernels for 28%

profile of v15, /device:TPU:0, one launch (start us, length us, event | category | flops | bytes accessed | tf_op | source)
XLA Modules:
  0.0 224.1 jit_solution(14156279190370024577)
XLA Ops:
  0.0 2.1 shard_map.109
  2.2 4.9 %collective-permute-start = (bf16[784,128]{1,0:T(8,128)(2,1)S(1)}, bf16[784,128]{1,0:T(8,128)(2,1)S(1)}, u32[]{:S(2)}, u32[]{:S(2)}) collective-permute-start(bf16[784,128]{1,0:T(8,128)(2,1)S(1)} %get-tuple-element.73), channel_id=1, source_target_pairs={{0,8},{8,16},{16,24},{1,9},{9,17},{17,25},{2,10},{10,18},{18,26},{... | collective-permute-start | bytes 602120 | tf_op jit(solution)/shard_map/ppermute | solution.py:30
  7.9 1.0 copy-done.4
  8.9 1.0 copy-done.6
  9.9 1.0 copy-done.7
  11.6 1.4 shard_map.110.intra_ref
  13.3 4.5 %collective-permute-start.1 = (bf16[784,128]{1,0:T(8,128)(2,1)S(1)}, bf16[784,128]{1,0:T(8,128)(2,1)S(1)}, u32[]{:S(2)}, u32[]{:S(2)}) collective-permute-start(bf16[784,128]{1,0:T(8,128)(2,1)S(1)} %concatenate.7), channel_id=1, source_target_pairs={{0,16},{8,24},{1,17},{9,25},{2,18},{10,26},{3,19},{11,27},{4,20},{... | collective-permute-start | bytes 602120 | tf_op jit(solution)/shard_map/ppermute | solution.py:30
  17.8 3.9 %collective-permute-done.1 = bf16[784,128]{1,0:T(8,128)(2,1)S(1)} collective-permute-done((bf16[784,128]{1,0:T(8,128)(2,1)S(1)}, bf16[784,128]{1,0:T(8,128)(2,1)S(1)}, u32[]{:S(2)}, u32[]{:S(2)}) %collective-permute-start.1) | collective-permute-done | bytes 200736 | tf_op jit(solution)/shard_map/ppermute | solution.py:30
  21.9 0.8 shard_map.111.refs_0_
  22.7 1.0 shard_map.112
  23.8 1.6 collective-permute-start.10
  26.0 5.7 %collective-permute-start.2 = (bf16[272,768]{1,0:T(8,128)(2,1)S(1)}, bf16[272,768]{1,0:T(8,128)(2,1)S(1)}, u32[]{:S(2)}, u32[]{:S(2)}) collective-permute-start(bf16[272,768]{1,0:T(8,128)(2,1)S(1)} %shard_map.111.refs_0_), channel_id=1, source_target_pairs={{0,8},{8,0},{16,24},{24,16},{1,9},{9,1},{17,25},{25,17},{2,10},{10... | collective-permute-start | bytes 1253384 | tf_op jit(solution)/shard_map/ppermute | solution.py:435
  31.8 1.0 pad_maximum_fusion.3.refs_2_
  32.7 1.5 collective-permute-start.11
  34.3 1.3 collective-permute-start.7
  35.5 4.5 %collective-permute-done.2.refs_0_ = bf16[272,768]{1,0:T(8,128)(2,1)S(1)} collective-permute-done((bf16[272,768]{1,0:T(8,128)(2,1)S(1)}, bf16[272,768]{1,0:T(8,128)(2,1)S(1)}, u32[]{:S(2)}, u32[]{:S(2)}) %collective-permute-start.2) | collective-permute-done | bytes 417824 | tf_op jit(solution)/shard_map/ppermute | solution.py:435
  40.0 1.0 shard_map.115
  41.1 1.6 collective-permute-start.9
  43.3 6.9 %collective-permute-done.7.refs_1_ = bf16[272,768]{1,0:T(8,128)(2,1)S(1)} collective-permute-done((bf16[272,768]{1,0:T(8,128)(2,1)S(1)}, bf16[272,768]{1,0:T(8,128)(2,1)S(1)}, u32[]{:S(2)}, u32[]{:S(2)}) %collective-permute-start.7) | collective-permute-done | bytes 417824 | tf_op jit(solution)/shard_map/ppermute | solution.py:536
  50.2 1.0 shard_map.114
  51.3 2.5 %collective-permute-start.8 = (bf16[768,256]{1,0:T(8,128)(2,1)S(1)}, bf16[768,256]{1,0:T(8,128)(2,1)S(1)}, u32[]{:S(2)}, u32[]{:S(2)}) collective-permute-start(bf16[768,256]{1,0:T(8,128)(2,1)S(1)} %get-tuple-element.76), channel_id=1, source_target_pairs={{0,2},{1,5},{2,0},{3,7},{4,6},{5,1},{6,4},{7,3},{8,10},{9,13},{10,... | collective-permute-start | bytes 1179656 | tf_op jit(solution)/shard_map/ppermute | solution.py:435
  54.1 1.5 collective-permute-start.4
  55.6 8.3 %collective-permute-done.8 = bf16[768,256]{1,0:T(8,128)(2,1)S(1)} collective-permute-done((bf16[768,256]{1,0:T(8,128)(2,1)S(1)}, bf16[768,256]{1,0:T(8,128)(2,1)S(1)}, u32[]{:S(2)}, u32[]{:S(2)}) %collective-permute-start.8) | collective-permute-done | bytes 393248 | tf_op jit(solution)/shard_map/ppermute | solution.py:435
  64.0 4.5 %collective-permute-done.4.refs_1_ = bf16[272,768]{1,0:T(8,128)(2,1)S(1)} collective-permute-done((bf16[272,768]{1,0:T(8,128)(2,1)S(1)}, bf16[272,768]{1,0:T(8,128)(2,1)S(1)}, u32[]{:S(2)}, u32[]{:S(2)}) %collective-permute-start.4) | collective-permute-done | bytes 417824 | tf_op jit(solution)/shard_map/ppermute | solution.py:536
  69.3 1.5 collective-permute-start.16
  70.9 1.0 copy-done.15
  71.9 1.0 copy-done.17
  72.9 1.0 shard_map.113
  74.6 1.2 collective-permute-start.5
  75.8 0.9 copy-done.12
  76.7 1.1 copy-done.13
  78.6 8.9 %shard_map.116 = (f32[2,576,256]{2,1,0:T(8,128)S(1)}, f32[2,576,256]{2,1,0:T(8,128)S(1)}, f32[2,2,256]{2,1,0:T(2,128)S(1)}) custom-call(s32[4]{0:T(128)S(1)} %get-tuple-element.142.plan_ref, bf16[2,768,256]{2,1,0:T(8,128)(2,1)S(1)} %pad_maximum_fusion.1.refs_0_, bf16[2,768,256]{2,1,0:T(8,128)(2,1)} %collective-permute-done.13.refs_1_, ...), custom_call_target="tpu_custom_call" | custom-call | flops 3623878656 | bytes 14155776 | tf_op jit(solution)/shard_map/pallas_call | solution.py:347
  87.5 1.0 copy-done.8
  89.0 1.0 pad_maximum_fusion.refs_0_
  90.0 1.7 collective-permute-start.15
  93.0 9.7 %shard_map.117.hidden_ref = bf16[2,256,576]{2,1,0:T(8,128)(2,1)S(1)} custom-call(s32[4]{0:T(128)S(1)} %add_add_fusion.plan_ref, bf16[2,768,256]{2,1,0:T(8,128)(2,1)} %collective-permute-done.16.refs_0_, bf16[2,768,256]{2,1,0:T(8,128)(2,1)} %collective-permute-done.17.refs_1_, bf16[2,768,256]{2,1,0:T(8,128)(2,1)S(1)} %collective-permute-done.12.refs_2_, ...), custom_call_target="tpu_custom_call" | custom-call | flops 3623878656 | bytes 14155776 | tf_op jit(solution)/shard_map/pallas_call | solution.py:347
  102.7 7.2 %shard_map.118 = (bf16[4,256,768]{2,1,0:T(8,128)(2,1)S(1)}, bf16[4,256,768]{2,1,0:T(8,128)(2,1)S(1)}) custom-call(s32[4]{0:T(128)S(1)} %get-tuple-element.143.plan_ref, bf16[2,256,576]{2,1,0:T(8,128)(2,1)S(1)} %shard_map.117.hidden_ref, bf16[2,576,6144]{2,1,0:T(8,128)(2,1)} %down_ref.5), custom_call_target="tpu_custom_call" | custom-call | flops 1811939328 | bytes 7077888 | tf_op jit(solution)/shard_map/pallas_call | solution.py:406
  111.1 7.2 %shard_map.119 = (bf16[4,256,768]{2,1,0:T(8,128)(2,1)S(1)}, bf16[4,256,768]{2,1,0:T(8,128)(2,1)S(1)}) custom-call(s32[4]{0:T(128)S(1)} %pad_add_fusion.3.plan_ref, bf16[2,256,576]{2,1,0:T(8,128)(2,1)S(1)} %shard_map.117.hidden_ref, bf16[2,576,6144]{2,1,0:T(8,128)(2,1)} %down_ref.5), custom_call_target="tpu_custom_call" | custom-call | flops 1811939328 | bytes 7077888 | tf_op jit(solution)/shard_map/pallas_call | solution.py:406
  118.5 1.8 collective-permute-start.24
  120.8 8.9 %shard_map.120 = (f32[2,576,256]{2,1,0:T(8,128)S(1)}, f32[2,576,256]{2,1,0:T(8,128)S(1)}, f32[2,2,256]{2,1,0:T(2,128)S(1)}) custom-call(s32[4]{0:T(128)S(1)} %get-tuple-element.142.plan_ref, bf16[2,768,256]{2,1,0:T(8,128)(2,1)} %pad_maximum_fusion.refs_0_, bf16[2,768,256]{2,1,0:T(8,128)(2,1)S(1)} %collective-permute-done.22.refs_1_, ...), custom_call_target="tpu_custom_call" | custom-call | flops 3623878656 | bytes 14155776 | tf_op jit(solution)/shard_map/pallas_call | solution.py:347
  129.8 1.1 add_convert_fusion.2
  131.0 1.5 collective-permute-start.27
  132.5 9.2 %shard_map.121.hidden_ref = bf16[2,256,576]{2,1,0:T(8,128)(2,1)S(1)} custom-call(s32[4]{0:T(128)S(1)} %add_add_fusion.plan_ref, bf16[2,768,256]{2,1,0:T(8,128)(2,1)} %collective-permute-done.15.refs_0_, bf16[2,768,256]{2,1,0:T(8,128)(2,1)S(1)} %collective-permute-done.20.refs_1_, bf16[2,768,256]{2,1,0:T(8,128)(2,1)S(1)} %copy-done.11, ...), custom_call_target="tpu_custom_call" | custom-call | flops 3623878656 | bytes 14155776 | tf_op jit(solution)/shard_map/pallas_call | solution.py:347
  141.7 2.8 %collective-permute-done.26 = bf16[256,768]{1,0:T(8,128)(2,1)S(1)} collective-permute-done((bf16[256,768]{1,0:T(8,128)(2,1)S(1)}, bf16[256,768]{1,0:T(8,128)(2,1)S(1)}, u32[]{:S(2)}, u32[]{:S(2)}) %collective-permute-start.26) | collective-permute-done | bytes 393248 | tf_op jit(solution)/shard_map/ppermute | solution.py:435
  145.0 1.4 collective-permute-start.28
  146.6 1.1 copy-done.3
  147.7 12.7 %shard_map.123 = (bf16[4,256,768]{2,1,0:T(8,128)(2,1)S(1)}, bf16[4,256,768]{2,1,0:T(8,128)(2,1)S(1)}, bf16[4,256,768]{2,1,0:T(8,128)(2,1)S(1)}, bf16[4,256,768]{2,1,0:T(8,128)(2,1)S(1)}) custom-call(s32[8]{0:T(128)S(1)} %concatenate.8.plan_ref, bf16[2,256,576]{2,1,0:T(8,128)(2,1)S(1)} %copy-done.3, bf16[2,576,6144]{2,1,0:T(8,128)(2,1)} %down_ref.5), custom_call_target="tpu_custom_call" | custom-call | flops 3623878656 | bytes 14155776 | tf_op jit(solution)/shard_map/pallas_call | solution.py:406
  161.0 2.9 %collective-permute-done.30.refs_1_ = bf16[4,256,768]{2,1,0:T(8,128)(2,1)S(1)} collective-permute-done((bf16[4,256,768]{2,1,0:T(8,128)(2,1)S(1)}, bf16[4,256,768]{2,1,0:T(8,128)(2,1)S(1)}, u32[]{:S(2)}, u32[]{:S(2)}) %collective-permute-start.30) | collective-permute-done | bytes 1572896 | tf_op jit(solution)/shard_map/ppermute | solution.py:435
  164.1 1.5 collective-permute-start.31
  165.6 1.1 fusion.1
  166.7 1.0 collective-permute-start.34
  167.8 6.2 %collective-permute-start.33 = (bf16[256,768]{1,0:T(8,128)(2,1)S(1)}, bf16[256,768]{1,0:T(8,128)(2,1)S(1)}, u32[]{:S(2)}, u32[]{:S(2)}) collective-permute-start(bf16[256,768]{1,0:T(8,128)(2,1)S(1)} %shard_map.122), channel_id=1, source_target_pairs={{0,16},{24,8},{1,17},{25,9},{2,18},{26,10},{3,19},{27,11},{4,20},{... | collective-permute-start | bytes 1179656 | tf_op jit(solution)/shard_map/ppermute | solution.py:615
  174.2 6.2 %collective-permute-done.31.refs_2_ = bf16[2,256,768]{2,1,0:T(8,128)(2,1)S(1)} collective-permute-done((bf16[2,256,768]{2,1,0:T(8,128)(2,1)S(1)}, bf16[2,256,768]{2,1,0:T(8,128)(2,1)S(1)}, u32[]{:S(2)}, u32[]{:S(2)}) %collective-permute-start.31) | collective-permute-done | bytes 786464 | tf_op jit(solution)/shard_map/ppermute | solution.py:435
  180.3 1.4 collective-permute-start.32
  182.0 1.1 collective-permute-start.35
  183.1 1.4 shard_map.126
  184.6 3.6 %collective-permute-start.37 = (bf16[256,768]{1,0:T(8,128)(2,1)S(1)}, bf16[256,768]{1,0:T(8,128)(2,1)S(1)}, u32[]{:S(2)}, u32[]{:S(2)}) collective-permute-start(bf16[256,768]{1,0:T(8,128)(2,1)S(1)} %shard_map.126), channel_id=1, source_target_pairs={{0,8},{8,0},{16,24},{24,16},{1,9},{9,1},{17,25},{25,17},{2,10},{10... | collective-permute-start | bytes 1179656 | tf_op jit(solution)/shard_map/ppermute | solution.py:435
  188.2 5.9 %collective-permute-done.35 = bf16[256,768]{1,0:T(8,128)(2,1)S(1)} collective-permute-done((bf16[256,768]{1,0:T(8,128)(2,1)S(1)}, bf16[256,768]{1,0:T(8,128)(2,1)S(1)}, u32[]{:S(2)}, u32[]{:S(2)}) %collective-permute-start.35) | collective-permute-done | bytes 393248 | tf_op jit(solution)/shard_map/ppermute | solution.py:435
  194.6 1.8 collective-permute-done.32.refs_2_
  197.2 7.7 %collective-permute-start.39 = (bf16[256,768]{1,0:T(8,128)(2,1)S(1)}, bf16[256,768]{1,0:T(8,128)(2,1)S(1)}, u32[]{:S(2)}, u32[]{:S(2)}) collective-permute-start(bf16[256,768]{1,0:T(8,128)(2,1)S(1)} %shard_map.124), channel_id=1, source_target_pairs={{0,24},{24,0},{1,25},{25,1},{2,26},{26,2},{3,27},{27,3},{4,28},{28... | collective-permute-start | bytes 1179656 | tf_op jit(solution)/shard_map/ppermute | solution.py:629
  205.0 1.3 collective-permute-start.38
  206.7 6.9 %collective-permute-done.39 = bf16[256,768]{1,0:T(8,128)(2,1)S(1)} collective-permute-done((bf16[256,768]{1,0:T(8,128)(2,1)S(1)}, bf16[256,768]{1,0:T(8,128)(2,1)S(1)}, u32[]{:S(2)}, u32[]{:S(2)}) %collective-permute-start.39) | collective-permute-done | bytes 393248 | tf_op jit(solution)/shard_map/ppermute | solution.py:629
  213.6 8.3 %collective-permute-done.38 = bf16[256,768]{1,0:T(8,128)(2,1)S(1)} collective-permute-done((bf16[256,768]{1,0:T(8,128)(2,1)S(1)}, bf16[256,768]{1,0:T(8,128)(2,1)S(1)}, u32[]{:S(2)}, u32[]{:S(2)}) %collective-permute-start.38) | collective-permute-done | bytes 393248 | tf_op jit(solution)/shard_map/ppermute | solution.py:628
  221.9 2.1 add_convert_fusion.8
  (127 shorter events, 13.2 us)
Async XLA Ops:
  2.2 10.8 %collective-permute-start = (bf16[784,128]{1,0:T(8,128)(2,1)S(1)}, bf16[784,128]{1,0:T(8,128)(2,1)S(1)}, u32[]{:S(2)}, u32[]{:S(2)}) collective-permute-start(bf16[784,128]{1,0:T(8,128)(2,1)S(1)} %get-tuple-element.73), channel_id=1, source_target_pairs={{0,8},{8,16},{16,24},{1,9},{9,17},{17,25},{2,10},{10,18},{18,26},{... | collective-permute-start | bytes 602120 | tf_op jit(solution)/shard_map/ppermute | solution.py:30
  9.9 1.0 copy-start.7
  13.0 8.9 %copy-start.5 = (bf16[256,768]{1,0:T(8,128)(2,1)S(1)}, bf16[256,768]{1,0:T(8,128)(2,1)}, u32[]{:S(2)}) copy-start(bf16[256,768]{1,0:T(8,128)(2,1)} %query_ref.3) | copy-start | bytes 1179652
  13.0 8.9 %copy-start.21 = (bf16[256,768]{1,0:T(8,128)(2,1)S(1)}, bf16[256,768]{1,0:T(8,128)(2,1)}, u32[]{:S(2)}) copy-start(bf16[256,768]{1,0:T(8,128)(2,1)} %residual_ref.1) | copy-start | bytes 1179652
  13.0 8.9 %copy-start.31 = (s32[256,2]{0,1:T(2,128)S(1)}, s32[256,2]{0,1:T(2,128)}, u32[]{:S(2)}) copy-start(s32[256,2]{0,1:T(2,128)} %param.17) | copy-start | bytes 6148
  13.3 8.5 %collective-permute-start.1 = (bf16[784,128]{1,0:T(8,128)(2,1)S(1)}, bf16[784,128]{1,0:T(8,128)(2,1)S(1)}, u32[]{:S(2)}, u32[]{:S(2)}) collective-permute-start(bf16[784,128]{1,0:T(8,128)(2,1)S(1)} %concatenate.7), channel_id=1, source_target_pairs={{0,16},{8,24},{1,17},{9,25},{2,18},{10,26},{3,19},{11,27},{4,20},{... | collective-permute-start | bytes 602120 | tf_op jit(solution)/shard_map/ppermute | solution.py:30
  22.7 28.5 %copy-start = (bf16[272,768]{1,0:T(8,128)(2,1)}, bf16[272,768]{1,0:T(8,128)(2,1)S(1)}, u32[]{:S(2)}) copy-start(bf16[272,768]{1,0:T(8,128)(2,1)S(1)} %shard_map.111.refs_0_) | copy-start | bytes 1253380
  23.8 10.5 %copy-start.22 = (bf16[256,256]{1,0:T(8,128)(2,1)}, bf16[256,256]{1,0:T(8,128)(2,1)S(1)}, u32[]{:S(2)}) copy-start(bf16[256,256]{1,0:T(8,128)(2,1)S(1)} %get-tuple-element.74.place_ref) | copy-start | bytes 393220
  23.8 8.0 %collective-permute-start.10 = (bf16[768,256]{1,0:T(8,128)(2,1)S(1)}, bf16[768,256]{1,0:T(8,128)(2,1)S(1)}, u32[]{:S(2)}, u32[]{:S(2)}) collective-permute-start(bf16[768,256]{1,0:T(8,128)(2,1)S(1)} %get-tuple-element.78), channel_id=1, source_target_pairs={{0,2},{1,5},{2,0},{3,7},{4,6},{5,1},{6,4},{7,3},{8,10},{9,13},{10,... | collective-permute-start | bytes 1179656 | tf_op jit(solution)/shard_map/ppermute | solution.py:435
  25.3 8.9 %collective-permute-start.6 = (bf16[272,768]{1,0:T(8,128)(2,1)S(1)}, bf16[272,768]{1,0:T(8,128)(2,1)S(1)}, u32[]{:S(2)}, u32[]{:S(2)}) collective-permute-start(bf16[272,768]{1,0:T(8,128)(2,1)S(1)} %shard_map.111.refs_0_), channel_id=1, source_target_pairs={{8,16},{16,8},{9,17},{17,9},{10,18},{18,10},{11,19},{19,11},{12,20... | collective-permute-start | bytes 1253384 | tf_op jit(solution)/shard_map/ppermute | solution.py:533
  26.0 14.0 %collective-permute-start.2 = (bf16[272,768]{1,0:T(8,128)(2,1)S(1)}, bf16[272,768]{1,0:T(8,128)(2,1)S(1)}, u32[]{:S(2)}, u32[]{:S(2)}) collective-permute-start(bf16[272,768]{1,0:T(8,128)(2,1)S(1)} %shard_map.111.refs_0_), channel_id=1, source_target_pairs={{0,8},{8,0},{16,24},{24,16},{1,9},{9,1},{17,25},{25,17},{2,10},{10... | collective-permute-start | bytes 1253384 | tf_op jit(solution)/shard_map/ppermute | solution.py:435
  32.7 21.2 %collective-permute-start.11 = (bf16[2,768,256]{2,1,0:T(8,128)(2,1)}, bf16[2,768,256]{2,1,0:T(8,128)(2,1)S(1)}, u32[]{:S(2)}, u32[]{:S(2)}) collective-permute-start(bf16[2,768,256]{2,1,0:T(8,128)(2,1)} %pad_maximum_fusion.3.refs_2_), channel_id=1, source_target_pairs={{0,4},{1,3},{2,6},{3,1},{4,0},{5,7},{6,2},{7,5},{8,12},{9,11},{10,... | collective-permute-start | bytes 2359304 | tf_op jit(solution)/shard_map/ppermute | solution.py:435
  34.3 16.0 %collective-permute-start.7 = (bf16[272,768]{1,0:T(8,128)(2,1)S(1)}, bf16[272,768]{1,0:T(8,128)(2,1)S(1)}, u32[]{:S(2)}, u32[]{:S(2)}) collective-permute-start(bf16[272,768]{1,0:T(8,128)(2,1)S(1)} %collective-permute-done.6.refs_0_), channel_id=1, source_target_pairs={{8,0},{16,24},{9,1},{17,25},{10,2},{18,26},{11,3},{19,27},{12,4},{... | collective-permute-start | bytes 1253384 | tf_op jit(solution)/shard_map/ppermute | solution.py:536
  41.0 22.9 %copy-start.24 = (bf16[256,256]{1,0:T(8,128)(2,1)}, bf16[256,256]{1,0:T(8,128)(2,1)S(1)}, u32[]{:S(2)}) copy-start(bf16[256,256]{1,0:T(8,128)(2,1)S(1)} %get-tuple-element.137.place_ref) | copy-start | bytes 393220
  41.1 12.8 %collective-permute-start.9 = (bf16[768,256]{1,0:T(8,128)(2,1)S(1)}, bf16[768,256]{1,0:T(8,128)(2,1)S(1)}, u32[]{:S(2)}, u32[]{:S(2)}) collective-permute-start(bf16[768,256]{1,0:T(8,128)(2,1)S(1)} %get-tuple-element.77), channel_id=1, source_target_pairs={{0,2},{1,5},{2,0},{3,7},{4,6},{5,1},{6,4},{7,3},{8,10},{9,13},{10,... | collective-permute-start | bytes 1179656 | tf_op jit(solution)/shard_map/ppermute | solution.py:435
  42.6 11.3 %collective-permute-start.3 = (bf16[272,768]{1,0:T(8,128)(2,1)S(1)}, bf16[272,768]{1,0:T(8,128)(2,1)S(1)}, u32[]{:S(2)}, u32[]{:S(2)}) collective-permute-start(bf16[272,768]{1,0:T(8,128)(2,1)S(1)} %collective-permute-done.2.refs_0_), channel_id=1, source_target_pairs={{8,16},{16,8},{9,17},{17,9},{10,18},{18,10},{11,19},{19,11},{12,20... | collective-permute-start | bytes 1253384 | tf_op jit(solution)/shard_map/ppermute | solution.py:533
  51.3 2.7 %copy-start.28 = (bf16[256,256]{1,0:T(8,128)(2,1)}, bf16[256,256]{1,0:T(8,128)(2,1)S(1)}, u32[]{:S(2)}) copy-start(bf16[256,256]{1,0:T(8,128)(2,1)S(1)} %get-tuple-element.122.place_ref) | copy-start | bytes 393220
  51.3 12.5 %collective-permute-start.8 = (bf16[768,256]{1,0:T(8,128)(2,1)S(1)}, bf16[768,256]{1,0:T(8,128)(2,1)S(1)}, u32[]{:S(2)}, u32[]{:S(2)}) collective-permute-start(bf16[768,256]{1,0:T(8,128)(2,1)S(1)} %get-tuple-element.76), channel_id=1, source_target_pairs={{0,2},{1,5},{2,0},{3,7},{4,6},{5,1},{6,4},{7,3},{8,10},{9,13},{10,... | collective-permute-start | bytes 1179656 | tf_op jit(solution)/shard_map/ppermute | solution.py:435
  53.9 15.4 %copy-start.14 = (bf16[272,768]{1,0:T(8,128)(2,1)}, bf16[272,768]{1,0:T(8,128)(2,1)S(1)}, u32[]{:S(2)}) copy-start(bf16[272,768]{1,0:T(8,128)(2,1)S(1)} %collective-permute-done.3.refs_0_) | copy-start | bytes 1253380
  53.9 15.4 %copy-start.10 = (bf16[2,768,256]{2,1,0:T(8,128)(2,1)}, bf16[2,768,256]{2,1,0:T(8,128)(2,1)S(1)}, u32[]{:S(2)}) copy-start(bf16[2,768,256]{2,1,0:T(8,128)(2,1)S(1)} %collective-permute-done.11.refs_2_) | copy-start | bytes 2359300
  53.9 15.4 %collective-permute-start.12 = (bf16[2,768,256]{2,1,0:T(8,128)(2,1)S(1)}, bf16[2,768,256]{2,1,0:T(8,128)(2,1)S(1)}, u32[]{:S(2)}, u32[]{:S(2)}) collective-permute-start(bf16[2,768,256]{2,1,0:T(8,128)(2,1)S(1)} %pad_maximum_fusion.2.refs_2_), channel_id=1, source_target_pairs={{0,4},{1,3},{2,6},{3,1},{4,0},{5,7},{6,2},{7,5},{8,12},{9,11},{10,... | collective-permute-start | bytes 2359304 | tf_op jit(solution)/shard_map/ppermute | solution.py:435
  54.0 21.8 %collective-permute-start.14 = (bf16[2,768,256]{2,1,0:T(8,128)(2,1)S(1)}, bf16[2,768,256]{2,1,0:T(8,128)(2,1)S(1)}, u32[]{:S(2)}, u32[]{:S(2)}) collective-permute-start(bf16[2,768,256]{2,1,0:T(8,128)(2,1)S(1)} %pad_maximum_fusion.2.refs_2_), channel_id=1, source_target_pairs={{0,1},{1,0},{2,3},{3,2},{4,5},{5,4},{6,7},{7,6},{8,9},{9,8},{10,11... | collective-permute-start | bytes 2359304 | tf_op jit(solution)/shard_map/ppermute | solution.py:435
  54.1 14.4 %collective-permute-start.4 = (bf16[272,768]{1,0:T(8,128)(2,1)S(1)}, bf16[272,768]{1,0:T(8,128)(2,1)S(1)}, u32[]{:S(2)}, u32[]{:S(2)}) collective-permute-start(bf16[272,768]{1,0:T(8,128)(2,1)S(1)} %collective-permute-done.3.refs_0_), channel_id=1, source_target_pairs={{8,0},{16,24},{9,1},{17,25},{10,2},{18,26},{11,3},{19,27},{12,4},{... | collective-permute-start | bytes 1253384 | tf_op jit(solution)/shard_map/ppermute | solution.py:536
  63.9 12.8 %collective-permute-start.13 = (bf16[2,768,256]{2,1,0:T(8,128)(2,1)S(1)}, bf16[2,768,256]{2,1,0:T(8,128)(2,1)}, u32[]{:S(2)}, u32[]{:S(2)}) collective-permute-start(bf16[2,768,256]{2,1,0:T(8,128)(2,1)S(1)} %pad_maximum_fusion.1.refs_0_), channel_id=1, source_target_pairs={{0,1},{1,0},{2,3},{3,2},{4,5},{5,4},{6,7},{7,6},{8,9},{9,8},{10,11... | collective-permute-start | bytes 2359304 | tf_op jit(solution)/shard_map/ppermute | solution.py:435
  69.3 19.2 %collective-permute-start.16 = (bf16[2,768,256]{2,1,0:T(8,128)(2,1)S(1)}, bf16[2,768,256]{2,1,0:T(8,128)(2,1)}, u32[]{:S(2)}, u32[]{:S(2)}) collective-permute-start(bf16[2,768,256]{2,1,0:T(8,128)(2,1)S(1)} %pad_maximum_fusion.1.refs_0_), channel_id=1, source_target_pairs={{0,4},{1,3},{2,6},{3,1},{4,0},{5,7},{6,2},{7,5},{8,12},{9,11},{10,... | collective-permute-start | bytes 2359304 | tf_op jit(solution)/shard_map/ppermute | solution.py:435
  70.9 1.0 copy-start.15
  71.9 1.0 copy-start.17
  74.6 14.4 %collective-permute-start.5 = (bf16[768,256]{1,0:T(8,128)(2,1)S(1)}, bf16[768,256]{1,0:T(8,128)(2,1)S(1)}, u32[]{:S(2)}, u32[]{:S(2)}) collective-permute-start(bf16[768,256]{1,0:T(8,128)(2,1)S(1)} %get-tuple-element.75), channel_id=1, source_target_pairs={{0,2},{1,5},{2,0},{3,7},{4,6},{5,1},{6,4},{7,3},{8,10},{9,13},{10,... | collective-permute-start | bytes 1179656 | tf_op jit(solution)/shard_map/ppermute | solution.py:435
  76.7 1.1 copy-start.13
  87.5 1.0 copy-start.8
  88.5 3.3 %collective-permute-start.18 = (bf16[2,768,256]{2,1,0:T(8,128)(2,1)S(1)}, bf16[2,768,256]{2,1,0:T(8,128)(2,1)}, u32[]{:S(2)}, u32[]{:S(2)}) collective-permute-start(bf16[2,768,256]{2,1,0:T(8,128)(2,1)S(1)} %collective-permute-done.12.refs_2_), channel_id=1, source_target_pairs={{0,1},{1,0},{2,3},{3,2},{4,5},{5,4},{6,7},{7,6},{8,9},{9,8},{10,11... | collective-permute-start | bytes 2359304 | tf_op jit(solution)/shard_map/ppermute | solution.py:435
  88.5 3.7 %copy-start.9 = (f32[2,576,256]{2,1,0:T(8,128)S(1)}, f32[2,576,256]{2,1,0:T(8,128)}, u32[]{:S(2)}) copy-start(f32[2,576,256]{2,1,0:T(8,128)} %copy-done.8) | copy-start | bytes 3538948
  88.5 3.7 %collective-permute-start.17 = (bf16[2,768,256]{2,1,0:T(8,128)(2,1)}, bf16[2,768,256]{2,1,0:T(8,128)(2,1)}, u32[]{:S(2)}, u32[]{:S(2)}) collective-permute-start(bf16[2,768,256]{2,1,0:T(8,128)(2,1)} %collective-permute-done.16.refs_0_), channel_id=1, source_target_pairs={{0,1},{1,0},{2,3},{3,2},{4,5},{5,4},{6,7},{7,6},{8,9},{9,8},{10,11... | collective-permute-start | bytes 2359304 | tf_op jit(solution)/shard_map/ppermute | solution.py:435
  90.0 12.7 %collective-permute-start.15 = (bf16[2,768,256]{2,1,0:T(8,128)(2,1)}, bf16[2,768,256]{2,1,0:T(8,128)(2,1)}, u32[]{:S(2)}, u32[]{:S(2)}) collective-permute-start(bf16[2,768,256]{2,1,0:T(8,128)(2,1)} %pad_maximum_fusion.refs_0_), channel_id=1, source_target_pairs={{0,4},{1,3},{2,6},{3,1},{4,0},{5,7},{6,2},{7,5},{8,12},{9,11},{10,... | collective-permute-start | bytes 2359304 | tf_op jit(solution)/shard_map/ppermute | solution.py:435
  109.9 8.4 %collective-permute-start.19 = (bf16[4,256,768]{2,1,0:T(8,128)(2,1)S(1)}, bf16[4,256,768]{2,1,0:T(8,128)(2,1)S(1)}, u32[]{:S(2)}, u32[]{:S(2)}) collective-permute-start(bf16[4,256,768]{2,1,0:T(8,128)(2,1)S(1)} %get-tuple-element.100), channel_id=1, source_target_pairs={{0,1},{1,0},{2,3},{3,2},{4,5},{5,4},{6,7},{7,6},{8,9},{9,8},{10,11... | collective-permute-start | bytes 4718600 | tf_op jit(solution)/shard_map/ppermute | solution.py:435
  110.1 19.6 %collective-permute-start.25 = (bf16[4,256,768]{2,1,0:T(8,128)(2,1)S(1)}, bf16[4,256,768]{2,1,0:T(8,128)(2,1)S(1)}, u32[]{:S(2)}, u32[]{:S(2)}) collective-permute-start(bf16[4,256,768]{2,1,0:T(8,128)(2,1)S(1)} %get-tuple-element.101), channel_id=1, source_target_pairs={{0,1},{1,0},{2,3},{3,2},{4,5},{5,4},{6,7},{7,6},{8,9},{9,8},{10,11... | collective-permute-start | bytes 4718600 | tf_op jit(solution)/shard_map/ppermute | solution.py:435
  110.5 9.8 %collective-permute-start.23 = (bf16[2,768,256]{2,1,0:T(8,128)(2,1)}, bf16[2,768,256]{2,1,0:T(8,128)(2,1)S(1)}, u32[]{:S(2)}, u32[]{:S(2)}) collective-permute-start(bf16[2,768,256]{2,1,0:T(8,128)(2,1)} %pad_maximum_fusion.3.refs_2_), channel_id=1, source_target_pairs={{0,1},{1,0},{2,3},{3,2},{4,5},{5,4},{6,7},{7,6},{8,9},{9,8},{10,11... | collective-permute-start | bytes 2359304 | tf_op jit(solution)/shard_map/ppermute | solution.py:435
  110.6 9.7 %collective-permute-start.22 = (bf16[2,768,256]{2,1,0:T(8,128)(2,1)}, bf16[2,768,256]{2,1,0:T(8,128)(2,1)S(1)}, u32[]{:S(2)}, u32[]{:S(2)}) collective-permute-start(bf16[2,768,256]{2,1,0:T(8,128)(2,1)} %pad_maximum_fusion.refs_0_), channel_id=1, source_target_pairs={{0,1},{1,0},{2,3},{3,2},{4,5},{5,4},{6,7},{7,6},{8,9},{9,8},{10,11... | collective-permute-start | bytes 2359304 | tf_op jit(solution)/shard_map/ppermute | solution.py:435
  118.3 2.0 copy-start.11
  118.3 2.5 %copy-start.20 = (bf16[6144,2]{0,1:T(2,128)(2,1)S(1)}, bf16[6144,2]{0,1:T(2,128)(2,1)}, u32[]{:S(2)}) copy-start(bf16[6144,2]{0,1:T(2,128)(2,1)} %param.18) | copy-start | bytes 73732
  118.5 12.3 %collective-permute-start.24 = (bf16[2,256,768]{2,1,0:T(8,128)(2,1)S(1)}, bf16[2,256,768]{2,1,0:T(8,128)(2,1)S(1)}, u32[]{:S(2)}, u32[]{:S(2)}) collective-permute-start(bf16[2,256,768]{2,1,0:T(8,128)(2,1)S(1)} %add_convert_fusion.3), channel_id=1, source_target_pairs={{0,4},{1,3},{2,6},{3,1},{4,0},{5,7},{6,2},{7,5},{8,12},{9,11},{10,... | collective-permute-start | bytes 2359304 | tf_op jit(solution)/shard_map/ppermute | solution.py:435
  120.3 12.2 %collective-permute-start.20 = (bf16[2,768,256]{2,1,0:T(8,128)(2,1)}, bf16[2,768,256]{2,1,0:T(8,128)(2,1)S(1)}, u32[]{:S(2)}, u32[]{:S(2)}) collective-permute-start(bf16[2,768,256]{2,1,0:T(8,128)(2,1)} %collective-permute-done.15.refs_0_), channel_id=1, source_target_pairs={{0,1},{1,0},{2,3},{3,2},{4,5},{5,4},{6,7},{7,6},{8,9},{9,8},{10,11... | collective-permute-start | bytes 2359304 | tf_op jit(solution)/shard_map/ppermute | solution.py:435
  120.3 12.2 %collective-permute-start.21 = (bf16[2,768,256]{2,1,0:T(8,128)(2,1)S(1)}, bf16[2,768,256]{2,1,0:T(8,128)(2,1)S(1)}, u32[]{:S(2)}, u32[]{:S(2)}) collective-permute-start(bf16[2,768,256]{2,1,0:T(8,128)(2,1)S(1)} %copy-done.11), channel_id=1, source_target_pairs={{0,1},{1,0},{2,3},{3,2},{4,5},{5,4},{6,7},{7,6},{8,9},{9,8},{10,11... | collective-permute-start | bytes 2359304 | tf_op jit(solution)/shard_map/ppermute | solution.py:435
  131.0 13.6 %copy-start.29 = (bf16[256,256]{1,0:T(8,128)(2,1)S(1)}, bf16[256,256]{1,0:T(8,128)(2,1)}, u32[]{:S(2)}) copy-start(bf16[256,256]{1,0:T(8,128)(2,1)} %copy-done.28) | copy-start | bytes 393220
  131.0 15.6 %collective-permute-start.27 = (bf16[2,256,768]{2,1,0:T(8,128)(2,1)}, bf16[2,256,768]{2,1,0:T(8,128)(2,1)}, u32[]{:S(2)}, u32[]{:S(2)}) collective-permute-start(bf16[2,256,768]{2,1,0:T(8,128)(2,1)} %add_convert_fusion.2), channel_id=1, source_target_pairs={{0,4},{1,3},{2,6},{3,1},{4,0},{5,7},{6,2},{7,5},{8,12},{9,11},{10,... | collective-permute-start | bytes 2359304 | tf_op jit(solution)/shard_map/ppermute | solution.py:435
  132.5 12.1 %collective-permute-start.26 = (bf16[256,768]{1,0:T(8,128)(2,1)S(1)}, bf16[256,768]{1,0:T(8,128)(2,1)S(1)}, u32[]{:S(2)}, u32[]{:S(2)}) collective-permute-start(bf16[256,768]{1,0:T(8,128)(2,1)S(1)} %fusion), channel_id=1, source_target_pairs={{0,2},{1,5},{2,0},{3,7},{4,6},{5,1},{6,4},{7,3},{8,10},{9,13},{10,... | collective-permute-start | bytes 1179656 | tf_op jit(solution)/shard_map/ppermute | solution.py:435
  141.7 3.3 %copy-start.2 = (bf16[2,256,576]{2,1,0:T(8,128)(2,1)}, bf16[2,256,576]{2,1,0:T(8,128)(2,1)S(1)}, u32[]{:S(2)}) copy-start(bf16[2,256,576]{2,1,0:T(8,128)(2,1)S(1)} %shard_map.121.hidden_ref) | copy-start | bytes 1769476
  145.0 15.4 %collective-permute-start.28 = (bf16[256,768]{1,0:T(8,128)(2,1)S(1)}, bf16[256,768]{1,0:T(8,128)(2,1)}, u32[]{:S(2)}, u32[]{:S(2)}) collective-permute-start(bf16[256,768]{1,0:T(8,128)(2,1)S(1)} %shard_map.122), channel_id=1, source_target_pairs={{8,16},{16,8},{9,17},{17,9},{10,18},{18,10},{11,19},{19,11},{12,20... | collective-permute-start | bytes 1179656 | tf_op jit(solution)/shard_map/ppermute | solution.py:608
  146.6 1.1 copy-start.3
  160.4 3.5 %collective-permute-start.30 = (bf16[4,256,768]{2,1,0:T(8,128)(2,1)S(1)}, bf16[4,256,768]{2,1,0:T(8,128)(2,1)S(1)}, u32[]{:S(2)}, u32[]{:S(2)}) collective-permute-start(bf16[4,256,768]{2,1,0:T(8,128)(2,1)S(1)} %get-tuple-element.131), channel_id=1, source_target_pairs={{0,1},{1,0},{2,3},{3,2},{4,5},{5,4},{6,7},{7,6},{8,9},{9,8},{10,11... | collective-permute-start | bytes 4718600 | tf_op jit(solution)/shard_map/ppermute | solution.py:435
  160.6 13.4 %collective-permute-start.29 = (bf16[4,256,768]{2,1,0:T(8,128)(2,1)S(1)}, bf16[4,256,768]{2,1,0:T(8,128)(2,1)S(1)}, u32[]{:S(2)}, u32[]{:S(2)}) collective-permute-start(bf16[4,256,768]{2,1,0:T(8,128)(2,1)S(1)} %get-tuple-element.129), channel_id=1, source_target_pairs={{0,1},{1,0},{2,3},{3,2},{4,5},{5,4},{6,7},{7,6},{8,9},{9,8},{10,11... | collective-permute-start | bytes 4718600 | tf_op jit(solution)/shard_map/ppermute | solution.py:435
  164.1 16.3 %collective-permute-start.31 = (bf16[2,256,768]{2,1,0:T(8,128)(2,1)S(1)}, bf16[2,256,768]{2,1,0:T(8,128)(2,1)S(1)}, u32[]{:S(2)}, u32[]{:S(2)}) collective-permute-start(bf16[2,256,768]{2,1,0:T(8,128)(2,1)S(1)} %add_convert_fusion), channel_id=1, source_target_pairs={{0,4},{1,3},{2,6},{3,1},{4,0},{5,7},{6,2},{7,5},{8,12},{9,11},{10,... | collective-permute-start | bytes 2359304 | tf_op jit(solution)/shard_map/ppermute | solution.py:435
  166.7 15.1 %collective-permute-start.34 = (bf16[256,768]{1,0:T(8,128)(2,1)S(1)}, bf16[256,768]{1,0:T(8,128)(2,1)S(1)}, u32[]{:S(2)}, u32[]{:S(2)}) collective-permute-start(bf16[256,768]{1,0:T(8,128)(2,1)S(1)} %fusion.1), channel_id=1, source_target_pairs={{0,2},{1,5},{2,0},{3,7},{4,6},{5,1},{6,4},{7,3},{8,10},{9,13},{10,... | collective-permute-start | bytes 1179656 | tf_op jit(solution)/shard_map/ppermute | solution.py:435
  167.8 14.1 %collective-permute-start.33 = (bf16[256,768]{1,0:T(8,128)(2,1)S(1)}, bf16[256,768]{1,0:T(8,128)(2,1)S(1)}, u32[]{:S(2)}, u32[]{:S(2)}) collective-permute-start(bf16[256,768]{1,0:T(8,128)(2,1)S(1)} %shard_map.122), channel_id=1, source_target_pairs={{0,16},{24,8},{1,17},{25,9},{2,18},{26,10},{3,19},{27,11},{4,20},{... | collective-permute-start | bytes 1179656 | tf_op jit(solution)/shard_map/ppermute | solution.py:615
  174.0 9.1 %copy-start.25 = (bf16[256,256]{1,0:T(8,128)(2,1)S(1)}, bf16[256,256]{1,0:T(8,128)(2,1)}, u32[]{:S(2)}) copy-start(bf16[256,256]{1,0:T(8,128)(2,1)} %copy-done.24) | copy-start | bytes 393220
  180.3 16.0 %collective-permute-start.32 = (bf16[2,256,768]{2,1,0:T(8,128)(2,1)S(1)}, bf16[2,256,768]{2,1,0:T(8,128)(2,1)S(1)}, u32[]{:S(2)}, u32[]{:S(2)}) collective-permute-start(bf16[2,256,768]{2,1,0:T(8,128)(2,1)S(1)} %add_convert_fusion.1), channel_id=1, source_target_pairs={{0,4},{1,3},{2,6},{3,1},{4,0},{5,7},{6,2},{7,5},{8,12},{9,11},{10,... | collective-permute-start | bytes 2359304 | tf_op jit(solution)/shard_map/ppermute | solution.py:435
  182.0 12.1 %collective-permute-start.35 = (bf16[256,768]{1,0:T(8,128)(2,1)S(1)}, bf16[256,768]{1,0:T(8,128)(2,1)S(1)}, u32[]{:S(2)}, u32[]{:S(2)}) collective-permute-start(bf16[256,768]{1,0:T(8,128)(2,1)S(1)} %fusion.2), channel_id=1, source_target_pairs={{0,2},{1,5},{2,0},{3,7},{4,6},{5,1},{6,4},{7,3},{8,10},{9,13},{10,... | collective-permute-start | bytes 1179656 | tf_op jit(solution)/shard_map/ppermute | solution.py:435
  183.1 11.0 %copy-start.27 = (bf16[256,256]{1,0:T(8,128)(2,1)S(1)}, bf16[256,256]{1,0:T(8,128)(2,1)}, u32[]{:S(2)}) copy-start(bf16[256,256]{1,0:T(8,128)(2,1)} %copy-done.26) | copy-start | bytes 393220
  184.6 12.7 %collective-permute-start.37 = (bf16[256,768]{1,0:T(8,128)(2,1)S(1)}, bf16[256,768]{1,0:T(8,128)(2,1)S(1)}, u32[]{:S(2)}, u32[]{:S(2)}) collective-permute-start(bf16[256,768]{1,0:T(8,128)(2,1)S(1)} %shard_map.126), channel_id=1, source_target_pairs={{0,8},{8,0},{16,24},{24,16},{1,9},{9,1},{17,25},{25,17},{2,10},{10... | collective-permute-start | bytes 1179656 | tf_op jit(solution)/shard_map/ppermute | solution.py:435
  194.6 11.7 %copy-start.23 = (bf16[256,256]{1,0:T(8,128)(2,1)S(1)}, bf16[256,256]{1,0:T(8,128)(2,1)}, u32[]{:S(2)}) copy-start(bf16[256,256]{1,0:T(8,128)(2,1)} %copy-done.22) | copy-start | bytes 393220
  196.6 9.7 %collective-permute-start.36 = (bf16[256,768]{1,0:T(8,128)(2,1)S(1)}, bf16[256,768]{1,0:T(8,128)(2,1)S(1)}, u32[]{:S(2)}, u32[]{:S(2)}) collective-permute-start(bf16[256,768]{1,0:T(8,128)(2,1)S(1)} %fusion.3), channel_id=1, source_target_pairs={{0,2},{1,5},{2,0},{3,7},{4,6},{5,1},{6,4},{7,3},{8,10},{9,13},{10,... | collective-permute-start | bytes 1179656 | tf_op jit(solution)/shard_map/ppermute | solution.py:435
  197.2 16.4 %collective-permute-start.39 = (bf16[256,768]{1,0:T(8,128)(2,1)S(1)}, bf16[256,768]{1,0:T(8,128)(2,1)S(1)}, u32[]{:S(2)}, u32[]{:S(2)}) collective-permute-start(bf16[256,768]{1,0:T(8,128)(2,1)S(1)} %shard_map.124), channel_id=1, source_target_pairs={{0,24},{24,0},{1,25},{25,1},{2,26},{26,2},{3,27},{27,3},{4,28},{28... | collective-permute-start | bytes 1179656 | tf_op jit(solution)/shard_map/ppermute | solution.py:629
  205.0 17.0 %collective-permute-start.38 = (bf16[256,768]{1,0:T(8,128)(2,1)S(1)}, bf16[256,768]{1,0:T(8,128)(2,1)S(1)}, u32[]{:S(2)}, u32[]{:S(2)}) collective-permute-start(bf16[256,768]{1,0:T(8,128)(2,1)S(1)} %shard_map.124), channel_id=1, source_target_pairs={{8,24},{16,0},{9,25},{17,1},{10,26},{18,2},{11,27},{19,3},{12,28},... | collective-permute-start | bytes 1179656 | tf_op jit(solution)/shard_map/ppermute | solution.py:628
  206.3 15.7 %copy-start.1 = (bf16[272,768]{1,0:T(8,128)(2,1)S(1)}, bf16[272,768]{1,0:T(8,128)(2,1)}, u32[]{:S(2)}) copy-start(bf16[272,768]{1,0:T(8,128)(2,1)} %copy-done) | copy-start | bytes 1253380
  (8 other events, 6.5 us)

commit v16 on v14

--- a/solution.py
+++ b/solution.py
@@ -225,9 +225,10 @@
     rows, width = parts[0].shape
     length = rows - ID_ROWS
     slots = experts * capacity
-    whole = pl.BlockSpec(memory_space=pltpu.VMEM)
+    whole = pl.BlockSpec((rows, width), lambda _: (0, 0))
     return pl.pallas_call(
         functools.partial(select_kernel, capacity, choices, experts),
+        grid=(1,),
         in_specs=[pl.BlockSpec(memory_space=pltpu.SMEM), *([whole] * len(parts))],
         out_shape=(
             jax.ShapeDtypeStruct((width, slots), BF16),
@@ -409,7 +410,7 @@
             num_scalar_prefetch=1,
             grid=(len(plans) * blocks,),
             in_specs=[
-                pl.BlockSpec(memory_space=pltpu.VMEM),
+                pl.BlockSpec(hidden.shape, lambda p, plan: (0, 0, 0)),
                 pl.BlockSpec((experts, units, width), lambda p, plan: (0, 0, plan[p])),
             ],
             out_specs=[out_spec(i) for i in range(len(plans)) for _ in range(sections)],

time: 221 us -> 221 us (level)
  no operation moved by 1% of the time
where the time goes in v16:
time: 221 us; the launch traced here: 219 us
  Pallas kernels  75.1 us (34%)
  waiting for transfers between devices  66.2 us (30%)
  starting transfers between devices  55.8 us (25%)
  local copies, waits for them, and re-layouts  13.8 us (6%)
  other arithmetic  7.92 us (4%)
    ppermute x30, waiting for transfers between devices, swapped(): return lax.ppermute(array, axis, pairs)  38.5 us
    pallas_call x4, Pallas kernels, gate_part(): pl.pallas_call(functools.partial(gate_kernel, counts, len(xs), last), gri...  36.8 us
    ppermute x30, starting transfers between devices, swapped(): return lax.ppermute(array, axis, pairs)  30.5 us
    pallas_call x3, Pallas kernels, down_part(): pl.pallas_call(functools.partial(down_kernel, blocks, sections), grid_spe...  27.1 us
    unnamed x60, local copies, waits for them, and re-layouts  12.8 us
    ppermute x2, starting transfers between devices, shifted(): return lax.ppermute(array, axis, pairs)  9.43 us
    ppermute x2, waiting for transfers between devices, outward(): return lax.ppermute(part, 'seq', [(1, 0), (2, 3)])  8.98 us
    ppermute x1, waiting for transfers between devices, paired_chunks(): lax.ppermute(fourth_piece, 'seq', [(1, 3), (2, 0)])  8.33 us
  transfers between devices with their start and end apart: 40, of which 20 were waited for; matrix products, arithmetic and copies ran while one was open for 3% of the time, Pallas kernels for 29%

profile of v16, /device:TPU:0, one launch (start us, length us, event | category | flops | bytes accessed | tf_op | source)
XLA Modules:
  0.0 219.5 jit_solution(649950630932734328)
XLA Ops:
  0.0 2.1 shard_map.109
  2.2 4.9 %collective-permute-start = (bf16[784,128]{1,0:T(8,128)(2,1)S(1)}, bf16[784,128]{1,0:T(8,128)(2,1)S(1)}, u32[]{:S(2)}, u32[]{:S(2)}) collective-permute-start(bf16[784,128]{1,0:T(8,128)(2,1)S(1)} %get-tuple-element.73), channel_id=1, source_target_pairs={{0,8},{8,16},{16,24},{1,9},{9,17},{17,25},{2,10},{10,18},{18,26},{... | collective-permute-start | bytes 602120 | tf_op jit(solution)/shard_map/ppermute | solution.py:30
  7.9 1.0 copy-done.4
  8.9 1.0 copy-done.6
  9.9 1.0 copy-done.7
  11.6 1.4 shard_map.110.intra_ref
  13.3 4.5 %collective-permute-start.1 = (bf16[784,128]{1,0:T(8,128)(2,1)S(1)}, bf16[784,128]{1,0:T(8,128)(2,1)S(1)}, u32[]{:S(2)}, u32[]{:S(2)}) collective-permute-start(bf16[784,128]{1,0:T(8,128)(2,1)S(1)} %concatenate.7), channel_id=1, source_target_pairs={{0,16},{8,24},{1,17},{9,25},{2,18},{10,26},{3,19},{11,27},{4,20},{... | collective-permute-start | bytes 602120 | tf_op jit(solution)/shard_map/ppermute | solution.py:30
  17.8 3.9 %collective-permute-done.1 = bf16[784,128]{1,0:T(8,128)(2,1)S(1)} collective-permute-done((bf16[784,128]{1,0:T(8,128)(2,1)S(1)}, bf16[784,128]{1,0:T(8,128)(2,1)S(1)}, u32[]{:S(2)}, u32[]{:S(2)}) %collective-permute-start.1) | collective-permute-done | bytes 200736 | tf_op jit(solution)/shard_map/ppermute | solution.py:30
  22.7 1.0 shard_map.112
  23.8 1.6 collective-permute-start.10
  25.3 4.4 %collective-permute-start.2 = (bf16[272,768]{1,0:T(8,128)(2,1)S(1)}, bf16[272,768]{1,0:T(8,128)(2,1)S(1)}, u32[]{:S(2)}, u32[]{:S(2)}) collective-permute-start(bf16[272,768]{1,0:T(8,128)(2,1)S(1)} %shard_map.111.refs_0_), channel_id=1, source_target_pairs={{0,8},{8,0},{16,24},{24,16},{1,9},{9,1},{17,25},{25,17},{2,10},{10... | collective-permute-start | bytes 1253384 | tf_op jit(solution)/shard_map/ppermute | solution.py:436
  30.5 1.2 collective-permute-done.10
  32.6 1.5 collective-permute-start.11
  34.1 3.9 %collective-permute-done.2.refs_0_ = bf16[272,768]{1,0:T(8,128)(2,1)S(1)} collective-permute-done((bf16[272,768]{1,0:T(8,128)(2,1)S(1)}, bf16[272,768]{1,0:T(8,128)(2,1)S(1)}, u32[]{:S(2)}, u32[]{:S(2)}) %collective-permute-start.2) | collective-permute-done | bytes 417824 | tf_op jit(solution)/shard_map/ppermute | solution.py:436
  38.0 1.0 shard_map.115
  39.1 1.6 collective-permute-start.9
  40.6 1.3 collective-permute-start.7
  42.6 4.3 %collective-permute-done.9 = bf16[768,256]{1,0:T(8,128)(2,1)S(1)} collective-permute-done((bf16[768,256]{1,0:T(8,128)(2,1)S(1)}, bf16[768,256]{1,0:T(8,128)(2,1)S(1)}, u32[]{:S(2)}, u32[]{:S(2)}) %collective-permute-start.9) | collective-permute-done | bytes 393248 | tf_op jit(solution)/shard_map/ppermute | solution.py:436
  47.0 5.3 %collective-permute-done.7.refs_1_ = bf16[272,768]{1,0:T(8,128)(2,1)S(1)} collective-permute-done((bf16[272,768]{1,0:T(8,128)(2,1)S(1)}, bf16[272,768]{1,0:T(8,128)(2,1)S(1)}, u32[]{:S(2)}, u32[]{:S(2)}) %collective-permute-start.7) | collective-permute-done | bytes 417824 | tf_op jit(solution)/shard_map/ppermute | solution.py:537
  52.4 1.0 shard_map.114
  53.4 2.5 %collective-permute-start.8 = (bf16[768,256]{1,0:T(8,128)(2,1)S(1)}, bf16[768,256]{1,0:T(8,128)(2,1)S(1)}, u32[]{:S(2)}, u32[]{:S(2)}) collective-permute-start(bf16[768,256]{1,0:T(8,128)(2,1)S(1)} %get-tuple-element.76), channel_id=1, source_target_pairs={{0,2},{1,5},{2,0},{3,7},{4,6},{5,1},{6,4},{7,3},{8,10},{9,13},{10,... | collective-permute-start | bytes 1179656 | tf_op jit(solution)/shard_map/ppermute | solution.py:436
  55.9 1.5 collective-permute-start.4
  57.5 8.5 %collective-permute-done.8 = bf16[768,256]{1,0:T(8,128)(2,1)S(1)} collective-permute-done((bf16[768,256]{1,0:T(8,128)(2,1)S(1)}, bf16[768,256]{1,0:T(8,128)(2,1)S(1)}, u32[]{:S(2)}, u32[]{:S(2)}) %collective-permute-start.8) | collective-permute-done | bytes 393248 | tf_op jit(solution)/shard_map/ppermute | solution.py:436
  66.0 3.7 %collective-permute-done.4.refs_1_ = bf16[272,768]{1,0:T(8,128)(2,1)S(1)} collective-permute-done((bf16[272,768]{1,0:T(8,128)(2,1)S(1)}, bf16[272,768]{1,0:T(8,128)(2,1)S(1)}, u32[]{:S(2)}, u32[]{:S(2)}) %collective-permute-start.4) | collective-permute-done | bytes 417824 | tf_op jit(solution)/shard_map/ppermute | solution.py:537
  71.0 1.0 copy-done.13
  72.0 1.0 copy-done.15
  73.0 1.0 shard_map.113
  75.9 1.1 copy-done.11
  77.8 8.9 %shard_map.116 = (f32[2,576,256]{2,1,0:T(8,128)S(1)}, f32[2,576,256]{2,1,0:T(8,128)S(1)}, f32[2,2,256]{2,1,0:T(2,128)S(1)}) custom-call(s32[4]{0:T(128)S(1)} %get-tuple-element.142.plan_ref, bf16[2,768,256]{2,1,0:T(8,128)(2,1)S(1)} %pad_maximum_fusion.1.refs_0_, bf16[2,768,256]{2,1,0:T(8,128)(2,1)} %collective-permute-done.13.refs_1_, ...), custom_call_target="tpu_custom_call" | custom-call | flops 3623878656 | bytes 14155776 | tf_op jit(solution)/shard_map/pallas_call | solution.py:348
  86.7 1.0 copy-done.8
  89.2 1.7 collective-permute-start.15
  92.0 9.7 %shard_map.117.hidden_ref = bf16[2,256,576]{2,1,0:T(8,128)(2,1)S(1)} custom-call(s32[4]{0:T(128)S(1)} %add_add_fusion.plan_ref, bf16[2,768,256]{2,1,0:T(8,128)(2,1)} %collective-permute-done.16.refs_0_, bf16[2,768,256]{2,1,0:T(8,128)(2,1)} %collective-permute-done.17.refs_1_, bf16[2,768,256]{2,1,0:T(8,128)(2,1)S(1)} %collective-permute-done.12.refs_2_, ...), custom_call_target="tpu_custom_call" | custom-call | flops 3623878656 | bytes 14155776 | tf_op jit(solution)/shard_map/pallas_call | solution.py:348
  101.7 7.2 %shard_map.118 = (bf16[4,256,768]{2,1,0:T(8,128)(2,1)S(1)}, bf16[4,256,768]{2,1,0:T(8,128)(2,1)S(1)}) custom-call(s32[4]{0:T(128)S(1)} %get-tuple-element.143.plan_ref, bf16[2,256,576]{2,1,0:T(8,128)(2,1)S(1)} %shard_map.117.hidden_ref, bf16[2,576,6144]{2,1,0:T(8,128)(2,1)} %down_ref.5), custom_call_target="tpu_custom_call" | custom-call | flops 1811939328 | bytes 7077888 | tf_op jit(solution)/shard_map/pallas_call | solution.py:407
  110.1 7.2 %shard_map.119 = (bf16[4,256,768]{2,1,0:T(8,128)(2,1)S(1)}, bf16[4,256,768]{2,1,0:T(8,128)(2,1)S(1)}) custom-call(s32[4]{0:T(128)S(1)} %pad_add_fusion.3.plan_ref, bf16[2,256,576]{2,1,0:T(8,128)(2,1)S(1)} %shard_map.117.hidden_ref, bf16[2,576,6144]{2,1,0:T(8,128)(2,1)} %down_ref.5), custom_call_target="tpu_custom_call" | custom-call | flops 1811939328 | bytes 7077888 | tf_op jit(solution)/shard_map/pallas_call | solution.py:407
  117.5 1.8 collective-permute-start.24
  119.8 8.9 %shard_map.120 = (f32[2,576,256]{2,1,0:T(8,128)S(1)}, f32[2,576,256]{2,1,0:T(8,128)S(1)}, f32[2,2,256]{2,1,0:T(2,128)S(1)}) custom-call(s32[4]{0:T(128)S(1)} %get-tuple-element.142.plan_ref, bf16[2,768,256]{2,1,0:T(8,128)(2,1)} %pad_maximum_fusion.refs_0_, bf16[2,768,256]{2,1,0:T(8,128)(2,1)S(1)} %collective-permute-done.22.refs_1_, ...), custom_call_target="tpu_custom_call" | custom-call | flops 3623878656 | bytes 14155776 | tf_op jit(solution)/shard_map/pallas_call | solution.py:348
  128.7 1.1 add_convert_fusion.2
  130.0 1.5 collective-permute-start.27
  131.5 1.7 collective-permute-start.26
  133.2 9.3 %shard_map.121.hidden_ref = bf16[2,256,576]{2,1,0:T(8,128)(2,1)S(1)} custom-call(s32[4]{0:T(128)S(1)} %add_add_fusion.plan_ref, bf16[2,768,256]{2,1,0:T(8,128)(2,1)} %collective-permute-done.15.refs_0_, bf16[2,768,256]{2,1,0:T(8,128)(2,1)S(1)} %collective-permute-done.20.refs_1_, bf16[2,768,256]{2,1,0:T(8,128)(2,1)} %collective-permute-done.11.refs_2_, ...), custom_call_target="tpu_custom_call" | custom-call | flops 3623878656 | bytes 14155776 | tf_op jit(solution)/shard_map/pallas_call | solution.py:348
  142.6 1.0 collective-permute-done.26
  144.0 1.4 collective-permute-start.28
  145.5 1.0 collective-permute-done.27.refs_2_
  146.6 1.1 copy-done.3
  147.7 12.7 %shard_map.123 = (bf16[4,256,768]{2,1,0:T(8,128)(2,1)S(1)}, bf16[4,256,768]{2,1,0:T(8,128)(2,1)S(1)}, bf16[4,256,768]{2,1,0:T(8,128)(2,1)S(1)}, bf16[4,256,768]{2,1,0:T(8,128)(2,1)S(1)}) custom-call(s32[8]{0:T(128)S(1)} %concatenate.8.plan_ref, bf16[2,256,576]{2,1,0:T(8,128)(2,1)S(1)} %copy-done.3, bf16[2,576,6144]{2,1,0:T(8,128)(2,1)} %down_ref.5), custom_call_target="tpu_custom_call" | custom-call | flops 3623878656 | bytes 14155776 | tf_op jit(solution)/shard_map/pallas_call | solution.py:407
  161.0 2.9 %collective-permute-done.30.refs_1_ = bf16[4,256,768]{2,1,0:T(8,128)(2,1)S(1)} collective-permute-done((bf16[4,256,768]{2,1,0:T(8,128)(2,1)S(1)}, bf16[4,256,768]{2,1,0:T(8,128)(2,1)S(1)}, u32[]{:S(2)}, u32[]{:S(2)}) %collective-permute-start.30) | collective-permute-done | bytes 1572896 | tf_op jit(solution)/shard_map/ppermute | solution.py:436
  164.1 1.1 collective-permute-start.31
  165.1 5.7 %collective-permute-start.33 = (bf16[256,768]{1,0:T(8,128)(2,1)S(1)}, bf16[256,768]{1,0:T(8,128)(2,1)S(1)}, u32[]{:S(2)}, u32[]{:S(2)}) collective-permute-start(bf16[256,768]{1,0:T(8,128)(2,1)S(1)} %shard_map.122), channel_id=1, source_target_pairs={{0,16},{24,8},{1,17},{25,9},{2,18},{26,10},{3,19},{27,11},{4,20},{... | collective-permute-start | bytes 1179656 | tf_op jit(solution)/shard_map/ppermute | solution.py:614
  170.9 1.1 fusion.1
  172.0 1.3 collective-permute-start.34
  173.5 4.6 %collective-permute-done.31.refs_2_ = bf16[2,256,768]{2,1,0:T(8,128)(2,1)S(1)} collective-permute-done((bf16[2,256,768]{2,1,0:T(8,128)(2,1)S(1)}, bf16[2,256,768]{2,1,0:T(8,128)(2,1)S(1)}, u32[]{:S(2)}, u32[]{:S(2)}) %collective-permute-start.31) | collective-permute-done | bytes 786464 | tf_op jit(solution)/shard_map/ppermute | solution.py:436
  178.9 2.7 %collective-permute-done.34 = bf16[256,768]{1,0:T(8,128)(2,1)S(1)} collective-permute-done((bf16[256,768]{1,0:T(8,128)(2,1)S(1)}, bf16[256,768]{1,0:T(8,128)(2,1)S(1)}, u32[]{:S(2)}, u32[]{:S(2)}) %collective-permute-start.34) | collective-permute-done | bytes 393248 | tf_op jit(solution)/shard_map/ppermute | solution.py:436
  181.8 1.7 collective-permute-start.35
  183.5 1.4 shard_map.126
  185.0 3.2 %collective-permute-start.37 = (bf16[256,768]{1,0:T(8,128)(2,1)S(1)}, bf16[256,768]{1,0:T(8,128)(2,1)S(1)}, u32[]{:S(2)}, u32[]{:S(2)}) collective-permute-start(bf16[256,768]{1,0:T(8,128)(2,1)S(1)} %shard_map.126), channel_id=1, source_target_pairs={{0,8},{8,0},{16,24},{24,16},{1,9},{9,1},{17,25},{25,17},{2,10},{10... | collective-permute-start | bytes 1179656 | tf_op jit(solution)/shard_map/ppermute | solution.py:436
  188.1 4.3 %collective-permute-done.35 = bf16[256,768]{1,0:T(8,128)(2,1)S(1)} collective-permute-done((bf16[256,768]{1,0:T(8,128)(2,1)S(1)}, bf16[256,768]{1,0:T(8,128)(2,1)S(1)}, u32[]{:S(2)}, u32[]{:S(2)}) %collective-permute-start.35) | collective-permute-done | bytes 393248 | tf_op jit(solution)/shard_map/ppermute | solution.py:436
  192.9 1.3 collective-permute-done.32.refs_2_
  195.1 1.0 collective-permute-done.37
  196.1 3.3 %collective-permute-start.39 = (bf16[256,768]{1,0:T(8,128)(2,1)S(1)}, bf16[256,768]{1,0:T(8,128)(2,1)S(1)}, u32[]{:S(2)}, u32[]{:S(2)}) collective-permute-start(bf16[256,768]{1,0:T(8,128)(2,1)S(1)} %shard_map.124), channel_id=1, source_target_pairs={{0,24},{24,0},{1,25},{25,1},{2,26},{26,2},{3,27},{27,3},{4,28},{28... | collective-permute-start | bytes 1179656 | tf_op jit(solution)/shard_map/ppermute | solution.py:628
  199.5 1.3 collective-permute-start.38
  200.8 1.5 collective-permute-done.36
  202.7 6.3 %collective-permute-done.39 = bf16[256,768]{1,0:T(8,128)(2,1)S(1)} collective-permute-done((bf16[256,768]{1,0:T(8,128)(2,1)S(1)}, bf16[256,768]{1,0:T(8,128)(2,1)S(1)}, u32[]{:S(2)}, u32[]{:S(2)}) %collective-permute-start.39) | collective-permute-done | bytes 393248 | tf_op jit(solution)/shard_map/ppermute | solution.py:628
  209.0 8.3 %collective-permute-done.38 = bf16[256,768]{1,0:T(8,128)(2,1)S(1)} collective-permute-done((bf16[256,768]{1,0:T(8,128)(2,1)S(1)}, bf16[256,768]{1,0:T(8,128)(2,1)S(1)}, u32[]{:S(2)}, u32[]{:S(2)}) %collective-permute-start.38) | collective-permute-done | bytes 393248 | tf_op jit(solution)/shard_map/ppermute | solution.py:627
  217.4 2.1 add_convert_fusion.8
  (123 shorter events, 18.0 us)
Async XLA Ops:
  2.2 10.8 %collective-permute-start = (bf16[784,128]{1,0:T(8,128)(2,1)S(1)}, bf16[784,128]{1,0:T(8,128)(2,1)S(1)}, u32[]{:S(2)}, u32[]{:S(2)}) collective-permute-start(bf16[784,128]{1,0:T(8,128)(2,1)S(1)} %get-tuple-element.73), channel_id=1, source_target_pairs={{0,8},{8,16},{16,24},{1,9},{9,17},{17,25},{2,10},{10,18},{18,26},{... | collective-permute-start | bytes 602120 | tf_op jit(solution)/shard_map/ppermute | solution.py:30
  7.9 1.0 copy-start.4
  8.9 1.0 copy-start.6
  9.9 1.0 copy-start.7
  13.0 8.9 %copy-start.5 = (bf16[256,768]{1,0:T(8,128)(2,1)S(1)}, bf16[256,768]{1,0:T(8,128)(2,1)}, u32[]{:S(2)}) copy-start(bf16[256,768]{1,0:T(8,128)(2,1)} %query_ref.3) | copy-start | bytes 1179652
  13.0 8.9 %copy-start.19 = (bf16[256,768]{1,0:T(8,128)(2,1)S(1)}, bf16[256,768]{1,0:T(8,128)(2,1)}, u32[]{:S(2)}) copy-start(bf16[256,768]{1,0:T(8,128)(2,1)} %residual_ref.1) | copy-start | bytes 1179652
  13.0 8.9 %copy-start.29 = (s32[256,2]{0,1:T(2,128)S(1)}, s32[256,2]{0,1:T(2,128)}, u32[]{:S(2)}) copy-start(s32[256,2]{0,1:T(2,128)} %param.17) | copy-start | bytes 6148
  13.3 8.5 %collective-permute-start.1 = (bf16[784,128]{1,0:T(8,128)(2,1)S(1)}, bf16[784,128]{1,0:T(8,128)(2,1)S(1)}, u32[]{:S(2)}, u32[]{:S(2)}) collective-permute-start(bf16[784,128]{1,0:T(8,128)(2,1)S(1)} %concatenate.7), channel_id=1, source_target_pairs={{0,16},{8,24},{1,17},{9,25},{2,18},{10,26},{3,19},{11,27},{4,20},{... | collective-permute-start | bytes 602120 | tf_op jit(solution)/shard_map/ppermute | solution.py:30
  22.7 24.3 %copy-start = (bf16[272,768]{1,0:T(8,128)(2,1)}, bf16[272,768]{1,0:T(8,128)(2,1)S(1)}, u32[]{:S(2)}) copy-start(bf16[272,768]{1,0:T(8,128)(2,1)S(1)} %shard_map.111.refs_0_) | copy-start | bytes 1253380
  23.8 10.3 %copy-start.20 = (bf16[256,256]{1,0:T(8,128)(2,1)}, bf16[256,256]{1,0:T(8,128)(2,1)S(1)}, u32[]{:S(2)}) copy-start(bf16[256,256]{1,0:T(8,128)(2,1)S(1)} %get-tuple-element.74.place_ref) | copy-start | bytes 393220
  23.8 7.8 %collective-permute-start.10 = (bf16[768,256]{1,0:T(8,128)(2,1)S(1)}, bf16[768,256]{1,0:T(8,128)(2,1)S(1)}, u32[]{:S(2)}, u32[]{:S(2)}) collective-permute-start(bf16[768,256]{1,0:T(8,128)(2,1)S(1)} %get-tuple-element.78), channel_id=1, source_target_pairs={{0,2},{1,5},{2,0},{3,7},{4,6},{5,1},{6,4},{7,3},{8,10},{9,13},{10,... | collective-permute-start | bytes 1179656 | tf_op jit(solution)/shard_map/ppermute | solution.py:436
  25.3 12.7 %collective-permute-start.2 = (bf16[272,768]{1,0:T(8,128)(2,1)S(1)}, bf16[272,768]{1,0:T(8,128)(2,1)S(1)}, u32[]{:S(2)}, u32[]{:S(2)}) collective-permute-start(bf16[272,768]{1,0:T(8,128)(2,1)S(1)} %shard_map.111.refs_0_), channel_id=1, source_target_pairs={{0,8},{8,0},{16,24},{24,16},{1,9},{9,1},{17,25},{25,17},{2,10},{10... | collective-permute-start | bytes 1253384 | tf_op jit(solution)/shard_map/ppermute | solution.py:436
  29.8 10.8 %collective-permute-start.6 = (bf16[272,768]{1,0:T(8,128)(2,1)S(1)}, bf16[272,768]{1,0:T(8,128)(2,1)S(1)}, u32[]{:S(2)}, u32[]{:S(2)}) collective-permute-start(bf16[272,768]{1,0:T(8,128)(2,1)S(1)} %shard_map.111.refs_0_), channel_id=1, source_target_pairs={{8,16},{16,8},{9,17},{17,9},{10,18},{18,10},{11,19},{19,11},{12,20... | collective-permute-start | bytes 1253384 | tf_op jit(solution)/shard_map/ppermute | solution.py:534
  32.6 19.7 %collective-permute-start.11 = (bf16[2,768,256]{2,1,0:T(8,128)(2,1)}, bf16[2,768,256]{2,1,0:T(8,128)(2,1)}, u32[]{:S(2)}, u32[]{:S(2)}) collective-permute-start(bf16[2,768,256]{2,1,0:T(8,128)(2,1)} %pad_maximum_fusion.3.refs_2_), channel_id=1, source_target_pairs={{0,4},{1,3},{2,6},{3,1},{4,0},{5,7},{6,2},{7,5},{8,12},{9,11},{10,... | collective-permute-start | bytes 2359304 | tf_op jit(solution)/shard_map/ppermute | solution.py:436
  39.1 27.0 %copy-start.22 = (bf16[256,256]{1,0:T(8,128)(2,1)}, bf16[256,256]{1,0:T(8,128)(2,1)S(1)}, u32[]{:S(2)}) copy-start(bf16[256,256]{1,0:T(8,128)(2,1)S(1)} %get-tuple-element.137.place_ref) | copy-start | bytes 393220
  39.1 7.8 %collective-permute-start.9 = (bf16[768,256]{1,0:T(8,128)(2,1)S(1)}, bf16[768,256]{1,0:T(8,128)(2,1)S(1)}, u32[]{:S(2)}, u32[]{:S(2)}) collective-permute-start(bf16[768,256]{1,0:T(8,128)(2,1)S(1)} %get-tuple-element.77), channel_id=1, source_target_pairs={{0,2},{1,5},{2,0},{3,7},{4,6},{5,1},{6,4},{7,3},{8,10},{9,13},{10,... | collective-permute-start | bytes 1179656 | tf_op jit(solution)/shard_map/ppermute | solution.py:436
  40.6 11.6 %collective-permute-start.7 = (bf16[272,768]{1,0:T(8,128)(2,1)S(1)}, bf16[272,768]{1,0:T(8,128)(2,1)S(1)}, u32[]{:S(2)}, u32[]{:S(2)}) collective-permute-start(bf16[272,768]{1,0:T(8,128)(2,1)S(1)} %collective-permute-done.6.refs_0_), channel_id=1, source_target_pairs={{8,0},{16,24},{9,1},{17,25},{10,2},{18,26},{11,3},{19,27},{12,4},{... | collective-permute-start | bytes 1253384 | tf_op jit(solution)/shard_map/ppermute | solution.py:537
  41.9 10.4 %collective-permute-start.3 = (bf16[272,768]{1,0:T(8,128)(2,1)S(1)}, bf16[272,768]{1,0:T(8,128)(2,1)S(1)}, u32[]{:S(2)}, u32[]{:S(2)}) collective-permute-start(bf16[272,768]{1,0:T(8,128)(2,1)S(1)} %collective-permute-done.2.refs_0_), channel_id=1, source_target_pairs={{8,16},{16,8},{9,17},{17,9},{10,18},{18,10},{11,19},{19,11},{12,20... | collective-permute-start | bytes 1253384 | tf_op jit(solution)/shard_map/ppermute | solution.py:534
  52.3 18.2 %copy-start.12 = (bf16[272,768]{1,0:T(8,128)(2,1)}, bf16[272,768]{1,0:T(8,128)(2,1)S(1)}, u32[]{:S(2)}) copy-start(bf16[272,768]{1,0:T(8,128)(2,1)S(1)} %collective-permute-done.3.refs_0_) | copy-start | bytes 1253380
  52.3 18.2 %collective-permute-start.12 = (bf16[2,768,256]{2,1,0:T(8,128)(2,1)S(1)}, bf16[2,768,256]{2,1,0:T(8,128)(2,1)S(1)}, u32[]{:S(2)}, u32[]{:S(2)}) collective-permute-start(bf16[2,768,256]{2,1,0:T(8,128)(2,1)S(1)} %pad_maximum_fusion.2.refs_2_), channel_id=1, source_target_pairs={{0,4},{1,3},{2,6},{3,1},{4,0},{5,7},{6,2},{7,5},{8,12},{9,11},{10,... | collective-permute-start | bytes 2359304 | tf_op jit(solution)/shard_map/ppermute | solution.py:436
  53.4 17.1 %copy-start.26 = (bf16[256,256]{1,0:T(8,128)(2,1)}, bf16[256,256]{1,0:T(8,128)(2,1)S(1)}, u32[]{:S(2)}) copy-start(bf16[256,256]{1,0:T(8,128)(2,1)S(1)} %get-tuple-element.122.place_ref) | copy-start | bytes 393220
  53.4 12.5 %collective-permute-start.8 = (bf16[768,256]{1,0:T(8,128)(2,1)S(1)}, bf16[768,256]{1,0:T(8,128)(2,1)S(1)}, u32[]{:S(2)}, u32[]{:S(2)}) collective-permute-start(bf16[768,256]{1,0:T(8,128)(2,1)S(1)} %get-tuple-element.76), channel_id=1, source_target_pairs={{0,2},{1,5},{2,0},{3,7},{4,6},{5,1},{6,4},{7,3},{8,10},{9,13},{10,... | collective-permute-start | bytes 1179656 | tf_op jit(solution)/shard_map/ppermute | solution.py:436
  55.9 13.8 %collective-permute-start.4 = (bf16[272,768]{1,0:T(8,128)(2,1)S(1)}, bf16[272,768]{1,0:T(8,128)(2,1)S(1)}, u32[]{:S(2)}, u32[]{:S(2)}) collective-permute-start(bf16[272,768]{1,0:T(8,128)(2,1)S(1)} %collective-permute-done.3.refs_0_), channel_id=1, source_target_pairs={{8,0},{16,24},{9,1},{17,25},{10,2},{18,26},{11,3},{19,27},{12,4},{... | collective-permute-start | bytes 1253384 | tf_op jit(solution)/shard_map/ppermute | solution.py:537
  57.4 17.6 %collective-permute-start.14 = (bf16[2,768,256]{2,1,0:T(8,128)(2,1)S(1)}, bf16[2,768,256]{2,1,0:T(8,128)(2,1)S(1)}, u32[]{:S(2)}, u32[]{:S(2)}) collective-permute-start(bf16[2,768,256]{2,1,0:T(8,128)(2,1)S(1)} %pad_maximum_fusion.2.refs_2_), channel_id=1, source_target_pairs={{0,1},{1,0},{2,3},{3,2},{4,5},{5,4},{6,7},{7,6},{8,9},{9,8},{10,11... | collective-permute-start | bytes 2359304 | tf_op jit(solution)/shard_map/ppermute | solution.py:436
  70.5 5.4 %collective-permute-start.13 = (bf16[2,768,256]{2,1,0:T(8,128)(2,1)S(1)}, bf16[2,768,256]{2,1,0:T(8,128)(2,1)}, u32[]{:S(2)}, u32[]{:S(2)}) collective-permute-start(bf16[2,768,256]{2,1,0:T(8,128)(2,1)S(1)} %pad_maximum_fusion.1.refs_0_), channel_id=1, source_target_pairs={{0,1},{1,0},{2,3},{3,2},{4,5},{5,4},{6,7},{7,6},{8,9},{9,8},{10,11... | collective-permute-start | bytes 2359304 | tf_op jit(solution)/shard_map/ppermute | solution.py:436
  70.5 17.2 %collective-permute-start.16 = (bf16[2,768,256]{2,1,0:T(8,128)(2,1)S(1)}, bf16[2,768,256]{2,1,0:T(8,128)(2,1)}, u32[]{:S(2)}, u32[]{:S(2)}) collective-permute-start(bf16[2,768,256]{2,1,0:T(8,128)(2,1)S(1)} %pad_maximum_fusion.1.refs_0_), channel_id=1, source_target_pairs={{0,4},{1,3},{2,6},{3,1},{4,0},{5,7},{6,2},{7,5},{8,12},{9,11},{10,... | collective-permute-start | bytes 2359304 | tf_op jit(solution)/shard_map/ppermute | solution.py:436
  71.0 1.0 copy-start.13
  72.0 1.0 copy-start.15
  74.7 13.5 %collective-permute-start.5 = (bf16[768,256]{1,0:T(8,128)(2,1)S(1)}, bf16[768,256]{1,0:T(8,128)(2,1)S(1)}, u32[]{:S(2)}, u32[]{:S(2)}) collective-permute-start(bf16[768,256]{1,0:T(8,128)(2,1)S(1)} %get-tuple-element.75), channel_id=1, source_target_pairs={{0,2},{1,5},{2,0},{3,7},{4,6},{5,1},{6,4},{7,3},{8,10},{9,13},{10,... | collective-permute-start | bytes 1179656 | tf_op jit(solution)/shard_map/ppermute | solution.py:436
  75.9 1.1 copy-start.11
  86.7 1.0 copy-start.8
  87.7 3.5 %copy-start.9 = (f32[2,576,256]{2,1,0:T(8,128)S(1)}, f32[2,576,256]{2,1,0:T(8,128)}, u32[]{:S(2)}) copy-start(f32[2,576,256]{2,1,0:T(8,128)} %copy-done.8) | copy-start | bytes 3538948
  87.7 3.3 %collective-permute-start.17 = (bf16[2,768,256]{2,1,0:T(8,128)(2,1)}, bf16[2,768,256]{2,1,0:T(8,128)(2,1)}, u32[]{:S(2)}, u32[]{:S(2)}) collective-permute-start(bf16[2,768,256]{2,1,0:T(8,128)(2,1)} %collective-permute-done.16.refs_0_), channel_id=1, source_target_pairs={{0,1},{1,0},{2,3},{3,2},{4,5},{5,4},{6,7},{7,6},{8,9},{9,8},{10,11... | collective-permute-start | bytes 2359304 | tf_op jit(solution)/shard_map/ppermute | solution.py:436
  87.7 3.5 %collective-permute-start.18 = (bf16[2,768,256]{2,1,0:T(8,128)(2,1)S(1)}, bf16[2,768,256]{2,1,0:T(8,128)(2,1)}, u32[]{:S(2)}, u32[]{:S(2)}) collective-permute-start(bf16[2,768,256]{2,1,0:T(8,128)(2,1)S(1)} %collective-permute-done.12.refs_2_), channel_id=1, source_target_pairs={{0,1},{1,0},{2,3},{3,2},{4,5},{5,4},{6,7},{7,6},{8,9},{9,8},{10,11... | collective-permute-start | bytes 2359304 | tf_op jit(solution)/shard_map/ppermute | solution.py:436
  89.2 12.5 %collective-permute-start.15 = (bf16[2,768,256]{2,1,0:T(8,128)(2,1)}, bf16[2,768,256]{2,1,0:T(8,128)(2,1)}, u32[]{:S(2)}, u32[]{:S(2)}) collective-permute-start(bf16[2,768,256]{2,1,0:T(8,128)(2,1)} %pad_maximum_fusion.refs_0_), channel_id=1, source_target_pairs={{0,4},{1,3},{2,6},{3,1},{4,0},{5,7},{6,2},{7,5},{8,12},{9,11},{10,... | collective-permute-start | bytes 2359304 | tf_op jit(solution)/shard_map/ppermute | solution.py:436
  108.9 8.4 %collective-permute-start.19 = (bf16[4,256,768]{2,1,0:T(8,128)(2,1)S(1)}, bf16[4,256,768]{2,1,0:T(8,128)(2,1)S(1)}, u32[]{:S(2)}, u32[]{:S(2)}) collective-permute-start(bf16[4,256,768]{2,1,0:T(8,128)(2,1)S(1)} %get-tuple-element.100), channel_id=1, source_target_pairs={{0,1},{1,0},{2,3},{3,2},{4,5},{5,4},{6,7},{7,6},{8,9},{9,8},{10,11... | collective-permute-start | bytes 4718600 | tf_op jit(solution)/shard_map/ppermute | solution.py:436
  109.1 19.6 %collective-permute-start.25 = (bf16[4,256,768]{2,1,0:T(8,128)(2,1)S(1)}, bf16[4,256,768]{2,1,0:T(8,128)(2,1)S(1)}, u32[]{:S(2)}, u32[]{:S(2)}) collective-permute-start(bf16[4,256,768]{2,1,0:T(8,128)(2,1)S(1)} %get-tuple-element.101), channel_id=1, source_target_pairs={{0,1},{1,0},{2,3},{3,2},{4,5},{5,4},{6,7},{7,6},{8,9},{9,8},{10,11... | collective-permute-start | bytes 4718600 | tf_op jit(solution)/shard_map/ppermute | solution.py:436
  109.5 9.8 %collective-permute-start.23 = (bf16[2,768,256]{2,1,0:T(8,128)(2,1)}, bf16[2,768,256]{2,1,0:T(8,128)(2,1)S(1)}, u32[]{:S(2)}, u32[]{:S(2)}) collective-permute-start(bf16[2,768,256]{2,1,0:T(8,128)(2,1)} %pad_maximum_fusion.3.refs_2_), channel_id=1, source_target_pairs={{0,1},{1,0},{2,3},{3,2},{4,5},{5,4},{6,7},{7,6},{8,9},{9,8},{10,11... | collective-permute-start | bytes 2359304 | tf_op jit(solution)/shard_map/ppermute | solution.py:436
  109.6 9.7 %collective-permute-start.22 = (bf16[2,768,256]{2,1,0:T(8,128)(2,1)}, bf16[2,768,256]{2,1,0:T(8,128)(2,1)S(1)}, u32[]{:S(2)}, u32[]{:S(2)}) collective-permute-start(bf16[2,768,256]{2,1,0:T(8,128)(2,1)} %pad_maximum_fusion.refs_0_), channel_id=1, source_target_pairs={{0,1},{1,0},{2,3},{3,2},{4,5},{5,4},{6,7},{7,6},{8,9},{9,8},{10,11... | collective-permute-start | bytes 2359304 | tf_op jit(solution)/shard_map/ppermute | solution.py:436
  117.3 2.5 %copy-start.18 = (bf16[6144,2]{0,1:T(2,128)(2,1)S(1)}, bf16[6144,2]{0,1:T(2,128)(2,1)}, u32[]{:S(2)}) copy-start(bf16[6144,2]{0,1:T(2,128)(2,1)} %param.18) | copy-start | bytes 73732
  117.5 12.3 %collective-permute-start.24 = (bf16[2,256,768]{2,1,0:T(8,128)(2,1)S(1)}, bf16[2,256,768]{2,1,0:T(8,128)(2,1)S(1)}, u32[]{:S(2)}, u32[]{:S(2)}) collective-permute-start(bf16[2,256,768]{2,1,0:T(8,128)(2,1)S(1)} %add_convert_fusion.3), channel_id=1, source_target_pairs={{0,4},{1,3},{2,6},{3,1},{4,0},{5,7},{6,2},{7,5},{8,12},{9,11},{10,... | collective-permute-start | bytes 2359304 | tf_op jit(solution)/shard_map/ppermute | solution.py:436
  119.3 14.0 %collective-permute-start.20 = (bf16[2,768,256]{2,1,0:T(8,128)(2,1)}, bf16[2,768,256]{2,1,0:T(8,128)(2,1)S(1)}, u32[]{:S(2)}, u32[]{:S(2)}) collective-permute-start(bf16[2,768,256]{2,1,0:T(8,128)(2,1)} %collective-permute-done.15.refs_0_), channel_id=1, source_target_pairs={{0,1},{1,0},{2,3},{3,2},{4,5},{5,4},{6,7},{7,6},{8,9},{9,8},{10,11... | collective-permute-start | bytes 2359304 | tf_op jit(solution)/shard_map/ppermute | solution.py:436
  119.3 13.9 %collective-permute-start.21 = (bf16[2,768,256]{2,1,0:T(8,128)(2,1)}, bf16[2,768,256]{2,1,0:T(8,128)(2,1)S(1)}, u32[]{:S(2)}, u32[]{:S(2)}) collective-permute-start(bf16[2,768,256]{2,1,0:T(8,128)(2,1)} %collective-permute-done.11.refs_2_), channel_id=1, source_target_pairs={{0,1},{1,0},{2,3},{3,2},{4,5},{5,4},{6,7},{7,6},{8,9},{9,8},{10,11... | collective-permute-start | bytes 2359304 | tf_op jit(solution)/shard_map/ppermute | solution.py:436
  130.0 13.6 %copy-start.27 = (bf16[256,256]{1,0:T(8,128)(2,1)S(1)}, bf16[256,256]{1,0:T(8,128)(2,1)}, u32[]{:S(2)}) copy-start(bf16[256,256]{1,0:T(8,128)(2,1)} %copy-done.26) | copy-start | bytes 393220
  130.0 16.6 %collective-permute-start.27 = (bf16[2,256,768]{2,1,0:T(8,128)(2,1)}, bf16[2,256,768]{2,1,0:T(8,128)(2,1)}, u32[]{:S(2)}, u32[]{:S(2)}) collective-permute-start(bf16[2,256,768]{2,1,0:T(8,128)(2,1)} %add_convert_fusion.2), channel_id=1, source_target_pairs={{0,4},{1,3},{2,6},{3,1},{4,0},{5,7},{6,2},{7,5},{8,12},{9,11},{10,... | collective-permute-start | bytes 2359304 | tf_op jit(solution)/shard_map/ppermute | solution.py:436
  131.5 12.1 %collective-permute-start.26 = (bf16[256,768]{1,0:T(8,128)(2,1)S(1)}, bf16[256,768]{1,0:T(8,128)(2,1)S(1)}, u32[]{:S(2)}, u32[]{:S(2)}) collective-permute-start(bf16[256,768]{1,0:T(8,128)(2,1)S(1)} %fusion), channel_id=1, source_target_pairs={{0,2},{1,5},{2,0},{3,7},{4,6},{5,1},{6,4},{7,3},{8,10},{9,13},{10,... | collective-permute-start | bytes 1179656 | tf_op jit(solution)/shard_map/ppermute | solution.py:436
  142.6 1.4 copy-start.2
  144.0 16.4 %collective-permute-start.28 = (bf16[256,768]{1,0:T(8,128)(2,1)S(1)}, bf16[256,768]{1,0:T(8,128)(2,1)}, u32[]{:S(2)}, u32[]{:S(2)}) collective-permute-start(bf16[256,768]{1,0:T(8,128)(2,1)S(1)} %shard_map.122), channel_id=1, source_target_pairs={{8,16},{16,8},{9,17},{17,9},{10,18},{18,10},{11,19},{19,11},{12,20... | collective-permute-start | bytes 1179656 | tf_op jit(solution)/shard_map/ppermute | solution.py:608
  146.6 1.1 copy-start.3
  160.4 3.5 %collective-permute-start.30 = (bf16[4,256,768]{2,1,0:T(8,128)(2,1)S(1)}, bf16[4,256,768]{2,1,0:T(8,128)(2,1)S(1)}, u32[]{:S(2)}, u32[]{:S(2)}) collective-permute-start(bf16[4,256,768]{2,1,0:T(8,128)(2,1)S(1)} %get-tuple-element.131), channel_id=1, source_target_pairs={{0,1},{1,0},{2,3},{3,2},{4,5},{5,4},{6,7},{7,6},{8,9},{9,8},{10,11... | collective-permute-start | bytes 4718600 | tf_op jit(solution)/shard_map/ppermute | solution.py:436
  160.5 12.8 %collective-permute-start.29 = (bf16[4,256,768]{2,1,0:T(8,128)(2,1)S(1)}, bf16[4,256,768]{2,1,0:T(8,128)(2,1)S(1)}, u32[]{:S(2)}, u32[]{:S(2)}) collective-permute-start(bf16[4,256,768]{2,1,0:T(8,128)(2,1)S(1)} %get-tuple-element.129), channel_id=1, source_target_pairs={{0,1},{1,0},{2,3},{3,2},{4,5},{5,4},{6,7},{7,6},{8,9},{9,8},{10,11... | collective-permute-start | bytes 4718600 | tf_op jit(solution)/shard_map/ppermute | solution.py:436
  164.1 14.0 %collective-permute-start.31 = (bf16[2,256,768]{2,1,0:T(8,128)(2,1)S(1)}, bf16[2,256,768]{2,1,0:T(8,128)(2,1)S(1)}, u32[]{:S(2)}, u32[]{:S(2)}) collective-permute-start(bf16[2,256,768]{2,1,0:T(8,128)(2,1)S(1)} %add_convert_fusion), channel_id=1, source_target_pairs={{0,4},{1,3},{2,6},{3,1},{4,0},{5,7},{6,2},{7,5},{8,12},{9,11},{10,... | collective-permute-start | bytes 2359304 | tf_op jit(solution)/shard_map/ppermute | solution.py:436
  165.1 13.8 %collective-permute-start.33 = (bf16[256,768]{1,0:T(8,128)(2,1)S(1)}, bf16[256,768]{1,0:T(8,128)(2,1)S(1)}, u32[]{:S(2)}, u32[]{:S(2)}) collective-permute-start(bf16[256,768]{1,0:T(8,128)(2,1)S(1)} %shard_map.122), channel_id=1, source_target_pairs={{0,16},{24,8},{1,17},{25,9},{2,18},{26,10},{3,19},{27,11},{4,20},{... | collective-permute-start | bytes 1179656 | tf_op jit(solution)/shard_map/ppermute | solution.py:614
  172.0 9.6 %collective-permute-start.34 = (bf16[256,768]{1,0:T(8,128)(2,1)S(1)}, bf16[256,768]{1,0:T(8,128)(2,1)S(1)}, u32[]{:S(2)}, u32[]{:S(2)}) collective-permute-start(bf16[256,768]{1,0:T(8,128)(2,1)S(1)} %fusion.1), channel_id=1, source_target_pairs={{0,2},{1,5},{2,0},{3,7},{4,6},{5,1},{6,4},{7,3},{8,10},{9,13},{10,... | collective-permute-start | bytes 1179656 | tf_op jit(solution)/shard_map/ppermute | solution.py:436
  173.3 10.2 %copy-start.23 = (bf16[256,256]{1,0:T(8,128)(2,1)S(1)}, bf16[256,256]{1,0:T(8,128)(2,1)}, u32[]{:S(2)}) copy-start(bf16[256,256]{1,0:T(8,128)(2,1)} %copy-done.22) | copy-start | bytes 393220
  178.0 16.2 %collective-permute-start.32 = (bf16[2,256,768]{2,1,0:T(8,128)(2,1)S(1)}, bf16[2,256,768]{2,1,0:T(8,128)(2,1)S(1)}, u32[]{:S(2)}, u32[]{:S(2)}) collective-permute-start(bf16[2,256,768]{2,1,0:T(8,128)(2,1)S(1)} %add_convert_fusion.1), channel_id=1, source_target_pairs={{0,4},{1,3},{2,6},{3,1},{4,0},{5,7},{6,2},{7,5},{8,12},{9,11},{10,... | collective-permute-start | bytes 2359304 | tf_op jit(solution)/shard_map/ppermute | solution.py:436
  181.8 10.7 %collective-permute-start.35 = (bf16[256,768]{1,0:T(8,128)(2,1)S(1)}, bf16[256,768]{1,0:T(8,128)(2,1)S(1)}, u32[]{:S(2)}, u32[]{:S(2)}) collective-permute-start(bf16[256,768]{1,0:T(8,128)(2,1)S(1)} %fusion.2), channel_id=1, source_target_pairs={{0,2},{1,5},{2,0},{3,7},{4,6},{5,1},{6,4},{7,3},{8,10},{9,13},{10,... | collective-permute-start | bytes 1179656 | tf_op jit(solution)/shard_map/ppermute | solution.py:436
  183.5 9.0 %copy-start.25 = (bf16[256,256]{1,0:T(8,128)(2,1)S(1)}, bf16[256,256]{1,0:T(8,128)(2,1)}, u32[]{:S(2)}) copy-start(bf16[256,256]{1,0:T(8,128)(2,1)} %copy-done.24) | copy-start | bytes 393220
  185.0 11.2 %collective-permute-start.37 = (bf16[256,768]{1,0:T(8,128)(2,1)S(1)}, bf16[256,768]{1,0:T(8,128)(2,1)S(1)}, u32[]{:S(2)}, u32[]{:S(2)}) collective-permute-start(bf16[256,768]{1,0:T(8,128)(2,1)S(1)} %shard_map.126), channel_id=1, source_target_pairs={{0,8},{8,0},{16,24},{24,16},{1,9},{9,1},{17,25},{25,17},{2,10},{10... | collective-permute-start | bytes 1179656 | tf_op jit(solution)/shard_map/ppermute | solution.py:436
  192.9 9.3 %copy-start.21 = (bf16[256,256]{1,0:T(8,128)(2,1)S(1)}, bf16[256,256]{1,0:T(8,128)(2,1)}, u32[]{:S(2)}) copy-start(bf16[256,256]{1,0:T(8,128)(2,1)} %copy-done.20) | copy-start | bytes 393220
  194.4 7.8 %collective-permute-start.36 = (bf16[256,768]{1,0:T(8,128)(2,1)S(1)}, bf16[256,768]{1,0:T(8,128)(2,1)S(1)}, u32[]{:S(2)}, u32[]{:S(2)}) collective-permute-start(bf16[256,768]{1,0:T(8,128)(2,1)S(1)} %fusion.3), channel_id=1, source_target_pairs={{0,2},{1,5},{2,0},{3,7},{4,6},{5,1},{6,4},{7,3},{8,10},{9,13},{10,... | collective-permute-start | bytes 1179656 | tf_op jit(solution)/shard_map/ppermute | solution.py:436
  196.1 12.9 %collective-permute-start.39 = (bf16[256,768]{1,0:T(8,128)(2,1)S(1)}, bf16[256,768]{1,0:T(8,128)(2,1)S(1)}, u32[]{:S(2)}, u32[]{:S(2)}) collective-permute-start(bf16[256,768]{1,0:T(8,128)(2,1)S(1)} %shard_map.124), channel_id=1, source_target_pairs={{0,24},{24,0},{1,25},{25,1},{2,26},{26,2},{3,27},{27,3},{4,28},{28... | collective-permute-start | bytes 1179656 | tf_op jit(solution)/shard_map/ppermute | solution.py:628
  199.5 17.9 %collective-permute-start.38 = (bf16[256,768]{1,0:T(8,128)(2,1)S(1)}, bf16[256,768]{1,0:T(8,128)(2,1)S(1)}, u32[]{:S(2)}, u32[]{:S(2)}) collective-permute-start(bf16[256,768]{1,0:T(8,128)(2,1)S(1)} %shard_map.124), channel_id=1, source_target_pairs={{8,24},{16,0},{9,25},{17,1},{10,26},{18,2},{11,27},{19,3},{12,28},... | collective-permute-start | bytes 1179656 | tf_op jit(solution)/shard_map/ppermute | solution.py:627
  202.3 15.1 %copy-start.1 = (bf16[272,768]{1,0:T(8,128)(2,1)S(1)}, bf16[272,768]{1,0:T(8,128)(2,1)}, u32[]{:S(2)}) copy-start(bf16[272,768]{1,0:T(8,128)(2,1)} %copy-done) | copy-start | bytes 1253380
  (6 other events, 4.5 us)

commit v17 on v14

--- a/solution.py
+++ b/solution.py
@@ -614,7 +614,7 @@
     neighbour_piece = neighbour.own_block([])
     neighbour_home = swapped(neighbour_piece, "seq", 1, 1)
     fourth.one_block([third_far_home, neighbour.got_one])
-    own.two_blocks(fourth.got_two)
+    own.two_blocks([])
     fourth_piece = fourth.own_block([])
     own.one_block(fourth_piece)
     fourth_piece, _ = tie((fourth_piece, [third_far_home, neighbour_home]))

time: 221 us -> 221 us (level)
  waiting for transfers between devices: 66.2 us -> 68.5 us
    ppermute x1, waiting for transfers between devices: 0.13 us -> 4.62 us  [paired_chunks(): lax.ppermute(tie((third_piece, third_home))[0], 'seq', [(0, 2), (3, 1)])]
    ppermute x30, starting transfers between devices: 30.5 us -> 27.3 us  [swapped(): return lax.ppermute(array, axis, pairs)]
    ppermute x30, waiting for transfers between devices: 38.5 us -> 36.1 us  [swapped(): return lax.ppermute(array, axis, pairs)]
  transfers between devices with their start and end apart: 40 -> 40, of which waited for: 20 -> 17; matrix products, arithmetic and copies ran while one was open for 3% -> 3% of each run, Pallas kernels for 29% -> 29%
where the time goes in v17:
time: 221 us; the launch traced here: 220 us
  Pallas kernels  75.1 us (34%)
  waiting for transfers between devices  68.5 us (31%)
  starting transfers between devices  53.8 us (24%)
  local copies, waits for them, and re-layouts  13.8 us (6%)
  other arithmetic  7.92 us (4%)
    pallas_call x4, Pallas kernels, gate_part(): pl.pallas_call(functools.partial(gate_kernel, counts, len(xs), last), gri...  36.8 us
    ppermute x30, waiting for transfers between devices, swapped(): return lax.ppermute(array, axis, pairs)  36.1 us
    ppermute x30, starting transfers between devices, swapped(): return lax.ppermute(array, axis, pairs)  27.3 us
    pallas_call x3, Pallas kernels, down_part(): pl.pallas_call(functools.partial(down_kernel, blocks, sections), grid_spe...  27.1 us
    unnamed x60, local copies, waits for them, and re-layouts  12.8 us
    ppermute x2, starting transfers between devices, shifted(): return lax.ppermute(array, axis, pairs)  9.43 us
    ppermute x2, waiting for transfers between devices, outward(): return lax.ppermute(part, 'seq', [(1, 0), (2, 3)])  8.98 us
    ppermute x1, waiting for transfers between devices, paired_chunks(): lax.ppermute(fourth_piece, 'seq', [(1, 3), (2, 0)])  8.33 us
  transfers between devices with their start and end apart: 40, of which 17 were waited for; matrix products, arithmetic and copies ran while one was open for 3% of the time, Pallas kernels for 29%

profile of v17, /device:TPU:0, one launch (start us, length us, event | category | flops | bytes accessed | tf_op | source)
XLA Modules:
  0.0 219.8 jit_solution(11706820587318434875)
XLA Ops:
  0.0 2.1 shard_map.109
  2.2 4.9 %collective-permute-start = (bf16[784,128]{1,0:T(8,128)(2,1)S(1)}, bf16[784,128]{1,0:T(8,128)(2,1)S(1)}, u32[]{:S(2)}, u32[]{:S(2)}) collective-permute-start(bf16[784,128]{1,0:T(8,128)(2,1)S(1)} %get-tuple-element.72), channel_id=1, source_target_pairs={{0,8},{8,16},{16,24},{1,9},{9,17},{17,25},{2,10},{10,18},{18,26},{... | collective-permute-start | bytes 602120 | tf_op jit(solution)/shard_map/ppermute | solution.py:30
  7.9 1.0 copy-done.4
  8.9 1.0 copy-done.6
  9.9 1.0 copy-done.7
  11.6 1.4 shard_map.110.intra_ref
  13.3 4.5 %collective-permute-start.1 = (bf16[784,128]{1,0:T(8,128)(2,1)S(1)}, bf16[784,128]{1,0:T(8,128)(2,1)S(1)}, u32[]{:S(2)}, u32[]{:S(2)}) collective-permute-start(bf16[784,128]{1,0:T(8,128)(2,1)S(1)} %concatenate.7), channel_id=1, source_target_pairs={{0,16},{8,24},{1,17},{9,25},{2,18},{10,26},{3,19},{11,27},{4,20},{... | collective-permute-start | bytes 602120 | tf_op jit(solution)/shard_map/ppermute | solution.py:30
  17.8 3.9 %collective-permute-done.1 = bf16[784,128]{1,0:T(8,128)(2,1)S(1)} collective-permute-done((bf16[784,128]{1,0:T(8,128)(2,1)S(1)}, bf16[784,128]{1,0:T(8,128)(2,1)S(1)}, u32[]{:S(2)}, u32[]{:S(2)}) %collective-permute-start.1) | collective-permute-done | bytes 200736 | tf_op jit(solution)/shard_map/ppermute | solution.py:30
  22.7 1.0 shard_map.112
  23.8 1.6 collective-permute-start.10
  25.3 4.4 %collective-permute-start.2 = (bf16[272,768]{1,0:T(8,128)(2,1)S(1)}, bf16[272,768]{1,0:T(8,128)(2,1)S(1)}, u32[]{:S(2)}, u32[]{:S(2)}) collective-permute-start(bf16[272,768]{1,0:T(8,128)(2,1)S(1)} %shard_map.111.refs_0_), channel_id=1, source_target_pairs={{0,8},{8,0},{16,24},{24,16},{1,9},{9,1},{17,25},{25,17},{2,10},{10... | collective-permute-start | bytes 1253384 | tf_op jit(solution)/shard_map/ppermute | solution.py:435
  30.5 1.2 collective-permute-done.10
  31.6 1.0 pad_maximum_fusion.3.refs_2_
  32.6 1.5 collective-permute-start.11
  34.1 3.9 %collective-permute-done.2.refs_0_ = bf16[272,768]{1,0:T(8,128)(2,1)S(1)} collective-permute-done((bf16[272,768]{1,0:T(8,128)(2,1)S(1)}, bf16[272,768]{1,0:T(8,128)(2,1)S(1)}, u32[]{:S(2)}, u32[]{:S(2)}) %collective-permute-start.2) | collective-permute-done | bytes 417824 | tf_op jit(solution)/shard_map/ppermute | solution.py:435
  38.0 1.0 shard_map.115
  39.1 1.6 collective-permute-start.9
  40.6 1.3 collective-permute-start.7
  42.6 4.3 %collective-permute-done.9 = bf16[768,256]{1,0:T(8,128)(2,1)S(1)} collective-permute-done((bf16[768,256]{1,0:T(8,128)(2,1)S(1)}, bf16[768,256]{1,0:T(8,128)(2,1)S(1)}, u32[]{:S(2)}, u32[]{:S(2)}) %collective-permute-start.9) | collective-permute-done | bytes 393248 | tf_op jit(solution)/shard_map/ppermute | solution.py:435
  47.0 5.3 %collective-permute-done.7.refs_1_ = bf16[272,768]{1,0:T(8,128)(2,1)S(1)} collective-permute-done((bf16[272,768]{1,0:T(8,128)(2,1)S(1)}, bf16[272,768]{1,0:T(8,128)(2,1)S(1)}, u32[]{:S(2)}, u32[]{:S(2)}) %collective-permute-start.7) | collective-permute-done | bytes 417824 | tf_op jit(solution)/shard_map/ppermute | solution.py:536
  52.4 1.0 shard_map.114
  53.4 2.5 %collective-permute-start.8 = (bf16[768,256]{1,0:T(8,128)(2,1)S(1)}, bf16[768,256]{1,0:T(8,128)(2,1)S(1)}, u32[]{:S(2)}, u32[]{:S(2)}) collective-permute-start(bf16[768,256]{1,0:T(8,128)(2,1)S(1)} %get-tuple-element.75), channel_id=1, source_target_pairs={{0,2},{1,5},{2,0},{3,7},{4,6},{5,1},{6,4},{7,3},{8,10},{9,13},{10,... | collective-permute-start | bytes 1179656 | tf_op jit(solution)/shard_map/ppermute | solution.py:435
  55.9 1.5 collective-permute-start.4
  57.5 8.5 %collective-permute-done.8 = bf16[768,256]{1,0:T(8,128)(2,1)S(1)} collective-permute-done((bf16[768,256]{1,0:T(8,128)(2,1)S(1)}, bf16[768,256]{1,0:T(8,128)(2,1)S(1)}, u32[]{:S(2)}, u32[]{:S(2)}) %collective-permute-start.8) | collective-permute-done | bytes 393248 | tf_op jit(solution)/shard_map/ppermute | solution.py:435
  66.0 3.7 %collective-permute-done.4.refs_1_ = bf16[272,768]{1,0:T(8,128)(2,1)S(1)} collective-permute-done((bf16[272,768]{1,0:T(8,128)(2,1)S(1)}, bf16[272,768]{1,0:T(8,128)(2,1)S(1)}, u32[]{:S(2)}, u32[]{:S(2)}) %collective-permute-start.4) | collective-permute-done | bytes 417824 | tf_op jit(solution)/shard_map/ppermute | solution.py:536
  71.0 1.0 copy-done.13
  72.0 1.0 copy-done.15
  73.0 1.0 shard_map.113
  75.9 1.1 copy-done.11
  77.8 8.9 %shard_map.116 = (f32[2,576,256]{2,1,0:T(8,128)S(1)}, f32[2,576,256]{2,1,0:T(8,128)S(1)}, f32[2,2,256]{2,1,0:T(2,128)S(1)}) custom-call(s32[4]{0:T(128)S(1)} %get-tuple-element.140.plan_ref, bf16[2,768,256]{2,1,0:T(8,128)(2,1)S(1)} %pad_maximum_fusion.1.refs_0_, bf16[2,768,256]{2,1,0:T(8,128)(2,1)} %collective-permute-done.13.refs_1_, ...), custom_call_target="tpu_custom_call" | custom-call | flops 3623878656 | bytes 14155776 | tf_op jit(solution)/shard_map/pallas_call | solution.py:347
  86.7 1.0 copy-done.8
  88.2 1.0 pad_maximum_fusion.refs_0_
  89.2 1.7 collective-permute-start.15
  92.0 9.7 %shard_map.117.hidden_ref = bf16[2,256,576]{2,1,0:T(8,128)(2,1)S(1)} custom-call(s32[4]{0:T(128)S(1)} %add_add_fusion.plan_ref, bf16[2,768,256]{2,1,0:T(8,128)(2,1)} %collective-permute-done.16.refs_0_, bf16[2,768,256]{2,1,0:T(8,128)(2,1)} %collective-permute-done.17.refs_1_, bf16[2,768,256]{2,1,0:T(8,128)(2,1)S(1)} %collective-permute-done.12.refs_2_, ...), custom_call_target="tpu_custom_call" | custom-call | flops 3623878656 | bytes 14155776 | tf_op jit(solution)/shard_map/pallas_call | solution.py:347
  101.7 7.2 %shard_map.118 = (bf16[4,256,768]{2,1,0:T(8,128)(2,1)S(1)}, bf16[4,256,768]{2,1,0:T(8,128)(2,1)S(1)}) custom-call(s32[4]{0:T(128)S(1)} %get-tuple-element.141.plan_ref, bf16[2,256,576]{2,1,0:T(8,128)(2,1)S(1)} %shard_map.117.hidden_ref, bf16[2,576,6144]{2,1,0:T(8,128)(2,1)} %down_ref.5), custom_call_target="tpu_custom_call" | custom-call | flops 1811939328 | bytes 7077888 | tf_op jit(solution)/shard_map/pallas_call | solution.py:406
  110.1 7.2 %shard_map.119 = (bf16[4,256,768]{2,1,0:T(8,128)(2,1)S(1)}, bf16[4,256,768]{2,1,0:T(8,128)(2,1)S(1)}) custom-call(s32[4]{0:T(128)S(1)} %pad_add_fusion.3.plan_ref, bf16[2,256,576]{2,1,0:T(8,128)(2,1)S(1)} %shard_map.117.hidden_ref, bf16[2,576,6144]{2,1,0:T(8,128)(2,1)} %down_ref.5), custom_call_target="tpu_custom_call" | custom-call | flops 1811939328 | bytes 7077888 | tf_op jit(solution)/shard_map/pallas_call | solution.py:406
  117.5 1.8 collective-permute-start.24
  119.8 8.9 %shard_map.120 = (f32[2,576,256]{2,1,0:T(8,128)S(1)}, f32[2,576,256]{2,1,0:T(8,128)S(1)}, f32[2,2,256]{2,1,0:T(2,128)S(1)}) custom-call(s32[4]{0:T(128)S(1)} %get-tuple-element.140.plan_ref, bf16[2,768,256]{2,1,0:T(8,128)(2,1)} %pad_maximum_fusion.refs_0_, bf16[2,768,256]{2,1,0:T(8,128)(2,1)S(1)} %collective-permute-done.22.refs_1_, ...), custom_call_target="tpu_custom_call" | custom-call | flops 3623878656 | bytes 14155776 | tf_op jit(solution)/shard_map/pallas_call | solution.py:347
  128.7 1.1 add_convert_fusion.2
  130.0 1.5 collective-permute-start.27
  131.5 1.7 collective-permute-start.26
  133.2 9.3 %shard_map.121.hidden_ref = bf16[2,256,576]{2,1,0:T(8,128)(2,1)S(1)} custom-call(s32[4]{0:T(128)S(1)} %add_add_fusion.plan_ref, bf16[2,768,256]{2,1,0:T(8,128)(2,1)} %collective-permute-done.15.refs_0_, bf16[2,768,256]{2,1,0:T(8,128)(2,1)S(1)} %collective-permute-done.20.refs_1_, bf16[2,768,256]{2,1,0:T(8,128)(2,1)} %collective-permute-done.11.refs_2_, ...), custom_call_target="tpu_custom_call" | custom-call | flops 3623878656 | bytes 14155776 | tf_op jit(solution)/shard_map/pallas_call | solution.py:347
  142.6 1.0 collective-permute-done.26
  144.0 1.4 collective-permute-start.28
  145.5 1.0 collective-permute-done.27.refs_2_
  146.6 1.1 copy-done.3
  147.7 12.7 %shard_map.123 = (bf16[4,256,768]{2,1,0:T(8,128)(2,1)S(1)}, bf16[4,256,768]{2,1,0:T(8,128)(2,1)S(1)}, bf16[4,256,768]{2,1,0:T(8,128)(2,1)S(1)}, bf16[4,256,768]{2,1,0:T(8,128)(2,1)S(1)}) custom-call(s32[8]{0:T(128)S(1)} %concatenate.8.plan_ref, bf16[2,256,576]{2,1,0:T(8,128)(2,1)S(1)} %copy-done.3, bf16[2,576,6144]{2,1,0:T(8,128)(2,1)} %down_ref.5), custom_call_target="tpu_custom_call" | custom-call | flops 3623878656 | bytes 14155776 | tf_op jit(solution)/shard_map/pallas_call | solution.py:406
  161.0 2.9 %collective-permute-done.31.refs_1_ = bf16[4,256,768]{2,1,0:T(8,128)(2,1)S(1)} collective-permute-done((bf16[4,256,768]{2,1,0:T(8,128)(2,1)S(1)}, bf16[4,256,768]{2,1,0:T(8,128)(2,1)S(1)}, u32[]{:S(2)}, u32[]{:S(2)}) %collective-permute-start.31) | collective-permute-done | bytes 1572896 | tf_op jit(solution)/shard_map/ppermute | solution.py:435
  164.1 1.1 collective-permute-start.32
  165.1 5.7 %collective-permute-start.33 = (bf16[256,768]{1,0:T(8,128)(2,1)S(1)}, bf16[256,768]{1,0:T(8,128)(2,1)S(1)}, u32[]{:S(2)}, u32[]{:S(2)}) collective-permute-start(bf16[256,768]{1,0:T(8,128)(2,1)S(1)} %shard_map.122), channel_id=1, source_target_pairs={{0,16},{24,8},{1,17},{25,9},{2,18},{26,10},{3,19},{27,11},{4,20},{... | collective-permute-start | bytes 1179656 | tf_op jit(solution)/shard_map/ppermute | solution.py:613
  170.9 1.1 fusion.1
  172.0 1.3 collective-permute-start.34
  174.3 4.6 %collective-permute-done.33 = bf16[256,768]{1,0:T(8,128)(2,1)S(1)} collective-permute-done((bf16[256,768]{1,0:T(8,128)(2,1)S(1)}, bf16[256,768]{1,0:T(8,128)(2,1)S(1)}, u32[]{:S(2)}, u32[]{:S(2)}) %collective-permute-start.33) | collective-permute-done | bytes 393248 | tf_op jit(solution)/shard_map/ppermute | solution.py:613
  178.9 5.1 %collective-permute-done.34 = bf16[256,768]{1,0:T(8,128)(2,1)S(1)} collective-permute-done((bf16[256,768]{1,0:T(8,128)(2,1)S(1)}, bf16[256,768]{1,0:T(8,128)(2,1)S(1)}, u32[]{:S(2)}, u32[]{:S(2)}) %collective-permute-start.34) | collective-permute-done | bytes 393248 | tf_op jit(solution)/shard_map/ppermute | solution.py:435
  184.2 1.2 collective-permute-start.35
  185.5 1.4 shard_map.126
  187.0 5.3 %collective-permute-done.35 = bf16[256,768]{1,0:T(8,128)(2,1)S(1)} collective-permute-done((bf16[256,768]{1,0:T(8,128)(2,1)S(1)}, bf16[256,768]{1,0:T(8,128)(2,1)S(1)}, u32[]{:S(2)}, u32[]{:S(2)}) %collective-permute-start.35) | collective-permute-done | bytes 393248 | tf_op jit(solution)/shard_map/ppermute | solution.py:435
  192.9 1.0 collective-permute-start.36
  193.9 2.6 %collective-permute-done.37 = bf16[256,768]{1,0:T(8,128)(2,1)S(1)} collective-permute-done((bf16[256,768]{1,0:T(8,128)(2,1)S(1)}, bf16[256,768]{1,0:T(8,128)(2,1)S(1)}, u32[]{:S(2)}, u32[]{:S(2)}) %collective-permute-start.37) | collective-permute-done | bytes 393248 | tf_op jit(solution)/shard_map/ppermute | solution.py:435
  196.5 4.5 %collective-permute-start.39 = (bf16[256,768]{1,0:T(8,128)(2,1)S(1)}, bf16[256,768]{1,0:T(8,128)(2,1)S(1)}, u32[]{:S(2)}, u32[]{:S(2)}) collective-permute-start(bf16[256,768]{1,0:T(8,128)(2,1)S(1)} %shard_map.124), channel_id=1, source_target_pairs={{0,24},{24,0},{1,25},{25,1},{2,26},{26,2},{3,27},{27,3},{4,28},{28... | collective-permute-start | bytes 1179656 | tf_op jit(solution)/shard_map/ppermute | solution.py:627
  201.1 1.3 collective-permute-start.38
  202.8 6.5 %collective-permute-done.39 = bf16[256,768]{1,0:T(8,128)(2,1)S(1)} collective-permute-done((bf16[256,768]{1,0:T(8,128)(2,1)S(1)}, bf16[256,768]{1,0:T(8,128)(2,1)S(1)}, u32[]{:S(2)}, u32[]{:S(2)}) %collective-permute-start.39) | collective-permute-done | bytes 393248 | tf_op jit(solution)/shard_map/ppermute | solution.py:627
  209.3 8.3 %collective-permute-done.38 = bf16[256,768]{1,0:T(8,128)(2,1)S(1)} collective-permute-done((bf16[256,768]{1,0:T(8,128)(2,1)S(1)}, bf16[256,768]{1,0:T(8,128)(2,1)S(1)}, u32[]{:S(2)}, u32[]{:S(2)}) %collective-permute-start.38) | collective-permute-done | bytes 393248 | tf_op jit(solution)/shard_map/ppermute | solution.py:626
  217.7 2.1 add_convert_fusion.8
  (123 shorter events, 15.4 us)
Async XLA Ops:
  2.2 10.8 %collective-permute-start = (bf16[784,128]{1,0:T(8,128)(2,1)S(1)}, bf16[784,128]{1,0:T(8,128)(2,1)S(1)}, u32[]{:S(2)}, u32[]{:S(2)}) collective-permute-start(bf16[784,128]{1,0:T(8,128)(2,1)S(1)} %get-tuple-element.72), channel_id=1, source_target_pairs={{0,8},{8,16},{16,24},{1,9},{9,17},{17,25},{2,10},{10,18},{18,26},{... | collective-permute-start | bytes 602120 | tf_op jit(solution)/shard_map/ppermute | solution.py:30
  7.9 1.0 copy-start.4
  8.9 1.0 copy-start.6
  9.9 1.0 copy-start.7
  13.0 8.9 %copy-start.5 = (bf16[256,768]{1,0:T(8,128)(2,1)S(1)}, bf16[256,768]{1,0:T(8,128)(2,1)}, u32[]{:S(2)}) copy-start(bf16[256,768]{1,0:T(8,128)(2,1)} %query_ref.3) | copy-start | bytes 1179652
  13.0 8.9 %copy-start.19 = (bf16[256,768]{1,0:T(8,128)(2,1)S(1)}, bf16[256,768]{1,0:T(8,128)(2,1)}, u32[]{:S(2)}) copy-start(bf16[256,768]{1,0:T(8,128)(2,1)} %residual_ref.1) | copy-start | bytes 1179652
  13.0 8.9 %copy-start.29 = (s32[256,2]{0,1:T(2,128)S(1)}, s32[256,2]{0,1:T(2,128)}, u32[]{:S(2)}) copy-start(s32[256,2]{0,1:T(2,128)} %param.17) | copy-start | bytes 6148
  13.3 8.5 %collective-permute-start.1 = (bf16[784,128]{1,0:T(8,128)(2,1)S(1)}, bf16[784,128]{1,0:T(8,128)(2,1)S(1)}, u32[]{:S(2)}, u32[]{:S(2)}) collective-permute-start(bf16[784,128]{1,0:T(8,128)(2,1)S(1)} %concatenate.7), channel_id=1, source_target_pairs={{0,16},{8,24},{1,17},{9,25},{2,18},{10,26},{3,19},{11,27},{4,20},{... | collective-permute-start | bytes 602120 | tf_op jit(solution)/shard_map/ppermute | solution.py:30
  22.7 24.3 %copy-start = (bf16[272,768]{1,0:T(8,128)(2,1)}, bf16[272,768]{1,0:T(8,128)(2,1)S(1)}, u32[]{:S(2)}) copy-start(bf16[272,768]{1,0:T(8,128)(2,1)S(1)} %shard_map.111.refs_0_) | copy-start | bytes 1253380
  23.8 10.3 %copy-start.20 = (bf16[256,256]{1,0:T(8,128)(2,1)}, bf16[256,256]{1,0:T(8,128)(2,1)S(1)}, u32[]{:S(2)}) copy-start(bf16[256,256]{1,0:T(8,128)(2,1)S(1)} %get-tuple-element.73.place_ref) | copy-start | bytes 393220
  23.8 7.8 %collective-permute-start.10 = (bf16[768,256]{1,0:T(8,128)(2,1)S(1)}, bf16[768,256]{1,0:T(8,128)(2,1)S(1)}, u32[]{:S(2)}, u32[]{:S(2)}) collective-permute-start(bf16[768,256]{1,0:T(8,128)(2,1)S(1)} %get-tuple-element.77), channel_id=1, source_target_pairs={{0,2},{1,5},{2,0},{3,7},{4,6},{5,1},{6,4},{7,3},{8,10},{9,13},{10,... | collective-permute-start | bytes 1179656 | tf_op jit(solution)/shard_map/ppermute | solution.py:435
  25.3 12.7 %collective-permute-start.2 = (bf16[272,768]{1,0:T(8,128)(2,1)S(1)}, bf16[272,768]{1,0:T(8,128)(2,1)S(1)}, u32[]{:S(2)}, u32[]{:S(2)}) collective-permute-start(bf16[272,768]{1,0:T(8,128)(2,1)S(1)} %shard_map.111.refs_0_), channel_id=1, source_target_pairs={{0,8},{8,0},{16,24},{24,16},{1,9},{9,1},{17,25},{25,17},{2,10},{10... | collective-permute-start | bytes 1253384 | tf_op jit(solution)/shard_map/ppermute | solution.py:435
  29.8 10.8 %collective-permute-start.6 = (bf16[272,768]{1,0:T(8,128)(2,1)S(1)}, bf16[272,768]{1,0:T(8,128)(2,1)S(1)}, u32[]{:S(2)}, u32[]{:S(2)}) collective-permute-start(bf16[272,768]{1,0:T(8,128)(2,1)S(1)} %shard_map.111.refs_0_), channel_id=1, source_target_pairs={{8,16},{16,8},{9,17},{17,9},{10,18},{18,10},{11,19},{19,11},{12,20... | collective-permute-start | bytes 1253384 | tf_op jit(solution)/shard_map/ppermute | solution.py:533
  32.6 19.7 %collective-permute-start.11 = (bf16[2,768,256]{2,1,0:T(8,128)(2,1)}, bf16[2,768,256]{2,1,0:T(8,128)(2,1)}, u32[]{:S(2)}, u32[]{:S(2)}) collective-permute-start(bf16[2,768,256]{2,1,0:T(8,128)(2,1)} %pad_maximum_fusion.3.refs_2_), channel_id=1, source_target_pairs={{0,4},{1,3},{2,6},{3,1},{4,0},{5,7},{6,2},{7,5},{8,12},{9,11},{10,... | collective-permute-start | bytes 2359304 | tf_op jit(solution)/shard_map/ppermute | solution.py:435
  39.1 27.0 %copy-start.22 = (bf16[256,256]{1,0:T(8,128)(2,1)}, bf16[256,256]{1,0:T(8,128)(2,1)S(1)}, u32[]{:S(2)}) copy-start(bf16[256,256]{1,0:T(8,128)(2,1)S(1)} %get-tuple-element.135.place_ref) | copy-start | bytes 393220
  39.1 7.8 %collective-permute-start.9 = (bf16[768,256]{1,0:T(8,128)(2,1)S(1)}, bf16[768,256]{1,0:T(8,128)(2,1)S(1)}, u32[]{:S(2)}, u32[]{:S(2)}) collective-permute-start(bf16[768,256]{1,0:T(8,128)(2,1)S(1)} %get-tuple-element.76), channel_id=1, source_target_pairs={{0,2},{1,5},{2,0},{3,7},{4,6},{5,1},{6,4},{7,3},{8,10},{9,13},{10,... | collective-permute-start | bytes 1179656 | tf_op jit(solution)/shard_map/ppermute | solution.py:435
  40.6 11.6 %collective-permute-start.7 = (bf16[272,768]{1,0:T(8,128)(2,1)S(1)}, bf16[272,768]{1,0:T(8,128)(2,1)S(1)}, u32[]{:S(2)}, u32[]{:S(2)}) collective-permute-start(bf16[272,768]{1,0:T(8,128)(2,1)S(1)} %collective-permute-done.6.refs_0_), channel_id=1, source_target_pairs={{8,0},{16,24},{9,1},{17,25},{10,2},{18,26},{11,3},{19,27},{12,4},{... | collective-permute-start | bytes 1253384 | tf_op jit(solution)/shard_map/ppermute | solution.py:536
  41.9 10.4 %collective-permute-start.3 = (bf16[272,768]{1,0:T(8,128)(2,1)S(1)}, bf16[272,768]{1,0:T(8,128)(2,1)S(1)}, u32[]{:S(2)}, u32[]{:S(2)}) collective-permute-start(bf16[272,768]{1,0:T(8,128)(2,1)S(1)} %collective-permute-done.2.refs_0_), channel_id=1, source_target_pairs={{8,16},{16,8},{9,17},{17,9},{10,18},{18,10},{11,19},{19,11},{12,20... | collective-permute-start | bytes 1253384 | tf_op jit(solution)/shard_map/ppermute | solution.py:533
  52.3 18.2 %copy-start.12 = (bf16[272,768]{1,0:T(8,128)(2,1)}, bf16[272,768]{1,0:T(8,128)(2,1)S(1)}, u32[]{:S(2)}) copy-start(bf16[272,768]{1,0:T(8,128)(2,1)S(1)} %collective-permute-done.3.refs_0_) | copy-start | bytes 1253380
  52.3 18.2 %collective-permute-start.12 = (bf16[2,768,256]{2,1,0:T(8,128)(2,1)S(1)}, bf16[2,768,256]{2,1,0:T(8,128)(2,1)S(1)}, u32[]{:S(2)}, u32[]{:S(2)}) collective-permute-start(bf16[2,768,256]{2,1,0:T(8,128)(2,1)S(1)} %pad_maximum_fusion.2.refs_2_), channel_id=1, source_target_pairs={{0,4},{1,3},{2,6},{3,1},{4,0},{5,7},{6,2},{7,5},{8,12},{9,11},{10,... | collective-permute-start | bytes 2359304 | tf_op jit(solution)/shard_map/ppermute | solution.py:435
  53.4 17.1 %copy-start.26 = (bf16[256,256]{1,0:T(8,128)(2,1)}, bf16[256,256]{1,0:T(8,128)(2,1)S(1)}, u32[]{:S(2)}) copy-start(bf16[256,256]{1,0:T(8,128)(2,1)S(1)} %get-tuple-element.121.place_ref) | copy-start | bytes 393220
  53.4 12.5 %collective-permute-start.8 = (bf16[768,256]{1,0:T(8,128)(2,1)S(1)}, bf16[768,256]{1,0:T(8,128)(2,1)S(1)}, u32[]{:S(2)}, u32[]{:S(2)}) collective-permute-start(bf16[768,256]{1,0:T(8,128)(2,1)S(1)} %get-tuple-element.75), channel_id=1, source_target_pairs={{0,2},{1,5},{2,0},{3,7},{4,6},{5,1},{6,4},{7,3},{8,10},{9,13},{10,... | collective-permute-start | bytes 1179656 | tf_op jit(solution)/shard_map/ppermute | solution.py:435
  55.9 13.8 %collective-permute-start.4 = (bf16[272,768]{1,0:T(8,128)(2,1)S(1)}, bf16[272,768]{1,0:T(8,128)(2,1)S(1)}, u32[]{:S(2)}, u32[]{:S(2)}) collective-permute-start(bf16[272,768]{1,0:T(8,128)(2,1)S(1)} %collective-permute-done.3.refs_0_), channel_id=1, source_target_pairs={{8,0},{16,24},{9,1},{17,25},{10,2},{18,26},{11,3},{19,27},{12,4},{... | collective-permute-start | bytes 1253384 | tf_op jit(solution)/shard_map/ppermute | solution.py:536
  57.4 17.6 %collective-permute-start.14 = (bf16[2,768,256]{2,1,0:T(8,128)(2,1)S(1)}, bf16[2,768,256]{2,1,0:T(8,128)(2,1)S(1)}, u32[]{:S(2)}, u32[]{:S(2)}) collective-permute-start(bf16[2,768,256]{2,1,0:T(8,128)(2,1)S(1)} %pad_maximum_fusion.2.refs_2_), channel_id=1, source_target_pairs={{0,1},{1,0},{2,3},{3,2},{4,5},{5,4},{6,7},{7,6},{8,9},{9,8},{10,11... | collective-permute-start | bytes 2359304 | tf_op jit(solution)/shard_map/ppermute | solution.py:435
  70.5 5.4 %collective-permute-start.13 = (bf16[2,768,256]{2,1,0:T(8,128)(2,1)S(1)}, bf16[2,768,256]{2,1,0:T(8,128)(2,1)}, u32[]{:S(2)}, u32[]{:S(2)}) collective-permute-start(bf16[2,768,256]{2,1,0:T(8,128)(2,1)S(1)} %pad_maximum_fusion.1.refs_0_), channel_id=1, source_target_pairs={{0,1},{1,0},{2,3},{3,2},{4,5},{5,4},{6,7},{7,6},{8,9},{9,8},{10,11... | collective-permute-start | bytes 2359304 | tf_op jit(solution)/shard_map/ppermute | solution.py:435
  70.5 17.2 %collective-permute-start.16 = (bf16[2,768,256]{2,1,0:T(8,128)(2,1)S(1)}, bf16[2,768,256]{2,1,0:T(8,128)(2,1)}, u32[]{:S(2)}, u32[]{:S(2)}) collective-permute-start(bf16[2,768,256]{2,1,0:T(8,128)(2,1)S(1)} %pad_maximum_fusion.1.refs_0_), channel_id=1, source_target_pairs={{0,4},{1,3},{2,6},{3,1},{4,0},{5,7},{6,2},{7,5},{8,12},{9,11},{10,... | collective-permute-start | bytes 2359304 | tf_op jit(solution)/shard_map/ppermute | solution.py:435
  71.0 1.0 copy-start.13
  72.0 1.0 copy-start.15
  74.7 13.5 %collective-permute-start.5 = (bf16[768,256]{1,0:T(8,128)(2,1)S(1)}, bf16[768,256]{1,0:T(8,128)(2,1)S(1)}, u32[]{:S(2)}, u32[]{:S(2)}) collective-permute-start(bf16[768,256]{1,0:T(8,128)(2,1)S(1)} %get-tuple-element.74), channel_id=1, source_target_pairs={{0,2},{1,5},{2,0},{3,7},{4,6},{5,1},{6,4},{7,3},{8,10},{9,13},{10,... | collective-permute-start | bytes 1179656 | tf_op jit(solution)/shard_map/ppermute | solution.py:435
  75.9 1.1 copy-start.11
  86.7 1.0 copy-start.8
  87.7 3.5 %copy-start.9 = (f32[2,576,256]{2,1,0:T(8,128)S(1)}, f32[2,576,256]{2,1,0:T(8,128)}, u32[]{:S(2)}) copy-start(f32[2,576,256]{2,1,0:T(8,128)} %copy-done.8) | copy-start | bytes 3538948
  87.7 3.3 %collective-permute-start.17 = (bf16[2,768,256]{2,1,0:T(8,128)(2,1)}, bf16[2,768,256]{2,1,0:T(8,128)(2,1)}, u32[]{:S(2)}, u32[]{:S(2)}) collective-permute-start(bf16[2,768,256]{2,1,0:T(8,128)(2,1)} %collective-permute-done.16.refs_0_), channel_id=1, source_target_pairs={{0,1},{1,0},{2,3},{3,2},{4,5},{5,4},{6,7},{7,6},{8,9},{9,8},{10,11... | collective-permute-start | bytes 2359304 | tf_op jit(solution)/shard_map/ppermute | solution.py:435
  87.7 3.5 %collective-permute-start.18 = (bf16[2,768,256]{2,1,0:T(8,128)(2,1)S(1)}, bf16[2,768,256]{2,1,0:T(8,128)(2,1)}, u32[]{:S(2)}, u32[]{:S(2)}) collective-permute-start(bf16[2,768,256]{2,1,0:T(8,128)(2,1)S(1)} %collective-permute-done.12.refs_2_), channel_id=1, source_target_pairs={{0,1},{1,0},{2,3},{3,2},{4,5},{5,4},{6,7},{7,6},{8,9},{9,8},{10,11... | collective-permute-start | bytes 2359304 | tf_op jit(solution)/shard_map/ppermute | solution.py:435
  89.2 12.5 %collective-permute-start.15 = (bf16[2,768,256]{2,1,0:T(8,128)(2,1)}, bf16[2,768,256]{2,1,0:T(8,128)(2,1)}, u32[]{:S(2)}, u32[]{:S(2)}) collective-permute-start(bf16[2,768,256]{2,1,0:T(8,128)(2,1)} %pad_maximum_fusion.refs_0_), channel_id=1, source_target_pairs={{0,4},{1,3},{2,6},{3,1},{4,0},{5,7},{6,2},{7,5},{8,12},{9,11},{10,... | collective-permute-start | bytes 2359304 | tf_op jit(solution)/shard_map/ppermute | solution.py:435
  108.9 8.4 %collective-permute-start.19 = (bf16[4,256,768]{2,1,0:T(8,128)(2,1)S(1)}, bf16[4,256,768]{2,1,0:T(8,128)(2,1)S(1)}, u32[]{:S(2)}, u32[]{:S(2)}) collective-permute-start(bf16[4,256,768]{2,1,0:T(8,128)(2,1)S(1)} %get-tuple-element.99), channel_id=1, source_target_pairs={{0,1},{1,0},{2,3},{3,2},{4,5},{5,4},{6,7},{7,6},{8,9},{9,8},{10,11... | collective-permute-start | bytes 4718600 | tf_op jit(solution)/shard_map/ppermute | solution.py:435
  109.1 19.6 %collective-permute-start.25 = (bf16[4,256,768]{2,1,0:T(8,128)(2,1)S(1)}, bf16[4,256,768]{2,1,0:T(8,128)(2,1)S(1)}, u32[]{:S(2)}, u32[]{:S(2)}) collective-permute-start(bf16[4,256,768]{2,1,0:T(8,128)(2,1)S(1)} %get-tuple-element.100), channel_id=1, source_target_pairs={{0,1},{1,0},{2,3},{3,2},{4,5},{5,4},{6,7},{7,6},{8,9},{9,8},{10,11... | collective-permute-start | bytes 4718600 | tf_op jit(solution)/shard_map/ppermute | solution.py:435
  109.5 9.8 %collective-permute-start.23 = (bf16[2,768,256]{2,1,0:T(8,128)(2,1)}, bf16[2,768,256]{2,1,0:T(8,128)(2,1)S(1)}, u32[]{:S(2)}, u32[]{:S(2)}) collective-permute-start(bf16[2,768,256]{2,1,0:T(8,128)(2,1)} %pad_maximum_fusion.3.refs_2_), channel_id=1, source_target_pairs={{0,1},{1,0},{2,3},{3,2},{4,5},{5,4},{6,7},{7,6},{8,9},{9,8},{10,11... | collective-permute-start | bytes 2359304 | tf_op jit(solution)/shard_map/ppermute | solution.py:435
  109.6 9.7 %collective-permute-start.22 = (bf16[2,768,256]{2,1,0:T(8,128)(2,1)}, bf16[2,768,256]{2,1,0:T(8,128)(2,1)S(1)}, u32[]{:S(2)}, u32[]{:S(2)}) collective-permute-start(bf16[2,768,256]{2,1,0:T(8,128)(2,1)} %pad_maximum_fusion.refs_0_), channel_id=1, source_target_pairs={{0,1},{1,0},{2,3},{3,2},{4,5},{5,4},{6,7},{7,6},{8,9},{9,8},{10,11... | collective-permute-start | bytes 2359304 | tf_op jit(solution)/shard_map/ppermute | solution.py:435
  117.3 2.5 %copy-start.18 = (bf16[6144,2]{0,1:T(2,128)(2,1)S(1)}, bf16[6144,2]{0,1:T(2,128)(2,1)}, u32[]{:S(2)}) copy-start(bf16[6144,2]{0,1:T(2,128)(2,1)} %param.18) | copy-start | bytes 73732
  117.5 12.3 %collective-permute-start.24 = (bf16[2,256,768]{2,1,0:T(8,128)(2,1)S(1)}, bf16[2,256,768]{2,1,0:T(8,128)(2,1)S(1)}, u32[]{:S(2)}, u32[]{:S(2)}) collective-permute-start(bf16[2,256,768]{2,1,0:T(8,128)(2,1)S(1)} %add_convert_fusion.3), channel_id=1, source_target_pairs={{0,4},{1,3},{2,6},{3,1},{4,0},{5,7},{6,2},{7,5},{8,12},{9,11},{10,... | collective-permute-start | bytes 2359304 | tf_op jit(solution)/shard_map/ppermute | solution.py:435
  119.3 14.0 %collective-permute-start.20 = (bf16[2,768,256]{2,1,0:T(8,128)(2,1)}, bf16[2,768,256]{2,1,0:T(8,128)(2,1)S(1)}, u32[]{:S(2)}, u32[]{:S(2)}) collective-permute-start(bf16[2,768,256]{2,1,0:T(8,128)(2,1)} %collective-permute-done.15.refs_0_), channel_id=1, source_target_pairs={{0,1},{1,0},{2,3},{3,2},{4,5},{5,4},{6,7},{7,6},{8,9},{9,8},{10,11... | collective-permute-start | bytes 2359304 | tf_op jit(solution)/shard_map/ppermute | solution.py:435
  119.3 13.9 %collective-permute-start.21 = (bf16[2,768,256]{2,1,0:T(8,128)(2,1)}, bf16[2,768,256]{2,1,0:T(8,128)(2,1)S(1)}, u32[]{:S(2)}, u32[]{:S(2)}) collective-permute-start(bf16[2,768,256]{2,1,0:T(8,128)(2,1)} %collective-permute-done.11.refs_2_), channel_id=1, source_target_pairs={{0,1},{1,0},{2,3},{3,2},{4,5},{5,4},{6,7},{7,6},{8,9},{9,8},{10,11... | collective-permute-start | bytes 2359304 | tf_op jit(solution)/shard_map/ppermute | solution.py:435
  130.0 13.6 %copy-start.27 = (bf16[256,256]{1,0:T(8,128)(2,1)S(1)}, bf16[256,256]{1,0:T(8,128)(2,1)}, u32[]{:S(2)}) copy-start(bf16[256,256]{1,0:T(8,128)(2,1)} %copy-done.26) | copy-start | bytes 393220
  130.0 16.6 %collective-permute-start.27 = (bf16[2,256,768]{2,1,0:T(8,128)(2,1)}, bf16[2,256,768]{2,1,0:T(8,128)(2,1)}, u32[]{:S(2)}, u32[]{:S(2)}) collective-permute-start(bf16[2,256,768]{2,1,0:T(8,128)(2,1)} %add_convert_fusion.2), channel_id=1, source_target_pairs={{0,4},{1,3},{2,6},{3,1},{4,0},{5,7},{6,2},{7,5},{8,12},{9,11},{10,... | collective-permute-start | bytes 2359304 | tf_op jit(solution)/shard_map/ppermute | solution.py:435
  131.5 12.1 %collective-permute-start.26 = (bf16[256,768]{1,0:T(8,128)(2,1)S(1)}, bf16[256,768]{1,0:T(8,128)(2,1)S(1)}, u32[]{:S(2)}, u32[]{:S(2)}) collective-permute-start(bf16[256,768]{1,0:T(8,128)(2,1)S(1)} %fusion), channel_id=1, source_target_pairs={{0,2},{1,5},{2,0},{3,7},{4,6},{5,1},{6,4},{7,3},{8,10},{9,13},{10,... | collective-permute-start | bytes 1179656 | tf_op jit(solution)/shard_map/ppermute | solution.py:435
  142.6 1.4 copy-start.2
  144.0 16.4 %collective-permute-start.28 = (bf16[256,768]{1,0:T(8,128)(2,1)S(1)}, bf16[256,768]{1,0:T(8,128)(2,1)}, u32[]{:S(2)}, u32[]{:S(2)}) collective-permute-start(bf16[256,768]{1,0:T(8,128)(2,1)S(1)} %shard_map.122), channel_id=1, source_target_pairs={{8,16},{16,8},{9,17},{17,9},{10,18},{18,10},{11,19},{19,11},{12,20... | collective-permute-start | bytes 1179656 | tf_op jit(solution)/shard_map/ppermute | solution.py:607
  146.6 1.1 copy-start.3
  160.4 3.5 %collective-permute-start.31 = (bf16[4,256,768]{2,1,0:T(8,128)(2,1)S(1)}, bf16[4,256,768]{2,1,0:T(8,128)(2,1)S(1)}, u32[]{:S(2)}, u32[]{:S(2)}) collective-permute-start(bf16[4,256,768]{2,1,0:T(8,128)(2,1)S(1)} %get-tuple-element.130), channel_id=1, source_target_pairs={{0,1},{1,0},{2,3},{3,2},{4,5},{5,4},{6,7},{7,6},{8,9},{9,8},{10,11... | collective-permute-start | bytes 4718600 | tf_op jit(solution)/shard_map/ppermute | solution.py:435
  160.5 12.8 %collective-permute-start.29 = (bf16[4,256,768]{2,1,0:T(8,128)(2,1)S(1)}, bf16[4,256,768]{2,1,0:T(8,128)(2,1)S(1)}, u32[]{:S(2)}, u32[]{:S(2)}) collective-permute-start(bf16[4,256,768]{2,1,0:T(8,128)(2,1)S(1)} %get-tuple-element.128), channel_id=1, source_target_pairs={{0,1},{1,0},{2,3},{3,2},{4,5},{5,4},{6,7},{7,6},{8,9},{9,8},{10,11... | collective-permute-start | bytes 4718600 | tf_op jit(solution)/shard_map/ppermute | solution.py:435
  164.1 20.0 %collective-permute-start.32 = (bf16[2,256,768]{2,1,0:T(8,128)(2,1)S(1)}, bf16[2,256,768]{2,1,0:T(8,128)(2,1)S(1)}, u32[]{:S(2)}, u32[]{:S(2)}) collective-permute-start(bf16[2,256,768]{2,1,0:T(8,128)(2,1)S(1)} %add_convert_fusion), channel_id=1, source_target_pairs={{0,4},{1,3},{2,6},{3,1},{4,0},{5,7},{6,2},{7,5},{8,12},{9,11},{10,... | collective-permute-start | bytes 2359304 | tf_op jit(solution)/shard_map/ppermute | solution.py:435
  165.1 13.8 %collective-permute-start.33 = (bf16[256,768]{1,0:T(8,128)(2,1)S(1)}, bf16[256,768]{1,0:T(8,128)(2,1)S(1)}, u32[]{:S(2)}, u32[]{:S(2)}) collective-permute-start(bf16[256,768]{1,0:T(8,128)(2,1)S(1)} %shard_map.122), channel_id=1, source_target_pairs={{0,16},{24,8},{1,17},{25,9},{2,18},{26,10},{3,19},{27,11},{4,20},{... | collective-permute-start | bytes 1179656 | tf_op jit(solution)/shard_map/ppermute | solution.py:613
  172.0 12.1 %collective-permute-start.34 = (bf16[256,768]{1,0:T(8,128)(2,1)S(1)}, bf16[256,768]{1,0:T(8,128)(2,1)S(1)}, u32[]{:S(2)}, u32[]{:S(2)}) collective-permute-start(bf16[256,768]{1,0:T(8,128)(2,1)S(1)} %fusion.1), channel_id=1, source_target_pairs={{0,2},{1,5},{2,0},{3,7},{4,6},{5,1},{6,4},{7,3},{8,10},{9,13},{10,... | collective-permute-start | bytes 1179656 | tf_op jit(solution)/shard_map/ppermute | solution.py:435
  173.3 12.2 %copy-start.23 = (bf16[256,256]{1,0:T(8,128)(2,1)S(1)}, bf16[256,256]{1,0:T(8,128)(2,1)}, u32[]{:S(2)}) copy-start(bf16[256,256]{1,0:T(8,128)(2,1)} %copy-done.22) | copy-start | bytes 393220
  173.5 19.2 %collective-permute-start.30 = (bf16[2,256,768]{2,1,0:T(8,128)(2,1)S(1)}, bf16[2,256,768]{2,1,0:T(8,128)(2,1)S(1)}, u32[]{:S(2)}, u32[]{:S(2)}) collective-permute-start(bf16[2,256,768]{2,1,0:T(8,128)(2,1)S(1)} %add_convert_fusion.1), channel_id=1, source_target_pairs={{0,4},{1,3},{2,6},{3,1},{4,0},{5,7},{6,2},{7,5},{8,12},{9,11},{10,... | collective-permute-start | bytes 2359304 | tf_op jit(solution)/shard_map/ppermute | solution.py:435
  184.2 8.0 %collective-permute-start.35 = (bf16[256,768]{1,0:T(8,128)(2,1)S(1)}, bf16[256,768]{1,0:T(8,128)(2,1)S(1)}, u32[]{:S(2)}, u32[]{:S(2)}) collective-permute-start(bf16[256,768]{1,0:T(8,128)(2,1)S(1)} %fusion.2), channel_id=1, source_target_pairs={{0,2},{1,5},{2,0},{3,7},{4,6},{5,1},{6,4},{7,3},{8,10},{9,13},{10,... | collective-permute-start | bytes 1179656 | tf_op jit(solution)/shard_map/ppermute | solution.py:435
  185.5 6.8 %copy-start.25 = (bf16[256,256]{1,0:T(8,128)(2,1)S(1)}, bf16[256,256]{1,0:T(8,128)(2,1)}, u32[]{:S(2)}) copy-start(bf16[256,256]{1,0:T(8,128)(2,1)} %copy-done.24) | copy-start | bytes 393220
  186.9 9.6 %collective-permute-start.37 = (bf16[256,768]{1,0:T(8,128)(2,1)S(1)}, bf16[256,768]{1,0:T(8,128)(2,1)S(1)}, u32[]{:S(2)}, u32[]{:S(2)}) collective-permute-start(bf16[256,768]{1,0:T(8,128)(2,1)S(1)} %shard_map.126), channel_id=1, source_target_pairs={{0,8},{8,0},{16,24},{24,16},{1,9},{9,1},{17,25},{25,17},{2,10},{10... | collective-permute-start | bytes 1179656 | tf_op jit(solution)/shard_map/ppermute | solution.py:435
  192.7 9.7 %copy-start.21 = (bf16[256,256]{1,0:T(8,128)(2,1)S(1)}, bf16[256,256]{1,0:T(8,128)(2,1)}, u32[]{:S(2)}) copy-start(bf16[256,256]{1,0:T(8,128)(2,1)} %copy-done.20) | copy-start | bytes 393220
  192.9 9.5 %collective-permute-start.36 = (bf16[256,768]{1,0:T(8,128)(2,1)S(1)}, bf16[256,768]{1,0:T(8,128)(2,1)S(1)}, u32[]{:S(2)}, u32[]{:S(2)}) collective-permute-start(bf16[256,768]{1,0:T(8,128)(2,1)S(1)} %fusion.3), channel_id=1, source_target_pairs={{0,2},{1,5},{2,0},{3,7},{4,6},{5,1},{6,4},{7,3},{8,10},{9,13},{10,... | collective-permute-start | bytes 1179656 | tf_op jit(solution)/shard_map/ppermute | solution.py:435
  196.5 12.8 %collective-permute-start.39 = (bf16[256,768]{1,0:T(8,128)(2,1)S(1)}, bf16[256,768]{1,0:T(8,128)(2,1)S(1)}, u32[]{:S(2)}, u32[]{:S(2)}) collective-permute-start(bf16[256,768]{1,0:T(8,128)(2,1)S(1)} %shard_map.124), channel_id=1, source_target_pairs={{0,24},{24,0},{1,25},{25,1},{2,26},{26,2},{3,27},{27,3},{4,28},{28... | collective-permute-start | bytes 1179656 | tf_op jit(solution)/shard_map/ppermute | solution.py:627
  201.1 16.6 %collective-permute-start.38 = (bf16[256,768]{1,0:T(8,128)(2,1)S(1)}, bf16[256,768]{1,0:T(8,128)(2,1)S(1)}, u32[]{:S(2)}, u32[]{:S(2)}) collective-permute-start(bf16[256,768]{1,0:T(8,128)(2,1)S(1)} %shard_map.124), channel_id=1, source_target_pairs={{8,24},{16,0},{9,25},{17,1},{10,26},{18,2},{11,27},{19,3},{12,28},... | collective-permute-start | bytes 1179656 | tf_op jit(solution)/shard_map/ppermute | solution.py:626
  202.4 15.3 %copy-start.1 = (bf16[272,768]{1,0:T(8,128)(2,1)S(1)}, bf16[272,768]{1,0:T(8,128)(2,1)}, u32[]{:S(2)}) copy-start(bf16[272,768]{1,0:T(8,128)(2,1)} %copy-done) | copy-start | bytes 1253380
  (6 other events, 4.5 us)
